TPU v7x, 32 devices: a whole 2x2x4 slice. The times are simulated.
32 devices in a mesh: seq: 16 (over z, x, core), tp: 2 (over y).
Axes of the slice: x: 2, y: 2, z: 4, core: 2. Of those that a mesh axis runs over, the one named last changes fastest.
Arguments:
- tokens: bfloat16 [4096, 3200], P('seq'), may hold values from -8 to 8
- norm_gain: float32 [3200], replicated, may hold values from 0.5 to 1.5
- qkv_weight: bfloat16 [3200, 3, 2048], P('seq', None, 'tp'), may hold values from -1 to 1
- q_gain: float32 [2048], P('tp'), may hold values from 0.5 to 5, as said below
- k_gain: float32 [2048], P('tp'), may hold values from 0.5 to 5, as said below
- out_weight: bfloat16 [2048, 3200], P('tp', 'seq'), may hold values from -0.125 to 0.125
- layer_scale: float32 [3200], P('tp'), may hold values from 0.5 to 2
- segment_ids: int32 [4096], replicated, may hold values from 0 to 15, never falling along the last dimension, each value on 1 to 512 neighbouring positions
Outputs:
- mixed: bfloat16 [4096, 3200], P('seq', 'tp')
Inputs may be any that keep to these rules, and one draw needn't show every extreme that they name: `segment_ids`: image numbers never fall along the row; each image has 1 to 512 patches, one exactly 512. `q_gain`: positive gains. `k_gain`: positive gains.
All inputs are finite; a program needn't handle non-finite values.
Results may differ from a plain program's by a relative error of at most 0.0078.
Values may be sent and summed in bfloat16 or wider, within the bound.
No kernel may reach another device: no remote copies, remote signals or barrier semaphores. Data moves between devices by JAX's collectives and lax.ppermute only.
A program may use at most 64 MiB of HBM per device.

v0:
```python
import jax
import jax.numpy as jnp
from jax import lax
from jax.sharding import PartitionSpec as P

HEAD_DIM = 128


eps = 1e-06
floor_score = -1e30


def passed_along(x, axis, by):
    size = lax.axis_size(axis)
    pairs = [(i, i + by) for i in range(size) if 0 <= i + by < size]
    return lax.ppermute(x, axis, pairs)


def masked_scores(query, keys, query_seg, key_seg):
    scores = jnp.einsum(
        "qhd,khd->hqk", query, keys, preferred_element_type=jnp.float32
    ) * HEAD_DIM ** (-0.5)
    mask = (query_seg[:, None] == key_seg[None, :])[None]
    return (jnp.where(mask, scores, floor_score), mask)


def shards(tokens, norm_gain, qkv_weight, q_gain, k_gain, out_weight, layer_scale, segment_ids):
    count = tokens.shape[0]
    source = tokens.astype(jnp.float32)
    normed = (
        source * lax.rsqrt(jnp.mean(source * source, axis=-1, keepdims=True) + eps) * norm_gain
    ).astype(jnp.bfloat16)
    local_width = qkv_weight.shape[2]
    heads = local_width // HEAD_DIM
    joined = jnp.einsum(
        "td,dch->tch",
        normed,
        lax.all_gather(qkv_weight, "seq", axis=0, tiled=True),
        preferred_element_type=jnp.float32,
    )
    query = joined[:, 0]
    keys = joined[:, 1]
    values = joined[:, 2]
    query_sq, key_sq = lax.psum(
        (jnp.sum(query * query, axis=-1), jnp.sum(keys * keys, axis=-1)), "tp"
    )
    full_width = local_width * lax.axis_size("tp")
    query_normed = (query * lax.rsqrt(query_sq / full_width + eps)[:, None] * q_gain).astype(
        jnp.bfloat16
    )
    key_normed = (keys * lax.rsqrt(key_sq / full_width + eps)[:, None] * k_gain).astype(
        jnp.bfloat16
    )
    paired = jnp.stack([key_normed, values.astype(jnp.bfloat16)], axis=1)
    pieces = []
    for offset in (2, 1, 0, -1, -2):
        if offset == 0:
            pieces.append(paired)
        else:
            pieces.append(passed_along(paired, "seq", offset))
    widened = jnp.concatenate(pieces, axis=0)
    position = lax.axis_index("seq")
    outside = jnp.full((2 * count,), -1, jnp.int32)
    seg_pad = jnp.concatenate([outside, segment_ids, outside], axis=0)
    key_seg = lax.dynamic_slice_in_dim(seg_pad, position * count, 5 * count, 0)
    query_seg = lax.dynamic_slice_in_dim(segment_ids, position * count, count, 0)
    query_heads = query_normed.reshape(count, heads, HEAD_DIM)
    key_heads = widened[:, 0].reshape(5 * count, heads, HEAD_DIM)
    value_heads = widened[:, 1].reshape(5 * count, heads, HEAD_DIM)
    scores, mask = masked_scores(query_heads, key_heads, query_seg, key_seg)
    peak = jnp.max(scores, axis=-1, keepdims=True)
    weights = jnp.where(mask, jnp.exp(scores - peak), 0.0)
    total = jnp.sum(weights, axis=-1)
    probs = weights.astype(jnp.bfloat16)
    summed = jnp.einsum("hqk,khd->qhd", probs, value_heads, preferred_element_type=jnp.float32)
    context = (
        (summed / jnp.transpose(total)[:, :, None]).reshape(count, local_width).astype(jnp.bfloat16)
    )
    terms = jnp.dot(
        context,
        lax.all_gather(out_weight, "seq", axis=1, tiled=True),
        preferred_element_type=jnp.float32,
    )
    projected = lax.psum_scatter(terms, "tp", scatter_dimension=1, tiled=True)
    share = layer_scale.shape[0]
    residual = lax.dynamic_slice_in_dim(source, lax.axis_index("tp") * share, share, 1)
    return (residual + layer_scale * projected).astype(jnp.bfloat16)


def solution(mesh):
    return jax.shard_map(
        shards,
        mesh=mesh,
        in_specs=(
            P("seq", None),
            P(),
            P("seq", None, "tp"),
            P("tp"),
            P("tp"),
            P("tp", "seq"),
            P("tp"),
            P(),
        ),
        out_specs=P("seq", "tp"),
        check_vma=False,
    )
```

profile of v0, /device:TPU:9, one launch (start us, length us, event | category | flops | bytes accessed | tf_op | source)
XLA Modules:
  0.0 306.2 jit_solution(17267970870475239437)
XLA Ops:
  8.1 3.0 copy.9
  12.2 100.9 %all-gather.3.cloned.1.call-done = bf16[3200,3,1024]{2,0,1:T(8,128)(2,1)} async-done(((bf16[200,3,1024]{2,0,1:T(8,128)(2,1)}), bf16[3200,3,1024]{2,0,1:T(8,128)(2,1)}) %all-gather.3.cloned.1.call-update) | async-done | bytes 19660816 | tf_op jit(solution)/shard_map/all_gather | solution.py:38
  113.2 10.1 %fusion.10 = f32[256,3,1024]{2,0,1:T(8,128)S(1)} fusion(bf16[3200,3,1024]{2,0,1:T(8,128)(2,1)} %all-gather.3.cloned.1.call-done, f32[3200]{0:T(1024)S(1)} %copy-done.6, f32[256]{0:T(256)S(1)} %add_rsqrt_fusion.2, bf16[256,3200]{0,1:T(8,128)(2,1)} %copy-done), kind=kOutput, calls=%fused_computation.15 | convolution fusion | flops 5036441600 | bytes 24458752 | tf_op jit(solution)/shard_map/td,dch->tch/dot_general | solution.py:35
  124.1 1.1 multiply_reduce_fusion.1
  125.3 4.2 %all-reduce = (f32[256]{0:T(256)S(1)}, f32[256]{0:T(256)S(1)}) all-reduce(f32[256]{0:T(256)S(1)} %get-tuple-element.6, f32[256]{0:T(256)S(1)} %get-tuple-element.5), channel_id=1, replica_groups=mesh['seq'=16,'tp'=2] {'tp'}, use_global_device_ids=true, to_apply=%region_2.0 | all-reduce | flops 512 | bytes 4096 | tf_op jit(solution)/shard_map/psum | solution.py:44
  130.4 1.1 pad_maximum_fusion
  131.6 2.9 collective-permute-start
  134.5 4.4 %collective-permute-start.1 = (bf16[256,2,1024]{2,0,1:T(8,128)(2,1)S(1)}, bf16[256,2,1024]{2,0,1:T(8,128)(2,1)S(1)}, u32[]{:S(2)}, u32[]{:S(2)}) collective-permute-start(bf16[256,2,1024]{2,0,1:T(8,128)(2,1)S(1)} %pad_maximum_fusion), channel_id=1, source_target_pairs={{0,2},{2,4},{4,6},{6,8},{8,10},{10,12},{12,14},{14,16},{16,18},{18... | collective-permute-start | bytes 3145736 | tf_op jit(solution)/shard_map/ppermute | solution.py:16
  139.0 1.9 collective-permute-start.2
  140.9 3.1 %collective-permute-start.3 = (bf16[256,2,1024]{2,0,1:T(8,128)(2,1)S(1)}, bf16[256,2,1024]{2,0,1:T(8,128)(2,1)}, u32[]{:S(2)}, u32[]{:S(2)}) collective-permute-start(bf16[256,2,1024]{2,0,1:T(8,128)(2,1)S(1)} %pad_maximum_fusion), channel_id=1, source_target_pairs={{4,0},{6,2},{8,4},{10,6},{12,8},{14,10},{16,12},{18,14},{20,16},{2... | collective-permute-start | bytes 3145736 | tf_op jit(solution)/shard_map/ppermute | solution.py:16
  144.5 2.5 copy.17
  146.9 54.6 %collective-permute-done = bf16[256,2,1024]{2,0,1:T(8,128)(2,1)} collective-permute-done((bf16[256,2,1024]{2,0,1:T(8,128)(2,1)S(1)}, bf16[256,2,1024]{2,0,1:T(8,128)(2,1)}, u32[]{:S(2)}, u32[]{:S(2)}) %collective-permute-start) | collective-permute-done | bytes 1048608 | tf_op jit(solution)/shard_map/ppermute | solution.py:16
  201.5 1.3 constant_dynamic-update-slice_fusion.4
  202.8 17.2 %collective-permute-done.1 = bf16[256,2,1024]{2,0,1:T(8,128)(2,1)S(1)} collective-permute-done((bf16[256,2,1024]{2,0,1:T(8,128)(2,1)S(1)}, bf16[256,2,1024]{2,0,1:T(8,128)(2,1)S(1)}, u32[]{:S(2)}, u32[]{:S(2)}) %collective-permute-start.1) | collective-permute-done | bytes 1048608 | tf_op jit(solution)/shard_map/ppermute | solution.py:16
  220.2 1.3 constant_dynamic-update-slice_fusion
  222.4 2.2 copy.18
  224.6 2.7 copy.16
  227.4 9.5 %fusion.39 = (f32[8,256]{1,0:T(8,128)S(1)}, bf16[8,256,1280]{2,1,0:T(8,128)(2,1)}) fusion(pred[256,1280]{1,0:T(8,128)(4,1)S(1)} %broadcast_compare_fusion, bf16[1280,8,128]{2,1,0:T(8,128)(2,1)} %bitcast.28, f32[256,8,128]{2,1,0:T(8,128)} %bitcast.30, f32[8,128]{1,0:T(8,128)S(1)} %bitcast.31, f32[256]{0:T(256)S(1)} %get-tuple-element.14), kind=kOutput, calls=%fused_computation.48 | convolution fusion | flops 687604992 | bytes 9253888 | tf_op jit(solution)/shard_map/sub | solution.py:72
  236.9 4.3 %fusion.21 = bf16[256,8,128]{0,2,1:T(8,128)(2,1)S(1)} fusion(bf16[1280,8,128]{0,2,1:T(8,128)(2,1)S(1)} %bitcast.29, bf16[8,256,1280]{2,1,0:T(8,128)(2,1)} %get-tuple-element.13, f32[256,8]{0,1:T(8,128)S(1)} %bitcast.33), kind=kOutput, calls=%fused_computation.22 | convolution fusion | flops 671612928 | bytes 8396800 | tf_op jit(solution)/shard_map/hqk,khd->qhd/dot_general | solution.py:75
  241.2 6.4 %fusion.44 = f32[256,3200]{0,1:T(8,128)} fusion(bf16[1024,3200]{0,1:T(8,128)(2,1)} %all-gather.5.cloned.1.call-done, bf16[256,1024]{0,1:T(8,128)(2,1)S(1)} %bitcast.32), kind=kOutput, calls=%fused_computation.49 | convolution fusion | flops 1677721600 | bytes 10354688 | tf_op jit(solution)/shard_map/dot_general | solution.py:79
  247.7 1.4 copy-done.1
  249.1 2.0 convert_element_type.28
  251.0 45.5 %reduce-scatter.2.cloned.1.call-done = f32[256,1600]{0,1:T(8,128)} async-done(((f32[256,3200]{0,1:T(8,128)}), f32[256,1600]{0,1:T(8,128)}) %reduce-scatter.2.cloned.1.call-update) | async-done | bytes 1638416 | tf_op jit(solution)/shard_map/reduce_scatter | solution.py:84
  296.6 3.1 %add_convert_fusion = bf16[256,1600]{0,1:T(8,128)(2,1)} fusion(f32[256,1600]{0,1:T(8,128)} %reduce-scatter.2.cloned.1.call-done, f32[256,3200]{0,1:T(8,128)} %convert_element_type.28, s32[]{:T(128)S(6)} %select_n.16, f32[1600]{0:T(1024)S(1)} %copy-done.8), kind=kLoop, calls=%fused_computation.16 | loop fusion | flops 1228800 | bytes 4102404 | tf_op jit(solution)/shard_map/convert_element_type | solution.py:87
  (43 shorter events, 6.1 us)
Async XLA Ops:
  6.5 106.6 %copy-start.6 = (f32[3200]{0:T(1024)S(1)}, f32[3200]{0:T(1024)}, u32[]{:S(2)}) copy-start(f32[3200]{0:T(1024)} %param.9) | copy-start | bytes 38404
  6.5 106.6 %all-gather.3.cloned.1.call-start = ((), (), s32[]{:S(2)}) async-start(), calls=%async_computation.1 | async-start | bytes 20889600 | tf_op jit(solution)/shard_map/all_gather | solution.py:38
  7.3 233.9 %all-gather.5.cloned.1.call-start = ((), (), s32[]{:S(2)}) async-start(), calls=%async_computation.2 | async-start | bytes 6963200 | tf_op jit(solution)/shard_map/all_gather | solution.py:81
  8.0 288.6 %reduce-scatter.2.cloned.1.call-start = ((), (), s32[]{:S(2)}) async-start(), calls=%async_computation.3 | async-start | bytes 4915200 | tf_op jit(solution)/shard_map/reduce_scatter | solution.py:84
  11.1 1.2 copy-start
  123.3 6.2 %copy-start.9 = (f32[1024]{0:T(1024)S(1)}, f32[1024]{0:T(1024)}, u32[]{:S(2)}) copy-start(f32[1024]{0:T(1024)} %param.12) | copy-start | bytes 12292
  124.1 19.9 %copy-start.7 = (s32[4096]{0:T(1024)S(1)}, s32[4096]{0:T(1024)}, u32[]{:S(2)}) copy-start(s32[4096]{0:T(1024)} %param.15) | copy-start | bytes 49156
  129.6 0.8 copy-start.3
  131.6 69.9 %collective-permute-start = (bf16[256,2,1024]{2,0,1:T(8,128)(2,1)S(1)}, bf16[256,2,1024]{2,0,1:T(8,128)(2,1)}, u32[]{:S(2)}, u32[]{:S(2)}) collective-permute-start(bf16[256,2,1024]{2,0,1:T(8,128)(2,1)S(1)} %pad_maximum_fusion), channel_id=1, source_target_pairs={{0,4},{2,6},{4,8},{6,10},{8,12},{10,14},{12,16},{14,18},{16,20},{1... | collective-permute-start | bytes 3145736 | tf_op jit(solution)/shard_map/ppermute | solution.py:16
  134.5 85.5 %collective-permute-start.1 = (bf16[256,2,1024]{2,0,1:T(8,128)(2,1)S(1)}, bf16[256,2,1024]{2,0,1:T(8,128)(2,1)S(1)}, u32[]{:S(2)}, u32[]{:S(2)}) collective-permute-start(bf16[256,2,1024]{2,0,1:T(8,128)(2,1)S(1)} %pad_maximum_fusion), channel_id=1, source_target_pairs={{0,2},{2,4},{4,6},{6,8},{8,10},{10,12},{12,14},{14,16},{16,18},{18... | collective-permute-start | bytes 3145736 | tf_op jit(solution)/shard_map/ppermute | solution.py:16
  139.0 81.2 %collective-permute-start.2 = (bf16[256,2,1024]{2,0,1:T(8,128)(2,1)S(1)}, bf16[256,2,1024]{2,0,1:T(8,128)(2,1)S(1)}, u32[]{:S(2)}, u32[]{:S(2)}) collective-permute-start(bf16[256,2,1024]{2,0,1:T(8,128)(2,1)S(1)} %pad_maximum_fusion), channel_id=1, source_target_pairs={{2,0},{4,2},{6,4},{8,6},{10,8},{12,10},{14,12},{16,14},{18,16},{20... | collective-permute-start | bytes 3145736 | tf_op jit(solution)/shard_map/ppermute | solution.py:16
  140.9 79.3 %collective-permute-start.3 = (bf16[256,2,1024]{2,0,1:T(8,128)(2,1)S(1)}, bf16[256,2,1024]{2,0,1:T(8,128)(2,1)}, u32[]{:S(2)}, u32[]{:S(2)}) collective-permute-start(bf16[256,2,1024]{2,0,1:T(8,128)(2,1)S(1)} %pad_maximum_fusion), channel_id=1, source_target_pairs={{4,0},{6,2},{8,4},{10,6},{12,8},{14,10},{16,12},{18,14},{20,16},{2... | collective-permute-start | bytes 3145736 | tf_op jit(solution)/shard_map/ppermute | solution.py:16
  144.2 75.9 %copy-start.2 = (bf16[256,1,1024]{2,0,1:T(8,128)(2,1)S(1)}, bf16[256,1,1024]{2,0,1:T(8,128)(2,1)}, u32[]{:S(2)}) copy-start(bf16[256,1,1024]{2,0,1:T(8,128)(2,1)} %slice.32) | copy-start | bytes 1572868
  144.2 75.9 %copy-start.4 = (bf16[256,1,1024]{2,0,1:T(8,128)(2,1)S(1)}, bf16[256,1,1024]{2,0,1:T(8,128)(2,1)}, u32[]{:S(2)}) copy-start(bf16[256,1,1024]{2,0,1:T(8,128)(2,1)} %copy-done.3) | copy-start | bytes 1572868
  224.6 2.7 copy-start.10
  227.4 9.5 %copy-start.5 = (bf16[1280,1,1024]{0,2,1:T(8,128)(2,1)S(1)}, bf16[1280,1,1024]{0,2,1:T(8,128)(2,1)}, u32[]{:S(2)}) copy-start(bf16[1280,1,1024]{0,2,1:T(8,128)(2,1)} %copy.16) | copy-start | bytes 7864324
  247.6 1.4 copy-start.1
  247.7 48.9 %copy-start.8 = (f32[1600]{0:T(1024)S(1)}, f32[1600]{0:T(1024)}, u32[]{:S(2)}) copy-start(f32[1600]{0:T(1024)} %param.14) | copy-start | bytes 19204
Sparse Core Ops, SparseCore 0:
  8.9 104.1 all-gather.2
  115.4 106.7 all-gather.4
  247.8 48.7 reduce-scatter.1
where the time goes:
time: 308 us; the launch traced here: 306 us
  waiting for transfers between devices  220 us (71%)
  matrix products  30.3 us (10%)
  local copies, waits for them, and re-layouts  17.9 us (6%)
  between operations  13.3 us (4%)
  starting transfers between devices  12.5 us (4%)
  other arithmetic  8.39 us (3%)
  blocking collectives  4.17 us (1%)
    all_gather x1, waiting for transfers between devices, shards(): lax.all_gather(qkv_weight, 'seq', axis=0, tiled=True)  101 us
    ppermute x4, waiting for transfers between devices, passed_along(): return lax.ppermute(x, axis, pairs)  71.8 us
    reduce_scatter x1, waiting for transfers between devices, shards(): projected = lax.psum_scatter(terms, 'tp', scatter_dimension=1, tiled=True)  45.5 us
    unnamed x29, local copies, waits for them, and re-layouts  12.9 us
    ppermute x4, starting transfers between devices, passed_along(): return lax.ppermute(x, axis, pairs)  12.4 us
    dot_general x1, matrix products, shards(): jnp.einsum('td,dch->tch', normed, lax.all_gather(qkv_weight, 'seq', axis=...  10.1 us
    sub x1, matrix products, shards(): weights = jnp.where(mask, jnp.exp(scores - peak), 0.0)  9.5 us
    dot_general x1, matrix products, shards(): jnp.dot(context, lax.all_gather(out_weight, 'seq', axis=1, tiled=True), p...  6.42 us
  transfers between devices with their start and end apart: 7, of which 4 were waited for; matrix products, arithmetic and copies ran while one was open for 14% of the time, Pallas kernels for 0%

commit v1 on v0

--- a/solution.py
+++ b/solution.py
@@ -1,10 +1,14 @@
+import functools
+
 import jax
 import jax.numpy as jnp
 from jax import lax
+from jax.experimental import pallas as pl
+from jax.experimental.pallas import tpu as pltpu
 from jax.sharding import PartitionSpec as P
 
 HEAD_DIM = 128
-
+SLAB = 4
 
 eps = 1e-06
 floor_score = -1e30
@@ -24,7 +28,7 @@
     return (jnp.where(mask, scores, floor_score), mask)
 
 
-def shards(tokens, norm_gain, qkv_weight, q_gain, k_gain, out_weight, layer_scale, segment_ids):
+def row_plan(tokens, norm_gain, qkv_weight, q_gain, k_gain, out_weight, layer_scale, segment_ids):
     count = tokens.shape[0]
     source = tokens.astype(jnp.float32)
     normed = (
@@ -87,7 +91,337 @@
     return (residual + layer_scale * projected).astype(jnp.bfloat16)
 
 
+ANY = pl.BlockSpec(memory_space=pl.ANY)
+VMEM = pl.BlockSpec(memory_space=pltpu.VMEM)
+SMEM = pl.BlockSpec(memory_space=pltpu.SMEM)
+
+
+def in_slab(x, flip):
+    size = lax.axis_size("seq")
+    return lax.ppermute(x, "seq", [(i, i ^ flip) for i in range(size)])
+
+
+def across(x):
+    return lax.ppermute(x, "tp", [(0, 1), (1, 0)])
+
+
+def along_z(x, by):
+    return passed_along(x, "seq", SLAB * by)
+
+
+def as_row(column):
+    wide = jnp.broadcast_to(column, (column.shape[0], 128))
+    return jnp.transpose(wide)[:8]
+
+
+def as_column(row):
+    return jnp.transpose(jnp.broadcast_to(row, (128, row.shape[1])))
+
+
+def project_kernel(
+    slabs, place, x0, x1, x2, x3, own, above, below, q_gain, k_gain,
+    query, keys, values, squares, x_all, w_all, x_sem, w_sem, up_sem, down_sem,
+):
+    z, q = place[0], place[1]
+    rows = own.shape[1]
+    w_copies = []
+
+    def weight_copy(src, at, sem):
+        at = pl.multiple_of(at * rows, 32)
+        return pltpu.make_async_copy(src, w_all.at[:, pl.ds(at, rows), :], sem)
+
+    mine = weight_copy(own, z, w_sem)
+    mine.start()
+    for r in range(1, slabs):
+        @pl.when(z + r < slabs)
+        def _():
+            weight_copy(above[r - 1], z + r, up_sem.at[r - 1]).start()
+
+        @pl.when(z - r >= 0)
+        def _():
+            weight_copy(below[r - 1], z - r, down_sem.at[r - 1]).start()
+
+    x_copies = []
+    for r, x in enumerate((x0, x1, x2, x3)):
+        copy = pltpu.make_async_copy(x, x_all.at[r], x_sem.at[r])
+        copy.start()
+        x_copies.append(copy)
+    mine.wait()
+    for r in range(1, slabs):
+        @pl.when(z + r < slabs)
+        def _():
+            weight_copy(above[r - 1], z + r, up_sem.at[r - 1]).wait()
+
+        @pl.when(z - r >= 0)
+        def _():
+            weight_copy(below[r - 1], z - r, down_sem.at[r - 1]).wait()
+
+    for r in range(SLAB):
+        x_copies[r].wait()
+        block = q ^ r
+        source = x_all[r]
+        part = jnp.dot(source, w_all[0], preferred_element_type=jnp.float32)
+        squares[block, 0] = as_row(jnp.sum(part * part, axis=1, keepdims=True))
+        query[block] = part * q_gain[...]
+        part = jnp.dot(source, w_all[1], preferred_element_type=jnp.float32)
+        squares[block, 1] = as_row(jnp.sum(part * part, axis=1, keepdims=True))
+        keys[block] = (part * k_gain[...]).astype(jnp.bfloat16)
+        part = jnp.dot(source, w_all[2], preferred_element_type=jnp.float32)
+        values[block] = part.astype(jnp.bfloat16)
+
+
+def project(place, xs, own, above, below, q_gain, k_gain):
+    slabs = len(above) + 1
+    count, depth = xs[0].shape
+    width = own.shape[2]
+    f32, bf16 = jnp.float32, jnp.bfloat16
+    body = functools.partial(project_body, slabs)
+    return pl.pallas_call(
+        body,
+        out_shape=(
+            jax.ShapeDtypeStruct((SLAB, count, width), f32),
+            jax.ShapeDtypeStruct((SLAB, count, width), bf16),
+            jax.ShapeDtypeStruct((SLAB, count, width), bf16),
+            jax.ShapeDtypeStruct((SLAB, 2, 8, count), f32),
+        ),
+        in_specs=[SMEM] + [ANY] * (4 + 2 * slabs - 1) + [VMEM, VMEM],
+        out_specs=(VMEM, VMEM, VMEM, VMEM),
+        scratch_shapes=[
+            pltpu.VMEM((SLAB, count, depth), bf16),
+            pltpu.VMEM((3, depth, width), bf16),
+            pltpu.SemaphoreType.DMA((SLAB,)),
+            pltpu.SemaphoreType.DMA,
+            pltpu.SemaphoreType.DMA((slabs,)),
+            pltpu.SemaphoreType.DMA((slabs,)),
+        ],
+        compiler_params=pltpu.CompilerParams(vmem_limit_bytes=40 * 1024 * 1024),
+        cost_estimate=pl.CostEstimate(
+            flops=2 * SLAB * count * depth * 3 * width,
+            bytes_accessed=2 * depth * (SLAB * count + 3 * width),
+            transcendentals=0,
+        ),
+        name="project",
+    )(place, *xs, own, *above, *below, q_gain, k_gain)
+
+
+def project_body(slabs, *refs):
+    place, x0, x1, x2, x3, own = refs[:6]
+    above = refs[6:6 + slabs - 1]
+    below = refs[6 + slabs - 1:6 + 2 * (slabs - 1)]
+    rest = refs[6 + 2 * (slabs - 1):]
+    project_kernel(slabs, place, x0, x1, x2, x3, own, above, below, *rest)
+
+
+def attend_kernel(
+    full_width, place, query, keys, k_low, k_high, values, v_low, v_high, sums, seg,
+    o0, o1, o2, o3, k_all, v_all, sems,
+):
+    q = place[1]
+    count = query.shape[1]
+    half = k_low.shape[0]
+    own = SLAB * count
+    copies = []
+    for i, (src, dst, at, n) in enumerate((
+        (k_low, k_all, 0, half), (keys, k_all, half, own), (k_high, k_all, half + own, half),
+        (v_low, v_all, 0, half), (values, v_all, half, own), (v_high, v_all, half + own, half),
+    )):
+        copy = pltpu.make_async_copy(src, dst.at[pl.ds(at, n), :], sems.at[i])
+        copy.start()
+        copies.append(copy)
+    for copy in copies:
+        copy.wait()
+    window = count + 2 * half
+    heads = query.shape[2] // HEAD_DIM
+    for r, out in ((1, o1), (2, o2), (3, o3), (0, o0)):
+        block = q ^ r
+        start = pl.multiple_of(block * count, count)
+        at_query = pl.multiple_of(block * count + half, count)
+        key_seg = seg[:, pl.ds(start, window)]
+        query_seg = as_column(seg[:, pl.ds(at_query, count)])
+        k_scale = lax.rsqrt(sums[1:2, pl.ds(start, window)] / full_width + eps)
+        q_scale = lax.rsqrt(as_column(sums[0:1, pl.ds(at_query, count)]) / full_width + eps)
+        mask = jnp.tile(query_seg, (1, window // 128)) == key_seg
+        for h in range(heads):
+            cols = slice(h * HEAD_DIM, (h + 1) * HEAD_DIM)
+            q_low = (query[block, :, cols] * (q_scale * HEAD_DIM ** (-0.5))).astype(jnp.bfloat16)
+            scores = lax.dot_general(
+                q_low, k_all[pl.ds(start, window), cols], (((1,), (1,)), ((), ())),
+                preferred_element_type=jnp.float32,
+            )
+            scores = jnp.where(mask, scores * k_scale, floor_score)
+            peak = jnp.max(scores, axis=1, keepdims=True)
+            weights = jnp.exp(scores - peak)
+            total = jnp.sum(weights, axis=1, keepdims=True)
+            summed = jnp.dot(
+                weights.astype(jnp.bfloat16), v_all[pl.ds(start, window), cols],
+                preferred_element_type=jnp.float32,
+            )
+            out[:, cols] = (summed / total).astype(jnp.bfloat16)
+
+
+def attend(full_width, place, query, keys, k_low, k_high, values, v_low, v_high, sums, seg):
+    count, width = query.shape[1:]
+    half = k_low.shape[0]
+    ext = SLAB * count + 2 * half
+    bf16 = jnp.bfloat16
+    block = jax.ShapeDtypeStruct((count, width), bf16)
+    window = count + 2 * half
+    return pl.pallas_call(
+        functools.partial(attend_kernel, full_width),
+        out_shape=(block,) * 4,
+        in_specs=[SMEM, VMEM] + [ANY] * 6 + [VMEM, VMEM],
+        out_specs=(VMEM,) * 4,
+        scratch_shapes=[
+            pltpu.VMEM((ext, width), bf16),
+            pltpu.VMEM((ext, width), bf16),
+            pltpu.SemaphoreType.DMA((6,)),
+        ],
+        compiler_params=pltpu.CompilerParams(vmem_limit_bytes=40 * 1024 * 1024),
+        cost_estimate=pl.CostEstimate(
+            flops=4 * SLAB * count * window * width,
+            bytes_accessed=4 * ext * width + 4 * SLAB * count * width,
+            transcendentals=SLAB * count * window * width // HEAD_DIM,
+        ),
+        name="attend",
+    )(place, query, keys, k_low, k_high, values, v_low, v_high, sums, seg)
+
+
+def gather_blocks(place, blocks, c_all):
+    for r, c in enumerate(blocks):
+        c_all[place[1] ^ r] = c[...]
+
+
+def away_kernel(place, c0, c1, c2, c3, w, out, c_all, w_vmem, sem):
+    share = w_vmem.shape[0]
+    at = pl.multiple_of((1 - place[2]) * share, 32)
+    copy = pltpu.make_async_copy(w.at[pl.ds(at, share), :], w_vmem, sem)
+    copy.start()
+    gather_blocks(place, (c0, c1, c2, c3), c_all)
+    copy.wait()
+    out[...] = out_terms(c_all, w_vmem).astype(jnp.bfloat16)
+
+
+def out_terms(c_all, w_vmem):
+    width = c_all.shape[2]
+    total = None
+    for b in range(SLAB):
+        term = lax.dot_general(
+            w_vmem[:, b * width:(b + 1) * width], c_all[b], (((1,), (1,)), ((), ())),
+            preferred_element_type=jnp.float32,
+        )
+        total = term if total is None else total + term
+    return total
+
+
+def home_kernel(place, c0, c1, c2, c3, w, sent, residual, scale, out, c_all, w_vmem, sem):
+    share = w_vmem.shape[0]
+    at = pl.multiple_of(place[2] * share, 32)
+    copy = pltpu.make_async_copy(w.at[pl.ds(at, share), :], w_vmem, sem)
+    copy.start()
+    gather_blocks(place, (c0, c1, c2, c3), c_all)
+    copy.wait()
+    total = out_terms(c_all, w_vmem) + sent[...].astype(jnp.float32)
+    out[...] = (residual[...].astype(jnp.float32) + scale[...] * total).astype(jnp.bfloat16)
+
+
+def out_call(kernel, place, blocks, w, share, extra):
+    count, width = blocks[0].shape
+    return pl.pallas_call(
+        kernel,
+        out_shape=jax.ShapeDtypeStruct((share, count), jnp.bfloat16),
+        in_specs=[SMEM] + [VMEM] * 4 + [ANY] + [VMEM] * len(extra),
+        out_specs=VMEM,
+        scratch_shapes=[
+            pltpu.VMEM((SLAB, count, width), jnp.bfloat16),
+            pltpu.VMEM((share, SLAB * width), jnp.bfloat16),
+            pltpu.SemaphoreType.DMA,
+        ],
+        compiler_params=pltpu.CompilerParams(vmem_limit_bytes=40 * 1024 * 1024),
+        cost_estimate=pl.CostEstimate(
+            flops=2 * share * count * SLAB * width,
+            bytes_accessed=2 * share * SLAB * width,
+            transcendentals=0,
+        ),
+        name=kernel.__name__,
+    )(place, *blocks, w, *extra)
+
+
+def slab_plan(tokens, norm_gain, qkv_weight, q_gain, k_gain, out_weight, layer_scale, segment_ids):
+    count = tokens.shape[0]
+    seq, tp = lax.axis_index("seq"), lax.axis_index("tp")
+    slabs = lax.axis_size("seq") // SLAB
+    z, q = seq // SLAB, seq % SLAB
+    place = jnp.stack([z, q, tp]).astype(jnp.int32)
+    width = qkv_weight.shape[2] // SLAB
+    full_width = qkv_weight.shape[2] * lax.axis_size("tp")
+
+    by_kind = jnp.transpose(qkv_weight, (1, 0, 2))
+    cut = [lax.dynamic_slice_in_dim(by_kind, (q ^ r) * width, width, 2) for r in range(SLAB)]
+    got = [cut[0]] + [in_slab(cut[r], r) for r in range(1, SLAB)]
+    placed = []
+    for b in range(SLAB):
+        piece = got[b]
+        for other in range(1, SLAB):
+            piece = jnp.where(q == other, got[b ^ other], piece)
+        placed.append(piece)
+    own = jnp.concatenate(placed, axis=1)
+
+    source = tokens.astype(jnp.float32)
+    normed = (
+        source * lax.rsqrt(jnp.mean(source * source, axis=-1, keepdims=True) + eps) * norm_gain
+    ).astype(jnp.bfloat16)
+
+    above, below = [], []
+    down, up = own, own
+    xs = None
+    for r in range(1, slabs):
+        down, up = along_z(down, -1), along_z(up, 1)
+        above.append(down)
+        below.append(up)
+        if r == 1:
+            x2 = in_slab(normed, 2)
+            xs = (normed, in_slab(normed, 1), x2, in_slab(x2, 1))
+
+    gains = [lax.dynamic_slice_in_dim(g, q * width, width, 0)[None] for g in (q_gain, k_gain)]
+    query, keys, values, squares = project(place, xs, own, above, below, *gains)
+
+    tied = lax.optimization_barrier((out_weight, above[-1], below[-1]))[0]
+    all_out = jnp.transpose(lax.all_gather(tied, "seq", axis=1, tiled=True))
+
+    half = 2 * count
+    flat_keys, flat_values = keys.reshape(-1, width), values.reshape(-1, width)
+    k_low, v_low = along_z(flat_keys[-half:], 1), along_z(flat_values[-half:], 1)
+    k_high, v_high = along_z(flat_keys[:half], -1), along_z(flat_values[:half], -1)
+    sums = jnp.transpose(squares[:, :, 0], (1, 0, 2)).reshape(2, SLAB * count)
+    sums = sums + in_slab(sums, 1)
+    sums = sums + in_slab(sums, 2)
+    sums = sums + across(sums)
+    sums_low, sums_high = along_z(sums[:, -half:], 1), along_z(sums[:, :half], -1)
+    sums = jnp.concatenate([sums_low, sums, sums_high], axis=1)
+    outside = jnp.full((half,), -1, jnp.int32)
+    seg = jnp.concatenate([outside, segment_ids, outside], axis=0)
+    seg = lax.dynamic_slice_in_dim(seg, z * SLAB * count, SLAB * count + 2 * half, 0)
+    seg = seg.astype(jnp.float32)[None]
+    blocks = attend(
+        full_width, place, query, flat_keys, k_low, k_high, flat_values, v_low, v_high, sums, seg
+    )
+    blocks = [blocks[0]] + [in_slab(blocks[r], r) for r in range(1, SLAB)]
+
+    share = layer_scale.shape[0]
+    residual = jnp.transpose(lax.dynamic_slice_in_dim(tokens, tp * share, share, 1))
+    sent = across(out_call(away_kernel, place, blocks, all_out, share, ()))
+    mixed = out_call(
+        home_kernel, place, blocks, all_out, share, (sent, residual, layer_scale[:, None])
+    )
+    return jnp.transpose(mixed)
+
+
 def solution(mesh):
+    def shards(*args):
+        heads = args[2].shape[2] // HEAD_DIM
+        slab = mesh.shape["seq"] == 16 and mesh.shape["tp"] == 2 and heads % SLAB == 0
+        return (slab_plan if slab else row_plan)(*args)
+
     return jax.shard_map(
         shards,
         mesh=mesh,

time: 308 us -> 278 us (0.903)
  waiting for transfers between devices: 220 us -> 150 us
  starting transfers between devices: 12.5 us -> 58.4 us
  matrix products: 30.3 us -> 0 us
  Pallas kernels: 0 us -> 20.2 us
  local copies, waits for them, and re-layouts: 17.9 us -> 30.8 us
  other arithmetic: 8.39 us -> 2.49 us
  blocking collectives: 4.17 us -> 0 us
    all_gather x2 -> x1, waiting for transfers between devices: 101 us -> 0.01 us  [slab_plan(): all_out = jnp.transpose(lax.all_gather(tied, 'seq', axis=1, tiled=True))]
    ppermute x0 -> x13, waiting for transfers between devices: none -> 77.3 us  [the longest x11 61.1 us: in_slab(): return lax.ppermute(x, 'seq', [(i, i ^ flip) for i in range(size)])]
    reduce_scatter x1 -> x0, waiting for transfers between devices: 45.5 us -> none  [shards(): projected = lax.psum_scatter(terms, 'tp', scatter_dimension=1, tiled=True)]
    ppermute x0 -> x13, starting transfers between devices: none -> 26.5 us  [the longest x11 24.7 us: in_slab(): return lax.ppermute(x, 'seq', [(i, i ^ flip) for i in range(size)])]
    dot_general x3 -> x0, matrix products: 20.8 us -> none  [the longest x1 10.1 us: shards(): jnp.einsum('td,dch->tch', normed, lax.all_gather(qkv_weight, 'seq', axis=...]
    pallas_call x0 -> x4, Pallas kernels: none -> 20.2 us  [the longest x1 9.01 us: project(): pl.pallas_call(body, out_shape=(jax.ShapeDtypeStruct((SLAB, count, width)...]
    ppermute x4 -> x12, starting transfers between devices: 12.4 us -> 32 us  [passed_along(): return lax.ppermute(x, axis, pairs)]
    unnamed x29 -> x48, local copies, waits for them, and re-layouts: 12.9 us -> 24.2 us
  transfers between devices with their start and end apart: 7 -> 26, of which waited for: 4 -> 16; matrix products, arithmetic and copies ran while one was open for 14% -> 3% of each run, Pallas kernels for 0% -> 5%
where the time goes in v1:
time: 278 us; the launch traced here: 275 us
  waiting for transfers between devices  150 us (54%)
  starting transfers between devices  58.4 us (21%)
  local copies, waits for them, and re-layouts  30.8 us (11%)
  Pallas kernels  20.2 us (7%)
  between operations  13.8 us (5%)
    ppermute x12, waiting for transfers between devices, passed_along(): return lax.ppermute(x, axis, pairs)  72.5 us
    ppermute x11, waiting for transfers between devices, in_slab(): return lax.ppermute(x, 'seq', [(i, i ^ flip) for i in range(size)])  61.1 us
    ppermute x12, starting transfers between devices, passed_along(): return lax.ppermute(x, axis, pairs)  32 us
    ppermute x11, starting transfers between devices, in_slab(): return lax.ppermute(x, 'seq', [(i, i ^ flip) for i in range(size)])  24.7 us
    unnamed x48, local copies, waits for them, and re-layouts  24.2 us
    ppermute x2, waiting for transfers between devices, across(): return lax.ppermute(x, 'tp', [(0, 1), (1, 0)])  16.2 us
    pallas_call x1, Pallas kernels, project(): pl.pallas_call(body, out_shape=(jax.ShapeDtypeStruct((SLAB, count, width)...  9.01 us
    pallas_call x1, Pallas kernels, attend(): pl.pallas_call(functools.partial(attend_kernel, full_width), out_shape=(b...  6.1 us
  transfers between devices with their start and end apart: 26, of which 16 were waited for; matrix products, arithmetic and copies ran while one was open for 3% of the time, Pallas kernels for 5%

profile of v1, /device:TPU:9, one launch (start us, length us, event | category | flops | bytes accessed | tf_op | source)
XLA Modules:
  0.0 275.5 jit_solution(18034628148878440378)
XLA Ops:
  10.1 7.6 %collective-permute-done.3 = bf16[3,200,256]{2,1,0:T(8,128)(2,1)S(1)} collective-permute-done((bf16[3,200,256]{2,1,0:T(8,128)(2,1)S(1)}, bf16[3,200,256]{2,1,0:T(8,128)(2,1)S(1)}, u32[]{:S(2)}, u32[]{:S(2)}) %collective-permute-start.3) | collective-permute-done | bytes 307232 | tf_op jit(solution)/shard_map/ppermute | solution.py:101
  17.6 6.6 %collective-permute-done.4 = bf16[3,200,256]{2,1,0:T(8,128)(2,1)S(1)} collective-permute-done((bf16[3,200,256]{2,1,0:T(8,128)(2,1)S(1)}, bf16[3,200,256]{2,1,0:T(8,128)(2,1)S(1)}, u32[]{:S(2)}, u32[]{:S(2)}) %collective-permute-start.4) | collective-permute-done | bytes 307232 | tf_op jit(solution)/shard_map/ppermute | solution.py:101
  27.7 3.4 %collective-permute-start.9 = (bf16[3,800,256]{2,1,0:T(8,128)(2,1)S(1)}, bf16[3,800,256]{2,1,0:T(8,128)(2,1)S(1)}, u32[]{:S(2)}, u32[]{:S(2)}) collective-permute-start(bf16[3,800,256]{2,1,0:T(8,128)(2,1)S(1)} %pad_maximum_fusion.refs_5_), channel_id=1, source_target_pairs={{0,8},{2,10},{4,12},{6,14},{8,16},{10,18},{12,20},{14,22},{16,24},... | collective-permute-start | bytes 3686408 | tf_op jit(solution)/shard_map/ppermute | solution.py:20
  31.1 24.7 %collective-permute-done.6.refs_6_ = bf16[3,800,256]{2,1,0:T(8,128)(2,1)S(1)} collective-permute-done((bf16[3,800,256]{2,1,0:T(8,128)(2,1)S(1)}, bf16[3,800,256]{2,1,0:T(8,128)(2,1)S(1)}, u32[]{:S(2)}, u32[]{:S(2)}) %collective-permute-start.6) | collective-permute-done | bytes 1228832 | tf_op jit(solution)/shard_map/ppermute | solution.py:20
  59.2 3.0 %collective-permute-start.10 = (bf16[3,800,256]{2,1,0:T(8,128)(2,1)S(1)}, bf16[3,800,256]{2,1,0:T(8,128)(2,1)S(1)}, u32[]{:S(2)}, u32[]{:S(2)}) collective-permute-start(bf16[3,800,256]{2,1,0:T(8,128)(2,1)S(1)} %collective-permute-done.9.refs_9_), channel_id=1, source_target_pairs={{0,8},{2,10},{4,12},{6,14},{8,16},{10,18},{12,20},{14,22},{16,24},... | collective-permute-start | bytes 3686408 | tf_op jit(solution)/shard_map/ppermute | solution.py:20
  63.3 21.7 %collective-permute-done.7.refs_7_ = bf16[3,800,256]{2,1,0:T(8,128)(2,1)S(1)} collective-permute-done((bf16[3,800,256]{2,1,0:T(8,128)(2,1)S(1)}, bf16[3,800,256]{2,1,0:T(8,128)(2,1)S(1)}, u32[]{:S(2)}, u32[]{:S(2)}) %collective-permute-start.7) | collective-permute-done | bytes 1228832 | tf_op jit(solution)/shard_map/ppermute | solution.py:20
  88.6 2.7 collective-permute-start.11
  92.3 20.8 %collective-permute-done.8.refs_8_ = bf16[3,800,256]{2,1,0:T(8,128)(2,1)S(1)} collective-permute-done((bf16[3,800,256]{2,1,0:T(8,128)(2,1)S(1)}, bf16[3,800,256]{2,1,0:T(8,128)(2,1)S(1)}, u32[]{:S(2)}, u32[]{:S(2)}) %collective-permute-start.8) | collective-permute-done | bytes 1228832 | tf_op jit(solution)/shard_map/ppermute | solution.py:20
  114.2 2.6 collective-permute-done.11.refs_11_
  120.4 3.6 %collective-permute-start = (bf16[256,3200]{1,0:T(8,128)(2,1)S(1)}, bf16[256,3200]{1,0:T(8,128)(2,1)}, u32[]{:S(2)}, u32[]{:S(2)}) collective-permute-start(bf16[256,3200]{1,0:T(8,128)(2,1)S(1)} %fusion.2.refs_1_), channel_id=1, source_target_pairs={{0,2},{2,0},{4,6},{6,4},{8,10},{10,8},{12,14},{14,12},{16,18},{18,... | collective-permute-start | bytes 4915208 | tf_op jit(solution)/shard_map/ppermute | solution.py:101
  124.1 36.4 %collective-permute-done.1.refs_3_ = bf16[256,3200]{1,0:T(8,128)(2,1)} collective-permute-done((bf16[256,3200]{1,0:T(8,128)(2,1)S(1)}, bf16[256,3200]{1,0:T(8,128)(2,1)}, u32[]{:S(2)}, u32[]{:S(2)}) %collective-permute-start.1) | collective-permute-done | bytes 1638432 | tf_op jit(solution)/shard_map/ppermute | solution.py:101
  160.5 11.2 %collective-permute-start.2 = (bf16[256,3200]{1,0:T(8,128)(2,1)}, bf16[256,3200]{1,0:T(8,128)(2,1)}, u32[]{:S(2)}, u32[]{:S(2)}) collective-permute-start(bf16[256,3200]{1,0:T(8,128)(2,1)} %collective-permute-done.1.refs_3_), channel_id=1, source_target_pairs={{0,2},{2,0},{4,6},{6,4},{8,10},{10,8},{12,14},{14,12},{16,18},{18,... | collective-permute-start | bytes 4915208 | tf_op jit(solution)/shard_map/ppermute | solution.py:101
  183.0 9.0 %project.1 = (f32[4,256,256]{2,1,0:T(8,128)S(1)}, bf16[4,256,256]{2,1,0:T(8,128)(2,1)S(1)}, bf16[4,256,256]{2,1,0:T(8,128)(2,1)S(1)}, f32[4,2,8,256]{3,2,1,0:T(8,128)S(1)}) custom-call(s32[3]{0:T(128)S(1)} %pad_add_fusion.refs_0_.place, bf16[256,3200]{1,0:T(8,128)(2,1)S(1)} %fusion.2.refs_1_, bf16[256,3200]{1,0:T(8,128)(2,1)} %collective-permute-done.refs_2_, ...), custom_call_target="tpu_custom_call" | custom-call | flops 5033164800 | bytes 11468800 | tf_op jit(solution)/shard_map/project/pallas_call | solution.py:179
  203.3 3.4 %collective-permute-start.12 = (bf16[512,256]{1,0:T(8,128)(2,1)S(1)}, bf16[512,256]{1,0:T(8,128)(2,1)S(1)}, u32[]{:S(2)}, u32[]{:S(2)}) collective-permute-start(bf16[512,256]{1,0:T(8,128)(2,1)S(1)} %bitcast.52), channel_id=1, source_target_pairs={{0,8},{2,10},{4,12},{6,14},{8,16},{10,18},{12,20},{14,22},{16,24},... | collective-permute-start | bytes 786440 | tf_op jit(solution)/shard_map/ppermute | solution.py:20
  208.6 3.4 %collective-permute-start.14 = (bf16[512,256]{1,0:T(8,128)(2,1)S(1)}, bf16[512,256]{1,0:T(8,128)(2,1)S(1)}, u32[]{:S(2)}, u32[]{:S(2)}) collective-permute-start(bf16[512,256]{1,0:T(8,128)(2,1)S(1)} %bitcast.50), channel_id=1, source_target_pairs={{0,8},{2,10},{4,12},{6,14},{8,16},{10,18},{12,20},{14,22},{16,24},... | collective-permute-start | bytes 786440 | tf_op jit(solution)/shard_map/ppermute | solution.py:20
  213.9 3.5 %collective-permute-start.19 = (f32[2,512]{1,0:T(2,128)S(1)}, f32[2,512]{1,0:T(2,128)S(1)}, u32[]{:S(2)}, u32[]{:S(2)}) collective-permute-start(f32[2,512]{1,0:T(2,128)S(1)} %get-tuple-element.34), channel_id=1, source_target_pairs={{0,8},{2,10},{4,12},{6,14},{8,16},{10,18},{12,20},{14,22},{16,24},... | collective-permute-start | bytes 12296 | tf_op jit(solution)/shard_map/ppermute | solution.py:20
  220.2 6.1 %attend.1 = (bf16[256,256]{1,0:T(8,128)(2,1)S(1)}, bf16[256,256]{1,0:T(8,128)(2,1)S(1)}, bf16[256,256]{1,0:T(8,128)(2,1)S(1)}, bf16[256,256]{1,0:T(8,128)(2,1)S(1)}) custom-call(s32[3]{0:T(128)S(1)} %pad_add_fusion.refs_0_.place, f32[4,256,256]{2,1,0:T(8,128)S(1)} %copy-done.17, bf16[1024,256]{1,0:T(8,128)(2,1)S(1)} %bitcast.44, ...), custom_call_target="tpu_custom_call" | custom-call | flops 1342177280 | bytes 3145728 | tf_op jit(solution)/shard_map/attend/pallas_call | solution.py:269
  226.3 3.8 %collective-permute-start.21 = (bf16[256,256]{1,0:T(8,128)(2,1)S(1)}, bf16[256,256]{1,0:T(8,128)(2,1)S(1)}, u32[]{:S(2)}, u32[]{:S(2)}) collective-permute-start(bf16[256,256]{1,0:T(8,128)(2,1)S(1)} %get-tuple-element.19), channel_id=1, source_target_pairs={{0,2},{2,0},{4,6},{6,4},{8,10},{10,8},{12,14},{14,12},{16,18},{18,... | collective-permute-start | bytes 393224 | tf_op jit(solution)/shard_map/ppermute | solution.py:101
  231.8 3.4 %collective-permute-done.22.c2 = bf16[256,256]{1,0:T(8,128)(2,1)S(1)} collective-permute-done((bf16[256,256]{1,0:T(8,128)(2,1)S(1)}, bf16[256,256]{1,0:T(8,128)(2,1)S(1)}, u32[]{:S(2)}, u32[]{:S(2)}) %collective-permute-start.22) | collective-permute-done | bytes 131104 | tf_op jit(solution)/shard_map/ppermute | solution.py:101
  235.2 3.0 %collective-permute-done.23.c3 = bf16[256,256]{1,0:T(8,128)(2,1)S(1)} collective-permute-done((bf16[256,256]{1,0:T(8,128)(2,1)S(1)}, bf16[256,256]{1,0:T(8,128)(2,1)S(1)}, u32[]{:S(2)}, u32[]{:S(2)}) %collective-permute-start.23) | collective-permute-done | bytes 131104 | tf_op jit(solution)/shard_map/ppermute | solution.py:101
  238.2 2.9 %copy-done = bf16[1024,3200]{0,1:T(8,128)(2,1)S(1)} copy-done((bf16[1024,3200]{0,1:T(8,128)(2,1)S(1)}, bf16[1024,3200]{0,1:T(8,128)(2,1)}, u32[]{:S(2)}) %copy-start) | copy-done | bytes 6553624
  248.2 14.5 %collective-permute-done.24.sent = bf16[1600,256]{1,0:T(8,128)(2,1)S(1)} collective-permute-done((bf16[1600,256]{1,0:T(8,128)(2,1)S(1)}, bf16[1600,256]{1,0:T(8,128)(2,1)S(1)}, u32[]{:S(2)}, u32[]{:S(2)}) %collective-permute-start.24) | collective-permute-done | bytes 819232 | tf_op jit(solution)/shard_map/ppermute | solution.py:105
  262.7 2.9 %copy-done.1 = bf16[1024,3200]{0,1:T(8,128)(2,1)S(1)} copy-done((bf16[1024,3200]{0,1:T(8,128)(2,1)S(1)}, bf16[1024,3200]{0,1:T(8,128)(2,1)}, u32[]{:S(2)}) %copy-start.1) | copy-done | bytes 6553624
  265.6 3.0 %home_kernel.1 = bf16[1600,256]{1,0:T(8,128)(2,1)} custom-call(s32[3]{0:T(128)S(1)} %pad_add_fusion.refs_0_.place, bf16[256,256]{1,0:T(8,128)(2,1)S(1)} %get-tuple-element.18.c0, bf16[256,256]{1,0:T(8,128)(2,1)S(1)} %collective-permute-done.21.c1, bf16[256,256]{1,0:T(8,128)(2,1)S(1)} %collective-permute-done.22.c2, ...), custom_call_target="tpu_custom_call" | custom-call | flops 838860800 | bytes 3276800 | tf_op jit(solution)/shard_map/home_kernel/pallas_call | solution.py:329
  (101 shorter events, 58.6 us)
Async XLA Ops:
  6.5 231.6 %all-gather.2.cloned.1.call-start = ((), (), s32[]{:S(2)}) async-start(), calls=%async_computation | async-start | bytes 6963200 | tf_op jit(solution)/shard_map/all_gather | solution.py:389
  7.8 9.9 %collective-permute-start.3 = (bf16[3,200,256]{2,1,0:T(8,128)(2,1)S(1)}, bf16[3,200,256]{2,1,0:T(8,128)(2,1)S(1)}, u32[]{:S(2)}, u32[]{:S(2)}) collective-permute-start(bf16[3,200,256]{2,1,0:T(8,128)(2,1)S(1)} %get-tuple-element.27), channel_id=1, source_target_pairs={{0,6},{2,4},{4,2},{6,0},{8,14},{10,12},{12,10},{14,8},{16,22},{18,... | collective-permute-start | bytes 921608 | tf_op jit(solution)/shard_map/ppermute | solution.py:101
  9.6 14.6 %collective-permute-start.4 = (bf16[3,200,256]{2,1,0:T(8,128)(2,1)S(1)}, bf16[3,200,256]{2,1,0:T(8,128)(2,1)S(1)}, u32[]{:S(2)}, u32[]{:S(2)}) collective-permute-start(bf16[3,200,256]{2,1,0:T(8,128)(2,1)S(1)} %get-tuple-element.28), channel_id=1, source_target_pairs={{0,4},{2,6},{4,0},{6,2},{8,12},{10,14},{12,8},{14,10},{16,20},{18,... | collective-permute-start | bytes 921608 | tf_op jit(solution)/shard_map/ppermute | solution.py:101
  9.9 14.4 %collective-permute-start.5 = (bf16[3,200,256]{2,1,0:T(8,128)(2,1)S(1)}, bf16[3,200,256]{2,1,0:T(8,128)(2,1)S(1)}, u32[]{:S(2)}, u32[]{:S(2)}) collective-permute-start(bf16[3,200,256]{2,1,0:T(8,128)(2,1)S(1)} %get-tuple-element.29), channel_id=1, source_target_pairs={{0,2},{2,0},{4,6},{6,4},{8,10},{10,8},{12,14},{14,12},{16,18},{18,... | collective-permute-start | bytes 921608 | tf_op jit(solution)/shard_map/ppermute | solution.py:101
  25.7 30.2 %collective-permute-start.6 = (bf16[3,800,256]{2,1,0:T(8,128)(2,1)S(1)}, bf16[3,800,256]{2,1,0:T(8,128)(2,1)S(1)}, u32[]{:S(2)}, u32[]{:S(2)}) collective-permute-start(bf16[3,800,256]{2,1,0:T(8,128)(2,1)S(1)} %pad_maximum_fusion.refs_5_), channel_id=1, source_target_pairs={{8,0},{10,2},{12,4},{14,6},{16,8},{18,10},{20,12},{22,14},{24,16},... | collective-permute-start | bytes 3686408 | tf_op jit(solution)/shard_map/ppermute | solution.py:20
  27.7 31.5 %collective-permute-start.9 = (bf16[3,800,256]{2,1,0:T(8,128)(2,1)S(1)}, bf16[3,800,256]{2,1,0:T(8,128)(2,1)S(1)}, u32[]{:S(2)}, u32[]{:S(2)}) collective-permute-start(bf16[3,800,256]{2,1,0:T(8,128)(2,1)S(1)} %pad_maximum_fusion.refs_5_), channel_id=1, source_target_pairs={{0,8},{2,10},{4,12},{6,14},{8,16},{10,18},{12,20},{14,22},{16,24},... | collective-permute-start | bytes 3686408 | tf_op jit(solution)/shard_map/ppermute | solution.py:20
  55.8 29.1 %collective-permute-start.7 = (bf16[3,800,256]{2,1,0:T(8,128)(2,1)S(1)}, bf16[3,800,256]{2,1,0:T(8,128)(2,1)S(1)}, u32[]{:S(2)}, u32[]{:S(2)}) collective-permute-start(bf16[3,800,256]{2,1,0:T(8,128)(2,1)S(1)} %collective-permute-done.6.refs_6_), channel_id=1, source_target_pairs={{8,0},{10,2},{12,4},{14,6},{16,8},{18,10},{20,12},{22,14},{24,16},... | collective-permute-start | bytes 3686408 | tf_op jit(solution)/shard_map/ppermute | solution.py:20
  59.2 29.4 %collective-permute-start.10 = (bf16[3,800,256]{2,1,0:T(8,128)(2,1)S(1)}, bf16[3,800,256]{2,1,0:T(8,128)(2,1)S(1)}, u32[]{:S(2)}, u32[]{:S(2)}) collective-permute-start(bf16[3,800,256]{2,1,0:T(8,128)(2,1)S(1)} %collective-permute-done.9.refs_9_), channel_id=1, source_target_pairs={{0,8},{2,10},{4,12},{6,14},{8,16},{10,18},{12,20},{14,22},{16,24},... | collective-permute-start | bytes 3686408 | tf_op jit(solution)/shard_map/ppermute | solution.py:20
  85.0 28.2 %collective-permute-start.8 = (bf16[3,800,256]{2,1,0:T(8,128)(2,1)S(1)}, bf16[3,800,256]{2,1,0:T(8,128)(2,1)S(1)}, u32[]{:S(2)}, u32[]{:S(2)}) collective-permute-start(bf16[3,800,256]{2,1,0:T(8,128)(2,1)S(1)} %collective-permute-done.7.refs_7_), channel_id=1, source_target_pairs={{8,0},{10,2},{12,4},{14,6},{16,8},{18,10},{20,12},{22,14},{24,16},... | collective-permute-start | bytes 3686408 | tf_op jit(solution)/shard_map/ppermute | solution.py:20
  88.6 28.2 %collective-permute-start.11 = (bf16[3,800,256]{2,1,0:T(8,128)(2,1)S(1)}, bf16[3,800,256]{2,1,0:T(8,128)(2,1)S(1)}, u32[]{:S(2)}, u32[]{:S(2)}) collective-permute-start(bf16[3,800,256]{2,1,0:T(8,128)(2,1)S(1)} %collective-permute-done.10.refs_10_), channel_id=1, source_target_pairs={{0,8},{2,10},{4,12},{6,14},{8,16},{10,18},{12,20},{14,22},{16,24},... | collective-permute-start | bytes 3686408 | tf_op jit(solution)/shard_map/ppermute | solution.py:20
  119.8 40.7 %collective-permute-start.1 = (bf16[256,3200]{1,0:T(8,128)(2,1)S(1)}, bf16[256,3200]{1,0:T(8,128)(2,1)}, u32[]{:S(2)}, u32[]{:S(2)}) collective-permute-start(bf16[256,3200]{1,0:T(8,128)(2,1)S(1)} %fusion.2.refs_1_), channel_id=1, source_target_pairs={{0,4},{2,6},{4,0},{6,2},{8,12},{10,14},{12,8},{14,10},{16,20},{18,... | collective-permute-start | bytes 4915208 | tf_op jit(solution)/shard_map/ppermute | solution.py:101
  120.4 52.9 %collective-permute-start = (bf16[256,3200]{1,0:T(8,128)(2,1)S(1)}, bf16[256,3200]{1,0:T(8,128)(2,1)}, u32[]{:S(2)}, u32[]{:S(2)}) collective-permute-start(bf16[256,3200]{1,0:T(8,128)(2,1)S(1)} %fusion.2.refs_1_), channel_id=1, source_target_pairs={{0,2},{2,0},{4,6},{6,4},{8,10},{10,8},{12,14},{14,12},{16,18},{18,... | collective-permute-start | bytes 4915208 | tf_op jit(solution)/shard_map/ppermute | solution.py:101
  160.5 14.7 %collective-permute-start.2 = (bf16[256,3200]{1,0:T(8,128)(2,1)}, bf16[256,3200]{1,0:T(8,128)(2,1)}, u32[]{:S(2)}, u32[]{:S(2)}) collective-permute-start(bf16[256,3200]{1,0:T(8,128)(2,1)} %collective-permute-done.1.refs_3_), channel_id=1, source_target_pairs={{0,2},{2,0},{4,6},{6,4},{8,10},{10,8},{12,14},{14,12},{16,18},{18,... | collective-permute-start | bytes 4915208 | tf_op jit(solution)/shard_map/ppermute | solution.py:101
  197.7 2.5 collective-permute-start.18
  200.2 13.7 %collective-permute-start.20 = (f32[2,512]{1,0:T(2,128)S(1)}, f32[2,512]{1,0:T(2,128)S(1)}, u32[]{:S(2)}, u32[]{:S(2)}) collective-permute-start(f32[2,512]{1,0:T(2,128)S(1)} %get-tuple-element.35), channel_id=1, source_target_pairs={{8,0},{10,2},{12,4},{14,6},{16,8},{18,10},{20,12},{22,14},{24,16},... | collective-permute-start | bytes 12296 | tf_op jit(solution)/shard_map/ppermute | solution.py:20
  203.3 15.4 %collective-permute-start.12 = (bf16[512,256]{1,0:T(8,128)(2,1)S(1)}, bf16[512,256]{1,0:T(8,128)(2,1)S(1)}, u32[]{:S(2)}, u32[]{:S(2)}) collective-permute-start(bf16[512,256]{1,0:T(8,128)(2,1)S(1)} %bitcast.52), channel_id=1, source_target_pairs={{0,8},{2,10},{4,12},{6,14},{8,16},{10,18},{12,20},{14,22},{16,24},... | collective-permute-start | bytes 786440 | tf_op jit(solution)/shard_map/ppermute | solution.py:20
  206.6 12.0 %collective-permute-start.13 = (bf16[512,256]{1,0:T(8,128)(2,1)S(1)}, bf16[512,256]{1,0:T(8,128)(2,1)S(1)}, u32[]{:S(2)}, u32[]{:S(2)}) collective-permute-start(bf16[512,256]{1,0:T(8,128)(2,1)S(1)} %bitcast.51), channel_id=1, source_target_pairs={{8,0},{10,2},{12,4},{14,6},{16,8},{18,10},{20,12},{22,14},{24,16},... | collective-permute-start | bytes 786440 | tf_op jit(solution)/shard_map/ppermute | solution.py:20
  208.6 10.1 %collective-permute-start.14 = (bf16[512,256]{1,0:T(8,128)(2,1)S(1)}, bf16[512,256]{1,0:T(8,128)(2,1)S(1)}, u32[]{:S(2)}, u32[]{:S(2)}) collective-permute-start(bf16[512,256]{1,0:T(8,128)(2,1)S(1)} %bitcast.50), channel_id=1, source_target_pairs={{0,8},{2,10},{4,12},{6,14},{8,16},{10,18},{12,20},{14,22},{16,24},... | collective-permute-start | bytes 786440 | tf_op jit(solution)/shard_map/ppermute | solution.py:20
  211.9 8.3 %collective-permute-start.15 = (bf16[512,256]{1,0:T(8,128)(2,1)S(1)}, bf16[512,256]{1,0:T(8,128)(2,1)S(1)}, u32[]{:S(2)}, u32[]{:S(2)}) collective-permute-start(bf16[512,256]{1,0:T(8,128)(2,1)S(1)} %bitcast.49), channel_id=1, source_target_pairs={{8,0},{10,2},{12,4},{14,6},{16,8},{18,10},{20,12},{22,14},{24,16},... | collective-permute-start | bytes 786440 | tf_op jit(solution)/shard_map/ppermute | solution.py:20
  213.9 4.8 %collective-permute-start.19 = (f32[2,512]{1,0:T(2,128)S(1)}, f32[2,512]{1,0:T(2,128)S(1)}, u32[]{:S(2)}, u32[]{:S(2)}) collective-permute-start(f32[2,512]{1,0:T(2,128)S(1)} %get-tuple-element.34), channel_id=1, source_target_pairs={{0,8},{2,10},{4,12},{6,14},{8,16},{10,18},{12,20},{14,22},{16,24},... | collective-permute-start | bytes 12296 | tf_op jit(solution)/shard_map/ppermute | solution.py:20
  226.3 5.5 %collective-permute-start.21 = (bf16[256,256]{1,0:T(8,128)(2,1)S(1)}, bf16[256,256]{1,0:T(8,128)(2,1)S(1)}, u32[]{:S(2)}, u32[]{:S(2)}) collective-permute-start(bf16[256,256]{1,0:T(8,128)(2,1)S(1)} %get-tuple-element.19), channel_id=1, source_target_pairs={{0,2},{2,0},{4,6},{6,4},{8,10},{10,8},{12,14},{14,12},{16,18},{18,... | collective-permute-start | bytes 393224 | tf_op jit(solution)/shard_map/ppermute | solution.py:101
  230.1 5.1 %collective-permute-start.22 = (bf16[256,256]{1,0:T(8,128)(2,1)S(1)}, bf16[256,256]{1,0:T(8,128)(2,1)S(1)}, u32[]{:S(2)}, u32[]{:S(2)}) collective-permute-start(bf16[256,256]{1,0:T(8,128)(2,1)S(1)} %get-tuple-element.20), channel_id=1, source_target_pairs={{0,4},{2,6},{4,0},{6,2},{8,12},{10,14},{12,8},{14,10},{16,20},{18,... | collective-permute-start | bytes 393224 | tf_op jit(solution)/shard_map/ppermute | solution.py:101
  231.1 7.0 %collective-permute-start.23 = (bf16[256,256]{1,0:T(8,128)(2,1)S(1)}, bf16[256,256]{1,0:T(8,128)(2,1)S(1)}, u32[]{:S(2)}, u32[]{:S(2)}) collective-permute-start(bf16[256,256]{1,0:T(8,128)(2,1)S(1)} %get-tuple-element.21), channel_id=1, source_target_pairs={{0,6},{2,4},{4,2},{6,0},{8,14},{10,12},{12,10},{14,8},{16,22},{18,... | collective-permute-start | bytes 393224 | tf_op jit(solution)/shard_map/ppermute | solution.py:101
  243.0 19.7 %collective-permute-start.24 = (bf16[1600,256]{1,0:T(8,128)(2,1)S(1)}, bf16[1600,256]{1,0:T(8,128)(2,1)S(1)}, u32[]{:S(2)}, u32[]{:S(2)}) collective-permute-start(bf16[1600,256]{1,0:T(8,128)(2,1)S(1)} %away_kernel.1), channel_id=1, source_target_pairs={{0,1},{1,0},{2,3},{3,2},{4,5},{5,4},{6,7},{7,6},{8,9},{9,8},{10,11... | collective-permute-start | bytes 2457608 | tf_op jit(solution)/shard_map/ppermute | solution.py:105
  (25 other events, 292.1 us)
Sparse Core Ops, SparseCore 0:
  118.0 74.9 all-gather.1

commit v2 on v0

--- a/solution.py
+++ b/solution.py
@@ -1,10 +1,14 @@
+import functools
+
 import jax
 import jax.numpy as jnp
 from jax import lax
+from jax.experimental import pallas as pl
+from jax.experimental.pallas import tpu as pltpu
 from jax.sharding import PartitionSpec as P
 
 HEAD_DIM = 128
-
+SLAB = 4
 
 eps = 1e-06
 floor_score = -1e30
@@ -24,7 +28,7 @@
     return (jnp.where(mask, scores, floor_score), mask)
 
 
-def shards(tokens, norm_gain, qkv_weight, q_gain, k_gain, out_weight, layer_scale, segment_ids):
+def row_plan(tokens, norm_gain, qkv_weight, q_gain, k_gain, out_weight, layer_scale, segment_ids):
     count = tokens.shape[0]
     source = tokens.astype(jnp.float32)
     normed = (
@@ -87,7 +91,419 @@
     return (residual + layer_scale * projected).astype(jnp.bfloat16)
 
 
+ANY = pl.BlockSpec(memory_space=pl.ANY)
+VMEM = pl.BlockSpec(memory_space=pltpu.VMEM)
+SMEM = pl.BlockSpec(memory_space=pltpu.SMEM)
+MIB = 1024 * 1024
+
+
+def permuted(x, to):
+    slabs, tps = lax.axis_size("seq") // SLAB, lax.axis_size("tp")
+    pairs = []
+    for i in range(slabs * SLAB * tps):
+        z, q, y = to(i // (SLAB * tps), i // tps % SLAB, i % tps)
+        pairs.append((i, (z * SLAB + q) * tps + y))
+    return lax.ppermute(x, ("seq", "tp"), pairs)
+
+
+def in_slab(x, flip):
+    return permuted(x, lambda z, q, y: (z, q ^ flip, y))
+
+
+def across(x):
+    return permuted(x, lambda z, q, y: (z, q, 1 - y))
+
+
+def even_of(z):
+    return z ^ 1
+
+
+def odd_of(z):
+    return 3 - z if z in (1, 2) else z
+
+
+def even_pair(x, flip=0):
+    return permuted(x, lambda z, q, y: (even_of(z), q, y ^ flip))
+
+
+def odd_pair(x, flip=0):
+    return permuted(x, lambda z, q, y: (odd_of(z), q, y ^ flip))
+
+
+def tied(*arrays):
+    return lax.optimization_barrier(arrays)
+
+
+def as_row(column):
+    wide = jnp.broadcast_to(column, (column.shape[0], 128))
+    return jnp.transpose(wide)[:8]
+
+
+def as_column(row):
+    return jnp.transpose(jnp.broadcast_to(row, (128, row.shape[1])))
+
+
+def norm_kernel(place, tokens, gain, first, pair):
+    half, part = pair.shape[2], pair.shape[3]
+    for i in range(2):
+        at = pl.multiple_of((place[2] ^ i) * half, half)
+        source = tokens[pl.ds(at, half), :].astype(jnp.float32)
+        mean = jnp.mean(source * source, axis=1, keepdims=True)
+        normed = source * lax.rsqrt(mean + eps) * gain[...]
+        for j in range(pair.shape[1]):
+            chunk = normed[:, j * part:(j + 1) * part].astype(jnp.bfloat16)
+            pair[i, j] = chunk
+            if i == 0:
+                first[j] = chunk
+
+
+def norm(place, tokens, gain, slabs):
+    count, depth = tokens.shape
+    shape = (slabs, count // 2, depth // slabs)
+    return pl.pallas_call(
+        norm_kernel,
+        out_shape=(
+            jax.ShapeDtypeStruct(shape, jnp.bfloat16),
+            jax.ShapeDtypeStruct((2,) + shape, jnp.bfloat16),
+        ),
+        in_specs=[SMEM, VMEM, VMEM],
+        out_specs=(VMEM, VMEM),
+        compiler_params=pltpu.CompilerParams(vmem_limit_bytes=16 * MIB),
+        name="norm",
+    )(place, tokens, gain[None])
+
+
+def far_slabs(z):
+    return jnp.where(z < 2, 2, 1), jnp.where(z < 2, 3, 0)
+
+
+def pick(z, middle, end, out):
+    inner = (z == 1) | (z == 2)
+
+    @pl.when(inner)
+    def _():
+        out[...] = middle[...]
+
+    @pl.when(jnp.logical_not(inner))
+    def _():
+        out[...] = end[...]
+
+
+def token_chunk(xs, r, at):
+    if r < 2:
+        return jnp.concatenate([xs[r][0, at], xs[r][1, at]], axis=0)
+    return jnp.concatenate([xs[2 * r - 2][at], xs[2 * r - 1][at]], axis=0)
+
+
+def early_kernel(place, xa, xb, xc, xd, xe, xf, own, near, middle, end, acc, far):
+    z = place[0]
+    pick(z, middle, end, far)
+    xs = (xa, xb, xc, xd, xe, xf)
+    for r in range(SLAB):
+        lhs = [token_chunk(xs, r, at) for at in (z, z ^ 1, far_slabs(z)[0])]
+        for kind in range(3):
+            total = None
+            for x, w in zip(lhs, (own, near, far)):
+                term = jnp.dot(x, w[kind], preferred_element_type=jnp.float32)
+                total = term if total is None else total + term
+            acc[kind, r] = total
+
+
+def early(place, xs, own, near, middle, end):
+    kinds, rows, width = own.shape
+    count = 2 * xs[0].shape[2]
+    return pl.pallas_call(
+        early_kernel,
+        out_shape=jax.ShapeDtypeStruct((kinds, SLAB, count, width), jnp.float32),
+        in_specs=[SMEM] + [VMEM] * 10,
+        out_specs=VMEM,
+        scratch_shapes=[pltpu.VMEM((kinds, rows, width), jnp.bfloat16)],
+        compiler_params=pltpu.CompilerParams(vmem_limit_bytes=24 * MIB),
+        cost_estimate=pl.CostEstimate(
+            flops=6 * kinds * SLAB * count * rows * width,
+            bytes_accessed=8 * kinds * rows * width + 6 * SLAB * count * rows,
+            transcendentals=0,
+        ),
+        name="early",
+    )(place, *xs, own, near, middle, end)
+
+
+def late_kernel(
+    place, xa, xb, xc, xd, xe, xf, acc, middle, end, q_gain, k_gain,
+    query, keys, values, squares, even, odd, far,
+):
+    z, q, y = place[0], place[1], place[2]
+    pick(z, middle, end, far)
+    xs = (xa, xb, xc, xd, xe, xf)
+    count = acc.shape[2]
+    half = count // 2
+    for r in range(SLAB):
+        x = token_chunk(xs, r, far_slabs(z)[1])
+        for kind in range(3):
+            part = acc[kind, r] + jnp.dot(x, far[kind], preferred_element_type=jnp.float32)
+            if kind < 2:
+                summed = as_row(jnp.sum(part * part, axis=1, keepdims=True))
+                part = part * (q_gain, k_gain)[kind][...]
+            for i in range(2):
+                at = pl.multiple_of((q ^ r) * count + (y ^ i) * half, half)
+                rows = slice(i * half, (i + 1) * half)
+                if kind == 0:
+                    query[pl.ds(at, half), :] = part[rows]
+                else:
+                    low = part[rows].astype(jnp.bfloat16)
+                    (keys, values)[kind - 1][pl.ds(at, half), :] = low
+                if kind < 2:
+                    squares[kind:kind + 1, pl.ds(at, half)] = summed[:1, rows]
+    reach = even.shape[1]
+    for out, at in ((even, 1 - z % 2), (odd, z % 2)):
+        rows = pl.ds(pl.multiple_of(at * reach, reach), reach)
+        out[0] = keys[rows, :]
+        out[1] = values[rows, :]
+
+
+def late(place, xs, acc, middle, end, q_gain, k_gain):
+    kinds, rows, width = middle.shape
+    count = acc.shape[2]
+    slab = SLAB * count
+    f32, bf16 = jnp.float32, jnp.bfloat16
+    return pl.pallas_call(
+        late_kernel,
+        out_shape=(
+            jax.ShapeDtypeStruct((slab, width), f32),
+            jax.ShapeDtypeStruct((slab, width), bf16),
+            jax.ShapeDtypeStruct((slab, width), bf16),
+            jax.ShapeDtypeStruct((2, slab), f32),
+            jax.ShapeDtypeStruct((2, 2 * count, width), bf16),
+            jax.ShapeDtypeStruct((2, 2 * count, width), bf16),
+        ),
+        in_specs=[SMEM] + [VMEM] * 11,
+        out_specs=(VMEM,) * 6,
+        scratch_shapes=[pltpu.VMEM((kinds, rows, width), bf16)],
+        compiler_params=pltpu.CompilerParams(vmem_limit_bytes=24 * MIB),
+        cost_estimate=pl.CostEstimate(
+            flops=2 * kinds * slab * rows * width,
+            bytes_accessed=2 * kinds * rows * width + 2 * slab * rows,
+            transcendentals=0,
+        ),
+        name="late",
+    )(place, *xs, acc, middle, end, q_gain, k_gain)
+
+
+def attend_kernel(
+    full_width, place, query, keys, values, even, odd, mine, mine_y, e, e_y, o, o_y, seg,
+    o0, o1, o2, o3, k_all, v_all, scale_all,
+):
+    z, q = place[0], place[1]
+    slab = query.shape[0]
+    count = slab // SLAB
+    half = even.shape[1]
+    sums = mine[...] + mine_y[...]
+    scale_all[:, pl.ds(half, slab)] = lax.rsqrt(sums / full_width + eps)
+    k_all[pl.ds(half, slab), :] = keys[...]
+    v_all[pl.ds(half, slab), :] = values[...]
+    upper = half + slab
+
+    def put(kv, a, b, high):
+        at = upper if high else 0
+        part = slice(0, half) if high else slice(slab - half, slab)
+        k_all[pl.ds(at, half), :] = kv[0]
+        v_all[pl.ds(at, half), :] = kv[1]
+        scale_all[:, pl.ds(at, half)] = lax.rsqrt((a[:, part] + b[:, part]) / full_width + eps)
+
+    @pl.when(z % 2 == 0)
+    def _():
+        put(even, e, e_y, True)
+        put(odd, o, o_y, False)
+
+    @pl.when(z % 2 == 1)
+    def _():
+        put(even, e, e_y, False)
+        put(odd, o, o_y, True)
+
+    window = count + 2 * half
+    heads = query.shape[1] // HEAD_DIM
+    for r, out in ((1, o1), (2, o2), (3, o3), (0, o0)):
+        start = pl.multiple_of((q ^ r) * count, count)
+        at_query = pl.multiple_of((q ^ r) * count + half, count)
+        key_seg = seg[:, pl.ds(start, window)]
+        query_seg = as_column(seg[:, pl.ds(at_query, count)])
+        k_scale = scale_all[1:2, pl.ds(start, window)]
+        q_scale = as_column(scale_all[0:1, pl.ds(at_query, count)])
+        mask = jnp.tile(query_seg, (1, window // 128)) == key_seg
+        for h in range(heads):
+            cols = slice(h * HEAD_DIM, (h + 1) * HEAD_DIM)
+            q_low = query[pl.ds(start, count), cols] * (q_scale * HEAD_DIM ** (-0.5))
+            scores = lax.dot_general(
+                q_low.astype(jnp.bfloat16), k_all[pl.ds(start, window), cols],
+                (((1,), (1,)), ((), ())), preferred_element_type=jnp.float32,
+            )
+            scores = jnp.where(mask, scores * k_scale, floor_score)
+            peak = jnp.max(scores, axis=1, keepdims=True)
+            weights = jnp.exp(scores - peak)
+            total = jnp.sum(weights, axis=1, keepdims=True)
+            summed = jnp.dot(
+                weights.astype(jnp.bfloat16), v_all[pl.ds(start, window), cols],
+                preferred_element_type=jnp.float32,
+            )
+            out[:, cols] = (summed / total).astype(jnp.bfloat16)
+
+
+def attend(full_width, place, query, keys, values, even, odd, sums, seg):
+    slab, width = query.shape
+    half = even.shape[1]
+    count = slab // SLAB
+    ext = slab + 2 * half
+    bf16 = jnp.bfloat16
+    block = jax.ShapeDtypeStruct((count, width), bf16)
+    window = count + 2 * half
+    return pl.pallas_call(
+        functools.partial(attend_kernel, full_width),
+        out_shape=(block,) * 4,
+        in_specs=[SMEM] + [VMEM] * 12,
+        out_specs=(VMEM,) * 4,
+        scratch_shapes=[
+            pltpu.VMEM((ext, width), bf16),
+            pltpu.VMEM((ext, width), bf16),
+            pltpu.VMEM((2, ext), jnp.float32),
+        ],
+        compiler_params=pltpu.CompilerParams(vmem_limit_bytes=24 * MIB),
+        cost_estimate=pl.CostEstimate(
+            flops=4 * slab * window * width,
+            bytes_accessed=4 * ext * width + 4 * slab * width,
+            transcendentals=slab * window * width // HEAD_DIM,
+        ),
+        name="attend",
+    )(place, query, keys, values, even, odd, *sums, seg)
+
+
+def gather_blocks(place, blocks, c_all):
+    for r, c in enumerate(blocks):
+        c_all[place[1] ^ r] = c[...]
+
+
+def away_kernel(place, c0, c1, c2, c3, w, out, c_all, w_vmem, sem):
+    share = w_vmem.shape[0]
+    at = pl.multiple_of((1 - place[2]) * share, 32)
+    copy = pltpu.make_async_copy(w.at[pl.ds(at, share), :], w_vmem, sem)
+    copy.start()
+    gather_blocks(place, (c0, c1, c2, c3), c_all)
+    copy.wait()
+    out[...] = out_terms(c_all, w_vmem).astype(jnp.bfloat16)
+
+
+def out_terms(c_all, w_vmem):
+    width = c_all.shape[2]
+    total = None
+    for b in range(SLAB):
+        term = lax.dot_general(
+            w_vmem[:, b * width:(b + 1) * width], c_all[b], (((1,), (1,)), ((), ())),
+            preferred_element_type=jnp.float32,
+        )
+        total = term if total is None else total + term
+    return total
+
+
+def home_kernel(place, c0, c1, c2, c3, w, sent, residual, scale, out, c_all, w_vmem, sem):
+    share = w_vmem.shape[0]
+    at = pl.multiple_of(place[2] * share, 32)
+    copy = pltpu.make_async_copy(w.at[pl.ds(at, share), :], w_vmem, sem)
+    copy.start()
+    gather_blocks(place, (c0, c1, c2, c3), c_all)
+    copy.wait()
+    total = out_terms(c_all, w_vmem) + sent[...].astype(jnp.float32)
+    out[...] = (residual[...].astype(jnp.float32) + scale[...] * total).astype(jnp.bfloat16)
+
+
+def out_call(kernel, place, blocks, w, share, extra):
+    count, width = blocks[0].shape
+    return pl.pallas_call(
+        kernel,
+        out_shape=jax.ShapeDtypeStruct((share, count), jnp.bfloat16),
+        in_specs=[SMEM] + [VMEM] * 4 + [ANY] + [VMEM] * len(extra),
+        out_specs=VMEM,
+        scratch_shapes=[
+            pltpu.VMEM((SLAB, count, width), jnp.bfloat16),
+            pltpu.VMEM((share, SLAB * width), jnp.bfloat16),
+            pltpu.SemaphoreType.DMA,
+        ],
+        compiler_params=pltpu.CompilerParams(vmem_limit_bytes=24 * MIB),
+        cost_estimate=pl.CostEstimate(
+            flops=2 * share * count * SLAB * width,
+            bytes_accessed=2 * share * SLAB * width,
+            transcendentals=0,
+        ),
+        name=kernel.__name__,
+    )(place, *blocks, w, *extra)
+
+
+def slab_plan(tokens, norm_gain, qkv_weight, q_gain, k_gain, out_weight, layer_scale, segment_ids):
+    count = tokens.shape[0]
+    seq, tp = lax.axis_index("seq"), lax.axis_index("tp")
+    slabs = lax.axis_size("seq") // SLAB
+    z, q = seq // SLAB, seq % SLAB
+    place = jnp.stack([z, q, tp]).astype(jnp.int32)
+    width = qkv_weight.shape[2] // SLAB
+    full_width = qkv_weight.shape[2] * lax.axis_size("tp")
+
+    by_kind = jnp.transpose(qkv_weight, (1, 0, 2))
+    cut = [lax.dynamic_slice_in_dim(by_kind, (q ^ r) * width, width, 2) for r in range(SLAB)]
+    got = [cut[0]] + [in_slab(cut[r], r) for r in range(1, SLAB)]
+    placed = []
+    for b in range(SLAB):
+        piece = got[b]
+        for other in range(1, SLAB):
+            piece = jnp.where(q == other, got[b ^ other], piece)
+        placed.append(piece)
+    own = jnp.concatenate(placed, axis=1)
+    first, pair = norm(place, tokens, norm_gain, slabs)
+
+    own, first, pair = tied(own, first, pair)
+    near, middle1 = even_pair(own), odd_pair(own)
+    x2a = in_slab(first, 2)
+    near, middle1, x2a, pair = tied(near, middle1, x2a, pair)
+    end1, middle2 = even_pair(middle1), odd_pair(near)
+    x2b = across(x2a)
+    x1, x3a = in_slab(pair, 1), in_slab(x2a, 1)
+    end1, middle2, x2b, x1, x3a, out_weight = tied(end1, middle2, x2b, x1, x3a, out_weight)
+    end2 = even_pair(middle2)
+    x3b = in_slab(x2b, 1)
+    xs = (pair, x1, x2a, x2b, x3a, x3b)
+    acc = early(place, xs, own, near, middle1, end1)
+    all_out = jnp.transpose(lax.all_gather(out_weight, "seq", axis=1, tiled=True))
+
+    gains = [lax.dynamic_slice_in_dim(g, q * width, width, 0)[None] for g in (q_gain, k_gain)]
+    query, keys, values, squares, even, odd = late(place, xs, acc, middle2, end2, *gains)
+    even, odd = even_pair(even), odd_pair(odd)
+    slab_sum = squares
+    for r in range(1, SLAB):
+        slab_sum = slab_sum + in_slab(squares, r)
+    sums = (
+        slab_sum, across(slab_sum), even_pair(slab_sum), even_pair(slab_sum, 1),
+        odd_pair(slab_sum), odd_pair(slab_sum, 1),
+    )
+    half = 2 * count
+    outside = jnp.full((half,), -1, jnp.int32)
+    seg = jnp.concatenate([outside, segment_ids, outside], axis=0)
+    seg = lax.dynamic_slice_in_dim(seg, z * SLAB * count, SLAB * count + 2 * half, 0)
+    seg = seg.astype(jnp.float32)[None]
+    blocks = attend(full_width, place, query, keys, values, even, odd, sums, seg)
+    blocks = [blocks[0]] + [in_slab(blocks[r], r) for r in range(1, SLAB)]
+
+    share = layer_scale.shape[0]
+    residual = jnp.transpose(lax.dynamic_slice_in_dim(tokens, tp * share, share, 1))
+    sent = across(out_call(away_kernel, place, blocks, all_out, share, ()))
+    mixed = out_call(
+        home_kernel, place, blocks, all_out, share, (sent, residual, layer_scale[:, None])
+    )
+    return jnp.transpose(mixed)
+
+
 def solution(mesh):
+    def shards(*args):
+        heads = args[2].shape[2] // HEAD_DIM
+        slab = mesh.shape["seq"] == 16 and mesh.shape["tp"] == 2 and heads % SLAB == 0
+        return (slab_plan if slab else row_plan)(*args)
+
     return jax.shard_map(
         shards,
         mesh=mesh,

time: 308 us -> 242 us (0.79)
  waiting for transfers between devices: 220 us -> 116 us
  matrix products: 30.3 us -> 0 us
  starting transfers between devices: 12.5 us -> 39.8 us
  local copies, waits for them, and re-layouts: 17.9 us -> 42.8 us
  Pallas kernels: 0 us -> 24 us
  other arithmetic: 8.39 us -> 1.86 us
  blocking collectives: 4.17 us -> 0 us
    all_gather x2 -> x1, waiting for transfers between devices: 101 us -> 0.01 us  [slab_plan(): lax.all_gather(out_weight, 'seq', axis=1, tiled=True)]
    reduce_scatter x1 -> x0, waiting for transfers between devices: 45.5 us -> none  [shards(): projected = lax.psum_scatter(terms, 'tp', scatter_dimension=1, tiled=True)]
    ppermute x4 -> x27, waiting for transfers between devices: 71.8 us -> 116 us  [permuted(): return lax.ppermute(x, ('seq', 'tp'), pairs)]
    ppermute x4 -> x27, starting transfers between devices: 12.4 us -> 39.8 us  [permuted(): return lax.ppermute(x, ('seq', 'tp'), pairs)]
    pallas_call x0 -> x6, Pallas kernels: none -> 24 us  [the longest x1 6.77 us: early(): pl.pallas_call(early_kernel, out_shape=jax.ShapeDtypeStruct((kinds, SLAB,...]
    dot_general x3 -> x0, matrix products: 20.8 us -> none  [the longest x1 10.1 us: shards(): jnp.einsum('td,dch->tch', normed, lax.all_gather(qkv_weight, 'seq', axis=...]
    optimization_barrier x0 -> x6, local copies, waits for them, and re-layouts: none -> 13.9 us  [tied(): return lax.optimization_barrier(arrays)]
    sub x1 -> x0, matrix products: 9.5 us -> none  [shards(): weights = jnp.where(mask, jnp.exp(scores - peak), 0.0)]
  transfers between devices with their start and end apart: 7 -> 28, of which waited for: 4 -> 18; matrix products, arithmetic and copies ran while one was open for 14% -> 8% of each run, Pallas kernels for 0% -> 8%
where the time goes in v2:
time: 242 us; the launch traced here: 238 us
  waiting for transfers between devices  116 us (48%)
  local copies, waits for them, and re-layouts  42.8 us (18%)
  starting transfers between devices  39.8 us (16%)
  Pallas kernels  24 us (10%)
  between operations  13.6 us (6%)
    ppermute x27, waiting for transfers between devices, permuted(): return lax.ppermute(x, ('seq', 'tp'), pairs)  116 us
    ppermute x27, starting transfers between devices, permuted(): return lax.ppermute(x, ('seq', 'tp'), pairs)  39.8 us
    unnamed x53, local copies, waits for them, and re-layouts  21.4 us
    optimization_barrier x6, local copies, waits for them, and re-layouts, tied(): return lax.optimization_barrier(arrays)  13.9 us
    pallas_call x1, Pallas kernels, early(): pl.pallas_call(early_kernel, out_shape=jax.ShapeDtypeStruct((kinds, SLAB,...  6.77 us
    pallas_call x1, Pallas kernels, attend(): pl.pallas_call(functools.partial(attend_kernel, full_width), out_shape=(b...  6.18 us
    pallas_call x2, Pallas kernels, out_call(): pl.pallas_call(kernel, out_shape=jax.ShapeDtypeStruct((share, count), jnp...  5.02 us
  transfers between devices with their start and end apart: 28, of which 18 were waited for; matrix products, arithmetic and copies ran while one was open for 8% of the time, Pallas kernels for 8%

profile of v2, /device:TPU:9, one launch (start us, length us, event | category | flops | bytes accessed | tf_op | source)
XLA Modules:
  0.0 237.9 jit_solution(7218688864483774202)
XLA Ops:
  12.5 6.4 %collective-permute-done = bf16[3,200,256]{2,1,0:T(8,128)(2,1)} collective-permute-done((bf16[3,200,256]{2,1,0:T(8,128)(2,1)}, bf16[3,200,256]{2,1,0:T(8,128)(2,1)}, u32[]{:S(2)}, u32[]{:S(2)}) %collective-permute-start) | collective-permute-done | bytes 307232 | tf_op jit(solution)/shard_map/ppermute | solution.py:106
  18.9 6.6 %collective-permute-done.1 = bf16[3,200,256]{2,1,0:T(8,128)(2,1)} collective-permute-done((bf16[3,200,256]{2,1,0:T(8,128)(2,1)}, bf16[3,200,256]{2,1,0:T(8,128)(2,1)}, u32[]{:S(2)}, u32[]{:S(2)}) %collective-permute-start.1) | collective-permute-done | bytes 307232 | tf_op jit(solution)/shard_map/ppermute | solution.py:106
  27.3 4.5 %collective-permute-start.4 = (bf16[3,800,256]{2,1,0:T(8,128)(2,1)S(1)}, bf16[3,800,256]{2,1,0:T(8,128)(2,1)}, u32[]{:S(2)}, u32[]{:S(2)}) collective-permute-start(bf16[3,800,256]{2,1,0:T(8,128)(2,1)S(1)} %pad_maximum_fusion.own), channel_id=1, source_target_pairs={{0,0},{1,1},{2,2},{3,3},{4,4},{5,5},{6,6},{7,7},{8,16},{9,17},{10,... | collective-permute-start | bytes 3686408 | tf_op jit(solution)/shard_map/ppermute | solution.py:106
  35.2 17.8 %collective-permute-done.5 = bf16[4,128,800]{1,2,0:T(8,128)(2,1)S(1)} collective-permute-done((bf16[4,128,800]{1,2,0:T(8,128)(2,1)}, bf16[4,128,800]{1,2,0:T(8,128)(2,1)S(1)}, u32[]{:S(2)}, u32[]{:S(2)}) %collective-permute-start.5) | collective-permute-done | bytes 819232 | tf_op jit(solution)/shard_map/ppermute | solution.py:106
  55.5 3.0 %collective-permute-done.4.middle = bf16[3,800,256]{2,1,0:T(8,128)(2,1)} collective-permute-done((bf16[3,800,256]{2,1,0:T(8,128)(2,1)S(1)}, bf16[3,800,256]{2,1,0:T(8,128)(2,1)}, u32[]{:S(2)}, u32[]{:S(2)}) %collective-permute-start.4) | collective-permute-done | bytes 1228832 | tf_op jit(solution)/shard_map/ppermute | solution.py:106
  62.2 3.4 %collective-permute-start.7 = (bf16[3,800,256]{2,1,0:T(8,128)(2,1)}, bf16[3,800,256]{2,1,0:T(8,128)(2,1)}, u32[]{:S(2)}, u32[]{:S(2)}) collective-permute-start(bf16[3,800,256]{2,1,0:T(8,128)(2,1)} %collective-permute-done.3.near), channel_id=1, source_target_pairs={{0,0},{1,1},{2,2},{3,3},{4,4},{5,5},{6,6},{7,7},{8,16},{9,17},{10,... | collective-permute-start | bytes 3686408 | tf_op jit(solution)/shard_map/ppermute | solution.py:106
  68.1 17.7 %collective-permute-done.8 = bf16[4,128,800]{1,2,0:T(8,128)(2,1)} collective-permute-done((bf16[4,128,800]{1,2,0:T(8,128)(2,1)}, bf16[4,128,800]{1,2,0:T(8,128)(2,1)}, u32[]{:S(2)}, u32[]{:S(2)}) %collective-permute-start.8) | collective-permute-done | bytes 819232 | tf_op jit(solution)/shard_map/ppermute | solution.py:106
  85.8 5.3 %collective-permute-done.6.end = bf16[3,800,256]{2,1,0:T(8,128)(2,1)S(1)} collective-permute-done((bf16[3,800,256]{2,1,0:T(8,128)(2,1)}, bf16[3,800,256]{2,1,0:T(8,128)(2,1)S(1)}, u32[]{:S(2)}, u32[]{:S(2)}) %collective-permute-start.6) | collective-permute-done | bytes 1228832 | tf_op jit(solution)/shard_map/ppermute | solution.py:106
  93.0 2.9 %collective-permute-start.12 = (bf16[3,800,256]{2,1,0:T(8,128)(2,1)}, bf16[3,800,256]{2,1,0:T(8,128)(2,1)}, u32[]{:S(2)}, u32[]{:S(2)}) collective-permute-start(bf16[3,800,256]{2,1,0:T(8,128)(2,1)} %collective-permute-done.7.middle), channel_id=1, source_target_pairs={{0,8},{1,9},{2,10},{3,11},{4,12},{5,13},{6,14},{7,15},{8,0},{9,1},... | collective-permute-start | bytes 3686408 | tf_op jit(solution)/shard_map/ppermute | solution.py:106
  102.5 3.4 %copy.19.xb = bf16[2,4,128,800]{3,2,1,0:T(8,128)(2,1)} copy(bf16[2,4,128,800]{2,3,1,0:T(8,128)(2,1)} %collective-permute-done.9) | data formatting | bytes 3276800 | tf_op jit(solution)/shard_map/optimization_barrier | solution.py:134
  118.0 6.8 %early.1.acc = f32[3,4,256,256]{3,2,1,0:T(8,128)S(1)} custom-call(s32[3]{0:T(128)S(1)} %pad_add_fusion.place, bf16[2,4,128,800]{3,2,1,0:T(8,128)(2,1)S(1)} %get-tuple-element.35.xa, bf16[2,4,128,800]{3,2,1,0:T(8,128)(2,1)S(1)} %copy-done.2, bf16[4,128,800]{2,1,0:T(8,128)(2,1)S(1)} %copy.20.xc, bf16[4,128,800]{2,1,0:T(8,128)(2,1)S(1)} %copy-done.3, ...), custom_call_target="tpu_custom_call" | custom-call | flops 3774873600 | bytes 9830400 | tf_op jit(solution)/shard_map/early/pallas_call | solution.py:215
  124.8 11.0 %collective-permute-done.12.end = bf16[3,800,256]{2,1,0:T(8,128)(2,1)} collective-permute-done((bf16[3,800,256]{2,1,0:T(8,128)(2,1)}, bf16[3,800,256]{2,1,0:T(8,128)(2,1)}, u32[]{:S(2)}, u32[]{:S(2)}) %collective-permute-start.12) | collective-permute-done | bytes 1228832 | tf_op jit(solution)/shard_map/ppermute | solution.py:106
  135.7 4.6 %late.1 = (f32[1024,256]{1,0:T(8,128)S(1)}, bf16[1024,256]{1,0:T(8,128)(2,1)S(1)}, bf16[1024,256]{1,0:T(8,128)(2,1)S(1)}, f32[2,1024]{1,0:T(2,128)S(1)}, bf16[2,...) custom-call(s32[3]{0:T(128)S(1)} %pad_add_fusion.place, bf16[2,4,128,800]{3,2,1,0:T(8,128)(2,1)S(1)} %get-tuple-element.35.xa, ...), custom_call_target="tpu_custom_call" | custom-call | flops 1258291200 | bytes 2867200 | tf_op jit(solution)/shard_map/late/pallas_call | solution.py:269
  143.3 3.4 %collective-permute-start.14 = (bf16[2,512,256]{2,1,0:T(8,128)(2,1)}, bf16[2,512,256]{2,1,0:T(8,128)(2,1)S(1)}, u32[]{:S(2)}, u32[]{:S(2)}) collective-permute-start(bf16[2,512,256]{2,1,0:T(8,128)(2,1)} %get-tuple-element.48), channel_id=1, source_target_pairs={{0,0},{1,1},{2,2},{3,3},{4,4},{5,5},{6,6},{7,7},{8,16},{9,17},{10,... | collective-permute-start | bytes 1572872 | tf_op jit(solution)/shard_map/ppermute | solution.py:106
  146.7 2.6 %collective-permute-start.15 = (f32[2,1024]{1,0:T(2,128)S(1)}, f32[2,1024]{1,0:T(2,128)S(1)}, u32[]{:S(2)}, u32[]{:S(2)}) collective-permute-start(f32[2,1024]{1,0:T(2,128)S(1)} %get-tuple-element.49), channel_id=1, source_target_pairs={{0,2},{1,3},{2,0},{3,1},{4,6},{5,7},{6,4},{7,5},{8,10},{9,11},{10,... | collective-permute-start | bytes 24584 | tf_op jit(solution)/shard_map/ppermute | solution.py:106
  159.1 17.6 %collective-permute-done.19.e = f32[2,1024]{1,0:T(2,128)S(1)} collective-permute-done((f32[2,1024]{1,0:T(2,128)S(1)}, f32[2,1024]{1,0:T(2,128)S(1)}, u32[]{:S(2)}, u32[]{:S(2)}) %collective-permute-start.19) | collective-permute-done | bytes 8224 | tf_op jit(solution)/shard_map/ppermute | solution.py:106
  176.7 2.6 %collective-permute-start.22 = (f32[2,1024]{1,0:T(2,128)S(1)}, f32[2,1024]{1,0:T(2,128)S(1)}, u32[]{:S(2)}, u32[]{:S(2)}) collective-permute-start(f32[2,1024]{1,0:T(2,128)S(1)} %add_add_fusion.mine), channel_id=1, source_target_pairs={{0,1},{1,0},{2,3},{3,2},{4,5},{5,4},{6,7},{7,6},{8,17},{9,16},{10,... | collective-permute-start | bytes 24584 | tf_op jit(solution)/shard_map/ppermute | solution.py:106
  182.7 6.2 %attend.1 = (bf16[256,256]{1,0:T(8,128)(2,1)S(1)}, bf16[256,256]{1,0:T(8,128)(2,1)S(1)}, bf16[256,256]{1,0:T(8,128)(2,1)S(1)}, bf16[256,256]{1,0:T(8,128)(2,1)S(1)}) custom-call(s32[3]{0:T(128)S(1)} %pad_add_fusion.place, f32[1024,256]{1,0:T(8,128)S(1)} %copy-done.18, bf16[1024,256]{1,0:T(8,128)(2,1)S(1)} %get-tuple-element.45.keys, ...), custom_call_target="tpu_custom_call" | custom-call | flops 1342177280 | bytes 3145728 | tf_op jit(solution)/shard_map/attend/pallas_call | solution.py:359
  193.0 3.4 %collective-permute-done.24.c2 = bf16[256,256]{1,0:T(8,128)(2,1)S(1)} collective-permute-done((bf16[256,256]{1,0:T(8,128)(2,1)S(1)}, bf16[256,256]{1,0:T(8,128)(2,1)S(1)}, u32[]{:S(2)}, u32[]{:S(2)}) %collective-permute-start.24) | collective-permute-done | bytes 131104 | tf_op jit(solution)/shard_map/ppermute | solution.py:106
  196.3 3.0 %collective-permute-done.25.c3 = bf16[256,256]{1,0:T(8,128)(2,1)S(1)} collective-permute-done((bf16[256,256]{1,0:T(8,128)(2,1)S(1)}, bf16[256,256]{1,0:T(8,128)(2,1)S(1)}, u32[]{:S(2)}, u32[]{:S(2)}) %collective-permute-start.25) | collective-permute-done | bytes 131104 | tf_op jit(solution)/shard_map/ppermute | solution.py:106
  199.3 2.9 %copy-done = bf16[1024,3200]{0,1:T(8,128)(2,1)S(1)} copy-done((bf16[1024,3200]{0,1:T(8,128)(2,1)S(1)}, bf16[1024,3200]{0,1:T(8,128)(2,1)}, u32[]{:S(2)}) %copy-start) | copy-done | bytes 6553624
  209.8 15.3 %collective-permute-done.26.sent = bf16[1600,256]{1,0:T(8,128)(2,1)S(1)} collective-permute-done((bf16[1600,256]{1,0:T(8,128)(2,1)S(1)}, bf16[1600,256]{1,0:T(8,128)(2,1)S(1)}, u32[]{:S(2)}, u32[]{:S(2)}) %collective-permute-start.26) | collective-permute-done | bytes 819232 | tf_op jit(solution)/shard_map/ppermute | solution.py:106
  225.2 2.9 %copy-done.1 = bf16[1024,3200]{0,1:T(8,128)(2,1)S(1)} copy-done((bf16[1024,3200]{0,1:T(8,128)(2,1)S(1)}, bf16[1024,3200]{0,1:T(8,128)(2,1)}, u32[]{:S(2)}) %copy-start.1) | copy-done | bytes 6553624
  228.0 3.0 %home_kernel.1 = bf16[1600,256]{1,0:T(8,128)(2,1)} custom-call(s32[3]{0:T(128)S(1)} %pad_add_fusion.place, bf16[256,256]{1,0:T(8,128)(2,1)S(1)} %get-tuple-element.50.c0, bf16[256,256]{1,0:T(8,128)(2,1)S(1)} %collective-permute-done.23.c1, bf16[256,256]{1,0:T(8,128)(2,1)S(1)} %copy-done.14, bf16[256,256]{1,0:T(8,128)(2,1)S(1)} %copy-done.16, ...), custom_call_target="tpu_custom_call" | custom-call | flops 838860800 | bytes 3276800 | tf_op jit(solution)/shard_map/home_kernel/pallas_call | solution.py:419
  (111 shorter events, 68.2 us)
Async XLA Ops:
  6.5 192.8 %all-gather.2.cloned.1.call-start = ((), (), s32[]{:S(2)}) async-start(), calls=%async_computation | async-start | bytes 6963200 | tf_op jit(solution)/shard_map/all_gather | solution.py:472
  8.8 10.1 %collective-permute-start = (bf16[3,200,256]{2,1,0:T(8,128)(2,1)}, bf16[3,200,256]{2,1,0:T(8,128)(2,1)}, u32[]{:S(2)}, u32[]{:S(2)}) collective-permute-start(bf16[3,200,256]{2,1,0:T(8,128)(2,1)} %get-tuple-element.59), channel_id=1, source_target_pairs={{0,6},{1,7},{2,4},{3,5},{4,2},{5,3},{6,0},{7,1},{8,14},{9,15},{10,... | collective-permute-start | bytes 921608 | tf_op jit(solution)/shard_map/ppermute | solution.py:106
  10.5 14.9 %collective-permute-start.1 = (bf16[3,200,256]{2,1,0:T(8,128)(2,1)}, bf16[3,200,256]{2,1,0:T(8,128)(2,1)}, u32[]{:S(2)}, u32[]{:S(2)}) collective-permute-start(bf16[3,200,256]{2,1,0:T(8,128)(2,1)} %get-tuple-element.60), channel_id=1, source_target_pairs={{0,4},{1,5},{2,6},{3,7},{4,0},{5,1},{6,2},{7,3},{8,12},{9,13},{10,... | collective-permute-start | bytes 921608 | tf_op jit(solution)/shard_map/ppermute | solution.py:106
  10.8 14.7 %collective-permute-start.2 = (bf16[3,200,256]{2,1,0:T(8,128)(2,1)}, bf16[3,200,256]{2,1,0:T(8,128)(2,1)}, u32[]{:S(2)}, u32[]{:S(2)}) collective-permute-start(bf16[3,200,256]{2,1,0:T(8,128)(2,1)} %get-tuple-element.61), channel_id=1, source_target_pairs={{0,2},{1,3},{2,0},{3,1},{4,6},{5,7},{6,4},{7,5},{8,10},{9,11},{10,... | collective-permute-start | bytes 921608 | tf_op jit(solution)/shard_map/ppermute | solution.py:106
  27.2 28.3 %collective-permute-start.3 = (bf16[3,800,256]{2,1,0:T(8,128)(2,1)S(1)}, bf16[3,800,256]{2,1,0:T(8,128)(2,1)}, u32[]{:S(2)}, u32[]{:S(2)}) collective-permute-start(bf16[3,800,256]{2,1,0:T(8,128)(2,1)S(1)} %pad_maximum_fusion.own), channel_id=1, source_target_pairs={{0,8},{1,9},{2,10},{3,11},{4,12},{5,13},{6,14},{7,15},{8,0},{9,1},... | collective-permute-start | bytes 3686408 | tf_op jit(solution)/shard_map/ppermute | solution.py:106
  27.3 31.3 %collective-permute-start.4 = (bf16[3,800,256]{2,1,0:T(8,128)(2,1)S(1)}, bf16[3,800,256]{2,1,0:T(8,128)(2,1)}, u32[]{:S(2)}, u32[]{:S(2)}) collective-permute-start(bf16[3,800,256]{2,1,0:T(8,128)(2,1)S(1)} %pad_maximum_fusion.own), channel_id=1, source_target_pairs={{0,0},{1,1},{2,2},{3,3},{4,4},{5,5},{6,6},{7,7},{8,16},{9,17},{10,... | collective-permute-start | bytes 3686408 | tf_op jit(solution)/shard_map/ppermute | solution.py:106
  34.0 19.1 %collective-permute-start.5 = (bf16[4,128,800]{1,2,0:T(8,128)(2,1)}, bf16[4,128,800]{1,2,0:T(8,128)(2,1)S(1)}, u32[]{:S(2)}, u32[]{:S(2)}) collective-permute-start(bf16[4,128,800]{1,2,0:T(8,128)(2,1)} %copy.12), channel_id=1, source_target_pairs={{0,4},{1,5},{2,6},{3,7},{4,0},{5,1},{6,2},{7,3},{8,12},{9,13},{10,... | collective-permute-start | bytes 2457608 | tf_op jit(solution)/shard_map/ppermute | solution.py:106
  60.9 32.1 %collective-permute-start.9 = (bf16[2,4,128,800]{2,3,1,0:T(8,128)(2,1)}, bf16[2,4,128,800]{2,3,1,0:T(8,128)(2,1)}, u32[]{:S(2)}, u32[]{:S(2)}) collective-permute-start(bf16[2,4,128,800]{2,3,1,0:T(8,128)(2,1)} %copy.13), channel_id=1, source_target_pairs={{0,2},{1,3},{2,0},{3,1},{4,6},{5,7},{6,4},{7,5},{8,10},{9,11},{10,... | collective-permute-start | bytes 4915208 | tf_op jit(solution)/shard_map/ppermute | solution.py:106
  62.1 29.0 %collective-permute-start.6 = (bf16[3,800,256]{2,1,0:T(8,128)(2,1)}, bf16[3,800,256]{2,1,0:T(8,128)(2,1)S(1)}, u32[]{:S(2)}, u32[]{:S(2)}) collective-permute-start(bf16[3,800,256]{2,1,0:T(8,128)(2,1)} %collective-permute-done.4.middle), channel_id=1, source_target_pairs={{0,8},{1,9},{2,10},{3,11},{4,12},{5,13},{6,14},{7,15},{8,0},{9,1},... | collective-permute-start | bytes 3686408 | tf_op jit(solution)/shard_map/ppermute | solution.py:106
  62.2 30.8 %collective-permute-start.7 = (bf16[3,800,256]{2,1,0:T(8,128)(2,1)}, bf16[3,800,256]{2,1,0:T(8,128)(2,1)}, u32[]{:S(2)}, u32[]{:S(2)}) collective-permute-start(bf16[3,800,256]{2,1,0:T(8,128)(2,1)} %collective-permute-done.3.near), channel_id=1, source_target_pairs={{0,0},{1,1},{2,2},{3,3},{4,4},{5,5},{6,6},{7,7},{8,16},{9,17},{10,... | collective-permute-start | bytes 3686408 | tf_op jit(solution)/shard_map/ppermute | solution.py:106
  65.9 20.0 %collective-permute-start.8 = (bf16[4,128,800]{1,2,0:T(8,128)(2,1)}, bf16[4,128,800]{1,2,0:T(8,128)(2,1)}, u32[]{:S(2)}, u32[]{:S(2)}) collective-permute-start(bf16[4,128,800]{1,2,0:T(8,128)(2,1)} %copy-done.21), channel_id=1, source_target_pairs={{0,1},{1,0},{2,3},{3,2},{4,5},{5,4},{6,7},{7,6},{8,9},{9,8},{10,11... | collective-permute-start | bytes 2457608 | tf_op jit(solution)/shard_map/ppermute | solution.py:106
  93.0 42.7 %collective-permute-start.12 = (bf16[3,800,256]{2,1,0:T(8,128)(2,1)}, bf16[3,800,256]{2,1,0:T(8,128)(2,1)}, u32[]{:S(2)}, u32[]{:S(2)}) collective-permute-start(bf16[3,800,256]{2,1,0:T(8,128)(2,1)} %collective-permute-done.7.middle), channel_id=1, source_target_pairs={{0,8},{1,9},{2,10},{3,11},{4,12},{5,13},{6,14},{7,15},{8,0},{9,1},... | collective-permute-start | bytes 3686408 | tf_op jit(solution)/shard_map/ppermute | solution.py:106
  95.9 12.2 %collective-permute-start.11 = (bf16[4,128,800]{1,2,0:T(8,128)(2,1)}, bf16[4,128,800]{1,2,0:T(8,128)(2,1)}, u32[]{:S(2)}, u32[]{:S(2)}) collective-permute-start(bf16[4,128,800]{1,2,0:T(8,128)(2,1)} %collective-permute-done.8), channel_id=1, source_target_pairs={{0,2},{1,3},{2,0},{3,1},{4,6},{5,7},{6,4},{7,5},{8,10},{9,11},{10,... | collective-permute-start | bytes 2457608 | tf_op jit(solution)/shard_map/ppermute | solution.py:106
  142.2 38.2 %collective-permute-start.13 = (bf16[2,512,256]{2,1,0:T(8,128)(2,1)}, bf16[2,512,256]{2,1,0:T(8,128)(2,1)S(1)}, u32[]{:S(2)}, u32[]{:S(2)}) collective-permute-start(bf16[2,512,256]{2,1,0:T(8,128)(2,1)} %get-tuple-element.47), channel_id=1, source_target_pairs={{0,8},{1,9},{2,10},{3,11},{4,12},{5,13},{6,14},{7,15},{8,0},{9,1},... | collective-permute-start | bytes 1572872 | tf_op jit(solution)/shard_map/ppermute | solution.py:106
  143.3 37.0 %collective-permute-start.14 = (bf16[2,512,256]{2,1,0:T(8,128)(2,1)}, bf16[2,512,256]{2,1,0:T(8,128)(2,1)S(1)}, u32[]{:S(2)}, u32[]{:S(2)}) collective-permute-start(bf16[2,512,256]{2,1,0:T(8,128)(2,1)} %get-tuple-element.48), channel_id=1, source_target_pairs={{0,0},{1,1},{2,2},{3,3},{4,4},{5,5},{6,6},{7,7},{8,16},{9,17},{10,... | collective-permute-start | bytes 1572872 | tf_op jit(solution)/shard_map/ppermute | solution.py:106
  146.7 4.3 %collective-permute-start.15 = (f32[2,1024]{1,0:T(2,128)S(1)}, f32[2,1024]{1,0:T(2,128)S(1)}, u32[]{:S(2)}, u32[]{:S(2)}) collective-permute-start(f32[2,1024]{1,0:T(2,128)S(1)} %get-tuple-element.49), channel_id=1, source_target_pairs={{0,2},{1,3},{2,0},{3,1},{4,6},{5,7},{6,4},{7,5},{8,10},{9,11},{10,... | collective-permute-start | bytes 24584 | tf_op jit(solution)/shard_map/ppermute | solution.py:106
  155.5 21.2 %collective-permute-start.19 = (f32[2,1024]{1,0:T(2,128)S(1)}, f32[2,1024]{1,0:T(2,128)S(1)}, u32[]{:S(2)}, u32[]{:S(2)}) collective-permute-start(f32[2,1024]{1,0:T(2,128)S(1)} %add_add_fusion.mine), channel_id=1, source_target_pairs={{0,8},{1,9},{2,10},{3,11},{4,12},{5,13},{6,14},{7,15},{8,0},{9,1},... | collective-permute-start | bytes 24584 | tf_op jit(solution)/shard_map/ppermute | solution.py:106
  155.5 23.9 %collective-permute-start.20 = (f32[2,1024]{1,0:T(2,128)S(1)}, f32[2,1024]{1,0:T(2,128)S(1)}, u32[]{:S(2)}, u32[]{:S(2)}) collective-permute-start(f32[2,1024]{1,0:T(2,128)S(1)} %add_add_fusion.mine), channel_id=1, source_target_pairs={{0,9},{1,8},{2,11},{3,10},{4,13},{5,12},{6,15},{7,14},{8,1},{9,0},... | collective-permute-start | bytes 24584 | tf_op jit(solution)/shard_map/ppermute | solution.py:106
  157.2 22.2 %collective-permute-start.21 = (f32[2,1024]{1,0:T(2,128)S(1)}, f32[2,1024]{1,0:T(2,128)S(1)}, u32[]{:S(2)}, u32[]{:S(2)}) collective-permute-start(f32[2,1024]{1,0:T(2,128)S(1)} %add_add_fusion.mine), channel_id=1, source_target_pairs={{0,0},{1,1},{2,2},{3,3},{4,4},{5,5},{6,6},{7,7},{8,16},{9,17},{10,... | collective-permute-start | bytes 24584 | tf_op jit(solution)/shard_map/ppermute | solution.py:106
  176.7 3.7 %collective-permute-start.22 = (f32[2,1024]{1,0:T(2,128)S(1)}, f32[2,1024]{1,0:T(2,128)S(1)}, u32[]{:S(2)}, u32[]{:S(2)}) collective-permute-start(f32[2,1024]{1,0:T(2,128)S(1)} %add_add_fusion.mine), channel_id=1, source_target_pairs={{0,1},{1,0},{2,3},{3,2},{4,5},{5,4},{6,7},{7,6},{8,17},{9,16},{10,... | collective-permute-start | bytes 24584 | tf_op jit(solution)/shard_map/ppermute | solution.py:106
  188.9 4.1 %collective-permute-start.23 = (bf16[256,256]{1,0:T(8,128)(2,1)S(1)}, bf16[256,256]{1,0:T(8,128)(2,1)S(1)}, u32[]{:S(2)}, u32[]{:S(2)}) collective-permute-start(bf16[256,256]{1,0:T(8,128)(2,1)S(1)} %get-tuple-element.51), channel_id=1, source_target_pairs={{0,2},{1,3},{2,0},{3,1},{4,6},{5,7},{6,4},{7,5},{8,10},{9,11},{10,... | collective-permute-start | bytes 393224 | tf_op jit(solution)/shard_map/ppermute | solution.py:106
  191.3 5.1 %collective-permute-start.24 = (bf16[256,256]{1,0:T(8,128)(2,1)S(1)}, bf16[256,256]{1,0:T(8,128)(2,1)S(1)}, u32[]{:S(2)}, u32[]{:S(2)}) collective-permute-start(bf16[256,256]{1,0:T(8,128)(2,1)S(1)} %get-tuple-element.52), channel_id=1, source_target_pairs={{0,4},{1,5},{2,6},{3,7},{4,0},{5,1},{6,2},{7,3},{8,12},{9,13},{10,... | collective-permute-start | bytes 393224 | tf_op jit(solution)/shard_map/ppermute | solution.py:106
  192.5 6.8 %collective-permute-start.25 = (bf16[256,256]{1,0:T(8,128)(2,1)S(1)}, bf16[256,256]{1,0:T(8,128)(2,1)S(1)}, u32[]{:S(2)}, u32[]{:S(2)}) collective-permute-start(bf16[256,256]{1,0:T(8,128)(2,1)S(1)} %get-tuple-element.53), channel_id=1, source_target_pairs={{0,6},{1,7},{2,4},{3,5},{4,2},{5,3},{6,0},{7,1},{8,14},{9,15},{10,... | collective-permute-start | bytes 393224 | tf_op jit(solution)/shard_map/ppermute | solution.py:106
  205.5 19.6 %collective-permute-start.26 = (bf16[1600,256]{1,0:T(8,128)(2,1)S(1)}, bf16[1600,256]{1,0:T(8,128)(2,1)S(1)}, u32[]{:S(2)}, u32[]{:S(2)}) collective-permute-start(bf16[1600,256]{1,0:T(8,128)(2,1)S(1)} %away_kernel.1), channel_id=1, source_target_pairs={{0,1},{1,0},{2,3},{3,2},{4,5},{5,4},{6,7},{7,6},{8,9},{9,8},{10,11... | collective-permute-start | bytes 2457608 | tf_op jit(solution)/shard_map/ppermute | solution.py:106
  (30 other events, 200.1 us)
Sparse Core Ops, SparseCore 0:
  93.1 88.7 all-gather.1

commit v3 on v2

--- a/solution.py
+++ b/solution.py
@@ -94,6 +94,7 @@
 ANY = pl.BlockSpec(memory_space=pl.ANY)
 VMEM = pl.BlockSpec(memory_space=pltpu.VMEM)
 SMEM = pl.BlockSpec(memory_space=pltpu.SMEM)
+HBM = pl.BlockSpec(memory_space=pltpu.HBM)
 MIB = 1024 * 1024
 
 
@@ -144,7 +145,9 @@
 
 
 def norm_kernel(place, tokens, gain, first, pair):
-    half, part = pair.shape[2], pair.shape[3]
+    half = pair.shape[2]
+    part = tokens.shape[1] // pair.shape[1]
+    blank = jnp.zeros((half, pair.shape[3] - part), jnp.bfloat16)
     for i in range(2):
         at = pl.multiple_of((place[2] ^ i) * half, half)
         source = tokens[pl.ds(at, half), :].astype(jnp.float32)
@@ -152,14 +155,14 @@
         normed = source * lax.rsqrt(mean + eps) * gain[...]
         for j in range(pair.shape[1]):
             chunk = normed[:, j * part:(j + 1) * part].astype(jnp.bfloat16)
-            pair[i, j] = chunk
-            if i == 0:
-                first[j] = chunk
+            for out in (pair.at[i, j],) + ((first.at[j],) if i == 0 else ()):
+                out[:, :part] = chunk
+                out[:, part:] = blank
 
 
 def norm(place, tokens, gain, slabs):
     count, depth = tokens.shape
-    shape = (slabs, count // 2, depth // slabs)
+    shape = (slabs, count // 2, pl.cdiv(depth // slabs, 128) * 128)
     return pl.pallas_call(
         norm_kernel,
         out_shape=(
@@ -177,51 +180,80 @@
     return jnp.where(z < 2, 2, 1), jnp.where(z < 2, 3, 0)
 
 
-def pick(z, middle, end, out):
+def token_copies(xs, at, out, sems):
+    copies = []
+    for r in range(SLAB):
+        for i in range(2):
+            src = xs[r].at[i, at] if r < 2 else xs[2 * r - 2 + i].at[at]
+            copies.append(pltpu.make_async_copy(src, out.at[r, i], sems.at[r, i]))
+    for copy in copies:
+        copy.start()
+    return copies
+
+
+def picked_copy(z, middle, end, out, sem, wait):
     inner = (z == 1) | (z == 2)
 
     @pl.when(inner)
     def _():
-        out[...] = middle[...]
+        copy = pltpu.make_async_copy(middle, out, sem)
+        copy.wait() if wait else copy.start()
 
     @pl.when(jnp.logical_not(inner))
     def _():
-        out[...] = end[...]
-
-
-def token_chunk(xs, r, at):
-    if r < 2:
-        return jnp.concatenate([xs[r][0, at], xs[r][1, at]], axis=0)
-    return jnp.concatenate([xs[2 * r - 2][at], xs[2 * r - 1][at]], axis=0)
-
-
-def early_kernel(place, xa, xb, xc, xd, xe, xf, own, near, middle, end, acc, far):
+        copy = pltpu.make_async_copy(end, out, sem)
+        copy.wait() if wait else copy.start()
+
+
+def chunk_of(x_all, r, rows):
+    return x_all[r].reshape(-1, x_all.shape[-1])[:, :rows]
+
+
+def early_kernel(place, xa, xb, xc, xd, xe, xf, own, near, middle, end, acc, x_all, w_all, x_sem, w_sem):
     z = place[0]
-    pick(z, middle, end, far)
     xs = (xa, xb, xc, xd, xe, xf)
-    for r in range(SLAB):
-        lhs = [token_chunk(xs, r, at) for at in (z, z ^ 1, far_slabs(z)[0])]
-        for kind in range(3):
-            total = None
-            for x, w in zip(lhs, (own, near, far)):
-                term = jnp.dot(x, w[kind], preferred_element_type=jnp.float32)
-                total = term if total is None else total + term
-            acc[kind, r] = total
+    near_copy = pltpu.make_async_copy(near, w_all.at[1], w_sem.at[1])
+    own_copy = pltpu.make_async_copy(own, w_all.at[0], w_sem.at[0])
+    own_copy.start()
+    steps = (z, z ^ 1, far_slabs(z)[0])
+    x_copies = [token_copies(xs, steps[0], x_all.at[0], x_sem.at[0])]
+    near_copy.start()
+    x_copies.append(token_copies(xs, steps[1], x_all.at[1], x_sem.at[1]))
+    picked_copy(z, middle, end, w_all.at[2], w_sem.at[2], False)
+    x_copies.append(token_copies(xs, steps[2], x_all.at[2], x_sem.at[2]))
+    rows = own.shape[1]
+    for step in range(3):
+        if step < 2:
+            (own_copy, near_copy)[step].wait()
+        else:
+            picked_copy(z, middle, end, w_all.at[2], w_sem.at[2], True)
+        for copy in x_copies[step]:
+            copy.wait()
+        for r in range(SLAB):
+            x = chunk_of(x_all.at[step], r, rows)
+            for kind in range(own.shape[0]):
+                term = jnp.dot(x, w_all[step, kind], preferred_element_type=jnp.float32)
+                acc[kind, r] = term if step == 0 else acc[kind, r] + term
 
 
 def early(place, xs, own, near, middle, end):
     kinds, rows, width = own.shape
-    count = 2 * xs[0].shape[2]
+    half, wide = xs[0].shape[2:]
     return pl.pallas_call(
         early_kernel,
-        out_shape=jax.ShapeDtypeStruct((kinds, SLAB, count, width), jnp.float32),
-        in_specs=[SMEM] + [VMEM] * 10,
+        out_shape=jax.ShapeDtypeStruct((kinds, SLAB, 2 * half, width), jnp.float32),
+        in_specs=[SMEM] + [HBM] * 10,
         out_specs=VMEM,
-        scratch_shapes=[pltpu.VMEM((kinds, rows, width), jnp.bfloat16)],
+        scratch_shapes=[
+            pltpu.VMEM((3, SLAB, 2, half, wide), jnp.bfloat16),
+            pltpu.VMEM((3, kinds, rows, width), jnp.bfloat16),
+            pltpu.SemaphoreType.DMA((3, SLAB, 2)),
+            pltpu.SemaphoreType.DMA((3,)),
+        ],
         compiler_params=pltpu.CompilerParams(vmem_limit_bytes=24 * MIB),
         cost_estimate=pl.CostEstimate(
-            flops=6 * kinds * SLAB * count * rows * width,
-            bytes_accessed=8 * kinds * rows * width + 6 * SLAB * count * rows,
+            flops=12 * kinds * SLAB * half * rows * width,
+            bytes_accessed=6 * kinds * rows * width + 12 * SLAB * half * rows,
             transcendentals=0,
         ),
         name="early",
@@ -230,15 +262,18 @@
 
 def late_kernel(
     place, xa, xb, xc, xd, xe, xf, acc, middle, end, q_gain, k_gain,
-    query, keys, values, squares, even, odd, far,
+    query, keys, values, squares, even, odd, x_all, far, x_sem, w_sem,
 ):
     z, q, y = place[0], place[1], place[2]
-    pick(z, middle, end, far)
-    xs = (xa, xb, xc, xd, xe, xf)
+    picked_copy(z, middle, end, far, w_sem, False)
+    copies = token_copies((xa, xb, xc, xd, xe, xf), far_slabs(z)[1], x_all, x_sem)
     count = acc.shape[2]
     half = count // 2
+    picked_copy(z, middle, end, far, w_sem, True)
     for r in range(SLAB):
-        x = token_chunk(xs, r, far_slabs(z)[1])
+        copies[2 * r].wait()
+        copies[2 * r + 1].wait()
+        x = chunk_of(x_all, r, far.shape[1])
         for kind in range(3):
             part = acc[kind, r] + jnp.dot(x, far[kind], preferred_element_type=jnp.float32)
             if kind < 2:
@@ -276,9 +311,14 @@
             jax.ShapeDtypeStruct((2, 2 * count, width), bf16),
             jax.ShapeDtypeStruct((2, 2 * count, width), bf16),
         ),
-        in_specs=[SMEM] + [VMEM] * 11,
+        in_specs=[SMEM] + [HBM] * 6 + [VMEM] + [HBM] * 2 + [VMEM] * 2,
         out_specs=(VMEM,) * 6,
-        scratch_shapes=[pltpu.VMEM((kinds, rows, width), bf16)],
+        scratch_shapes=[
+            pltpu.VMEM((SLAB,) + xs[0].shape[:1] + xs[0].shape[2:], bf16),
+            pltpu.VMEM((kinds, rows, width), bf16),
+            pltpu.SemaphoreType.DMA((SLAB, 2)),
+            pltpu.SemaphoreType.DMA,
+        ],
         compiler_params=pltpu.CompilerParams(vmem_limit_bytes=24 * MIB),
         cost_estimate=pl.CostEstimate(
             flops=2 * kinds * slab * rows * width,
@@ -376,64 +416,63 @@
     )(place, query, keys, values, even, odd, *sums, seg)
 
 
-def gather_blocks(place, blocks, c_all):
-    for r, c in enumerate(blocks):
-        c_all[place[1] ^ r] = c[...]
-
-
-def away_kernel(place, c0, c1, c2, c3, w, out, c_all, w_vmem, sem):
-    share = w_vmem.shape[0]
-    at = pl.multiple_of((1 - place[2]) * share, 32)
-    copy = pltpu.make_async_copy(w.at[pl.ds(at, share), :], w_vmem, sem)
-    copy.start()
-    gather_blocks(place, (c0, c1, c2, c3), c_all)
-    copy.wait()
-    out[...] = out_terms(c_all, w_vmem).astype(jnp.bfloat16)
-
-
-def out_terms(c_all, w_vmem):
-    width = c_all.shape[2]
-    total = None
-    for b in range(SLAB):
-        term = lax.dot_general(
-            w_vmem[:, b * width:(b + 1) * width], c_all[b], (((1,), (1,)), ((), ())),
-            preferred_element_type=jnp.float32,
-        )
-        total = term if total is None else total + term
-    return total
-
-
-def home_kernel(place, c0, c1, c2, c3, w, sent, residual, scale, out, c_all, w_vmem, sem):
-    share = w_vmem.shape[0]
-    at = pl.multiple_of(place[2] * share, 32)
-    copy = pltpu.make_async_copy(w.at[pl.ds(at, share), :], w_vmem, sem)
-    copy.start()
-    gather_blocks(place, (c0, c1, c2, c3), c_all)
-    copy.wait()
-    total = out_terms(c_all, w_vmem) + sent[...].astype(jnp.float32)
-    out[...] = (residual[...].astype(jnp.float32) + scale[...] * total).astype(jnp.bfloat16)
-
-
-def out_call(kernel, place, blocks, w, share, extra):
+def out_kernel(
+    place, c00, c01, c10, c11, c20, c21, c30, c31, wa0, wa1, wb0, wb1, wc0, wc1, wd0, wd1,
+    residual, scale, out, c_all, w_all, total, sems,
+):
+    z, q, y = place[0], place[1], place[2]
+    copies = []
+    for r, pair in enumerate(((wa0, wa1), (wb0, wb1), (wc0, wc1), (wd0, wd1))):
+        for j in range(2):
+            copy = pltpu.make_async_copy(pair[j], w_all.at[r, j], sems.at[r, j])
+            copy.start()
+            copies.append(copy)
+    width = c00.shape[1]
+    for r, pair in enumerate(((c00, c01), (c10, c11), (c20, c21), (c30, c31))):
+        at = pl.multiple_of((q ^ r) * width, width)
+        for i in range(2):
+            c_all[i, :, pl.ds(at, width)] = pair[i][...]
+    rows = wa0.shape[1]
+    home = z // 2 == y
+    for r in range(SLAB):
+        for j in range(2):
+            copies[2 * r + j].wait()
+            slab = jnp.where(home, z ^ j, far_slabs(z)[j]) % 2
+            at = pl.multiple_of((slab * SLAB + (q ^ r)) * rows, 8)
+            term = None
+            for i in range(2):
+                part = lax.dot_general(
+                    w_all[r, j, i], c_all[i], (((1,), (1,)), ((), ())),
+                    preferred_element_type=jnp.float32,
+                )
+                term = part if term is None else term + part
+            total[pl.ds(at, rows), :] = term
+    out[...] = (residual[...].astype(jnp.float32) + scale[...] * total[...]).astype(jnp.bfloat16)
+
+
+def output(place, blocks, pieces, residual, scale):
     count, width = blocks[0].shape
+    rows, depth = pieces[0].shape[1:]
+    share = residual.shape[0]
     return pl.pallas_call(
-        kernel,
+        out_kernel,
         out_shape=jax.ShapeDtypeStruct((share, count), jnp.bfloat16),
-        in_specs=[SMEM] + [VMEM] * 4 + [ANY] + [VMEM] * len(extra),
+        in_specs=[SMEM] + [VMEM] * 8 + [HBM] * 8 + [VMEM] * 2,
         out_specs=VMEM,
         scratch_shapes=[
-            pltpu.VMEM((SLAB, count, width), jnp.bfloat16),
-            pltpu.VMEM((share, SLAB * width), jnp.bfloat16),
-            pltpu.SemaphoreType.DMA,
+            pltpu.VMEM((2, count, depth), jnp.bfloat16),
+            pltpu.VMEM((SLAB, 2, 2, rows, depth), jnp.bfloat16),
+            pltpu.VMEM((share, count), jnp.float32),
+            pltpu.SemaphoreType.DMA((SLAB, 2)),
         ],
         compiler_params=pltpu.CompilerParams(vmem_limit_bytes=24 * MIB),
         cost_estimate=pl.CostEstimate(
-            flops=2 * share * count * SLAB * width,
-            bytes_accessed=2 * share * SLAB * width,
+            flops=4 * share * count * depth,
+            bytes_accessed=4 * share * depth,
             transcendentals=0,
         ),
-        name=kernel.__name__,
-    )(place, *blocks, w, *extra)
+        name="output",
+    )(place, *blocks, *pieces, residual, scale)
 
 
 def slab_plan(tokens, norm_gain, qkv_weight, q_gain, k_gain, out_weight, layer_scale, segment_ids):
@@ -457,23 +496,43 @@
     own = jnp.concatenate(placed, axis=1)
     first, pair = norm(place, tokens, norm_gain, slabs)
 
-    own, first, pair = tied(own, first, pair)
+    out_own = jnp.transpose(out_weight)
+    out_near, out_mid1 = even_pair(out_own), odd_pair(out_own)
+    out_end1, out_mid2 = even_pair(out_mid1), odd_pair(out_near)
+    inner, home = (z == 1) | (z == 2), z // 2 == tp
+
+    def over_tp(close, far):
+        keep, give = jnp.where(home, close, far), jnp.where(home, far, close)
+        return keep, across(give)
+
+    own, first, pair, out_end1, out_mid2 = tied(own, first, pair, out_end1, out_mid2)
     near, middle1 = even_pair(own), odd_pair(own)
     x2a = in_slab(first, 2)
-    near, middle1, x2a, pair = tied(near, middle1, x2a, pair)
+    out_end2 = even_pair(out_mid2)
+    keep0, got0 = over_tp(out_own, jnp.where(inner, out_mid1, out_end1))
+    near, middle1, x2a, pair, out_end2, keep0, got0 = tied(
+        near, middle1, x2a, pair, out_end2, keep0, got0
+    )
     end1, middle2 = even_pair(middle1), odd_pair(near)
     x2b = across(x2a)
     x1, x3a = in_slab(pair, 1), in_slab(x2a, 1)
-    end1, middle2, x2b, x1, x3a, out_weight = tied(end1, middle2, x2b, x1, x3a, out_weight)
+    wa0 = jnp.stack([keep0, got0])
+    wc0 = in_slab(wa0, 2)
+    keep1, got1 = over_tp(out_near, jnp.where(inner, out_mid2, out_end2))
+    end1, middle2, x2b, x1, x3a, wa0, wc0, keep1, got1 = tied(
+        end1, middle2, x2b, x1, x3a, wa0, wc0, keep1, got1
+    )
     end2 = even_pair(middle2)
     x3b = in_slab(x2b, 1)
+    wa1 = jnp.stack([keep1, got1])
+    wc1 = in_slab(wa1, 2)
+    wb0, wd0 = in_slab(wa0, 1), in_slab(wc0, 1)
     xs = (pair, x1, x2a, x2b, x3a, x3b)
     acc = early(place, xs, own, near, middle1, end1)
-    all_out = jnp.transpose(lax.all_gather(out_weight, "seq", axis=1, tiled=True))
+    end2, acc, wc1 = tied(end2, acc, wc1)
 
     gains = [lax.dynamic_slice_in_dim(g, q * width, width, 0)[None] for g in (q_gain, k_gain)]
     query, keys, values, squares, even, odd = late(place, xs, acc, middle2, end2, *gains)
-    even, odd = even_pair(even), odd_pair(odd)
     slab_sum = squares
     for r in range(1, SLAB):
         slab_sum = slab_sum + in_slab(squares, r)
@@ -481,21 +540,24 @@
         slab_sum, across(slab_sum), even_pair(slab_sum), even_pair(slab_sum, 1),
         odd_pair(slab_sum), odd_pair(slab_sum, 1),
     )
+    even, odd = even_pair(even), odd_pair(odd)
+    wb1, wd1 = in_slab(wa1, 1), in_slab(wc1, 1)
     half = 2 * count
     outside = jnp.full((half,), -1, jnp.int32)
     seg = jnp.concatenate([outside, segment_ids, outside], axis=0)
     seg = lax.dynamic_slice_in_dim(seg, z * SLAB * count, SLAB * count + 2 * half, 0)
     seg = seg.astype(jnp.float32)[None]
     blocks = attend(full_width, place, query, keys, values, even, odd, sums, seg)
-    blocks = [blocks[0]] + [in_slab(blocks[r], r) for r in range(1, SLAB)]
+    spread = []
+    for r in range(SLAB):
+        for i in range(2):
+            to = functools.partial(lambda r, i, z, q, y: (z, q ^ r, y ^ i), r, i)
+            spread.append(permuted(blocks[r], to) if r or i else blocks[r])
+    pieces = (wa0, wa1, wb0, wb1, wc0, wc1, wd0, wd1)
 
     share = layer_scale.shape[0]
     residual = jnp.transpose(lax.dynamic_slice_in_dim(tokens, tp * share, share, 1))
-    sent = across(out_call(away_kernel, place, blocks, all_out, share, ()))
-    mixed = out_call(
-        home_kernel, place, blocks, all_out, share, (sent, residual, layer_scale[:, None])
-    )
-    return jnp.transpose(mixed)
+    return jnp.transpose(output(place, spread, pieces, residual, layer_scale[:, None]))
 
 
 def solution(mesh):

time: 242 us -> 229 us (0.946); the launches traced: 238 us -> 227 us
  starting transfers between devices: 39.8 us -> 67.8 us
  waiting for transfers between devices: 116 us -> 92 us
  local copies, waits for them, and re-layouts: 42.8 us -> 23.5 us
  Pallas kernels: 24 us -> 37.5 us
  between operations: 13.6 us -> 0.44 us
  other arithmetic: 1.86 us -> 6.11 us
    ppermute x27 -> x43, starting transfers between devices: 39.8 us -> 67.8 us  [permuted(): return lax.ppermute(x, ('seq', 'tp'), pairs)]
    ppermute x27 -> x43, waiting for transfers between devices: 116 us -> 92 us  [permuted(): return lax.ppermute(x, ('seq', 'tp'), pairs)]
    optimization_barrier x6 -> x0, local copies, waits for them, and re-layouts: 13.9 us -> none  [tied(): return lax.optimization_barrier(arrays)]
    pallas_call x1, Pallas kernels: 6.77 us -> 12.7 us  [early(): pl.pallas_call(early_kernel, out_shape=jax.ShapeDtypeStruct((kinds, SLAB,...]
    pallas_call x2 -> x1, Pallas kernels: 5.02 us -> 9.34 us  [output(): pl.pallas_call(out_kernel, out_shape=jax.ShapeDtypeStruct((share, count),...]
    unnamed x53 -> x59, local copies, waits for them, and re-layouts: 21.4 us -> 18.4 us
  transfers between devices with their start and end apart: 28 -> 43, of which waited for: 18 -> 21; matrix products, arithmetic and copies ran while one was open for 8% -> 6% of each run, Pallas kernels for 8% -> 9%
where the time goes in v3:
time: 229 us; the launch traced here: 227 us
  waiting for transfers between devices  92 us (40%)
  starting transfers between devices  67.8 us (30%)
  Pallas kernels  37.5 us (16%)
  local copies, waits for them, and re-layouts  23.5 us (10%)
  other arithmetic  6.11 us (3%)
    ppermute x43, waiting for transfers between devices, permuted(): return lax.ppermute(x, ('seq', 'tp'), pairs)  92 us
    ppermute x43, starting transfers between devices, permuted(): return lax.ppermute(x, ('seq', 'tp'), pairs)  67.8 us
    unnamed x59, local copies, waits for them, and re-layouts  18.4 us
    pallas_call x1, Pallas kernels, early(): pl.pallas_call(early_kernel, out_shape=jax.ShapeDtypeStruct((kinds, SLAB,...  12.7 us
    pallas_call x1, Pallas kernels, output(): pl.pallas_call(out_kernel, out_shape=jax.ShapeDtypeStruct((share, count),...  9.34 us
    pallas_call x1, Pallas kernels, late(): pl.pallas_call(late_kernel, out_shape=(jax.ShapeDtypeStruct((slab, width)...  6.75 us
    pallas_call x1, Pallas kernels, attend(): pl.pallas_call(functools.partial(attend_kernel, full_width), out_shape=(b...  6.71 us
  transfers between devices with their start and end apart: 43, of which 21 were waited for; matrix products, arithmetic and copies ran while one was open for 6% of the time, Pallas kernels for 9%

profile of v3, /device:TPU:9, one launch (start us, length us, event | category | flops | bytes accessed | tf_op | source)
XLA Modules:
  0.0 227.4 jit_solution(17972782740080072002)
XLA Ops:
  0.0 3.3 %collective-permute-start.3 = (bf16[200,1024]{1,0:T(8,128)(2,1)}, bf16[200,1024]{1,0:T(8,128)(2,1)}, u32[]{:S(2)}, u32[]{:S(2)}) collective-permute-start(bf16[200,1024]{1,0:T(8,128)(2,1)} %bitcast.42), channel_id=1, source_target_pairs={{0,0},{1,1},{2,2},{3,3},{4,4},{5,5},{6,6},{7,7},{8,16},{9,17},{10,... | collective-permute-start | bytes 1228808 | tf_op jit(solution)/shard_map/ppermute | solution.py:107
  13.7 5.3 %collective-permute-start.6 = (bf16[200,1024]{1,0:T(8,128)(2,1)}, bf16[200,1024]{1,0:T(8,128)(2,1)S(1)}, u32[]{:S(2)}, u32[]{:S(2)}) collective-permute-start(bf16[200,1024]{1,0:T(8,128)(2,1)} %collective-permute-done.5), channel_id=1, source_target_pairs={{0,0},{1,1},{2,2},{3,3},{4,4},{5,5},{6,6},{7,7},{8,16},{9,17},{10,... | collective-permute-start | bytes 1228808 | tf_op jit(solution)/shard_map/ppermute | solution.py:107
  19.0 4.0 %collective-permute-done.1 = bf16[3,200,256]{2,1,0:T(8,128)(2,1)} collective-permute-done((bf16[3,200,256]{2,1,0:T(8,128)(2,1)}, bf16[3,200,256]{2,1,0:T(8,128)(2,1)}, u32[]{:S(2)}, u32[]{:S(2)}) %collective-permute-start.1) | collective-permute-done | bytes 307232 | tf_op jit(solution)/shard_map/ppermute | solution.py:107
  28.0 3.2 %collective-permute-start.8 = (bf16[3,800,256]{2,1,0:T(8,128)(2,1)S(1)}, bf16[3,800,256]{2,1,0:T(8,128)(2,1)}, u32[]{:S(2)}, u32[]{:S(2)}) collective-permute-start(bf16[3,800,256]{2,1,0:T(8,128)(2,1)S(1)} %pad_maximum_fusion.own), channel_id=1, source_target_pairs={{0,0},{1,1},{2,2},{3,3},{4,4},{5,5},{6,6},{7,7},{8,16},{9,17},{10,... | collective-permute-start | bytes 3686408 | tf_op jit(solution)/shard_map/ppermute | solution.py:107
  34.7 6.4 %collective-permute-done.11 = bf16[200,1024]{1,0:T(8,128)(2,1)S(1)} collective-permute-done((bf16[200,1024]{1,0:T(8,128)(2,1)S(1)}, bf16[200,1024]{1,0:T(8,128)(2,1)S(1)}, u32[]{:S(2)}, u32[]{:S(2)}) %collective-permute-start.11) | collective-permute-done | bytes 409632 | tf_op jit(solution)/shard_map/ppermute | solution.py:107
  41.1 21.8 %collective-permute-done.10 = bf16[200,1024]{1,0:T(8,128)(2,1)S(1)} collective-permute-done((bf16[200,1024]{1,0:T(8,128)(2,1)S(1)}, bf16[200,1024]{1,0:T(8,128)(2,1)S(1)}, u32[]{:S(2)}, u32[]{:S(2)}) %collective-permute-start.10) | collective-permute-done | bytes 409632 | tf_op jit(solution)/shard_map/ppermute | solution.py:107
  62.9 3.4 %collective-permute-start.15 = (bf16[2,4,128,896]{3,2,1,0:T(8,128)(2,1)S(1)}, bf16[2,4,128,896]{3,2,1,0:T(8,128)(2,1)S(1)}, u32[]{:S(2)}, u32[]{:S(2)}) collective-permute-start(bf16[2,4,128,896]{3,2,1,0:T(8,128)(2,1)S(1)} %get-tuple-element.48.xa), channel_id=1, source_target_pairs={{0,2},{1,3},{2,0},{3,1},{4,6},{5,7},{6,4},{7,5},{8,10},{9,11},{10,... | collective-permute-start | bytes 5505032 | tf_op jit(solution)/shard_map/ppermute | solution.py:107
  70.8 3.1 %collective-permute-start.13 = (bf16[3,800,256]{2,1,0:T(8,128)(2,1)}, bf16[3,800,256]{2,1,0:T(8,128)(2,1)S(1)}, u32[]{:S(2)}, u32[]{:S(2)}) collective-permute-start(bf16[3,800,256]{2,1,0:T(8,128)(2,1)} %collective-permute-done.7.near), channel_id=1, source_target_pairs={{0,0},{1,1},{2,2},{3,3},{4,4},{5,5},{6,6},{7,7},{8,16},{9,17},{10,... | collective-permute-start | bytes 3686408 | tf_op jit(solution)/shard_map/ppermute | solution.py:107
  73.9 6.6 %collective-permute-done.18 = bf16[200,1024]{1,0:T(8,128)(2,1)S(1)} collective-permute-done((bf16[200,1024]{1,0:T(8,128)(2,1)S(1)}, bf16[200,1024]{1,0:T(8,128)(2,1)S(1)}, u32[]{:S(2)}, u32[]{:S(2)}) %collective-permute-start.18) | collective-permute-done | bytes 409632 | tf_op jit(solution)/shard_map/ppermute | solution.py:107
  81.6 5.8 %collective-permute-done.17.wc0 = bf16[2,200,1024]{2,1,0:T(8,128)(2,1)} collective-permute-done((bf16[2,200,1024]{2,1,0:T(8,128)(2,1)}, bf16[2,200,1024]{2,1,0:T(8,128)(2,1)}, u32[]{:S(2)}, u32[]{:S(2)}) %collective-permute-start.17) | collective-permute-done | bytes 819232 | tf_op jit(solution)/shard_map/ppermute | solution.py:107
  88.3 13.2 %collective-permute-done.14.xd = bf16[4,128,896]{2,1,0:T(8,128)(2,1)S(1)} collective-permute-done((bf16[4,128,896]{2,1,0:T(8,128)(2,1)}, bf16[4,128,896]{2,1,0:T(8,128)(2,1)S(1)}, u32[]{:S(2)}, u32[]{:S(2)}) %collective-permute-start.14) | collective-permute-done | bytes 917536 | tf_op jit(solution)/shard_map/ppermute | solution.py:107
  106.4 12.7 %early.1.acc = f32[3,4,256,256]{3,2,1,0:T(8,128)S(1)} custom-call(s32[3]{0:T(128)S(1)} %pad_add_fusion.place, bf16[2,4,128,896]{3,2,1,0:T(8,128)(2,1)S(1)} %get-tuple-element.48.xa, bf16[2,4,128,896]{3,2,1,0:T(8,128)(2,1)S(1)} %collective-permute-done.15.xb, bf16[4,128,896]{2,1,0:T(8,128)(2,1)} %collective-permute-done.9.xc, ...), custom_call_target="tpu_custom_call" | custom-call | flops 3774873600 | bytes 8601600 | tf_op jit(solution)/shard_map/early/pallas_call | solution.py:242
  119.1 5.2 %collective-permute-done.21.wc1 = bf16[2,200,1024]{2,1,0:T(8,128)(2,1)} collective-permute-done((bf16[2,200,1024]{2,1,0:T(8,128)(2,1)}, bf16[2,200,1024]{2,1,0:T(8,128)(2,1)}, u32[]{:S(2)}, u32[]{:S(2)}) %collective-permute-start.21) | collective-permute-done | bytes 819232 | tf_op jit(solution)/shard_map/ppermute | solution.py:107
  124.3 7.8 %collective-permute-done.20.end = bf16[3,800,256]{2,1,0:T(8,128)(2,1)S(1)} collective-permute-done((bf16[3,800,256]{2,1,0:T(8,128)(2,1)S(1)}, bf16[3,800,256]{2,1,0:T(8,128)(2,1)S(1)}, u32[]{:S(2)}, u32[]{:S(2)}) %collective-permute-start.20) | collective-permute-done | bytes 1228832 | tf_op jit(solution)/shard_map/ppermute | solution.py:107
  132.1 6.8 %late.1 = (f32[1024,256]{1,0:T(8,128)S(1)}, bf16[1024,256]{1,0:T(8,128)(2,1)S(1)}, bf16[1024,256]{1,0:T(8,128)(2,1)S(1)}, f32[2,1024]{1,0:T(2,128)S(1)}, bf16[2,...) custom-call(s32[3]{0:T(128)S(1)} %pad_add_fusion.place, bf16[2,4,128,896]{3,2,1,0:T(8,128)(2,1)S(1)} %get-tuple-element.48.xa, ...), custom_call_target="tpu_custom_call" | custom-call | flops 1258291200 | bytes 2867200 | tf_op jit(solution)/shard_map/late/pallas_call | solution.py:304
  150.7 3.5 %collective-permute-done.28.e = f32[2,1024]{1,0:T(2,128)S(1)} collective-permute-done((f32[2,1024]{1,0:T(2,128)S(1)}, f32[2,1024]{1,0:T(2,128)S(1)}, u32[]{:S(2)}, u32[]{:S(2)}) %collective-permute-start.28) | collective-permute-done | bytes 8224 | tf_op jit(solution)/shard_map/ppermute | solution.py:107
  158.8 3.1 %collective-permute-start.30 = (f32[2,1024]{1,0:T(2,128)S(1)}, f32[2,1024]{1,0:T(2,128)S(1)}, u32[]{:S(2)}, u32[]{:S(2)}) collective-permute-start(f32[2,1024]{1,0:T(2,128)S(1)} %add_add_fusion.mine), channel_id=1, source_target_pairs={{0,0},{1,1},{2,2},{3,3},{4,4},{5,5},{6,6},{7,7},{8,16},{9,17},{10,... | collective-permute-start | bytes 24584 | tf_op jit(solution)/shard_map/ppermute | solution.py:107
  167.8 3.1 %collective-permute-start.23 = (bf16[2,512,256]{2,1,0:T(8,128)(2,1)}, bf16[2,512,256]{2,1,0:T(8,128)(2,1)S(1)}, u32[]{:S(2)}, u32[]{:S(2)}) collective-permute-start(bf16[2,512,256]{2,1,0:T(8,128)(2,1)} %get-tuple-element.68), channel_id=1, source_target_pairs={{0,0},{1,1},{2,2},{3,3},{4,4},{5,5},{6,6},{7,7},{8,16},{9,17},{10,... | collective-permute-start | bytes 1572872 | tf_op jit(solution)/shard_map/ppermute | solution.py:107
  171.7 5.5 %collective-permute-start.42 = (bf16[2,200,1024]{2,1,0:T(8,128)(2,1)}, bf16[2,200,1024]{2,1,0:T(8,128)(2,1)}, u32[]{:S(2)}, u32[]{:S(2)}) collective-permute-start(bf16[2,200,1024]{2,1,0:T(8,128)(2,1)} %collective-permute-done.21.wc1), channel_id=1, source_target_pairs={{0,2},{1,3},{2,0},{3,1},{4,6},{5,7},{6,4},{7,5},{8,10},{9,11},{10,... | collective-permute-start | bytes 2457608 | tf_op jit(solution)/shard_map/ppermute | solution.py:107
  186.9 6.7 %attend.1 = (bf16[256,256]{1,0:T(8,128)(2,1)S(1)}, bf16[256,256]{1,0:T(8,128)(2,1)}, bf16[256,256]{1,0:T(8,128)(2,1)S(1)}, bf16[256,256]{1,0:T(8,128)(2,1)S(1)}) custom-call(s32[3]{0:T(128)S(1)} %pad_add_fusion.place, f32[1024,256]{1,0:T(8,128)S(1)} %copy-done.3, bf16[1024,256]{1,0:T(8,128)(2,1)S(1)} %copy-done.5, bf16[1024,256]{1,0:T(8,128)(2,1)S(1)} %copy-done.7, ...), custom_call_target="tpu_custom_call" | custom-call | flops 1342177280 | bytes 3145728 | tf_op jit(solution)/shard_map/attend/pallas_call | solution.py:399
  196.2 6.6 %collective-permute-start.33 = (bf16[256,256]{1,0:T(8,128)(2,1)}, bf16[256,256]{1,0:T(8,128)(2,1)}, u32[]{:S(2)}, u32[]{:S(2)}) collective-permute-start(bf16[256,256]{1,0:T(8,128)(2,1)} %get-tuple-element.71), channel_id=1, source_target_pairs={{0,2},{1,3},{2,0},{3,1},{4,6},{5,7},{6,4},{7,5},{8,10},{9,11},{10,... | collective-permute-start | bytes 393224 | tf_op jit(solution)/shard_map/ppermute | solution.py:107
  205.4 4.6 %collective-permute-start.37 = (bf16[256,256]{1,0:T(8,128)(2,1)}, bf16[256,256]{1,0:T(8,128)(2,1)}, u32[]{:S(2)}, u32[]{:S(2)}) collective-permute-start(bf16[256,256]{1,0:T(8,128)(2,1)} %copy-done.12), channel_id=1, source_target_pairs={{0,6},{1,7},{2,4},{3,5},{4,2},{5,3},{6,0},{7,1},{8,14},{9,15},{10,... | collective-permute-start | bytes 393224 | tf_op jit(solution)/shard_map/ppermute | solution.py:107
  213.1 4.0 %collective-permute-done.37.c30 = bf16[256,256]{1,0:T(8,128)(2,1)} collective-permute-done((bf16[256,256]{1,0:T(8,128)(2,1)}, bf16[256,256]{1,0:T(8,128)(2,1)}, u32[]{:S(2)}, u32[]{:S(2)}) %collective-permute-start.37) | collective-permute-done | bytes 131104 | tf_op jit(solution)/shard_map/ppermute | solution.py:107
  217.9 9.3 %output.1 = bf16[1600,256]{1,0:T(8,128)(2,1)} custom-call(s32[3]{0:T(128)S(1)} %pad_add_fusion.place, bf16[256,256]{1,0:T(8,128)(2,1)S(1)} %get-tuple-element.70.c00, bf16[256,256]{1,0:T(8,128)(2,1)S(1)} %collective-permute-done.32.c01, bf16[256,256]{1,0:T(8,128)(2,1)} %collective-permute-done.33.c10, bf16[256,256]{1,0:T(8,128)(2,1)} %collective-permute-done.34.c11, ...), custom_call_target="tpu_custom_call" | custom-call | flops 1677721600 | bytes 6553600 | tf_op jit(solution)/shard_map/output/pallas_call | solution.py:457
  (142 shorter events, 72.1 us)
Async XLA Ops:
  0.0 12.7 %collective-permute-start.3 = (bf16[200,1024]{1,0:T(8,128)(2,1)}, bf16[200,1024]{1,0:T(8,128)(2,1)}, u32[]{:S(2)}, u32[]{:S(2)}) collective-permute-start(bf16[200,1024]{1,0:T(8,128)(2,1)} %bitcast.42), channel_id=1, source_target_pairs={{0,0},{1,1},{2,2},{3,3},{4,4},{5,5},{6,6},{7,7},{8,16},{9,17},{10,... | collective-permute-start | bytes 1228808 | tf_op jit(solution)/shard_map/ppermute | solution.py:107
  6.5 12.6 %collective-permute-start = (bf16[3,200,256]{2,1,0:T(8,128)(2,1)}, bf16[3,200,256]{2,1,0:T(8,128)(2,1)}, u32[]{:S(2)}, u32[]{:S(2)}) collective-permute-start(bf16[3,200,256]{2,1,0:T(8,128)(2,1)} %get-tuple-element.85), channel_id=1, source_target_pairs={{0,6},{1,7},{2,4},{3,5},{4,2},{5,3},{6,0},{7,1},{8,14},{9,15},{10,... | collective-permute-start | bytes 921608 | tf_op jit(solution)/shard_map/ppermute | solution.py:107
  9.3 13.7 %collective-permute-start.1 = (bf16[3,200,256]{2,1,0:T(8,128)(2,1)}, bf16[3,200,256]{2,1,0:T(8,128)(2,1)}, u32[]{:S(2)}, u32[]{:S(2)}) collective-permute-start(bf16[3,200,256]{2,1,0:T(8,128)(2,1)} %get-tuple-element.86), channel_id=1, source_target_pairs={{0,4},{1,5},{2,6},{3,7},{4,0},{5,1},{6,2},{7,3},{8,12},{9,13},{10,... | collective-permute-start | bytes 921608 | tf_op jit(solution)/shard_map/ppermute | solution.py:107
  9.3 13.7 %collective-permute-start.2 = (bf16[3,200,256]{2,1,0:T(8,128)(2,1)}, bf16[3,200,256]{2,1,0:T(8,128)(2,1)}, u32[]{:S(2)}, u32[]{:S(2)}) collective-permute-start(bf16[3,200,256]{2,1,0:T(8,128)(2,1)} %get-tuple-element.87), channel_id=1, source_target_pairs={{0,2},{1,3},{2,0},{3,1},{4,6},{5,7},{6,4},{7,5},{8,10},{9,11},{10,... | collective-permute-start | bytes 921608 | tf_op jit(solution)/shard_map/ppermute | solution.py:107
  12.7 12.1 %collective-permute-start.4 = (bf16[200,1024]{1,0:T(8,128)(2,1)}, bf16[200,1024]{1,0:T(8,128)(2,1)S(1)}, u32[]{:S(2)}, u32[]{:S(2)}) collective-permute-start(bf16[200,1024]{1,0:T(8,128)(2,1)} %collective-permute-done.3), channel_id=1, source_target_pairs={{0,8},{1,9},{2,10},{3,11},{4,12},{5,13},{6,14},{7,15},{8,0},{9,1},... | collective-permute-start | bytes 1228808 | tf_op jit(solution)/shard_map/ppermute | solution.py:107
  13.7 13.5 %collective-permute-start.6 = (bf16[200,1024]{1,0:T(8,128)(2,1)}, bf16[200,1024]{1,0:T(8,128)(2,1)S(1)}, u32[]{:S(2)}, u32[]{:S(2)}) collective-permute-start(bf16[200,1024]{1,0:T(8,128)(2,1)} %collective-permute-done.5), channel_id=1, source_target_pairs={{0,0},{1,1},{2,2},{3,3},{4,4},{5,5},{6,6},{7,7},{8,16},{9,17},{10,... | collective-permute-start | bytes 1228808 | tf_op jit(solution)/shard_map/ppermute | solution.py:107
  28.0 34.9 %collective-permute-start.7 = (bf16[3,800,256]{2,1,0:T(8,128)(2,1)S(1)}, bf16[3,800,256]{2,1,0:T(8,128)(2,1)}, u32[]{:S(2)}, u32[]{:S(2)}) collective-permute-start(bf16[3,800,256]{2,1,0:T(8,128)(2,1)S(1)} %pad_maximum_fusion.own), channel_id=1, source_target_pairs={{0,8},{1,9},{2,10},{3,11},{4,12},{5,13},{6,14},{7,15},{8,0},{9,1},... | collective-permute-start | bytes 3686408 | tf_op jit(solution)/shard_map/ppermute | solution.py:107
  28.0 34.9 %collective-permute-start.8 = (bf16[3,800,256]{2,1,0:T(8,128)(2,1)S(1)}, bf16[3,800,256]{2,1,0:T(8,128)(2,1)}, u32[]{:S(2)}, u32[]{:S(2)}) collective-permute-start(bf16[3,800,256]{2,1,0:T(8,128)(2,1)S(1)} %pad_maximum_fusion.own), channel_id=1, source_target_pairs={{0,0},{1,1},{2,2},{3,3},{4,4},{5,5},{6,6},{7,7},{8,16},{9,17},{10,... | collective-permute-start | bytes 3686408 | tf_op jit(solution)/shard_map/ppermute | solution.py:107
  31.2 31.7 %collective-permute-start.9 = (bf16[4,128,896]{2,1,0:T(8,128)(2,1)}, bf16[4,128,896]{2,1,0:T(8,128)(2,1)}, u32[]{:S(2)}, u32[]{:S(2)}) collective-permute-start(bf16[4,128,896]{2,1,0:T(8,128)(2,1)} %get-tuple-element.44), channel_id=1, source_target_pairs={{0,4},{1,5},{2,6},{3,7},{4,0},{5,1},{6,2},{7,3},{8,12},{9,13},{10,... | collective-permute-start | bytes 2752520 | tf_op jit(solution)/shard_map/ppermute | solution.py:107
  34.7 28.2 %collective-permute-start.10 = (bf16[200,1024]{1,0:T(8,128)(2,1)S(1)}, bf16[200,1024]{1,0:T(8,128)(2,1)S(1)}, u32[]{:S(2)}, u32[]{:S(2)}) collective-permute-start(bf16[200,1024]{1,0:T(8,128)(2,1)S(1)} %copy-done.24), channel_id=1, source_target_pairs={{0,8},{1,9},{2,10},{3,11},{4,12},{5,13},{6,14},{7,15},{8,0},{9,1},... | collective-permute-start | bytes 1228808 | tf_op jit(solution)/shard_map/ppermute | solution.py:107
  62.9 38.5 %collective-permute-start.15 = (bf16[2,4,128,896]{3,2,1,0:T(8,128)(2,1)S(1)}, bf16[2,4,128,896]{3,2,1,0:T(8,128)(2,1)S(1)}, u32[]{:S(2)}, u32[]{:S(2)}) collective-permute-start(bf16[2,4,128,896]{3,2,1,0:T(8,128)(2,1)S(1)} %get-tuple-element.48.xa), channel_id=1, source_target_pairs={{0,2},{1,3},{2,0},{3,1},{4,6},{5,7},{6,4},{7,5},{8,10},{9,11},{10,... | collective-permute-start | bytes 5505032 | tf_op jit(solution)/shard_map/ppermute | solution.py:107
  67.3 20.2 %collective-permute-start.17 = (bf16[2,200,1024]{2,1,0:T(8,128)(2,1)}, bf16[2,200,1024]{2,1,0:T(8,128)(2,1)}, u32[]{:S(2)}, u32[]{:S(2)}) collective-permute-start(bf16[2,200,1024]{2,1,0:T(8,128)(2,1)} %pad_maximum_fusion.1.wa0), channel_id=1, source_target_pairs={{0,4},{1,5},{2,6},{3,7},{4,0},{5,1},{6,2},{7,3},{8,12},{9,13},{10,... | collective-permute-start | bytes 2457608 | tf_op jit(solution)/shard_map/ppermute | solution.py:107
  70.8 30.7 %collective-permute-start.12 = (bf16[3,800,256]{2,1,0:T(8,128)(2,1)}, bf16[3,800,256]{2,1,0:T(8,128)(2,1)S(1)}, u32[]{:S(2)}, u32[]{:S(2)}) collective-permute-start(bf16[3,800,256]{2,1,0:T(8,128)(2,1)} %collective-permute-done.8.middle), channel_id=1, source_target_pairs={{0,8},{1,9},{2,10},{3,11},{4,12},{5,13},{6,14},{7,15},{8,0},{9,1},... | collective-permute-start | bytes 3686408 | tf_op jit(solution)/shard_map/ppermute | solution.py:107
  70.8 30.7 %collective-permute-start.13 = (bf16[3,800,256]{2,1,0:T(8,128)(2,1)}, bf16[3,800,256]{2,1,0:T(8,128)(2,1)S(1)}, u32[]{:S(2)}, u32[]{:S(2)}) collective-permute-start(bf16[3,800,256]{2,1,0:T(8,128)(2,1)} %collective-permute-done.7.near), channel_id=1, source_target_pairs={{0,0},{1,1},{2,2},{3,3},{4,4},{5,5},{6,6},{7,7},{8,16},{9,17},{10,... | collective-permute-start | bytes 3686408 | tf_op jit(solution)/shard_map/ppermute | solution.py:107
  80.4 21.0 %collective-permute-start.14 = (bf16[4,128,896]{2,1,0:T(8,128)(2,1)}, bf16[4,128,896]{2,1,0:T(8,128)(2,1)S(1)}, u32[]{:S(2)}, u32[]{:S(2)}) collective-permute-start(bf16[4,128,896]{2,1,0:T(8,128)(2,1)} %collective-permute-done.9.xc), channel_id=1, source_target_pairs={{0,1},{1,0},{2,3},{3,2},{4,5},{5,4},{6,7},{7,6},{8,9},{9,8},{10,11... | collective-permute-start | bytes 2752520 | tf_op jit(solution)/shard_map/ppermute | solution.py:107
  87.5 14.0 %collective-permute-start.16 = (bf16[4,128,896]{2,1,0:T(8,128)(2,1)}, bf16[4,128,896]{2,1,0:T(8,128)(2,1)S(1)}, u32[]{:S(2)}, u32[]{:S(2)}) collective-permute-start(bf16[4,128,896]{2,1,0:T(8,128)(2,1)} %collective-permute-done.9.xc), channel_id=1, source_target_pairs={{0,2},{1,3},{2,0},{3,1},{4,6},{5,7},{6,4},{7,5},{8,10},{9,11},{10,... | collective-permute-start | bytes 2752520 | tf_op jit(solution)/shard_map/ppermute | solution.py:107
  103.5 28.6 %collective-permute-start.20 = (bf16[3,800,256]{2,1,0:T(8,128)(2,1)S(1)}, bf16[3,800,256]{2,1,0:T(8,128)(2,1)S(1)}, u32[]{:S(2)}, u32[]{:S(2)}) collective-permute-start(bf16[3,800,256]{2,1,0:T(8,128)(2,1)S(1)} %collective-permute-done.13.middle), channel_id=1, source_target_pairs={{0,8},{1,9},{2,10},{3,11},{4,12},{5,13},{6,14},{7,15},{8,0},{9,1},... | collective-permute-start | bytes 3686408 | tf_op jit(solution)/shard_map/ppermute | solution.py:107
  104.5 19.8 %collective-permute-start.21 = (bf16[2,200,1024]{2,1,0:T(8,128)(2,1)}, bf16[2,200,1024]{2,1,0:T(8,128)(2,1)}, u32[]{:S(2)}, u32[]{:S(2)}) collective-permute-start(bf16[2,200,1024]{2,1,0:T(8,128)(2,1)} %pad_maximum_fusion.2.wa1), channel_id=1, source_target_pairs={{0,4},{1,5},{2,6},{3,7},{4,0},{5,1},{6,2},{7,3},{8,12},{9,13},{10,... | collective-permute-start | bytes 2457608 | tf_op jit(solution)/shard_map/ppermute | solution.py:107
  141.5 29.4 %collective-permute-start.22 = (bf16[2,512,256]{2,1,0:T(8,128)(2,1)S(1)}, bf16[2,512,256]{2,1,0:T(8,128)(2,1)S(1)}, u32[]{:S(2)}, u32[]{:S(2)}) collective-permute-start(bf16[2,512,256]{2,1,0:T(8,128)(2,1)S(1)} %get-tuple-element.67), channel_id=1, source_target_pairs={{0,8},{1,9},{2,10},{3,11},{4,12},{5,13},{6,14},{7,15},{8,0},{9,1},... | collective-permute-start | bytes 1572872 | tf_op jit(solution)/shard_map/ppermute | solution.py:107
  144.2 51.9 %collective-permute-start.40 = (bf16[2,200,1024]{2,1,0:T(8,128)(2,1)}, bf16[2,200,1024]{2,1,0:T(8,128)(2,1)S(1)}, u32[]{:S(2)}, u32[]{:S(2)}) collective-permute-start(bf16[2,200,1024]{2,1,0:T(8,128)(2,1)} %pad_maximum_fusion.2.wa1), channel_id=1, source_target_pairs={{0,2},{1,3},{2,0},{3,1},{4,6},{5,7},{6,4},{7,5},{8,10},{9,11},{10,... | collective-permute-start | bytes 2457608 | tf_op jit(solution)/shard_map/ppermute | solution.py:107
  144.5 58.3 %collective-permute-start.39 = (bf16[2,200,1024]{2,1,0:T(8,128)(2,1)}, bf16[2,200,1024]{2,1,0:T(8,128)(2,1)S(1)}, u32[]{:S(2)}, u32[]{:S(2)}) collective-permute-start(bf16[2,200,1024]{2,1,0:T(8,128)(2,1)} %pad_maximum_fusion.1.wa0), channel_id=1, source_target_pairs={{0,2},{1,3},{2,0},{3,1},{4,6},{5,7},{6,4},{7,5},{8,10},{9,11},{10,... | collective-permute-start | bytes 2457608 | tf_op jit(solution)/shard_map/ppermute | solution.py:107
  147.7 55.3 %collective-permute-start.41 = (bf16[2,200,1024]{2,1,0:T(8,128)(2,1)}, bf16[2,200,1024]{2,1,0:T(8,128)(2,1)}, u32[]{:S(2)}, u32[]{:S(2)}) collective-permute-start(bf16[2,200,1024]{2,1,0:T(8,128)(2,1)} %collective-permute-done.17.wc0), channel_id=1, source_target_pairs={{0,2},{1,3},{2,0},{3,1},{4,6},{5,7},{6,4},{7,5},{8,10},{9,11},{10,... | collective-permute-start | bytes 2457608 | tf_op jit(solution)/shard_map/ppermute | solution.py:107
  171.7 46.2 %collective-permute-start.42 = (bf16[2,200,1024]{2,1,0:T(8,128)(2,1)}, bf16[2,200,1024]{2,1,0:T(8,128)(2,1)}, u32[]{:S(2)}, u32[]{:S(2)}) collective-permute-start(bf16[2,200,1024]{2,1,0:T(8,128)(2,1)} %collective-permute-done.21.wc1), channel_id=1, source_target_pairs={{0,2},{1,3},{2,0},{3,1},{4,6},{5,7},{6,4},{7,5},{8,10},{9,11},{10,... | collective-permute-start | bytes 2457608 | tf_op jit(solution)/shard_map/ppermute | solution.py:107
  205.4 11.7 %collective-permute-start.37 = (bf16[256,256]{1,0:T(8,128)(2,1)}, bf16[256,256]{1,0:T(8,128)(2,1)}, u32[]{:S(2)}, u32[]{:S(2)}) collective-permute-start(bf16[256,256]{1,0:T(8,128)(2,1)} %copy-done.12), channel_id=1, source_target_pairs={{0,6},{1,7},{2,4},{3,5},{4,2},{5,3},{6,0},{7,1},{8,14},{9,15},{10,... | collective-permute-start | bytes 393224 | tf_op jit(solution)/shard_map/ppermute | solution.py:107
  (48 other events, 244.1 us)

commit v4 on v0

--- a/solution.py
+++ b/solution.py
@@ -1,10 +1,15 @@
+import functools
+import math
+
 import jax
 import jax.numpy as jnp
 from jax import lax
+from jax.experimental import pallas as pl
+from jax.experimental.pallas import tpu as pltpu
 from jax.sharding import PartitionSpec as P
 
 HEAD_DIM = 128
-
+SLAB = 4
 
 eps = 1e-06
 floor_score = -1e30
@@ -24,7 +29,7 @@
     return (jnp.where(mask, scores, floor_score), mask)
 
 
-def shards(tokens, norm_gain, qkv_weight, q_gain, k_gain, out_weight, layer_scale, segment_ids):
+def row_plan(tokens, norm_gain, qkv_weight, q_gain, k_gain, out_weight, layer_scale, segment_ids):
     count = tokens.shape[0]
     source = tokens.astype(jnp.float32)
     normed = (
@@ -87,7 +92,467 @@
     return (residual + layer_scale * projected).astype(jnp.bfloat16)
 
 
+ANY = pl.BlockSpec(memory_space=pl.ANY)
+VMEM = pl.BlockSpec(memory_space=pltpu.VMEM)
+SMEM = pl.BlockSpec(memory_space=pltpu.SMEM)
+HBM = pl.BlockSpec(memory_space=pltpu.HBM)
+MIB = 1024 * 1024
+
+
+def permuted(x, to):
+    slabs, tps = lax.axis_size("seq") // SLAB, lax.axis_size("tp")
+    pairs = []
+    for i in range(slabs * SLAB * tps):
+        z, q, y = to(i // (SLAB * tps), i // tps % SLAB, i % tps)
+        pairs.append((i, (z * SLAB + q) * tps + y))
+    return lax.ppermute(x, ("seq", "tp"), pairs)
+
+
+def in_slab(x, flip):
+    return permuted(x, lambda z, q, y: (z, q ^ flip, y))
+
+
+def across(x):
+    return permuted(x, lambda z, q, y: (z, q, 1 - y))
+
+
+def even_pair(x):
+    return permuted(x, lambda z, q, y: (z ^ 1, q, y))
+
+
+def odd_pair(x):
+    return permuted(x, lambda z, q, y: (3 - z if z in (1, 2) else z, q, y))
+
+
+def z_line(x):
+    size = lax.axis_size("seq")
+    groups = [list(range(i, size, SLAB)) for i in range(SLAB)]
+    return lax.all_gather(x, "seq", axis_index_groups=groups)
+
+
+def tied(*arrays):
+    return lax.optimization_barrier(arrays)
+
+
+def as_row(column):
+    wide = jnp.broadcast_to(column, (column.shape[0], 128))
+    return jnp.transpose(wide)[:8]
+
+
+def as_column(row):
+    return jnp.transpose(jnp.broadcast_to(row, (128, row.shape[1])))
+
+
+def norm_kernel(place, tokens, gain, first, pair):
+    half = pair.shape[2]
+    part = tokens.shape[1] // pair.shape[1]
+    blank = jnp.zeros((half, pair.shape[3] - part), jnp.bfloat16)
+    for i in range(2):
+        at = pl.multiple_of((place[2] ^ i) * half, half)
+        source = tokens[pl.ds(at, half), :].astype(jnp.float32)
+        mean = jnp.mean(source * source, axis=1, keepdims=True)
+        normed = source * lax.rsqrt(mean + eps) * gain[...]
+        for j in range(pair.shape[1]):
+            chunk = normed[:, j * part:(j + 1) * part].astype(jnp.bfloat16)
+            for out in (pair.at[i, j],) + ((first.at[j],) if i == 0 else ()):
+                out[:, :part] = chunk
+                out[:, part:] = blank
+
+
+def norm(place, tokens, gain, slabs):
+    count, depth = tokens.shape
+    shape = (slabs, count // 2, pl.cdiv(depth // slabs, 128) * 128)
+    return pl.pallas_call(
+        norm_kernel,
+        out_shape=(
+            jax.ShapeDtypeStruct(shape, jnp.bfloat16),
+            jax.ShapeDtypeStruct((2,) + shape, jnp.bfloat16),
+        ),
+        in_specs=[SMEM, VMEM, VMEM],
+        out_specs=(VMEM, VMEM),
+        compiler_params=pltpu.CompilerParams(vmem_limit_bytes=16 * MIB),
+        name="norm",
+    )(place, tokens, gain[None])
+
+
+def token_copies(xs, at, out, sems):
+    copies = []
+    for r in range(SLAB):
+        for i in range(2):
+            src = xs[r].at[i, at] if r < 2 else xs[2 * r - 2 + i].at[at]
+            copies.append(pltpu.make_async_copy(src, out.at[r, i], sems.at[r, i]))
+    return copies
+
+
+def start(copies):
+    for copy in copies:
+        copy.start()
+
+
+def wait(copies):
+    for copy in copies:
+        copy.wait()
+
+
+def add_products(xs, w, x_all, w_all, acc, x_sem, w_sem):
+    slabs, kinds, rows = w.shape[:3]
+    steps = []
+    for j in range(slabs):
+        copies = [pltpu.make_async_copy(w.at[j], w_all.at[j], w_sem.at[j])]
+        copies += token_copies(xs, j, x_all.at[j], x_sem.at[j])
+        start(copies)
+        steps.append(copies)
+    for j in range(slabs):
+        wait(steps[j])
+        for r in range(SLAB):
+            x = x_all[j, r].reshape(-1, x_all.shape[-1])[:, :rows]
+            for kind in range(kinds):
+                term = jnp.dot(x, w_all[j, kind], preferred_element_type=jnp.float32)
+                acc[kind, r] = term if j == 0 else acc[kind, r] + term
+
+
+def block_rows(place, r, i, count):
+    half = count // 2
+    at = (place[1] ^ r) * count + (place[2] ^ i) * half
+    return pl.ds(pl.multiple_of(at, half), half), slice(i * half, (i + 1) * half)
+
+
+def pair_rows(place, reach):
+    z = place[0]
+    return [pl.ds(pl.multiple_of(at * reach, reach), reach) for at in (1 - z % 2, z % 2)]
+
+
+def query_key_kernel(
+    place, xa, xb, xc, xd, xe, xf, w, both, squares, x_all, w_all, acc, both_all, x_sem, w_sem, sem,
+):
+    add_products((xa, xb, xc, xd, xe, xf), w, x_all, w_all, acc, x_sem, w_sem)
+    for kind in range(2):
+        for r in range(SLAB):
+            part = acc[kind, r]
+            summed = as_row(jnp.sum(part * part, axis=1, keepdims=True))
+            for i in range(2):
+                rows, cut = block_rows(place, r, i, part.shape[0])
+                both_all[kind, rows, :] = part[cut]
+                squares[kind:kind + 1, rows] = summed[:1, cut]
+    copy = pltpu.make_async_copy(both_all, both, sem)
+    copy.start()
+    copy.wait()
+
+
+def value_kernel(
+    place, xa, xb, xc, xd, xe, xf, w, values, even, odd, x_all, w_all, acc, v_all, x_sem, w_sem, sem,
+):
+    add_products((xa, xb, xc, xd, xe, xf), w, x_all, w_all, acc, x_sem, w_sem)
+    for r in range(SLAB):
+        low = acc[0, r].astype(jnp.bfloat16)
+        for i in range(2):
+            rows, cut = block_rows(place, r, i, low.shape[0])
+            v_all[rows, :] = low[cut]
+    copy = pltpu.make_async_copy(v_all, values, sem)
+    copy.start()
+    for out, rows in zip((even, odd), pair_rows(place, even.shape[0])):
+        out[...] = v_all[rows, :]
+    copy.wait()
+
+
+def project(kernel, out_shape, out_specs, held, place, xs, w):
+    slabs, kinds, rows, width = w.shape
+    half, wide = xs[0].shape[2:]
+    slab = 2 * SLAB * half
+    return pl.pallas_call(
+        kernel,
+        out_shape=out_shape,
+        in_specs=[SMEM] + [HBM] * 7,
+        out_specs=out_specs,
+        scratch_shapes=[
+            pltpu.VMEM((slabs, SLAB, 2, half, wide), jnp.bfloat16),
+            pltpu.VMEM((slabs, kinds, rows, width), jnp.bfloat16),
+            pltpu.VMEM((kinds, SLAB, 2 * half, width), jnp.float32),
+            held,
+            pltpu.SemaphoreType.DMA((slabs, SLAB, 2)),
+            pltpu.SemaphoreType.DMA((slabs,)),
+            pltpu.SemaphoreType.DMA,
+        ],
+        compiler_params=pltpu.CompilerParams(vmem_limit_bytes=28 * MIB),
+        cost_estimate=pl.CostEstimate(
+            flops=2 * kinds * slab * slabs * rows * width,
+            bytes_accessed=2 * slabs * rows * (kinds * width + slab),
+            transcendentals=0,
+        ),
+        name=kernel.__name__,
+    )(place, *xs, w)
+
+
+def norm_heads_kernel(
+    full_width, place, both, mine, other, q_gain, k_gain, query, keys, even, odd,
+    held, q_all, k_all, sems,
+):
+    load = pltpu.make_async_copy(both, held, sems.at[0])
+    load.start()
+    scale = lax.rsqrt((mine[...] + other[...]) / full_width + eps)
+    count = 2 * 128
+    load.wait()
+    for kind, gain, out in ((1, k_gain, k_all), (0, q_gain, q_all)):
+        for at in range(0, held.shape[1], count):
+            column = as_column(scale[kind:kind + 1, at:at + count])
+            column = jnp.tile(column, (1, held.shape[2] // 128))
+            out[at:at + count, :] = (held[kind, at:at + count, :] * column * gain[...]).astype(
+                jnp.bfloat16
+            )
+    stores = [
+        pltpu.make_async_copy(k_all, keys, sems.at[1]),
+        pltpu.make_async_copy(q_all, query, sems.at[2]),
+    ]
+    start(stores)
+    for out, rows in zip((even, odd), pair_rows(place, even.shape[0])):
+        out[...] = k_all[rows, :]
+    wait(stores)
+
+
+def norm_heads(full_width, place, both, mine, other, q_gain, k_gain, reach):
+    slab, width = both.shape[1:]
+    bf16 = jnp.bfloat16
+    whole, part = jax.ShapeDtypeStruct((slab, width), bf16), jax.ShapeDtypeStruct((reach, width), bf16)
+    return pl.pallas_call(
+        functools.partial(norm_heads_kernel, full_width),
+        out_shape=(whole, whole, part, part),
+        in_specs=[SMEM, HBM] + [VMEM] * 4,
+        out_specs=(HBM, HBM, VMEM, VMEM),
+        scratch_shapes=[
+            pltpu.VMEM((2, slab, width), jnp.float32),
+            pltpu.VMEM((slab, width), bf16),
+            pltpu.VMEM((slab, width), bf16),
+            pltpu.SemaphoreType.DMA((3,)),
+        ],
+        compiler_params=pltpu.CompilerParams(vmem_limit_bytes=16 * MIB),
+        name="norm_heads",
+    )(place, both, mine, other, q_gain, k_gain)
+
+
+def attend_kernel(
+    place, query, keys, k_even, k_odd, values, v_even, v_odd, seg, o0, o1, o2, o3,
+    q_all, k_all, v_all, sems,
+):
+    z, q = place[0], place[1]
+    slab = query.shape[0]
+    count = slab // SLAB
+    half = k_even.shape[0]
+    upper = half + slab
+    even_at = pl.multiple_of(jnp.where(z % 2 == 0, upper, 0), half)
+    odd_at = pl.multiple_of(jnp.where(z % 2 == 0, 0, upper), half)
+    copies = [pltpu.make_async_copy(query, q_all, sems.at[0])]
+    for k, (whole, even, odd, out) in enumerate(
+        ((keys, k_even, k_odd, k_all), (values, v_even, v_odd, v_all))
+    ):
+        for n, (src, at) in enumerate(((whole, half), (even, even_at), (odd, odd_at))):
+            dst = out.at[pl.ds(at, src.shape[0]), :]
+            copies.append(pltpu.make_async_copy(src, dst, sems.at[1 + 3 * k + n]))
+    start(copies)
+    wait(copies)
+    window = count + 2 * half
+    heads = query.shape[1] // HEAD_DIM
+    factor = HEAD_DIM ** (-0.5) * math.log2(math.e)
+    for r, out in ((1, o1), (2, o2), (3, o3), (0, o0)):
+        begin = pl.multiple_of((q ^ r) * count, count)
+        at_query = pl.multiple_of((q ^ r) * count + half, count)
+        key_seg = seg[:, pl.ds(begin, window)]
+        query_seg = as_column(seg[:, pl.ds(at_query, count)])
+        mask = jnp.tile(query_seg, (1, window // 128)) == key_seg
+        for h in range(heads):
+            cols = slice(h * HEAD_DIM, (h + 1) * HEAD_DIM)
+            scores = lax.dot_general(
+                q_all[pl.ds(begin, count), cols], k_all[pl.ds(begin, window), cols],
+                (((1,), (1,)), ((), ())), preferred_element_type=jnp.float32,
+            )
+            scores = jnp.where(mask, scores, floor_score)
+            peak = jnp.max(scores, axis=1, keepdims=True)
+            weights = jnp.exp2((scores - peak) * factor)
+            total = jnp.sum(weights, axis=1, keepdims=True)
+            summed = jnp.dot(
+                weights.astype(jnp.bfloat16), v_all[pl.ds(begin, window), cols],
+                preferred_element_type=jnp.float32,
+            )
+            out[:, cols] = (summed / total).astype(jnp.bfloat16)
+
+
+def attend(place, query, keys, k_even, k_odd, values, v_even, v_odd, seg):
+    slab, width = query.shape
+    half = k_even.shape[0]
+    count = slab // SLAB
+    ext = slab + 2 * half
+    bf16 = jnp.bfloat16
+    window = count + 2 * half
+    return pl.pallas_call(
+        attend_kernel,
+        out_shape=(jax.ShapeDtypeStruct((count, width), bf16),) * 4,
+        in_specs=[SMEM] + [HBM] * 7 + [VMEM],
+        out_specs=(VMEM,) * 4,
+        scratch_shapes=[
+            pltpu.VMEM((slab, width), bf16),
+            pltpu.VMEM((ext, width), bf16),
+            pltpu.VMEM((ext, width), bf16),
+            pltpu.SemaphoreType.DMA((7,)),
+        ],
+        compiler_params=pltpu.CompilerParams(vmem_limit_bytes=24 * MIB),
+        cost_estimate=pl.CostEstimate(
+            flops=4 * slab * window * width,
+            bytes_accessed=4 * ext * width + 4 * slab * width,
+            transcendentals=slab * window * width // HEAD_DIM,
+        ),
+        name="attend",
+    )(place, query, keys, k_even, k_odd, values, v_even, v_odd, seg)
+
+
+def out_kernel(
+    place, c00, c01, c10, c11, c20, c21, c30, c31, wa, wb, wc, wd, residual, scale,
+    out, c_all, w_all, total, sems,
+):
+    q = place[1]
+    copies = []
+    for r, w in enumerate((wa, wb, wc, wd)):
+        copy = pltpu.make_async_copy(w, w_all.at[r], sems.at[r])
+        copy.start()
+        copies.append(copy)
+    width = c00.shape[1]
+    for r, pair in enumerate(((c00, c01), (c10, c11), (c20, c21), (c30, c31))):
+        at = pl.multiple_of((q ^ r) * width, width)
+        for i in range(2):
+            c_all[i, :, pl.ds(at, width)] = pair[i][...]
+    rows = wa.shape[2]
+    for r in range(SLAB):
+        copies[r].wait()
+        for j in range(2):
+            at = pl.multiple_of((j * SLAB + (q ^ r)) * rows, 8)
+            term = None
+            for i in range(2):
+                part = lax.dot_general(
+                    w_all[r, i, j], c_all[i], (((1,), (1,)), ((), ())),
+                    preferred_element_type=jnp.float32,
+                )
+                term = part if term is None else term + part
+            total[pl.ds(at, rows), :] = term
+    out[...] = (residual[...].astype(jnp.float32) + scale[...] * total[...]).astype(jnp.bfloat16)
+
+
+def output(place, blocks, pieces, residual, scale):
+    count, width = blocks[0].shape
+    rows, depth = pieces[0].shape[2:]
+    share = residual.shape[0]
+    return pl.pallas_call(
+        out_kernel,
+        out_shape=jax.ShapeDtypeStruct((share, count), jnp.bfloat16),
+        in_specs=[SMEM] + [VMEM] * 8 + [HBM] * 4 + [VMEM] * 2,
+        out_specs=VMEM,
+        scratch_shapes=[
+            pltpu.VMEM((2, count, depth), jnp.bfloat16),
+            pltpu.VMEM((SLAB, 2, 2, rows, depth), jnp.bfloat16),
+            pltpu.VMEM((share, count), jnp.float32),
+            pltpu.SemaphoreType.DMA((SLAB,)),
+        ],
+        compiler_params=pltpu.CompilerParams(vmem_limit_bytes=24 * MIB),
+        cost_estimate=pl.CostEstimate(
+            flops=4 * share * count * depth,
+            bytes_accessed=4 * share * depth,
+            transcendentals=0,
+        ),
+        name="output",
+    )(place, *blocks, *pieces, residual, scale)
+
+
+def rows_of_slab(q, cut):
+    got = [cut[0]] + [in_slab(cut[r], r) for r in range(1, SLAB)]
+    placed = []
+    for b in range(SLAB):
+        piece = got[b]
+        for other in range(1, SLAB):
+            piece = jnp.where(q == other, got[b ^ other], piece)
+        placed.append(piece)
+    return jnp.concatenate(placed, axis=1)
+
+
+def slab_plan(tokens, norm_gain, qkv_weight, q_gain, k_gain, out_weight, layer_scale, segment_ids):
+    count = tokens.shape[0]
+    seq, tp = lax.axis_index("seq"), lax.axis_index("tp")
+    slabs = lax.axis_size("seq") // SLAB
+    z, q = seq // SLAB, seq % SLAB
+    place = jnp.stack([z, q, tp]).astype(jnp.int32)
+    width = qkv_weight.shape[2] // SLAB
+    full_width = qkv_weight.shape[2] * lax.axis_size("tp")
+    slab, half = SLAB * count, 2 * count
+    f32, bf16 = jnp.float32, jnp.bfloat16
+
+    out_all = z_line(jnp.transpose(out_weight))
+
+    by_kind = jnp.transpose(qkv_weight, (1, 0, 2))
+    cut = [lax.dynamic_slice_in_dim(by_kind, (q ^ r) * width, width, 2) for r in range(SLAB)]
+    own_qk = rows_of_slab(q, [c[:2] for c in cut])
+    w_qk = z_line(own_qk)
+    first, pair = norm(place, tokens, norm_gain, slabs)
+
+    tied_cut = tied(own_qk, first, pair, *[c[2:] for c in cut])
+    _, first, pair = tied_cut[:3]
+    own_v = rows_of_slab(q, tied_cut[3:])
+    w_v = z_line(tied(own_v, w_qk)[0])
+    x2a = in_slab(first, 2)
+    x1 = in_slab(pair, 1)
+    own_v, x2a, x1 = tied(own_v, x2a, x1)
+    x2b, x3a = across(x2a), in_slab(x2a, 1)
+    x3b = in_slab(x2b, 1)
+    xs = (pair, x1, x2a, x2b, x3a, x3b)
+
+    close, far = out_all[:2], out_all[2:]
+    close, far, x2b, x3a = tied(close, far, x2b, x3a)
+    wa = jnp.stack(
+        [jnp.where(tp == 0, close, far), across(jnp.where(tp == 0, far, close))]
+    )
+    wc = in_slab(wa, 2)
+    pieces = (wa, in_slab(wa, 1), wc, in_slab(wc, 1))
+
+    both, squares = project(
+        query_key_kernel,
+        (jax.ShapeDtypeStruct((2, slab, width), f32), jax.ShapeDtypeStruct((2, slab), f32)),
+        (HBM, VMEM), pltpu.VMEM((2, slab, width), f32), place, xs, w_qk,
+    )
+    mine = squares
+    for r in range(1, SLAB):
+        mine = mine + in_slab(squares, r)
+    gains = [lax.dynamic_slice_in_dim(g, q * width, width, 0)[None] for g in (q_gain, k_gain)]
+    query, keys, k_even, k_odd = norm_heads(
+        full_width, place, both, mine, across(mine), *gains, half
+    )
+    k_even, k_odd = even_pair(k_even), odd_pair(k_odd)
+
+    values, v_even, v_odd = project(
+        value_kernel,
+        (
+            jax.ShapeDtypeStruct((slab, width), bf16),
+            jax.ShapeDtypeStruct((half, width), bf16),
+            jax.ShapeDtypeStruct((half, width), bf16),
+        ),
+        (HBM, VMEM, VMEM), pltpu.VMEM((slab, width), bf16), place, xs, w_v,
+    )
+    v_even, v_odd = even_pair(v_even), odd_pair(v_odd)
+    outside = jnp.full((half,), -1, jnp.int32)
+    seg = jnp.concatenate([outside, segment_ids, outside], axis=0)
+    seg = lax.dynamic_slice_in_dim(seg, z * slab, slab + 2 * half, 0).astype(f32)[None]
+    blocks = attend(place, query, keys, k_even, k_odd, values, v_even, v_odd, seg)
+    spread = []
+    for r in range(SLAB):
+        for i in range(2):
+            to = functools.partial(lambda r, i, z, q, y: (z, q ^ r, y ^ i), r, i)
+            spread.append(permuted(blocks[r], to) if r or i else blocks[r])
+
+    share = layer_scale.shape[0]
+    residual = jnp.transpose(lax.dynamic_slice_in_dim(tokens, tp * share, share, 1))
+    return jnp.transpose(output(place, spread, pieces, residual, layer_scale[:, None]))
+
+
 def solution(mesh):
+    def shards(*args):
+        heads = args[2].shape[2] // HEAD_DIM
+        slab = mesh.shape["seq"] == 16 and mesh.shape["tp"] == 2 and heads % SLAB == 0
+        return (slab_plan if slab else row_plan)(*args)
+
     return jax.shard_map(
         shards,
         mesh=mesh,

time: 308 us -> 227 us (0.74)
  waiting for transfers between devices: 220 us -> 112 us
  Pallas kernels: 0 us -> 35.3 us
  matrix products: 30.3 us -> 0 us
  starting transfers between devices: 12.5 us -> 38.1 us
  local copies, waits for them, and re-layouts: 17.9 us -> 23.5 us
  other arithmetic: 8.39 us -> 3.03 us
  blocking collectives: 4.17 us -> 0 us
    all_gather x2 -> x3, waiting for transfers between devices: 101 us -> 17.8 us  [z_line(): return lax.all_gather(x, 'seq', axis_index_groups=groups)]
    reduce_scatter x1 -> x0, waiting for transfers between devices: 45.5 us -> none  [shards(): projected = lax.psum_scatter(terms, 'tp', scatter_dimension=1, tiled=True)]
    pallas_call x0 -> x6, Pallas kernels: none -> 35.3 us  [the longest x2 16.2 us: project(): pl.pallas_call(kernel, out_shape=out_shape, in_specs=[SMEM] + [HBM] * 7,...]
    ppermute x4 -> x30, starting transfers between devices: 12.4 us -> 38 us  [permuted(): return lax.ppermute(x, ('seq', 'tp'), pairs)]
    ppermute x4 -> x30, waiting for transfers between devices: 71.8 us -> 93.5 us  [permuted(): return lax.ppermute(x, ('seq', 'tp'), pairs)]
    dot_general x3 -> x0, matrix products: 20.8 us -> none  [the longest x1 10.1 us: shards(): jnp.einsum('td,dch->tch', normed, lax.all_gather(qkv_weight, 'seq', axis=...]
    sub x1 -> x0, matrix products: 9.5 us -> none  [shards(): weights = jnp.where(mask, jnp.exp(scores - peak), 0.0)]
    unnamed x29 -> x41, local copies, waits for them, and re-layouts: 12.9 us -> 17.4 us
  transfers between devices with their start and end apart: 7 -> 33, of which waited for: 4 -> 15; matrix products, arithmetic and copies ran while one was open for 14% -> 5% of each run, Pallas kernels for 0% -> 13%
where the time goes in v4:
time: 227 us; the launch traced here: 225 us
  waiting for transfers between devices  112 us (49%)
  starting transfers between devices  38.1 us (17%)
  Pallas kernels  35.3 us (16%)
  local copies, waits for them, and re-layouts  23.5 us (10%)
  between operations  13.5 us (6%)
  other arithmetic  3.03 us (1%)
    ppermute x30, waiting for transfers between devices, permuted(): return lax.ppermute(x, ('seq', 'tp'), pairs)  93.5 us
    ppermute x30, starting transfers between devices, permuted(): return lax.ppermute(x, ('seq', 'tp'), pairs)  38 us
    all_gather x3, waiting for transfers between devices, z_line(): return lax.all_gather(x, 'seq', axis_index_groups=groups)  17.8 us
    unnamed x41, local copies, waits for them, and re-layouts  17.4 us
    pallas_call x2, Pallas kernels, project(): pl.pallas_call(kernel, out_shape=out_shape, in_specs=[SMEM] + [HBM] * 7,...  16.2 us
    pallas_call x1, Pallas kernels, attend(): pl.pallas_call(attend_kernel, out_shape=(jax.ShapeDtypeStruct((count, wid...  7.57 us
    pallas_call x1, Pallas kernels, output(): pl.pallas_call(out_kernel, out_shape=jax.ShapeDtypeStruct((share, count),...  6.61 us
  transfers between devices with their start and end apart: 33, of which 15 were waited for; matrix products, arithmetic and copies ran while one was open for 5% of the time, Pallas kernels for 13%

profile of v4, /device:TPU:9, one launch (start us, length us, event | category | flops | bytes accessed | tf_op | source)
XLA Modules:
  0.0 225.5 jit_solution(691466658427679076)
XLA Ops:
  8.7 1.8 collective-permute-start
  11.1 5.3 %collective-permute-done = bf16[2,200,256]{2,1,0:T(8,128)(2,1)S(1)} collective-permute-done((bf16[2,200,256]{2,1,0:T(8,128)(2,1)S(1)}, bf16[2,200,256]{2,1,0:T(8,128)(2,1)S(1)}, u32[]{:S(2)}, u32[]{:S(2)}) %collective-permute-start) | collective-permute-done | bytes 204832 | tf_op jit(solution)/shard_map/ppermute | solution.py:108
  16.4 4.4 %collective-permute-done.1 = bf16[2,200,256]{2,1,0:T(8,128)(2,1)S(1)} collective-permute-done((bf16[2,200,256]{2,1,0:T(8,128)(2,1)S(1)}, bf16[2,200,256]{2,1,0:T(8,128)(2,1)S(1)}, u32[]{:S(2)}, u32[]{:S(2)}) %collective-permute-start.1) | collective-permute-done | bytes 204832 | tf_op jit(solution)/shard_map/ppermute | solution.py:108
  22.6 2.9 %norm.1 = (bf16[4,128,896]{2,1,0:T(8,128)(2,1)}, bf16[2,4,128,896]{3,2,1,0:T(8,128)(2,1)}) custom-call(s32[3]{0:T(128)S(1)} %pad_add_fusion.place, bf16[256,3200]{1,0:T(8,128)(2,1)S(1)} %copy-done, f32[1,3200]{1,0:T(1,128)S(1)} %broadcast_in_dim.18.gain), custom_call_target="tpu_custom_call" | custom-call | tf_op jit(solution)/shard_map/norm/pallas_call | solution.py:165
  29.4 21.5 %collective-permute-done.3 = bf16[1,200,256]{2,1,0:T(8,128)(2,1)S(1)} collective-permute-done((bf16[1,200,256]{2,1,0:T(8,128)(2,1)S(1)}, bf16[1,200,256]{2,1,0:T(8,128)(2,1)S(1)}, u32[]{:S(2)}, u32[]{:S(2)}) %collective-permute-start.3) | collective-permute-done | bytes 102432 | tf_op jit(solution)/shard_map/ppermute | solution.py:108
  57.5 17.1 %collective-permute-done.8.xd = bf16[4,128,896]{2,1,0:T(8,128)(2,1)} collective-permute-done((bf16[4,128,896]{2,1,0:T(8,128)(2,1)S(1)}, bf16[4,128,896]{2,1,0:T(8,128)(2,1)}, u32[]{:S(2)}, u32[]{:S(2)}) %collective-permute-start.8) | collective-permute-done | bytes 917536 | tf_op jit(solution)/shard_map/ppermute | solution.py:108
  76.0 16.9 %collective-permute-done.26 = bf16[2,200,1024]{2,1,0:T(8,128)(2,1)S(1)} collective-permute-done((bf16[2,200,1024]{2,1,0:T(8,128)(2,1)S(1)}, bf16[2,200,1024]{2,1,0:T(8,128)(2,1)S(1)}, u32[]{:S(2)}, u32[]{:S(2)}) %collective-permute-start.26) | collective-permute-done | bytes 819232 | tf_op jit(solution)/shard_map/ppermute | solution.py:108
  94.2 17.7 %all-gather.7.cloned.1.call-done = bf16[8,800,256]{2,1,0:T(8,128)(2,1)} async-done(((bf16[2,800,256]{2,1,0:T(8,128)(2,1)}), bf16[8,800,256]{2,1,0:T(8,128)(2,1)}) %all-gather.7.cloned.1.call-update) | async-done | bytes 3276816 | tf_op jit(solution)/shard_map/all_gather | solution.py:130
  112.8 15.1 %collective-permute-done.28.wc = bf16[2,2,200,1024]{3,2,1,0:T(8,128)(2,1)} collective-permute-done((bf16[2,2,200,1024]{3,2,1,0:T(8,128)(2,1)S(1)}, bf16[2,2,200,1024]{3,2,1,0:T(8,128)(2,1)}, u32[]{:S(2)}, u32[]{:S(2)}) %collective-permute-start.28) | collective-permute-done | bytes 1638432 | tf_op jit(solution)/shard_map/ppermute | solution.py:108
  127.9 3.5 %collective-permute-start.29 = (bf16[2,2,200,1024]{3,2,1,0:T(8,128)(2,1)}, bf16[2,2,200,1024]{3,2,1,0:T(8,128)(2,1)}, u32[]{:S(2)}, u32[]{:S(2)}) collective-permute-start(bf16[2,2,200,1024]{3,2,1,0:T(8,128)(2,1)} %collective-permute-done.28.wc), channel_id=1, source_target_pairs={{0,2},{1,3},{2,0},{3,1},{4,6},{5,7},{6,4},{7,5},{8,10},{9,11},{10,... | collective-permute-start | bytes 4915208 | tf_op jit(solution)/shard_map/ppermute | solution.py:108
  132.5 1.9 copy-done.7
  134.5 8.7 %query_key_kernel.1 = (f32[2,1024,256]{2,1,0:T(8,128)S(1)}, f32[2,1024]{1,0:T(2,128)S(1)}) custom-call(s32[3]{0:T(128)S(1)} %pad_add_fusion.place, bf16[2,4,128,896]{3,2,1,0:T(8,128)(2,1)} %get-tuple-element.33.xa, bf16[2,4,128,896]{3,2,1,0:T(8,128)(2,1)} %collective-permute-done.7.xb, bf16[4,128,896]{2,1,0:T(8,128)(2,1)S(1)} %copy-done.3, ...), custom_call_target="tpu_custom_call" | custom-call | flops 3355443200 | bytes 9830400 | tf_op jit(solution)/shard_map/query_key_kernel/pallas_call | solution.py:262
  150.2 2.0 norm_heads.1
  153.8 4.0 %collective-permute-start.16 = (bf16[512,256]{1,0:T(8,128)(2,1)}, bf16[512,256]{1,0:T(8,128)(2,1)}, u32[]{:S(2)}, u32[]{:S(2)}) collective-permute-start(bf16[512,256]{1,0:T(8,128)(2,1)} %get-tuple-element.46), channel_id=1, source_target_pairs={{0,0},{1,1},{2,2},{3,3},{4,4},{5,5},{6,6},{7,7},{8,16},{9,17},{10,... | collective-permute-start | bytes 786440 | tf_op jit(solution)/shard_map/ppermute | solution.py:108
  161.6 7.5 %value_kernel.1 = (bf16[1024,256]{1,0:T(8,128)(2,1)S(1)}, bf16[512,256]{1,0:T(8,128)(2,1)}, bf16[512,256]{1,0:T(8,128)(2,1)}) custom-call(s32[3]{0:T(128)S(1)} %pad_add_fusion.place, bf16[2,4,128,896]{3,2,1,0:T(8,128)(2,1)} %get-tuple-element.33.xa, bf16[2,4,128,896]{3,2,1,0:T(8,128)(2,1)} %collective-permute-done.7.xb, bf16[4,128,896]{2,1,0:T(8,128)(2,1)S(1)} %copy-done.4, ...), custom_call_target="tpu_custom_call" | custom-call | flops 1677721600 | bytes 8192000 | tf_op jit(solution)/shard_map/value_kernel/pallas_call | solution.py:262
  171.7 2.9 %collective-permute-start.18 = (bf16[512,256]{1,0:T(8,128)(2,1)}, bf16[512,256]{1,0:T(8,128)(2,1)}, u32[]{:S(2)}, u32[]{:S(2)}) collective-permute-start(bf16[512,256]{1,0:T(8,128)(2,1)} %get-tuple-element.50), channel_id=1, source_target_pairs={{0,0},{1,1},{2,2},{3,3},{4,4},{5,5},{6,6},{7,7},{8,16},{9,17},{10,... | collective-permute-start | bytes 786440 | tf_op jit(solution)/shard_map/ppermute | solution.py:108
  175.5 3.6 %collective-permute-done.18.v_odd = bf16[512,256]{1,0:T(8,128)(2,1)} collective-permute-done((bf16[512,256]{1,0:T(8,128)(2,1)}, bf16[512,256]{1,0:T(8,128)(2,1)}, u32[]{:S(2)}, u32[]{:S(2)}) %collective-permute-start.18) | collective-permute-done | bytes 262176 | tf_op jit(solution)/shard_map/ppermute | solution.py:108
  183.2 7.6 %attend.1 = (bf16[256,256]{1,0:T(8,128)(2,1)S(1)}, bf16[256,256]{1,0:T(8,128)(2,1)}, bf16[256,256]{1,0:T(8,128)(2,1)S(1)}, bf16[256,256]{1,0:T(8,128)(2,1)S(1)}) custom-call(s32[3]{0:T(128)S(1)} %pad_add_fusion.place, bf16[1024,256]{1,0:T(8,128)(2,1)S(1)} %copy-done.9, bf16[1024,256]{1,0:T(8,128)(2,1)S(1)} %copy-done.11, bf16[512,256]{1,0:T(8,128)(2,1)S(1)} %copy-done.15, ...), custom_call_target="tpu_custom_call" | custom-call | flops 1342177280 | bytes 3145728 | tf_op jit(solution)/shard_map/attend/pallas_call | solution.py:385
  193.3 4.0 %collective-permute-start.20 = (bf16[256,256]{1,0:T(8,128)(2,1)}, bf16[256,256]{1,0:T(8,128)(2,1)}, u32[]{:S(2)}, u32[]{:S(2)}) collective-permute-start(bf16[256,256]{1,0:T(8,128)(2,1)} %get-tuple-element.52), channel_id=1, source_target_pairs={{0,2},{1,3},{2,0},{3,1},{4,6},{5,7},{6,4},{7,5},{8,10},{9,11},{10,... | collective-permute-start | bytes 393224 | tf_op jit(solution)/shard_map/ppermute | solution.py:108
  197.8 2.0 collective-permute-start.23
  201.3 1.9 collective-permute-start.25
  206.3 3.5 %collective-permute-done.24.c30 = bf16[256,256]{1,0:T(8,128)(2,1)} collective-permute-done((bf16[256,256]{1,0:T(8,128)(2,1)}, bf16[256,256]{1,0:T(8,128)(2,1)}, u32[]{:S(2)}, u32[]{:S(2)}) %collective-permute-start.24) | collective-permute-done | bytes 131104 | tf_op jit(solution)/shard_map/ppermute | solution.py:108
  209.8 2.5 %collective-permute-done.25.c31 = bf16[256,256]{1,0:T(8,128)(2,1)} collective-permute-done((bf16[256,256]{1,0:T(8,128)(2,1)}, bf16[256,256]{1,0:T(8,128)(2,1)}, u32[]{:S(2)}, u32[]{:S(2)}) %collective-permute-start.25) | collective-permute-done | bytes 131104 | tf_op jit(solution)/shard_map/ppermute | solution.py:108
  212.3 6.6 %output.1 = bf16[1600,256]{1,0:T(8,128)(2,1)} custom-call(s32[3]{0:T(128)S(1)} %pad_add_fusion.place, bf16[256,256]{1,0:T(8,128)(2,1)S(1)} %get-tuple-element.51.c00, bf16[256,256]{1,0:T(8,128)(2,1)S(1)} %collective-permute-done.19.c01, bf16[256,256]{1,0:T(8,128)(2,1)} %collective-permute-done.20.c10, bf16[256,256]{1,0:T(8,128)(2,1)} %collective-permute-done.21.c11, ...), custom_call_target="tpu_custom_call" | custom-call | flops 1677721600 | bytes 6553600 | tf_op jit(solution)/shard_map/output/pallas_call | solution.py:441
  (116 shorter events, 47.1 us)
Async XLA Ops:
  6.5 49.3 %all-gather.11.cloned.1.call-start = ((), (), s32[]{:S(2)}) async-start(), calls=%async_computation.2 | async-start | bytes 2048000 | tf_op jit(solution)/shard_map/all_gather | solution.py:130
  7.3 104.7 %all-gather.7.cloned.1.call-start = ((), (), s32[]{:S(2)}) async-start(), calls=%async_computation | async-start | bytes 4096000 | tf_op jit(solution)/shard_map/all_gather | solution.py:130
  10.6 10.2 %collective-permute-start.1 = (bf16[2,200,256]{2,1,0:T(8,128)(2,1)S(1)}, bf16[2,200,256]{2,1,0:T(8,128)(2,1)S(1)}, u32[]{:S(2)}, u32[]{:S(2)}) collective-permute-start(bf16[2,200,256]{2,1,0:T(8,128)(2,1)S(1)} %slice.43), channel_id=1, source_target_pairs={{0,4},{1,5},{2,6},{3,7},{4,0},{5,1},{6,2},{7,3},{8,12},{9,13},{10,... | collective-permute-start | bytes 614408 | tf_op jit(solution)/shard_map/ppermute | solution.py:108
  10.9 9.9 %collective-permute-start.2 = (bf16[2,200,256]{2,1,0:T(8,128)(2,1)S(1)}, bf16[2,200,256]{2,1,0:T(8,128)(2,1)S(1)}, u32[]{:S(2)}, u32[]{:S(2)}) collective-permute-start(bf16[2,200,256]{2,1,0:T(8,128)(2,1)S(1)} %slice.44), channel_id=1, source_target_pairs={{0,2},{1,3},{2,0},{3,1},{4,6},{5,7},{6,4},{7,5},{8,10},{9,11},{10,... | collective-permute-start | bytes 614408 | tf_op jit(solution)/shard_map/ppermute | solution.py:108
  21.9 135.9 %all-gather.9.cloned.1.call-start = ((), (), s32[]{:S(2)}) async-start(), calls=%async_computation.1 | async-start | bytes 2048000 | tf_op jit(solution)/shard_map/all_gather | solution.py:130
  25.5 27.8 %collective-permute-start.7 = (bf16[2,4,128,896]{3,2,1,0:T(8,128)(2,1)}, bf16[2,4,128,896]{3,2,1,0:T(8,128)(2,1)}, u32[]{:S(2)}, u32[]{:S(2)}) collective-permute-start(bf16[2,4,128,896]{3,2,1,0:T(8,128)(2,1)} %get-tuple-element.33.xa), channel_id=1, source_target_pairs={{0,2},{1,3},{2,0},{3,1},{4,6},{5,7},{6,4},{7,5},{8,10},{9,11},{10,... | collective-permute-start | bytes 5505032 | tf_op jit(solution)/shard_map/ppermute | solution.py:108
  26.0 27.4 %collective-permute-start.6 = (bf16[4,128,896]{2,1,0:T(8,128)(2,1)}, bf16[4,128,896]{2,1,0:T(8,128)(2,1)S(1)}, u32[]{:S(2)}, u32[]{:S(2)}) collective-permute-start(bf16[4,128,896]{2,1,0:T(8,128)(2,1)} %get-tuple-element.38), channel_id=1, source_target_pairs={{0,4},{1,5},{2,6},{3,7},{4,0},{5,1},{6,2},{7,3},{8,12},{9,13},{10,... | collective-permute-start | bytes 2752520 | tf_op jit(solution)/shard_map/ppermute | solution.py:108
  27.2 23.7 %collective-permute-start.3 = (bf16[1,200,256]{2,1,0:T(8,128)(2,1)S(1)}, bf16[1,200,256]{2,1,0:T(8,128)(2,1)S(1)}, u32[]{:S(2)}, u32[]{:S(2)}) collective-permute-start(bf16[1,200,256]{2,1,0:T(8,128)(2,1)S(1)} %slice.49), channel_id=1, source_target_pairs={{0,6},{1,7},{2,4},{3,5},{4,2},{5,3},{6,0},{7,1},{8,14},{9,15},{10,... | collective-permute-start | bytes 307208 | tf_op jit(solution)/shard_map/ppermute | solution.py:108
  27.7 24.8 %collective-permute-start.4 = (bf16[1,200,256]{2,1,0:T(8,128)(2,1)S(1)}, bf16[1,200,256]{2,1,0:T(8,128)(2,1)S(1)}, u32[]{:S(2)}, u32[]{:S(2)}) collective-permute-start(bf16[1,200,256]{2,1,0:T(8,128)(2,1)S(1)} %slice.48), channel_id=1, source_target_pairs={{0,4},{1,5},{2,6},{3,7},{4,0},{5,1},{6,2},{7,3},{8,12},{9,13},{10,... | collective-permute-start | bytes 307208 | tf_op jit(solution)/shard_map/ppermute | solution.py:108
  28.9 23.6 %collective-permute-start.5 = (bf16[1,200,256]{2,1,0:T(8,128)(2,1)S(1)}, bf16[1,200,256]{2,1,0:T(8,128)(2,1)S(1)}, u32[]{:S(2)}, u32[]{:S(2)}) collective-permute-start(bf16[1,200,256]{2,1,0:T(8,128)(2,1)S(1)} %slice.47), channel_id=1, source_target_pairs={{0,2},{1,3},{2,0},{3,1},{4,6},{5,7},{6,4},{7,5},{8,10},{9,11},{10,... | collective-permute-start | bytes 307208 | tf_op jit(solution)/shard_map/ppermute | solution.py:108
  53.3 21.2 %collective-permute-start.8 = (bf16[4,128,896]{2,1,0:T(8,128)(2,1)S(1)}, bf16[4,128,896]{2,1,0:T(8,128)(2,1)}, u32[]{:S(2)}, u32[]{:S(2)}) collective-permute-start(bf16[4,128,896]{2,1,0:T(8,128)(2,1)S(1)} %collective-permute-done.6.xc), channel_id=1, source_target_pairs={{0,1},{1,0},{2,3},{3,2},{4,5},{5,4},{6,7},{7,6},{8,9},{9,8},{10,11... | collective-permute-start | bytes 2752520 | tf_op jit(solution)/shard_map/ppermute | solution.py:108
  54.7 19.9 %collective-permute-start.9 = (bf16[4,128,896]{2,1,0:T(8,128)(2,1)S(1)}, bf16[4,128,896]{2,1,0:T(8,128)(2,1)}, u32[]{:S(2)}, u32[]{:S(2)}) collective-permute-start(bf16[4,128,896]{2,1,0:T(8,128)(2,1)S(1)} %collective-permute-done.6.xc), channel_id=1, source_target_pairs={{0,2},{1,3},{2,0},{3,1},{4,6},{5,7},{6,4},{7,5},{8,10},{9,11},{10,... | collective-permute-start | bytes 2752520 | tf_op jit(solution)/shard_map/ppermute | solution.py:108
  74.7 18.2 %collective-permute-start.26 = (bf16[2,200,1024]{2,1,0:T(8,128)(2,1)S(1)}, bf16[2,200,1024]{2,1,0:T(8,128)(2,1)S(1)}, u32[]{:S(2)}, u32[]{:S(2)}) collective-permute-start(bf16[2,200,1024]{2,1,0:T(8,128)(2,1)S(1)} %get-tuple-element.58), channel_id=1, source_target_pairs={{0,1},{1,0},{2,3},{3,2},{4,5},{5,4},{6,7},{7,6},{8,9},{9,8},{10,11... | collective-permute-start | bytes 2457608 | tf_op jit(solution)/shard_map/ppermute | solution.py:108
  93.0 34.9 %collective-permute-start.28 = (bf16[2,2,200,1024]{3,2,1,0:T(8,128)(2,1)S(1)}, bf16[2,2,200,1024]{3,2,1,0:T(8,128)(2,1)}, u32[]{:S(2)}, u32[]{:S(2)}) collective-permute-start(bf16[2,2,200,1024]{3,2,1,0:T(8,128)(2,1)S(1)} %pad_maximum_fusion.wa), channel_id=1, source_target_pairs={{0,4},{1,5},{2,6},{3,7},{4,0},{5,1},{6,2},{7,3},{8,12},{9,13},{10,... | collective-permute-start | bytes 4915208 | tf_op jit(solution)/shard_map/ppermute | solution.py:108
  112.0 19.4 %collective-permute-start.10 = (bf16[4,128,896]{2,1,0:T(8,128)(2,1)}, bf16[4,128,896]{2,1,0:T(8,128)(2,1)S(1)}, u32[]{:S(2)}, u32[]{:S(2)}) collective-permute-start(bf16[4,128,896]{2,1,0:T(8,128)(2,1)} %collective-permute-done.8.xd), channel_id=1, source_target_pairs={{0,2},{1,3},{2,0},{3,1},{4,6},{5,7},{6,4},{7,5},{8,10},{9,11},{10,... | collective-permute-start | bytes 2752520 | tf_op jit(solution)/shard_map/ppermute | solution.py:108
  112.7 84.7 %collective-permute-start.27 = (bf16[2,2,200,1024]{3,2,1,0:T(8,128)(2,1)S(1)}, bf16[2,2,200,1024]{3,2,1,0:T(8,128)(2,1)}, u32[]{:S(2)}, u32[]{:S(2)}) collective-permute-start(bf16[2,2,200,1024]{3,2,1,0:T(8,128)(2,1)S(1)} %pad_maximum_fusion.wa), channel_id=1, source_target_pairs={{0,2},{1,3},{2,0},{3,1},{4,6},{5,7},{6,4},{7,5},{8,10},{9,11},{10,... | collective-permute-start | bytes 4915208 | tf_op jit(solution)/shard_map/ppermute | solution.py:108
  127.9 69.9 %collective-permute-start.29 = (bf16[2,2,200,1024]{3,2,1,0:T(8,128)(2,1)}, bf16[2,2,200,1024]{3,2,1,0:T(8,128)(2,1)}, u32[]{:S(2)}, u32[]{:S(2)}) collective-permute-start(bf16[2,2,200,1024]{3,2,1,0:T(8,128)(2,1)} %collective-permute-done.28.wc), channel_id=1, source_target_pairs={{0,2},{1,3},{2,0},{3,1},{4,6},{5,7},{6,4},{7,5},{8,10},{9,11},{10,... | collective-permute-start | bytes 4915208 | tf_op jit(solution)/shard_map/ppermute | solution.py:108
  153.8 17.2 %collective-permute-start.15 = (bf16[512,256]{1,0:T(8,128)(2,1)}, bf16[512,256]{1,0:T(8,128)(2,1)S(1)}, u32[]{:S(2)}, u32[]{:S(2)}) collective-permute-start(bf16[512,256]{1,0:T(8,128)(2,1)} %get-tuple-element.45), channel_id=1, source_target_pairs={{0,8},{1,9},{2,10},{3,11},{4,12},{5,13},{6,14},{7,15},{8,0},{9,1},... | collective-permute-start | bytes 786440 | tf_op jit(solution)/shard_map/ppermute | solution.py:108
  153.8 21.6 %collective-permute-start.16 = (bf16[512,256]{1,0:T(8,128)(2,1)}, bf16[512,256]{1,0:T(8,128)(2,1)}, u32[]{:S(2)}, u32[]{:S(2)}) collective-permute-start(bf16[512,256]{1,0:T(8,128)(2,1)} %get-tuple-element.46), channel_id=1, source_target_pairs={{0,0},{1,1},{2,2},{3,3},{4,4},{5,5},{6,6},{7,7},{8,16},{9,17},{10,... | collective-permute-start | bytes 786440 | tf_op jit(solution)/shard_map/ppermute | solution.py:108
  197.3 9.0 %collective-permute-start.21 = (bf16[256,256]{1,0:T(8,128)(2,1)}, bf16[256,256]{1,0:T(8,128)(2,1)}, u32[]{:S(2)}, u32[]{:S(2)}) collective-permute-start(bf16[256,256]{1,0:T(8,128)(2,1)} %get-tuple-element.52), channel_id=1, source_target_pairs={{0,3},{1,2},{2,1},{3,0},{4,7},{5,6},{6,5},{7,4},{8,11},{9,10},{10,... | collective-permute-start | bytes 393224 | tf_op jit(solution)/shard_map/ppermute | solution.py:108
  197.4 8.9 %collective-permute-start.22 = (bf16[256,256]{1,0:T(8,128)(2,1)}, bf16[256,256]{1,0:T(8,128)(2,1)}, u32[]{:S(2)}, u32[]{:S(2)}) collective-permute-start(bf16[256,256]{1,0:T(8,128)(2,1)} %copy-done.17), channel_id=1, source_target_pairs={{0,4},{1,5},{2,6},{3,7},{4,0},{5,1},{6,2},{7,3},{8,12},{9,13},{10,... | collective-permute-start | bytes 393224 | tf_op jit(solution)/shard_map/ppermute | solution.py:108
  197.8 8.5 %collective-permute-start.23 = (bf16[256,256]{1,0:T(8,128)(2,1)}, bf16[256,256]{1,0:T(8,128)(2,1)}, u32[]{:S(2)}, u32[]{:S(2)}) collective-permute-start(bf16[256,256]{1,0:T(8,128)(2,1)} %copy-done.17), channel_id=1, source_target_pairs={{0,5},{1,4},{2,7},{3,6},{4,1},{5,0},{6,3},{7,2},{8,13},{9,12},{10,... | collective-permute-start | bytes 393224 | tf_op jit(solution)/shard_map/ppermute | solution.py:108
  199.8 10.0 %collective-permute-start.24 = (bf16[256,256]{1,0:T(8,128)(2,1)}, bf16[256,256]{1,0:T(8,128)(2,1)}, u32[]{:S(2)}, u32[]{:S(2)}) collective-permute-start(bf16[256,256]{1,0:T(8,128)(2,1)} %copy-done.16), channel_id=1, source_target_pairs={{0,6},{1,7},{2,4},{3,5},{4,2},{5,3},{6,0},{7,1},{8,14},{9,15},{10,... | collective-permute-start | bytes 393224 | tf_op jit(solution)/shard_map/ppermute | solution.py:108
  201.3 11.0 %collective-permute-start.25 = (bf16[256,256]{1,0:T(8,128)(2,1)}, bf16[256,256]{1,0:T(8,128)(2,1)}, u32[]{:S(2)}, u32[]{:S(2)}) collective-permute-start(bf16[256,256]{1,0:T(8,128)(2,1)} %copy-done.16), channel_id=1, source_target_pairs={{0,7},{1,6},{2,5},{3,4},{4,3},{5,2},{6,1},{7,0},{8,15},{9,14},{10,... | collective-permute-start | bytes 393224 | tf_op jit(solution)/shard_map/ppermute | solution.py:108
  (29 other events, 85.6 us)
Sparse Core Ops, SparseCore 0:
  8.9 38.0 all-gather.10
  48.6 63.3 all-gather.6
  113.5 37.9 all-gather.8

commit v5 on v4

--- a/solution.py
+++ b/solution.py
@@ -96,7 +96,7 @@
 VMEM = pl.BlockSpec(memory_space=pltpu.VMEM)
 SMEM = pl.BlockSpec(memory_space=pltpu.SMEM)
 HBM = pl.BlockSpec(memory_space=pltpu.HBM)
-MIB = 1024 * 1024
+KERNEL_VMEM = 60 * 1024 * 1024
 
 
 def permuted(x, to):
@@ -170,7 +170,7 @@
         ),
         in_specs=[SMEM, VMEM, VMEM],
         out_specs=(VMEM, VMEM),
-        compiler_params=pltpu.CompilerParams(vmem_limit_bytes=16 * MIB),
+        compiler_params=pltpu.CompilerParams(vmem_limit_bytes=KERNEL_VMEM),
         name="norm",
     )(place, tokens, gain[None])
 
@@ -273,7 +273,7 @@
             pltpu.SemaphoreType.DMA((slabs,)),
             pltpu.SemaphoreType.DMA,
         ],
-        compiler_params=pltpu.CompilerParams(vmem_limit_bytes=28 * MIB),
+        compiler_params=pltpu.CompilerParams(vmem_limit_bytes=KERNEL_VMEM),
         cost_estimate=pl.CostEstimate(
             flops=2 * kinds * slab * slabs * rows * width,
             bytes_accessed=2 * slabs * rows * (kinds * width + slab),
@@ -324,7 +324,7 @@
             pltpu.VMEM((slab, width), bf16),
             pltpu.SemaphoreType.DMA((3,)),
         ],
-        compiler_params=pltpu.CompilerParams(vmem_limit_bytes=16 * MIB),
+        compiler_params=pltpu.CompilerParams(vmem_limit_bytes=KERNEL_VMEM),
         name="norm_heads",
     )(place, both, mine, other, q_gain, k_gain)
 
@@ -393,7 +393,7 @@
             pltpu.VMEM((ext, width), bf16),
             pltpu.SemaphoreType.DMA((7,)),
         ],
-        compiler_params=pltpu.CompilerParams(vmem_limit_bytes=24 * MIB),
+        compiler_params=pltpu.CompilerParams(vmem_limit_bytes=KERNEL_VMEM),
         cost_estimate=pl.CostEstimate(
             flops=4 * slab * window * width,
             bytes_accessed=4 * ext * width + 4 * slab * width,
@@ -405,24 +405,30 @@
 
 def out_kernel(
     place, c00, c01, c10, c11, c20, c21, c30, c31, wa, wb, wc, wd, residual, scale,
-    out, c_all, w_all, total, sems,
+    out, c_all, w_all, total, c_sem, w_sem,
 ):
-    q = place[1]
-    copies = []
-    for r, w in enumerate((wa, wb, wc, wd)):
-        copy = pltpu.make_async_copy(w, w_all.at[r], sems.at[r])
-        copy.start()
-        copies.append(copy)
+    z, q, y = place[0], place[1], place[2]
     width = c00.shape[1]
+    c_copies = []
     for r, pair in enumerate(((c00, c01), (c10, c11), (c20, c21), (c30, c31))):
         at = pl.multiple_of((q ^ r) * width, width)
         for i in range(2):
-            c_all[i, :, pl.ds(at, width)] = pair[i][...]
+            dst = c_all.at[i, :, pl.ds(at, width)]
+            c_copies.append(pltpu.make_async_copy(pair[i], dst, c_sem.at[r, i]))
+    start(c_copies)
+    w_copies = [
+        pltpu.make_async_copy(w, w_all.at[r], w_sem.at[r]) for r, w in enumerate((wa, wb, wc, wd))
+    ]
+    start(w_copies)
+    column = as_column(scale[...])[:out.shape[0]]
+    column = jnp.tile(column, (1, out.shape[1] // 128))
+    wait(c_copies)
     rows = wa.shape[2]
     for r in range(SLAB):
-        copies[r].wait()
+        w_copies[r].wait()
         for j in range(2):
-            at = pl.multiple_of((j * SLAB + (q ^ r)) * rows, 8)
+            slab = jnp.where(z // 2 == y, (z % 2) ^ j, jnp.where(z < 2, j, 1 - j))
+            at = pl.multiple_of((slab * SLAB + (q ^ r)) * rows, 8)
             term = None
             for i in range(2):
                 part = lax.dot_general(
@@ -431,25 +437,27 @@
                 )
                 term = part if term is None else term + part
             total[pl.ds(at, rows), :] = term
-    out[...] = (residual[...].astype(jnp.float32) + scale[...] * total[...]).astype(jnp.bfloat16)
+    out[...] = (residual[...].astype(jnp.float32) + column * total[...]).astype(jnp.bfloat16)
 
 
 def output(place, blocks, pieces, residual, scale):
     count, width = blocks[0].shape
     rows, depth = pieces[0].shape[2:]
     share = residual.shape[0]
+    scale = jnp.pad(scale, (0, -share % 128))[None]
     return pl.pallas_call(
         out_kernel,
         out_shape=jax.ShapeDtypeStruct((share, count), jnp.bfloat16),
-        in_specs=[SMEM] + [VMEM] * 8 + [HBM] * 4 + [VMEM] * 2,
+        in_specs=[SMEM] + [HBM] * 12 + [VMEM] * 2,
         out_specs=VMEM,
         scratch_shapes=[
             pltpu.VMEM((2, count, depth), jnp.bfloat16),
             pltpu.VMEM((SLAB, 2, 2, rows, depth), jnp.bfloat16),
             pltpu.VMEM((share, count), jnp.float32),
+            pltpu.SemaphoreType.DMA((SLAB, 2)),
             pltpu.SemaphoreType.DMA((SLAB,)),
         ],
-        compiler_params=pltpu.CompilerParams(vmem_limit_bytes=24 * MIB),
+        compiler_params=pltpu.CompilerParams(vmem_limit_bytes=KERNEL_VMEM),
         cost_estimate=pl.CostEstimate(
             flops=4 * share * count * depth,
             bytes_accessed=4 * share * depth,
@@ -481,7 +489,15 @@
     slab, half = SLAB * count, 2 * count
     f32, bf16 = jnp.float32, jnp.bfloat16
 
-    out_all = z_line(jnp.transpose(out_weight))
+    out_own = jnp.transpose(out_weight)
+    out_near, out_mid1 = even_pair(out_own), odd_pair(out_own)
+    out_end1, out_mid2 = even_pair(out_mid1), odd_pair(out_near)
+    out_end2 = even_pair(out_mid2)
+    inner, home = (z == 1) | (z == 2), z // 2 == tp
+    close = jnp.stack([out_own, out_near])
+    far = jnp.stack(
+        [jnp.where(inner, out_mid1, out_end1), jnp.where(inner, out_mid2, out_end2)]
+    )
 
     by_kind = jnp.transpose(qkv_weight, (1, 0, 2))
     cut = [lax.dynamic_slice_in_dim(by_kind, (q ^ r) * width, width, 2) for r in range(SLAB)]
@@ -492,22 +508,19 @@
     tied_cut = tied(own_qk, first, pair, *[c[2:] for c in cut])
     _, first, pair = tied_cut[:3]
     own_v = rows_of_slab(q, tied_cut[3:])
-    w_v = z_line(tied(own_v, w_qk)[0])
+    w_v = z_line(own_v)
     x2a = in_slab(first, 2)
     x1 = in_slab(pair, 1)
     own_v, x2a, x1 = tied(own_v, x2a, x1)
     x2b, x3a = across(x2a), in_slab(x2a, 1)
     x3b = in_slab(x2b, 1)
-    xs = (pair, x1, x2a, x2b, x3a, x3b)
-
-    close, far = out_all[:2], out_all[2:]
-    close, far, x2b, x3a = tied(close, far, x2b, x3a)
-    wa = jnp.stack(
-        [jnp.where(tp == 0, close, far), across(jnp.where(tp == 0, far, close))]
-    )
+
+    wa = jnp.stack([jnp.where(home, close, far), across(jnp.where(home, far, close))])
     wc = in_slab(wa, 2)
     pieces = (wa, in_slab(wa, 1), wc, in_slab(wc, 1))
 
+    w_qk, x3b, *pieces = tied(w_qk, x3b, *pieces)
+    xs = (pair, x1, x2a, x2b, x3a, x3b)
     both, squares = project(
         query_key_kernel,
         (jax.ShapeDtypeStruct((2, slab, width), f32), jax.ShapeDtypeStruct((2, slab), f32)),
@@ -544,7 +557,7 @@
 
     share = layer_scale.shape[0]
     residual = jnp.transpose(lax.dynamic_slice_in_dim(tokens, tp * share, share, 1))
-    return jnp.transpose(output(place, spread, pieces, residual, layer_scale[:, None]))
+    return jnp.transpose(output(place, spread, pieces, residual, layer_scale))
 
 
 def solution(mesh):

time: 227 us -> 300 us (1.32)
  waiting for transfers between devices: 112 us -> 177 us
  local copies, waits for them, and re-layouts: 23.5 us -> 12.6 us
  Pallas kernels: 35.3 us -> 44.3 us
  starting transfers between devices: 38.1 us -> 45.2 us
  other arithmetic: 3.03 us -> 6.52 us
    ppermute x30 -> x35, waiting for transfers between devices: 93.5 us -> 177 us  [permuted(): return lax.ppermute(x, ('seq', 'tp'), pairs)]
    all_gather x3 -> x2, waiting for transfers between devices: 17.8 us -> 0.01 us  [z_line(): return lax.all_gather(x, 'seq', axis_index_groups=groups)]
    unnamed x41 -> x53, local copies, waits for them, and re-layouts: 17.4 us -> 4.49 us
    ppermute x30 -> x35, starting transfers between devices: 38 us -> 45.1 us  [permuted(): return lax.ppermute(x, ('seq', 'tp'), pairs)]
  transfers between devices with their start and end apart: 33 -> 37, of which waited for: 15 -> 16; matrix products, arithmetic and copies ran while one was open for 5% -> 4% of each run, Pallas kernels for 13% -> 9%
where the time goes in v5:
time: 300 us; the launch traced here: 299 us
  waiting for transfers between devices  177 us (59%)
  starting transfers between devices  45.2 us (15%)
  Pallas kernels  44.3 us (15%)
  between operations  13.8 us (5%)
  local copies, waits for them, and re-layouts  12.6 us (4%)
  other arithmetic  6.52 us (2%)
    ppermute x35, waiting for transfers between devices, permuted(): return lax.ppermute(x, ('seq', 'tp'), pairs)  177 us
    ppermute x35, starting transfers between devices, permuted(): return lax.ppermute(x, ('seq', 'tp'), pairs)  45.1 us
    pallas_call x2, Pallas kernels, project(): pl.pallas_call(kernel, out_shape=out_shape, in_specs=[SMEM] + [HBM] * 7,...  19.2 us
    pallas_call x1, Pallas kernels, output(): pl.pallas_call(out_kernel, out_shape=jax.ShapeDtypeStruct((share, count),...  8.58 us
    pallas_call x1, Pallas kernels, attend(): pl.pallas_call(attend_kernel, out_shape=(jax.ShapeDtypeStruct((count, wid...  8.41 us
  transfers between devices with their start and end apart: 37, of which 16 were waited for; matrix products, arithmetic and copies ran while one was open for 4% of the time, Pallas kernels for 9%

profile of v5, /device:TPU:9, one launch (start us, length us, event | category | flops | bytes accessed | tf_op | source)
XLA Modules:
  0.0 299.2 jit_solution(251364178900051350)
XLA Ops:
  10.3 5.3 %collective-permute-done = bf16[2,200,256]{2,1,0:T(8,128)(2,1)S(1)} collective-permute-done((bf16[2,200,256]{2,1,0:T(8,128)(2,1)S(1)}, bf16[2,200,256]{2,1,0:T(8,128)(2,1)S(1)}, u32[]{:S(2)}, u32[]{:S(2)}) %collective-permute-start) | collective-permute-done | bytes 204832 | tf_op jit(solution)/shard_map/ppermute | solution.py:108
  15.6 4.4 %collective-permute-done.1 = bf16[2,200,256]{2,1,0:T(8,128)(2,1)S(1)} collective-permute-done((bf16[2,200,256]{2,1,0:T(8,128)(2,1)S(1)}, bf16[2,200,256]{2,1,0:T(8,128)(2,1)S(1)}, u32[]{:S(2)}, u32[]{:S(2)}) %collective-permute-start.1) | collective-permute-done | bytes 204832 | tf_op jit(solution)/shard_map/ppermute | solution.py:108
  21.2 4.5 %collective-permute-start.12 = (bf16[200,1024]{1,0:T(8,128)(2,1)S(1)}, bf16[200,1024]{1,0:T(8,128)(2,1)S(1)}, u32[]{:S(2)}, u32[]{:S(2)}) collective-permute-start(bf16[200,1024]{1,0:T(8,128)(2,1)S(1)} %bitcast.37), channel_id=1, source_target_pairs={{0,0},{1,1},{2,2},{3,3},{4,4},{5,5},{6,6},{7,7},{8,16},{9,17},{10,... | collective-permute-start | bytes 1228808 | tf_op jit(solution)/shard_map/ppermute | solution.py:108
  25.7 6.1 %collective-permute-done.11 = bf16[200,1024]{1,0:T(8,128)(2,1)S(1)} collective-permute-done((bf16[200,1024]{1,0:T(8,128)(2,1)S(1)}, bf16[200,1024]{1,0:T(8,128)(2,1)S(1)}, u32[]{:S(2)}, u32[]{:S(2)}) %collective-permute-start.11) | collective-permute-done | bytes 409632 | tf_op jit(solution)/shard_map/ppermute | solution.py:108
  31.8 3.2 %collective-permute-start.14 = (bf16[200,1024]{1,0:T(8,128)(2,1)S(1)}, bf16[200,1024]{1,0:T(8,128)(2,1)S(1)}, u32[]{:S(2)}, u32[]{:S(2)}) collective-permute-start(bf16[200,1024]{1,0:T(8,128)(2,1)S(1)} %collective-permute-done.11), channel_id=1, source_target_pairs={{0,0},{1,1},{2,2},{3,3},{4,4},{5,5},{6,6},{7,7},{8,16},{9,17},{10,... | collective-permute-start | bytes 1228808 | tf_op jit(solution)/shard_map/ppermute | solution.py:108
  35.0 5.5 %collective-permute-done.12 = bf16[200,1024]{1,0:T(8,128)(2,1)S(1)} collective-permute-done((bf16[200,1024]{1,0:T(8,128)(2,1)S(1)}, bf16[200,1024]{1,0:T(8,128)(2,1)S(1)}, u32[]{:S(2)}, u32[]{:S(2)}) %collective-permute-start.12) | collective-permute-done | bytes 409632 | tf_op jit(solution)/shard_map/ppermute | solution.py:108
  40.5 26.3 %collective-permute-done.14 = bf16[200,1024]{1,0:T(8,128)(2,1)S(1)} collective-permute-done((bf16[200,1024]{1,0:T(8,128)(2,1)S(1)}, bf16[200,1024]{1,0:T(8,128)(2,1)S(1)}, u32[]{:S(2)}, u32[]{:S(2)}) %collective-permute-start.14) | collective-permute-done | bytes 409632 | tf_op jit(solution)/shard_map/ppermute | solution.py:108
  66.9 33.1 %collective-permute-done.15 = bf16[200,1024]{1,0:T(8,128)(2,1)S(1)} collective-permute-done((bf16[200,1024]{1,0:T(8,128)(2,1)S(1)}, bf16[200,1024]{1,0:T(8,128)(2,1)S(1)}, u32[]{:S(2)}, u32[]{:S(2)}) %collective-permute-start.15) | collective-permute-done | bytes 409632 | tf_op jit(solution)/shard_map/ppermute | solution.py:108
  106.2 3.6 %norm.1 = (bf16[4,128,896]{2,1,0:T(8,128)(2,1)}, bf16[2,4,128,896]{3,2,1,0:T(8,128)(2,1)}) custom-call(s32[3]{0:T(128)} %pad_add_fusion.place, bf16[256,3200]{1,0:T(8,128)(2,1)} %tokens.1, f32[1,3200]{1,0:T(1,128)} %broadcast_in_dim.18.gain), custom_call_target="tpu_custom_call" | custom-call | tf_op jit(solution)/shard_map/norm/pallas_call | solution.py:165
  111.9 7.4 %collective-permute-done.16 = bf16[2,200,1024]{2,1,0:T(8,128)(2,1)} collective-permute-done((bf16[2,200,1024]{2,1,0:T(8,128)(2,1)}, bf16[2,200,1024]{2,1,0:T(8,128)(2,1)}, u32[]{:S(2)}, u32[]{:S(2)}) %collective-permute-start.16) | collective-permute-done | bytes 819232 | tf_op jit(solution)/shard_map/ppermute | solution.py:108
  122.3 4.4 %collective-permute-start.3 = (bf16[1,200,256]{2,1,0:T(8,128)(2,1)S(1)}, bf16[1,200,256]{2,1,0:T(8,128)(2,1)S(1)}, u32[]{:S(2)}, u32[]{:S(2)}) collective-permute-start(bf16[1,200,256]{2,1,0:T(8,128)(2,1)S(1)} %copy-done.16), channel_id=1, source_target_pairs={{0,6},{1,7},{2,4},{3,5},{4,2},{5,3},{6,0},{7,1},{8,14},{9,15},{10,... | collective-permute-start | bytes 307208 | tf_op jit(solution)/shard_map/ppermute | solution.py:108
  126.9 54.3 %collective-permute-done.3 = bf16[1,200,256]{2,1,0:T(8,128)(2,1)S(1)} collective-permute-done((bf16[1,200,256]{2,1,0:T(8,128)(2,1)S(1)}, bf16[1,200,256]{2,1,0:T(8,128)(2,1)S(1)}, u32[]{:S(2)}, u32[]{:S(2)}) %collective-permute-start.3) | collective-permute-done | bytes 102432 | tf_op jit(solution)/shard_map/ppermute | solution.py:108
  185.7 19.6 %collective-permute-done.8.xd = bf16[4,128,896]{2,1,0:T(8,128)(2,1)S(1)} collective-permute-done((bf16[4,128,896]{2,1,0:T(8,128)(2,1)}, bf16[4,128,896]{2,1,0:T(8,128)(2,1)S(1)}, u32[]{:S(2)}, u32[]{:S(2)}) %collective-permute-start.8) | collective-permute-done | bytes 917536 | tf_op jit(solution)/shard_map/ppermute | solution.py:108
  210.3 11.0 %query_key_kernel.1 = (f32[2,1024,256]{2,1,0:T(8,128)}, f32[2,1024]{1,0:T(2,128)}) custom-call(s32[3]{0:T(128)} %pad_add_fusion.place, bf16[2,4,128,896]{3,2,1,0:T(8,128)(2,1)} %get-tuple-element.36.xa, bf16[2,4,128,896]{3,2,1,0:T(8,128)(2,1)} %copy-done.2, bf16[4,128,896]{2,1,0:T(8,128)(2,1)} %collective-permute-done.6.xc, bf16[4,128,896]{2,1,0:T(8,128)(2,1)} %copy-done.5, ...), custom_call_target="tpu_custom_call" | custom-call | flops 3355443200 | bytes 9830400 | tf_op jit(solution)/shard_map/query_key_kernel/pallas_call | solution.py:262
  228.3 8.2 %value_kernel.1 = (bf16[1024,256]{1,0:T(8,128)(2,1)}, bf16[512,256]{1,0:T(8,128)(2,1)}, bf16[512,256]{1,0:T(8,128)(2,1)}) custom-call(s32[3]{0:T(128)} %pad_add_fusion.place, bf16[2,4,128,896]{3,2,1,0:T(8,128)(2,1)} %get-tuple-element.36.xa, bf16[2,4,128,896]{3,2,1,0:T(8,128)(2,1)} %copy-done.2, bf16[4,128,896]{2,1,0:T(8,128)(2,1)} %collective-permute-done.6.xc, ...), custom_call_target="tpu_custom_call" | custom-call | flops 1677721600 | bytes 8192000 | tf_op jit(solution)/shard_map/value_kernel/pallas_call | solution.py:262
  236.5 2.4 collective-permute-start.26
  239.0 3.5 %collective-permute-start.27 = (bf16[512,256]{1,0:T(8,128)(2,1)}, bf16[512,256]{1,0:T(8,128)(2,1)S(1)}, u32[]{:S(2)}, u32[]{:S(2)}) collective-permute-start(bf16[512,256]{1,0:T(8,128)(2,1)} %get-tuple-element.54), channel_id=1, source_target_pairs={{0,0},{1,1},{2,2},{3,3},{4,4},{5,5},{6,6},{7,7},{8,16},{9,17},{10,... | collective-permute-start | bytes 786440 | tf_op jit(solution)/shard_map/ppermute | solution.py:108
  243.1 4.5 %norm_heads.1 = (bf16[1024,256]{1,0:T(8,128)(2,1)}, bf16[1024,256]{1,0:T(8,128)(2,1)}, bf16[512,256]{1,0:T(8,128)(2,1)}, bf16[512,256]{1,0:T(8,128)(2,1)}) custom-call(s32[3]{0:T(128)} %pad_add_fusion.place, f32[2,1024,256]{2,1,0:T(8,128)} %get-tuple-element.46.both, f32[2,1024]{1,0:T(2,128)} %copy-done.17, f32[2,1024]{1,0:T(2,128)} %copy-done.20, ...), custom_call_target="tpu_custom_call" | custom-call | tf_op jit(solution)/shard_map/norm_heads/pallas_call | solution.py:316
  250.5 3.5 %collective-permute-done.24.k_even = bf16[512,256]{1,0:T(8,128)(2,1)S(1)} collective-permute-done((bf16[512,256]{1,0:T(8,128)(2,1)}, bf16[512,256]{1,0:T(8,128)(2,1)S(1)}, u32[]{:S(2)}, u32[]{:S(2)}) %collective-permute-start.24) | collective-permute-done | bytes 262176 | tf_op jit(solution)/shard_map/ppermute | solution.py:108
  256.6 8.4 %attend.1 = (bf16[256,256]{1,0:T(8,128)(2,1)}, bf16[256,256]{1,0:T(8,128)(2,1)}, bf16[256,256]{1,0:T(8,128)(2,1)}, bf16[256,256]{1,0:T(8,128)(2,1)}) custom-call(s32[3]{0:T(128)} %pad_add_fusion.place, bf16[1024,256]{1,0:T(8,128)(2,1)} %get-tuple-element.48.query, bf16[1024,256]{1,0:T(8,128)(2,1)} %get-tuple-element.49.keys, bf16[512,256]{1,0:T(8,128)(2,1)} %copy-done.24, ...), custom_call_target="tpu_custom_call" | custom-call | flops 1342177280 | bytes 3145728 | tf_op jit(solution)/shard_map/attend/pallas_call | solution.py:385
  265.3 2.9 collective-permute-start.29
  270.7 4.7 %collective-permute-start.33 = (bf16[256,256]{1,0:T(8,128)(2,1)}, bf16[256,256]{1,0:T(8,128)(2,1)S(1)}, u32[]{:S(2)}, u32[]{:S(2)}) collective-permute-start(bf16[256,256]{1,0:T(8,128)(2,1)} %get-tuple-element.58), channel_id=1, source_target_pairs={{0,6},{1,7},{2,4},{3,5},{4,2},{5,3},{6,0},{7,1},{8,14},{9,15},{10,... | collective-permute-start | bytes 393224 | tf_op jit(solution)/shard_map/ppermute | solution.py:108
  277.7 3.8 %collective-permute-done.33.c30 = bf16[256,256]{1,0:T(8,128)(2,1)S(1)} collective-permute-done((bf16[256,256]{1,0:T(8,128)(2,1)}, bf16[256,256]{1,0:T(8,128)(2,1)S(1)}, u32[]{:S(2)}, u32[]{:S(2)}) %collective-permute-start.33) | collective-permute-done | bytes 131104 | tf_op jit(solution)/shard_map/ppermute | solution.py:108
  283.8 8.6 %output.1 = bf16[1600,256]{1,0:T(8,128)(2,1)} custom-call(s32[3]{0:T(128)} %pad_add_fusion.place, bf16[256,256]{1,0:T(8,128)(2,1)} %get-tuple-element.55.c00, bf16[256,256]{1,0:T(8,128)(2,1)} %copy-done.7, bf16[256,256]{1,0:T(8,128)(2,1)} %copy-done.8, bf16[256,256]{1,0:T(8,128)(2,1)} %copy-done.9, bf16[256,256]{1,0:T(8,128)(2,1)} %copy-done.10, ...), custom_call_target="tpu_custom_call" | custom-call | flops 1677721600 | bytes 6553600 | tf_op jit(solution)/shard_map/output/pallas_call | solution.py:448
  (138 shorter events, 46.1 us)
Async XLA Ops:
  6.5 203.5 %all-gather.5.cloned.1.call-start = ((), (), s32[]{:S(2)}) async-start(), calls=%async_computation | async-start | bytes 4096000 | tf_op jit(solution)/shard_map/all_gather | solution.py:130
  9.8 10.2 %collective-permute-start.1 = (bf16[2,200,256]{2,1,0:T(8,128)(2,1)S(1)}, bf16[2,200,256]{2,1,0:T(8,128)(2,1)S(1)}, u32[]{:S(2)}, u32[]{:S(2)}) collective-permute-start(bf16[2,200,256]{2,1,0:T(8,128)(2,1)S(1)} %slice.33), channel_id=1, source_target_pairs={{0,4},{1,5},{2,6},{3,7},{4,0},{5,1},{6,2},{7,3},{8,12},{9,13},{10,... | collective-permute-start | bytes 614408 | tf_op jit(solution)/shard_map/ppermute | solution.py:108
  10.1 9.9 %collective-permute-start.2 = (bf16[2,200,256]{2,1,0:T(8,128)(2,1)S(1)}, bf16[2,200,256]{2,1,0:T(8,128)(2,1)S(1)}, u32[]{:S(2)}, u32[]{:S(2)}) collective-permute-start(bf16[2,200,256]{2,1,0:T(8,128)(2,1)S(1)} %slice.34), channel_id=1, source_target_pairs={{0,2},{1,3},{2,0},{3,1},{4,6},{5,7},{6,4},{7,5},{8,10},{9,11},{10,... | collective-permute-start | bytes 614408 | tf_op jit(solution)/shard_map/ppermute | solution.py:108
  21.1 207.2 %all-gather.7.cloned.1.call-start = ((), (), s32[]{:S(2)}) async-start(), calls=%async_computation.1 | async-start | bytes 2048000 | tf_op jit(solution)/shard_map/all_gather | solution.py:130
  21.2 10.6 %collective-permute-start.11 = (bf16[200,1024]{1,0:T(8,128)(2,1)S(1)}, bf16[200,1024]{1,0:T(8,128)(2,1)S(1)}, u32[]{:S(2)}, u32[]{:S(2)}) collective-permute-start(bf16[200,1024]{1,0:T(8,128)(2,1)S(1)} %bitcast.36), channel_id=1, source_target_pairs={{0,8},{1,9},{2,10},{3,11},{4,12},{5,13},{6,14},{7,15},{8,0},{9,1},... | collective-permute-start | bytes 1228808 | tf_op jit(solution)/shard_map/ppermute | solution.py:108
  21.2 19.3 %collective-permute-start.12 = (bf16[200,1024]{1,0:T(8,128)(2,1)S(1)}, bf16[200,1024]{1,0:T(8,128)(2,1)S(1)}, u32[]{:S(2)}, u32[]{:S(2)}) collective-permute-start(bf16[200,1024]{1,0:T(8,128)(2,1)S(1)} %bitcast.37), channel_id=1, source_target_pairs={{0,0},{1,1},{2,2},{3,3},{4,4},{5,5},{6,6},{7,7},{8,16},{9,17},{10,... | collective-permute-start | bytes 1228808 | tf_op jit(solution)/shard_map/ppermute | solution.py:108
  31.8 35.0 %collective-permute-start.14 = (bf16[200,1024]{1,0:T(8,128)(2,1)S(1)}, bf16[200,1024]{1,0:T(8,128)(2,1)S(1)}, u32[]{:S(2)}, u32[]{:S(2)}) collective-permute-start(bf16[200,1024]{1,0:T(8,128)(2,1)S(1)} %collective-permute-done.11), channel_id=1, source_target_pairs={{0,0},{1,1},{2,2},{3,3},{4,4},{5,5},{6,6},{7,7},{8,16},{9,17},{10,... | collective-permute-start | bytes 1228808 | tf_op jit(solution)/shard_map/ppermute | solution.py:108
  40.5 26.3 %collective-permute-start.13 = (bf16[200,1024]{1,0:T(8,128)(2,1)S(1)}, bf16[200,1024]{1,0:T(8,128)(2,1)}, u32[]{:S(2)}, u32[]{:S(2)}) collective-permute-start(bf16[200,1024]{1,0:T(8,128)(2,1)S(1)} %collective-permute-done.12), channel_id=1, source_target_pairs={{0,8},{1,9},{2,10},{3,11},{4,12},{5,13},{6,14},{7,15},{8,0},{9,1},... | collective-permute-start | bytes 1228808 | tf_op jit(solution)/shard_map/ppermute | solution.py:108
  66.8 33.2 %collective-permute-start.15 = (bf16[200,1024]{1,0:T(8,128)(2,1)S(1)}, bf16[200,1024]{1,0:T(8,128)(2,1)S(1)}, u32[]{:S(2)}, u32[]{:S(2)}) collective-permute-start(bf16[200,1024]{1,0:T(8,128)(2,1)S(1)} %collective-permute-done.14), channel_id=1, source_target_pairs={{0,8},{1,9},{2,10},{3,11},{4,12},{5,13},{6,14},{7,15},{8,0},{9,1},... | collective-permute-start | bytes 1228808 | tf_op jit(solution)/shard_map/ppermute | solution.py:108
  101.1 18.2 %collective-permute-start.16 = (bf16[2,200,1024]{2,1,0:T(8,128)(2,1)}, bf16[2,200,1024]{2,1,0:T(8,128)(2,1)}, u32[]{:S(2)}, u32[]{:S(2)}) collective-permute-start(bf16[2,200,1024]{2,1,0:T(8,128)(2,1)} %maximum_select_fusion.1), channel_id=1, source_target_pairs={{0,1},{1,0},{2,3},{3,2},{4,5},{5,4},{6,7},{7,6},{8,9},{9,8},{10,11... | collective-permute-start | bytes 2457608 | tf_op jit(solution)/shard_map/ppermute | solution.py:108
  109.7 73.7 %collective-permute-start.7 = (bf16[2,4,128,896]{3,2,1,0:T(8,128)(2,1)}, bf16[2,4,128,896]{3,2,1,0:T(8,128)(2,1)S(1)}, u32[]{:S(2)}, u32[]{:S(2)}) collective-permute-start(bf16[2,4,128,896]{3,2,1,0:T(8,128)(2,1)} %get-tuple-element.36.xa), channel_id=1, source_target_pairs={{0,2},{1,3},{2,0},{3,1},{4,6},{5,7},{6,4},{7,5},{8,10},{9,11},{10,... | collective-permute-start | bytes 5505032 | tf_op jit(solution)/shard_map/ppermute | solution.py:108
  120.7 65.0 %collective-permute-start.18 = (bf16[2,2,200,1024]{3,2,1,0:T(8,128)(2,1)S(1)}, bf16[2,2,200,1024]{3,2,1,0:T(8,128)(2,1)}, u32[]{:S(2)}, u32[]{:S(2)}) collective-permute-start(bf16[2,2,200,1024]{3,2,1,0:T(8,128)(2,1)S(1)} %pad_maximum_fusion.wa), channel_id=1, source_target_pairs={{0,4},{1,5},{2,6},{3,7},{4,0},{5,1},{6,2},{7,3},{8,12},{9,13},{10,... | collective-permute-start | bytes 4915208 | tf_op jit(solution)/shard_map/ppermute | solution.py:108
  122.2 61.2 %collective-permute-start.6 = (bf16[4,128,896]{2,1,0:T(8,128)(2,1)}, bf16[4,128,896]{2,1,0:T(8,128)(2,1)}, u32[]{:S(2)}, u32[]{:S(2)}) collective-permute-start(bf16[4,128,896]{2,1,0:T(8,128)(2,1)} %get-tuple-element.41), channel_id=1, source_target_pairs={{0,4},{1,5},{2,6},{3,7},{4,0},{5,1},{6,2},{7,3},{8,12},{9,13},{10,... | collective-permute-start | bytes 2752520 | tf_op jit(solution)/shard_map/ppermute | solution.py:108
  122.3 58.9 %collective-permute-start.3 = (bf16[1,200,256]{2,1,0:T(8,128)(2,1)S(1)}, bf16[1,200,256]{2,1,0:T(8,128)(2,1)S(1)}, u32[]{:S(2)}, u32[]{:S(2)}) collective-permute-start(bf16[1,200,256]{2,1,0:T(8,128)(2,1)S(1)} %copy-done.16), channel_id=1, source_target_pairs={{0,6},{1,7},{2,4},{3,5},{4,2},{5,3},{6,0},{7,1},{8,14},{9,15},{10,... | collective-permute-start | bytes 307208 | tf_op jit(solution)/shard_map/ppermute | solution.py:108
  126.8 54.5 %collective-permute-start.4 = (bf16[1,200,256]{2,1,0:T(8,128)(2,1)S(1)}, bf16[1,200,256]{2,1,0:T(8,128)(2,1)S(1)}, u32[]{:S(2)}, u32[]{:S(2)}) collective-permute-start(bf16[1,200,256]{2,1,0:T(8,128)(2,1)S(1)} %copy-done.15), channel_id=1, source_target_pairs={{0,4},{1,5},{2,6},{3,7},{4,0},{5,1},{6,2},{7,3},{8,12},{9,13},{10,... | collective-permute-start | bytes 307208 | tf_op jit(solution)/shard_map/ppermute | solution.py:108
  183.5 21.8 %collective-permute-start.8 = (bf16[4,128,896]{2,1,0:T(8,128)(2,1)}, bf16[4,128,896]{2,1,0:T(8,128)(2,1)S(1)}, u32[]{:S(2)}, u32[]{:S(2)}) collective-permute-start(bf16[4,128,896]{2,1,0:T(8,128)(2,1)} %collective-permute-done.6.xc), channel_id=1, source_target_pairs={{0,1},{1,0},{2,3},{3,2},{4,5},{5,4},{6,7},{7,6},{8,9},{9,8},{10,11... | collective-permute-start | bytes 2752520 | tf_op jit(solution)/shard_map/ppermute | solution.py:108
  184.9 21.6 %collective-permute-start.17 = (bf16[2,2,200,1024]{3,2,1,0:T(8,128)(2,1)S(1)}, bf16[2,2,200,1024]{3,2,1,0:T(8,128)(2,1)S(1)}, u32[]{:S(2)}, u32[]{:S(2)}) collective-permute-start(bf16[2,2,200,1024]{3,2,1,0:T(8,128)(2,1)S(1)} %pad_maximum_fusion.wa), channel_id=1, source_target_pairs={{0,2},{1,3},{2,0},{3,1},{4,6},{5,7},{6,4},{7,5},{8,10},{9,11},{10,... | collective-permute-start | bytes 4915208 | tf_op jit(solution)/shard_map/ppermute | solution.py:108
  185.7 24.4 %collective-permute-start.19 = (bf16[2,2,200,1024]{3,2,1,0:T(8,128)(2,1)}, bf16[2,2,200,1024]{3,2,1,0:T(8,128)(2,1)}, u32[]{:S(2)}, u32[]{:S(2)}) collective-permute-start(bf16[2,2,200,1024]{3,2,1,0:T(8,128)(2,1)} %collective-permute-done.18.wc), channel_id=1, source_target_pairs={{0,2},{1,3},{2,0},{3,1},{4,6},{5,7},{6,4},{7,5},{8,10},{9,11},{10,... | collective-permute-start | bytes 4915208 | tf_op jit(solution)/shard_map/ppermute | solution.py:108
  226.8 15.6 %collective-permute-start.23 = (f32[2,1024]{1,0:T(2,128)S(1)}, f32[2,1024]{1,0:T(2,128)S(1)}, u32[]{:S(2)}, u32[]{:S(2)}) collective-permute-start(f32[2,1024]{1,0:T(2,128)S(1)} %add_add_fusion.mine), channel_id=1, source_target_pairs={{0,1},{1,0},{2,3},{3,2},{4,5},{5,4},{6,7},{7,6},{8,9},{9,8},{10,11... | collective-permute-start | bytes 24584 | tf_op jit(solution)/shard_map/ppermute | solution.py:108
  236.5 14.0 %collective-permute-start.26 = (bf16[512,256]{1,0:T(8,128)(2,1)}, bf16[512,256]{1,0:T(8,128)(2,1)S(1)}, u32[]{:S(2)}, u32[]{:S(2)}) collective-permute-start(bf16[512,256]{1,0:T(8,128)(2,1)} %get-tuple-element.53), channel_id=1, source_target_pairs={{0,8},{1,9},{2,10},{3,11},{4,12},{5,13},{6,14},{7,15},{8,0},{9,1},... | collective-permute-start | bytes 786440 | tf_op jit(solution)/shard_map/ppermute | solution.py:108
  239.0 11.5 %collective-permute-start.27 = (bf16[512,256]{1,0:T(8,128)(2,1)}, bf16[512,256]{1,0:T(8,128)(2,1)S(1)}, u32[]{:S(2)}, u32[]{:S(2)}) collective-permute-start(bf16[512,256]{1,0:T(8,128)(2,1)} %get-tuple-element.54), channel_id=1, source_target_pairs={{0,0},{1,1},{2,2},{3,3},{4,4},{5,5},{6,6},{7,7},{8,16},{9,17},{10,... | collective-permute-start | bytes 786440 | tf_op jit(solution)/shard_map/ppermute | solution.py:108
  265.3 10.2 %collective-permute-start.29 = (bf16[256,256]{1,0:T(8,128)(2,1)}, bf16[256,256]{1,0:T(8,128)(2,1)S(1)}, u32[]{:S(2)}, u32[]{:S(2)}) collective-permute-start(bf16[256,256]{1,0:T(8,128)(2,1)} %get-tuple-element.56), channel_id=1, source_target_pairs={{0,2},{1,3},{2,0},{3,1},{4,6},{5,7},{6,4},{7,5},{8,10},{9,11},{10,... | collective-permute-start | bytes 393224 | tf_op jit(solution)/shard_map/ppermute | solution.py:108
  268.2 9.5 %collective-permute-start.30 = (bf16[256,256]{1,0:T(8,128)(2,1)}, bf16[256,256]{1,0:T(8,128)(2,1)S(1)}, u32[]{:S(2)}, u32[]{:S(2)}) collective-permute-start(bf16[256,256]{1,0:T(8,128)(2,1)} %get-tuple-element.56), channel_id=1, source_target_pairs={{0,3},{1,2},{2,1},{3,0},{4,7},{5,6},{6,5},{7,4},{8,11},{9,10},{10,... | collective-permute-start | bytes 393224 | tf_op jit(solution)/shard_map/ppermute | solution.py:108
  270.7 10.8 %collective-permute-start.33 = (bf16[256,256]{1,0:T(8,128)(2,1)}, bf16[256,256]{1,0:T(8,128)(2,1)S(1)}, u32[]{:S(2)}, u32[]{:S(2)}) collective-permute-start(bf16[256,256]{1,0:T(8,128)(2,1)} %get-tuple-element.58), channel_id=1, source_target_pairs={{0,6},{1,7},{2,4},{3,5},{4,2},{5,3},{6,0},{7,1},{8,14},{9,15},{10,... | collective-permute-start | bytes 393224 | tf_op jit(solution)/shard_map/ppermute | solution.py:108
  (39 other events, 432.1 us)
Sparse Core Ops, SparseCore 0:
  21.2 82.0 all-gather.4
  183.6 39.4 all-gather.6

commit v6 on v3

v6 whole, which is shorter than its diff:
```python
import functools
import math

import jax
import jax.numpy as jnp
from jax import lax
from jax.experimental import pallas as pl
from jax.experimental.pallas import tpu as pltpu
from jax.sharding import PartitionSpec as P

HEAD_DIM = 128
SLAB = 4

eps = 1e-06
floor_score = -1e30


def passed_along(x, axis, by):
    size = lax.axis_size(axis)
    pairs = [(i, i + by) for i in range(size) if 0 <= i + by < size]
    return lax.ppermute(x, axis, pairs)


def masked_scores(query, keys, query_seg, key_seg):
    scores = jnp.einsum(
        "qhd,khd->hqk", query, keys, preferred_element_type=jnp.float32
    ) * HEAD_DIM ** (-0.5)
    mask = (query_seg[:, None] == key_seg[None, :])[None]
    return (jnp.where(mask, scores, floor_score), mask)


def row_plan(tokens, norm_gain, qkv_weight, q_gain, k_gain, out_weight, layer_scale, segment_ids):
    count = tokens.shape[0]
    source = tokens.astype(jnp.float32)
    normed = (
        source * lax.rsqrt(jnp.mean(source * source, axis=-1, keepdims=True) + eps) * norm_gain
    ).astype(jnp.bfloat16)
    local_width = qkv_weight.shape[2]
    heads = local_width // HEAD_DIM
    joined = jnp.einsum(
        "td,dch->tch",
        normed,
        lax.all_gather(qkv_weight, "seq", axis=0, tiled=True),
        preferred_element_type=jnp.float32,
    )
    query = joined[:, 0]
    keys = joined[:, 1]
    values = joined[:, 2]
    query_sq, key_sq = lax.psum(
        (jnp.sum(query * query, axis=-1), jnp.sum(keys * keys, axis=-1)), "tp"
    )
    full_width = local_width * lax.axis_size("tp")
    query_normed = (query * lax.rsqrt(query_sq / full_width + eps)[:, None] * q_gain).astype(
        jnp.bfloat16
    )
    key_normed = (keys * lax.rsqrt(key_sq / full_width + eps)[:, None] * k_gain).astype(
        jnp.bfloat16
    )
    paired = jnp.stack([key_normed, values.astype(jnp.bfloat16)], axis=1)
    pieces = []
    for offset in (2, 1, 0, -1, -2):
        if offset == 0:
            pieces.append(paired)
        else:
            pieces.append(passed_along(paired, "seq", offset))
    widened = jnp.concatenate(pieces, axis=0)
    position = lax.axis_index("seq")
    outside = jnp.full((2 * count,), -1, jnp.int32)
    seg_pad = jnp.concatenate([outside, segment_ids, outside], axis=0)
    key_seg = lax.dynamic_slice_in_dim(seg_pad, position * count, 5 * count, 0)
    query_seg = lax.dynamic_slice_in_dim(segment_ids, position * count, count, 0)
    query_heads = query_normed.reshape(count, heads, HEAD_DIM)
    key_heads = widened[:, 0].reshape(5 * count, heads, HEAD_DIM)
    value_heads = widened[:, 1].reshape(5 * count, heads, HEAD_DIM)
    scores, mask = masked_scores(query_heads, key_heads, query_seg, key_seg)
    peak = jnp.max(scores, axis=-1, keepdims=True)
    weights = jnp.where(mask, jnp.exp(scores - peak), 0.0)
    total = jnp.sum(weights, axis=-1)
    probs = weights.astype(jnp.bfloat16)
    summed = jnp.einsum("hqk,khd->qhd", probs, value_heads, preferred_element_type=jnp.float32)
    context = (
        (summed / jnp.transpose(total)[:, :, None]).reshape(count, local_width).astype(jnp.bfloat16)
    )
    terms = jnp.dot(
        context,
        lax.all_gather(out_weight, "seq", axis=1, tiled=True),
        preferred_element_type=jnp.float32,
    )
    projected = lax.psum_scatter(terms, "tp", scatter_dimension=1, tiled=True)
    share = layer_scale.shape[0]
    residual = lax.dynamic_slice_in_dim(source, lax.axis_index("tp") * share, share, 1)
    return (residual + layer_scale * projected).astype(jnp.bfloat16)


ANY = pl.BlockSpec(memory_space=pl.ANY)
VMEM = pl.BlockSpec(memory_space=pltpu.VMEM)
SMEM = pl.BlockSpec(memory_space=pltpu.SMEM)
HBM = pl.BlockSpec(memory_space=pltpu.HBM)
KERNEL_VMEM = 60 * 1024 * 1024


def permuted(x, to):
    slabs, tps = lax.axis_size("seq") // SLAB, lax.axis_size("tp")
    pairs = []
    for i in range(slabs * SLAB * tps):
        z, q, y = to(i // (SLAB * tps), i // tps % SLAB, i % tps)
        pairs.append((i, (z * SLAB + q) * tps + y))
    return lax.ppermute(x, ("seq", "tp"), pairs)


def in_slab(x, flip):
    return permuted(x, lambda z, q, y: (z, q ^ flip, y))


def across(x):
    return permuted(x, lambda z, q, y: (z, q, 1 - y))


def even_pair(x):
    return permuted(x, lambda z, q, y: (z ^ 1, q, y))


def odd_pair(x):
    return permuted(x, lambda z, q, y: (3 - z if z in (1, 2) else z, q, y))


def tied(*arrays):
    return lax.optimization_barrier(arrays)


def as_row(column):
    wide = jnp.broadcast_to(column, (column.shape[0], 128))
    return jnp.transpose(wide)[:8]


def as_column(row):
    return jnp.transpose(jnp.broadcast_to(row, (128, row.shape[1])))


def start(copies):
    for copy in copies:
        copy.start()


def wait(copies):
    for copy in copies:
        copy.wait()


def norm_kernel(tokens, gain, out):
    part = tokens.shape[1] // out.shape[0]
    source = tokens[...].astype(jnp.float32)
    mean = jnp.mean(source * source, axis=1, keepdims=True)
    normed = source * lax.rsqrt(mean + eps) * gain[...]
    for j in range(out.shape[0]):
        out[j, :, :part] = normed[:, j * part:(j + 1) * part].astype(jnp.bfloat16)
        out[j, :, part:] = jnp.zeros((out.shape[1], out.shape[2] - part), jnp.bfloat16)


def norm(tokens, gain, slabs):
    count, depth = tokens.shape
    shape = (slabs, count, pl.cdiv(depth // slabs, 128) * 128)
    return pl.pallas_call(
        norm_kernel,
        out_shape=jax.ShapeDtypeStruct(shape, jnp.bfloat16),
        in_specs=[VMEM, VMEM],
        out_specs=VMEM,
        compiler_params=pltpu.CompilerParams(vmem_limit_bytes=KERNEL_VMEM),
        name="norm",
    )(tokens, gain[None])


def far_slabs(z):
    return jnp.where(z < 2, 2, 1), jnp.where(z < 2, 3, 0)


def token_copies(xs, at, out, sems):
    return [
        pltpu.make_async_copy(x.at[at], out.at[r], sems.at[r]) for r, x in enumerate(xs)
    ]


def picked_copy(z, middle, end, out, sem, wait):
    inner = (z == 1) | (z == 2)

    @pl.when(inner)
    def _():
        copy = pltpu.make_async_copy(middle, out, sem)
        copy.wait() if wait else copy.start()

    @pl.when(jnp.logical_not(inner))
    def _():
        copy = pltpu.make_async_copy(end, out, sem)
        copy.wait() if wait else copy.start()


def early_kernel(
    place, xa, xb, xc, xd, own, near, middle, end, acc, x_all, w_all, held, x_sem, w_sem, sems,
):
    z = place[0]
    xs = (xa, xb, xc, xd)
    near_copy = pltpu.make_async_copy(near, w_all.at[1], w_sem.at[1])
    own_copy = pltpu.make_async_copy(own, w_all.at[0], w_sem.at[0])
    x_copies = [
        token_copies(xs, at, x_all.at[i], x_sem.at[i])
        for i, at in enumerate((z, z ^ 1, far_slabs(z)[0]))
    ]
    own_copy.start()
    start(x_copies[0])
    near_copy.start()
    start(x_copies[1])
    picked_copy(z, middle, end, w_all.at[2], w_sem.at[2], False)
    start(x_copies[2])
    kinds, rows = own.shape[:2]
    stores = []
    for step in range(3):
        if step < 2:
            (own_copy, near_copy)[step].wait()
        else:
            picked_copy(z, middle, end, w_all.at[2], w_sem.at[2], True)
        wait(x_copies[step])
        for r in range(SLAB):
            x = x_all[step, r][:, :rows]
            for kind in range(kinds):
                term = jnp.dot(x, w_all[step, kind], preferred_element_type=jnp.float32)
                held[r, kind] = term if step == 0 else held[r, kind] + term
            if step == 2:
                stores.append(pltpu.make_async_copy(held.at[r], acc.at[r], sems.at[r]))
                stores[-1].start()
    wait(stores)


def early(place, xs, own, near, middle, end):
    kinds, rows, width = own.shape
    slabs, count, wide = xs[0].shape
    return pl.pallas_call(
        early_kernel,
        out_shape=jax.ShapeDtypeStruct((SLAB, kinds, count, width), jnp.float32),
        in_specs=[SMEM] + [HBM] * 8,
        out_specs=HBM,
        scratch_shapes=[
            pltpu.VMEM((3, SLAB, count, wide), jnp.bfloat16),
            pltpu.VMEM((3, kinds, rows, width), jnp.bfloat16),
            pltpu.VMEM((SLAB, kinds, count, width), jnp.float32),
            pltpu.SemaphoreType.DMA((3, SLAB)),
            pltpu.SemaphoreType.DMA((3,)),
            pltpu.SemaphoreType.DMA((SLAB,)),
        ],
        compiler_params=pltpu.CompilerParams(vmem_limit_bytes=KERNEL_VMEM),
        cost_estimate=pl.CostEstimate(
            flops=6 * kinds * SLAB * count * rows * width,
            bytes_accessed=6 * kinds * rows * width + 6 * SLAB * count * rows,
            transcendentals=0,
        ),
        name="early",
    )(place, *xs, own, near, middle, end)


def late_kernel(
    place, xa, xb, xc, xd, acc, middle, end, q_gain, k_gain,
    query, keys, values, squares, even, odd,
    x_all, far, held, q_all, k_all, v_all, x_sem, w_sem, acc_sem, sems,
):
    z, q = place[0], place[1]
    picked_copy(z, middle, end, far, w_sem, False)
    copies = token_copies((xa, xb, xc, xd), far_slabs(z)[1], x_all, x_sem)
    loads = [pltpu.make_async_copy(acc.at[r], held.at[r], acc_sem.at[r]) for r in range(SLAB)]
    for r in range(SLAB):
        copies[r].start()
        loads[r].start()
    count = held.shape[2]
    picked_copy(z, middle, end, far, w_sem, True)
    for r in range(SLAB):
        copies[r].wait()
        loads[r].wait()
        x = x_all[r][:, :far.shape[1]]
        rows = pl.ds(pl.multiple_of((q ^ r) * count, count), count)
        for kind in range(3):
            part = held[r, kind] + jnp.dot(x, far[kind], preferred_element_type=jnp.float32)
            if kind < 2:
                summed = as_row(jnp.sum(part * part, axis=1, keepdims=True))
                squares[kind:kind + 1, rows] = summed[:1]
                part = part * (q_gain, k_gain)[kind][...]
            (q_all, k_all, v_all)[kind][rows, :] = part.astype((q_all, k_all, v_all)[kind].dtype)
    reach = even.shape[1]
    stores = []
    for n, (out, at) in enumerate(((even, 1 - z % 2), (odd, z % 2))):
        rows = pl.ds(pl.multiple_of(at * reach, reach), reach)
        stores.append(pltpu.make_async_copy(k_all.at[rows, :], out.at[0], sems.at[2 * n]))
        stores.append(pltpu.make_async_copy(v_all.at[rows, :], out.at[1], sems.at[2 * n + 1]))
    for n, (src, out) in enumerate(((q_all, query), (k_all, keys), (v_all, values))):
        stores.append(pltpu.make_async_copy(src, out, sems.at[4 + n]))
    start(stores)
    wait(stores)


def late(place, xs, acc, middle, end, q_gain, k_gain):
    kinds, rows, width = middle.shape
    count, wide = xs[0].shape[1:]
    slab = SLAB * count
    f32, bf16 = jnp.float32, jnp.bfloat16
    return pl.pallas_call(
        late_kernel,
        out_shape=(
            jax.ShapeDtypeStruct((slab, width), f32),
            jax.ShapeDtypeStruct((slab, width), bf16),
            jax.ShapeDtypeStruct((slab, width), bf16),
            jax.ShapeDtypeStruct((2, slab), f32),
            jax.ShapeDtypeStruct((2, 2 * count, width), bf16),
            jax.ShapeDtypeStruct((2, 2 * count, width), bf16),
        ),
        in_specs=[SMEM] + [HBM] * 7 + [VMEM] * 2,
        out_specs=(HBM, HBM, HBM, VMEM, HBM, HBM),
        scratch_shapes=[
            pltpu.VMEM((SLAB, count, wide), bf16),
            pltpu.VMEM((kinds, rows, width), bf16),
            pltpu.VMEM((SLAB, kinds, count, width), f32),
            pltpu.VMEM((slab, width), f32),
            pltpu.VMEM((slab, width), bf16),
            pltpu.VMEM((slab, width), bf16),
            pltpu.SemaphoreType.DMA((SLAB,)),
            pltpu.SemaphoreType.DMA,
            pltpu.SemaphoreType.DMA((SLAB,)),
            pltpu.SemaphoreType.DMA((7,)),
        ],
        compiler_params=pltpu.CompilerParams(vmem_limit_bytes=KERNEL_VMEM),
        cost_estimate=pl.CostEstimate(
            flops=2 * kinds * slab * rows * width,
            bytes_accessed=2 * kinds * rows * width + 2 * slab * rows,
            transcendentals=0,
        ),
        name="late",
    )(place, *xs, acc, middle, end, q_gain, k_gain)


def attend_kernel(
    full_width, flips, place, query, keys, values, even, odd, mine, other, seg, *rest,
):
    outs, (q_all, k_all, v_all, scale_all, sems) = rest[:len(flips)], rest[len(flips):]
    z, q = place[0], place[1]
    slab = query.shape[0]
    count = slab // SLAB
    half = even.shape[1]
    upper = half + slab
    is_even = z % 2 == 0
    even_at = pl.multiple_of(jnp.where(is_even, upper, 0), half)
    odd_at = pl.multiple_of(jnp.where(is_even, 0, upper), half)
    copies = [pltpu.make_async_copy(query, q_all, sems.at[0])]
    for k, (whole, out) in enumerate(((keys, k_all), (values, v_all))):
        for n, (src, at) in enumerate(((whole, half), (even.at[k], even_at), (odd.at[k], odd_at))):
            dst = out.at[pl.ds(at, src.shape[0]), :]
            copies.append(pltpu.make_async_copy(src, dst, sems.at[1 + 3 * k + n]))
    start(copies)
    scale = [lax.rsqrt((mine[n] + other[n]) / full_width + eps) for n in range(3)]
    scale_all[:, half:upper] = scale[0]
    scale_all[:, :half] = jnp.where(is_even, scale[2], scale[1])[:, slab - half:]
    scale_all[:, upper:] = jnp.where(is_even, scale[1], scale[2])[:, :half]
    wait(copies)
    window = count + 2 * half
    heads = query.shape[1] // HEAD_DIM
    factor = HEAD_DIM ** (-0.5) * math.log2(math.e)
    for r, out in zip(flips, outs):
        begin = pl.multiple_of((q ^ r) * count, count)
        at_query = pl.multiple_of((q ^ r) * count + half, count)
        key_seg = seg[:, pl.ds(begin, window)]
        query_seg = as_column(seg[:, pl.ds(at_query, count)])
        k_scale = scale_all[1:2, pl.ds(begin, window)] * factor
        q_scale = as_column(scale_all[0:1, pl.ds(at_query, count)])
        mask = jnp.tile(query_seg, (1, window // 128)) == key_seg
        for h in range(heads):
            cols = slice(h * HEAD_DIM, (h + 1) * HEAD_DIM)
            q_low = (q_all[pl.ds(begin, count), cols] * q_scale).astype(jnp.bfloat16)
            scores = lax.dot_general(
                q_low, k_all[pl.ds(begin, window), cols],
                (((1,), (1,)), ((), ())), preferred_element_type=jnp.float32,
            )
            scores = jnp.where(mask, scores * k_scale, floor_score)
            peak = jnp.max(scores, axis=1, keepdims=True)
            weights = jnp.exp2(scores - peak)
            total = jnp.sum(weights, axis=1, keepdims=True)
            summed = jnp.dot(
                weights.astype(jnp.bfloat16), v_all[pl.ds(begin, window), cols],
                preferred_element_type=jnp.float32,
            )
            out[:, cols] = (summed / total).astype(jnp.bfloat16)


def attend(full_width, flips, place, query, keys, values, even, odd, mine, other, seg):
    slab, width = query.shape
    half = even.shape[1]
    count = slab // SLAB
    ext = slab + 2 * half
    bf16 = jnp.bfloat16
    window = count + 2 * half
    return pl.pallas_call(
        functools.partial(attend_kernel, full_width, flips),
        out_shape=(jax.ShapeDtypeStruct((count, width), bf16),) * len(flips),
        in_specs=[SMEM] + [HBM] * 5 + [VMEM] * 3,
        out_specs=(VMEM,) * len(flips),
        scratch_shapes=[
            pltpu.VMEM((slab, width), jnp.float32),
            pltpu.VMEM((ext, width), bf16),
            pltpu.VMEM((ext, width), bf16),
            pltpu.VMEM((2, ext), jnp.float32),
            pltpu.SemaphoreType.DMA((7,)),
        ],
        compiler_params=pltpu.CompilerParams(vmem_limit_bytes=KERNEL_VMEM),
        cost_estimate=pl.CostEstimate(
            flops=len(flips) * 4 * count * window * width,
            bytes_accessed=4 * ext * width + 4 * slab * width,
            transcendentals=len(flips) * count * window * width // HEAD_DIM,
        ),
        name="attend",
    )(place, query, keys, values, even, odd, mine, other, seg)


def out_kernel(
    place, c00, c01, c10, c11, c20, c21, c30, c31, wa0, wa1, wb0, wb1, wc0, wc1, wd0, wd1,
    residual, scale, out, c_all, w_all, total, c_sem, w_sem,
):
    z, q, y = place[0], place[1], place[2]
    width = c00.shape[1]
    c_copies = []
    for r, pair in enumerate(((c00, c01), (c10, c11), (c20, c21), (c30, c31))):
        at = pl.multiple_of((q ^ r) * width, width)
        for i in range(2):
            dst = c_all.at[i, :, pl.ds(at, width)]
            c_copies.append(pltpu.make_async_copy(pair[i], dst, c_sem.at[r, i]))
    start(c_copies)
    w_copies = [
        pltpu.make_async_copy(w, w_all.at[r, j], w_sem.at[r, j])
        for r, pair in enumerate(((wa0, wa1), (wb0, wb1), (wc0, wc1), (wd0, wd1)))
        for j, w in enumerate(pair)
    ]
    start(w_copies)
    column = as_column(scale[...])[:out.shape[0]]
    column = jnp.tile(column, (1, out.shape[1] // 128))
    wait(c_copies)
    rows = wa0.shape[1]
    for r in range(SLAB):
        for j in range(2):
            w_copies[2 * r + j].wait()
            slab = jnp.where(z // 2 == y, (z % 2) ^ j, jnp.where(z < 2, j, 1 - j))
            at = pl.multiple_of((slab * SLAB + (q ^ r)) * rows, 8)
            term = None
            for i in range(2):
                part = lax.dot_general(
                    w_all[r, j, i], c_all[i], (((1,), (1,)), ((), ())),
                    preferred_element_type=jnp.float32,
                )
                term = part if term is None else term + part
            total[pl.ds(at, rows), :] = term
    out[...] = (residual[...].astype(jnp.float32) + column * total[...]).astype(jnp.bfloat16)


def output(place, blocks, pieces, residual, scale):
    count, width = blocks[0].shape
    rows, depth = pieces[0].shape[1:]
    share = residual.shape[0]
    scale = jnp.pad(scale, (0, -share % 128))[None]
    return pl.pallas_call(
        out_kernel,
        out_shape=jax.ShapeDtypeStruct((share, count), jnp.bfloat16),
        in_specs=[SMEM] + [HBM] * 16 + [VMEM] * 2,
        out_specs=VMEM,
        scratch_shapes=[
            pltpu.VMEM((2, count, depth), jnp.bfloat16),
            pltpu.VMEM((SLAB, 2, 2, rows, depth), jnp.bfloat16),
            pltpu.VMEM((share, count), jnp.float32),
            pltpu.SemaphoreType.DMA((SLAB, 2)),
            pltpu.SemaphoreType.DMA((SLAB, 2)),
        ],
        compiler_params=pltpu.CompilerParams(vmem_limit_bytes=KERNEL_VMEM),
        cost_estimate=pl.CostEstimate(
            flops=4 * share * count * depth,
            bytes_accessed=4 * share * depth,
            transcendentals=0,
        ),
        name="output",
    )(place, *blocks, *pieces, residual, scale)


def rows_of_slab(q, cut):
    got = [cut[0]] + [in_slab(cut[r], r) for r in range(1, SLAB)]
    placed = []
    for b in range(SLAB):
        piece = got[b]
        for other in range(1, SLAB):
            piece = jnp.where(q == other, got[b ^ other], piece)
        placed.append(piece)
    return jnp.concatenate(placed, axis=1)


def slab_plan(tokens, norm_gain, qkv_weight, q_gain, k_gain, out_weight, layer_scale, segment_ids):
    count = tokens.shape[0]
    seq, tp = lax.axis_index("seq"), lax.axis_index("tp")
    slabs = lax.axis_size("seq") // SLAB
    z, q = seq // SLAB, seq % SLAB
    place = jnp.stack([z, q, tp]).astype(jnp.int32)
    width = qkv_weight.shape[2] // SLAB
    full_width = qkv_weight.shape[2] * lax.axis_size("tp")
    slab, half = SLAB * count, 2 * count
    inner, home = (z == 1) | (z == 2), z // 2 == tp

    by_kind = jnp.transpose(qkv_weight, (1, 0, 2))
    cut = [lax.dynamic_slice_in_dim(by_kind, (q ^ r) * width, width, 2) for r in range(SLAB)]
    *cut, out_own = tied(*cut, jnp.transpose(out_weight))
    own = rows_of_slab(q, cut)
    out_near, out_mid1 = even_pair(out_own), odd_pair(out_own)
    x0 = norm(tokens, norm_gain, slabs)
    out_end1, out_mid2 = even_pair(out_mid1), odd_pair(out_near)

    def over_tp(close, far):
        keep, give = jnp.where(home, close, far), jnp.where(home, far, close)
        return keep, across(give)

    own, x0, out_end1, out_mid2 = tied(own, x0, out_end1, out_mid2)
    near, middle1 = even_pair(own), odd_pair(own)
    x2 = in_slab(x0, 2)
    out_end2 = even_pair(out_mid2)
    keep0, got0 = over_tp(out_own, jnp.where(inner, out_mid1, out_end1))
    near, middle1 = tied(near, middle1)
    end1, middle2 = even_pair(middle1), odd_pair(near)
    x2, x0, out_end2, keep0, got0, _ = tied(x2, x0, out_end2, keep0, got0, near)
    wa0 = jnp.stack([keep0, got0])
    wc0 = in_slab(wa0, 2)
    x1 = in_slab(x0, 1)
    keep1, got1 = over_tp(out_near, jnp.where(inner, out_mid2, out_end2))
    end1, middle2, x1, x2, wa0, wc0, keep1, got1 = tied(
        end1, middle2, x1, x2, wa0, wc0, keep1, got1
    )
    end2 = even_pair(middle2)
    x3 = in_slab(x2, 1)
    wa1 = jnp.stack([keep1, got1])
    wc1 = in_slab(wa1, 2)
    xs = (x0, x1, x2, x3)
    acc = early(place, xs, own, near, middle1, end1)
    wb0, wd0 = in_slab(wa0, 1), in_slab(wc0, 1)
    end2, acc, wc1, wb0, wd0 = tied(end2, acc, wc1, wb0, wd0)

    gains = [lax.dynamic_slice_in_dim(g, q * width, width, 0)[None] for g in (q_gain, k_gain)]
    query, keys, values, squares, even, odd = late(place, xs, acc, middle2, end2, *gains)
    sums = jnp.stack([squares, even_pair(squares), odd_pair(squares)])
    sums, even, odd = tied(sums, even, odd)
    even, odd = even_pair(even), odd_pair(odd)
    mine = sums
    for r in range(1, SLAB):
        mine = mine + in_slab(sums, r)
    other = across(mine)
    wb1, wd1 = in_slab(wa1, 1), in_slab(wc1, 1)
    even, odd, other, wb1, wd1 = tied(even, odd, other, wb1, wd1)
    pieces = (wa0, wa1, wb0, wb1, wc0, wc1, wd0, wd1)

    outside = jnp.full((half,), -1, jnp.int32)
    seg = jnp.concatenate([outside, segment_ids, outside], axis=0)
    seg = lax.dynamic_slice_in_dim(seg, z * slab, slab + 2 * half, 0)
    seg = seg.astype(jnp.float32)[None]
    blocks, spread = {}, {}
    for flips in ((2, 3), (1, 0)):
        found = attend(
            full_width, flips, place, query, keys, values, even, odd, mine, other, seg
        )
        blocks.update(zip(flips, found))
    for r in (2, 3, 1, 0):
        for i in range(2):
            to = functools.partial(lambda r, i, z, q, y: (z, q ^ r, y ^ i), r, i)
            spread[r, i] = permuted(blocks[r], to) if r or i else blocks[r]
    spread = [spread[r, i] for r in range(SLAB) for i in range(2)]

    share = layer_scale.shape[0]
    residual = jnp.transpose(lax.dynamic_slice_in_dim(tokens, tp * share, share, 1))
    return jnp.transpose(output(place, spread, pieces, residual, layer_scale))


def solution(mesh):
    def shards(*args):
        heads = args[2].shape[2] // HEAD_DIM
        slab = mesh.shape["seq"] == 16 and mesh.shape["tp"] == 2 and heads % SLAB == 0
        return (slab_plan if slab else row_plan)(*args)

    return jax.shard_map(
        shards,
        mesh=mesh,
        in_specs=(
            P("seq", None),
            P(),
            P("seq", None, "tp"),
            P("tp"),
            P("tp"),
            P("tp", "seq"),
            P("tp"),
            P(),
        ),
        out_specs=P("seq", "tp"),
        check_vma=False,
    )
```

time: 229 us -> 209 us (0.913)
  starting transfers between devices: 67.8 us -> 49.1 us
  local copies, waits for them, and re-layouts: 23.5 us -> 10.6 us
  Pallas kernels: 37.5 us -> 44.4 us
  waiting for transfers between devices: 92 us -> 95.1 us
    ppermute x43 -> x39, starting transfers between devices: 67.8 us -> 49.1 us  [permuted(): return lax.ppermute(x, ('seq', 'tp'), pairs)]
    unnamed x59 -> x53, local copies, waits for them, and re-layouts: 18.4 us -> 5 us
    pallas_call x3 -> x4, Pallas kernels: 21.4 us -> 25.3 us  [the longest x2 12.3 us: attend(): pl.pallas_call(functools.partial(attend_kernel, full_width, flips), out_s...]
    ppermute x43 -> x39, waiting for transfers between devices: 92 us -> 95.1 us  [permuted(): return lax.ppermute(x, ('seq', 'tp'), pairs)]
  transfers between devices with their start and end apart: 43 -> 39, of which waited for: 21 -> 20; matrix products, arithmetic and copies ran while one was open for 6% -> 5% of each run, Pallas kernels for 9% -> 13%
where the time goes in v6:
time: 209 us; the launch traced here: 205 us
  waiting for transfers between devices  95.1 us (46%)
  starting transfers between devices  49.1 us (23%)
  Pallas kernels  44.4 us (21%)
  local copies, waits for them, and re-layouts  10.6 us (5%)
  other arithmetic  5.54 us (3%)
    ppermute x39, waiting for transfers between devices, permuted(): return lax.ppermute(x, ('seq', 'tp'), pairs)  95.1 us
    ppermute x39, starting transfers between devices, permuted(): return lax.ppermute(x, ('seq', 'tp'), pairs)  49.1 us
    pallas_call x2, Pallas kernels, attend(): pl.pallas_call(functools.partial(attend_kernel, full_width, flips), out_s...  12.3 us
    pallas_call x1, Pallas kernels, output(): pl.pallas_call(out_kernel, out_shape=jax.ShapeDtypeStruct((share, count),...  11.1 us
    pallas_call x1, Pallas kernels, early(): pl.pallas_call(early_kernel, out_shape=jax.ShapeDtypeStruct((SLAB, kinds,...  9.43 us
    pallas_call x1, Pallas kernels, late(): pl.pallas_call(late_kernel, out_shape=(jax.ShapeDtypeStruct((slab, width)...  8.01 us
    unnamed x53, local copies, waits for them, and re-layouts  5 us
  transfers between devices with their start and end apart: 39, of which 20 were waited for; matrix products, arithmetic and copies ran while one was open for 5% of the time, Pallas kernels for 13%

profile of v6, /device:TPU:9, one launch (start us, length us, event | category | flops | bytes accessed | tf_op | source)
XLA Modules:
  0.0 205.3 jit_solution(5552857743926641214)
XLA Ops:
  1.4 3.2 %collective-permute-start.3 = (bf16[200,1024]{1,0:T(8,128)(2,1)S(1)}, bf16[200,1024]{1,0:T(8,128)(2,1)}, u32[]{:S(2)}, u32[]{:S(2)}) collective-permute-start(bf16[200,1024]{1,0:T(8,128)(2,1)S(1)} %bitcast.27), channel_id=1, source_target_pairs={{0,0},{1,1},{2,2},{3,3},{4,4},{5,5},{6,6},{7,7},{8,16},{9,17},{10,... | collective-permute-start | bytes 1228808 | tf_op jit(solution)/shard_map/ppermute | solution.py:108
  7.9 3.6 %norm.1.xa = bf16[4,256,896]{2,1,0:T(8,128)(2,1)} custom-call(bf16[256,3200]{1,0:T(8,128)(2,1)} %tokens.1, f32[1,3200]{1,0:T(1,128)} %broadcast_in_dim.18.gain), custom_call_target="tpu_custom_call" | custom-call | tf_op jit(solution)/shard_map/norm/pallas_call | solution.py:163
  11.5 2.3 %collective-permute-done.3 = bf16[200,1024]{1,0:T(8,128)(2,1)} collective-permute-done((bf16[200,1024]{1,0:T(8,128)(2,1)S(1)}, bf16[200,1024]{1,0:T(8,128)(2,1)}, u32[]{:S(2)}, u32[]{:S(2)}) %collective-permute-start.3) | collective-permute-done | bytes 409632 | tf_op jit(solution)/shard_map/ppermute | solution.py:108
  17.0 4.5 %collective-permute-done.1 = bf16[3,200,256]{2,1,0:T(8,128)(2,1)S(1)} collective-permute-done((bf16[3,200,256]{2,1,0:T(8,128)(2,1)S(1)}, bf16[3,200,256]{2,1,0:T(8,128)(2,1)S(1)}, u32[]{:S(2)}, u32[]{:S(2)}) %collective-permute-start.1) | collective-permute-done | bytes 307232 | tf_op jit(solution)/shard_map/ppermute | solution.py:108
  23.4 2.6 %collective-permute-done.6 = bf16[200,1024]{1,0:T(8,128)(2,1)S(1)} collective-permute-done((bf16[200,1024]{1,0:T(8,128)(2,1)}, bf16[200,1024]{1,0:T(8,128)(2,1)S(1)}, u32[]{:S(2)}, u32[]{:S(2)}) %collective-permute-start.6) | collective-permute-done | bytes 409632 | tf_op jit(solution)/shard_map/ppermute | solution.py:108
  32.8 19.9 %collective-permute-done.10.near = bf16[3,800,256]{2,1,0:T(8,128)(2,1)} collective-permute-done((bf16[3,800,256]{2,1,0:T(8,128)(2,1)S(1)}, bf16[3,800,256]{2,1,0:T(8,128)(2,1)}, u32[]{:S(2)}, u32[]{:S(2)}) %collective-permute-start.10) | collective-permute-done | bytes 1228832 | tf_op jit(solution)/shard_map/ppermute | solution.py:108
  54.7 6.9 %collective-permute-done.8 = bf16[200,1024]{1,0:T(8,128)(2,1)S(1)} collective-permute-done((bf16[200,1024]{1,0:T(8,128)(2,1)S(1)}, bf16[200,1024]{1,0:T(8,128)(2,1)S(1)}, u32[]{:S(2)}, u32[]{:S(2)}) %collective-permute-start.8) | collective-permute-done | bytes 409632 | tf_op jit(solution)/shard_map/ppermute | solution.py:108
  61.5 3.3 %collective-permute-done.7.xc = bf16[4,256,896]{2,1,0:T(8,128)(2,1)} collective-permute-done((bf16[4,256,896]{2,1,0:T(8,128)(2,1)S(1)}, bf16[4,256,896]{2,1,0:T(8,128)(2,1)}, u32[]{:S(2)}, u32[]{:S(2)}) %collective-permute-start.7) | collective-permute-done | bytes 1835040 | tf_op jit(solution)/shard_map/ppermute | solution.py:108
  64.8 3.7 %collective-permute-start.14 = (bf16[4,256,896]{2,1,0:T(8,128)(2,1)S(1)}, bf16[4,256,896]{2,1,0:T(8,128)(2,1)S(1)}, u32[]{:S(2)}, u32[]{:S(2)}) collective-permute-start(bf16[4,256,896]{2,1,0:T(8,128)(2,1)S(1)} %copy-done), channel_id=1, source_target_pairs={{0,2},{1,3},{2,0},{3,1},{4,6},{5,7},{6,4},{7,5},{8,10},{9,11},{10,... | collective-permute-start | bytes 5505032 | tf_op jit(solution)/shard_map/ppermute | solution.py:108
  75.3 9.3 %collective-permute-done.16 = bf16[200,1024]{1,0:T(8,128)(2,1)S(1)} collective-permute-done((bf16[200,1024]{1,0:T(8,128)(2,1)S(1)}, bf16[200,1024]{1,0:T(8,128)(2,1)S(1)}, u32[]{:S(2)}, u32[]{:S(2)}) %collective-permute-start.16) | collective-permute-done | bytes 409632 | tf_op jit(solution)/shard_map/ppermute | solution.py:108
  84.6 12.9 %collective-permute-done.12.end = bf16[3,800,256]{2,1,0:T(8,128)(2,1)S(1)} collective-permute-done((bf16[3,800,256]{2,1,0:T(8,128)(2,1)}, bf16[3,800,256]{2,1,0:T(8,128)(2,1)S(1)}, u32[]{:S(2)}, u32[]{:S(2)}) %collective-permute-start.12) | collective-permute-done | bytes 1228832 | tf_op jit(solution)/shard_map/ppermute | solution.py:108
  101.5 2.6 %collective-permute-start.18 = (bf16[3,800,256]{2,1,0:T(8,128)(2,1)}, bf16[3,800,256]{2,1,0:T(8,128)(2,1)}, u32[]{:S(2)}, u32[]{:S(2)}) collective-permute-start(bf16[3,800,256]{2,1,0:T(8,128)(2,1)} %collective-permute-done.13.middle), channel_id=1, source_target_pairs={{0,8},{1,9},{2,10},{3,11},{4,12},{5,13},{6,14},{7,15},{8,0},{9,1},... | collective-permute-start | bytes 3686408 | tf_op jit(solution)/shard_map/ppermute | solution.py:108
  108.0 9.4 %early.1.acc = f32[4,3,256,256]{3,2,1,0:T(8,128)} custom-call(s32[3]{0:T(128)} %pad_add_fusion.place, bf16[4,256,896]{2,1,0:T(8,128)(2,1)} %norm.1.xa, bf16[4,256,896]{2,1,0:T(8,128)(2,1)} %copy-done.1, bf16[4,256,896]{2,1,0:T(8,128)(2,1)} %collective-permute-done.7.xc, bf16[4,256,896]{2,1,0:T(8,128)(2,1)} %copy-done.2, bf16[3,800,256]{2,1,0:T(8,128)(2,1)} %copy-done.3, ...), custom_call_target="tpu_custom_call" | custom-call | flops 3774873600 | bytes 8601600 | tf_op jit(solution)/shard_map/early/pallas_call | solution.py:236
  117.4 6.5 %collective-permute-done.19.wc1 = bf16[2,200,1024]{2,1,0:T(8,128)(2,1)} collective-permute-done((bf16[2,200,1024]{2,1,0:T(8,128)(2,1)S(1)}, bf16[2,200,1024]{2,1,0:T(8,128)(2,1)}, u32[]{:S(2)}, u32[]{:S(2)}) %collective-permute-start.19) | collective-permute-done | bytes 819232 | tf_op jit(solution)/shard_map/ppermute | solution.py:108
  124.0 7.9 %collective-permute-done.18.end = bf16[3,800,256]{2,1,0:T(8,128)(2,1)} collective-permute-done((bf16[3,800,256]{2,1,0:T(8,128)(2,1)}, bf16[3,800,256]{2,1,0:T(8,128)(2,1)}, u32[]{:S(2)}, u32[]{:S(2)}) %collective-permute-start.18) | collective-permute-done | bytes 1228832 | tf_op jit(solution)/shard_map/ppermute | solution.py:108
  135.1 8.0 %late.1 = (f32[1024,256]{1,0:T(8,128)}, bf16[1024,256]{1,0:T(8,128)(2,1)}, bf16[1024,256]{1,0:T(8,128)(2,1)}, f32[2,1024]{1,0:T(2,128)}, bf16[2,512,256]{2,1,0:T(8,128)(2,1)}, /*index=5*/bf16[2,512,256]{2,1,0:T(8,128)(2,1)}) custom-call(s32[3]{0:T(128)} %pad_add_fusion.place, bf16[4,256,896]{2,1,0:T(8,128)(2,1)} %norm.1.xa, bf16[4,256,896]{2,1,0:T(8,128)(2,1)} %copy-done.1, ...), custom_call_target="tpu_custom_call" | custom-call | flops 1258291200 | bytes 2867200 | tf_op jit(solution)/shard_map/late/pallas_call | solution.py:302
  147.2 2.4 %collective-permute-done.23 = f32[2,1024]{1,0:T(2,128)S(1)} collective-permute-done((f32[2,1024]{1,0:T(2,128)}, f32[2,1024]{1,0:T(2,128)S(1)}, u32[]{:S(2)}, u32[]{:S(2)}) %collective-permute-start.23) | collective-permute-done | bytes 8224 | tf_op jit(solution)/shard_map/ppermute | solution.py:108
  150.4 2.4 %collective-permute-start.25 = (bf16[2,512,256]{2,1,0:T(8,128)(2,1)}, bf16[2,512,256]{2,1,0:T(8,128)(2,1)S(1)}, u32[]{:S(2)}, u32[]{:S(2)}) collective-permute-start(bf16[2,512,256]{2,1,0:T(8,128)(2,1)} %get-tuple-element.85), channel_id=1, source_target_pairs={{0,0},{1,1},{2,2},{3,3},{4,4},{5,5},{6,6},{7,7},{8,16},{9,17},{10,... | collective-permute-start | bytes 1572872 | tf_op jit(solution)/shard_map/ppermute | solution.py:108
  158.4 2.3 %collective-permute-start.28 = (f32[3,2,1024]{2,1,0:T(2,128)S(1)}, f32[3,2,1024]{2,1,0:T(2,128)S(1)}, u32[]{:S(2)}, u32[]{:S(2)}) collective-permute-start(f32[3,2,1024]{2,1,0:T(2,128)S(1)} %pad_maximum_fusion.3), channel_id=1, source_target_pairs={{0,6},{1,7},{2,4},{3,5},{4,2},{5,3},{6,0},{7,1},{8,14},{9,15},{10,... | collective-permute-start | bytes 73736 | tf_op jit(solution)/shard_map/ppermute | solution.py:108
  166.8 6.2 %attend.3 = (bf16[256,256]{1,0:T(8,128)(2,1)}, bf16[256,256]{1,0:T(8,128)(2,1)}) custom-call(s32[3]{0:T(128)} %pad_add_fusion.place, f32[1024,256]{1,0:T(8,128)} %get-tuple-element.78.query, bf16[1024,256]{1,0:T(8,128)(2,1)} %get-tuple-element.79.keys, bf16[1024,256]{1,0:T(8,128)(2,1)} %get-tuple-element.80.values, bf16[2,512,256]{2,1,0:T(8,128)(2,1)} %copy-done.6, ...), custom_call_target="tpu_custom_call" | custom-call | flops 671088640 | bytes 3145728 | tf_op jit(solution)/shard_map/attend/pallas_call | solution.py:395
  175.5 2.6 %collective-permute-start.37 = (bf16[256,256]{1,0:T(8,128)(2,1)}, bf16[256,256]{1,0:T(8,128)(2,1)S(1)}, u32[]{:S(2)}, u32[]{:S(2)}) collective-permute-start(bf16[256,256]{1,0:T(8,128)(2,1)} %get-tuple-element.94), channel_id=1, source_target_pairs={{0,6},{1,7},{2,4},{3,5},{4,2},{5,3},{6,0},{7,1},{8,14},{9,15},{10,... | collective-permute-start | bytes 393224 | tf_op jit(solution)/shard_map/ppermute | solution.py:108
  178.1 6.2 %attend.2 = (bf16[256,256]{1,0:T(8,128)(2,1)}, bf16[256,256]{1,0:T(8,128)(2,1)}) custom-call(s32[3]{0:T(128)} %pad_add_fusion.place, f32[1024,256]{1,0:T(8,128)} %get-tuple-element.78.query, bf16[1024,256]{1,0:T(8,128)(2,1)} %get-tuple-element.79.keys, bf16[1024,256]{1,0:T(8,128)(2,1)} %get-tuple-element.80.values, bf16[2,512,256]{2,1,0:T(8,128)(2,1)} %copy-done.6, ...), custom_call_target="tpu_custom_call" | custom-call | flops 671088640 | bytes 3145728 | tf_op jit(solution)/shard_map/attend/pallas_call | solution.py:395
  188.9 4.4 %collective-permute-done.32.c01 = bf16[256,256]{1,0:T(8,128)(2,1)S(1)} collective-permute-done((bf16[256,256]{1,0:T(8,128)(2,1)}, bf16[256,256]{1,0:T(8,128)(2,1)S(1)}, u32[]{:S(2)}, u32[]{:S(2)}) %collective-permute-start.32) | collective-permute-done | bytes 131104 | tf_op jit(solution)/shard_map/ppermute | solution.py:108
  194.1 11.1 %output.1 = bf16[1600,256]{1,0:T(8,128)(2,1)} custom-call(s32[3]{0:T(128)} %pad_add_fusion.place, bf16[256,256]{1,0:T(8,128)(2,1)} %get-tuple-element.91.c00, bf16[256,256]{1,0:T(8,128)(2,1)} %copy-done.21, bf16[256,256]{1,0:T(8,128)(2,1)} %copy-done.19, bf16[256,256]{1,0:T(8,128)(2,1)} %copy-done.20, bf16[256,256]{1,0:T(8,128)(2,1)} %copy-done.15, ...), custom_call_target="tpu_custom_call" | custom-call | flops 1677721600 | bytes 6553600 | tf_op jit(solution)/shard_map/output/pallas_call | solution.py:461
  (131 shorter events, 60.6 us)
Async XLA Ops:
  1.4 12.3 %collective-permute-start.3 = (bf16[200,1024]{1,0:T(8,128)(2,1)S(1)}, bf16[200,1024]{1,0:T(8,128)(2,1)}, u32[]{:S(2)}, u32[]{:S(2)}) collective-permute-start(bf16[200,1024]{1,0:T(8,128)(2,1)S(1)} %bitcast.27), channel_id=1, source_target_pairs={{0,0},{1,1},{2,2},{3,3},{4,4},{5,5},{6,6},{7,7},{8,16},{9,17},{10,... | collective-permute-start | bytes 1228808 | tf_op jit(solution)/shard_map/ppermute | solution.py:108
  4.7 12.3 %collective-permute-start = (bf16[3,200,256]{2,1,0:T(8,128)(2,1)S(1)}, bf16[3,200,256]{2,1,0:T(8,128)(2,1)S(1)}, u32[]{:S(2)}, u32[]{:S(2)}) collective-permute-start(bf16[3,200,256]{2,1,0:T(8,128)(2,1)S(1)} %get-tuple-element.52), channel_id=1, source_target_pairs={{0,6},{1,7},{2,4},{3,5},{4,2},{5,3},{6,0},{7,1},{8,14},{9,15},{10,... | collective-permute-start | bytes 921608 | tf_op jit(solution)/shard_map/ppermute | solution.py:108
  6.8 14.6 %collective-permute-start.1 = (bf16[3,200,256]{2,1,0:T(8,128)(2,1)S(1)}, bf16[3,200,256]{2,1,0:T(8,128)(2,1)S(1)}, u32[]{:S(2)}, u32[]{:S(2)}) collective-permute-start(bf16[3,200,256]{2,1,0:T(8,128)(2,1)S(1)} %get-tuple-element.53), channel_id=1, source_target_pairs={{0,4},{1,5},{2,6},{3,7},{4,0},{5,1},{6,2},{7,3},{8,12},{9,13},{10,... | collective-permute-start | bytes 921608 | tf_op jit(solution)/shard_map/ppermute | solution.py:108
  7.1 14.4 %collective-permute-start.2 = (bf16[3,200,256]{2,1,0:T(8,128)(2,1)S(1)}, bf16[3,200,256]{2,1,0:T(8,128)(2,1)S(1)}, u32[]{:S(2)}, u32[]{:S(2)}) collective-permute-start(bf16[3,200,256]{2,1,0:T(8,128)(2,1)S(1)} %get-tuple-element.54), channel_id=1, source_target_pairs={{0,2},{1,3},{2,0},{3,1},{4,6},{5,7},{6,4},{7,5},{8,10},{9,11},{10,... | collective-permute-start | bytes 921608 | tf_op jit(solution)/shard_map/ppermute | solution.py:108
  26.0 38.8 %collective-permute-start.7 = (bf16[4,256,896]{2,1,0:T(8,128)(2,1)S(1)}, bf16[4,256,896]{2,1,0:T(8,128)(2,1)}, u32[]{:S(2)}, u32[]{:S(2)}) collective-permute-start(bf16[4,256,896]{2,1,0:T(8,128)(2,1)S(1)} %copy-done), channel_id=1, source_target_pairs={{0,4},{1,5},{2,6},{3,7},{4,0},{5,1},{6,2},{7,3},{8,12},{9,13},{10,... | collective-permute-start | bytes 5505032 | tf_op jit(solution)/shard_map/ppermute | solution.py:108
  27.2 25.6 %collective-permute-start.10 = (bf16[3,800,256]{2,1,0:T(8,128)(2,1)S(1)}, bf16[3,800,256]{2,1,0:T(8,128)(2,1)}, u32[]{:S(2)}, u32[]{:S(2)}) collective-permute-start(bf16[3,800,256]{2,1,0:T(8,128)(2,1)S(1)} %pad_maximum_fusion.own), channel_id=1, source_target_pairs={{0,8},{1,9},{2,10},{3,11},{4,12},{5,13},{6,14},{7,15},{8,0},{9,1},... | collective-permute-start | bytes 3686408 | tf_op jit(solution)/shard_map/ppermute | solution.py:108
  27.2 27.4 %collective-permute-start.11 = (bf16[3,800,256]{2,1,0:T(8,128)(2,1)S(1)}, bf16[3,800,256]{2,1,0:T(8,128)(2,1)}, u32[]{:S(2)}, u32[]{:S(2)}) collective-permute-start(bf16[3,800,256]{2,1,0:T(8,128)(2,1)S(1)} %pad_maximum_fusion.own), channel_id=1, source_target_pairs={{0,0},{1,1},{2,2},{3,3},{4,4},{5,5},{6,6},{7,7},{8,16},{9,17},{10,... | collective-permute-start | bytes 3686408 | tf_op jit(solution)/shard_map/ppermute | solution.py:108
  30.6 24.0 %collective-permute-start.9 = (bf16[200,1024]{1,0:T(8,128)(2,1)S(1)}, bf16[200,1024]{1,0:T(8,128)(2,1)S(1)}, u32[]{:S(2)}, u32[]{:S(2)}) collective-permute-start(bf16[200,1024]{1,0:T(8,128)(2,1)S(1)} %get-tuple-element.101), channel_id=1, source_target_pairs={{0,1},{1,0},{2,3},{3,2},{4,5},{5,4},{6,7},{7,6},{8,9},{9,8},{10,11... | collective-permute-start | bytes 1228808 | tf_op jit(solution)/shard_map/ppermute | solution.py:108
  31.9 29.6 %collective-permute-start.8 = (bf16[200,1024]{1,0:T(8,128)(2,1)S(1)}, bf16[200,1024]{1,0:T(8,128)(2,1)S(1)}, u32[]{:S(2)}, u32[]{:S(2)}) collective-permute-start(bf16[200,1024]{1,0:T(8,128)(2,1)S(1)} %copy-done.12), channel_id=1, source_target_pairs={{0,8},{1,9},{2,10},{3,11},{4,12},{5,13},{6,14},{7,15},{8,0},{9,1},... | collective-permute-start | bytes 1228808 | tf_op jit(solution)/shard_map/ppermute | solution.py:108
  64.8 34.6 %collective-permute-start.14 = (bf16[4,256,896]{2,1,0:T(8,128)(2,1)S(1)}, bf16[4,256,896]{2,1,0:T(8,128)(2,1)S(1)}, u32[]{:S(2)}, u32[]{:S(2)}) collective-permute-start(bf16[4,256,896]{2,1,0:T(8,128)(2,1)S(1)} %copy-done), channel_id=1, source_target_pairs={{0,2},{1,3},{2,0},{3,1},{4,6},{5,7},{6,4},{7,5},{8,10},{9,11},{10,... | collective-permute-start | bytes 5505032 | tf_op jit(solution)/shard_map/ppermute | solution.py:108
  68.5 29.0 %collective-permute-start.12 = (bf16[3,800,256]{2,1,0:T(8,128)(2,1)}, bf16[3,800,256]{2,1,0:T(8,128)(2,1)S(1)}, u32[]{:S(2)}, u32[]{:S(2)}) collective-permute-start(bf16[3,800,256]{2,1,0:T(8,128)(2,1)} %collective-permute-done.11.middle), channel_id=1, source_target_pairs={{0,8},{1,9},{2,10},{3,11},{4,12},{5,13},{6,14},{7,15},{8,0},{9,1},... | collective-permute-start | bytes 3686408 | tf_op jit(solution)/shard_map/ppermute | solution.py:108
  68.5 30.9 %collective-permute-start.13 = (bf16[3,800,256]{2,1,0:T(8,128)(2,1)}, bf16[3,800,256]{2,1,0:T(8,128)(2,1)}, u32[]{:S(2)}, u32[]{:S(2)}) collective-permute-start(bf16[3,800,256]{2,1,0:T(8,128)(2,1)} %collective-permute-done.10.near), channel_id=1, source_target_pairs={{0,0},{1,1},{2,2},{3,3},{4,4},{5,5},{6,6},{7,7},{8,16},{9,17},{10,... | collective-permute-start | bytes 3686408 | tf_op jit(solution)/shard_map/ppermute | solution.py:108
  71.7 27.7 %collective-permute-start.15 = (bf16[2,200,1024]{2,1,0:T(8,128)(2,1)}, bf16[2,200,1024]{2,1,0:T(8,128)(2,1)}, u32[]{:S(2)}, u32[]{:S(2)}) collective-permute-start(bf16[2,200,1024]{2,1,0:T(8,128)(2,1)} %pad_maximum_fusion.1.wa0), channel_id=1, source_target_pairs={{0,4},{1,5},{2,6},{3,7},{4,0},{5,1},{6,2},{7,3},{8,12},{9,13},{10,... | collective-permute-start | bytes 2457608 | tf_op jit(solution)/shard_map/ppermute | solution.py:108
  101.5 30.3 %collective-permute-start.18 = (bf16[3,800,256]{2,1,0:T(8,128)(2,1)}, bf16[3,800,256]{2,1,0:T(8,128)(2,1)}, u32[]{:S(2)}, u32[]{:S(2)}) collective-permute-start(bf16[3,800,256]{2,1,0:T(8,128)(2,1)} %collective-permute-done.13.middle), channel_id=1, source_target_pairs={{0,8},{1,9},{2,10},{3,11},{4,12},{5,13},{6,14},{7,15},{8,0},{9,1},... | collective-permute-start | bytes 3686408 | tf_op jit(solution)/shard_map/ppermute | solution.py:108
  104.2 19.7 %collective-permute-start.19 = (bf16[2,200,1024]{2,1,0:T(8,128)(2,1)S(1)}, bf16[2,200,1024]{2,1,0:T(8,128)(2,1)}, u32[]{:S(2)}, u32[]{:S(2)}) collective-permute-start(bf16[2,200,1024]{2,1,0:T(8,128)(2,1)S(1)} %pad_maximum_fusion.2.wa1), channel_id=1, source_target_pairs={{0,4},{1,5},{2,6},{3,7},{4,0},{5,1},{6,2},{7,3},{8,12},{9,13},{10,... | collective-permute-start | bytes 2457608 | tf_op jit(solution)/shard_map/ppermute | solution.py:108
  105.5 18.5 %collective-permute-start.20 = (bf16[2,200,1024]{2,1,0:T(8,128)(2,1)}, bf16[2,200,1024]{2,1,0:T(8,128)(2,1)S(1)}, u32[]{:S(2)}, u32[]{:S(2)}) collective-permute-start(bf16[2,200,1024]{2,1,0:T(8,128)(2,1)} %pad_maximum_fusion.1.wa0), channel_id=1, source_target_pairs={{0,2},{1,3},{2,0},{3,1},{4,6},{5,7},{6,4},{7,5},{8,10},{9,11},{10,... | collective-permute-start | bytes 2457608 | tf_op jit(solution)/shard_map/ppermute | solution.py:108
  106.1 17.9 %collective-permute-start.21 = (bf16[2,200,1024]{2,1,0:T(8,128)(2,1)}, bf16[2,200,1024]{2,1,0:T(8,128)(2,1)}, u32[]{:S(2)}, u32[]{:S(2)}) collective-permute-start(bf16[2,200,1024]{2,1,0:T(8,128)(2,1)} %collective-permute-done.15.wc0), channel_id=1, source_target_pairs={{0,2},{1,3},{2,0},{3,1},{4,6},{5,7},{6,4},{7,5},{8,10},{9,11},{10,... | collective-permute-start | bytes 2457608 | tf_op jit(solution)/shard_map/ppermute | solution.py:108
  106.7 58.0 %collective-permute-start.30 = (bf16[2,200,1024]{2,1,0:T(8,128)(2,1)S(1)}, bf16[2,200,1024]{2,1,0:T(8,128)(2,1)}, u32[]{:S(2)}, u32[]{:S(2)}) collective-permute-start(bf16[2,200,1024]{2,1,0:T(8,128)(2,1)S(1)} %pad_maximum_fusion.2.wa1), channel_id=1, source_target_pairs={{0,2},{1,3},{2,0},{3,1},{4,6},{5,7},{6,4},{7,5},{8,10},{9,11},{10,... | collective-permute-start | bytes 2457608 | tf_op jit(solution)/shard_map/ppermute | solution.py:108
  131.8 34.0 %collective-permute-start.31 = (bf16[2,200,1024]{2,1,0:T(8,128)(2,1)}, bf16[2,200,1024]{2,1,0:T(8,128)(2,1)}, u32[]{:S(2)}, u32[]{:S(2)}) collective-permute-start(bf16[2,200,1024]{2,1,0:T(8,128)(2,1)} %collective-permute-done.19.wc1), channel_id=1, source_target_pairs={{0,2},{1,3},{2,0},{3,1},{4,6},{5,7},{6,4},{7,5},{8,10},{9,11},{10,... | collective-permute-start | bytes 2457608 | tf_op jit(solution)/shard_map/ppermute | solution.py:108
  150.3 15.5 %collective-permute-start.24 = (bf16[2,512,256]{2,1,0:T(8,128)(2,1)}, bf16[2,512,256]{2,1,0:T(8,128)(2,1)S(1)}, u32[]{:S(2)}, u32[]{:S(2)}) collective-permute-start(bf16[2,512,256]{2,1,0:T(8,128)(2,1)} %get-tuple-element.84), channel_id=1, source_target_pairs={{0,8},{1,9},{2,10},{3,11},{4,12},{5,13},{6,14},{7,15},{8,0},{9,1},... | collective-permute-start | bytes 1572872 | tf_op jit(solution)/shard_map/ppermute | solution.py:108
  150.4 15.4 %collective-permute-start.25 = (bf16[2,512,256]{2,1,0:T(8,128)(2,1)}, bf16[2,512,256]{2,1,0:T(8,128)(2,1)S(1)}, u32[]{:S(2)}, u32[]{:S(2)}) collective-permute-start(bf16[2,512,256]{2,1,0:T(8,128)(2,1)} %get-tuple-element.85), channel_id=1, source_target_pairs={{0,0},{1,1},{2,2},{3,3},{4,4},{5,5},{6,6},{7,7},{8,16},{9,17},{10,... | collective-permute-start | bytes 1572872 | tf_op jit(solution)/shard_map/ppermute | solution.py:108
  173.0 12.2 %collective-permute-start.35 = (bf16[256,256]{1,0:T(8,128)(2,1)}, bf16[256,256]{1,0:T(8,128)(2,1)S(1)}, u32[]{:S(2)}, u32[]{:S(2)}) collective-permute-start(bf16[256,256]{1,0:T(8,128)(2,1)} %get-tuple-element.93), channel_id=1, source_target_pairs={{0,4},{1,5},{2,6},{3,7},{4,0},{5,1},{6,2},{7,3},{8,12},{9,13},{10,... | collective-permute-start | bytes 393224 | tf_op jit(solution)/shard_map/ppermute | solution.py:108
  173.5 12.9 %collective-permute-start.36 = (bf16[256,256]{1,0:T(8,128)(2,1)}, bf16[256,256]{1,0:T(8,128)(2,1)S(1)}, u32[]{:S(2)}, u32[]{:S(2)}) collective-permute-start(bf16[256,256]{1,0:T(8,128)(2,1)} %get-tuple-element.93), channel_id=1, source_target_pairs={{0,5},{1,4},{2,7},{3,6},{4,1},{5,0},{6,3},{7,2},{8,13},{9,12},{10,... | collective-permute-start | bytes 393224 | tf_op jit(solution)/shard_map/ppermute | solution.py:108
  175.5 13.4 %collective-permute-start.37 = (bf16[256,256]{1,0:T(8,128)(2,1)}, bf16[256,256]{1,0:T(8,128)(2,1)S(1)}, u32[]{:S(2)}, u32[]{:S(2)}) collective-permute-start(bf16[256,256]{1,0:T(8,128)(2,1)} %get-tuple-element.94), channel_id=1, source_target_pairs={{0,6},{1,7},{2,4},{3,5},{4,2},{5,3},{6,0},{7,1},{8,14},{9,15},{10,... | collective-permute-start | bytes 393224 | tf_op jit(solution)/shard_map/ppermute | solution.py:108
  (41 other events, 284.9 us)

commit v7 on v6

--- a/solution.py
+++ b/solution.py
@@ -269,6 +269,7 @@
         copies[r].start()
         loads[r].start()
     count = held.shape[2]
+    stores = []
     picked_copy(z, middle, end, far, w_sem, True)
     for r in range(SLAB):
         copies[r].wait()
@@ -281,16 +282,18 @@
                 summed = as_row(jnp.sum(part * part, axis=1, keepdims=True))
                 squares[kind:kind + 1, rows] = summed[:1]
                 part = part * (q_gain, k_gain)[kind][...]
-            (q_all, k_all, v_all)[kind][rows, :] = part.astype((q_all, k_all, v_all)[kind].dtype)
+            held_out, out = ((q_all, query), (k_all, keys), (v_all, values))[kind]
+            held_out[rows, :] = part.astype(held_out.dtype)
+            store = pltpu.make_async_copy(held_out.at[rows, :], out.at[rows, :], sems.at[3 * r + kind])
+            store.start()
+            stores.append(store)
     reach = even.shape[1]
-    stores = []
     for n, (out, at) in enumerate(((even, 1 - z % 2), (odd, z % 2))):
         rows = pl.ds(pl.multiple_of(at * reach, reach), reach)
-        stores.append(pltpu.make_async_copy(k_all.at[rows, :], out.at[0], sems.at[2 * n]))
-        stores.append(pltpu.make_async_copy(v_all.at[rows, :], out.at[1], sems.at[2 * n + 1]))
-    for n, (src, out) in enumerate(((q_all, query), (k_all, keys), (v_all, values))):
-        stores.append(pltpu.make_async_copy(src, out, sems.at[4 + n]))
-    start(stores)
+        for k, src in enumerate((k_all, v_all)):
+            sem = sems.at[3 * SLAB + 2 * n + k]
+            stores.append(pltpu.make_async_copy(src.at[rows, :], out.at[k], sem))
+            stores[-1].start()
     wait(stores)
 
 
@@ -321,7 +324,7 @@
             pltpu.SemaphoreType.DMA((SLAB,)),
             pltpu.SemaphoreType.DMA,
             pltpu.SemaphoreType.DMA((SLAB,)),
-            pltpu.SemaphoreType.DMA((7,)),
+            pltpu.SemaphoreType.DMA((3 * SLAB + 4,)),
         ],
         compiler_params=pltpu.CompilerParams(vmem_limit_bytes=KERNEL_VMEM),
         cost_estimate=pl.CostEstimate(
@@ -334,9 +337,9 @@
 
 
 def attend_kernel(
-    full_width, flips, place, query, keys, values, even, odd, mine, other, seg, *rest,
+    full_width, place, query, keys, values, even, odd, mine, other, seg, o0, o1, o2, o3,
+    q_all, k_all, v_all, k_turned, scale_all, sems,
 ):
-    outs, (q_all, k_all, v_all, scale_all, sems) = rest[:len(flips)], rest[len(flips):]
     z, q = place[0], place[1]
     slab = query.shape[0]
     count = slab // SLAB
@@ -356,10 +359,12 @@
     scale_all[:, :half] = jnp.where(is_even, scale[2], scale[1])[:, slab - half:]
     scale_all[:, upper:] = jnp.where(is_even, scale[1], scale[2])[:, :half]
     wait(copies)
+    for at in range(0, k_all.shape[0], count):
+        k_turned[:, at:at + count] = jnp.transpose(k_all[at:at + count, :])
     window = count + 2 * half
     heads = query.shape[1] // HEAD_DIM
     factor = HEAD_DIM ** (-0.5) * math.log2(math.e)
-    for r, out in zip(flips, outs):
+    for r, out in ((2, o2), (3, o3), (1, o1), (0, o0)):
         begin = pl.multiple_of((q ^ r) * count, count)
         at_query = pl.multiple_of((q ^ r) * count + half, count)
         key_seg = seg[:, pl.ds(begin, window)]
@@ -370,9 +375,8 @@
         for h in range(heads):
             cols = slice(h * HEAD_DIM, (h + 1) * HEAD_DIM)
             q_low = (q_all[pl.ds(begin, count), cols] * q_scale).astype(jnp.bfloat16)
-            scores = lax.dot_general(
-                q_low, k_all[pl.ds(begin, window), cols],
-                (((1,), (1,)), ((), ())), preferred_element_type=jnp.float32,
+            scores = jnp.dot(
+                q_low, k_turned[cols, pl.ds(begin, window)], preferred_element_type=jnp.float32
             )
             scores = jnp.where(mask, scores * k_scale, floor_score)
             peak = jnp.max(scores, axis=1, keepdims=True)
@@ -382,10 +386,10 @@
                 weights.astype(jnp.bfloat16), v_all[pl.ds(begin, window), cols],
                 preferred_element_type=jnp.float32,
             )
-            out[:, cols] = (summed / total).astype(jnp.bfloat16)
-
-
-def attend(full_width, flips, place, query, keys, values, even, odd, mine, other, seg):
+            out[cols, :] = jnp.transpose(summed / total).astype(jnp.bfloat16)
+
+
+def attend(full_width, place, query, keys, values, even, odd, mine, other, seg):
     slab, width = query.shape
     half = even.shape[1]
     count = slab // SLAB
@@ -393,22 +397,23 @@
     bf16 = jnp.bfloat16
     window = count + 2 * half
     return pl.pallas_call(
-        functools.partial(attend_kernel, full_width, flips),
-        out_shape=(jax.ShapeDtypeStruct((count, width), bf16),) * len(flips),
+        functools.partial(attend_kernel, full_width),
+        out_shape=(jax.ShapeDtypeStruct((width, count), bf16),) * SLAB,
         in_specs=[SMEM] + [HBM] * 5 + [VMEM] * 3,
-        out_specs=(VMEM,) * len(flips),
+        out_specs=(VMEM,) * SLAB,
         scratch_shapes=[
             pltpu.VMEM((slab, width), jnp.float32),
             pltpu.VMEM((ext, width), bf16),
             pltpu.VMEM((ext, width), bf16),
+            pltpu.VMEM((width, ext), bf16),
             pltpu.VMEM((2, ext), jnp.float32),
             pltpu.SemaphoreType.DMA((7,)),
         ],
         compiler_params=pltpu.CompilerParams(vmem_limit_bytes=KERNEL_VMEM),
         cost_estimate=pl.CostEstimate(
-            flops=len(flips) * 4 * count * window * width,
+            flops=SLAB * 4 * count * window * width,
             bytes_accessed=4 * ext * width + 4 * slab * width,
-            transcendentals=len(flips) * count * window * width // HEAD_DIM,
+            transcendentals=SLAB * count * window * width // HEAD_DIM,
         ),
         name="attend",
     )(place, query, keys, values, even, odd, mine, other, seg)
@@ -419,12 +424,12 @@
     residual, scale, out, c_all, w_all, total, c_sem, w_sem,
 ):
     z, q, y = place[0], place[1], place[2]
-    width = c00.shape[1]
+    width = c00.shape[0]
     c_copies = []
     for r, pair in enumerate(((c00, c01), (c10, c11), (c20, c21), (c30, c31))):
         at = pl.multiple_of((q ^ r) * width, width)
         for i in range(2):
-            dst = c_all.at[i, :, pl.ds(at, width)]
+            dst = c_all.at[i, pl.ds(at, width), :]
             c_copies.append(pltpu.make_async_copy(pair[i], dst, c_sem.at[r, i]))
     start(c_copies)
     w_copies = [
@@ -444,17 +449,14 @@
             at = pl.multiple_of((slab * SLAB + (q ^ r)) * rows, 8)
             term = None
             for i in range(2):
-                part = lax.dot_general(
-                    w_all[r, j, i], c_all[i], (((1,), (1,)), ((), ())),
-                    preferred_element_type=jnp.float32,
-                )
+                part = jnp.dot(w_all[r, j, i], c_all[i], preferred_element_type=jnp.float32)
                 term = part if term is None else term + part
             total[pl.ds(at, rows), :] = term
     out[...] = (residual[...].astype(jnp.float32) + column * total[...]).astype(jnp.bfloat16)
 
 
 def output(place, blocks, pieces, residual, scale):
-    count, width = blocks[0].shape
+    count = blocks[0].shape[1]
     rows, depth = pieces[0].shape[1:]
     share = residual.shape[0]
     scale = jnp.pad(scale, (0, -share % 128))[None]
@@ -464,7 +466,7 @@
         in_specs=[SMEM] + [HBM] * 16 + [VMEM] * 2,
         out_specs=VMEM,
         scratch_shapes=[
-            pltpu.VMEM((2, count, depth), jnp.bfloat16),
+            pltpu.VMEM((2, depth, count), jnp.bfloat16),
             pltpu.VMEM((SLAB, 2, 2, rows, depth), jnp.bfloat16),
             pltpu.VMEM((share, count), jnp.float32),
             pltpu.SemaphoreType.DMA((SLAB, 2)),
@@ -480,8 +482,7 @@
     )(place, *blocks, *pieces, residual, scale)
 
 
-def rows_of_slab(q, cut):
-    got = [cut[0]] + [in_slab(cut[r], r) for r in range(1, SLAB)]
+def rows_of_slab(q, got):
     placed = []
     for b in range(SLAB):
         piece = got[b]
@@ -504,41 +505,44 @@
 
     by_kind = jnp.transpose(qkv_weight, (1, 0, 2))
     cut = [lax.dynamic_slice_in_dim(by_kind, (q ^ r) * width, width, 2) for r in range(SLAB)]
-    *cut, out_own = tied(*cut, jnp.transpose(out_weight))
-    own = rows_of_slab(q, cut)
+    got = [cut[0]] + [in_slab(cut[r], r) for r in range(1, SLAB)]
+    x0, out_own = norm(tokens, norm_gain, slabs), jnp.transpose(out_weight)
+    own = rows_of_slab(q, got)
     out_near, out_mid1 = even_pair(out_own), odd_pair(out_own)
-    x0 = norm(tokens, norm_gain, slabs)
-    out_end1, out_mid2 = even_pair(out_mid1), odd_pair(out_near)
+    gains = [lax.dynamic_slice_in_dim(g, q * width, width, 0)[None] for g in (q_gain, k_gain)]
 
     def over_tp(close, far):
         keep, give = jnp.where(home, close, far), jnp.where(home, far, close)
         return keep, across(give)
 
-    own, x0, out_end1, out_mid2 = tied(own, x0, out_end1, out_mid2)
+    own, x0, out_near, out_mid1, *gains = tied(own, x0, out_near, out_mid1, *gains)
     near, middle1 = even_pair(own), odd_pair(own)
+    out_end1, out_mid2 = even_pair(out_mid1), odd_pair(out_near)
     x2 = in_slab(x0, 2)
     out_end2 = even_pair(out_mid2)
     keep0, got0 = over_tp(out_own, jnp.where(inner, out_mid1, out_end1))
-    near, middle1 = tied(near, middle1)
+    near, middle1, x0, x2, keep0, got0, out_end2 = tied(
+        near, middle1, x0, x2, keep0, got0, out_end2
+    )
     end1, middle2 = even_pair(middle1), odd_pair(near)
-    x2, x0, out_end2, keep0, got0, _ = tied(x2, x0, out_end2, keep0, got0, near)
+    x1, x3 = in_slab(x0, 1), in_slab(x2, 1)
+    x1, out_end2, keep0, got0 = tied(x1, out_end2, keep0, got0)
     wa0 = jnp.stack([keep0, got0])
     wc0 = in_slab(wa0, 2)
-    x1 = in_slab(x0, 1)
     keep1, got1 = over_tp(out_near, jnp.where(inner, out_mid2, out_end2))
-    end1, middle2, x1, x2, wa0, wc0, keep1, got1 = tied(
-        end1, middle2, x1, x2, wa0, wc0, keep1, got1
+    end1, middle2, x1, x3, wa0, wc0, keep1, got1 = tied(
+        end1, middle2, x1, x3, wa0, wc0, keep1, got1
     )
     end2 = even_pair(middle2)
-    x3 = in_slab(x2, 1)
     wa1 = jnp.stack([keep1, got1])
     wc1 = in_slab(wa1, 2)
+    wb0, wd0 = in_slab(wa0, 1), in_slab(wc0, 1)
     xs = (x0, x1, x2, x3)
     acc = early(place, xs, own, near, middle1, end1)
-    wb0, wd0 = in_slab(wa0, 1), in_slab(wc0, 1)
-    end2, acc, wc1, wb0, wd0 = tied(end2, acc, wc1, wb0, wd0)
-
-    gains = [lax.dynamic_slice_in_dim(g, q * width, width, 0)[None] for g in (q_gain, k_gain)]
+    wb1, wd1 = in_slab(wa1, 1), in_slab(wc1, 1)
+    end2, acc, wb0, wd0, wb1, wd1 = tied(end2, acc, wb0, wd0, wb1, wd1)
+    pieces = (wa0, wa1, wb0, wb1, wc0, wc1, wd0, wd1)
+
     query, keys, values, squares, even, odd = late(place, xs, acc, middle2, end2, *gains)
     sums = jnp.stack([squares, even_pair(squares), odd_pair(squares)])
     sums, even, odd = tied(sums, even, odd)
@@ -547,25 +551,17 @@
     for r in range(1, SLAB):
         mine = mine + in_slab(sums, r)
     other = across(mine)
-    wb1, wd1 = in_slab(wa1, 1), in_slab(wc1, 1)
-    even, odd, other, wb1, wd1 = tied(even, odd, other, wb1, wd1)
-    pieces = (wa0, wa1, wb0, wb1, wc0, wc1, wd0, wd1)
 
     outside = jnp.full((half,), -1, jnp.int32)
     seg = jnp.concatenate([outside, segment_ids, outside], axis=0)
     seg = lax.dynamic_slice_in_dim(seg, z * slab, slab + 2 * half, 0)
     seg = seg.astype(jnp.float32)[None]
-    blocks, spread = {}, {}
-    for flips in ((2, 3), (1, 0)):
-        found = attend(
-            full_width, flips, place, query, keys, values, even, odd, mine, other, seg
-        )
-        blocks.update(zip(flips, found))
-    for r in (2, 3, 1, 0):
+    blocks = attend(full_width, place, query, keys, values, even, odd, mine, other, seg)
+    spread = []
+    for r in range(SLAB):
         for i in range(2):
             to = functools.partial(lambda r, i, z, q, y: (z, q ^ r, y ^ i), r, i)
-            spread[r, i] = permuted(blocks[r], to) if r or i else blocks[r]
-    spread = [spread[r, i] for r in range(SLAB) for i in range(2)]
+            spread.append(permuted(blocks[r], to) if r or i else blocks[r])
 
     share = layer_scale.shape[0]
     residual = jnp.transpose(lax.dynamic_slice_in_dim(tokens, tp * share, share, 1))

time: 209 us -> 208 us (level)
  starting transfers between devices: 49.1 us -> 55 us
  Pallas kernels: 44.4 us -> 39.5 us
  waiting for transfers between devices: 95.1 us -> 92.9 us
    ppermute x39, starting transfers between devices: 49.1 us -> 55 us  [permuted(): return lax.ppermute(x, ('seq', 'tp'), pairs)]
    pallas_call x2 -> x1, Pallas kernels: 12.3 us -> 8.9 us  [attend(): pl.pallas_call(functools.partial(attend_kernel, full_width), out_shape=(j...]
    ppermute x39, waiting for transfers between devices: 95.1 us -> 92.9 us  [permuted(): return lax.ppermute(x, ('seq', 'tp'), pairs)]
    unnamed x53 -> x49, local copies, waits for them, and re-layouts: 5 us -> 7 us
  transfers between devices with their start and end apart: 39 -> 39, of which waited for: 20 -> 17; matrix products, arithmetic and copies ran while one was open for 5% -> 5% of each run, Pallas kernels for 13% -> 6%
where the time goes in v7:
time: 208 us; the launch traced here: 206 us
  waiting for transfers between devices  92.9 us (45%)
  starting transfers between devices  55 us (26%)
  Pallas kernels  39.5 us (19%)
  local copies, waits for them, and re-layouts  12.5 us (6%)
  other arithmetic  5.85 us (3%)
    ppermute x39, waiting for transfers between devices, permuted(): return lax.ppermute(x, ('seq', 'tp'), pairs)  92.9 us
    ppermute x39, starting transfers between devices, permuted(): return lax.ppermute(x, ('seq', 'tp'), pairs)  55 us
    pallas_call x1, Pallas kernels, output(): pl.pallas_call(out_kernel, out_shape=jax.ShapeDtypeStruct((share, count),...  10.1 us
    pallas_call x1, Pallas kernels, early(): pl.pallas_call(early_kernel, out_shape=jax.ShapeDtypeStruct((SLAB, kinds,...  9.45 us
    pallas_call x1, Pallas kernels, attend(): pl.pallas_call(functools.partial(attend_kernel, full_width), out_shape=(j...  8.9 us
    pallas_call x1, Pallas kernels, late(): pl.pallas_call(late_kernel, out_shape=(jax.ShapeDtypeStruct((slab, width)...  7.45 us
    unnamed x49, local copies, waits for them, and re-layouts  7 us
  transfers between devices with their start and end apart: 39, of which 17 were waited for; matrix products, arithmetic and copies ran while one was open for 5% of the time, Pallas kernels for 6%

profile of v7, /device:TPU:9, one launch (start us, length us, event | category | flops | bytes accessed | tf_op | source)
XLA Modules:
  0.0 206.3 jit_solution(16829900051369325669)
XLA Ops:
  3.8 4.3 %collective-permute-start.4 = (bf16[200,1024]{1,0:T(8,128)(2,1)S(1)}, bf16[200,1024]{1,0:T(8,128)(2,1)}, u32[]{:S(2)}, u32[]{:S(2)}) collective-permute-start(bf16[200,1024]{1,0:T(8,128)(2,1)S(1)} %bitcast.43), channel_id=1, source_target_pairs={{0,0},{1,1},{2,2},{3,3},{4,4},{5,5},{6,6},{7,7},{8,16},{9,17},{10,... | collective-permute-start | bytes 1228808 | tf_op jit(solution)/shard_map/ppermute | solution.py:108
  11.4 3.6 %norm.1.xa = bf16[4,256,896]{2,1,0:T(8,128)(2,1)} custom-call(bf16[256,3200]{1,0:T(8,128)(2,1)} %tokens.1, f32[1,3200]{1,0:T(1,128)} %broadcast_in_dim.18.gain), custom_call_target="tpu_custom_call" | custom-call | tf_op jit(solution)/shard_map/norm/pallas_call | solution.py:163
  15.0 2.8 %collective-permute-done.1 = bf16[3,200,256]{2,1,0:T(8,128)(2,1)S(1)} collective-permute-done((bf16[3,200,256]{2,1,0:T(8,128)(2,1)S(1)}, bf16[3,200,256]{2,1,0:T(8,128)(2,1)S(1)}, u32[]{:S(2)}, u32[]{:S(2)}) %collective-permute-start.1) | collective-permute-done | bytes 307232 | tf_op jit(solution)/shard_map/ppermute | solution.py:108
  22.4 4.3 %collective-permute-start.6 = (bf16[3,800,256]{2,1,0:T(8,128)(2,1)S(1)}, bf16[3,800,256]{2,1,0:T(8,128)(2,1)}, u32[]{:S(2)}, u32[]{:S(2)}) collective-permute-start(bf16[3,800,256]{2,1,0:T(8,128)(2,1)S(1)} %pad_maximum_fusion.own), channel_id=1, source_target_pairs={{0,0},{1,1},{2,2},{3,3},{4,4},{5,5},{6,6},{7,7},{8,16},{9,17},{10,... | collective-permute-start | bytes 3686408 | tf_op jit(solution)/shard_map/ppermute | solution.py:108
  28.8 30.4 %collective-permute-done.8 = bf16[200,1024]{1,0:T(8,128)(2,1)} collective-permute-done((bf16[200,1024]{1,0:T(8,128)(2,1)}, bf16[200,1024]{1,0:T(8,128)(2,1)}, u32[]{:S(2)}, u32[]{:S(2)}) %collective-permute-start.8) | collective-permute-done | bytes 409632 | tf_op jit(solution)/shard_map/ppermute | solution.py:108
  62.0 7.9 %collective-permute-done.9 = bf16[200,1024]{1,0:T(8,128)(2,1)S(1)} collective-permute-done((bf16[200,1024]{1,0:T(8,128)(2,1)S(1)}, bf16[200,1024]{1,0:T(8,128)(2,1)S(1)}, u32[]{:S(2)}, u32[]{:S(2)}) %collective-permute-start.9) | collective-permute-done | bytes 409632 | tf_op jit(solution)/shard_map/ppermute | solution.py:108
  71.7 2.5 %collective-permute-start.14 = (bf16[4,256,896]{2,1,0:T(8,128)(2,1)S(1)}, bf16[4,256,896]{2,1,0:T(8,128)(2,1)S(1)}, u32[]{:S(2)}, u32[]{:S(2)}) collective-permute-start(bf16[4,256,896]{2,1,0:T(8,128)(2,1)S(1)} %copy-done), channel_id=1, source_target_pairs={{0,2},{1,3},{2,0},{3,1},{4,6},{5,7},{6,4},{7,5},{8,10},{9,11},{10,... | collective-permute-start | bytes 5505032 | tf_op jit(solution)/shard_map/ppermute | solution.py:108
  74.3 3.9 %collective-permute-start.13 = (bf16[3,800,256]{2,1,0:T(8,128)(2,1)}, bf16[3,800,256]{2,1,0:T(8,128)(2,1)}, u32[]{:S(2)}, u32[]{:S(2)}) collective-permute-start(bf16[3,800,256]{2,1,0:T(8,128)(2,1)} %collective-permute-done.5.near), channel_id=1, source_target_pairs={{0,0},{1,1},{2,2},{3,3},{4,4},{5,5},{6,6},{7,7},{8,16},{9,17},{10,... | collective-permute-start | bytes 3686408 | tf_op jit(solution)/shard_map/ppermute | solution.py:108
  83.7 19.1 %collective-permute-done.12.end = bf16[3,800,256]{2,1,0:T(8,128)(2,1)S(1)} collective-permute-done((bf16[3,800,256]{2,1,0:T(8,128)(2,1)}, bf16[3,800,256]{2,1,0:T(8,128)(2,1)S(1)}, u32[]{:S(2)}, u32[]{:S(2)}) %collective-permute-start.12) | collective-permute-done | bytes 1228832 | tf_op jit(solution)/shard_map/ppermute | solution.py:108
  102.8 2.4 %collective-permute-done.13.middle = bf16[3,800,256]{2,1,0:T(8,128)(2,1)} collective-permute-done((bf16[3,800,256]{2,1,0:T(8,128)(2,1)}, bf16[3,800,256]{2,1,0:T(8,128)(2,1)}, u32[]{:S(2)}, u32[]{:S(2)}) %collective-permute-start.13) | collective-permute-done | bytes 1228832 | tf_op jit(solution)/shard_map/ppermute | solution.py:108
  105.5 2.2 %collective-permute-start.18 = (bf16[3,800,256]{2,1,0:T(8,128)(2,1)}, bf16[3,800,256]{2,1,0:T(8,128)(2,1)S(1)}, u32[]{:S(2)}, u32[]{:S(2)}) collective-permute-start(bf16[3,800,256]{2,1,0:T(8,128)(2,1)} %collective-permute-done.13.middle), channel_id=1, source_target_pairs={{0,8},{1,9},{2,10},{3,11},{4,12},{5,13},{6,14},{7,15},{8,0},{9,1},... | collective-permute-start | bytes 3686408 | tf_op jit(solution)/shard_map/ppermute | solution.py:108
  110.4 13.4 %collective-permute-done.22.wc1 = bf16[2,200,1024]{2,1,0:T(8,128)(2,1)S(1)} collective-permute-done((bf16[2,200,1024]{2,1,0:T(8,128)(2,1)S(1)}, bf16[2,200,1024]{2,1,0:T(8,128)(2,1)S(1)}, u32[]{:S(2)}, u32[]{:S(2)}) %collective-permute-start.22) | collective-permute-done | bytes 819232 | tf_op jit(solution)/shard_map/ppermute | solution.py:108
  123.8 2.2 %collective-permute-start.23 = (bf16[2,200,1024]{2,1,0:T(8,128)(2,1)S(1)}, bf16[2,200,1024]{2,1,0:T(8,128)(2,1)}, u32[]{:S(2)}, u32[]{:S(2)}) collective-permute-start(bf16[2,200,1024]{2,1,0:T(8,128)(2,1)S(1)} %collective-permute-done.22.wc1), channel_id=1, source_target_pairs={{0,2},{1,3},{2,0},{3,1},{4,6},{5,7},{6,4},{7,5},{8,10},{9,11},{10,... | collective-permute-start | bytes 2457608 | tf_op jit(solution)/shard_map/ppermute | solution.py:108
  126.5 9.4 %early.1.acc = f32[4,3,256,256]{3,2,1,0:T(8,128)} custom-call(s32[3]{0:T(128)} %pad_add_fusion.place, bf16[4,256,896]{2,1,0:T(8,128)(2,1)} %norm.1.xa, bf16[4,256,896]{2,1,0:T(8,128)(2,1)} %copy-done.1, bf16[4,256,896]{2,1,0:T(8,128)(2,1)} %collective-permute-done.7.xc, bf16[4,256,896]{2,1,0:T(8,128)(2,1)} %collective-permute-done.15.xd, ...), custom_call_target="tpu_custom_call" | custom-call | flops 3774873600 | bytes 8601600 | tf_op jit(solution)/shard_map/early/pallas_call | solution.py:236
  137.2 7.5 %late.1 = (f32[1024,256]{1,0:T(8,128)}, bf16[1024,256]{1,0:T(8,128)(2,1)}, bf16[1024,256]{1,0:T(8,128)(2,1)}, f32[2,1024]{1,0:T(2,128)}, bf16[2,512,256]{2,1,0:T(8,128)(2,1)}, /*index=5*/bf16[2,512,256]{2,1,0:T(8,128)(2,1)}) custom-call(s32[3]{0:T(128)} %pad_add_fusion.place, bf16[4,256,896]{2,1,0:T(8,128)(2,1)} %norm.1.xa, bf16[4,256,896]{2,1,0:T(8,128)(2,1)} %copy-done.1, ...), custom_call_target="tpu_custom_call" | custom-call | flops 1258291200 | bytes 2867200 | tf_op jit(solution)/shard_map/late/pallas_call | solution.py:305
  144.6 2.6 %collective-permute-start.24 = (f32[2,1024]{1,0:T(2,128)}, f32[2,1024]{1,0:T(2,128)S(1)}, u32[]{:S(2)}, u32[]{:S(2)}) collective-permute-start(f32[2,1024]{1,0:T(2,128)} %get-tuple-element.79), channel_id=1, source_target_pairs={{0,8},{1,9},{2,10},{3,11},{4,12},{5,13},{6,14},{7,15},{8,0},{9,1},... | collective-permute-start | bytes 24584 | tf_op jit(solution)/shard_map/ppermute | solution.py:108
  147.3 3.0 %collective-permute-start.25 = (f32[2,1024]{1,0:T(2,128)}, f32[2,1024]{1,0:T(2,128)S(1)}, u32[]{:S(2)}, u32[]{:S(2)}) collective-permute-start(f32[2,1024]{1,0:T(2,128)} %get-tuple-element.79), channel_id=1, source_target_pairs={{0,0},{1,1},{2,2},{3,3},{4,4},{5,5},{6,6},{7,7},{8,16},{9,17},{10,... | collective-permute-start | bytes 24584 | tf_op jit(solution)/shard_map/ppermute | solution.py:108
  152.7 3.2 %collective-permute-start.27 = (bf16[2,512,256]{2,1,0:T(8,128)(2,1)}, bf16[2,512,256]{2,1,0:T(8,128)(2,1)S(1)}, u32[]{:S(2)}, u32[]{:S(2)}) collective-permute-start(bf16[2,512,256]{2,1,0:T(8,128)(2,1)} %get-tuple-element.83), channel_id=1, source_target_pairs={{0,0},{1,1},{2,2},{3,3},{4,4},{5,5},{6,6},{7,7},{8,16},{9,17},{10,... | collective-permute-start | bytes 1572872 | tf_op jit(solution)/shard_map/ppermute | solution.py:108
  167.5 8.9 %attend.1 = (bf16[256,256]{1,0:T(8,128)(2,1)}, bf16[256,256]{1,0:T(8,128)(2,1)}, bf16[256,256]{1,0:T(8,128)(2,1)}, bf16[256,256]{1,0:T(8,128)(2,1)}) custom-call(s32[3]{0:T(128)} %pad_add_fusion.place, f32[1024,256]{1,0:T(8,128)} %get-tuple-element.76.query, bf16[1024,256]{1,0:T(8,128)(2,1)} %get-tuple-element.77.keys, ...), custom_call_target="tpu_custom_call" | custom-call | flops 1342177280 | bytes 3145728 | tf_op jit(solution)/shard_map/attend/pallas_call | solution.py:399
  177.7 2.7 %collective-permute-start.33 = (bf16[256,256]{1,0:T(8,128)(2,1)}, bf16[256,256]{1,0:T(8,128)(2,1)S(1)}, u32[]{:S(2)}, u32[]{:S(2)}) collective-permute-start(bf16[256,256]{1,0:T(8,128)(2,1)} %get-tuple-element.86), channel_id=1, source_target_pairs={{0,2},{1,3},{2,0},{3,1},{4,6},{5,7},{6,4},{7,5},{8,10},{9,11},{10,... | collective-permute-start | bytes 393224 | tf_op jit(solution)/shard_map/ppermute | solution.py:108
  180.7 2.3 %collective-permute-start.36 = (bf16[256,256]{1,0:T(8,128)(2,1)}, bf16[256,256]{1,0:T(8,128)(2,1)S(1)}, u32[]{:S(2)}, u32[]{:S(2)}) collective-permute-start(bf16[256,256]{1,0:T(8,128)(2,1)} %get-tuple-element.87), channel_id=1, source_target_pairs={{0,5},{1,4},{2,7},{3,6},{4,1},{5,0},{6,3},{7,2},{8,13},{9,12},{10,... | collective-permute-start | bytes 393224 | tf_op jit(solution)/shard_map/ppermute | solution.py:108
  189.1 3.8 %collective-permute-done.37.c30 = bf16[256,256]{1,0:T(8,128)(2,1)S(1)} collective-permute-done((bf16[256,256]{1,0:T(8,128)(2,1)}, bf16[256,256]{1,0:T(8,128)(2,1)S(1)}, u32[]{:S(2)}, u32[]{:S(2)}) %collective-permute-start.37) | collective-permute-done | bytes 131104 | tf_op jit(solution)/shard_map/ppermute | solution.py:108
  192.8 2.5 %collective-permute-done.38.c31 = bf16[256,256]{1,0:T(8,128)(2,1)S(1)} collective-permute-done((bf16[256,256]{1,0:T(8,128)(2,1)}, bf16[256,256]{1,0:T(8,128)(2,1)S(1)}, u32[]{:S(2)}, u32[]{:S(2)}) %collective-permute-start.38) | collective-permute-done | bytes 131104 | tf_op jit(solution)/shard_map/ppermute | solution.py:108
  196.0 10.1 %output.1 = bf16[1600,256]{1,0:T(8,128)(2,1)} custom-call(s32[3]{0:T(128)} %pad_add_fusion.place, bf16[256,256]{1,0:T(8,128)(2,1)} %get-tuple-element.85.c00, bf16[256,256]{1,0:T(8,128)(2,1)} %copy-done.10, bf16[256,256]{1,0:T(8,128)(2,1)} %copy-done.11, bf16[256,256]{1,0:T(8,128)(2,1)} %copy-done.12, bf16[256,256]{1,0:T(8,128)(2,1)} %copy-done.13, ...), custom_call_target="tpu_custom_call" | custom-call | flops 1677721600 | bytes 6553600 | tf_op jit(solution)/shard_map/output/pallas_call | solution.py:463
  (126 shorter events, 50.6 us)
Async XLA Ops:
  1.3 13.7 %collective-permute-start = (bf16[3,200,256]{2,1,0:T(8,128)(2,1)S(1)}, bf16[3,200,256]{2,1,0:T(8,128)(2,1)S(1)}, u32[]{:S(2)}, u32[]{:S(2)}) collective-permute-start(bf16[3,200,256]{2,1,0:T(8,128)(2,1)S(1)} %get-tuple-element.101), channel_id=1, source_target_pairs={{0,6},{1,7},{2,4},{3,5},{4,2},{5,3},{6,0},{7,1},{8,14},{9,15},{10,... | collective-permute-start | bytes 921608 | tf_op jit(solution)/shard_map/ppermute | solution.py:108
  3.1 14.7 %collective-permute-start.1 = (bf16[3,200,256]{2,1,0:T(8,128)(2,1)S(1)}, bf16[3,200,256]{2,1,0:T(8,128)(2,1)S(1)}, u32[]{:S(2)}, u32[]{:S(2)}) collective-permute-start(bf16[3,200,256]{2,1,0:T(8,128)(2,1)S(1)} %get-tuple-element.102), channel_id=1, source_target_pairs={{0,4},{1,5},{2,6},{3,7},{4,0},{5,1},{6,2},{7,3},{8,12},{9,13},{10,... | collective-permute-start | bytes 921608 | tf_op jit(solution)/shard_map/ppermute | solution.py:108
  3.4 14.5 %collective-permute-start.2 = (bf16[3,200,256]{2,1,0:T(8,128)(2,1)S(1)}, bf16[3,200,256]{2,1,0:T(8,128)(2,1)S(1)}, u32[]{:S(2)}, u32[]{:S(2)}) collective-permute-start(bf16[3,200,256]{2,1,0:T(8,128)(2,1)S(1)} %get-tuple-element.103), channel_id=1, source_target_pairs={{0,2},{1,3},{2,0},{3,1},{4,6},{5,7},{6,4},{7,5},{8,10},{9,11},{10,... | collective-permute-start | bytes 921608 | tf_op jit(solution)/shard_map/ppermute | solution.py:108
  3.6 15.7 %collective-permute-start.3 = (bf16[200,1024]{1,0:T(8,128)(2,1)S(1)}, bf16[200,1024]{1,0:T(8,128)(2,1)}, u32[]{:S(2)}, u32[]{:S(2)}) collective-permute-start(bf16[200,1024]{1,0:T(8,128)(2,1)S(1)} %bitcast.42), channel_id=1, source_target_pairs={{0,8},{1,9},{2,10},{3,11},{4,12},{5,13},{6,14},{7,15},{8,0},{9,1},... | collective-permute-start | bytes 1228808 | tf_op jit(solution)/shard_map/ppermute | solution.py:108
  3.8 15.5 %collective-permute-start.4 = (bf16[200,1024]{1,0:T(8,128)(2,1)S(1)}, bf16[200,1024]{1,0:T(8,128)(2,1)}, u32[]{:S(2)}, u32[]{:S(2)}) collective-permute-start(bf16[200,1024]{1,0:T(8,128)(2,1)S(1)} %bitcast.43), channel_id=1, source_target_pairs={{0,0},{1,1},{2,2},{3,3},{4,4},{5,5},{6,6},{7,7},{8,16},{9,17},{10,... | collective-permute-start | bytes 1228808 | tf_op jit(solution)/shard_map/ppermute | solution.py:108
  21.1 50.5 %collective-permute-start.7 = (bf16[4,256,896]{2,1,0:T(8,128)(2,1)S(1)}, bf16[4,256,896]{2,1,0:T(8,128)(2,1)}, u32[]{:S(2)}, u32[]{:S(2)}) collective-permute-start(bf16[4,256,896]{2,1,0:T(8,128)(2,1)S(1)} %copy-done), channel_id=1, source_target_pairs={{0,4},{1,5},{2,6},{3,7},{4,0},{5,1},{6,2},{7,3},{8,12},{9,13},{10,... | collective-permute-start | bytes 5505032 | tf_op jit(solution)/shard_map/ppermute | solution.py:108
  22.4 49.3 %collective-permute-start.5 = (bf16[3,800,256]{2,1,0:T(8,128)(2,1)S(1)}, bf16[3,800,256]{2,1,0:T(8,128)(2,1)}, u32[]{:S(2)}, u32[]{:S(2)}) collective-permute-start(bf16[3,800,256]{2,1,0:T(8,128)(2,1)S(1)} %pad_maximum_fusion.own), channel_id=1, source_target_pairs={{0,8},{1,9},{2,10},{3,11},{4,12},{5,13},{6,14},{7,15},{8,0},{9,1},... | collective-permute-start | bytes 3686408 | tf_op jit(solution)/shard_map/ppermute | solution.py:108
  22.4 49.2 %collective-permute-start.6 = (bf16[3,800,256]{2,1,0:T(8,128)(2,1)S(1)}, bf16[3,800,256]{2,1,0:T(8,128)(2,1)}, u32[]{:S(2)}, u32[]{:S(2)}) collective-permute-start(bf16[3,800,256]{2,1,0:T(8,128)(2,1)S(1)} %pad_maximum_fusion.own), channel_id=1, source_target_pairs={{0,0},{1,1},{2,2},{3,3},{4,4},{5,5},{6,6},{7,7},{8,16},{9,17},{10,... | collective-permute-start | bytes 3686408 | tf_op jit(solution)/shard_map/ppermute | solution.py:108
  26.8 32.5 %collective-permute-start.8 = (bf16[200,1024]{1,0:T(8,128)(2,1)}, bf16[200,1024]{1,0:T(8,128)(2,1)}, u32[]{:S(2)}, u32[]{:S(2)}) collective-permute-start(bf16[200,1024]{1,0:T(8,128)(2,1)} %collective-permute-done.4), channel_id=1, source_target_pairs={{0,8},{1,9},{2,10},{3,11},{4,12},{5,13},{6,14},{7,15},{8,0},{9,1},... | collective-permute-start | bytes 1228808 | tf_op jit(solution)/shard_map/ppermute | solution.py:108
  26.8 35.2 %collective-permute-start.10 = (bf16[200,1024]{1,0:T(8,128)(2,1)}, bf16[200,1024]{1,0:T(8,128)(2,1)}, u32[]{:S(2)}, u32[]{:S(2)}) collective-permute-start(bf16[200,1024]{1,0:T(8,128)(2,1)} %collective-permute-done.3), channel_id=1, source_target_pairs={{0,0},{1,1},{2,2},{3,3},{4,4},{5,5},{6,6},{7,7},{8,16},{9,17},{10,... | collective-permute-start | bytes 1228808 | tf_op jit(solution)/shard_map/ppermute | solution.py:108
  74.2 30.9 %collective-permute-start.15 = (bf16[4,256,896]{2,1,0:T(8,128)(2,1)}, bf16[4,256,896]{2,1,0:T(8,128)(2,1)}, u32[]{:S(2)}, u32[]{:S(2)}) collective-permute-start(bf16[4,256,896]{2,1,0:T(8,128)(2,1)} %collective-permute-done.7.xc), channel_id=1, source_target_pairs={{0,2},{1,3},{2,0},{3,1},{4,6},{5,7},{6,4},{7,5},{8,10},{9,11},{10,... | collective-permute-start | bytes 5505032 | tf_op jit(solution)/shard_map/ppermute | solution.py:108
  74.3 28.5 %collective-permute-start.12 = (bf16[3,800,256]{2,1,0:T(8,128)(2,1)}, bf16[3,800,256]{2,1,0:T(8,128)(2,1)S(1)}, u32[]{:S(2)}, u32[]{:S(2)}) collective-permute-start(bf16[3,800,256]{2,1,0:T(8,128)(2,1)} %collective-permute-done.6.middle), channel_id=1, source_target_pairs={{0,8},{1,9},{2,10},{3,11},{4,12},{5,13},{6,14},{7,15},{8,0},{9,1},... | collective-permute-start | bytes 3686408 | tf_op jit(solution)/shard_map/ppermute | solution.py:108
  74.3 30.9 %collective-permute-start.13 = (bf16[3,800,256]{2,1,0:T(8,128)(2,1)}, bf16[3,800,256]{2,1,0:T(8,128)(2,1)}, u32[]{:S(2)}, u32[]{:S(2)}) collective-permute-start(bf16[3,800,256]{2,1,0:T(8,128)(2,1)} %collective-permute-done.5.near), channel_id=1, source_target_pairs={{0,0},{1,1},{2,2},{3,3},{4,4},{5,5},{6,6},{7,7},{8,16},{9,17},{10,... | collective-permute-start | bytes 3686408 | tf_op jit(solution)/shard_map/ppermute | solution.py:108
  80.9 24.3 %collective-permute-start.16 = (bf16[2,200,1024]{2,1,0:T(8,128)(2,1)S(1)}, bf16[2,200,1024]{2,1,0:T(8,128)(2,1)}, u32[]{:S(2)}, u32[]{:S(2)}) collective-permute-start(bf16[2,200,1024]{2,1,0:T(8,128)(2,1)S(1)} %pad_maximum_fusion.1.wa0), channel_id=1, source_target_pairs={{0,4},{1,5},{2,6},{3,7},{4,0},{5,1},{6,2},{7,3},{8,12},{9,13},{10,... | collective-permute-start | bytes 2457608 | tf_op jit(solution)/shard_map/ppermute | solution.py:108
  82.4 22.8 %collective-permute-start.17 = (bf16[200,1024]{1,0:T(8,128)(2,1)S(1)}, bf16[200,1024]{1,0:T(8,128)(2,1)S(1)}, u32[]{:S(2)}, u32[]{:S(2)}) collective-permute-start(bf16[200,1024]{1,0:T(8,128)(2,1)S(1)} %get-tuple-element.97), channel_id=1, source_target_pairs={{0,1},{1,0},{2,3},{3,2},{4,5},{5,4},{6,7},{7,6},{8,9},{9,8},{10,11... | collective-permute-start | bytes 1228808 | tf_op jit(solution)/shard_map/ppermute | solution.py:108
  105.3 18.5 %collective-permute-start.22 = (bf16[2,200,1024]{2,1,0:T(8,128)(2,1)S(1)}, bf16[2,200,1024]{2,1,0:T(8,128)(2,1)S(1)}, u32[]{:S(2)}, u32[]{:S(2)}) collective-permute-start(bf16[2,200,1024]{2,1,0:T(8,128)(2,1)S(1)} %pad_maximum_fusion.2.wa1), channel_id=1, source_target_pairs={{0,4},{1,5},{2,6},{3,7},{4,0},{5,1},{6,2},{7,3},{8,12},{9,13},{10,... | collective-permute-start | bytes 2457608 | tf_op jit(solution)/shard_map/ppermute | solution.py:108
  105.5 30.6 %collective-permute-start.18 = (bf16[3,800,256]{2,1,0:T(8,128)(2,1)}, bf16[3,800,256]{2,1,0:T(8,128)(2,1)S(1)}, u32[]{:S(2)}, u32[]{:S(2)}) collective-permute-start(bf16[3,800,256]{2,1,0:T(8,128)(2,1)} %collective-permute-done.13.middle), channel_id=1, source_target_pairs={{0,8},{1,9},{2,10},{3,11},{4,12},{5,13},{6,14},{7,15},{8,0},{9,1},... | collective-permute-start | bytes 3686408 | tf_op jit(solution)/shard_map/ppermute | solution.py:108
  107.7 28.3 %collective-permute-start.21 = (bf16[2,200,1024]{2,1,0:T(8,128)(2,1)S(1)}, bf16[2,200,1024]{2,1,0:T(8,128)(2,1)}, u32[]{:S(2)}, u32[]{:S(2)}) collective-permute-start(bf16[2,200,1024]{2,1,0:T(8,128)(2,1)S(1)} %pad_maximum_fusion.2.wa1), channel_id=1, source_target_pairs={{0,2},{1,3},{2,0},{3,1},{4,6},{5,7},{6,4},{7,5},{8,10},{9,11},{10,... | collective-permute-start | bytes 2457608 | tf_op jit(solution)/shard_map/ppermute | solution.py:108
  109.8 26.2 %collective-permute-start.19 = (bf16[2,200,1024]{2,1,0:T(8,128)(2,1)S(1)}, bf16[2,200,1024]{2,1,0:T(8,128)(2,1)}, u32[]{:S(2)}, u32[]{:S(2)}) collective-permute-start(bf16[2,200,1024]{2,1,0:T(8,128)(2,1)S(1)} %pad_maximum_fusion.1.wa0), channel_id=1, source_target_pairs={{0,2},{1,3},{2,0},{3,1},{4,6},{5,7},{6,4},{7,5},{8,10},{9,11},{10,... | collective-permute-start | bytes 2457608 | tf_op jit(solution)/shard_map/ppermute | solution.py:108
  109.9 26.2 %collective-permute-start.20 = (bf16[2,200,1024]{2,1,0:T(8,128)(2,1)}, bf16[2,200,1024]{2,1,0:T(8,128)(2,1)}, u32[]{:S(2)}, u32[]{:S(2)}) collective-permute-start(bf16[2,200,1024]{2,1,0:T(8,128)(2,1)} %collective-permute-done.16.wc0), channel_id=1, source_target_pairs={{0,2},{1,3},{2,0},{3,1},{4,6},{5,7},{6,4},{7,5},{8,10},{9,11},{10,... | collective-permute-start | bytes 2457608 | tf_op jit(solution)/shard_map/ppermute | solution.py:108
  123.8 12.3 %collective-permute-start.23 = (bf16[2,200,1024]{2,1,0:T(8,128)(2,1)S(1)}, bf16[2,200,1024]{2,1,0:T(8,128)(2,1)}, u32[]{:S(2)}, u32[]{:S(2)}) collective-permute-start(bf16[2,200,1024]{2,1,0:T(8,128)(2,1)S(1)} %collective-permute-done.22.wc1), channel_id=1, source_target_pairs={{0,2},{1,3},{2,0},{3,1},{4,6},{5,7},{6,4},{7,5},{8,10},{9,11},{10,... | collective-permute-start | bytes 2457608 | tf_op jit(solution)/shard_map/ppermute | solution.py:108
  152.6 12.3 %collective-permute-start.26 = (bf16[2,512,256]{2,1,0:T(8,128)(2,1)}, bf16[2,512,256]{2,1,0:T(8,128)(2,1)S(1)}, u32[]{:S(2)}, u32[]{:S(2)}) collective-permute-start(bf16[2,512,256]{2,1,0:T(8,128)(2,1)} %get-tuple-element.82), channel_id=1, source_target_pairs={{0,8},{1,9},{2,10},{3,11},{4,12},{5,13},{6,14},{7,15},{8,0},{9,1},... | collective-permute-start | bytes 1572872 | tf_op jit(solution)/shard_map/ppermute | solution.py:108
  152.7 14.0 %collective-permute-start.27 = (bf16[2,512,256]{2,1,0:T(8,128)(2,1)}, bf16[2,512,256]{2,1,0:T(8,128)(2,1)S(1)}, u32[]{:S(2)}, u32[]{:S(2)}) collective-permute-start(bf16[2,512,256]{2,1,0:T(8,128)(2,1)} %get-tuple-element.83), channel_id=1, source_target_pairs={{0,0},{1,1},{2,2},{3,3},{4,4},{5,5},{6,6},{7,7},{8,16},{9,17},{10,... | collective-permute-start | bytes 1572872 | tf_op jit(solution)/shard_map/ppermute | solution.py:108
  184.6 10.7 %collective-permute-start.38 = (bf16[256,256]{1,0:T(8,128)(2,1)}, bf16[256,256]{1,0:T(8,128)(2,1)S(1)}, u32[]{:S(2)}, u32[]{:S(2)}) collective-permute-start(bf16[256,256]{1,0:T(8,128)(2,1)} %get-tuple-element.88), channel_id=1, source_target_pairs={{0,7},{1,6},{2,5},{3,4},{4,3},{5,2},{6,1},{7,0},{8,15},{9,14},{10,... | collective-permute-start | bytes 393224 | tf_op jit(solution)/shard_map/ppermute | solution.py:108
  (39 other events, 364.2 us)

commit v8 on v7

--- a/solution.py
+++ b/solution.py
@@ -121,7 +121,7 @@
 
 
 def odd_pair(x):
-    return permuted(x, lambda z, q, y: (3 - z if z in (1, 2) else z, q, y))
+    return permuted(x, lambda z, q, y: (3 - z, q, y) if z in (1, 2) else (z, q ^ 1, y))
 
 
 def tied(*arrays):
@@ -421,7 +421,7 @@
 
 def out_kernel(
     place, c00, c01, c10, c11, c20, c21, c30, c31, wa0, wa1, wb0, wb1, wc0, wc1, wd0, wd1,
-    residual, scale, out, c_all, w_all, total, c_sem, w_sem,
+    residual, scale, out, c_all, w_all, total, placed, c_sem, w_sem,
 ):
     z, q, y = place[0], place[1], place[2]
     width = c00.shape[0]
@@ -432,27 +432,28 @@
             dst = c_all.at[i, pl.ds(at, width), :]
             c_copies.append(pltpu.make_async_copy(pair[i], dst, c_sem.at[r, i]))
     start(c_copies)
-    w_copies = [
-        pltpu.make_async_copy(w, w_all.at[r, j], w_sem.at[r, j])
-        for r, pair in enumerate(((wa0, wa1), (wb0, wb1), (wc0, wc1), (wd0, wd1)))
-        for j, w in enumerate(pair)
-    ]
+    rows = wa0.shape[1]
+    w_copies = []
+    for r, pair in enumerate(((wa0, wa1), (wb0, wb1), (wc0, wc1), (wd0, wd1))):
+        for j in range(2):
+            for i in range(2):
+                dst = w_all.at[i, pl.ds((2 * r + j) * rows, rows), :]
+                w_copies.append(pltpu.make_async_copy(pair[j].at[i], dst, w_sem.at[r, j, i]))
     start(w_copies)
     column = as_column(scale[...])[:out.shape[0]]
     column = jnp.tile(column, (1, out.shape[1] // 128))
     wait(c_copies)
-    rows = wa0.shape[1]
+    wait(w_copies)
+    total[...] = jnp.dot(w_all[0], c_all[0], preferred_element_type=jnp.float32)
+    total[...] += jnp.dot(w_all[1], c_all[1], preferred_element_type=jnp.float32)
+    kept = out.shape[0] // (2 * SLAB)
     for r in range(SLAB):
         for j in range(2):
-            w_copies[2 * r + j].wait()
             slab = jnp.where(z // 2 == y, (z % 2) ^ j, jnp.where(z < 2, j, 1 - j))
-            at = pl.multiple_of((slab * SLAB + (q ^ r)) * rows, 8)
-            term = None
-            for i in range(2):
-                part = jnp.dot(w_all[r, j, i], c_all[i], preferred_element_type=jnp.float32)
-                term = part if term is None else term + part
-            total[pl.ds(at, rows), :] = term
-    out[...] = (residual[...].astype(jnp.float32) + column * total[...]).astype(jnp.bfloat16)
+            at = pl.multiple_of((slab * SLAB + (q ^ r)) * kept, 8)
+            begin = (2 * r + j) * rows
+            placed[pl.ds(at, kept), :] = total[begin:begin + kept, :]
+    out[...] = (residual[...].astype(jnp.float32) + column * placed[...]).astype(jnp.bfloat16)
 
 
 def output(place, blocks, pieces, residual, scale):
@@ -467,10 +468,11 @@
         out_specs=VMEM,
         scratch_shapes=[
             pltpu.VMEM((2, depth, count), jnp.bfloat16),
-            pltpu.VMEM((SLAB, 2, 2, rows, depth), jnp.bfloat16),
+            pltpu.VMEM((2, 2 * SLAB * rows, depth), jnp.bfloat16),
+            pltpu.VMEM((2 * SLAB * rows, count), jnp.float32),
             pltpu.VMEM((share, count), jnp.float32),
             pltpu.SemaphoreType.DMA((SLAB, 2)),
-            pltpu.SemaphoreType.DMA((SLAB, 2)),
+            pltpu.SemaphoreType.DMA((SLAB, 2, 2)),
         ],
         compiler_params=pltpu.CompilerParams(vmem_limit_bytes=KERNEL_VMEM),
         cost_estimate=pl.CostEstimate(
@@ -506,18 +508,19 @@
     by_kind = jnp.transpose(qkv_weight, (1, 0, 2))
     cut = [lax.dynamic_slice_in_dim(by_kind, (q ^ r) * width, width, 2) for r in range(SLAB)]
     got = [cut[0]] + [in_slab(cut[r], r) for r in range(1, SLAB)]
-    x0, out_own = norm(tokens, norm_gain, slabs), jnp.transpose(out_weight)
+    x0 = norm(tokens, norm_gain, slabs)
+    out_own = jnp.pad(jnp.transpose(out_weight), ((0, -out_weight.shape[1] % 16), (0, 0)))
     own = rows_of_slab(q, got)
     out_near, out_mid1 = even_pair(out_own), odd_pair(out_own)
+    out_end1, out_mid2 = even_pair(out_mid1), odd_pair(out_near)
     gains = [lax.dynamic_slice_in_dim(g, q * width, width, 0)[None] for g in (q_gain, k_gain)]
 
     def over_tp(close, far):
         keep, give = jnp.where(home, close, far), jnp.where(home, far, close)
         return keep, across(give)
 
-    own, x0, out_near, out_mid1, *gains = tied(own, x0, out_near, out_mid1, *gains)
+    own, x0, out_end1, out_mid2, *gains = tied(own, x0, out_end1, out_mid2, *gains)
     near, middle1 = even_pair(own), odd_pair(own)
-    out_end1, out_mid2 = even_pair(out_mid1), odd_pair(out_near)
     x2 = in_slab(x0, 2)
     out_end2 = even_pair(out_mid2)
     keep0, got0 = over_tp(out_own, jnp.where(inner, out_mid1, out_end1))

time: 208 us -> 192 us (0.923)
  starting transfers between devices: 55 us -> 45.4 us
  waiting for transfers between devices: 92.9 us -> 88.2 us
  Pallas kernels: 39.5 us -> 37.4 us
    ppermute x39, starting transfers between devices: 55 us -> 45.4 us  [permuted(): return lax.ppermute(x, ('seq', 'tp'), pairs)]
    ppermute x39, waiting for transfers between devices: 92.9 us -> 88.2 us  [permuted(): return lax.ppermute(x, ('seq', 'tp'), pairs)]
    pallas_call x1, Pallas kernels: 10.1 us -> 7.77 us  [output(): pl.pallas_call(out_kernel, out_shape=jax.ShapeDtypeStruct((share, count),...]
  transfers between devices with their start and end apart: 39 -> 39, of which waited for: 17 -> 19; matrix products, arithmetic and copies ran while one was open for 5% -> 6% of each run, Pallas kernels for 6% -> 7%
where the time goes in v8:
time: 192 us; the launch traced here: 191 us
  waiting for transfers between devices  88.2 us (46%)
  starting transfers between devices  45.4 us (24%)
  Pallas kernels  37.4 us (19%)
  local copies, waits for them, and re-layouts  13.1 us (7%)
  other arithmetic  6.1 us (3%)
    ppermute x39, waiting for transfers between devices, permuted(): return lax.ppermute(x, ('seq', 'tp'), pairs)  88.2 us
    ppermute x39, starting transfers between devices, permuted(): return lax.ppermute(x, ('seq', 'tp'), pairs)  45.4 us
    pallas_call x1, Pallas kernels, early(): pl.pallas_call(early_kernel, out_shape=jax.ShapeDtypeStruct((SLAB, kinds,...  9.45 us
    pallas_call x1, Pallas kernels, attend(): pl.pallas_call(functools.partial(attend_kernel, full_width), out_shape=(j...  9.11 us
    pallas_call x1, Pallas kernels, output(): pl.pallas_call(out_kernel, out_shape=jax.ShapeDtypeStruct((share, count),...  7.77 us
    pallas_call x1, Pallas kernels, late(): pl.pallas_call(late_kernel, out_shape=(jax.ShapeDtypeStruct((slab, width)...  7.44 us
    unnamed x49, local copies, waits for them, and re-layouts  6.62 us
  transfers between devices with their start and end apart: 39, of which 19 were waited for; matrix products, arithmetic and copies ran while one was open for 6% of the time, Pallas kernels for 7%

profile of v8, /device:TPU:9, one launch (start us, length us, event | category | flops | bytes accessed | tf_op | source)
XLA Modules:
  0.0 190.6 jit_solution(11162351223773850611)
XLA Ops:
  3.6 2.1 %collective-permute-start = (bf16[3,200,256]{2,1,0:T(8,128)(2,1)S(1)}, bf16[3,200,256]{2,1,0:T(8,128)(2,1)S(1)}, u32[]{:S(2)}, u32[]{:S(2)}) collective-permute-start(bf16[3,200,256]{2,1,0:T(8,128)(2,1)S(1)} %get-tuple-element.101), channel_id=1, source_target_pairs={{0,6},{1,7},{2,4},{3,5},{4,2},{5,3},{6,0},{7,1},{8,14},{9,15},{10,... | collective-permute-start | bytes 921608 | tf_op jit(solution)/shard_map/ppermute | solution.py:108
  6.2 5.7 %collective-permute-done.3 = bf16[208,1024]{1,0:T(8,128)(2,1)} collective-permute-done((bf16[208,1024]{1,0:T(8,128)(2,1)S(1)}, bf16[208,1024]{1,0:T(8,128)(2,1)}, u32[]{:S(2)}, u32[]{:S(2)}) %collective-permute-start.3) | collective-permute-done | bytes 426016 | tf_op jit(solution)/shard_map/ppermute | solution.py:108
  17.1 3.6 %norm.1.xa = bf16[4,256,896]{2,1,0:T(8,128)(2,1)} custom-call(bf16[256,3200]{1,0:T(8,128)(2,1)} %tokens.1, f32[1,3200]{1,0:T(1,128)} %broadcast_in_dim.18.gain), custom_call_target="tpu_custom_call" | custom-call | tf_op jit(solution)/shard_map/norm/pallas_call | solution.py:163
  26.6 1.6 collective-permute-start.8
  31.5 8.6 %collective-permute-done.10 = bf16[208,1024]{1,0:T(8,128)(2,1)S(1)} collective-permute-done((bf16[208,1024]{1,0:T(8,128)(2,1)S(1)}, bf16[208,1024]{1,0:T(8,128)(2,1)S(1)}, u32[]{:S(2)}, u32[]{:S(2)}) %collective-permute-start.10) | collective-permute-done | bytes 426016 | tf_op jit(solution)/shard_map/ppermute | solution.py:108
  40.1 21.8 %collective-permute-done.11 = bf16[208,1024]{1,0:T(8,128)(2,1)S(1)} collective-permute-done((bf16[208,1024]{1,0:T(8,128)(2,1)}, bf16[208,1024]{1,0:T(8,128)(2,1)S(1)}, u32[]{:S(2)}, u32[]{:S(2)}) %collective-permute-start.11) | collective-permute-done | bytes 426016 | tf_op jit(solution)/shard_map/ppermute | solution.py:108
  61.9 1.9 collective-permute-done.9.xc
  63.8 2.7 %collective-permute-start.14 = (bf16[4,256,896]{2,1,0:T(8,128)(2,1)S(1)}, bf16[4,256,896]{2,1,0:T(8,128)(2,1)S(1)}, u32[]{:S(2)}, u32[]{:S(2)}) collective-permute-start(bf16[4,256,896]{2,1,0:T(8,128)(2,1)S(1)} %copy-done), channel_id=1, source_target_pairs={{0,2},{1,3},{2,0},{3,1},{4,6},{5,7},{6,4},{7,5},{8,10},{9,11},{10,... | collective-permute-start | bytes 5505032 | tf_op jit(solution)/shard_map/ppermute | solution.py:108
  69.5 3.0 %collective-permute-done.14.xb = bf16[4,256,896]{2,1,0:T(8,128)(2,1)S(1)} collective-permute-done((bf16[4,256,896]{2,1,0:T(8,128)(2,1)S(1)}, bf16[4,256,896]{2,1,0:T(8,128)(2,1)S(1)}, u32[]{:S(2)}, u32[]{:S(2)}) %collective-permute-start.14) | collective-permute-done | bytes 1835040 | tf_op jit(solution)/shard_map/ppermute | solution.py:108
  77.7 17.4 %collective-permute-done.12.end = bf16[3,800,256]{2,1,0:T(8,128)(2,1)S(1)} collective-permute-done((bf16[3,800,256]{2,1,0:T(8,128)(2,1)}, bf16[3,800,256]{2,1,0:T(8,128)(2,1)S(1)}, u32[]{:S(2)}, u32[]{:S(2)}) %collective-permute-start.12) | collective-permute-done | bytes 1228832 | tf_op jit(solution)/shard_map/ppermute | solution.py:108
  97.7 1.8 collective-permute-start.21
  100.0 15.0 %collective-permute-done.22.wc1 = bf16[2,208,1024]{2,1,0:T(8,128)(2,1)S(1)} collective-permute-done((bf16[2,208,1024]{2,1,0:T(8,128)(2,1)S(1)}, bf16[2,208,1024]{2,1,0:T(8,128)(2,1)S(1)}, u32[]{:S(2)}, u32[]{:S(2)}) %collective-permute-start.22) | collective-permute-done | bytes 852000 | tf_op jit(solution)/shard_map/ppermute | solution.py:108
  115.1 2.6 %collective-permute-start.23 = (bf16[2,208,1024]{2,1,0:T(8,128)(2,1)S(1)}, bf16[2,208,1024]{2,1,0:T(8,128)(2,1)}, u32[]{:S(2)}, u32[]{:S(2)}) collective-permute-start(bf16[2,208,1024]{2,1,0:T(8,128)(2,1)S(1)} %collective-permute-done.22.wc1), channel_id=1, source_target_pairs={{0,2},{1,3},{2,0},{3,1},{4,6},{5,7},{6,4},{7,5},{8,10},{9,11},{10,... | collective-permute-start | bytes 2555912 | tf_op jit(solution)/shard_map/ppermute | solution.py:108
  118.3 9.4 %early.1.acc = f32[4,3,256,256]{3,2,1,0:T(8,128)} custom-call(s32[3]{0:T(128)} %pad_add_fusion.place, bf16[4,256,896]{2,1,0:T(8,128)(2,1)} %norm.1.xa, bf16[4,256,896]{2,1,0:T(8,128)(2,1)} %copy-done.1, bf16[4,256,896]{2,1,0:T(8,128)(2,1)} %collective-permute-done.9.xc, bf16[4,256,896]{2,1,0:T(8,128)(2,1)} %collective-permute-done.15.xd, ...), custom_call_target="tpu_custom_call" | custom-call | flops 3774873600 | bytes 8601600 | tf_op jit(solution)/shard_map/early/pallas_call | solution.py:236
  128.9 7.4 %late.1 = (f32[1024,256]{1,0:T(8,128)}, bf16[1024,256]{1,0:T(8,128)(2,1)}, bf16[1024,256]{1,0:T(8,128)(2,1)}, f32[2,1024]{1,0:T(2,128)}, bf16[2,512,256]{2,1,0:T(8,128)(2,1)}, /*index=5*/bf16[2,512,256]{2,1,0:T(8,128)(2,1)}) custom-call(s32[3]{0:T(128)} %pad_add_fusion.place, bf16[4,256,896]{2,1,0:T(8,128)(2,1)} %norm.1.xa, bf16[4,256,896]{2,1,0:T(8,128)(2,1)} %copy-done.1, ...), custom_call_target="tpu_custom_call" | custom-call | flops 1258291200 | bytes 2867200 | tf_op jit(solution)/shard_map/late/pallas_call | solution.py:305
  142.3 1.7 collective-permute-start.28
  147.0 1.8 collective-permute-done.30
  154.1 9.1 %attend.1 = (bf16[256,256]{1,0:T(8,128)(2,1)}, bf16[256,256]{1,0:T(8,128)(2,1)}, bf16[256,256]{1,0:T(8,128)(2,1)}, bf16[256,256]{1,0:T(8,128)(2,1)}) custom-call(s32[3]{0:T(128)} %pad_add_fusion.place, f32[1024,256]{1,0:T(8,128)} %get-tuple-element.76.query, bf16[1024,256]{1,0:T(8,128)(2,1)} %get-tuple-element.77.keys, ...), custom_call_target="tpu_custom_call" | custom-call | flops 1342177280 | bytes 3145728 | tf_op jit(solution)/shard_map/attend/pallas_call | solution.py:399
  164.5 2.6 %collective-permute-start.33 = (bf16[256,256]{1,0:T(8,128)(2,1)}, bf16[256,256]{1,0:T(8,128)(2,1)S(1)}, u32[]{:S(2)}, u32[]{:S(2)}) collective-permute-start(bf16[256,256]{1,0:T(8,128)(2,1)} %get-tuple-element.86), channel_id=1, source_target_pairs={{0,2},{1,3},{2,0},{3,1},{4,6},{5,7},{6,4},{7,5},{8,10},{9,11},{10,... | collective-permute-start | bytes 393224 | tf_op jit(solution)/shard_map/ppermute | solution.py:108
  169.6 2.8 %collective-permute-start.37 = (bf16[256,256]{1,0:T(8,128)(2,1)}, bf16[256,256]{1,0:T(8,128)(2,1)S(1)}, u32[]{:S(2)}, u32[]{:S(2)}) collective-permute-start(bf16[256,256]{1,0:T(8,128)(2,1)} %get-tuple-element.88), channel_id=1, source_target_pairs={{0,6},{1,7},{2,4},{3,5},{4,2},{5,3},{6,0},{7,1},{8,14},{9,15},{10,... | collective-permute-start | bytes 393224 | tf_op jit(solution)/shard_map/ppermute | solution.py:108
  172.4 1.9 collective-permute-start.38
  176.6 2.7 %collective-permute-done.37.c30 = bf16[256,256]{1,0:T(8,128)(2,1)S(1)} collective-permute-done((bf16[256,256]{1,0:T(8,128)(2,1)}, bf16[256,256]{1,0:T(8,128)(2,1)S(1)}, u32[]{:S(2)}, u32[]{:S(2)}) %collective-permute-start.37) | collective-permute-done | bytes 131104 | tf_op jit(solution)/shard_map/ppermute | solution.py:108
  179.3 2.7 %collective-permute-done.38.c31 = bf16[256,256]{1,0:T(8,128)(2,1)S(1)} collective-permute-done((bf16[256,256]{1,0:T(8,128)(2,1)}, bf16[256,256]{1,0:T(8,128)(2,1)S(1)}, u32[]{:S(2)}, u32[]{:S(2)}) %collective-permute-start.38) | collective-permute-done | bytes 131104 | tf_op jit(solution)/shard_map/ppermute | solution.py:108
  182.7 7.8 %output.1 = bf16[1600,256]{1,0:T(8,128)(2,1)} custom-call(s32[3]{0:T(128)} %pad_add_fusion.place, bf16[256,256]{1,0:T(8,128)(2,1)} %get-tuple-element.85.c00, bf16[256,256]{1,0:T(8,128)(2,1)} %copy-done.10, bf16[256,256]{1,0:T(8,128)(2,1)} %copy-done.11, bf16[256,256]{1,0:T(8,128)(2,1)} %copy-done.12, bf16[256,256]{1,0:T(8,128)(2,1)} %copy-done.13, ...), custom_call_target="tpu_custom_call" | custom-call | flops 1677721600 | bytes 6553600 | tf_op jit(solution)/shard_map/output/pallas_call | solution.py:464
  (127 shorter events, 52.5 us)
Async XLA Ops:
  1.0 10.9 %collective-permute-start.3 = (bf16[208,1024]{1,0:T(8,128)(2,1)S(1)}, bf16[208,1024]{1,0:T(8,128)(2,1)}, u32[]{:S(2)}, u32[]{:S(2)}) collective-permute-start(bf16[208,1024]{1,0:T(8,128)(2,1)S(1)} %pad.8), channel_id=1, source_target_pairs={{0,2},{1,3},{2,0},{3,1},{4,6},{5,7},{6,4},{7,5},{8,16},{9,17},{10,... | collective-permute-start | bytes 1277960 | tf_op jit(solution)/shard_map/ppermute | solution.py:108
  2.4 10.5 %collective-permute-start.5 = (bf16[208,1024]{1,0:T(8,128)(2,1)S(1)}, bf16[208,1024]{1,0:T(8,128)(2,1)}, u32[]{:S(2)}, u32[]{:S(2)}) collective-permute-start(bf16[208,1024]{1,0:T(8,128)(2,1)S(1)} %pad.8), channel_id=1, source_target_pairs={{0,8},{1,9},{2,10},{3,11},{4,12},{5,13},{6,14},{7,15},{8,0},{9,1},... | collective-permute-start | bytes 1277960 | tf_op jit(solution)/shard_map/ppermute | solution.py:108
  3.6 17.0 %collective-permute-start = (bf16[3,200,256]{2,1,0:T(8,128)(2,1)S(1)}, bf16[3,200,256]{2,1,0:T(8,128)(2,1)S(1)}, u32[]{:S(2)}, u32[]{:S(2)}) collective-permute-start(bf16[3,200,256]{2,1,0:T(8,128)(2,1)S(1)} %get-tuple-element.101), channel_id=1, source_target_pairs={{0,6},{1,7},{2,4},{3,5},{4,2},{5,3},{6,0},{7,1},{8,14},{9,15},{10,... | collective-permute-start | bytes 921608 | tf_op jit(solution)/shard_map/ppermute | solution.py:108
  5.8 14.9 %collective-permute-start.1 = (bf16[3,200,256]{2,1,0:T(8,128)(2,1)S(1)}, bf16[3,200,256]{2,1,0:T(8,128)(2,1)S(1)}, u32[]{:S(2)}, u32[]{:S(2)}) collective-permute-start(bf16[3,200,256]{2,1,0:T(8,128)(2,1)S(1)} %get-tuple-element.102), channel_id=1, source_target_pairs={{0,4},{1,5},{2,6},{3,7},{4,0},{5,1},{6,2},{7,3},{8,12},{9,13},{10,... | collective-permute-start | bytes 921608 | tf_op jit(solution)/shard_map/ppermute | solution.py:108
  6.0 14.6 %collective-permute-start.2 = (bf16[3,200,256]{2,1,0:T(8,128)(2,1)S(1)}, bf16[3,200,256]{2,1,0:T(8,128)(2,1)S(1)}, u32[]{:S(2)}, u32[]{:S(2)}) collective-permute-start(bf16[3,200,256]{2,1,0:T(8,128)(2,1)S(1)} %get-tuple-element.103), channel_id=1, source_target_pairs={{0,2},{1,3},{2,0},{3,1},{4,6},{5,7},{6,4},{7,5},{8,10},{9,11},{10,... | collective-permute-start | bytes 921608 | tf_op jit(solution)/shard_map/ppermute | solution.py:108
  11.9 10.2 %collective-permute-start.4 = (bf16[208,1024]{1,0:T(8,128)(2,1)}, bf16[208,1024]{1,0:T(8,128)(2,1)}, u32[]{:S(2)}, u32[]{:S(2)}) collective-permute-start(bf16[208,1024]{1,0:T(8,128)(2,1)} %collective-permute-done.3), channel_id=1, source_target_pairs={{0,8},{1,9},{2,10},{3,11},{4,12},{5,13},{6,14},{7,15},{8,0},{9,1},... | collective-permute-start | bytes 1277960 | tf_op jit(solution)/shard_map/ppermute | solution.py:108
  23.9 39.8 %collective-permute-start.9 = (bf16[4,256,896]{2,1,0:T(8,128)(2,1)S(1)}, bf16[4,256,896]{2,1,0:T(8,128)(2,1)}, u32[]{:S(2)}, u32[]{:S(2)}) collective-permute-start(bf16[4,256,896]{2,1,0:T(8,128)(2,1)S(1)} %copy-done), channel_id=1, source_target_pairs={{0,4},{1,5},{2,6},{3,7},{4,0},{5,1},{6,2},{7,3},{8,12},{9,13},{10,... | collective-permute-start | bytes 5505032 | tf_op jit(solution)/shard_map/ppermute | solution.py:108
  25.1 36.7 %collective-permute-start.7 = (bf16[3,800,256]{2,1,0:T(8,128)(2,1)S(1)}, bf16[3,800,256]{2,1,0:T(8,128)(2,1)}, u32[]{:S(2)}, u32[]{:S(2)}) collective-permute-start(bf16[3,800,256]{2,1,0:T(8,128)(2,1)S(1)} %pad_maximum_fusion.own), channel_id=1, source_target_pairs={{0,8},{1,9},{2,10},{3,11},{4,12},{5,13},{6,14},{7,15},{8,0},{9,1},... | collective-permute-start | bytes 3686408 | tf_op jit(solution)/shard_map/ppermute | solution.py:108
  26.6 35.3 %collective-permute-start.8 = (bf16[3,800,256]{2,1,0:T(8,128)(2,1)S(1)}, bf16[3,800,256]{2,1,0:T(8,128)(2,1)}, u32[]{:S(2)}, u32[]{:S(2)}) collective-permute-start(bf16[3,800,256]{2,1,0:T(8,128)(2,1)S(1)} %pad_maximum_fusion.own), channel_id=1, source_target_pairs={{0,2},{1,3},{2,0},{3,1},{4,6},{5,7},{6,4},{7,5},{8,16},{9,17},{10,... | collective-permute-start | bytes 3686408 | tf_op jit(solution)/shard_map/ppermute | solution.py:108
  29.4 10.7 %collective-permute-start.10 = (bf16[208,1024]{1,0:T(8,128)(2,1)S(1)}, bf16[208,1024]{1,0:T(8,128)(2,1)S(1)}, u32[]{:S(2)}, u32[]{:S(2)}) collective-permute-start(bf16[208,1024]{1,0:T(8,128)(2,1)S(1)} %get-tuple-element.99), channel_id=1, source_target_pairs={{0,1},{1,0},{2,3},{3,2},{4,5},{5,4},{6,7},{7,6},{8,9},{9,8},{10,11... | collective-permute-start | bytes 1277960 | tf_op jit(solution)/shard_map/ppermute | solution.py:108
  30.7 31.1 %collective-permute-start.11 = (bf16[208,1024]{1,0:T(8,128)(2,1)}, bf16[208,1024]{1,0:T(8,128)(2,1)S(1)}, u32[]{:S(2)}, u32[]{:S(2)}) collective-permute-start(bf16[208,1024]{1,0:T(8,128)(2,1)} %collective-permute-done.6), channel_id=1, source_target_pairs={{0,8},{1,9},{2,10},{3,11},{4,12},{5,13},{6,14},{7,15},{8,0},{9,1},... | collective-permute-start | bytes 1277960 | tf_op jit(solution)/shard_map/ppermute | solution.py:108
  66.5 29.6 %collective-permute-start.15 = (bf16[4,256,896]{2,1,0:T(8,128)(2,1)}, bf16[4,256,896]{2,1,0:T(8,128)(2,1)}, u32[]{:S(2)}, u32[]{:S(2)}) collective-permute-start(bf16[4,256,896]{2,1,0:T(8,128)(2,1)} %collective-permute-done.9.xc), channel_id=1, source_target_pairs={{0,2},{1,3},{2,0},{3,1},{4,6},{5,7},{6,4},{7,5},{8,10},{9,11},{10,... | collective-permute-start | bytes 5505032 | tf_op jit(solution)/shard_map/ppermute | solution.py:108
  66.5 28.6 %collective-permute-start.12 = (bf16[3,800,256]{2,1,0:T(8,128)(2,1)}, bf16[3,800,256]{2,1,0:T(8,128)(2,1)S(1)}, u32[]{:S(2)}, u32[]{:S(2)}) collective-permute-start(bf16[3,800,256]{2,1,0:T(8,128)(2,1)} %collective-permute-done.8.middle), channel_id=1, source_target_pairs={{0,8},{1,9},{2,10},{3,11},{4,12},{5,13},{6,14},{7,15},{8,0},{9,1},... | collective-permute-start | bytes 3686408 | tf_op jit(solution)/shard_map/ppermute | solution.py:108
  68.0 28.1 %collective-permute-start.13 = (bf16[3,800,256]{2,1,0:T(8,128)(2,1)}, bf16[3,800,256]{2,1,0:T(8,128)(2,1)}, u32[]{:S(2)}, u32[]{:S(2)}) collective-permute-start(bf16[3,800,256]{2,1,0:T(8,128)(2,1)} %collective-permute-done.7.near), channel_id=1, source_target_pairs={{0,2},{1,3},{2,0},{3,1},{4,6},{5,7},{6,4},{7,5},{8,16},{9,17},{10,... | collective-permute-start | bytes 3686408 | tf_op jit(solution)/shard_map/ppermute | solution.py:108
  73.9 22.2 %collective-permute-start.16 = (bf16[2,208,1024]{2,1,0:T(8,128)(2,1)S(1)}, bf16[2,208,1024]{2,1,0:T(8,128)(2,1)}, u32[]{:S(2)}, u32[]{:S(2)}) collective-permute-start(bf16[2,208,1024]{2,1,0:T(8,128)(2,1)S(1)} %pad_maximum_fusion.1.wa0), channel_id=1, source_target_pairs={{0,4},{1,5},{2,6},{3,7},{4,0},{5,1},{6,2},{7,3},{8,12},{9,13},{10,... | collective-permute-start | bytes 2555912 | tf_op jit(solution)/shard_map/ppermute | solution.py:108
  76.4 19.7 %collective-permute-start.17 = (bf16[208,1024]{1,0:T(8,128)(2,1)S(1)}, bf16[208,1024]{1,0:T(8,128)(2,1)S(1)}, u32[]{:S(2)}, u32[]{:S(2)}) collective-permute-start(bf16[208,1024]{1,0:T(8,128)(2,1)S(1)} %get-tuple-element.97), channel_id=1, source_target_pairs={{0,1},{1,0},{2,3},{3,2},{4,5},{5,4},{6,7},{7,6},{8,9},{9,8},{10,11... | collective-permute-start | bytes 1277960 | tf_op jit(solution)/shard_map/ppermute | solution.py:108
  96.2 18.8 %collective-permute-start.22 = (bf16[2,208,1024]{2,1,0:T(8,128)(2,1)S(1)}, bf16[2,208,1024]{2,1,0:T(8,128)(2,1)S(1)}, u32[]{:S(2)}, u32[]{:S(2)}) collective-permute-start(bf16[2,208,1024]{2,1,0:T(8,128)(2,1)S(1)} %pad_maximum_fusion.2.wa1), channel_id=1, source_target_pairs={{0,4},{1,5},{2,6},{3,7},{4,0},{5,1},{6,2},{7,3},{8,12},{9,13},{10,... | collective-permute-start | bytes 2555912 | tf_op jit(solution)/shard_map/ppermute | solution.py:108
  97.6 30.2 %collective-permute-start.18 = (bf16[3,800,256]{2,1,0:T(8,128)(2,1)}, bf16[3,800,256]{2,1,0:T(8,128)(2,1)S(1)}, u32[]{:S(2)}, u32[]{:S(2)}) collective-permute-start(bf16[3,800,256]{2,1,0:T(8,128)(2,1)} %collective-permute-done.13.middle), channel_id=1, source_target_pairs={{0,8},{1,9},{2,10},{3,11},{4,12},{5,13},{6,14},{7,15},{8,0},{9,1},... | collective-permute-start | bytes 3686408 | tf_op jit(solution)/shard_map/ppermute | solution.py:108
  97.7 30.1 %collective-permute-start.21 = (bf16[2,208,1024]{2,1,0:T(8,128)(2,1)S(1)}, bf16[2,208,1024]{2,1,0:T(8,128)(2,1)}, u32[]{:S(2)}, u32[]{:S(2)}) collective-permute-start(bf16[2,208,1024]{2,1,0:T(8,128)(2,1)S(1)} %pad_maximum_fusion.2.wa1), channel_id=1, source_target_pairs={{0,2},{1,3},{2,0},{3,1},{4,6},{5,7},{6,4},{7,5},{8,10},{9,11},{10,... | collective-permute-start | bytes 2555912 | tf_op jit(solution)/shard_map/ppermute | solution.py:108
  99.5 28.2 %collective-permute-start.19 = (bf16[2,208,1024]{2,1,0:T(8,128)(2,1)S(1)}, bf16[2,208,1024]{2,1,0:T(8,128)(2,1)}, u32[]{:S(2)}, u32[]{:S(2)}) collective-permute-start(bf16[2,208,1024]{2,1,0:T(8,128)(2,1)S(1)} %pad_maximum_fusion.1.wa0), channel_id=1, source_target_pairs={{0,2},{1,3},{2,0},{3,1},{4,6},{5,7},{6,4},{7,5},{8,10},{9,11},{10,... | collective-permute-start | bytes 2555912 | tf_op jit(solution)/shard_map/ppermute | solution.py:108
  99.5 28.3 %collective-permute-start.20 = (bf16[2,208,1024]{2,1,0:T(8,128)(2,1)}, bf16[2,208,1024]{2,1,0:T(8,128)(2,1)}, u32[]{:S(2)}, u32[]{:S(2)}) collective-permute-start(bf16[2,208,1024]{2,1,0:T(8,128)(2,1)} %collective-permute-done.16.wc0), channel_id=1, source_target_pairs={{0,2},{1,3},{2,0},{3,1},{4,6},{5,7},{6,4},{7,5},{8,10},{9,11},{10,... | collective-permute-start | bytes 2555912 | tf_op jit(solution)/shard_map/ppermute | solution.py:108
  115.1 12.8 %collective-permute-start.23 = (bf16[2,208,1024]{2,1,0:T(8,128)(2,1)S(1)}, bf16[2,208,1024]{2,1,0:T(8,128)(2,1)}, u32[]{:S(2)}, u32[]{:S(2)}) collective-permute-start(bf16[2,208,1024]{2,1,0:T(8,128)(2,1)S(1)} %collective-permute-done.22.wc1), channel_id=1, source_target_pairs={{0,2},{1,3},{2,0},{3,1},{4,6},{5,7},{6,4},{7,5},{8,10},{9,11},{10,... | collective-permute-start | bytes 2555912 | tf_op jit(solution)/shard_map/ppermute | solution.py:108
  140.7 12.3 %collective-permute-start.26 = (bf16[2,512,256]{2,1,0:T(8,128)(2,1)}, bf16[2,512,256]{2,1,0:T(8,128)(2,1)S(1)}, u32[]{:S(2)}, u32[]{:S(2)}) collective-permute-start(bf16[2,512,256]{2,1,0:T(8,128)(2,1)} %get-tuple-element.82), channel_id=1, source_target_pairs={{0,8},{1,9},{2,10},{3,11},{4,12},{5,13},{6,14},{7,15},{8,0},{9,1},... | collective-permute-start | bytes 1572872 | tf_op jit(solution)/shard_map/ppermute | solution.py:108
  140.8 12.3 %collective-permute-start.27 = (bf16[2,512,256]{2,1,0:T(8,128)(2,1)}, bf16[2,512,256]{2,1,0:T(8,128)(2,1)S(1)}, u32[]{:S(2)}, u32[]{:S(2)}) collective-permute-start(bf16[2,512,256]{2,1,0:T(8,128)(2,1)} %get-tuple-element.83), channel_id=1, source_target_pairs={{0,2},{1,3},{2,0},{3,1},{4,6},{5,7},{6,4},{7,5},{8,16},{9,17},{10,... | collective-permute-start | bytes 1572872 | tf_op jit(solution)/shard_map/ppermute | solution.py:108
  (39 other events, 352.0 us)

commit v9 on v8

--- a/solution.py
+++ b/solution.py
@@ -256,75 +256,108 @@
     )(place, *xs, own, near, middle, end)
 
 
-def late_kernel(
-    place, xa, xb, xc, xd, acc, middle, end, q_gain, k_gain,
-    query, keys, values, squares, even, odd,
-    x_all, far, held, q_all, k_all, v_all, x_sem, w_sem, acc_sem, sems,
-):
-    z, q = place[0], place[1]
+def last_step(place, xs, acc, middle, end, kinds, x_all, far, held, x_sem, w_sem, acc_sem, use):
+    z = place[0]
     picked_copy(z, middle, end, far, w_sem, False)
-    copies = token_copies((xa, xb, xc, xd), far_slabs(z)[1], x_all, x_sem)
-    loads = [pltpu.make_async_copy(acc.at[r], held.at[r], acc_sem.at[r]) for r in range(SLAB)]
+    copies = token_copies(xs, far_slabs(z)[1], x_all, x_sem)
+    loads = [
+        pltpu.make_async_copy(acc.at[r, pl.ds(kinds[0], len(kinds))], held.at[r], acc_sem.at[r])
+        for r in range(SLAB)
+    ]
     for r in range(SLAB):
         copies[r].start()
         loads[r].start()
-    count = held.shape[2]
-    stores = []
     picked_copy(z, middle, end, far, w_sem, True)
     for r in range(SLAB):
         copies[r].wait()
         loads[r].wait()
         x = x_all[r][:, :far.shape[1]]
-        rows = pl.ds(pl.multiple_of((q ^ r) * count, count), count)
-        for kind in range(3):
-            part = held[r, kind] + jnp.dot(x, far[kind], preferred_element_type=jnp.float32)
-            if kind < 2:
-                summed = as_row(jnp.sum(part * part, axis=1, keepdims=True))
-                squares[kind:kind + 1, rows] = summed[:1]
-                part = part * (q_gain, k_gain)[kind][...]
-            held_out, out = ((q_all, query), (k_all, keys), (v_all, values))[kind]
-            held_out[rows, :] = part.astype(held_out.dtype)
-            store = pltpu.make_async_copy(held_out.at[rows, :], out.at[rows, :], sems.at[3 * r + kind])
-            store.start()
-            stores.append(store)
-    reach = even.shape[1]
-    for n, (out, at) in enumerate(((even, 1 - z % 2), (odd, z % 2))):
-        rows = pl.ds(pl.multiple_of(at * reach, reach), reach)
-        for k, src in enumerate((k_all, v_all)):
-            sem = sems.at[3 * SLAB + 2 * n + k]
-            stores.append(pltpu.make_async_copy(src.at[rows, :], out.at[k], sem))
-            stores[-1].start()
-    wait(stores)
-
-
-def late(place, xs, acc, middle, end, q_gain, k_gain):
+        for n, kind in enumerate(kinds):
+            use(r, kind, held[r, n] + jnp.dot(x, far[n], preferred_element_type=jnp.float32))
+
+
+def block_rows(place, r, count):
+    return pl.ds(pl.multiple_of((place[1] ^ r) * count, count), count)
+
+
+def halo_copies(place, src, even, odd, sems):
+    z, reach = place[0], even.shape[0]
+    return [
+        pltpu.make_async_copy(
+            src.at[pl.ds(pl.multiple_of(at * reach, reach), reach), :], out, sems.at[n]
+        )
+        for n, (out, at) in enumerate(((even, 1 - z % 2), (odd, z % 2)))
+    ]
+
+
+def late_qk_kernel(
+    place, xa, xb, xc, xd, acc, middle, end, q_gain, k_gain, query, keys, even, odd, squares,
+    x_all, far, held, q_all, k_all, x_sem, w_sem, acc_sem, sems, halo_sems,
+):
+    count = held.shape[2]
+    stores = []
+
+    def use(r, kind, part):
+        rows = block_rows(place, r, count)
+        squares[kind:kind + 1, rows] = as_row(jnp.sum(part * part, axis=1, keepdims=True))[:1]
+        gain, whole, out = ((q_gain, q_all, query), (k_gain, k_all, keys))[kind]
+        whole[rows, :] = (part * gain[...]).astype(whole.dtype)
+        sem = sems.at[r, kind]
+        stores.append(pltpu.make_async_copy(whole.at[rows, :], out.at[rows, :], sem))
+        stores[-1].start()
+
+    last_step(
+        place, (xa, xb, xc, xd), acc, middle, end, (0, 1), x_all, far, held, x_sem, w_sem, acc_sem, use
+    )
+    halo = halo_copies(place, k_all, even, odd, halo_sems)
+    start(halo)
+    wait(stores + halo)
+
+
+def late_v_kernel(
+    place, xa, xb, xc, xd, acc, middle, end, values, even, odd,
+    x_all, far, held, v_all, x_sem, w_sem, acc_sem, sems, halo_sems,
+):
+    count = held.shape[2]
+    stores = []
+
+    def use(r, kind, part):
+        rows = block_rows(place, r, count)
+        v_all[rows, :] = part.astype(v_all.dtype)
+        stores.append(pltpu.make_async_copy(v_all.at[rows, :], values.at[rows, :], sems.at[r, 0]))
+        stores[-1].start()
+
+    last_step(
+        place, (xa, xb, xc, xd), acc, middle, end, (2,), x_all, far, held, x_sem, w_sem, acc_sem, use
+    )
+    halo = halo_copies(place, v_all, even, odd, halo_sems)
+    start(halo)
+    wait(stores + halo)
+
+
+def late(kernel, place, xs, acc, middle, end, gains):
     kinds, rows, width = middle.shape
     count, wide = xs[0].shape[1:]
-    slab = SLAB * count
+    slab, reach = SLAB * count, 2 * count
     f32, bf16 = jnp.float32, jnp.bfloat16
+    types = (f32, bf16) if gains else (bf16,)
     return pl.pallas_call(
-        late_kernel,
-        out_shape=(
-            jax.ShapeDtypeStruct((slab, width), f32),
-            jax.ShapeDtypeStruct((slab, width), bf16),
-            jax.ShapeDtypeStruct((slab, width), bf16),
-            jax.ShapeDtypeStruct((2, slab), f32),
-            jax.ShapeDtypeStruct((2, 2 * count, width), bf16),
-            jax.ShapeDtypeStruct((2, 2 * count, width), bf16),
-        ),
-        in_specs=[SMEM] + [HBM] * 7 + [VMEM] * 2,
-        out_specs=(HBM, HBM, HBM, VMEM, HBM, HBM),
+        kernel,
+        out_shape=tuple(jax.ShapeDtypeStruct((slab, width), t) for t in types)
+        + (jax.ShapeDtypeStruct((reach, width), bf16),) * 2
+        + ((jax.ShapeDtypeStruct((2, slab), f32),) if gains else ()),
+        in_specs=[SMEM] + [HBM] * 7 + [VMEM] * len(gains),
+        out_specs=(HBM,) * (len(types) + 2) + ((VMEM,) if gains else ()),
         scratch_shapes=[
             pltpu.VMEM((SLAB, count, wide), bf16),
             pltpu.VMEM((kinds, rows, width), bf16),
             pltpu.VMEM((SLAB, kinds, count, width), f32),
-            pltpu.VMEM((slab, width), f32),
-            pltpu.VMEM((slab, width), bf16),
-            pltpu.VMEM((slab, width), bf16),
+            *[pltpu.VMEM((slab, width), t) for t in types],
             pltpu.SemaphoreType.DMA((SLAB,)),
             pltpu.SemaphoreType.DMA,
             pltpu.SemaphoreType.DMA((SLAB,)),
-            pltpu.SemaphoreType.DMA((3 * SLAB + 4,)),
+            pltpu.SemaphoreType.DMA((SLAB, len(types))),
+            pltpu.SemaphoreType.DMA((2,)),
         ],
         compiler_params=pltpu.CompilerParams(vmem_limit_bytes=KERNEL_VMEM),
         cost_estimate=pl.CostEstimate(
@@ -332,29 +365,32 @@
             bytes_accessed=2 * kinds * rows * width + 2 * slab * rows,
             transcendentals=0,
         ),
-        name="late",
-    )(place, *xs, acc, middle, end, q_gain, k_gain)
+        name=kernel.__name__,
+    )(place, *xs, acc, middle, end, *gains)
 
 
 def attend_kernel(
-    full_width, place, query, keys, values, even, odd, mine, other, seg, o0, o1, o2, o3,
+    full_width, place, query, keys, k_even, k_odd, values, v_even, v_odd, mine, near, mid, seg,
+    o0, o1, o2, o3,
     q_all, k_all, v_all, k_turned, scale_all, sems,
 ):
     z, q = place[0], place[1]
     slab = query.shape[0]
     count = slab // SLAB
-    half = even.shape[1]
+    half = k_even.shape[0]
     upper = half + slab
     is_even = z % 2 == 0
     even_at = pl.multiple_of(jnp.where(is_even, upper, 0), half)
     odd_at = pl.multiple_of(jnp.where(is_even, 0, upper), half)
     copies = [pltpu.make_async_copy(query, q_all, sems.at[0])]
-    for k, (whole, out) in enumerate(((keys, k_all), (values, v_all))):
-        for n, (src, at) in enumerate(((whole, half), (even.at[k], even_at), (odd.at[k], odd_at))):
+    for k, (whole, even, odd, out) in enumerate(
+        ((keys, k_even, k_odd, k_all), (values, v_even, v_odd, v_all))
+    ):
+        for n, (src, at) in enumerate(((whole, half), (even, even_at), (odd, odd_at))):
             dst = out.at[pl.ds(at, src.shape[0]), :]
             copies.append(pltpu.make_async_copy(src, dst, sems.at[1 + 3 * k + n]))
     start(copies)
-    scale = [lax.rsqrt((mine[n] + other[n]) / full_width + eps) for n in range(3)]
+    scale = [lax.rsqrt(sums[...] / full_width + eps) for sums in (mine, near, mid)]
     scale_all[:, half:upper] = scale[0]
     scale_all[:, :half] = jnp.where(is_even, scale[2], scale[1])[:, slab - half:]
     scale_all[:, upper:] = jnp.where(is_even, scale[1], scale[2])[:, :half]
@@ -389,9 +425,9 @@
             out[cols, :] = jnp.transpose(summed / total).astype(jnp.bfloat16)
 
 
-def attend(full_width, place, query, keys, values, even, odd, mine, other, seg):
+def attend(full_width, place, query, keys, k_even, k_odd, values, v_even, v_odd, sums, seg):
     slab, width = query.shape
-    half = even.shape[1]
+    half = k_even.shape[0]
     count = slab // SLAB
     ext = slab + 2 * half
     bf16 = jnp.bfloat16
@@ -399,7 +435,7 @@
     return pl.pallas_call(
         functools.partial(attend_kernel, full_width),
         out_shape=(jax.ShapeDtypeStruct((width, count), bf16),) * SLAB,
-        in_specs=[SMEM] + [HBM] * 5 + [VMEM] * 3,
+        in_specs=[SMEM] + [HBM] * 7 + [VMEM] * 4,
         out_specs=(VMEM,) * SLAB,
         scratch_shapes=[
             pltpu.VMEM((slab, width), jnp.float32),
@@ -416,7 +452,7 @@
             transcendentals=SLAB * count * window * width // HEAD_DIM,
         ),
         name="attend",
-    )(place, query, keys, values, even, odd, mine, other, seg)
+    )(place, query, keys, k_even, k_odd, values, v_even, v_odd, *sums, seg)
 
 
 def out_kernel(
@@ -536,30 +572,38 @@
     end1, middle2, x1, x3, wa0, wc0, keep1, got1 = tied(
         end1, middle2, x1, x3, wa0, wc0, keep1, got1
     )
-    end2 = even_pair(middle2)
+    middle2 = middle2[:2], middle2[2:]
+    end2_qk, end2_v = even_pair(middle2[0]), even_pair(middle2[1])
     wa1 = jnp.stack([keep1, got1])
     wc1 = in_slab(wa1, 2)
     wb0, wd0 = in_slab(wa0, 1), in_slab(wc0, 1)
     xs = (x0, x1, x2, x3)
     acc = early(place, xs, own, near, middle1, end1)
+    acc, wc1, wa1 = tied(acc, wc1, wa1)
     wb1, wd1 = in_slab(wa1, 1), in_slab(wc1, 1)
-    end2, acc, wb0, wd0, wb1, wd1 = tied(end2, acc, wb0, wd0, wb1, wd1)
+    end2_qk, acc, wb0, wd0, wb1, wd1 = tied(end2_qk, acc, wb0, wd0, wb1, wd1)
     pieces = (wa0, wa1, wb0, wb1, wc0, wc1, wd0, wd1)
 
-    query, keys, values, squares, even, odd = late(place, xs, acc, middle2, end2, *gains)
-    sums = jnp.stack([squares, even_pair(squares), odd_pair(squares)])
-    sums, even, odd = tied(sums, even, odd)
-    even, odd = even_pair(even), odd_pair(odd)
-    mine = sums
+    query, keys, k_even, k_odd, squares = late(
+        late_qk_kernel, place, xs, acc, middle2[0], end2_qk, gains
+    )
+    sums = squares
     for r in range(1, SLAB):
-        mine = mine + in_slab(sums, r)
-    other = across(mine)
+        sums = sums + in_slab(squares, r)
+    sums = sums + across(sums)
+    sums, k_even, k_odd, end2_v, acc = tied(sums, k_even, k_odd, end2_v, acc)
+    k_even, k_odd = even_pair(k_even), odd_pair(k_odd)
+    values, v_even, v_odd = late(late_v_kernel, place, xs, acc, middle2[1], end2_v, ())
+    v_even, v_odd = even_pair(v_even), odd_pair(v_odd)
+    sums = (sums, even_pair(sums), odd_pair(sums))
 
     outside = jnp.full((half,), -1, jnp.int32)
     seg = jnp.concatenate([outside, segment_ids, outside], axis=0)
     seg = lax.dynamic_slice_in_dim(seg, z * slab, slab + 2 * half, 0)
     seg = seg.astype(jnp.float32)[None]
-    blocks = attend(full_width, place, query, keys, values, even, odd, mine, other, seg)
+    blocks = attend(
+        full_width, place, query, keys, k_even, k_odd, values, v_even, v_odd, sums, seg
+    )
     spread = []
     for r in range(SLAB):
         for i in range(2):

time: 192 us -> 196 us (1.021)
  Pallas kernels: 37.4 us -> 41.2 us
  waiting for transfers between devices: 88.2 us -> 84.7 us
  starting transfers between devices: 45.4 us -> 48 us
    pallas_call x1 -> x2, Pallas kernels: 7.44 us -> 11.3 us  [late(): pl.pallas_call(kernel, out_shape=tuple((jax.ShapeDtypeStruct((slab, width...]
    ppermute x39 -> x42, waiting for transfers between devices: 88.2 us -> 84.7 us  [permuted(): return lax.ppermute(x, ('seq', 'tp'), pairs)]
    ppermute x39 -> x42, starting transfers between devices: 45.4 us -> 48 us  [permuted(): return lax.ppermute(x, ('seq', 'tp'), pairs)]
    unnamed x49 -> x69, local copies, waits for them, and re-layouts: 6.62 us -> 7.11 us
  transfers between devices with their start and end apart: 39 -> 42, of which waited for: 19 -> 19; matrix products, arithmetic and copies ran while one was open for 6% -> 7% of each run, Pallas kernels for 7% -> 10%
where the time goes in v9:
time: 196 us; the launch traced here: 195 us
  waiting for transfers between devices  84.7 us (43%)
  starting transfers between devices  48 us (24%)
  Pallas kernels  41.2 us (21%)
  local copies, waits for them, and re-layouts  14.6 us (7%)
  other arithmetic  6.07 us (3%)
    ppermute x42, waiting for transfers between devices, permuted(): return lax.ppermute(x, ('seq', 'tp'), pairs)  84.7 us
    ppermute x42, starting transfers between devices, permuted(): return lax.ppermute(x, ('seq', 'tp'), pairs)  48 us
    pallas_call x2, Pallas kernels, late(): pl.pallas_call(kernel, out_shape=tuple((jax.ShapeDtypeStruct((slab, width...  11.3 us
    pallas_call x1, Pallas kernels, early(): pl.pallas_call(early_kernel, out_shape=jax.ShapeDtypeStruct((SLAB, kinds,...  9.43 us
    pallas_call x1, Pallas kernels, attend(): pl.pallas_call(functools.partial(attend_kernel, full_width), out_shape=(j...  9.11 us
    pallas_call x1, Pallas kernels, output(): pl.pallas_call(out_kernel, out_shape=jax.ShapeDtypeStruct((share, count),...  7.77 us
    unnamed x69, local copies, waits for them, and re-layouts  7.11 us
  transfers between devices with their start and end apart: 42, of which 19 were waited for; matrix products, arithmetic and copies ran while one was open for 7% of the time, Pallas kernels for 10%

profile of v9, /device:TPU:9, one launch (start us, length us, event | category | flops | bytes accessed | tf_op | source)
XLA Modules:
  0.0 195.1 jit_solution(10960258414694885898)
XLA Ops:
  3.6 2.1 %collective-permute-start = (bf16[3,200,256]{2,1,0:T(8,128)(2,1)S(1)}, bf16[3,200,256]{2,1,0:T(8,128)(2,1)S(1)}, u32[]{:S(2)}, u32[]{:S(2)}) collective-permute-start(bf16[3,200,256]{2,1,0:T(8,128)(2,1)S(1)} %get-tuple-element.115), channel_id=1, source_target_pairs={{0,6},{1,7},{2,4},{3,5},{4,2},{5,3},{6,0},{7,1},{8,14},{9,15},{10,... | collective-permute-start | bytes 921608 | tf_op jit(solution)/shard_map/ppermute | solution.py:108
  6.2 5.7 %collective-permute-done.3 = bf16[208,1024]{1,0:T(8,128)(2,1)} collective-permute-done((bf16[208,1024]{1,0:T(8,128)(2,1)S(1)}, bf16[208,1024]{1,0:T(8,128)(2,1)}, u32[]{:S(2)}, u32[]{:S(2)}) %collective-permute-start.3) | collective-permute-done | bytes 426016 | tf_op jit(solution)/shard_map/ppermute | solution.py:108
  17.0 3.5 %norm.1.xa = bf16[4,256,896]{2,1,0:T(8,128)(2,1)} custom-call(bf16[256,3200]{1,0:T(8,128)(2,1)} %tokens.1, f32[1,3200]{1,0:T(1,128)} %broadcast_in_dim.18.gain), custom_call_target="tpu_custom_call" | custom-call | tf_op jit(solution)/shard_map/norm/pallas_call | solution.py:163
  31.4 8.6 %collective-permute-done.10 = bf16[208,1024]{1,0:T(8,128)(2,1)S(1)} collective-permute-done((bf16[208,1024]{1,0:T(8,128)(2,1)S(1)}, bf16[208,1024]{1,0:T(8,128)(2,1)S(1)}, u32[]{:S(2)}, u32[]{:S(2)}) %collective-permute-start.10) | collective-permute-done | bytes 426016 | tf_op jit(solution)/shard_map/ppermute | solution.py:108
  40.0 21.8 %collective-permute-done.11 = bf16[208,1024]{1,0:T(8,128)(2,1)S(1)} collective-permute-done((bf16[208,1024]{1,0:T(8,128)(2,1)}, bf16[208,1024]{1,0:T(8,128)(2,1)S(1)}, u32[]{:S(2)}, u32[]{:S(2)}) %collective-permute-start.11) | collective-permute-done | bytes 426016 | tf_op jit(solution)/shard_map/ppermute | solution.py:108
  61.8 1.9 collective-permute-done.9.xc
  63.7 2.7 %collective-permute-start.14 = (bf16[4,256,896]{2,1,0:T(8,128)(2,1)S(1)}, bf16[4,256,896]{2,1,0:T(8,128)(2,1)S(1)}, u32[]{:S(2)}, u32[]{:S(2)}) collective-permute-start(bf16[4,256,896]{2,1,0:T(8,128)(2,1)S(1)} %copy-done), channel_id=1, source_target_pairs={{0,2},{1,3},{2,0},{3,1},{4,6},{5,7},{6,4},{7,5},{8,10},{9,11},{10,... | collective-permute-start | bytes 5505032 | tf_op jit(solution)/shard_map/ppermute | solution.py:108
  69.4 3.0 %collective-permute-done.14.xb = bf16[4,256,896]{2,1,0:T(8,128)(2,1)S(1)} collective-permute-done((bf16[4,256,896]{2,1,0:T(8,128)(2,1)S(1)}, bf16[4,256,896]{2,1,0:T(8,128)(2,1)S(1)}, u32[]{:S(2)}, u32[]{:S(2)}) %collective-permute-start.14) | collective-permute-done | bytes 1835040 | tf_op jit(solution)/shard_map/ppermute | solution.py:108
  77.6 17.5 %collective-permute-done.12.end = bf16[3,800,256]{2,1,0:T(8,128)(2,1)S(1)} collective-permute-done((bf16[3,800,256]{2,1,0:T(8,128)(2,1)}, bf16[3,800,256]{2,1,0:T(8,128)(2,1)S(1)}, u32[]{:S(2)}, u32[]{:S(2)}) %collective-permute-start.12) | collective-permute-done | bytes 1228832 | tf_op jit(solution)/shard_map/ppermute | solution.py:108
  100.3 9.4 %early.1.acc = f32[4,3,256,256]{3,2,1,0:T(8,128)} custom-call(s32[3]{0:T(128)} %pad_add_fusion.place, bf16[4,256,896]{2,1,0:T(8,128)(2,1)} %norm.1.xa, bf16[4,256,896]{2,1,0:T(8,128)(2,1)} %copy-done.1, bf16[4,256,896]{2,1,0:T(8,128)(2,1)} %collective-permute-done.9.xc, bf16[4,256,896]{2,1,0:T(8,128)(2,1)} %copy-done.2, bf16[3,800,256]{2,1,0:T(8,128)(2,1)} %copy-done.3, ...), custom_call_target="tpu_custom_call" | custom-call | flops 3774873600 | bytes 8601600 | tf_op jit(solution)/shard_map/early/pallas_call | solution.py:236
  109.7 5.3 %collective-permute-done.19.wc1 = bf16[2,208,1024]{2,1,0:T(8,128)(2,1)S(1)} collective-permute-done((bf16[2,208,1024]{2,1,0:T(8,128)(2,1)S(1)}, bf16[2,208,1024]{2,1,0:T(8,128)(2,1)S(1)}, u32[]{:S(2)}, u32[]{:S(2)}) %collective-permute-start.19) | collective-permute-done | bytes 852000 | tf_op jit(solution)/shard_map/ppermute | solution.py:108
  115.1 2.5 %collective-permute-start.22 = (bf16[2,208,1024]{2,1,0:T(8,128)(2,1)S(1)}, bf16[2,208,1024]{2,1,0:T(8,128)(2,1)S(1)}, u32[]{:S(2)}, u32[]{:S(2)}) collective-permute-start(bf16[2,208,1024]{2,1,0:T(8,128)(2,1)S(1)} %pad_maximum_fusion.2.wa1), channel_id=1, source_target_pairs={{0,2},{1,3},{2,0},{3,1},{4,6},{5,7},{6,4},{7,5},{8,10},{9,11},{10,... | collective-permute-start | bytes 2555912 | tf_op jit(solution)/shard_map/ppermute | solution.py:108
  121.0 6.4 %late_qk_kernel.1 = (f32[1024,256]{1,0:T(8,128)}, bf16[1024,256]{1,0:T(8,128)(2,1)}, bf16[512,256]{1,0:T(8,128)(2,1)}, bf16[512,256]{1,0:T(8,128)(2,1)}, f32[2,1024]{1,0:T(2,128)}) custom-call(s32[3]{0:T(128)} %pad_add_fusion.place, bf16[4,256,896]{2,1,0:T(8,128)(2,1)} %norm.1.xa, bf16[4,256,896]{2,1,0:T(8,128)(2,1)} %copy-done.1, ...), custom_call_target="tpu_custom_call" | custom-call | flops 838860800 | bytes 2457600 | tf_op jit(solution)/shard_map/late_qk_kernel/pallas_call | solution.py:344
  130.6 1.8 collective-permute-done.26
  136.5 4.9 %late_v_kernel.1 = (bf16[1024,256]{1,0:T(8,128)(2,1)}, bf16[512,256]{1,0:T(8,128)(2,1)}, bf16[512,256]{1,0:T(8,128)(2,1)}) custom-call(s32[3]{0:T(128)} %pad_add_fusion.place, bf16[4,256,896]{2,1,0:T(8,128)(2,1)} %norm.1.xa, bf16[4,256,896]{2,1,0:T(8,128)(2,1)} %copy-done.1, bf16[4,256,896]{2,1,0:T(8,128)(2,1)} %collective-permute-done.9.xc, ...), custom_call_target="tpu_custom_call" | custom-call | flops 419430400 | bytes 2048000 | tf_op jit(solution)/shard_map/late_v_kernel/pallas_call | solution.py:344
  147.6 6.2 %collective-permute-done.33.near = f32[2,1024]{1,0:T(2,128)S(1)} collective-permute-done((f32[2,1024]{1,0:T(2,128)S(1)}, f32[2,1024]{1,0:T(2,128)S(1)}, u32[]{:S(2)}, u32[]{:S(2)}) %collective-permute-start.33) | collective-permute-done | bytes 8224 | tf_op jit(solution)/shard_map/ppermute | solution.py:108
  157.7 9.1 %attend.1 = (bf16[256,256]{1,0:T(8,128)(2,1)}, bf16[256,256]{1,0:T(8,128)(2,1)}, bf16[256,256]{1,0:T(8,128)(2,1)}, bf16[256,256]{1,0:T(8,128)(2,1)}) custom-call(s32[3]{0:T(128)} %pad_add_fusion.place, f32[1024,256]{1,0:T(8,128)} %get-tuple-element.86.query, bf16[1024,256]{1,0:T(8,128)(2,1)} %get-tuple-element.87.keys, bf16[512,256]{1,0:T(8,128)(2,1)} %copy-done.30, ...), custom_call_target="tpu_custom_call" | custom-call | flops 1342177280 | bytes 3145728 | tf_op jit(solution)/shard_map/attend/pallas_call | solution.py:435
  168.1 3.4 %collective-permute-start.36 = (bf16[256,256]{1,0:T(8,128)(2,1)}, bf16[256,256]{1,0:T(8,128)(2,1)S(1)}, u32[]{:S(2)}, u32[]{:S(2)}) collective-permute-start(bf16[256,256]{1,0:T(8,128)(2,1)} %get-tuple-element.100), channel_id=1, source_target_pairs={{0,2},{1,3},{2,0},{3,1},{4,6},{5,7},{6,4},{7,5},{8,10},{9,11},{10,... | collective-permute-start | bytes 393224 | tf_op jit(solution)/shard_map/ppermute | solution.py:108
  172.0 2.1 %collective-permute-start.39 = (bf16[256,256]{1,0:T(8,128)(2,1)}, bf16[256,256]{1,0:T(8,128)(2,1)S(1)}, u32[]{:S(2)}, u32[]{:S(2)}) collective-permute-start(bf16[256,256]{1,0:T(8,128)(2,1)} %get-tuple-element.101), channel_id=1, source_target_pairs={{0,5},{1,4},{2,7},{3,6},{4,1},{5,0},{6,3},{7,2},{8,13},{9,12},{10,... | collective-permute-start | bytes 393224 | tf_op jit(solution)/shard_map/ppermute | solution.py:108
  174.1 1.8 collective-permute-start.40
  175.9 1.9 collective-permute-start.41
  180.2 3.8 %collective-permute-done.40.c30 = bf16[256,256]{1,0:T(8,128)(2,1)S(1)} collective-permute-done((bf16[256,256]{1,0:T(8,128)(2,1)}, bf16[256,256]{1,0:T(8,128)(2,1)S(1)}, u32[]{:S(2)}, u32[]{:S(2)}) %collective-permute-start.40) | collective-permute-done | bytes 131104 | tf_op jit(solution)/shard_map/ppermute | solution.py:108
  184.0 2.5 %collective-permute-done.41.c31 = bf16[256,256]{1,0:T(8,128)(2,1)S(1)} collective-permute-done((bf16[256,256]{1,0:T(8,128)(2,1)}, bf16[256,256]{1,0:T(8,128)(2,1)S(1)}, u32[]{:S(2)}, u32[]{:S(2)}) %collective-permute-start.41) | collective-permute-done | bytes 131104 | tf_op jit(solution)/shard_map/ppermute | solution.py:108
  187.1 7.8 %output.1 = bf16[1600,256]{1,0:T(8,128)(2,1)} custom-call(s32[3]{0:T(128)} %pad_add_fusion.place, bf16[256,256]{1,0:T(8,128)(2,1)} %get-tuple-element.99.c00, bf16[256,256]{1,0:T(8,128)(2,1)} %copy-done.15, bf16[256,256]{1,0:T(8,128)(2,1)} %copy-done.16, bf16[256,256]{1,0:T(8,128)(2,1)} %copy-done.17, bf16[256,256]{1,0:T(8,128)(2,1)} %copy-done.18, ...), custom_call_target="tpu_custom_call" | custom-call | flops 1677721600 | bytes 6553600 | tf_op jit(solution)/shard_map/output/pallas_call | solution.py:500
  (156 shorter events, 58.7 us)
Async XLA Ops:
  1.0 10.9 %collective-permute-start.3 = (bf16[208,1024]{1,0:T(8,128)(2,1)S(1)}, bf16[208,1024]{1,0:T(8,128)(2,1)}, u32[]{:S(2)}, u32[]{:S(2)}) collective-permute-start(bf16[208,1024]{1,0:T(8,128)(2,1)S(1)} %pad.8), channel_id=1, source_target_pairs={{0,2},{1,3},{2,0},{3,1},{4,6},{5,7},{6,4},{7,5},{8,16},{9,17},{10,... | collective-permute-start | bytes 1277960 | tf_op jit(solution)/shard_map/ppermute | solution.py:108
  3.6 16.9 %collective-permute-start = (bf16[3,200,256]{2,1,0:T(8,128)(2,1)S(1)}, bf16[3,200,256]{2,1,0:T(8,128)(2,1)S(1)}, u32[]{:S(2)}, u32[]{:S(2)}) collective-permute-start(bf16[3,200,256]{2,1,0:T(8,128)(2,1)S(1)} %get-tuple-element.115), channel_id=1, source_target_pairs={{0,6},{1,7},{2,4},{3,5},{4,2},{5,3},{6,0},{7,1},{8,14},{9,15},{10,... | collective-permute-start | bytes 921608 | tf_op jit(solution)/shard_map/ppermute | solution.py:108
  5.8 14.8 %collective-permute-start.1 = (bf16[3,200,256]{2,1,0:T(8,128)(2,1)S(1)}, bf16[3,200,256]{2,1,0:T(8,128)(2,1)S(1)}, u32[]{:S(2)}, u32[]{:S(2)}) collective-permute-start(bf16[3,200,256]{2,1,0:T(8,128)(2,1)S(1)} %get-tuple-element.116), channel_id=1, source_target_pairs={{0,4},{1,5},{2,6},{3,7},{4,0},{5,1},{6,2},{7,3},{8,12},{9,13},{10,... | collective-permute-start | bytes 921608 | tf_op jit(solution)/shard_map/ppermute | solution.py:108
  6.0 14.5 %collective-permute-start.2 = (bf16[3,200,256]{2,1,0:T(8,128)(2,1)S(1)}, bf16[3,200,256]{2,1,0:T(8,128)(2,1)S(1)}, u32[]{:S(2)}, u32[]{:S(2)}) collective-permute-start(bf16[3,200,256]{2,1,0:T(8,128)(2,1)S(1)} %get-tuple-element.117), channel_id=1, source_target_pairs={{0,2},{1,3},{2,0},{3,1},{4,6},{5,7},{6,4},{7,5},{8,10},{9,11},{10,... | collective-permute-start | bytes 921608 | tf_op jit(solution)/shard_map/ppermute | solution.py:108
  23.8 39.8 %collective-permute-start.9 = (bf16[4,256,896]{2,1,0:T(8,128)(2,1)S(1)}, bf16[4,256,896]{2,1,0:T(8,128)(2,1)}, u32[]{:S(2)}, u32[]{:S(2)}) collective-permute-start(bf16[4,256,896]{2,1,0:T(8,128)(2,1)S(1)} %copy-done), channel_id=1, source_target_pairs={{0,4},{1,5},{2,6},{3,7},{4,0},{5,1},{6,2},{7,3},{8,12},{9,13},{10,... | collective-permute-start | bytes 5505032 | tf_op jit(solution)/shard_map/ppermute | solution.py:108
  25.0 36.7 %collective-permute-start.7 = (bf16[3,800,256]{2,1,0:T(8,128)(2,1)S(1)}, bf16[3,800,256]{2,1,0:T(8,128)(2,1)}, u32[]{:S(2)}, u32[]{:S(2)}) collective-permute-start(bf16[3,800,256]{2,1,0:T(8,128)(2,1)S(1)} %pad_maximum_fusion.own), channel_id=1, source_target_pairs={{0,8},{1,9},{2,10},{3,11},{4,12},{5,13},{6,14},{7,15},{8,0},{9,1},... | collective-permute-start | bytes 3686408 | tf_op jit(solution)/shard_map/ppermute | solution.py:108
  26.5 35.3 %collective-permute-start.8 = (bf16[3,800,256]{2,1,0:T(8,128)(2,1)S(1)}, bf16[3,800,256]{2,1,0:T(8,128)(2,1)}, u32[]{:S(2)}, u32[]{:S(2)}) collective-permute-start(bf16[3,800,256]{2,1,0:T(8,128)(2,1)S(1)} %pad_maximum_fusion.own), channel_id=1, source_target_pairs={{0,2},{1,3},{2,0},{3,1},{4,6},{5,7},{6,4},{7,5},{8,16},{9,17},{10,... | collective-permute-start | bytes 3686408 | tf_op jit(solution)/shard_map/ppermute | solution.py:108
  29.3 10.7 %collective-permute-start.10 = (bf16[208,1024]{1,0:T(8,128)(2,1)S(1)}, bf16[208,1024]{1,0:T(8,128)(2,1)S(1)}, u32[]{:S(2)}, u32[]{:S(2)}) collective-permute-start(bf16[208,1024]{1,0:T(8,128)(2,1)S(1)} %get-tuple-element.113), channel_id=1, source_target_pairs={{0,1},{1,0},{2,3},{3,2},{4,5},{5,4},{6,7},{7,6},{8,9},{9,8},{10,11... | collective-permute-start | bytes 1277960 | tf_op jit(solution)/shard_map/ppermute | solution.py:108
  30.6 31.1 %collective-permute-start.11 = (bf16[208,1024]{1,0:T(8,128)(2,1)}, bf16[208,1024]{1,0:T(8,128)(2,1)S(1)}, u32[]{:S(2)}, u32[]{:S(2)}) collective-permute-start(bf16[208,1024]{1,0:T(8,128)(2,1)} %collective-permute-done.6), channel_id=1, source_target_pairs={{0,8},{1,9},{2,10},{3,11},{4,12},{5,13},{6,14},{7,15},{8,0},{9,1},... | collective-permute-start | bytes 1277960 | tf_op jit(solution)/shard_map/ppermute | solution.py:108
  66.3 29.7 %collective-permute-start.15 = (bf16[4,256,896]{2,1,0:T(8,128)(2,1)}, bf16[4,256,896]{2,1,0:T(8,128)(2,1)S(1)}, u32[]{:S(2)}, u32[]{:S(2)}) collective-permute-start(bf16[4,256,896]{2,1,0:T(8,128)(2,1)} %collective-permute-done.9.xc), channel_id=1, source_target_pairs={{0,2},{1,3},{2,0},{3,1},{4,6},{5,7},{6,4},{7,5},{8,10},{9,11},{10,... | collective-permute-start | bytes 5505032 | tf_op jit(solution)/shard_map/ppermute | solution.py:108
  66.4 28.8 %collective-permute-start.12 = (bf16[3,800,256]{2,1,0:T(8,128)(2,1)}, bf16[3,800,256]{2,1,0:T(8,128)(2,1)S(1)}, u32[]{:S(2)}, u32[]{:S(2)}) collective-permute-start(bf16[3,800,256]{2,1,0:T(8,128)(2,1)} %collective-permute-done.8.middle), channel_id=1, source_target_pairs={{0,8},{1,9},{2,10},{3,11},{4,12},{5,13},{6,14},{7,15},{8,0},{9,1},... | collective-permute-start | bytes 3686408 | tf_op jit(solution)/shard_map/ppermute | solution.py:108
  68.0 28.0 %collective-permute-start.13 = (bf16[3,800,256]{2,1,0:T(8,128)(2,1)}, bf16[3,800,256]{2,1,0:T(8,128)(2,1)S(1)}, u32[]{:S(2)}, u32[]{:S(2)}) collective-permute-start(bf16[3,800,256]{2,1,0:T(8,128)(2,1)} %collective-permute-done.7.near), channel_id=1, source_target_pairs={{0,2},{1,3},{2,0},{3,1},{4,6},{5,7},{6,4},{7,5},{8,16},{9,17},{10,... | collective-permute-start | bytes 3686408 | tf_op jit(solution)/shard_map/ppermute | solution.py:108
  73.8 22.2 %collective-permute-start.16 = (bf16[2,208,1024]{2,1,0:T(8,128)(2,1)S(1)}, bf16[2,208,1024]{2,1,0:T(8,128)(2,1)}, u32[]{:S(2)}, u32[]{:S(2)}) collective-permute-start(bf16[2,208,1024]{2,1,0:T(8,128)(2,1)S(1)} %pad_maximum_fusion.1.wa0), channel_id=1, source_target_pairs={{0,4},{1,5},{2,6},{3,7},{4,0},{5,1},{6,2},{7,3},{8,12},{9,13},{10,... | collective-permute-start | bytes 2555912 | tf_op jit(solution)/shard_map/ppermute | solution.py:108
  76.3 19.7 %collective-permute-start.17 = (bf16[208,1024]{1,0:T(8,128)(2,1)S(1)}, bf16[208,1024]{1,0:T(8,128)(2,1)S(1)}, u32[]{:S(2)}, u32[]{:S(2)}) collective-permute-start(bf16[208,1024]{1,0:T(8,128)(2,1)S(1)} %get-tuple-element.111), channel_id=1, source_target_pairs={{0,1},{1,0},{2,3},{3,2},{4,5},{5,4},{6,7},{7,6},{8,9},{9,8},{10,11... | collective-permute-start | bytes 1277960 | tf_op jit(solution)/shard_map/ppermute | solution.py:108
  96.1 18.9 %collective-permute-start.19 = (bf16[2,208,1024]{2,1,0:T(8,128)(2,1)S(1)}, bf16[2,208,1024]{2,1,0:T(8,128)(2,1)S(1)}, u32[]{:S(2)}, u32[]{:S(2)}) collective-permute-start(bf16[2,208,1024]{2,1,0:T(8,128)(2,1)S(1)} %pad_maximum_fusion.2.wa1), channel_id=1, source_target_pairs={{0,4},{1,5},{2,6},{3,7},{4,0},{5,1},{6,2},{7,3},{8,12},{9,13},{10,... | collective-permute-start | bytes 2555912 | tf_op jit(solution)/shard_map/ppermute | solution.py:108
  98.1 20.6 %collective-permute-start.18 = (bf16[2,800,256]{2,1,0:T(8,128)(2,1)S(1)}, bf16[2,800,256]{2,1,0:T(8,128)(2,1)}, u32[]{:S(2)}, u32[]{:S(2)}) collective-permute-start(bf16[2,800,256]{2,1,0:T(8,128)(2,1)S(1)} %slice.6.middle), channel_id=1, source_target_pairs={{0,8},{1,9},{2,10},{3,11},{4,12},{5,13},{6,14},{7,15},{8,0},{9,1},... | collective-permute-start | bytes 2457608 | tf_op jit(solution)/shard_map/ppermute | solution.py:108
  98.7 20.5 %collective-permute-start.20 = (bf16[2,208,1024]{2,1,0:T(8,128)(2,1)S(1)}, bf16[2,208,1024]{2,1,0:T(8,128)(2,1)}, u32[]{:S(2)}, u32[]{:S(2)}) collective-permute-start(bf16[2,208,1024]{2,1,0:T(8,128)(2,1)S(1)} %pad_maximum_fusion.1.wa0), channel_id=1, source_target_pairs={{0,2},{1,3},{2,0},{3,1},{4,6},{5,7},{6,4},{7,5},{8,10},{9,11},{10,... | collective-permute-start | bytes 2555912 | tf_op jit(solution)/shard_map/ppermute | solution.py:108
  100.2 19.0 %collective-permute-start.21 = (bf16[2,208,1024]{2,1,0:T(8,128)(2,1)}, bf16[2,208,1024]{2,1,0:T(8,128)(2,1)}, u32[]{:S(2)}, u32[]{:S(2)}) collective-permute-start(bf16[2,208,1024]{2,1,0:T(8,128)(2,1)} %collective-permute-done.16.wc0), channel_id=1, source_target_pairs={{0,2},{1,3},{2,0},{3,1},{4,6},{5,7},{6,4},{7,5},{8,10},{9,11},{10,... | collective-permute-start | bytes 2555912 | tf_op jit(solution)/shard_map/ppermute | solution.py:108
  118.7 17.0 %collective-permute-start.28 = (bf16[1,800,256]{2,1,0:T(8,128)(2,1)S(1)}, bf16[1,800,256]{2,1,0:T(8,128)(2,1)S(1)}, u32[]{:S(2)}, u32[]{:S(2)}) collective-permute-start(bf16[1,800,256]{2,1,0:T(8,128)(2,1)S(1)} %slice.7.middle), channel_id=1, source_target_pairs={{0,8},{1,9},{2,10},{3,11},{4,12},{5,13},{6,14},{7,15},{8,0},{9,1},... | collective-permute-start | bytes 1228808 | tf_op jit(solution)/shard_map/ppermute | solution.py:108
  141.4 15.3 %collective-permute-start.31 = (bf16[512,256]{1,0:T(8,128)(2,1)}, bf16[512,256]{1,0:T(8,128)(2,1)S(1)}, u32[]{:S(2)}, u32[]{:S(2)}) collective-permute-start(bf16[512,256]{1,0:T(8,128)(2,1)} %get-tuple-element.96), channel_id=1, source_target_pairs={{0,8},{1,9},{2,10},{3,11},{4,12},{5,13},{6,14},{7,15},{8,0},{9,1},... | collective-permute-start | bytes 786440 | tf_op jit(solution)/shard_map/ppermute | solution.py:108
  142.5 14.2 %collective-permute-start.32 = (bf16[512,256]{1,0:T(8,128)(2,1)}, bf16[512,256]{1,0:T(8,128)(2,1)S(1)}, u32[]{:S(2)}, u32[]{:S(2)}) collective-permute-start(bf16[512,256]{1,0:T(8,128)(2,1)} %get-tuple-element.97), channel_id=1, source_target_pairs={{0,2},{1,3},{2,0},{3,1},{4,6},{5,7},{6,4},{7,5},{8,16},{9,17},{10,... | collective-permute-start | bytes 786440 | tf_op jit(solution)/shard_map/ppermute | solution.py:108
  143.8 12.9 %collective-permute-start.29 = (bf16[512,256]{1,0:T(8,128)(2,1)S(1)}, bf16[512,256]{1,0:T(8,128)(2,1)S(1)}, u32[]{:S(2)}, u32[]{:S(2)}) collective-permute-start(bf16[512,256]{1,0:T(8,128)(2,1)S(1)} %copy-done.27), channel_id=1, source_target_pairs={{0,8},{1,9},{2,10},{3,11},{4,12},{5,13},{6,14},{7,15},{8,0},{9,1},... | collective-permute-start | bytes 786440 | tf_op jit(solution)/shard_map/ppermute | solution.py:108
  144.7 12.0 %collective-permute-start.30 = (bf16[512,256]{1,0:T(8,128)(2,1)S(1)}, bf16[512,256]{1,0:T(8,128)(2,1)S(1)}, u32[]{:S(2)}, u32[]{:S(2)}) collective-permute-start(bf16[512,256]{1,0:T(8,128)(2,1)S(1)} %copy-done.26), channel_id=1, source_target_pairs={{0,2},{1,3},{2,0},{3,1},{4,6},{5,7},{6,4},{7,5},{8,16},{9,17},{10,... | collective-permute-start | bytes 786440 | tf_op jit(solution)/shard_map/ppermute | solution.py:108
  175.9 10.6 %collective-permute-start.41 = (bf16[256,256]{1,0:T(8,128)(2,1)}, bf16[256,256]{1,0:T(8,128)(2,1)S(1)}, u32[]{:S(2)}, u32[]{:S(2)}) collective-permute-start(bf16[256,256]{1,0:T(8,128)(2,1)} %get-tuple-element.102), channel_id=1, source_target_pairs={{0,7},{1,6},{2,5},{3,4},{4,3},{5,2},{6,1},{7,0},{8,15},{9,14},{10,... | collective-permute-start | bytes 393224 | tf_op jit(solution)/shard_map/ppermute | solution.py:108
  (52 other events, 400.0 us)

commit v10 on v8

--- a/solution.py
+++ b/solution.py
@@ -194,13 +194,20 @@
         copy.wait() if wait else copy.start()
 
 
+def blank_tail(w, rows):
+    tail = w.shape[-2] - rows
+    w[..., rows:, :] = jnp.zeros(w.shape[:-2] + (tail, w.shape[-1]), w.dtype)
+
+
 def early_kernel(
     place, xa, xb, xc, xd, own, near, middle, end, acc, x_all, w_all, held, x_sem, w_sem, sems,
 ):
     z = place[0]
     xs = (xa, xb, xc, xd)
-    near_copy = pltpu.make_async_copy(near, w_all.at[1], w_sem.at[1])
-    own_copy = pltpu.make_async_copy(own, w_all.at[0], w_sem.at[0])
+    kinds, rows = own.shape[:2]
+    taken = pl.ds(0, rows)
+    near_copy = pltpu.make_async_copy(near, w_all.at[1, :, taken, :], w_sem.at[1])
+    own_copy = pltpu.make_async_copy(own, w_all.at[0, :, taken, :], w_sem.at[0])
     x_copies = [
         token_copies(xs, at, x_all.at[i], x_sem.at[i])
         for i, at in enumerate((z, z ^ 1, far_slabs(z)[0]))
@@ -209,18 +216,18 @@
     start(x_copies[0])
     near_copy.start()
     start(x_copies[1])
-    picked_copy(z, middle, end, w_all.at[2], w_sem.at[2], False)
+    picked_copy(z, middle, end, w_all.at[2, :, taken, :], w_sem.at[2], False)
     start(x_copies[2])
-    kinds, rows = own.shape[:2]
+    blank_tail(w_all, rows)
     stores = []
     for step in range(3):
         if step < 2:
             (own_copy, near_copy)[step].wait()
         else:
-            picked_copy(z, middle, end, w_all.at[2], w_sem.at[2], True)
+            picked_copy(z, middle, end, w_all.at[2, :, taken, :], w_sem.at[2], True)
         wait(x_copies[step])
         for r in range(SLAB):
-            x = x_all[step, r][:, :rows]
+            x = x_all[step, r]
             for kind in range(kinds):
                 term = jnp.dot(x, w_all[step, kind], preferred_element_type=jnp.float32)
                 held[r, kind] = term if step == 0 else held[r, kind] + term
@@ -240,7 +247,7 @@
         out_specs=HBM,
         scratch_shapes=[
             pltpu.VMEM((3, SLAB, count, wide), jnp.bfloat16),
-            pltpu.VMEM((3, kinds, rows, width), jnp.bfloat16),
+            pltpu.VMEM((3, kinds, wide, width), jnp.bfloat16),
             pltpu.VMEM((SLAB, kinds, count, width), jnp.float32),
             pltpu.SemaphoreType.DMA((3, SLAB)),
             pltpu.SemaphoreType.DMA((3,)),
@@ -262,7 +269,8 @@
     x_all, far, held, q_all, k_all, v_all, x_sem, w_sem, acc_sem, sems,
 ):
     z, q = place[0], place[1]
-    picked_copy(z, middle, end, far, w_sem, False)
+    taken = far.at[:, pl.ds(0, middle.shape[1]), :]
+    picked_copy(z, middle, end, taken, w_sem, False)
     copies = token_copies((xa, xb, xc, xd), far_slabs(z)[1], x_all, x_sem)
     loads = [pltpu.make_async_copy(acc.at[r], held.at[r], acc_sem.at[r]) for r in range(SLAB)]
     for r in range(SLAB):
@@ -270,11 +278,12 @@
         loads[r].start()
     count = held.shape[2]
     stores = []
-    picked_copy(z, middle, end, far, w_sem, True)
+    blank_tail(far, middle.shape[1])
+    picked_copy(z, middle, end, taken, w_sem, True)
     for r in range(SLAB):
         copies[r].wait()
         loads[r].wait()
-        x = x_all[r][:, :far.shape[1]]
+        x = x_all[r]
         rows = pl.ds(pl.multiple_of((q ^ r) * count, count), count)
         for kind in range(3):
             part = held[r, kind] + jnp.dot(x, far[kind], preferred_element_type=jnp.float32)
@@ -316,7 +325,7 @@
         out_specs=(HBM, HBM, HBM, VMEM, HBM, HBM),
         scratch_shapes=[
             pltpu.VMEM((SLAB, count, wide), bf16),
-            pltpu.VMEM((kinds, rows, width), bf16),
+            pltpu.VMEM((kinds, wide, width), bf16),
             pltpu.VMEM((SLAB, kinds, count, width), f32),
             pltpu.VMEM((slab, width), f32),
             pltpu.VMEM((slab, width), bf16),
@@ -337,7 +346,7 @@
 
 
 def attend_kernel(
-    full_width, place, query, keys, values, even, odd, mine, other, seg, o0, o1, o2, o3,
+    full_width, place, query, keys, values, even, odd, mine, near, mid, seg, o0, o1, o2, o3,
     q_all, k_all, v_all, k_turned, scale_all, sems,
 ):
     z, q = place[0], place[1]
@@ -354,7 +363,7 @@
             dst = out.at[pl.ds(at, src.shape[0]), :]
             copies.append(pltpu.make_async_copy(src, dst, sems.at[1 + 3 * k + n]))
     start(copies)
-    scale = [lax.rsqrt((mine[n] + other[n]) / full_width + eps) for n in range(3)]
+    scale = [lax.rsqrt(sums[...] / full_width + eps) for sums in (mine, near, mid)]
     scale_all[:, half:upper] = scale[0]
     scale_all[:, :half] = jnp.where(is_even, scale[2], scale[1])[:, slab - half:]
     scale_all[:, upper:] = jnp.where(is_even, scale[1], scale[2])[:, :half]
@@ -389,7 +398,7 @@
             out[cols, :] = jnp.transpose(summed / total).astype(jnp.bfloat16)
 
 
-def attend(full_width, place, query, keys, values, even, odd, mine, other, seg):
+def attend(full_width, place, query, keys, values, even, odd, sums, seg):
     slab, width = query.shape
     half = even.shape[1]
     count = slab // SLAB
@@ -399,7 +408,7 @@
     return pl.pallas_call(
         functools.partial(attend_kernel, full_width),
         out_shape=(jax.ShapeDtypeStruct((width, count), bf16),) * SLAB,
-        in_specs=[SMEM] + [HBM] * 5 + [VMEM] * 3,
+        in_specs=[SMEM] + [HBM] * 5 + [VMEM] * 4,
         out_specs=(VMEM,) * SLAB,
         scratch_shapes=[
             pltpu.VMEM((slab, width), jnp.float32),
@@ -416,35 +425,35 @@
             transcendentals=SLAB * count * window * width // HEAD_DIM,
         ),
         name="attend",
-    )(place, query, keys, values, even, odd, mine, other, seg)
+    )(place, query, keys, values, even, odd, *sums, seg)
 
 
 def out_kernel(
-    place, c00, c01, c10, c11, c20, c21, c30, c31, wa0, wa1, wb0, wb1, wc0, wc1, wd0, wd1,
+    place, c20, c01, c31, c30, c11, c21, c10, c00, wa0, wa1, wb0, wb1, wc0, wc1, wd0, wd1,
     residual, scale, out, c_all, w_all, total, placed, c_sem, w_sem,
 ):
     z, q, y = place[0], place[1], place[2]
     width = c00.shape[0]
     c_copies = []
-    for r, pair in enumerate(((c00, c01), (c10, c11), (c20, c21), (c30, c31))):
-        at = pl.multiple_of((q ^ r) * width, width)
-        for i in range(2):
+    for i in range(2):
+        for r, pair in enumerate(((c00, c01), (c10, c11), (c20, c21), (c30, c31))):
+            at = pl.multiple_of((q ^ r) * width, width)
             dst = c_all.at[i, pl.ds(at, width), :]
             c_copies.append(pltpu.make_async_copy(pair[i], dst, c_sem.at[r, i]))
     start(c_copies)
     rows = wa0.shape[1]
     w_copies = []
-    for r, pair in enumerate(((wa0, wa1), (wb0, wb1), (wc0, wc1), (wd0, wd1))):
-        for j in range(2):
-            for i in range(2):
+    for i in range(2):
+        for r, pair in enumerate(((wa0, wa1), (wb0, wb1), (wc0, wc1), (wd0, wd1))):
+            for j in range(2):
                 dst = w_all.at[i, pl.ds((2 * r + j) * rows, rows), :]
                 w_copies.append(pltpu.make_async_copy(pair[j].at[i], dst, w_sem.at[r, j, i]))
     start(w_copies)
     column = as_column(scale[...])[:out.shape[0]]
     column = jnp.tile(column, (1, out.shape[1] // 128))
-    wait(c_copies)
-    wait(w_copies)
+    wait(c_copies[:SLAB] + w_copies[:2 * SLAB])
     total[...] = jnp.dot(w_all[0], c_all[0], preferred_element_type=jnp.float32)
+    wait(c_copies[SLAB:] + w_copies[2 * SLAB:])
     total[...] += jnp.dot(w_all[1], c_all[1], preferred_element_type=jnp.float32)
     kept = out.shape[0] // (2 * SLAB)
     for r in range(SLAB):
@@ -542,29 +551,28 @@
     wb0, wd0 = in_slab(wa0, 1), in_slab(wc0, 1)
     xs = (x0, x1, x2, x3)
     acc = early(place, xs, own, near, middle1, end1)
+    acc, wc1, wa1 = tied(acc, wc1, wa1)
     wb1, wd1 = in_slab(wa1, 1), in_slab(wc1, 1)
     end2, acc, wb0, wd0, wb1, wd1 = tied(end2, acc, wb0, wd0, wb1, wd1)
     pieces = (wa0, wa1, wb0, wb1, wc0, wc1, wd0, wd1)
 
     query, keys, values, squares, even, odd = late(place, xs, acc, middle2, end2, *gains)
-    sums = jnp.stack([squares, even_pair(squares), odd_pair(squares)])
-    sums, even, odd = tied(sums, even, odd)
     even, odd = even_pair(even), odd_pair(odd)
-    mine = sums
+    sums = squares
     for r in range(1, SLAB):
-        mine = mine + in_slab(sums, r)
-    other = across(mine)
+        sums = sums + in_slab(squares, r)
+    sums = sums + across(sums)
+    sums = (sums, even_pair(sums), odd_pair(sums))
 
     outside = jnp.full((half,), -1, jnp.int32)
     seg = jnp.concatenate([outside, segment_ids, outside], axis=0)
     seg = lax.dynamic_slice_in_dim(seg, z * slab, slab + 2 * half, 0)
     seg = seg.astype(jnp.float32)[None]
-    blocks = attend(full_width, place, query, keys, values, even, odd, mine, other, seg)
+    blocks = attend(full_width, place, query, keys, values, even, odd, sums, seg)
     spread = []
-    for r in range(SLAB):
-        for i in range(2):
-            to = functools.partial(lambda r, i, z, q, y: (z, q ^ r, y ^ i), r, i)
-            spread.append(permuted(blocks[r], to) if r or i else blocks[r])
+    for r, i in ((2, 0), (0, 1), (3, 1), (3, 0), (1, 1), (2, 1), (1, 0), (0, 0)):
+        to = functools.partial(lambda r, i, z, q, y: (z, q ^ r, y ^ i), r, i)
+        spread.append(permuted(blocks[r], to) if r or i else blocks[r])
 
     share = layer_scale.shape[0]
     residual = jnp.transpose(lax.dynamic_slice_in_dim(tokens, tp * share, share, 1))

time: 192 us -> 187 us (0.974)
  waiting for transfers between devices: 88.2 us -> 81.2 us
    ppermute x39, waiting for transfers between devices: 88.2 us -> 81.2 us  [permuted(): return lax.ppermute(x, ('seq', 'tp'), pairs)]
    unnamed x49 -> x53, local copies, waits for them, and re-layouts: 6.62 us -> 7.14 us
  transfers between devices with their start and end apart: 39 -> 39, of which waited for: 19 -> 17; matrix products, arithmetic and copies ran while one was open for 6% -> 7% of each run, Pallas kernels for 7% -> 7%
where the time goes in v10:
time: 187 us; the launch traced here: 185 us
  waiting for transfers between devices  81.2 us (43%)
  starting transfers between devices  45.9 us (25%)
  Pallas kernels  38.1 us (20%)
  local copies, waits for them, and re-layouts  13.6 us (7%)
  other arithmetic  6.05 us (3%)
    ppermute x39, waiting for transfers between devices, permuted(): return lax.ppermute(x, ('seq', 'tp'), pairs)  81.2 us
    ppermute x39, starting transfers between devices, permuted(): return lax.ppermute(x, ('seq', 'tp'), pairs)  45.9 us
    pallas_call x1, Pallas kernels, early(): pl.pallas_call(early_kernel, out_shape=jax.ShapeDtypeStruct((SLAB, kinds,...  9.29 us
    pallas_call x1, Pallas kernels, attend(): pl.pallas_call(functools.partial(attend_kernel, full_width), out_shape=(j...  9.11 us
    pallas_call x1, Pallas kernels, output(): pl.pallas_call(out_kernel, out_shape=jax.ShapeDtypeStruct((share, count),...  9.02 us
    unnamed x53, local copies, waits for them, and re-layouts  7.14 us
    pallas_call x1, Pallas kernels, late(): pl.pallas_call(late_kernel, out_shape=(jax.ShapeDtypeStruct((slab, width)...  7.05 us
  transfers between devices with their start and end apart: 39, of which 17 were waited for; matrix products, arithmetic and copies ran while one was open for 7% of the time, Pallas kernels for 7%

profile of v10, /device:TPU:9, one launch (start us, length us, event | category | flops | bytes accessed | tf_op | source)
XLA Modules:
  0.0 185.4 jit_solution(567769565502167737)
XLA Ops:
  3.6 2.1 %collective-permute-start = (bf16[3,200,256]{2,1,0:T(8,128)(2,1)S(1)}, bf16[3,200,256]{2,1,0:T(8,128)(2,1)S(1)}, u32[]{:S(2)}, u32[]{:S(2)}) collective-permute-start(bf16[3,200,256]{2,1,0:T(8,128)(2,1)S(1)} %get-tuple-element.101), channel_id=1, source_target_pairs={{0,6},{1,7},{2,4},{3,5},{4,2},{5,3},{6,0},{7,1},{8,14},{9,15},{10,... | collective-permute-start | bytes 921608 | tf_op jit(solution)/shard_map/ppermute | solution.py:108
  6.2 5.7 %collective-permute-done.3 = bf16[208,1024]{1,0:T(8,128)(2,1)} collective-permute-done((bf16[208,1024]{1,0:T(8,128)(2,1)S(1)}, bf16[208,1024]{1,0:T(8,128)(2,1)}, u32[]{:S(2)}, u32[]{:S(2)}) %collective-permute-start.3) | collective-permute-done | bytes 426016 | tf_op jit(solution)/shard_map/ppermute | solution.py:108
  17.1 3.6 %norm.1.xa = bf16[4,256,896]{2,1,0:T(8,128)(2,1)} custom-call(bf16[256,3200]{1,0:T(8,128)(2,1)} %tokens.1, f32[1,3200]{1,0:T(1,128)} %broadcast_in_dim.18.gain), custom_call_target="tpu_custom_call" | custom-call | tf_op jit(solution)/shard_map/norm/pallas_call | solution.py:163
  26.7 1.6 collective-permute-start.8
  31.6 8.6 %collective-permute-done.10 = bf16[208,1024]{1,0:T(8,128)(2,1)S(1)} collective-permute-done((bf16[208,1024]{1,0:T(8,128)(2,1)S(1)}, bf16[208,1024]{1,0:T(8,128)(2,1)S(1)}, u32[]{:S(2)}, u32[]{:S(2)}) %collective-permute-start.10) | collective-permute-done | bytes 426016 | tf_op jit(solution)/shard_map/ppermute | solution.py:108
  40.2 21.8 %collective-permute-done.11 = bf16[208,1024]{1,0:T(8,128)(2,1)S(1)} collective-permute-done((bf16[208,1024]{1,0:T(8,128)(2,1)}, bf16[208,1024]{1,0:T(8,128)(2,1)S(1)}, u32[]{:S(2)}, u32[]{:S(2)}) %collective-permute-start.11) | collective-permute-done | bytes 426016 | tf_op jit(solution)/shard_map/ppermute | solution.py:108
  62.0 1.9 %collective-permute-done.9.xc = bf16[4,256,896]{2,1,0:T(8,128)(2,1)} collective-permute-done((bf16[4,256,896]{2,1,0:T(8,128)(2,1)S(1)}, bf16[4,256,896]{2,1,0:T(8,128)(2,1)}, u32[]{:S(2)}, u32[]{:S(2)}) %collective-permute-start.9) | collective-permute-done | bytes 1835040 | tf_op jit(solution)/shard_map/ppermute | solution.py:108
  63.9 2.7 %collective-permute-start.14 = (bf16[4,256,896]{2,1,0:T(8,128)(2,1)S(1)}, bf16[4,256,896]{2,1,0:T(8,128)(2,1)S(1)}, u32[]{:S(2)}, u32[]{:S(2)}) collective-permute-start(bf16[4,256,896]{2,1,0:T(8,128)(2,1)S(1)} %copy-done), channel_id=1, source_target_pairs={{0,2},{1,3},{2,0},{3,1},{4,6},{5,7},{6,4},{7,5},{8,10},{9,11},{10,... | collective-permute-start | bytes 5505032 | tf_op jit(solution)/shard_map/ppermute | solution.py:108
  69.6 3.0 %collective-permute-done.14.xb = bf16[4,256,896]{2,1,0:T(8,128)(2,1)S(1)} collective-permute-done((bf16[4,256,896]{2,1,0:T(8,128)(2,1)S(1)}, bf16[4,256,896]{2,1,0:T(8,128)(2,1)S(1)}, u32[]{:S(2)}, u32[]{:S(2)}) %collective-permute-start.14) | collective-permute-done | bytes 1835040 | tf_op jit(solution)/shard_map/ppermute | solution.py:108
  77.8 17.2 %collective-permute-done.12.end = bf16[3,800,256]{2,1,0:T(8,128)(2,1)S(1)} collective-permute-done((bf16[3,800,256]{2,1,0:T(8,128)(2,1)}, bf16[3,800,256]{2,1,0:T(8,128)(2,1)S(1)}, u32[]{:S(2)}, u32[]{:S(2)}) %collective-permute-start.12) | collective-permute-done | bytes 1228832 | tf_op jit(solution)/shard_map/ppermute | solution.py:108
  98.4 1.8 collective-permute-start.20
  100.3 9.3 %early.1.acc = f32[4,3,256,256]{3,2,1,0:T(8,128)} custom-call(s32[3]{0:T(128)} %pad_add_fusion.place, bf16[4,256,896]{2,1,0:T(8,128)(2,1)} %norm.1.xa, bf16[4,256,896]{2,1,0:T(8,128)(2,1)} %copy-done.1, bf16[4,256,896]{2,1,0:T(8,128)(2,1)} %collective-permute-done.9.xc, bf16[4,256,896]{2,1,0:T(8,128)(2,1)} %collective-permute-done.15.xd, ...), custom_call_target="tpu_custom_call" | custom-call | flops 3774873600 | bytes 8601600 | tf_op jit(solution)/shard_map/early/pallas_call | solution.py:243
  109.6 5.7 %collective-permute-done.19.wc1 = bf16[2,208,1024]{2,1,0:T(8,128)(2,1)S(1)} collective-permute-done((bf16[2,208,1024]{2,1,0:T(8,128)(2,1)S(1)}, bf16[2,208,1024]{2,1,0:T(8,128)(2,1)S(1)}, u32[]{:S(2)}, u32[]{:S(2)}) %collective-permute-start.19) | collective-permute-done | bytes 852000 | tf_op jit(solution)/shard_map/ppermute | solution.py:108
  115.3 2.5 %collective-permute-start.22 = (bf16[2,208,1024]{2,1,0:T(8,128)(2,1)S(1)}, bf16[2,208,1024]{2,1,0:T(8,128)(2,1)S(1)}, u32[]{:S(2)}, u32[]{:S(2)}) collective-permute-start(bf16[2,208,1024]{2,1,0:T(8,128)(2,1)S(1)} %pad_maximum_fusion.2.wa1), channel_id=1, source_target_pairs={{0,2},{1,3},{2,0},{3,1},{4,6},{5,7},{6,4},{7,5},{8,10},{9,11},{10,... | collective-permute-start | bytes 2555912 | tf_op jit(solution)/shard_map/ppermute | solution.py:108
  117.9 6.7 %collective-permute-done.18.end = bf16[3,800,256]{2,1,0:T(8,128)(2,1)S(1)} collective-permute-done((bf16[3,800,256]{2,1,0:T(8,128)(2,1)}, bf16[3,800,256]{2,1,0:T(8,128)(2,1)S(1)}, u32[]{:S(2)}, u32[]{:S(2)}) %collective-permute-start.18) | collective-permute-done | bytes 1228832 | tf_op jit(solution)/shard_map/ppermute | solution.py:108
  125.9 7.0 %late.1 = (f32[1024,256]{1,0:T(8,128)}, bf16[1024,256]{1,0:T(8,128)(2,1)}, bf16[1024,256]{1,0:T(8,128)(2,1)}, f32[2,1024]{1,0:T(2,128)}, bf16[2,512,256]{2,1,0:T(8,128)(2,1)}, /*index=5*/bf16[2,512,256]{2,1,0:T(8,128)(2,1)}) custom-call(s32[3]{0:T(128)} %pad_add_fusion.place, bf16[4,256,896]{2,1,0:T(8,128)(2,1)} %norm.1.xa, bf16[4,256,896]{2,1,0:T(8,128)(2,1)} %copy-done.1, ...), custom_call_target="tpu_custom_call" | custom-call | flops 1258291200 | bytes 2867200 | tf_op jit(solution)/shard_map/late/pallas_call | solution.py:314
  133.9 1.6 collective-permute-start.25
  135.4 3.0 %collective-permute-start.26 = (f32[2,1024]{1,0:T(2,128)}, f32[2,1024]{1,0:T(2,128)S(1)}, u32[]{:S(2)}, u32[]{:S(2)}) collective-permute-start(f32[2,1024]{1,0:T(2,128)} %get-tuple-element.84), channel_id=1, source_target_pairs={{0,2},{1,3},{2,0},{3,1},{4,6},{5,7},{6,4},{7,5},{8,10},{9,11},{10,... | collective-permute-start | bytes 24584 | tf_op jit(solution)/shard_map/ppermute | solution.py:108
  149.6 9.1 %attend.1 = (bf16[256,256]{1,0:T(8,128)(2,1)}, bf16[256,256]{1,0:T(8,128)(2,1)}, bf16[256,256]{1,0:T(8,128)(2,1)}, bf16[256,256]{1,0:T(8,128)(2,1)}) custom-call(s32[3]{0:T(128)} %pad_add_fusion.place, f32[1024,256]{1,0:T(8,128)} %get-tuple-element.79.query, bf16[1024,256]{1,0:T(8,128)(2,1)} %get-tuple-element.80.keys, ...), custom_call_target="tpu_custom_call" | custom-call | flops 1342177280 | bytes 3145728 | tf_op jit(solution)/shard_map/attend/pallas_call | solution.py:408
  161.2 2.7 %collective-permute-start.34 = (bf16[256,256]{1,0:T(8,128)(2,1)}, bf16[256,256]{1,0:T(8,128)(2,1)S(1)}, u32[]{:S(2)}, u32[]{:S(2)}) collective-permute-start(bf16[256,256]{1,0:T(8,128)(2,1)} %get-tuple-element.87), channel_id=1, source_target_pairs={{0,7},{1,6},{2,5},{3,4},{4,3},{5,2},{6,1},{7,0},{8,15},{9,14},{10,... | collective-permute-start | bytes 393224 | tf_op jit(solution)/shard_map/ppermute | solution.py:108
  164.0 2.0 %collective-permute-start.37 = (bf16[256,256]{1,0:T(8,128)(2,1)}, bf16[256,256]{1,0:T(8,128)(2,1)S(1)}, u32[]{:S(2)}, u32[]{:S(2)}) collective-permute-start(bf16[256,256]{1,0:T(8,128)(2,1)} %get-tuple-element.85), channel_id=1, source_target_pairs={{0,5},{1,4},{2,7},{3,6},{4,1},{5,0},{6,3},{7,2},{8,13},{9,12},{10,... | collective-permute-start | bytes 393224 | tf_op jit(solution)/shard_map/ppermute | solution.py:108
  167.2 2.9 %collective-permute-start.38 = (bf16[256,256]{1,0:T(8,128)(2,1)}, bf16[256,256]{1,0:T(8,128)(2,1)S(1)}, u32[]{:S(2)}, u32[]{:S(2)}) collective-permute-start(bf16[256,256]{1,0:T(8,128)(2,1)} %get-tuple-element.88), channel_id=1, source_target_pairs={{0,2},{1,3},{2,0},{3,1},{4,6},{5,7},{6,4},{7,5},{8,10},{9,11},{10,... | collective-permute-start | bytes 393224 | tf_op jit(solution)/shard_map/ppermute | solution.py:108
  172.4 3.0 %collective-permute-done.36.c11 = bf16[256,256]{1,0:T(8,128)(2,1)S(1)} collective-permute-done((bf16[256,256]{1,0:T(8,128)(2,1)}, bf16[256,256]{1,0:T(8,128)(2,1)S(1)}, u32[]{:S(2)}, u32[]{:S(2)}) %collective-permute-start.36) | collective-permute-done | bytes 131104 | tf_op jit(solution)/shard_map/ppermute | solution.py:108
  176.2 9.0 %output.1 = bf16[1600,256]{1,0:T(8,128)(2,1)} custom-call(s32[3]{0:T(128)} %pad_add_fusion.place, bf16[256,256]{1,0:T(8,128)(2,1)} %copy-done.11, bf16[256,256]{1,0:T(8,128)(2,1)} %copy-done.12, bf16[256,256]{1,0:T(8,128)(2,1)} %copy-done.13, bf16[256,256]{1,0:T(8,128)(2,1)} %copy-done.14, bf16[256,256]{1,0:T(8,128)(2,1)} %copy-done.16, ...), custom_call_target="tpu_custom_call" | custom-call | flops 1677721600 | bytes 6553600 | tf_op jit(solution)/shard_map/output/pallas_call | solution.py:473
  (131 shorter events, 50.2 us)
Async XLA Ops:
  1.0 10.9 %collective-permute-start.3 = (bf16[208,1024]{1,0:T(8,128)(2,1)S(1)}, bf16[208,1024]{1,0:T(8,128)(2,1)}, u32[]{:S(2)}, u32[]{:S(2)}) collective-permute-start(bf16[208,1024]{1,0:T(8,128)(2,1)S(1)} %pad.8), channel_id=1, source_target_pairs={{0,2},{1,3},{2,0},{3,1},{4,6},{5,7},{6,4},{7,5},{8,16},{9,17},{10,... | collective-permute-start | bytes 1277960 | tf_op jit(solution)/shard_map/ppermute | solution.py:108
  2.4 10.5 %collective-permute-start.5 = (bf16[208,1024]{1,0:T(8,128)(2,1)S(1)}, bf16[208,1024]{1,0:T(8,128)(2,1)}, u32[]{:S(2)}, u32[]{:S(2)}) collective-permute-start(bf16[208,1024]{1,0:T(8,128)(2,1)S(1)} %pad.8), channel_id=1, source_target_pairs={{0,8},{1,9},{2,10},{3,11},{4,12},{5,13},{6,14},{7,15},{8,0},{9,1},... | collective-permute-start | bytes 1277960 | tf_op jit(solution)/shard_map/ppermute | solution.py:108
  3.6 17.1 %collective-permute-start = (bf16[3,200,256]{2,1,0:T(8,128)(2,1)S(1)}, bf16[3,200,256]{2,1,0:T(8,128)(2,1)S(1)}, u32[]{:S(2)}, u32[]{:S(2)}) collective-permute-start(bf16[3,200,256]{2,1,0:T(8,128)(2,1)S(1)} %get-tuple-element.101), channel_id=1, source_target_pairs={{0,6},{1,7},{2,4},{3,5},{4,2},{5,3},{6,0},{7,1},{8,14},{9,15},{10,... | collective-permute-start | bytes 921608 | tf_op jit(solution)/shard_map/ppermute | solution.py:108
  5.8 15.0 %collective-permute-start.1 = (bf16[3,200,256]{2,1,0:T(8,128)(2,1)S(1)}, bf16[3,200,256]{2,1,0:T(8,128)(2,1)S(1)}, u32[]{:S(2)}, u32[]{:S(2)}) collective-permute-start(bf16[3,200,256]{2,1,0:T(8,128)(2,1)S(1)} %get-tuple-element.102), channel_id=1, source_target_pairs={{0,4},{1,5},{2,6},{3,7},{4,0},{5,1},{6,2},{7,3},{8,12},{9,13},{10,... | collective-permute-start | bytes 921608 | tf_op jit(solution)/shard_map/ppermute | solution.py:108
  6.0 14.7 %collective-permute-start.2 = (bf16[3,200,256]{2,1,0:T(8,128)(2,1)S(1)}, bf16[3,200,256]{2,1,0:T(8,128)(2,1)S(1)}, u32[]{:S(2)}, u32[]{:S(2)}) collective-permute-start(bf16[3,200,256]{2,1,0:T(8,128)(2,1)S(1)} %get-tuple-element.103), channel_id=1, source_target_pairs={{0,2},{1,3},{2,0},{3,1},{4,6},{5,7},{6,4},{7,5},{8,10},{9,11},{10,... | collective-permute-start | bytes 921608 | tf_op jit(solution)/shard_map/ppermute | solution.py:108
  11.9 10.3 %collective-permute-start.4 = (bf16[208,1024]{1,0:T(8,128)(2,1)}, bf16[208,1024]{1,0:T(8,128)(2,1)}, u32[]{:S(2)}, u32[]{:S(2)}) collective-permute-start(bf16[208,1024]{1,0:T(8,128)(2,1)} %collective-permute-done.3), channel_id=1, source_target_pairs={{0,8},{1,9},{2,10},{3,11},{4,12},{5,13},{6,14},{7,15},{8,0},{9,1},... | collective-permute-start | bytes 1277960 | tf_op jit(solution)/shard_map/ppermute | solution.py:108
  24.0 39.8 %collective-permute-start.9 = (bf16[4,256,896]{2,1,0:T(8,128)(2,1)S(1)}, bf16[4,256,896]{2,1,0:T(8,128)(2,1)}, u32[]{:S(2)}, u32[]{:S(2)}) collective-permute-start(bf16[4,256,896]{2,1,0:T(8,128)(2,1)S(1)} %copy-done), channel_id=1, source_target_pairs={{0,4},{1,5},{2,6},{3,7},{4,0},{5,1},{6,2},{7,3},{8,12},{9,13},{10,... | collective-permute-start | bytes 5505032 | tf_op jit(solution)/shard_map/ppermute | solution.py:108
  25.2 36.7 %collective-permute-start.7 = (bf16[3,800,256]{2,1,0:T(8,128)(2,1)S(1)}, bf16[3,800,256]{2,1,0:T(8,128)(2,1)}, u32[]{:S(2)}, u32[]{:S(2)}) collective-permute-start(bf16[3,800,256]{2,1,0:T(8,128)(2,1)S(1)} %pad_maximum_fusion.own), channel_id=1, source_target_pairs={{0,8},{1,9},{2,10},{3,11},{4,12},{5,13},{6,14},{7,15},{8,0},{9,1},... | collective-permute-start | bytes 3686408 | tf_op jit(solution)/shard_map/ppermute | solution.py:108
  26.7 35.3 %collective-permute-start.8 = (bf16[3,800,256]{2,1,0:T(8,128)(2,1)S(1)}, bf16[3,800,256]{2,1,0:T(8,128)(2,1)}, u32[]{:S(2)}, u32[]{:S(2)}) collective-permute-start(bf16[3,800,256]{2,1,0:T(8,128)(2,1)S(1)} %pad_maximum_fusion.own), channel_id=1, source_target_pairs={{0,2},{1,3},{2,0},{3,1},{4,6},{5,7},{6,4},{7,5},{8,16},{9,17},{10,... | collective-permute-start | bytes 3686408 | tf_op jit(solution)/shard_map/ppermute | solution.py:108
  29.5 10.7 %collective-permute-start.10 = (bf16[208,1024]{1,0:T(8,128)(2,1)S(1)}, bf16[208,1024]{1,0:T(8,128)(2,1)S(1)}, u32[]{:S(2)}, u32[]{:S(2)}) collective-permute-start(bf16[208,1024]{1,0:T(8,128)(2,1)S(1)} %get-tuple-element.99), channel_id=1, source_target_pairs={{0,1},{1,0},{2,3},{3,2},{4,5},{5,4},{6,7},{7,6},{8,9},{9,8},{10,11... | collective-permute-start | bytes 1277960 | tf_op jit(solution)/shard_map/ppermute | solution.py:108
  30.8 31.1 %collective-permute-start.11 = (bf16[208,1024]{1,0:T(8,128)(2,1)}, bf16[208,1024]{1,0:T(8,128)(2,1)S(1)}, u32[]{:S(2)}, u32[]{:S(2)}) collective-permute-start(bf16[208,1024]{1,0:T(8,128)(2,1)} %collective-permute-done.6), channel_id=1, source_target_pairs={{0,8},{1,9},{2,10},{3,11},{4,12},{5,13},{6,14},{7,15},{8,0},{9,1},... | collective-permute-start | bytes 1277960 | tf_op jit(solution)/shard_map/ppermute | solution.py:108
  66.6 29.7 %collective-permute-start.15 = (bf16[4,256,896]{2,1,0:T(8,128)(2,1)}, bf16[4,256,896]{2,1,0:T(8,128)(2,1)}, u32[]{:S(2)}, u32[]{:S(2)}) collective-permute-start(bf16[4,256,896]{2,1,0:T(8,128)(2,1)} %collective-permute-done.9.xc), channel_id=1, source_target_pairs={{0,2},{1,3},{2,0},{3,1},{4,6},{5,7},{6,4},{7,5},{8,10},{9,11},{10,... | collective-permute-start | bytes 5505032 | tf_op jit(solution)/shard_map/ppermute | solution.py:108
  66.6 28.4 %collective-permute-start.12 = (bf16[3,800,256]{2,1,0:T(8,128)(2,1)}, bf16[3,800,256]{2,1,0:T(8,128)(2,1)S(1)}, u32[]{:S(2)}, u32[]{:S(2)}) collective-permute-start(bf16[3,800,256]{2,1,0:T(8,128)(2,1)} %collective-permute-done.8.middle), channel_id=1, source_target_pairs={{0,8},{1,9},{2,10},{3,11},{4,12},{5,13},{6,14},{7,15},{8,0},{9,1},... | collective-permute-start | bytes 3686408 | tf_op jit(solution)/shard_map/ppermute | solution.py:108
  68.0 28.2 %collective-permute-start.13 = (bf16[3,800,256]{2,1,0:T(8,128)(2,1)}, bf16[3,800,256]{2,1,0:T(8,128)(2,1)}, u32[]{:S(2)}, u32[]{:S(2)}) collective-permute-start(bf16[3,800,256]{2,1,0:T(8,128)(2,1)} %collective-permute-done.7.near), channel_id=1, source_target_pairs={{0,2},{1,3},{2,0},{3,1},{4,6},{5,7},{6,4},{7,5},{8,16},{9,17},{10,... | collective-permute-start | bytes 3686408 | tf_op jit(solution)/shard_map/ppermute | solution.py:108
  74.0 22.3 %collective-permute-start.16 = (bf16[2,208,1024]{2,1,0:T(8,128)(2,1)S(1)}, bf16[2,208,1024]{2,1,0:T(8,128)(2,1)}, u32[]{:S(2)}, u32[]{:S(2)}) collective-permute-start(bf16[2,208,1024]{2,1,0:T(8,128)(2,1)S(1)} %pad_maximum_fusion.1.wa0), channel_id=1, source_target_pairs={{0,4},{1,5},{2,6},{3,7},{4,0},{5,1},{6,2},{7,3},{8,12},{9,13},{10,... | collective-permute-start | bytes 2555912 | tf_op jit(solution)/shard_map/ppermute | solution.py:108
  76.5 19.8 %collective-permute-start.17 = (bf16[208,1024]{1,0:T(8,128)(2,1)S(1)}, bf16[208,1024]{1,0:T(8,128)(2,1)S(1)}, u32[]{:S(2)}, u32[]{:S(2)}) collective-permute-start(bf16[208,1024]{1,0:T(8,128)(2,1)S(1)} %get-tuple-element.97), channel_id=1, source_target_pairs={{0,1},{1,0},{2,3},{3,2},{4,5},{5,4},{6,7},{7,6},{8,9},{9,8},{10,11... | collective-permute-start | bytes 1277960 | tf_op jit(solution)/shard_map/ppermute | solution.py:108
  96.4 18.9 %collective-permute-start.19 = (bf16[2,208,1024]{2,1,0:T(8,128)(2,1)S(1)}, bf16[2,208,1024]{2,1,0:T(8,128)(2,1)S(1)}, u32[]{:S(2)}, u32[]{:S(2)}) collective-permute-start(bf16[2,208,1024]{2,1,0:T(8,128)(2,1)S(1)} %pad_maximum_fusion.2.wa1), channel_id=1, source_target_pairs={{0,4},{1,5},{2,6},{3,7},{4,0},{5,1},{6,2},{7,3},{8,12},{9,13},{10,... | collective-permute-start | bytes 2555912 | tf_op jit(solution)/shard_map/ppermute | solution.py:108
  97.7 26.9 %collective-permute-start.18 = (bf16[3,800,256]{2,1,0:T(8,128)(2,1)}, bf16[3,800,256]{2,1,0:T(8,128)(2,1)S(1)}, u32[]{:S(2)}, u32[]{:S(2)}) collective-permute-start(bf16[3,800,256]{2,1,0:T(8,128)(2,1)} %collective-permute-done.13.middle), channel_id=1, source_target_pairs={{0,8},{1,9},{2,10},{3,11},{4,12},{5,13},{6,14},{7,15},{8,0},{9,1},... | collective-permute-start | bytes 3686408 | tf_op jit(solution)/shard_map/ppermute | solution.py:108
  98.4 19.5 %collective-permute-start.20 = (bf16[2,208,1024]{2,1,0:T(8,128)(2,1)S(1)}, bf16[2,208,1024]{2,1,0:T(8,128)(2,1)}, u32[]{:S(2)}, u32[]{:S(2)}) collective-permute-start(bf16[2,208,1024]{2,1,0:T(8,128)(2,1)S(1)} %pad_maximum_fusion.1.wa0), channel_id=1, source_target_pairs={{0,2},{1,3},{2,0},{3,1},{4,6},{5,7},{6,4},{7,5},{8,10},{9,11},{10,... | collective-permute-start | bytes 2555912 | tf_op jit(solution)/shard_map/ppermute | solution.py:108
  100.2 17.7 %collective-permute-start.21 = (bf16[2,208,1024]{2,1,0:T(8,128)(2,1)}, bf16[2,208,1024]{2,1,0:T(8,128)(2,1)}, u32[]{:S(2)}, u32[]{:S(2)}) collective-permute-start(bf16[2,208,1024]{2,1,0:T(8,128)(2,1)} %collective-permute-done.16.wc0), channel_id=1, source_target_pairs={{0,2},{1,3},{2,0},{3,1},{4,6},{5,7},{6,4},{7,5},{8,10},{9,11},{10,... | collective-permute-start | bytes 2555912 | tf_op jit(solution)/shard_map/ppermute | solution.py:108
  133.0 15.5 %collective-permute-start.24 = (bf16[2,512,256]{2,1,0:T(8,128)(2,1)}, bf16[2,512,256]{2,1,0:T(8,128)(2,1)S(1)}, u32[]{:S(2)}, u32[]{:S(2)}) collective-permute-start(bf16[2,512,256]{2,1,0:T(8,128)(2,1)} %get-tuple-element.82), channel_id=1, source_target_pairs={{0,8},{1,9},{2,10},{3,11},{4,12},{5,13},{6,14},{7,15},{8,0},{9,1},... | collective-permute-start | bytes 1572872 | tf_op jit(solution)/shard_map/ppermute | solution.py:108
  133.9 14.7 %collective-permute-start.25 = (bf16[2,512,256]{2,1,0:T(8,128)(2,1)}, bf16[2,512,256]{2,1,0:T(8,128)(2,1)S(1)}, u32[]{:S(2)}, u32[]{:S(2)}) collective-permute-start(bf16[2,512,256]{2,1,0:T(8,128)(2,1)} %get-tuple-element.83), channel_id=1, source_target_pairs={{0,2},{1,3},{2,0},{3,1},{4,6},{5,7},{6,4},{7,5},{8,16},{9,17},{10,... | collective-permute-start | bytes 1572872 | tf_op jit(solution)/shard_map/ppermute | solution.py:108
  161.2 11.2 %collective-permute-start.34 = (bf16[256,256]{1,0:T(8,128)(2,1)}, bf16[256,256]{1,0:T(8,128)(2,1)S(1)}, u32[]{:S(2)}, u32[]{:S(2)}) collective-permute-start(bf16[256,256]{1,0:T(8,128)(2,1)} %get-tuple-element.87), channel_id=1, source_target_pairs={{0,7},{1,6},{2,5},{3,4},{4,3},{5,2},{6,1},{7,0},{8,15},{9,14},{10,... | collective-permute-start | bytes 393224 | tf_op jit(solution)/shard_map/ppermute | solution.py:108
  164.0 11.4 %collective-permute-start.37 = (bf16[256,256]{1,0:T(8,128)(2,1)}, bf16[256,256]{1,0:T(8,128)(2,1)S(1)}, u32[]{:S(2)}, u32[]{:S(2)}) collective-permute-start(bf16[256,256]{1,0:T(8,128)(2,1)} %get-tuple-element.85), channel_id=1, source_target_pairs={{0,5},{1,4},{2,7},{3,6},{4,1},{5,0},{6,3},{7,2},{8,13},{9,12},{10,... | collective-permute-start | bytes 393224 | tf_op jit(solution)/shard_map/ppermute | solution.py:108
  (41 other events, 329.2 us)

commit v11 on v10

--- a/solution.py
+++ b/solution.py
@@ -124,6 +124,10 @@
     return permuted(x, lambda z, q, y: (3 - z, q, y) if z in (1, 2) else (z, q ^ 1, y))
 
 
+def half_pair(x):
+    return permuted(x, lambda z, q, y: (z ^ 2, q, y))
+
+
 def tied(*arrays):
     return lax.optimization_barrier(arrays)
 
@@ -170,62 +174,32 @@
     )(tokens, gain[None])
 
 
-def far_slabs(z):
-    return jnp.where(z < 2, 2, 1), jnp.where(z < 2, 3, 0)
-
-
 def token_copies(xs, at, out, sems):
     return [
         pltpu.make_async_copy(x.at[at], out.at[r], sems.at[r]) for r, x in enumerate(xs)
     ]
 
 
-def picked_copy(z, middle, end, out, sem, wait):
-    inner = (z == 1) | (z == 2)
-
-    @pl.when(inner)
-    def _():
-        copy = pltpu.make_async_copy(middle, out, sem)
-        copy.wait() if wait else copy.start()
-
-    @pl.when(jnp.logical_not(inner))
-    def _():
-        copy = pltpu.make_async_copy(end, out, sem)
-        copy.wait() if wait else copy.start()
-
-
 def blank_tail(w, rows):
     tail = w.shape[-2] - rows
     w[..., rows:, :] = jnp.zeros(w.shape[:-2] + (tail, w.shape[-1]), w.dtype)
 
 
 def early_kernel(
-    place, xa, xb, xc, xd, own, near, middle, end, acc, x_all, w_all, held, x_sem, w_sem, sems,
+    place, xa, xb, xc, xd, own, near, far, acc, x_all, w_all, held, x_sem, w_sem, sems,
 ):
     z = place[0]
-    xs = (xa, xb, xc, xd)
     kinds, rows = own.shape[:2]
-    taken = pl.ds(0, rows)
-    near_copy = pltpu.make_async_copy(near, w_all.at[1, :, taken, :], w_sem.at[1])
-    own_copy = pltpu.make_async_copy(own, w_all.at[0, :, taken, :], w_sem.at[0])
-    x_copies = [
-        token_copies(xs, at, x_all.at[i], x_sem.at[i])
-        for i, at in enumerate((z, z ^ 1, far_slabs(z)[0]))
-    ]
-    own_copy.start()
-    start(x_copies[0])
-    near_copy.start()
-    start(x_copies[1])
-    picked_copy(z, middle, end, w_all.at[2, :, taken, :], w_sem.at[2], False)
-    start(x_copies[2])
+    copies = []
+    for i, w in enumerate((own, near, far)):
+        dst = w_all.at[i, :, pl.ds(0, rows), :]
+        copies.append([pltpu.make_async_copy(w, dst, w_sem.at[i])])
+        copies[i] += token_copies((xa, xb, xc, xd), z ^ i, x_all.at[i], x_sem.at[i])
+        start(copies[i])
     blank_tail(w_all, rows)
     stores = []
     for step in range(3):
-        if step < 2:
-            (own_copy, near_copy)[step].wait()
-        else:
-            picked_copy(z, middle, end, w_all.at[2, :, taken, :], w_sem.at[2], True)
-        wait(x_copies[step])
+        wait(copies[step])
         for r in range(SLAB):
             x = x_all[step, r]
             for kind in range(kinds):
@@ -237,13 +211,13 @@
     wait(stores)
 
 
-def early(place, xs, own, near, middle, end):
+def early(place, xs, own, near, far):
     kinds, rows, width = own.shape
     slabs, count, wide = xs[0].shape
     return pl.pallas_call(
         early_kernel,
         out_shape=jax.ShapeDtypeStruct((SLAB, kinds, count, width), jnp.float32),
-        in_specs=[SMEM] + [HBM] * 8,
+        in_specs=[SMEM] + [HBM] * 7,
         out_specs=HBM,
         scratch_shapes=[
             pltpu.VMEM((3, SLAB, count, wide), jnp.bfloat16),
@@ -255,38 +229,39 @@
         ],
         compiler_params=pltpu.CompilerParams(vmem_limit_bytes=KERNEL_VMEM),
         cost_estimate=pl.CostEstimate(
-            flops=6 * kinds * SLAB * count * rows * width,
+            flops=12 * kinds * SLAB * count * rows * width,
             bytes_accessed=6 * kinds * rows * width + 6 * SLAB * count * rows,
             transcendentals=0,
         ),
         name="early",
-    )(place, *xs, own, near, middle, end)
+    )(place, *xs, own, near, far)
 
 
 def late_kernel(
-    place, xa, xb, xc, xd, acc, middle, end, q_gain, k_gain,
+    place, xa, xb, xc, xd, acc, last, q_gain, k_gain,
     query, keys, values, squares, even, odd,
-    x_all, far, held, q_all, k_all, v_all, x_sem, w_sem, acc_sem, sems,
+    x_all, w_all, held, q_all, k_all, v_all, x_sem, w_sem, acc_sem, sems,
 ):
     z, q = place[0], place[1]
-    taken = far.at[:, pl.ds(0, middle.shape[1]), :]
-    picked_copy(z, middle, end, taken, w_sem, False)
-    copies = token_copies((xa, xb, xc, xd), far_slabs(z)[1], x_all, x_sem)
+    rows = last.shape[1]
+    w_copy = pltpu.make_async_copy(last, w_all.at[:, pl.ds(0, rows), :], w_sem)
+    w_copy.start()
+    copies = token_copies((xa, xb, xc, xd), z ^ 3, x_all, x_sem)
     loads = [pltpu.make_async_copy(acc.at[r], held.at[r], acc_sem.at[r]) for r in range(SLAB)]
     for r in range(SLAB):
         copies[r].start()
         loads[r].start()
     count = held.shape[2]
     stores = []
-    blank_tail(far, middle.shape[1])
-    picked_copy(z, middle, end, taken, w_sem, True)
+    blank_tail(w_all, rows)
+    w_copy.wait()
     for r in range(SLAB):
         copies[r].wait()
         loads[r].wait()
         x = x_all[r]
         rows = pl.ds(pl.multiple_of((q ^ r) * count, count), count)
         for kind in range(3):
-            part = held[r, kind] + jnp.dot(x, far[kind], preferred_element_type=jnp.float32)
+            part = held[r, kind] + jnp.dot(x, w_all[kind], preferred_element_type=jnp.float32)
             if kind < 2:
                 summed = as_row(jnp.sum(part * part, axis=1, keepdims=True))
                 squares[kind:kind + 1, rows] = summed[:1]
@@ -306,8 +281,8 @@
     wait(stores)
 
 
-def late(place, xs, acc, middle, end, q_gain, k_gain):
-    kinds, rows, width = middle.shape
+def late(place, xs, acc, last, q_gain, k_gain):
+    kinds, rows, width = last.shape
     count, wide = xs[0].shape[1:]
     slab = SLAB * count
     f32, bf16 = jnp.float32, jnp.bfloat16
@@ -321,7 +296,7 @@
             jax.ShapeDtypeStruct((2, 2 * count, width), bf16),
             jax.ShapeDtypeStruct((2, 2 * count, width), bf16),
         ),
-        in_specs=[SMEM] + [HBM] * 7 + [VMEM] * 2,
+        in_specs=[SMEM] + [HBM] * 6 + [VMEM] * 2,
         out_specs=(HBM, HBM, HBM, VMEM, HBM, HBM),
         scratch_shapes=[
             pltpu.VMEM((SLAB, count, wide), bf16),
@@ -342,7 +317,7 @@
             transcendentals=0,
         ),
         name="late",
-    )(place, *xs, acc, middle, end, q_gain, k_gain)
+    )(place, *xs, acc, last, q_gain, k_gain)
 
 
 def attend_kernel(
@@ -429,10 +404,10 @@
 
 
 def out_kernel(
-    place, c20, c01, c31, c30, c11, c21, c10, c00, wa0, wa1, wb0, wb1, wc0, wc1, wd0, wd1,
+    place, c20, c01, c31, c30, c11, c21, c10, c00, wa, wb, wc, wd,
     residual, scale, out, c_all, w_all, total, placed, c_sem, w_sem,
 ):
-    z, q, y = place[0], place[1], place[2]
+    z, q = place[0], place[1]
     width = c00.shape[0]
     c_copies = []
     for i in range(2):
@@ -441,13 +416,13 @@
             dst = c_all.at[i, pl.ds(at, width), :]
             c_copies.append(pltpu.make_async_copy(pair[i], dst, c_sem.at[r, i]))
     start(c_copies)
-    rows = wa0.shape[1]
+    rows = wa.shape[2]
     w_copies = []
     for i in range(2):
-        for r, pair in enumerate(((wa0, wa1), (wb0, wb1), (wc0, wc1), (wd0, wd1))):
+        for r, w in enumerate((wa, wb, wc, wd)):
             for j in range(2):
                 dst = w_all.at[i, pl.ds((2 * r + j) * rows, rows), :]
-                w_copies.append(pltpu.make_async_copy(pair[j].at[i], dst, w_sem.at[r, j, i]))
+                w_copies.append(pltpu.make_async_copy(w.at[i, j], dst, w_sem.at[r, j, i]))
     start(w_copies)
     column = as_column(scale[...])[:out.shape[0]]
     column = jnp.tile(column, (1, out.shape[1] // 128))
@@ -458,8 +433,7 @@
     kept = out.shape[0] // (2 * SLAB)
     for r in range(SLAB):
         for j in range(2):
-            slab = jnp.where(z // 2 == y, (z % 2) ^ j, jnp.where(z < 2, j, 1 - j))
-            at = pl.multiple_of((slab * SLAB + (q ^ r)) * kept, 8)
+            at = pl.multiple_of((((z % 2) ^ j) * SLAB + (q ^ r)) * kept, 8)
             begin = (2 * r + j) * rows
             placed[pl.ds(at, kept), :] = total[begin:begin + kept, :]
     out[...] = (residual[...].astype(jnp.float32) + column * placed[...]).astype(jnp.bfloat16)
@@ -467,13 +441,13 @@
 
 def output(place, blocks, pieces, residual, scale):
     count = blocks[0].shape[1]
-    rows, depth = pieces[0].shape[1:]
+    rows, depth = pieces[0].shape[2:]
     share = residual.shape[0]
     scale = jnp.pad(scale, (0, -share % 128))[None]
     return pl.pallas_call(
         out_kernel,
         out_shape=jax.ShapeDtypeStruct((share, count), jnp.bfloat16),
-        in_specs=[SMEM] + [HBM] * 16 + [VMEM] * 2,
+        in_specs=[SMEM] + [HBM] * 12 + [VMEM] * 2,
         out_specs=VMEM,
         scratch_shapes=[
             pltpu.VMEM((2, depth, count), jnp.bfloat16),
@@ -512,7 +486,7 @@
     width = qkv_weight.shape[2] // SLAB
     full_width = qkv_weight.shape[2] * lax.axis_size("tp")
     slab, half = SLAB * count, 2 * count
-    inner, home = (z == 1) | (z == 2), z // 2 == tp
+    home = z // 2 == tp
 
     by_kind = jnp.transpose(qkv_weight, (1, 0, 2))
     cut = [lax.dynamic_slice_in_dim(by_kind, (q ^ r) * width, width, 2) for r in range(SLAB)]
@@ -520,55 +494,41 @@
     x0 = norm(tokens, norm_gain, slabs)
     out_own = jnp.pad(jnp.transpose(out_weight), ((0, -out_weight.shape[1] % 16), (0, 0)))
     own = rows_of_slab(q, got)
-    out_near, out_mid1 = even_pair(out_own), odd_pair(out_own)
-    out_end1, out_mid2 = even_pair(out_mid1), odd_pair(out_near)
+    out_near, out_far = even_pair(out_own), half_pair(out_own)
     gains = [lax.dynamic_slice_in_dim(g, q * width, width, 0)[None] for g in (q_gain, k_gain)]
 
-    def over_tp(close, far):
-        keep, give = jnp.where(home, close, far), jnp.where(home, far, close)
-        return keep, across(give)
-
-    own, x0, out_end1, out_mid2, *gains = tied(own, x0, out_end1, out_mid2, *gains)
-    near, middle1 = even_pair(own), odd_pair(own)
-    x2 = in_slab(x0, 2)
-    out_end2 = even_pair(out_mid2)
-    keep0, got0 = over_tp(out_own, jnp.where(inner, out_mid1, out_end1))
-    near, middle1, x0, x2, keep0, got0, out_end2 = tied(
-        near, middle1, x0, x2, keep0, got0, out_end2
-    )
-    end1, middle2 = even_pair(middle1), odd_pair(near)
-    x1, x3 = in_slab(x0, 1), in_slab(x2, 1)
-    x1, out_end2, keep0, got0 = tied(x1, out_end2, keep0, got0)
-    wa0 = jnp.stack([keep0, got0])
-    wc0 = in_slab(wa0, 2)
-    keep1, got1 = over_tp(out_near, jnp.where(inner, out_mid2, out_end2))
-    end1, middle2, x1, x3, wa0, wc0, keep1, got1 = tied(
-        end1, middle2, x1, x3, wa0, wc0, keep1, got1
-    )
-    end2 = even_pair(middle2)
-    wa1 = jnp.stack([keep1, got1])
-    wc1 = in_slab(wa1, 2)
-    wb0, wd0 = in_slab(wa0, 1), in_slab(wc0, 1)
+    own, x0, out_near, out_far, *gains = tied(own, x0, out_near, out_far, *gains)
+    out_last = even_pair(out_far)
+    near, far = even_pair(own), half_pair(own)
+    x1, x2 = in_slab(x0, 1), in_slab(x0, 2)
+    out_last, x1 = tied(out_last, x1)
+    close, away = jnp.stack([out_own, out_near]), jnp.stack([out_far, out_last])
+    keep, give = jnp.where(home, close, away), jnp.where(home, away, close)
+    wa = jnp.stack([keep, across(give)])
+    near, far, x2, wa = tied(near, far, x2, wa)
+    last = even_pair(far)
+    x3 = in_slab(x2, 1)
+    wc, wb = in_slab(wa, 2), in_slab(wa, 1)
     xs = (x0, x1, x2, x3)
-    acc = early(place, xs, own, near, middle1, end1)
-    acc, wc1, wa1 = tied(acc, wc1, wa1)
-    wb1, wd1 = in_slab(wa1, 1), in_slab(wc1, 1)
-    end2, acc, wb0, wd0, wb1, wd1 = tied(end2, acc, wb0, wd0, wb1, wd1)
-    pieces = (wa0, wa1, wb0, wb1, wc0, wc1, wd0, wd1)
-
-    query, keys, values, squares, even, odd = late(place, xs, acc, middle2, end2, *gains)
+    acc = early(place, xs, own, near, far)
+    last, acc, wb = tied(last, acc, wb)
+
+    query, keys, values, squares, even, odd = late(place, xs, acc, last, *gains)
     even, odd = even_pair(even), odd_pair(odd)
-    sums = squares
-    for r in range(1, SLAB):
-        sums = sums + in_slab(squares, r)
+    sums = squares + in_slab(squares, 1)
+    sums = sums + in_slab(sums, 2)
     sums = sums + across(sums)
     sums = (sums, even_pair(sums), odd_pair(sums))
+    query, wc = tied(query, wc)
+    wd = in_slab(wc, 1)
 
     outside = jnp.full((half,), -1, jnp.int32)
     seg = jnp.concatenate([outside, segment_ids, outside], axis=0)
     seg = lax.dynamic_slice_in_dim(seg, z * slab, slab + 2 * half, 0)
     seg = seg.astype(jnp.float32)[None]
     blocks = attend(full_width, place, query, keys, values, even, odd, sums, seg)
+    *blocks, wd = tied(*blocks, wd)
+    pieces = (wa, wb, wc, wd)
     spread = []
     for r, i in ((2, 0), (0, 1), (3, 1), (3, 0), (1, 1), (2, 1), (1, 0), (0, 0)):
         to = functools.partial(lambda r, i, z, q, y: (z, q ^ r, y ^ i), r, i)

time: 187 us -> 186 us (level)
  waiting for transfers between devices: 81.2 us -> 96 us
  starting transfers between devices: 45.9 us -> 32.6 us
  local copies, waits for them, and re-layouts: 13.6 us -> 9.88 us
    ppermute x39 -> x30, waiting for transfers between devices: 81.2 us -> 96 us  [permuted(): return lax.ppermute(x, ('seq', 'tp'), pairs)]
    ppermute x39 -> x30, starting transfers between devices: 45.9 us -> 32.6 us  [permuted(): return lax.ppermute(x, ('seq', 'tp'), pairs)]
    unnamed x53 -> x31, local copies, waits for them, and re-layouts: 7.14 us -> 3.47 us
  transfers between devices with their start and end apart: 39 -> 30, of which waited for: 17 -> 18; matrix products, arithmetic and copies ran while one was open for 7% -> 7% of each run, Pallas kernels for 7% -> 16%
where the time goes in v11:
time: 186 us; the launch traced here: 184 us
  waiting for transfers between devices  96 us (52%)
  Pallas kernels  38.4 us (21%)
  starting transfers between devices  32.6 us (18%)
  local copies, waits for them, and re-layouts  9.88 us (5%)
  other arithmetic  7.1 us (4%)
    ppermute x30, waiting for transfers between devices, permuted(): return lax.ppermute(x, ('seq', 'tp'), pairs)  96 us
    ppermute x30, starting transfers between devices, permuted(): return lax.ppermute(x, ('seq', 'tp'), pairs)  32.6 us
    pallas_call x1, Pallas kernels, early(): pl.pallas_call(early_kernel, out_shape=jax.ShapeDtypeStruct((SLAB, kinds,...  9.42 us
    pallas_call x1, Pallas kernels, attend(): pl.pallas_call(functools.partial(attend_kernel, full_width), out_shape=(j...  9.08 us
    pallas_call x1, Pallas kernels, output(): pl.pallas_call(out_kernel, out_shape=jax.ShapeDtypeStruct((share, count),...  8.97 us
    pallas_call x1, Pallas kernels, late(): pl.pallas_call(late_kernel, out_shape=(jax.ShapeDtypeStruct((slab, width)...  7.42 us
  transfers between devices with their start and end apart: 30, of which 18 were waited for; matrix products, arithmetic and copies ran while one was open for 7% of the time, Pallas kernels for 16%

profile of v11, /device:TPU:9, one launch (start us, length us, event | category | flops | bytes accessed | tf_op | source)
XLA Modules:
  0.0 184.4 jit_solution(5315461030548682026)
XLA Ops:
  1.3 1.8 collective-permute-start
  4.7 2.3 %collective-permute-start.4 = (bf16[208,1024]{1,0:T(8,128)(2,1)}, bf16[208,1024]{1,0:T(8,128)(2,1)S(1)}, u32[]{:S(2)}, u32[]{:S(2)}) collective-permute-start(bf16[208,1024]{1,0:T(8,128)(2,1)} %get-tuple-element.78), channel_id=1, source_target_pairs={{0,16},{1,17},{2,18},{3,19},{4,20},{5,21},{6,22},{7,23},{8,24},{9,... | collective-permute-start | bytes 1277960 | tf_op jit(solution)/shard_map/ppermute | solution.py:108
  10.3 3.6 %norm.1.xa = bf16[4,256,896]{2,1,0:T(8,128)(2,1)} custom-call(bf16[256,3200]{1,0:T(8,128)(2,1)} %tokens.1, f32[1,3200]{1,0:T(1,128)} %broadcast_in_dim.18.gain), custom_call_target="tpu_custom_call" | custom-call | tf_op jit(solution)/shard_map/norm/pallas_call | solution.py:167
  13.8 3.9 %collective-permute-done.1 = bf16[3,200,256]{2,1,0:T(8,128)(2,1)S(1)} collective-permute-done((bf16[3,200,256]{2,1,0:T(8,128)(2,1)S(1)}, bf16[3,200,256]{2,1,0:T(8,128)(2,1)S(1)}, u32[]{:S(2)}, u32[]{:S(2)}) %collective-permute-start.1) | collective-permute-done | bytes 307232 | tf_op jit(solution)/shard_map/ppermute | solution.py:108
  20.3 2.9 %collective-permute-done.3 = bf16[208,1024]{1,0:T(8,128)(2,1)S(1)} collective-permute-done((bf16[208,1024]{1,0:T(8,128)(2,1)}, bf16[208,1024]{1,0:T(8,128)(2,1)S(1)}, u32[]{:S(2)}, u32[]{:S(2)}) %collective-permute-start.3) | collective-permute-done | bytes 426016 | tf_op jit(solution)/shard_map/ppermute | solution.py:108
  23.2 2.8 %collective-permute-done.4 = bf16[208,1024]{1,0:T(8,128)(2,1)S(1)} collective-permute-done((bf16[208,1024]{1,0:T(8,128)(2,1)}, bf16[208,1024]{1,0:T(8,128)(2,1)S(1)}, u32[]{:S(2)}, u32[]{:S(2)}) %collective-permute-start.4) | collective-permute-done | bytes 426016 | tf_op jit(solution)/shard_map/ppermute | solution.py:108
  29.8 2.3 %collective-permute-start.8 = (bf16[3,800,256]{2,1,0:T(8,128)(2,1)}, bf16[3,800,256]{2,1,0:T(8,128)(2,1)}, u32[]{:S(2)}, u32[]{:S(2)}) collective-permute-start(bf16[3,800,256]{2,1,0:T(8,128)(2,1)} %pad_maximum_fusion.1.own), channel_id=1, source_target_pairs={{0,16},{1,17},{2,18},{3,19},{4,20},{5,21},{6,22},{7,23},{8,24},{9,... | collective-permute-start | bytes 3686408 | tf_op jit(solution)/shard_map/ppermute | solution.py:108
  32.1 32.8 %collective-permute-done.5 = bf16[208,1024]{1,0:T(8,128)(2,1)} collective-permute-done((bf16[208,1024]{1,0:T(8,128)(2,1)S(1)}, bf16[208,1024]{1,0:T(8,128)(2,1)}, u32[]{:S(2)}, u32[]{:S(2)}) %collective-permute-start.5) | collective-permute-done | bytes 426016 | tf_op jit(solution)/shard_map/ppermute | solution.py:108
  68.5 16.3 %collective-permute-done.10 = bf16[2,208,1024]{2,1,0:T(8,128)(2,1)S(1)} collective-permute-done((bf16[2,208,1024]{2,1,0:T(8,128)(2,1)S(1)}, bf16[2,208,1024]{2,1,0:T(8,128)(2,1)S(1)}, u32[]{:S(2)}, u32[]{:S(2)}) %collective-permute-start.10) | collective-permute-done | bytes 852000 | tf_op jit(solution)/shard_map/ppermute | solution.py:108
  85.0 6.3 %collective-permute-done.7.near = bf16[3,800,256]{2,1,0:T(8,128)(2,1)} collective-permute-done((bf16[3,800,256]{2,1,0:T(8,128)(2,1)}, bf16[3,800,256]{2,1,0:T(8,128)(2,1)}, u32[]{:S(2)}, u32[]{:S(2)}) %collective-permute-start.7) | collective-permute-done | bytes 1228832 | tf_op jit(solution)/shard_map/ppermute | solution.py:108
  91.3 2.1 %collective-permute-done.8.far = bf16[3,800,256]{2,1,0:T(8,128)(2,1)} collective-permute-done((bf16[3,800,256]{2,1,0:T(8,128)(2,1)}, bf16[3,800,256]{2,1,0:T(8,128)(2,1)}, u32[]{:S(2)}, u32[]{:S(2)}) %collective-permute-start.8) | collective-permute-done | bytes 1228832 | tf_op jit(solution)/shard_map/ppermute | solution.py:108
  95.7 4.5 %collective-permute-done.11.xd = bf16[4,256,896]{2,1,0:T(8,128)(2,1)S(1)} collective-permute-done((bf16[4,256,896]{2,1,0:T(8,128)(2,1)}, bf16[4,256,896]{2,1,0:T(8,128)(2,1)S(1)}, u32[]{:S(2)}, u32[]{:S(2)}) %collective-permute-start.11) | collective-permute-done | bytes 1835040 | tf_op jit(solution)/shard_map/ppermute | solution.py:108
  101.4 9.4 %early.1.acc = f32[4,3,256,256]{3,2,1,0:T(8,128)} custom-call(s32[3]{0:T(128)} %pad_add_fusion.place, bf16[4,256,896]{2,1,0:T(8,128)(2,1)} %norm.1.xa, bf16[4,256,896]{2,1,0:T(8,128)(2,1)} %collective-permute-done.6.xb, bf16[4,256,896]{2,1,0:T(8,128)(2,1)} %collective-permute-done.9.xc, bf16[4,256,896]{2,1,0:T(8,128)(2,1)} %copy-done.3, ...), custom_call_target="tpu_custom_call" | custom-call | flops 7549747200 | bytes 8601600 | tf_op jit(solution)/shard_map/early/pallas_call | solution.py:217
  110.9 11.7 %collective-permute-done.12.last = bf16[3,800,256]{2,1,0:T(8,128)(2,1)} collective-permute-done((bf16[3,800,256]{2,1,0:T(8,128)(2,1)}, bf16[3,800,256]{2,1,0:T(8,128)(2,1)}, u32[]{:S(2)}, u32[]{:S(2)}) %collective-permute-start.12) | collective-permute-done | bytes 1228832 | tf_op jit(solution)/shard_map/ppermute | solution.py:108
  122.6 7.4 %late.1 = (f32[1024,256]{1,0:T(8,128)}, bf16[1024,256]{1,0:T(8,128)(2,1)}, bf16[1024,256]{1,0:T(8,128)(2,1)}, f32[2,1024]{1,0:T(2,128)}, bf16[2,512,256]{2,1,0:T(8,128)(2,1)}, /*index=5*/bf16[2,512,256]{2,1,0:T(8,128)(2,1)}) custom-call(s32[3]{0:T(128)} %pad_add_fusion.place, bf16[4,256,896]{2,1,0:T(8,128)(2,1)} %norm.1.xa, ...), custom_call_target="tpu_custom_call" | custom-call | flops 1258291200 | bytes 2867200 | tf_op jit(solution)/shard_map/late/pallas_call | solution.py:289
  130.0 2.5 %collective-permute-done.14.wc = bf16[2,2,208,1024]{3,2,1,0:T(8,128)(2,1)} collective-permute-done((bf16[2,2,208,1024]{3,2,1,0:T(8,128)(2,1)S(1)}, bf16[2,2,208,1024]{3,2,1,0:T(8,128)(2,1)}, u32[]{:S(2)}, u32[]{:S(2)}) %collective-permute-start.14) | collective-permute-done | bytes 1703968 | tf_op jit(solution)/shard_map/ppermute | solution.py:108
  138.4 2.4 %collective-permute-done.18 = f32[2,1024]{1,0:T(2,128)S(1)} collective-permute-done((f32[2,1024]{1,0:T(2,128)S(1)}, f32[2,1024]{1,0:T(2,128)S(1)}, u32[]{:S(2)}, u32[]{:S(2)}) %collective-permute-start.18) | collective-permute-done | bytes 8224 | tf_op jit(solution)/shard_map/ppermute | solution.py:108
  142.1 1.6 collective-permute-done.19
  149.1 9.1 %attend.1 = (bf16[256,256]{1,0:T(8,128)(2,1)}, bf16[256,256]{1,0:T(8,128)(2,1)}, bf16[256,256]{1,0:T(8,128)(2,1)}, bf16[256,256]{1,0:T(8,128)(2,1)}) custom-call(s32[3]{0:T(128)} %pad_add_fusion.place, f32[1024,256]{1,0:T(8,128)} %get-tuple-element.52.query, bf16[1024,256]{1,0:T(8,128)(2,1)} %get-tuple-element.53.keys, ...), custom_call_target="tpu_custom_call" | custom-call | flops 1342177280 | bytes 3145728 | tf_op jit(solution)/shard_map/attend/pallas_call | solution.py:383
  159.8 4.4 %collective-permute-start.25 = (bf16[256,256]{1,0:T(8,128)(2,1)}, bf16[256,256]{1,0:T(8,128)(2,1)}, u32[]{:S(2)}, u32[]{:S(2)}) collective-permute-start(bf16[256,256]{1,0:T(8,128)(2,1)} %get-tuple-element.65), channel_id=1, source_target_pairs={{0,7},{1,6},{2,5},{3,4},{4,3},{5,2},{6,1},{7,0},{8,15},{9,14},{10,... | collective-permute-start | bytes 393224 | tf_op jit(solution)/shard_map/ppermute | solution.py:108
  165.6 1.9 %collective-permute-start.27 = (bf16[256,256]{1,0:T(8,128)(2,1)}, bf16[256,256]{1,0:T(8,128)(2,1)}, u32[]{:S(2)}, u32[]{:S(2)}) collective-permute-start(bf16[256,256]{1,0:T(8,128)(2,1)} %get-tuple-element.66), channel_id=1, source_target_pairs={{0,3},{1,2},{2,1},{3,0},{4,7},{5,6},{6,5},{7,4},{8,11},{9,10},{10,... | collective-permute-start | bytes 393224 | tf_op jit(solution)/shard_map/ppermute | solution.py:108
  167.5 1.5 collective-permute-start.29
  172.2 3.0 %collective-permute-done.28.c21 = bf16[256,256]{1,0:T(8,128)(2,1)} collective-permute-done((bf16[256,256]{1,0:T(8,128)(2,1)}, bf16[256,256]{1,0:T(8,128)(2,1)}, u32[]{:S(2)}, u32[]{:S(2)}) %collective-permute-start.28) | collective-permute-done | bytes 131104 | tf_op jit(solution)/shard_map/ppermute | solution.py:108
  175.3 9.0 %output.1 = bf16[1600,256]{1,0:T(8,128)(2,1)} custom-call(s32[3]{0:T(128)} %pad_add_fusion.place, bf16[256,256]{1,0:T(8,128)(2,1)} %copy-done.6, bf16[256,256]{1,0:T(8,128)(2,1)} %collective-permute-done.24.c01, bf16[256,256]{1,0:T(8,128)(2,1)} %collective-permute-done.25.c31, bf16[256,256]{1,0:T(8,128)(2,1)} %collective-permute-done.26.c30, ...), custom_call_target="tpu_custom_call" | custom-call | flops 1677721600 | bytes 6553600 | tf_op jit(solution)/shard_map/output/pallas_call | solution.py:447
  (91 shorter events, 38.5 us)
Async XLA Ops:
  1.3 12.5 %collective-permute-start = (bf16[3,200,256]{2,1,0:T(8,128)(2,1)S(1)}, bf16[3,200,256]{2,1,0:T(8,128)(2,1)S(1)}, u32[]{:S(2)}, u32[]{:S(2)}) collective-permute-start(bf16[3,200,256]{2,1,0:T(8,128)(2,1)S(1)} %get-tuple-element.73), channel_id=1, source_target_pairs={{0,6},{1,7},{2,4},{3,5},{4,2},{5,3},{6,0},{7,1},{8,14},{9,15},{10,... | collective-permute-start | bytes 921608 | tf_op jit(solution)/shard_map/ppermute | solution.py:108
  3.1 14.6 %collective-permute-start.1 = (bf16[3,200,256]{2,1,0:T(8,128)(2,1)S(1)}, bf16[3,200,256]{2,1,0:T(8,128)(2,1)S(1)}, u32[]{:S(2)}, u32[]{:S(2)}) collective-permute-start(bf16[3,200,256]{2,1,0:T(8,128)(2,1)S(1)} %get-tuple-element.74), channel_id=1, source_target_pairs={{0,4},{1,5},{2,6},{3,7},{4,0},{5,1},{6,2},{7,3},{8,12},{9,13},{10,... | collective-permute-start | bytes 921608 | tf_op jit(solution)/shard_map/ppermute | solution.py:108
  3.4 14.4 %collective-permute-start.2 = (bf16[3,200,256]{2,1,0:T(8,128)(2,1)S(1)}, bf16[3,200,256]{2,1,0:T(8,128)(2,1)}, u32[]{:S(2)}, u32[]{:S(2)}) collective-permute-start(bf16[3,200,256]{2,1,0:T(8,128)(2,1)S(1)} %get-tuple-element.75), channel_id=1, source_target_pairs={{0,2},{1,3},{2,0},{3,1},{4,6},{5,7},{6,4},{7,5},{8,10},{9,11},{10,... | collective-permute-start | bytes 921608 | tf_op jit(solution)/shard_map/ppermute | solution.py:108
  4.5 18.7 %collective-permute-start.3 = (bf16[208,1024]{1,0:T(8,128)(2,1)}, bf16[208,1024]{1,0:T(8,128)(2,1)S(1)}, u32[]{:S(2)}, u32[]{:S(2)}) collective-permute-start(bf16[208,1024]{1,0:T(8,128)(2,1)} %get-tuple-element.78), channel_id=1, source_target_pairs={{0,8},{1,9},{2,10},{3,11},{4,12},{5,13},{6,14},{7,15},{8,0},{9,1},... | collective-permute-start | bytes 1277960 | tf_op jit(solution)/shard_map/ppermute | solution.py:108
  4.7 21.4 %collective-permute-start.4 = (bf16[208,1024]{1,0:T(8,128)(2,1)}, bf16[208,1024]{1,0:T(8,128)(2,1)S(1)}, u32[]{:S(2)}, u32[]{:S(2)}) collective-permute-start(bf16[208,1024]{1,0:T(8,128)(2,1)} %get-tuple-element.78), channel_id=1, source_target_pairs={{0,16},{1,17},{2,18},{3,19},{4,20},{5,21},{6,22},{7,23},{8,24},{9,... | collective-permute-start | bytes 1277960 | tf_op jit(solution)/shard_map/ppermute | solution.py:108
  26.0 38.8 %collective-permute-start.6 = (bf16[4,256,896]{2,1,0:T(8,128)(2,1)S(1)}, bf16[4,256,896]{2,1,0:T(8,128)(2,1)}, u32[]{:S(2)}, u32[]{:S(2)}) collective-permute-start(bf16[4,256,896]{2,1,0:T(8,128)(2,1)S(1)} %copy-done), channel_id=1, source_target_pairs={{0,2},{1,3},{2,0},{3,1},{4,6},{5,7},{6,4},{7,5},{8,10},{9,11},{10,... | collective-permute-start | bytes 5505032 | tf_op jit(solution)/shard_map/ppermute | solution.py:108
  27.2 66.2 %collective-permute-start.9 = (bf16[4,256,896]{2,1,0:T(8,128)(2,1)S(1)}, bf16[4,256,896]{2,1,0:T(8,128)(2,1)}, u32[]{:S(2)}, u32[]{:S(2)}) collective-permute-start(bf16[4,256,896]{2,1,0:T(8,128)(2,1)S(1)} %copy-done), channel_id=1, source_target_pairs={{0,4},{1,5},{2,6},{3,7},{4,0},{5,1},{6,2},{7,3},{8,12},{9,13},{10,... | collective-permute-start | bytes 5505032 | tf_op jit(solution)/shard_map/ppermute | solution.py:108
  28.3 36.6 %collective-permute-start.5 = (bf16[208,1024]{1,0:T(8,128)(2,1)S(1)}, bf16[208,1024]{1,0:T(8,128)(2,1)}, u32[]{:S(2)}, u32[]{:S(2)}) collective-permute-start(bf16[208,1024]{1,0:T(8,128)(2,1)S(1)} %collective-permute-done.4), channel_id=1, source_target_pairs={{0,8},{1,9},{2,10},{3,11},{4,12},{5,13},{6,14},{7,15},{8,0},{9,1},... | collective-permute-start | bytes 1277960 | tf_op jit(solution)/shard_map/ppermute | solution.py:108
  29.6 61.7 %collective-permute-start.7 = (bf16[3,800,256]{2,1,0:T(8,128)(2,1)}, bf16[3,800,256]{2,1,0:T(8,128)(2,1)}, u32[]{:S(2)}, u32[]{:S(2)}) collective-permute-start(bf16[3,800,256]{2,1,0:T(8,128)(2,1)} %pad_maximum_fusion.1.own), channel_id=1, source_target_pairs={{0,8},{1,9},{2,10},{3,11},{4,12},{5,13},{6,14},{7,15},{8,0},{9,1},... | collective-permute-start | bytes 3686408 | tf_op jit(solution)/shard_map/ppermute | solution.py:108
  29.8 63.6 %collective-permute-start.8 = (bf16[3,800,256]{2,1,0:T(8,128)(2,1)}, bf16[3,800,256]{2,1,0:T(8,128)(2,1)}, u32[]{:S(2)}, u32[]{:S(2)}) collective-permute-start(bf16[3,800,256]{2,1,0:T(8,128)(2,1)} %pad_maximum_fusion.1.own), channel_id=1, source_target_pairs={{0,16},{1,17},{2,18},{3,19},{4,20},{5,21},{6,22},{7,23},{8,24},{9,... | collective-permute-start | bytes 3686408 | tf_op jit(solution)/shard_map/ppermute | solution.py:108
  66.0 18.8 %collective-permute-start.10 = (bf16[2,208,1024]{2,1,0:T(8,128)(2,1)S(1)}, bf16[2,208,1024]{2,1,0:T(8,128)(2,1)S(1)}, u32[]{:S(2)}, u32[]{:S(2)}) collective-permute-start(bf16[2,208,1024]{2,1,0:T(8,128)(2,1)S(1)} %maximum_select_fusion.1), channel_id=1, source_target_pairs={{0,1},{1,0},{2,3},{3,2},{4,5},{5,4},{6,7},{7,6},{8,9},{9,8},{10,11... | collective-permute-start | bytes 2555912 | tf_op jit(solution)/shard_map/ppermute | solution.py:108
  93.4 6.8 %collective-permute-start.11 = (bf16[4,256,896]{2,1,0:T(8,128)(2,1)}, bf16[4,256,896]{2,1,0:T(8,128)(2,1)S(1)}, u32[]{:S(2)}, u32[]{:S(2)}) collective-permute-start(bf16[4,256,896]{2,1,0:T(8,128)(2,1)} %collective-permute-done.9.xc), channel_id=1, source_target_pairs={{0,2},{1,3},{2,0},{3,1},{4,6},{5,7},{6,4},{7,5},{8,10},{9,11},{10,... | collective-permute-start | bytes 5505032 | tf_op jit(solution)/shard_map/ppermute | solution.py:108
  94.2 28.4 %collective-permute-start.13 = (bf16[2,2,208,1024]{3,2,1,0:T(8,128)(2,1)S(1)}, bf16[2,2,208,1024]{3,2,1,0:T(8,128)(2,1)}, u32[]{:S(2)}, u32[]{:S(2)}) collective-permute-start(bf16[2,2,208,1024]{3,2,1,0:T(8,128)(2,1)S(1)} %pad_maximum_fusion.wa), channel_id=1, source_target_pairs={{0,2},{1,3},{2,0},{3,1},{4,6},{5,7},{6,4},{7,5},{8,10},{9,11},{10,... | collective-permute-start | bytes 5111816 | tf_op jit(solution)/shard_map/ppermute | solution.py:108
  94.2 38.4 %collective-permute-start.14 = (bf16[2,2,208,1024]{3,2,1,0:T(8,128)(2,1)S(1)}, bf16[2,2,208,1024]{3,2,1,0:T(8,128)(2,1)}, u32[]{:S(2)}, u32[]{:S(2)}) collective-permute-start(bf16[2,2,208,1024]{3,2,1,0:T(8,128)(2,1)S(1)} %pad_maximum_fusion.wa), channel_id=1, source_target_pairs={{0,4},{1,5},{2,6},{3,7},{4,0},{5,1},{6,2},{7,3},{8,12},{9,13},{10,... | collective-permute-start | bytes 5111816 | tf_op jit(solution)/shard_map/ppermute | solution.py:108
  94.5 28.1 %collective-permute-start.12 = (bf16[3,800,256]{2,1,0:T(8,128)(2,1)}, bf16[3,800,256]{2,1,0:T(8,128)(2,1)}, u32[]{:S(2)}, u32[]{:S(2)}) collective-permute-start(bf16[3,800,256]{2,1,0:T(8,128)(2,1)} %collective-permute-done.8.far), channel_id=1, source_target_pairs={{0,8},{1,9},{2,10},{3,11},{4,12},{5,13},{6,14},{7,15},{8,0},{9,1},... | collective-permute-start | bytes 3686408 | tf_op jit(solution)/shard_map/ppermute | solution.py:108
  132.5 25.6 %collective-permute-start.22 = (bf16[2,2,208,1024]{3,2,1,0:T(8,128)(2,1)}, bf16[2,2,208,1024]{3,2,1,0:T(8,128)(2,1)S(1)}, u32[]{:S(2)}, u32[]{:S(2)}) collective-permute-start(bf16[2,2,208,1024]{3,2,1,0:T(8,128)(2,1)} %collective-permute-done.14.wc), channel_id=1, source_target_pairs={{0,2},{1,3},{2,0},{3,1},{4,6},{5,7},{6,4},{7,5},{8,10},{9,11},{10,... | collective-permute-start | bytes 5111816 | tf_op jit(solution)/shard_map/ppermute | solution.py:108
  133.9 14.2 %collective-permute-start.15 = (bf16[2,512,256]{2,1,0:T(8,128)(2,1)}, bf16[2,512,256]{2,1,0:T(8,128)(2,1)S(1)}, u32[]{:S(2)}, u32[]{:S(2)}) collective-permute-start(bf16[2,512,256]{2,1,0:T(8,128)(2,1)} %get-tuple-element.55), channel_id=1, source_target_pairs={{0,8},{1,9},{2,10},{3,11},{4,12},{5,13},{6,14},{7,15},{8,0},{9,1},... | collective-permute-start | bytes 1572872 | tf_op jit(solution)/shard_map/ppermute | solution.py:108
  134.4 13.6 %collective-permute-start.16 = (bf16[2,512,256]{2,1,0:T(8,128)(2,1)}, bf16[2,512,256]{2,1,0:T(8,128)(2,1)S(1)}, u32[]{:S(2)}, u32[]{:S(2)}) collective-permute-start(bf16[2,512,256]{2,1,0:T(8,128)(2,1)} %get-tuple-element.56), channel_id=1, source_target_pairs={{0,2},{1,3},{2,0},{3,1},{4,6},{5,7},{6,4},{7,5},{8,16},{9,17},{10,... | collective-permute-start | bytes 1572872 | tf_op jit(solution)/shard_map/ppermute | solution.py:108
  158.2 7.5 %collective-permute-start.23 = (bf16[256,256]{1,0:T(8,128)(2,1)}, bf16[256,256]{1,0:T(8,128)(2,1)S(1)}, u32[]{:S(2)}, u32[]{:S(2)}) collective-permute-start(bf16[256,256]{1,0:T(8,128)(2,1)} %get-tuple-element.63), channel_id=1, source_target_pairs={{0,4},{1,5},{2,6},{3,7},{4,0},{5,1},{6,2},{7,3},{8,12},{9,13},{10,... | collective-permute-start | bytes 393224 | tf_op jit(solution)/shard_map/ppermute | solution.py:108
  158.6 8.9 %collective-permute-start.24 = (bf16[256,256]{1,0:T(8,128)(2,1)}, bf16[256,256]{1,0:T(8,128)(2,1)}, u32[]{:S(2)}, u32[]{:S(2)}) collective-permute-start(bf16[256,256]{1,0:T(8,128)(2,1)} %get-tuple-element.64.c00), channel_id=1, source_target_pairs={{0,1},{1,0},{2,3},{3,2},{4,5},{5,4},{6,7},{7,6},{8,9},{9,8},{10,11... | collective-permute-start | bytes 393224 | tf_op jit(solution)/shard_map/ppermute | solution.py:108
  159.8 11.4 %collective-permute-start.25 = (bf16[256,256]{1,0:T(8,128)(2,1)}, bf16[256,256]{1,0:T(8,128)(2,1)}, u32[]{:S(2)}, u32[]{:S(2)}) collective-permute-start(bf16[256,256]{1,0:T(8,128)(2,1)} %get-tuple-element.65), channel_id=1, source_target_pairs={{0,7},{1,6},{2,5},{3,4},{4,3},{5,2},{6,1},{7,0},{8,15},{9,14},{10,... | collective-permute-start | bytes 393224 | tf_op jit(solution)/shard_map/ppermute | solution.py:108
  164.3 7.6 %collective-permute-start.26 = (bf16[256,256]{1,0:T(8,128)(2,1)}, bf16[256,256]{1,0:T(8,128)(2,1)}, u32[]{:S(2)}, u32[]{:S(2)}) collective-permute-start(bf16[256,256]{1,0:T(8,128)(2,1)} %get-tuple-element.65), channel_id=1, source_target_pairs={{0,6},{1,7},{2,4},{3,5},{4,2},{5,3},{6,0},{7,1},{8,14},{9,15},{10,... | collective-permute-start | bytes 393224 | tf_op jit(solution)/shard_map/ppermute | solution.py:108
  164.4 10.9 %collective-permute-start.28 = (bf16[256,256]{1,0:T(8,128)(2,1)}, bf16[256,256]{1,0:T(8,128)(2,1)}, u32[]{:S(2)}, u32[]{:S(2)}) collective-permute-start(bf16[256,256]{1,0:T(8,128)(2,1)} %get-tuple-element.63), channel_id=1, source_target_pairs={{0,5},{1,4},{2,7},{3,6},{4,1},{5,0},{6,3},{7,2},{8,13},{9,12},{10,... | collective-permute-start | bytes 393224 | tf_op jit(solution)/shard_map/ppermute | solution.py:108
  167.5 7.8 %collective-permute-start.29 = (bf16[256,256]{1,0:T(8,128)(2,1)}, bf16[256,256]{1,0:T(8,128)(2,1)}, u32[]{:S(2)}, u32[]{:S(2)}) collective-permute-start(bf16[256,256]{1,0:T(8,128)(2,1)} %get-tuple-element.66), channel_id=1, source_target_pairs={{0,2},{1,3},{2,0},{3,1},{4,6},{5,7},{6,4},{7,5},{8,10},{9,11},{10,... | collective-permute-start | bytes 393224 | tf_op jit(solution)/shard_map/ppermute | solution.py:108
  (21 other events, 164.5 us)

commit v12 on v11

--- a/solution.py
+++ b/solution.py
@@ -321,8 +321,8 @@
 
 
 def attend_kernel(
-    full_width, place, query, keys, values, even, odd, mine, near, mid, seg, o0, o1, o2, o3,
-    q_all, k_all, v_all, k_turned, scale_all, sems,
+    full_width, place, spans, query, keys, values, even, odd, mine, near, mid, seg, o0, o1, o2, o3,
+    q_all, k_all, v_all, o_all, scale_all, sems,
 ):
     z, q = place[0], place[1]
     slab = query.shape[0]
@@ -343,37 +343,62 @@
     scale_all[:, :half] = jnp.where(is_even, scale[2], scale[1])[:, slab - half:]
     scale_all[:, upper:] = jnp.where(is_even, scale[1], scale[2])[:, :half]
     wait(copies)
-    for at in range(0, k_all.shape[0], count):
-        k_turned[:, at:at + count] = jnp.transpose(k_all[at:at + count, :])
-    window = count + 2 * half
+    ext = k_all.shape[0]
     heads = query.shape[1] // HEAD_DIM
     factor = HEAD_DIM ** (-0.5) * math.log2(math.e)
-    for r, out in ((2, o2), (3, o3), (1, o1), (0, o0)):
-        begin = pl.multiple_of((q ^ r) * count, count)
-        at_query = pl.multiple_of((q ^ r) * count + half, count)
-        key_seg = seg[:, pl.ds(begin, window)]
+
+    def block(r, _):
+        b = q ^ r
+        at_query = pl.multiple_of(b * count + half, count)
         query_seg = as_column(seg[:, pl.ds(at_query, count)])
-        k_scale = scale_all[1:2, pl.ds(begin, window)] * factor
         q_scale = as_column(scale_all[0:1, pl.ds(at_query, count)])
-        mask = jnp.tile(query_seg, (1, window // 128)) == key_seg
-        for h in range(heads):
-            cols = slice(h * HEAD_DIM, (h + 1) * HEAD_DIM)
-            q_low = (q_all[pl.ds(begin, count), cols] * q_scale).astype(jnp.bfloat16)
-            scores = jnp.dot(
-                q_low, k_turned[cols, pl.ds(begin, window)], preferred_element_type=jnp.float32
-            )
-            scores = jnp.where(mask, scores * k_scale, floor_score)
-            peak = jnp.max(scores, axis=1, keepdims=True)
-            weights = jnp.exp2(scores - peak)
-            total = jnp.sum(weights, axis=1, keepdims=True)
-            summed = jnp.dot(
-                weights.astype(jnp.bfloat16), v_all[pl.ds(begin, window), cols],
-                preferred_element_type=jnp.float32,
-            )
-            out[cols, :] = jnp.transpose(summed / total).astype(jnp.bfloat16)
-
-
-def attend(full_width, place, query, keys, values, even, odd, sums, seg):
+        for tiles in range(2, 2 * half // count + 2):
+            @pl.when(spans[b, 1] == tiles)
+            def _():
+                width = tiles * count
+                begin = pl.multiple_of(spans[b, 0], 128)
+                keys_at = pl.ds(begin, width)
+                mask = jnp.tile(query_seg, (1, width // 128)) == seg[:, keys_at]
+                k_scale = scale_all[1:2, keys_at] * factor
+                for h in range(heads):
+                    cols = slice(h * HEAD_DIM, (h + 1) * HEAD_DIM)
+                    q_low = q_all[pl.ds(pl.multiple_of(b * count, count), count), cols] * q_scale
+                    scores = lax.dot_general(
+                        q_low.astype(jnp.bfloat16), k_all[keys_at, cols],
+                        (((1,), (1,)), ((), ())), preferred_element_type=jnp.float32,
+                    )
+                    scores = jnp.where(mask, scores * k_scale, floor_score)
+                    peak = jnp.max(scores, axis=1, keepdims=True)
+                    weights = jnp.exp2(scores - peak)
+                    total = jnp.sum(weights, axis=1, keepdims=True)
+                    summed = jnp.dot(
+                        weights.astype(jnp.bfloat16), v_all[keys_at, cols],
+                        preferred_element_type=jnp.float32,
+                    )
+                    o_all[r, cols, :] = jnp.transpose(summed / total).astype(jnp.bfloat16)
+
+        return 0
+
+    lax.fori_loop(0, SLAB, block, 0)
+    stores = [
+        pltpu.make_async_copy(o_all.at[r], out, sems.at[r]) for r, out in enumerate((o0, o1, o2, o3))
+    ]
+    start(stores)
+    wait(stores)
+
+
+def key_spans(seg, slab, count, half):
+    ext = seg.shape[0]
+    index = jnp.arange(ext, dtype=jnp.int32)
+    blocks = seg[half:half + slab].reshape(-1, count)
+    first, last = blocks[:, :1], blocks[:, -1:]
+    begin = jnp.min(jnp.where(seg == first, index, ext), axis=1) // 128 * 128
+    end = jnp.max(jnp.where(seg == last, index, -1), axis=1) + 1
+    tiles = jnp.maximum((end - begin + count - 1) // count, 2)
+    return jnp.stack([jnp.minimum(begin, ext - tiles * count), tiles], axis=1)
+
+
+def attend(full_width, place, spans, query, keys, values, even, odd, sums, seg):
     slab, width = query.shape
     half = even.shape[1]
     count = slab // SLAB
@@ -383,13 +408,13 @@
     return pl.pallas_call(
         functools.partial(attend_kernel, full_width),
         out_shape=(jax.ShapeDtypeStruct((width, count), bf16),) * SLAB,
-        in_specs=[SMEM] + [HBM] * 5 + [VMEM] * 4,
-        out_specs=(VMEM,) * SLAB,
+        in_specs=[SMEM] * 2 + [HBM] * 5 + [VMEM] * 4,
+        out_specs=(HBM,) * SLAB,
         scratch_shapes=[
             pltpu.VMEM((slab, width), jnp.float32),
             pltpu.VMEM((ext, width), bf16),
             pltpu.VMEM((ext, width), bf16),
-            pltpu.VMEM((width, ext), bf16),
+            pltpu.VMEM((SLAB, width, count), bf16),
             pltpu.VMEM((2, ext), jnp.float32),
             pltpu.SemaphoreType.DMA((7,)),
         ],
@@ -400,7 +425,7 @@
             transcendentals=SLAB * count * window * width // HEAD_DIM,
         ),
         name="attend",
-    )(place, query, keys, values, even, odd, *sums, seg)
+    )(place, spans, query, keys, values, even, odd, *sums, seg)
 
 
 def out_kernel(
@@ -515,20 +540,21 @@
 
     query, keys, values, squares, even, odd = late(place, xs, acc, last, *gains)
     even, odd = even_pair(even), odd_pair(odd)
-    sums = squares + in_slab(squares, 1)
-    sums = sums + in_slab(sums, 2)
+    squares, wc = tied(squares, wc)
+    sums = squares
+    for r in range(1, SLAB):
+        sums = sums + in_slab(squares, r)
     sums = sums + across(sums)
     sums = (sums, even_pair(sums), odd_pair(sums))
-    query, wc = tied(query, wc)
-    wd = in_slab(wc, 1)
 
     outside = jnp.full((half,), -1, jnp.int32)
     seg = jnp.concatenate([outside, segment_ids, outside], axis=0)
     seg = lax.dynamic_slice_in_dim(seg, z * slab, slab + 2 * half, 0)
+    spans = key_spans(seg, slab, count, half)
     seg = seg.astype(jnp.float32)[None]
-    blocks = attend(full_width, place, query, keys, values, even, odd, sums, seg)
-    *blocks, wd = tied(*blocks, wd)
-    pieces = (wa, wb, wc, wd)
+    blocks = attend(full_width, place, spans, query, keys, values, even, odd, sums, seg)
+    *blocks, wc = tied(*blocks, wc)
+    pieces = (wa, wb, wc, in_slab(wc, 1))
     spread = []
     for r, i in ((2, 0), (0, 1), (3, 1), (3, 0), (1, 1), (2, 1), (1, 0), (0, 0)):
         to = functools.partial(lambda r, i, z, q, y: (z, q ^ r, y ^ i), r, i)

time: 186 us -> 188 us (1.011)
    ppermute x30 -> x31, waiting for transfers between devices: 96 us -> 97.2 us  [permuted(): return lax.ppermute(x, ('seq', 'tp'), pairs)]
    ppermute x30 -> x31, starting transfers between devices: 32.6 us -> 31.6 us  [permuted(): return lax.ppermute(x, ('seq', 'tp'), pairs)]
    unnamed x31 -> x39, local copies, waits for them, and re-layouts: 3.47 us -> 4.14 us
  transfers between devices with their start and end apart: 30 -> 31, of which waited for: 18 -> 15; matrix products, arithmetic and copies ran while one was open for 7% -> 8% of each run, Pallas kernels for 16% -> 11%
where the time goes in v12:
time: 188 us; the launch traced here: 187 us
  waiting for transfers between devices  97.2 us (52%)
  Pallas kernels  37.9 us (20%)
  starting transfers between devices  31.6 us (17%)
  local copies, waits for them, and re-layouts  10.9 us (6%)
  other arithmetic  8.73 us (5%)
    ppermute x31, waiting for transfers between devices, permuted(): return lax.ppermute(x, ('seq', 'tp'), pairs)  97.2 us
    ppermute x31, starting transfers between devices, permuted(): return lax.ppermute(x, ('seq', 'tp'), pairs)  31.6 us
    pallas_call x1, Pallas kernels, early(): pl.pallas_call(early_kernel, out_shape=jax.ShapeDtypeStruct((SLAB, kinds,...  9.43 us
    pallas_call x1, Pallas kernels, output(): pl.pallas_call(out_kernel, out_shape=jax.ShapeDtypeStruct((share, count),...  8.95 us
    pallas_call x1, Pallas kernels, attend(): pl.pallas_call(functools.partial(attend_kernel, full_width), out_shape=(j...  8.49 us
    pallas_call x1, Pallas kernels, late(): pl.pallas_call(late_kernel, out_shape=(jax.ShapeDtypeStruct((slab, width)...  7.44 us
    unnamed x39, local copies, waits for them, and re-layouts  4.14 us
  transfers between devices with their start and end apart: 31, of which 15 were waited for; matrix products, arithmetic and copies ran while one was open for 8% of the time, Pallas kernels for 11%

profile of v12, /device:TPU:9, one launch (start us, length us, event | category | flops | bytes accessed | tf_op | source)
XLA Modules:
  0.0 186.7 jit_solution(11915510370124625232)
XLA Ops:
  1.3 1.8 collective-permute-start
  4.7 2.3 %collective-permute-start.4 = (bf16[208,1024]{1,0:T(8,128)(2,1)}, bf16[208,1024]{1,0:T(8,128)(2,1)S(1)}, u32[]{:S(2)}, u32[]{:S(2)}) collective-permute-start(bf16[208,1024]{1,0:T(8,128)(2,1)} %get-tuple-element.86), channel_id=1, source_target_pairs={{0,16},{1,17},{2,18},{3,19},{4,20},{5,21},{6,22},{7,23},{8,24},{9,... | collective-permute-start | bytes 1277960 | tf_op jit(solution)/shard_map/ppermute | solution.py:108
  10.3 3.5 %norm.1.xa = bf16[4,256,896]{2,1,0:T(8,128)(2,1)} custom-call(bf16[256,3200]{1,0:T(8,128)(2,1)} %tokens.1, f32[1,3200]{1,0:T(1,128)} %broadcast_in_dim.39.gain), custom_call_target="tpu_custom_call" | custom-call | tf_op jit(solution)/shard_map/norm/pallas_call | solution.py:167
  13.8 3.9 %collective-permute-done.1 = bf16[3,200,256]{2,1,0:T(8,128)(2,1)S(1)} collective-permute-done((bf16[3,200,256]{2,1,0:T(8,128)(2,1)S(1)}, bf16[3,200,256]{2,1,0:T(8,128)(2,1)S(1)}, u32[]{:S(2)}, u32[]{:S(2)}) %collective-permute-start.1) | collective-permute-done | bytes 307232 | tf_op jit(solution)/shard_map/ppermute | solution.py:108
  20.3 2.9 %collective-permute-done.3 = bf16[208,1024]{1,0:T(8,128)(2,1)S(1)} collective-permute-done((bf16[208,1024]{1,0:T(8,128)(2,1)}, bf16[208,1024]{1,0:T(8,128)(2,1)S(1)}, u32[]{:S(2)}, u32[]{:S(2)}) %collective-permute-start.3) | collective-permute-done | bytes 426016 | tf_op jit(solution)/shard_map/ppermute | solution.py:108
  23.2 2.8 %collective-permute-done.4 = bf16[208,1024]{1,0:T(8,128)(2,1)S(1)} collective-permute-done((bf16[208,1024]{1,0:T(8,128)(2,1)}, bf16[208,1024]{1,0:T(8,128)(2,1)S(1)}, u32[]{:S(2)}, u32[]{:S(2)}) %collective-permute-start.4) | collective-permute-done | bytes 426016 | tf_op jit(solution)/shard_map/ppermute | solution.py:108
  29.8 2.3 %collective-permute-start.8 = (bf16[3,800,256]{2,1,0:T(8,128)(2,1)}, bf16[3,800,256]{2,1,0:T(8,128)(2,1)}, u32[]{:S(2)}, u32[]{:S(2)}) collective-permute-start(bf16[3,800,256]{2,1,0:T(8,128)(2,1)} %pad_maximum_fusion.1.own), channel_id=1, source_target_pairs={{0,16},{1,17},{2,18},{3,19},{4,20},{5,21},{6,22},{7,23},{8,24},{9,... | collective-permute-start | bytes 3686408 | tf_op jit(solution)/shard_map/ppermute | solution.py:108
  32.1 32.8 %collective-permute-done.5 = bf16[208,1024]{1,0:T(8,128)(2,1)} collective-permute-done((bf16[208,1024]{1,0:T(8,128)(2,1)S(1)}, bf16[208,1024]{1,0:T(8,128)(2,1)}, u32[]{:S(2)}, u32[]{:S(2)}) %collective-permute-start.5) | collective-permute-done | bytes 426016 | tf_op jit(solution)/shard_map/ppermute | solution.py:108
  68.5 16.3 %collective-permute-done.10 = bf16[2,208,1024]{2,1,0:T(8,128)(2,1)S(1)} collective-permute-done((bf16[2,208,1024]{2,1,0:T(8,128)(2,1)S(1)}, bf16[2,208,1024]{2,1,0:T(8,128)(2,1)S(1)}, u32[]{:S(2)}, u32[]{:S(2)}) %collective-permute-start.10) | collective-permute-done | bytes 852000 | tf_op jit(solution)/shard_map/ppermute | solution.py:108
  85.0 6.3 %collective-permute-done.7.near = bf16[3,800,256]{2,1,0:T(8,128)(2,1)} collective-permute-done((bf16[3,800,256]{2,1,0:T(8,128)(2,1)}, bf16[3,800,256]{2,1,0:T(8,128)(2,1)}, u32[]{:S(2)}, u32[]{:S(2)}) %collective-permute-start.7) | collective-permute-done | bytes 1228832 | tf_op jit(solution)/shard_map/ppermute | solution.py:108
  91.3 2.1 %collective-permute-done.8.far = bf16[3,800,256]{2,1,0:T(8,128)(2,1)} collective-permute-done((bf16[3,800,256]{2,1,0:T(8,128)(2,1)}, bf16[3,800,256]{2,1,0:T(8,128)(2,1)}, u32[]{:S(2)}, u32[]{:S(2)}) %collective-permute-start.8) | collective-permute-done | bytes 1228832 | tf_op jit(solution)/shard_map/ppermute | solution.py:108
  97.5 2.7 %collective-permute-done.11.xd = bf16[4,256,896]{2,1,0:T(8,128)(2,1)S(1)} collective-permute-done((bf16[4,256,896]{2,1,0:T(8,128)(2,1)}, bf16[4,256,896]{2,1,0:T(8,128)(2,1)S(1)}, u32[]{:S(2)}, u32[]{:S(2)}) %collective-permute-start.11) | collective-permute-done | bytes 1835040 | tf_op jit(solution)/shard_map/ppermute | solution.py:108
  101.4 9.4 %early.1.acc = f32[4,3,256,256]{3,2,1,0:T(8,128)} custom-call(s32[3]{0:T(128)} %pad_add_fusion.1.place, bf16[4,256,896]{2,1,0:T(8,128)(2,1)} %norm.1.xa, bf16[4,256,896]{2,1,0:T(8,128)(2,1)} %collective-permute-done.6.xb, bf16[4,256,896]{2,1,0:T(8,128)(2,1)} %collective-permute-done.9.xc, bf16[4,256,896]{2,1,0:T(8,128)(2,1)} %copy-done.3, ...), custom_call_target="tpu_custom_call" | custom-call | flops 7549747200 | bytes 8601600 | tf_op jit(solution)/shard_map/early/pallas_call | solution.py:217
  110.9 11.7 %collective-permute-done.12.last = bf16[3,800,256]{2,1,0:T(8,128)(2,1)} collective-permute-done((bf16[3,800,256]{2,1,0:T(8,128)(2,1)}, bf16[3,800,256]{2,1,0:T(8,128)(2,1)}, u32[]{:S(2)}, u32[]{:S(2)}) %collective-permute-start.12) | collective-permute-done | bytes 1228832 | tf_op jit(solution)/shard_map/ppermute | solution.py:108
  122.6 7.4 %late.1 = (f32[1024,256]{1,0:T(8,128)}, bf16[1024,256]{1,0:T(8,128)(2,1)}, bf16[1024,256]{1,0:T(8,128)(2,1)}, f32[2,1024]{1,0:T(2,128)}, bf16[2,512,256]{2,1,0:T(8,128)(2,1)}, /*index=5*/bf16[2,512,256]{2,1,0:T(8,128)(2,1)}) custom-call(s32[3]{0:T(128)} %pad_add_fusion.1.place, bf16[4,256,896]{2,1,0:T(8,128)(2,1)} %norm.1.xa, ...), custom_call_target="tpu_custom_call" | custom-call | flops 1258291200 | bytes 2867200 | tf_op jit(solution)/shard_map/late/pallas_call | solution.py:289
  130.1 2.5 %collective-permute-done.16.wc = bf16[2,2,208,1024]{3,2,1,0:T(8,128)(2,1)} collective-permute-done((bf16[2,2,208,1024]{3,2,1,0:T(8,128)(2,1)S(1)}, bf16[2,2,208,1024]{3,2,1,0:T(8,128)(2,1)}, u32[]{:S(2)}, u32[]{:S(2)}) %collective-permute-start.16) | collective-permute-done | bytes 1703968 | tf_op jit(solution)/shard_map/ppermute | solution.py:108
  139.6 1.5 collective-permute-done.20
  143.7 5.7 %collective-permute-done.21.near = f32[2,1024]{1,0:T(2,128)S(1)} collective-permute-done((f32[2,1024]{1,0:T(2,128)S(1)}, f32[2,1024]{1,0:T(2,128)S(1)}, u32[]{:S(2)}, u32[]{:S(2)}) %collective-permute-start.21) | collective-permute-done | bytes 8224 | tf_op jit(solution)/shard_map/ppermute | solution.py:108
  150.6 8.5 %attend.1 = (bf16[256,256]{1,0:T(8,128)(2,1)}, bf16[256,256]{1,0:T(8,128)(2,1)}, bf16[256,256]{1,0:T(8,128)(2,1)}, bf16[256,256]{1,0:T(8,128)(2,1)}) custom-call(s32[3]{0:T(128)} %pad_add_fusion.1.place, s32[4,2]{1,0:T(4,128)} %pad_add_fusion.spans, f32[1024,256]{1,0:T(8,128)} %get-tuple-element.51.query, bf16[1024,256]{1,0:T(8,128)(2,1)} %get-tuple-element.52.keys, ...), custom_call_target="tpu_custom_call" | custom-call | flops 1342177280 | bytes 3145728 | tf_op jit(solution)/shard_map/attend/pallas_call | solution.py:408
  162.1 1.6 collective-permute-start.25
  163.8 2.0 %collective-permute-done.23.c20 = bf16[256,256]{1,0:T(8,128)(2,1)S(1)} collective-permute-done((bf16[256,256]{1,0:T(8,128)(2,1)}, bf16[256,256]{1,0:T(8,128)(2,1)S(1)}, u32[]{:S(2)}, u32[]{:S(2)}) %collective-permute-start.23) | collective-permute-done | bytes 131104 | tf_op jit(solution)/shard_map/ppermute | solution.py:108
  167.1 3.7 %collective-permute-start.27 = (bf16[256,256]{1,0:T(8,128)(2,1)}, bf16[256,256]{1,0:T(8,128)(2,1)S(1)}, u32[]{:S(2)}, u32[]{:S(2)}) collective-permute-start(bf16[256,256]{1,0:T(8,128)(2,1)} %get-tuple-element.66), channel_id=1, source_target_pairs={{0,3},{1,2},{2,1},{3,0},{4,7},{5,6},{6,5},{7,4},{8,11},{9,10},{10,... | collective-permute-start | bytes 393224 | tf_op jit(solution)/shard_map/ppermute | solution.py:108
  173.1 3.8 %collective-permute-done.27.c11 = bf16[256,256]{1,0:T(8,128)(2,1)S(1)} collective-permute-done((bf16[256,256]{1,0:T(8,128)(2,1)}, bf16[256,256]{1,0:T(8,128)(2,1)S(1)}, u32[]{:S(2)}, u32[]{:S(2)}) %collective-permute-start.27) | collective-permute-done | bytes 131104 | tf_op jit(solution)/shard_map/ppermute | solution.py:108
  177.6 9.0 %output.1 = bf16[1600,256]{1,0:T(8,128)(2,1)} custom-call(s32[3]{0:T(128)} %pad_add_fusion.1.place, bf16[256,256]{1,0:T(8,128)(2,1)} %copy-done.5, bf16[256,256]{1,0:T(8,128)(2,1)} %copy-done.6, bf16[256,256]{1,0:T(8,128)(2,1)} %copy-done.7, bf16[256,256]{1,0:T(8,128)(2,1)} %copy-done.8, bf16[256,256]{1,0:T(8,128)(2,1)} %copy-done.10, ...), custom_call_target="tpu_custom_call" | custom-call | flops 1677721600 | bytes 6553600 | tf_op jit(solution)/shard_map/output/pallas_call | solution.py:472
  (109 shorter events, 39.8 us)
Async XLA Ops:
  1.3 12.5 %collective-permute-start = (bf16[3,200,256]{2,1,0:T(8,128)(2,1)S(1)}, bf16[3,200,256]{2,1,0:T(8,128)(2,1)S(1)}, u32[]{:S(2)}, u32[]{:S(2)}) collective-permute-start(bf16[3,200,256]{2,1,0:T(8,128)(2,1)S(1)} %get-tuple-element.81), channel_id=1, source_target_pairs={{0,6},{1,7},{2,4},{3,5},{4,2},{5,3},{6,0},{7,1},{8,14},{9,15},{10,... | collective-permute-start | bytes 921608 | tf_op jit(solution)/shard_map/ppermute | solution.py:108
  3.1 14.6 %collective-permute-start.1 = (bf16[3,200,256]{2,1,0:T(8,128)(2,1)S(1)}, bf16[3,200,256]{2,1,0:T(8,128)(2,1)S(1)}, u32[]{:S(2)}, u32[]{:S(2)}) collective-permute-start(bf16[3,200,256]{2,1,0:T(8,128)(2,1)S(1)} %get-tuple-element.82), channel_id=1, source_target_pairs={{0,4},{1,5},{2,6},{3,7},{4,0},{5,1},{6,2},{7,3},{8,12},{9,13},{10,... | collective-permute-start | bytes 921608 | tf_op jit(solution)/shard_map/ppermute | solution.py:108
  3.4 14.4 %collective-permute-start.2 = (bf16[3,200,256]{2,1,0:T(8,128)(2,1)S(1)}, bf16[3,200,256]{2,1,0:T(8,128)(2,1)}, u32[]{:S(2)}, u32[]{:S(2)}) collective-permute-start(bf16[3,200,256]{2,1,0:T(8,128)(2,1)S(1)} %get-tuple-element.83), channel_id=1, source_target_pairs={{0,2},{1,3},{2,0},{3,1},{4,6},{5,7},{6,4},{7,5},{8,10},{9,11},{10,... | collective-permute-start | bytes 921608 | tf_op jit(solution)/shard_map/ppermute | solution.py:108
  4.5 18.7 %collective-permute-start.3 = (bf16[208,1024]{1,0:T(8,128)(2,1)}, bf16[208,1024]{1,0:T(8,128)(2,1)S(1)}, u32[]{:S(2)}, u32[]{:S(2)}) collective-permute-start(bf16[208,1024]{1,0:T(8,128)(2,1)} %get-tuple-element.86), channel_id=1, source_target_pairs={{0,8},{1,9},{2,10},{3,11},{4,12},{5,13},{6,14},{7,15},{8,0},{9,1},... | collective-permute-start | bytes 1277960 | tf_op jit(solution)/shard_map/ppermute | solution.py:108
  4.7 21.4 %collective-permute-start.4 = (bf16[208,1024]{1,0:T(8,128)(2,1)}, bf16[208,1024]{1,0:T(8,128)(2,1)S(1)}, u32[]{:S(2)}, u32[]{:S(2)}) collective-permute-start(bf16[208,1024]{1,0:T(8,128)(2,1)} %get-tuple-element.86), channel_id=1, source_target_pairs={{0,16},{1,17},{2,18},{3,19},{4,20},{5,21},{6,22},{7,23},{8,24},{9,... | collective-permute-start | bytes 1277960 | tf_op jit(solution)/shard_map/ppermute | solution.py:108
  26.0 38.8 %collective-permute-start.6 = (bf16[4,256,896]{2,1,0:T(8,128)(2,1)S(1)}, bf16[4,256,896]{2,1,0:T(8,128)(2,1)}, u32[]{:S(2)}, u32[]{:S(2)}) collective-permute-start(bf16[4,256,896]{2,1,0:T(8,128)(2,1)S(1)} %copy-done), channel_id=1, source_target_pairs={{0,2},{1,3},{2,0},{3,1},{4,6},{5,7},{6,4},{7,5},{8,10},{9,11},{10,... | collective-permute-start | bytes 5505032 | tf_op jit(solution)/shard_map/ppermute | solution.py:108
  27.2 66.2 %collective-permute-start.9 = (bf16[4,256,896]{2,1,0:T(8,128)(2,1)S(1)}, bf16[4,256,896]{2,1,0:T(8,128)(2,1)}, u32[]{:S(2)}, u32[]{:S(2)}) collective-permute-start(bf16[4,256,896]{2,1,0:T(8,128)(2,1)S(1)} %copy-done), channel_id=1, source_target_pairs={{0,4},{1,5},{2,6},{3,7},{4,0},{5,1},{6,2},{7,3},{8,12},{9,13},{10,... | collective-permute-start | bytes 5505032 | tf_op jit(solution)/shard_map/ppermute | solution.py:108
  28.3 36.6 %collective-permute-start.5 = (bf16[208,1024]{1,0:T(8,128)(2,1)S(1)}, bf16[208,1024]{1,0:T(8,128)(2,1)}, u32[]{:S(2)}, u32[]{:S(2)}) collective-permute-start(bf16[208,1024]{1,0:T(8,128)(2,1)S(1)} %collective-permute-done.4), channel_id=1, source_target_pairs={{0,8},{1,9},{2,10},{3,11},{4,12},{5,13},{6,14},{7,15},{8,0},{9,1},... | collective-permute-start | bytes 1277960 | tf_op jit(solution)/shard_map/ppermute | solution.py:108
  29.6 61.7 %collective-permute-start.7 = (bf16[3,800,256]{2,1,0:T(8,128)(2,1)}, bf16[3,800,256]{2,1,0:T(8,128)(2,1)}, u32[]{:S(2)}, u32[]{:S(2)}) collective-permute-start(bf16[3,800,256]{2,1,0:T(8,128)(2,1)} %pad_maximum_fusion.1.own), channel_id=1, source_target_pairs={{0,8},{1,9},{2,10},{3,11},{4,12},{5,13},{6,14},{7,15},{8,0},{9,1},... | collective-permute-start | bytes 3686408 | tf_op jit(solution)/shard_map/ppermute | solution.py:108
  29.8 63.6 %collective-permute-start.8 = (bf16[3,800,256]{2,1,0:T(8,128)(2,1)}, bf16[3,800,256]{2,1,0:T(8,128)(2,1)}, u32[]{:S(2)}, u32[]{:S(2)}) collective-permute-start(bf16[3,800,256]{2,1,0:T(8,128)(2,1)} %pad_maximum_fusion.1.own), channel_id=1, source_target_pairs={{0,16},{1,17},{2,18},{3,19},{4,20},{5,21},{6,22},{7,23},{8,24},{9,... | collective-permute-start | bytes 3686408 | tf_op jit(solution)/shard_map/ppermute | solution.py:108
  66.0 18.8 %collective-permute-start.10 = (bf16[2,208,1024]{2,1,0:T(8,128)(2,1)S(1)}, bf16[2,208,1024]{2,1,0:T(8,128)(2,1)S(1)}, u32[]{:S(2)}, u32[]{:S(2)}) collective-permute-start(bf16[2,208,1024]{2,1,0:T(8,128)(2,1)S(1)} %maximum_select_fusion.1), channel_id=1, source_target_pairs={{0,1},{1,0},{2,3},{3,2},{4,5},{5,4},{6,7},{7,6},{8,9},{9,8},{10,11... | collective-permute-start | bytes 2555912 | tf_op jit(solution)/shard_map/ppermute | solution.py:108
  93.4 6.8 %collective-permute-start.11 = (bf16[4,256,896]{2,1,0:T(8,128)(2,1)}, bf16[4,256,896]{2,1,0:T(8,128)(2,1)S(1)}, u32[]{:S(2)}, u32[]{:S(2)}) collective-permute-start(bf16[4,256,896]{2,1,0:T(8,128)(2,1)} %collective-permute-done.9.xc), channel_id=1, source_target_pairs={{0,2},{1,3},{2,0},{3,1},{4,6},{5,7},{6,4},{7,5},{8,10},{9,11},{10,... | collective-permute-start | bytes 5505032 | tf_op jit(solution)/shard_map/ppermute | solution.py:108
  94.2 28.4 %collective-permute-start.13 = (bf16[2,2,208,1024]{3,2,1,0:T(8,128)(2,1)S(1)}, bf16[2,2,208,1024]{3,2,1,0:T(8,128)(2,1)}, u32[]{:S(2)}, u32[]{:S(2)}) collective-permute-start(bf16[2,2,208,1024]{3,2,1,0:T(8,128)(2,1)S(1)} %pad_maximum_fusion.wa), channel_id=1, source_target_pairs={{0,2},{1,3},{2,0},{3,1},{4,6},{5,7},{6,4},{7,5},{8,10},{9,11},{10,... | collective-permute-start | bytes 5111816 | tf_op jit(solution)/shard_map/ppermute | solution.py:108
  94.2 38.4 %collective-permute-start.16 = (bf16[2,2,208,1024]{3,2,1,0:T(8,128)(2,1)S(1)}, bf16[2,2,208,1024]{3,2,1,0:T(8,128)(2,1)}, u32[]{:S(2)}, u32[]{:S(2)}) collective-permute-start(bf16[2,2,208,1024]{3,2,1,0:T(8,128)(2,1)S(1)} %pad_maximum_fusion.wa), channel_id=1, source_target_pairs={{0,4},{1,5},{2,6},{3,7},{4,0},{5,1},{6,2},{7,3},{8,12},{9,13},{10,... | collective-permute-start | bytes 5111816 | tf_op jit(solution)/shard_map/ppermute | solution.py:108
  94.5 28.1 %collective-permute-start.12 = (bf16[3,800,256]{2,1,0:T(8,128)(2,1)}, bf16[3,800,256]{2,1,0:T(8,128)(2,1)}, u32[]{:S(2)}, u32[]{:S(2)}) collective-permute-start(bf16[3,800,256]{2,1,0:T(8,128)(2,1)} %collective-permute-done.8.far), channel_id=1, source_target_pairs={{0,8},{1,9},{2,10},{3,11},{4,12},{5,13},{6,14},{7,15},{8,0},{9,1},... | collective-permute-start | bytes 3686408 | tf_op jit(solution)/shard_map/ppermute | solution.py:108
  135.7 13.9 %collective-permute-start.14 = (bf16[2,512,256]{2,1,0:T(8,128)(2,1)}, bf16[2,512,256]{2,1,0:T(8,128)(2,1)S(1)}, u32[]{:S(2)}, u32[]{:S(2)}) collective-permute-start(bf16[2,512,256]{2,1,0:T(8,128)(2,1)} %get-tuple-element.54), channel_id=1, source_target_pairs={{0,8},{1,9},{2,10},{3,11},{4,12},{5,13},{6,14},{7,15},{8,0},{9,1},... | collective-permute-start | bytes 1572872 | tf_op jit(solution)/shard_map/ppermute | solution.py:108
  136.3 13.4 %collective-permute-start.15 = (bf16[2,512,256]{2,1,0:T(8,128)(2,1)}, bf16[2,512,256]{2,1,0:T(8,128)(2,1)S(1)}, u32[]{:S(2)}, u32[]{:S(2)}) collective-permute-start(bf16[2,512,256]{2,1,0:T(8,128)(2,1)} %get-tuple-element.55), channel_id=1, source_target_pairs={{0,2},{1,3},{2,0},{3,1},{4,6},{5,7},{6,4},{7,5},{8,16},{9,17},{10,... | collective-permute-start | bytes 1572872 | tf_op jit(solution)/shard_map/ppermute | solution.py:108
  141.1 8.3 %collective-permute-start.21 = (f32[2,1024]{1,0:T(2,128)S(1)}, f32[2,1024]{1,0:T(2,128)S(1)}, u32[]{:S(2)}, u32[]{:S(2)}) collective-permute-start(f32[2,1024]{1,0:T(2,128)S(1)} %add.111.mine), channel_id=1, source_target_pairs={{0,8},{1,9},{2,10},{3,11},{4,12},{5,13},{6,14},{7,15},{8,0},{9,1},... | collective-permute-start | bytes 24584 | tf_op jit(solution)/shard_map/ppermute | solution.py:108
  141.7 7.9 %collective-permute-start.22 = (f32[2,1024]{1,0:T(2,128)S(1)}, f32[2,1024]{1,0:T(2,128)S(1)}, u32[]{:S(2)}, u32[]{:S(2)}) collective-permute-start(f32[2,1024]{1,0:T(2,128)S(1)} %add.111.mine), channel_id=1, source_target_pairs={{0,2},{1,3},{2,0},{3,1},{4,6},{5,7},{6,4},{7,5},{8,16},{9,17},{10,... | collective-permute-start | bytes 24584 | tf_op jit(solution)/shard_map/ppermute | solution.py:108
  159.1 17.8 %collective-permute-start.30 = (bf16[2,2,208,1024]{3,2,1,0:T(8,128)(2,1)}, bf16[2,2,208,1024]{3,2,1,0:T(8,128)(2,1)}, u32[]{:S(2)}, u32[]{:S(2)}) collective-permute-start(bf16[2,2,208,1024]{3,2,1,0:T(8,128)(2,1)} %collective-permute-done.16.wc), channel_id=1, source_target_pairs={{0,2},{1,3},{2,0},{3,1},{4,6},{5,7},{6,4},{7,5},{8,10},{9,11},{10,... | collective-permute-start | bytes 5111816 | tf_op jit(solution)/shard_map/ppermute | solution.py:108
  162.1 8.7 %collective-permute-start.25 = (bf16[256,256]{1,0:T(8,128)(2,1)}, bf16[256,256]{1,0:T(8,128)(2,1)S(1)}, u32[]{:S(2)}, u32[]{:S(2)}) collective-permute-start(bf16[256,256]{1,0:T(8,128)(2,1)} %get-tuple-element.65), channel_id=1, source_target_pairs={{0,7},{1,6},{2,5},{3,4},{4,3},{5,2},{6,1},{7,0},{8,15},{9,14},{10,... | collective-permute-start | bytes 393224 | tf_op jit(solution)/shard_map/ppermute | solution.py:108
  163.7 9.4 %collective-permute-start.26 = (bf16[256,256]{1,0:T(8,128)(2,1)}, bf16[256,256]{1,0:T(8,128)(2,1)S(1)}, u32[]{:S(2)}, u32[]{:S(2)}) collective-permute-start(bf16[256,256]{1,0:T(8,128)(2,1)} %get-tuple-element.65), channel_id=1, source_target_pairs={{0,6},{1,7},{2,4},{3,5},{4,2},{5,3},{6,0},{7,1},{8,14},{9,15},{10,... | collective-permute-start | bytes 393224 | tf_op jit(solution)/shard_map/ppermute | solution.py:108
  165.8 11.1 %collective-permute-start.28 = (bf16[256,256]{1,0:T(8,128)(2,1)}, bf16[256,256]{1,0:T(8,128)(2,1)S(1)}, u32[]{:S(2)}, u32[]{:S(2)}) collective-permute-start(bf16[256,256]{1,0:T(8,128)(2,1)} %get-tuple-element.63), channel_id=1, source_target_pairs={{0,5},{1,4},{2,7},{3,6},{4,1},{5,0},{6,3},{7,2},{8,13},{9,12},{10,... | collective-permute-start | bytes 393224 | tf_op jit(solution)/shard_map/ppermute | solution.py:108
  167.1 9.7 %collective-permute-start.27 = (bf16[256,256]{1,0:T(8,128)(2,1)}, bf16[256,256]{1,0:T(8,128)(2,1)S(1)}, u32[]{:S(2)}, u32[]{:S(2)}) collective-permute-start(bf16[256,256]{1,0:T(8,128)(2,1)} %get-tuple-element.66), channel_id=1, source_target_pairs={{0,3},{1,2},{2,1},{3,0},{4,7},{5,6},{6,5},{7,4},{8,11},{9,10},{10,... | collective-permute-start | bytes 393224 | tf_op jit(solution)/shard_map/ppermute | solution.py:108
  (26 other events, 157.7 us)

commit v13 on v12

--- a/solution.py
+++ b/solution.py
@@ -420,7 +420,7 @@
         ],
         compiler_params=pltpu.CompilerParams(vmem_limit_bytes=KERNEL_VMEM),
         cost_estimate=pl.CostEstimate(
-            flops=SLAB * 4 * count * window * width,
+            flops=64 * SLAB * count * window * width,
             bytes_accessed=4 * ext * width + 4 * slab * width,
             transcendentals=SLAB * count * window * width // HEAD_DIM,
         ),
@@ -522,30 +522,36 @@
     out_near, out_far = even_pair(out_own), half_pair(out_own)
     gains = [lax.dynamic_slice_in_dim(g, q * width, width, 0)[None] for g in (q_gain, k_gain)]
 
-    own, x0, out_near, out_far, *gains = tied(own, x0, out_near, out_far, *gains)
+    x0, out_near, out_far, *gains = tied(x0, out_near, out_far, *gains)
     out_last = even_pair(out_far)
+    x2 = in_slab(x0, 2)
+    out_last, own, x0 = tied(out_last, own, x0)
     near, far = even_pair(own), half_pair(own)
-    x1, x2 = in_slab(x0, 1), in_slab(x0, 2)
+    x1 = in_slab(x0, 1)
     out_last, x1 = tied(out_last, x1)
     close, away = jnp.stack([out_own, out_near]), jnp.stack([out_far, out_last])
     keep, give = jnp.where(home, close, away), jnp.where(home, away, close)
-    wa = jnp.stack([keep, across(give)])
-    near, far, x2, wa = tied(near, far, x2, wa)
+    got = across(give)
+    keep_x = in_slab(keep, 2)
+    near, far, x1, x2, got, keep_x = tied(near, far, x1, x2, got, keep_x)
     last = even_pair(far)
-    x3 = in_slab(x2, 1)
-    wc, wb = in_slab(wa, 2), in_slab(wa, 1)
+    x3, got_x = in_slab(x2, 1), in_slab(got, 2)
+    wa = jnp.stack([keep, got])
+    wb = in_slab(wa, 1)
     xs = (x0, x1, x2, x3)
     acc = early(place, xs, own, near, far)
-    last, acc, wb = tied(last, acc, wb)
+    last, acc, wb, got_x = tied(last, acc, wb, got_x)
+    wc = jnp.stack([keep_x, got_x])
 
     query, keys, values, squares, even, odd = late(place, xs, acc, last, *gains)
     even, odd = even_pair(even), odd_pair(odd)
-    squares, wc = tied(squares, wc)
     sums = squares
     for r in range(1, SLAB):
         sums = sums + in_slab(squares, r)
     sums = sums + across(sums)
     sums = (sums, even_pair(sums), odd_pair(sums))
+    query, wc = tied(query, wc)
+    wd = in_slab(wc, 1)
 
     outside = jnp.full((half,), -1, jnp.int32)
     seg = jnp.concatenate([outside, segment_ids, outside], axis=0)
@@ -553,8 +559,8 @@
     spans = key_spans(seg, slab, count, half)
     seg = seg.astype(jnp.float32)[None]
     blocks = attend(full_width, place, spans, query, keys, values, even, odd, sums, seg)
-    *blocks, wc = tied(*blocks, wc)
-    pieces = (wa, wb, wc, in_slab(wc, 1))
+    *blocks, wd = tied(*blocks, wd)
+    pieces = (wa, wb, wc, wd)
     spread = []
     for r, i in ((2, 0), (0, 1), (3, 1), (3, 0), (1, 1), (2, 1), (1, 0), (0, 0)):
         to = functools.partial(lambda r, i, z, q, y: (z, q ^ r, y ^ i), r, i)

time: 188 us -> 189 us (level)
  waiting for transfers between devices: 97.2 us -> 93.9 us
  starting transfers between devices: 31.6 us -> 34.3 us
    ppermute x31 -> x32, waiting for transfers between devices: 97.2 us -> 93.9 us  [permuted(): return lax.ppermute(x, ('seq', 'tp'), pairs)]
    ppermute x31 -> x32, starting transfers between devices: 31.6 us -> 34.3 us  [permuted(): return lax.ppermute(x, ('seq', 'tp'), pairs)]
    another operation x1 -> x2, other arithmetic: 0.16 us -> 2.63 us  [the longest x1 1.31 us: slab_plan(): wa = jnp.stack([keep, got])]
    select_n x2, other arithmetic: 2.31 us -> 0.3 us  [slab_plan(): keep, give = (jnp.where(home, close, away), jnp.where(home, away, close))]
    unnamed x39 -> x47, local copies, waits for them, and re-layouts: 4.14 us -> 4.36 us
  transfers between devices with their start and end apart: 31 -> 32, of which waited for: 15 -> 13; matrix products, arithmetic and copies ran while one was open for 8% -> 9% of each run, Pallas kernels for 11% -> 12%
where the time goes in v13:
time: 189 us; the launch traced here: 188 us
  waiting for transfers between devices  93.9 us (50%)
  Pallas kernels  38.4 us (20%)
  starting transfers between devices  34.3 us (18%)
  local copies, waits for them, and re-layouts  12 us (6%)
  other arithmetic  9.14 us (5%)
    ppermute x32, waiting for transfers between devices, permuted(): return lax.ppermute(x, ('seq', 'tp'), pairs)  93.9 us
    ppermute x32, starting transfers between devices, permuted(): return lax.ppermute(x, ('seq', 'tp'), pairs)  34.3 us
    pallas_call x1, Pallas kernels, early(): pl.pallas_call(early_kernel, out_shape=jax.ShapeDtypeStruct((SLAB, kinds,...  9.41 us
    pallas_call x1, Pallas kernels, attend(): pl.pallas_call(functools.partial(attend_kernel, full_width), out_shape=(j...  9.14 us
    pallas_call x1, Pallas kernels, output(): pl.pallas_call(out_kernel, out_shape=jax.ShapeDtypeStruct((share, count),...  8.89 us
    pallas_call x1, Pallas kernels, late(): pl.pallas_call(late_kernel, out_shape=(jax.ShapeDtypeStruct((slab, width)...  7.43 us
    unnamed x47, local copies, waits for them, and re-layouts  4.36 us
  transfers between devices with their start and end apart: 32, of which 13 were waited for; matrix products, arithmetic and copies ran while one was open for 9% of the time, Pallas kernels for 12%

profile of v13, /device:TPU:9, one launch (start us, length us, event | category | flops | bytes accessed | tf_op | source)
XLA Modules:
  0.0 188.2 jit_solution(3052304853191675239)
XLA Ops:
  0.0 2.0 %pad_bitcast_fusion = (bf16[1,1,208,1024]{3,2,1,0:T(8,128)(2,1)}, bf16[1,208,1024]{2,1,0:T(8,128)(2,1)S(1)}, bf16[208,1024]{1,0:T(8,128)(2,1)S(1)}) fusion(bf16[200,1024]{1,0:T(8,128)(2,1)} %bitcast.54), kind=kLoop, calls=%fused_computation.52 | loop fusion | bytes 1687552 | tf_op jit(solution)/shard_map/stack | solution.py:532
  2.0 2.5 %collective-permute-start.1 = (bf16[208,1024]{1,0:T(8,128)(2,1)S(1)}, bf16[208,1024]{1,0:T(8,128)(2,1)S(1)}, u32[]{:S(2)}, u32[]{:S(2)}) collective-permute-start(bf16[208,1024]{1,0:T(8,128)(2,1)S(1)} %get-tuple-element.98), channel_id=1, source_target_pairs={{0,16},{1,17},{2,18},{3,19},{4,20},{5,21},{6,22},{7,23},{8,24},{9,... | collective-permute-start | bytes 1277960 | tf_op jit(solution)/shard_map/ppermute | solution.py:108
  5.5 2.3 %collective-permute-start.3 = (bf16[3,200,256]{2,1,0:T(8,128)(2,1)}, bf16[3,200,256]{2,1,0:T(8,128)(2,1)}, u32[]{:S(2)}, u32[]{:S(2)}) collective-permute-start(bf16[3,200,256]{2,1,0:T(8,128)(2,1)} %get-tuple-element.93), channel_id=1, source_target_pairs={{0,6},{1,7},{2,4},{3,5},{4,2},{5,3},{6,0},{7,1},{8,14},{9,15},{10,... | collective-permute-start | bytes 921608 | tf_op jit(solution)/shard_map/ppermute | solution.py:108
  11.5 3.6 %norm.1.xa = bf16[4,256,896]{2,1,0:T(8,128)(2,1)} custom-call(bf16[256,3200]{1,0:T(8,128)(2,1)} %tokens.1, f32[1,3200]{1,0:T(1,128)} %broadcast_in_dim.39.gain), custom_call_target="tpu_custom_call" | custom-call | tf_op jit(solution)/shard_map/norm/pallas_call | solution.py:167
  15.1 4.7 %collective-permute-done = bf16[208,1024]{1,0:T(8,128)(2,1)S(1)} collective-permute-done((bf16[208,1024]{1,0:T(8,128)(2,1)S(1)}, bf16[208,1024]{1,0:T(8,128)(2,1)S(1)}, u32[]{:S(2)}, u32[]{:S(2)}) %collective-permute-start) | collective-permute-done | bytes 426016 | tf_op jit(solution)/shard_map/ppermute | solution.py:108
  19.8 3.1 %collective-permute-done.1 = bf16[208,1024]{1,0:T(8,128)(2,1)S(1)} collective-permute-done((bf16[208,1024]{1,0:T(8,128)(2,1)S(1)}, bf16[208,1024]{1,0:T(8,128)(2,1)S(1)}, u32[]{:S(2)}, u32[]{:S(2)}) %collective-permute-start.1) | collective-permute-done | bytes 426016 | tf_op jit(solution)/shard_map/ppermute | solution.py:108
  25.6 7.0 %collective-permute-done.2 = bf16[208,1024]{1,0:T(8,128)(2,1)S(1)} collective-permute-done((bf16[208,1024]{1,0:T(8,128)(2,1)S(1)}, bf16[208,1024]{1,0:T(8,128)(2,1)S(1)}, u32[]{:S(2)}, u32[]{:S(2)}) %collective-permute-start.2) | collective-permute-done | bytes 426016 | tf_op jit(solution)/shard_map/ppermute | solution.py:108
  32.6 2.5 %collective-permute-start.8 = (bf16[4,256,896]{2,1,0:T(8,128)(2,1)S(1)}, bf16[4,256,896]{2,1,0:T(8,128)(2,1)}, u32[]{:S(2)}, u32[]{:S(2)}) collective-permute-start(bf16[4,256,896]{2,1,0:T(8,128)(2,1)S(1)} %copy-done), channel_id=1, source_target_pairs={{0,2},{1,3},{2,0},{3,1},{4,6},{5,7},{6,4},{7,5},{8,10},{9,11},{10,... | collective-permute-start | bytes 5505032 | tf_op jit(solution)/shard_map/ppermute | solution.py:108
  41.3 46.5 %collective-permute-done.6.near = bf16[3,800,256]{2,1,0:T(8,128)(2,1)} collective-permute-done((bf16[3,800,256]{2,1,0:T(8,128)(2,1)}, bf16[3,800,256]{2,1,0:T(8,128)(2,1)}, u32[]{:S(2)}, u32[]{:S(2)}) %collective-permute-start.6) | collective-permute-done | bytes 1228832 | tf_op jit(solution)/shard_map/ppermute | solution.py:108
  87.9 3.4 %collective-permute-done.7.far = bf16[3,800,256]{2,1,0:T(8,128)(2,1)} collective-permute-done((bf16[3,800,256]{2,1,0:T(8,128)(2,1)}, bf16[3,800,256]{2,1,0:T(8,128)(2,1)}, u32[]{:S(2)}, u32[]{:S(2)}) %collective-permute-start.7) | collective-permute-done | bytes 1228832 | tf_op jit(solution)/shard_map/ppermute | solution.py:108
  91.3 3.8 %collective-permute-done.11 = bf16[2,208,1024]{2,1,0:T(8,128)(2,1)S(1)} collective-permute-done((bf16[2,208,1024]{2,1,0:T(8,128)(2,1)S(1)}, bf16[2,208,1024]{2,1,0:T(8,128)(2,1)S(1)}, u32[]{:S(2)}, u32[]{:S(2)}) %collective-permute-start.11) | collective-permute-done | bytes 852000 | tf_op jit(solution)/shard_map/ppermute | solution.py:108
  103.4 9.4 %early.1.acc = f32[4,3,256,256]{3,2,1,0:T(8,128)} custom-call(s32[3]{0:T(128)} %pad_add_fusion.1.place, bf16[4,256,896]{2,1,0:T(8,128)(2,1)} %norm.1.xa, bf16[4,256,896]{2,1,0:T(8,128)(2,1)} %collective-permute-done.8.xb, bf16[4,256,896]{2,1,0:T(8,128)(2,1)} %collective-permute-done.9.xc, bf16[4,256,896]{2,1,0:T(8,128)(2,1)} %copy-done.4, ...), custom_call_target="tpu_custom_call" | custom-call | flops 7549747200 | bytes 8601600 | tf_op jit(solution)/shard_map/early/pallas_call | solution.py:217
  112.9 7.9 %collective-permute-done.15 = bf16[2,208,1024]{2,1,0:T(8,128)(2,1)} collective-permute-done((bf16[2,208,1024]{2,1,0:T(8,128)(2,1)}, bf16[2,208,1024]{2,1,0:T(8,128)(2,1)}, u32[]{:S(2)}, u32[]{:S(2)}) %collective-permute-start.15) | collective-permute-done | bytes 852000 | tf_op jit(solution)/shard_map/ppermute | solution.py:108
  120.7 7.9 %collective-permute-done.13.last = bf16[3,800,256]{2,1,0:T(8,128)(2,1)} collective-permute-done((bf16[3,800,256]{2,1,0:T(8,128)(2,1)}, bf16[3,800,256]{2,1,0:T(8,128)(2,1)}, u32[]{:S(2)}, u32[]{:S(2)}) %collective-permute-start.13) | collective-permute-done | bytes 1228832 | tf_op jit(solution)/shard_map/ppermute | solution.py:108
  128.6 7.4 %late.1 = (f32[1024,256]{1,0:T(8,128)}, bf16[1024,256]{1,0:T(8,128)(2,1)}, bf16[1024,256]{1,0:T(8,128)(2,1)}, f32[2,1024]{1,0:T(2,128)}, bf16[2,512,256]{2,1,0:T(8,128)(2,1)}, /*index=5*/bf16[2,512,256]{2,1,0:T(8,128)(2,1)}) custom-call(s32[3]{0:T(128)} %pad_add_fusion.1.place, bf16[4,256,896]{2,1,0:T(8,128)(2,1)} %norm.1.xa, ...), custom_call_target="tpu_custom_call" | custom-call | flops 1258291200 | bytes 2867200 | tf_op jit(solution)/shard_map/late/pallas_call | solution.py:289
  139.8 1.7 collective-permute-done.20
  147.6 1.8 collective-permute-start.24
  149.4 3.1 %collective-permute-done.22.near = f32[2,1024]{1,0:T(2,128)S(1)} collective-permute-done((f32[2,1024]{1,0:T(2,128)S(1)}, f32[2,1024]{1,0:T(2,128)S(1)}, u32[]{:S(2)}, u32[]{:S(2)}) %collective-permute-start.22) | collective-permute-done | bytes 8224 | tf_op jit(solution)/shard_map/ppermute | solution.py:108
  153.5 9.1 %attend.1 = (bf16[256,256]{1,0:T(8,128)(2,1)}, bf16[256,256]{1,0:T(8,128)(2,1)}, bf16[256,256]{1,0:T(8,128)(2,1)}, bf16[256,256]{1,0:T(8,128)(2,1)}) custom-call(s32[3]{0:T(128)} %pad_add_fusion.1.place, s32[4,2]{1,0:T(4,128)} %pad_add_fusion.spans, f32[1024,256]{1,0:T(8,128)} %get-tuple-element.62.query, bf16[1024,256]{1,0:T(8,128)(2,1)} %get-tuple-element.63.keys, ...), custom_call_target="tpu_custom_call" | custom-call | flops 21474836480 | bytes 3145728 | tf_op jit(solution)/shard_map/attend/pallas_call | solution.py:408
  165.2 1.6 collective-permute-start.27
  166.9 2.1 %collective-permute-start.30 = (bf16[256,256]{1,0:T(8,128)(2,1)}, bf16[256,256]{1,0:T(8,128)(2,1)S(1)}, u32[]{:S(2)}, u32[]{:S(2)}) collective-permute-start(bf16[256,256]{1,0:T(8,128)(2,1)} %get-tuple-element.73), channel_id=1, source_target_pairs={{0,5},{1,4},{2,7},{3,6},{4,1},{5,0},{6,3},{7,2},{8,13},{9,12},{10,... | collective-permute-start | bytes 393224 | tf_op jit(solution)/shard_map/ppermute | solution.py:108
  170.0 3.1 %collective-permute-start.31 = (bf16[256,256]{1,0:T(8,128)(2,1)}, bf16[256,256]{1,0:T(8,128)(2,1)S(1)}, u32[]{:S(2)}, u32[]{:S(2)}) collective-permute-start(bf16[256,256]{1,0:T(8,128)(2,1)} %get-tuple-element.76), channel_id=1, source_target_pairs={{0,2},{1,3},{2,0},{3,1},{4,6},{5,7},{6,4},{7,5},{8,10},{9,11},{10,... | collective-permute-start | bytes 393224 | tf_op jit(solution)/shard_map/ppermute | solution.py:108
  175.4 3.0 %collective-permute-done.29.c11 = bf16[256,256]{1,0:T(8,128)(2,1)S(1)} collective-permute-done((bf16[256,256]{1,0:T(8,128)(2,1)}, bf16[256,256]{1,0:T(8,128)(2,1)S(1)}, u32[]{:S(2)}, u32[]{:S(2)}) %collective-permute-start.29) | collective-permute-done | bytes 131104 | tf_op jit(solution)/shard_map/ppermute | solution.py:108
  179.1 8.9 %output.1 = bf16[1600,256]{1,0:T(8,128)(2,1)} custom-call(s32[3]{0:T(128)} %pad_add_fusion.1.place, bf16[256,256]{1,0:T(8,128)(2,1)} %copy-done.9, bf16[256,256]{1,0:T(8,128)(2,1)} %copy-done.10, bf16[256,256]{1,0:T(8,128)(2,1)} %copy-done.11, bf16[256,256]{1,0:T(8,128)(2,1)} %copy-done.12, bf16[256,256]{1,0:T(8,128)(2,1)} %copy-done.14, ...), custom_call_target="tpu_custom_call" | custom-call | flops 1677721600 | bytes 6553600 | tf_op jit(solution)/shard_map/output/pallas_call | solution.py:472
  (120 shorter events, 39.3 us)
Async XLA Ops:
  2.0 17.8 %collective-permute-start = (bf16[208,1024]{1,0:T(8,128)(2,1)S(1)}, bf16[208,1024]{1,0:T(8,128)(2,1)S(1)}, u32[]{:S(2)}, u32[]{:S(2)}) collective-permute-start(bf16[208,1024]{1,0:T(8,128)(2,1)S(1)} %get-tuple-element.98), channel_id=1, source_target_pairs={{0,8},{1,9},{2,10},{3,11},{4,12},{5,13},{6,14},{7,15},{8,0},{9,1},... | collective-permute-start | bytes 1277960 | tf_op jit(solution)/shard_map/ppermute | solution.py:108
  2.0 20.9 %collective-permute-start.1 = (bf16[208,1024]{1,0:T(8,128)(2,1)S(1)}, bf16[208,1024]{1,0:T(8,128)(2,1)S(1)}, u32[]{:S(2)}, u32[]{:S(2)}) collective-permute-start(bf16[208,1024]{1,0:T(8,128)(2,1)S(1)} %get-tuple-element.98), channel_id=1, source_target_pairs={{0,16},{1,17},{2,18},{3,19},{4,20},{5,21},{6,22},{7,23},{8,24},{9,... | collective-permute-start | bytes 1277960 | tf_op jit(solution)/shard_map/ppermute | solution.py:108
  5.5 17.4 %collective-permute-start.3 = (bf16[3,200,256]{2,1,0:T(8,128)(2,1)}, bf16[3,200,256]{2,1,0:T(8,128)(2,1)}, u32[]{:S(2)}, u32[]{:S(2)}) collective-permute-start(bf16[3,200,256]{2,1,0:T(8,128)(2,1)} %get-tuple-element.93), channel_id=1, source_target_pairs={{0,6},{1,7},{2,4},{3,5},{4,2},{5,3},{6,0},{7,1},{8,14},{9,15},{10,... | collective-permute-start | bytes 921608 | tf_op jit(solution)/shard_map/ppermute | solution.py:108
  7.8 15.1 %collective-permute-start.4 = (bf16[3,200,256]{2,1,0:T(8,128)(2,1)}, bf16[3,200,256]{2,1,0:T(8,128)(2,1)}, u32[]{:S(2)}, u32[]{:S(2)}) collective-permute-start(bf16[3,200,256]{2,1,0:T(8,128)(2,1)} %get-tuple-element.94), channel_id=1, source_target_pairs={{0,4},{1,5},{2,6},{3,7},{4,0},{5,1},{6,2},{7,3},{8,12},{9,13},{10,... | collective-permute-start | bytes 921608 | tf_op jit(solution)/shard_map/ppermute | solution.py:108
  8.1 14.8 %collective-permute-start.5 = (bf16[3,200,256]{2,1,0:T(8,128)(2,1)}, bf16[3,200,256]{2,1,0:T(8,128)(2,1)}, u32[]{:S(2)}, u32[]{:S(2)}) collective-permute-start(bf16[3,200,256]{2,1,0:T(8,128)(2,1)} %get-tuple-element.95), channel_id=1, source_target_pairs={{0,2},{1,3},{2,0},{3,1},{4,6},{5,7},{6,4},{7,5},{8,10},{9,11},{10,... | collective-permute-start | bytes 921608 | tf_op jit(solution)/shard_map/ppermute | solution.py:108
  22.9 9.7 %collective-permute-start.2 = (bf16[208,1024]{1,0:T(8,128)(2,1)S(1)}, bf16[208,1024]{1,0:T(8,128)(2,1)S(1)}, u32[]{:S(2)}, u32[]{:S(2)}) collective-permute-start(bf16[208,1024]{1,0:T(8,128)(2,1)S(1)} %collective-permute-done.1), channel_id=1, source_target_pairs={{0,8},{1,9},{2,10},{3,11},{4,12},{5,13},{6,14},{7,15},{8,0},{9,1},... | collective-permute-start | bytes 1277960 | tf_op jit(solution)/shard_map/ppermute | solution.py:108
  35.1 56.1 %collective-permute-start.9 = (bf16[4,256,896]{2,1,0:T(8,128)(2,1)S(1)}, bf16[4,256,896]{2,1,0:T(8,128)(2,1)}, u32[]{:S(2)}, u32[]{:S(2)}) collective-permute-start(bf16[4,256,896]{2,1,0:T(8,128)(2,1)S(1)} %copy-done), channel_id=1, source_target_pairs={{0,4},{1,5},{2,6},{3,7},{4,0},{5,1},{6,2},{7,3},{8,12},{9,13},{10,... | collective-permute-start | bytes 5505032 | tf_op jit(solution)/shard_map/ppermute | solution.py:108
  36.3 51.5 %collective-permute-start.6 = (bf16[3,800,256]{2,1,0:T(8,128)(2,1)}, bf16[3,800,256]{2,1,0:T(8,128)(2,1)}, u32[]{:S(2)}, u32[]{:S(2)}) collective-permute-start(bf16[3,800,256]{2,1,0:T(8,128)(2,1)} %pad_maximum_fusion.2.own), channel_id=1, source_target_pairs={{0,8},{1,9},{2,10},{3,11},{4,12},{5,13},{6,14},{7,15},{8,0},{9,1},... | collective-permute-start | bytes 3686408 | tf_op jit(solution)/shard_map/ppermute | solution.py:108
  36.3 54.9 %collective-permute-start.7 = (bf16[3,800,256]{2,1,0:T(8,128)(2,1)}, bf16[3,800,256]{2,1,0:T(8,128)(2,1)}, u32[]{:S(2)}, u32[]{:S(2)}) collective-permute-start(bf16[3,800,256]{2,1,0:T(8,128)(2,1)} %pad_maximum_fusion.2.own), channel_id=1, source_target_pairs={{0,16},{1,17},{2,18},{3,19},{4,20},{5,21},{6,22},{7,23},{8,24},{9,... | collective-permute-start | bytes 3686408 | tf_op jit(solution)/shard_map/ppermute | solution.py:108
  38.8 52.4 %collective-permute-start.10 = (bf16[2,208,1024]{2,1,0:T(8,128)(2,1)S(1)}, bf16[2,208,1024]{2,1,0:T(8,128)(2,1)}, u32[]{:S(2)}, u32[]{:S(2)}) collective-permute-start(bf16[2,208,1024]{2,1,0:T(8,128)(2,1)S(1)} %get-tuple-element.92), channel_id=1, source_target_pairs={{0,1},{1,0},{2,3},{3,2},{4,5},{5,4},{6,7},{7,6},{8,9},{9,8},{10,11... | collective-permute-start | bytes 2555912 | tf_op jit(solution)/shard_map/ppermute | solution.py:108
  40.1 54.9 %collective-permute-start.11 = (bf16[2,208,1024]{2,1,0:T(8,128)(2,1)S(1)}, bf16[2,208,1024]{2,1,0:T(8,128)(2,1)S(1)}, u32[]{:S(2)}, u32[]{:S(2)}) collective-permute-start(bf16[2,208,1024]{2,1,0:T(8,128)(2,1)S(1)} %get-tuple-element.91), channel_id=1, source_target_pairs={{0,4},{1,5},{2,6},{3,7},{4,0},{5,1},{6,2},{7,3},{8,12},{9,13},{10,... | collective-permute-start | bytes 2555912 | tf_op jit(solution)/shard_map/ppermute | solution.py:108
  97.4 31.2 %collective-permute-start.14 = (bf16[2,2,208,1024]{3,2,1,0:T(8,128)(2,1)S(1)}, bf16[2,2,208,1024]{3,2,1,0:T(8,128)(2,1)}, u32[]{:S(2)}, u32[]{:S(2)}) collective-permute-start(bf16[2,2,208,1024]{3,2,1,0:T(8,128)(2,1)S(1)} %pad_maximum_fusion.wa), channel_id=1, source_target_pairs={{0,2},{1,3},{2,0},{3,1},{4,6},{5,7},{6,4},{7,5},{8,10},{9,11},{10,... | collective-permute-start | bytes 5111816 | tf_op jit(solution)/shard_map/ppermute | solution.py:108
  99.7 29.0 %collective-permute-start.13 = (bf16[3,800,256]{2,1,0:T(8,128)(2,1)}, bf16[3,800,256]{2,1,0:T(8,128)(2,1)}, u32[]{:S(2)}, u32[]{:S(2)}) collective-permute-start(bf16[3,800,256]{2,1,0:T(8,128)(2,1)} %collective-permute-done.7.far), channel_id=1, source_target_pairs={{0,8},{1,9},{2,10},{3,11},{4,12},{5,13},{6,14},{7,15},{8,0},{9,1},... | collective-permute-start | bytes 3686408 | tf_op jit(solution)/shard_map/ppermute | solution.py:108
  100.2 20.6 %collective-permute-start.15 = (bf16[2,208,1024]{2,1,0:T(8,128)(2,1)}, bf16[2,208,1024]{2,1,0:T(8,128)(2,1)}, u32[]{:S(2)}, u32[]{:S(2)}) collective-permute-start(bf16[2,208,1024]{2,1,0:T(8,128)(2,1)} %collective-permute-done.10), channel_id=1, source_target_pairs={{0,4},{1,5},{2,6},{3,7},{4,0},{5,1},{6,2},{7,3},{8,12},{9,13},{10,... | collective-permute-start | bytes 2555912 | tf_op jit(solution)/shard_map/ppermute | solution.py:108
  138.7 13.8 %collective-permute-start.16 = (bf16[2,512,256]{2,1,0:T(8,128)(2,1)}, bf16[2,512,256]{2,1,0:T(8,128)(2,1)S(1)}, u32[]{:S(2)}, u32[]{:S(2)}) collective-permute-start(bf16[2,512,256]{2,1,0:T(8,128)(2,1)} %get-tuple-element.65), channel_id=1, source_target_pairs={{0,8},{1,9},{2,10},{3,11},{4,12},{5,13},{6,14},{7,15},{8,0},{9,1},... | collective-permute-start | bytes 1572872 | tf_op jit(solution)/shard_map/ppermute | solution.py:108
  138.7 13.8 %collective-permute-start.17 = (bf16[2,512,256]{2,1,0:T(8,128)(2,1)}, bf16[2,512,256]{2,1,0:T(8,128)(2,1)S(1)}, u32[]{:S(2)}, u32[]{:S(2)}) collective-permute-start(bf16[2,512,256]{2,1,0:T(8,128)(2,1)} %get-tuple-element.66), channel_id=1, source_target_pairs={{0,2},{1,3},{2,0},{3,1},{4,6},{5,7},{6,4},{7,5},{8,16},{9,17},{10,... | collective-permute-start | bytes 1572872 | tf_op jit(solution)/shard_map/ppermute | solution.py:108
  145.1 7.4 %collective-permute-start.22 = (f32[2,1024]{1,0:T(2,128)S(1)}, f32[2,1024]{1,0:T(2,128)S(1)}, u32[]{:S(2)}, u32[]{:S(2)}) collective-permute-start(f32[2,1024]{1,0:T(2,128)S(1)} %add.111.mine), channel_id=1, source_target_pairs={{0,8},{1,9},{2,10},{3,11},{4,12},{5,13},{6,14},{7,15},{8,0},{9,1},... | collective-permute-start | bytes 24584 | tf_op jit(solution)/shard_map/ppermute | solution.py:108
  145.2 7.3 %collective-permute-start.23 = (f32[2,1024]{1,0:T(2,128)S(1)}, f32[2,1024]{1,0:T(2,128)S(1)}, u32[]{:S(2)}, u32[]{:S(2)}) collective-permute-start(f32[2,1024]{1,0:T(2,128)S(1)} %add.111.mine), channel_id=1, source_target_pairs={{0,2},{1,3},{2,0},{3,1},{4,6},{5,7},{6,4},{7,5},{8,16},{9,17},{10,... | collective-permute-start | bytes 24584 | tf_op jit(solution)/shard_map/ppermute | solution.py:108
  147.6 15.1 %collective-permute-start.24 = (bf16[2,2,208,1024]{3,2,1,0:T(8,128)(2,1)S(1)}, bf16[2,2,208,1024]{3,2,1,0:T(8,128)(2,1)}, u32[]{:S(2)}, u32[]{:S(2)}) collective-permute-start(bf16[2,2,208,1024]{3,2,1,0:T(8,128)(2,1)S(1)} %pad_maximum_fusion.1.wc), channel_id=1, source_target_pairs={{0,2},{1,3},{2,0},{3,1},{4,6},{5,7},{6,4},{7,5},{8,10},{9,11},{10,... | collective-permute-start | bytes 5111816 | tf_op jit(solution)/shard_map/ppermute | solution.py:108
  165.2 10.2 %collective-permute-start.27 = (bf16[256,256]{1,0:T(8,128)(2,1)}, bf16[256,256]{1,0:T(8,128)(2,1)S(1)}, u32[]{:S(2)}, u32[]{:S(2)}) collective-permute-start(bf16[256,256]{1,0:T(8,128)(2,1)} %get-tuple-element.75), channel_id=1, source_target_pairs={{0,7},{1,6},{2,5},{3,4},{4,3},{5,2},{6,1},{7,0},{8,15},{9,14},{10,... | collective-permute-start | bytes 393224 | tf_op jit(solution)/shard_map/ppermute | solution.py:108
  166.8 8.6 %collective-permute-start.28 = (bf16[256,256]{1,0:T(8,128)(2,1)}, bf16[256,256]{1,0:T(8,128)(2,1)S(1)}, u32[]{:S(2)}, u32[]{:S(2)}) collective-permute-start(bf16[256,256]{1,0:T(8,128)(2,1)} %get-tuple-element.75), channel_id=1, source_target_pairs={{0,6},{1,7},{2,4},{3,5},{4,2},{5,3},{6,0},{7,1},{8,14},{9,15},{10,... | collective-permute-start | bytes 393224 | tf_op jit(solution)/shard_map/ppermute | solution.py:108
  166.9 11.5 %collective-permute-start.30 = (bf16[256,256]{1,0:T(8,128)(2,1)}, bf16[256,256]{1,0:T(8,128)(2,1)S(1)}, u32[]{:S(2)}, u32[]{:S(2)}) collective-permute-start(bf16[256,256]{1,0:T(8,128)(2,1)} %get-tuple-element.73), channel_id=1, source_target_pairs={{0,5},{1,4},{2,7},{3,6},{4,1},{5,0},{6,3},{7,2},{8,13},{9,12},{10,... | collective-permute-start | bytes 393224 | tf_op jit(solution)/shard_map/ppermute | solution.py:108
  169.0 9.4 %collective-permute-start.29 = (bf16[256,256]{1,0:T(8,128)(2,1)}, bf16[256,256]{1,0:T(8,128)(2,1)S(1)}, u32[]{:S(2)}, u32[]{:S(2)}) collective-permute-start(bf16[256,256]{1,0:T(8,128)(2,1)} %get-tuple-element.76), channel_id=1, source_target_pairs={{0,3},{1,2},{2,1},{3,0},{4,7},{5,6},{6,5},{7,4},{8,11},{9,10},{10,... | collective-permute-start | bytes 393224 | tf_op jit(solution)/shard_map/ppermute | solution.py:108
  170.0 8.4 %collective-permute-start.31 = (bf16[256,256]{1,0:T(8,128)(2,1)}, bf16[256,256]{1,0:T(8,128)(2,1)S(1)}, u32[]{:S(2)}, u32[]{:S(2)}) collective-permute-start(bf16[256,256]{1,0:T(8,128)(2,1)} %get-tuple-element.76), channel_id=1, source_target_pairs={{0,2},{1,3},{2,0},{3,1},{4,6},{5,7},{6,4},{7,5},{8,10},{9,11},{10,... | collective-permute-start | bytes 393224 | tf_op jit(solution)/shard_map/ppermute | solution.py:108
  (31 other events, 249.3 us)

commit v14 on v13

--- a/solution.py
+++ b/solution.py
@@ -97,6 +97,7 @@
 SMEM = pl.BlockSpec(memory_space=pltpu.SMEM)
 HBM = pl.BlockSpec(memory_space=pltpu.HBM)
 KERNEL_VMEM = 60 * 1024 * 1024
+HELD_VMEM = 24 * 1024 * 1024
 
 
 def permuted(x, to):
@@ -186,7 +187,7 @@
 
 
 def early_kernel(
-    place, xa, xb, xc, xd, own, near, far, acc, x_all, w_all, held, x_sem, w_sem, sems,
+    place, xa, xb, xc, xd, own, near, far, acc, x_last, x_all, w_all, x_sem, w_sem, last_sem,
 ):
     z = place[0]
     kinds, rows = own.shape[:2]
@@ -196,19 +197,17 @@
         copies.append([pltpu.make_async_copy(w, dst, w_sem.at[i])])
         copies[i] += token_copies((xa, xb, xc, xd), z ^ i, x_all.at[i], x_sem.at[i])
         start(copies[i])
+    last_copies = token_copies((xa, xb, xc, xd), z ^ 3, x_last, last_sem)
+    start(last_copies)
     blank_tail(w_all, rows)
-    stores = []
     for step in range(3):
         wait(copies[step])
         for r in range(SLAB):
             x = x_all[step, r]
             for kind in range(kinds):
                 term = jnp.dot(x, w_all[step, kind], preferred_element_type=jnp.float32)
-                held[r, kind] = term if step == 0 else held[r, kind] + term
-            if step == 2:
-                stores.append(pltpu.make_async_copy(held.at[r], acc.at[r], sems.at[r]))
-                stores[-1].start()
-    wait(stores)
+                acc[r, kind] = term if step == 0 else acc[r, kind] + term
+    wait(last_copies)
 
 
 def early(place, xs, own, near, far):
@@ -216,18 +215,20 @@
     slabs, count, wide = xs[0].shape
     return pl.pallas_call(
         early_kernel,
-        out_shape=jax.ShapeDtypeStruct((SLAB, kinds, count, width), jnp.float32),
+        out_shape=(
+            jax.ShapeDtypeStruct((SLAB, kinds, count, width), jnp.float32),
+            jax.ShapeDtypeStruct((SLAB, count, wide), jnp.bfloat16),
+        ),
         in_specs=[SMEM] + [HBM] * 7,
-        out_specs=HBM,
+        out_specs=(VMEM, VMEM),
         scratch_shapes=[
             pltpu.VMEM((3, SLAB, count, wide), jnp.bfloat16),
             pltpu.VMEM((3, kinds, wide, width), jnp.bfloat16),
-            pltpu.VMEM((SLAB, kinds, count, width), jnp.float32),
             pltpu.SemaphoreType.DMA((3, SLAB)),
             pltpu.SemaphoreType.DMA((3,)),
             pltpu.SemaphoreType.DMA((SLAB,)),
         ],
-        compiler_params=pltpu.CompilerParams(vmem_limit_bytes=KERNEL_VMEM),
+        compiler_params=pltpu.CompilerParams(vmem_limit_bytes=HELD_VMEM),
         cost_estimate=pl.CostEstimate(
             flops=12 * kinds * SLAB * count * rows * width,
             bytes_accessed=6 * kinds * rows * width + 6 * SLAB * count * rows,
@@ -238,30 +239,21 @@
 
 
 def late_kernel(
-    place, xa, xb, xc, xd, acc, last, q_gain, k_gain,
-    query, keys, values, squares, even, odd,
-    x_all, w_all, held, q_all, k_all, v_all, x_sem, w_sem, acc_sem, sems,
+    place, x_last, acc, last, q_gain, k_gain, query, keys, values, squares, even, odd,
+    w_all, q_all, k_all, v_all, sems,
 ):
     z, q = place[0], place[1]
     rows = last.shape[1]
-    w_copy = pltpu.make_async_copy(last, w_all.at[:, pl.ds(0, rows), :], w_sem)
-    w_copy.start()
-    copies = token_copies((xa, xb, xc, xd), z ^ 3, x_all, x_sem)
-    loads = [pltpu.make_async_copy(acc.at[r], held.at[r], acc_sem.at[r]) for r in range(SLAB)]
+    w_all[:, :rows, :] = last[...]
+    blank_tail(w_all, rows)
+    count = acc.shape[2]
+    stores = []
     for r in range(SLAB):
-        copies[r].start()
-        loads[r].start()
-    count = held.shape[2]
-    stores = []
-    blank_tail(w_all, rows)
-    w_copy.wait()
-    for r in range(SLAB):
-        copies[r].wait()
-        loads[r].wait()
-        x = x_all[r]
         rows = pl.ds(pl.multiple_of((q ^ r) * count, count), count)
         for kind in range(3):
-            part = held[r, kind] + jnp.dot(x, w_all[kind], preferred_element_type=jnp.float32)
+            part = acc[r, kind] + jnp.dot(
+                x_last[r], w_all[kind], preferred_element_type=jnp.float32
+            )
             if kind < 2:
                 summed = as_row(jnp.sum(part * part, axis=1, keepdims=True))
                 squares[kind:kind + 1, rows] = summed[:1]
@@ -281,9 +273,9 @@
     wait(stores)
 
 
-def late(place, xs, acc, last, q_gain, k_gain):
+def late(place, x_last, acc, last, q_gain, k_gain):
     kinds, rows, width = last.shape
-    count, wide = xs[0].shape[1:]
+    count, wide = x_last.shape[1:]
     slab = SLAB * count
     f32, bf16 = jnp.float32, jnp.bfloat16
     return pl.pallas_call(
@@ -296,28 +288,23 @@
             jax.ShapeDtypeStruct((2, 2 * count, width), bf16),
             jax.ShapeDtypeStruct((2, 2 * count, width), bf16),
         ),
-        in_specs=[SMEM] + [HBM] * 6 + [VMEM] * 2,
+        in_specs=[SMEM] + [VMEM] * 5,
         out_specs=(HBM, HBM, HBM, VMEM, HBM, HBM),
         scratch_shapes=[
-            pltpu.VMEM((SLAB, count, wide), bf16),
             pltpu.VMEM((kinds, wide, width), bf16),
-            pltpu.VMEM((SLAB, kinds, count, width), f32),
             pltpu.VMEM((slab, width), f32),
             pltpu.VMEM((slab, width), bf16),
             pltpu.VMEM((slab, width), bf16),
-            pltpu.SemaphoreType.DMA((SLAB,)),
-            pltpu.SemaphoreType.DMA,
-            pltpu.SemaphoreType.DMA((SLAB,)),
             pltpu.SemaphoreType.DMA((3 * SLAB + 4,)),
         ],
-        compiler_params=pltpu.CompilerParams(vmem_limit_bytes=KERNEL_VMEM),
+        compiler_params=pltpu.CompilerParams(vmem_limit_bytes=HELD_VMEM),
         cost_estimate=pl.CostEstimate(
             flops=2 * kinds * slab * rows * width,
             bytes_accessed=2 * kinds * rows * width + 2 * slab * rows,
             transcendentals=0,
         ),
         name="late",
-    )(place, *xs, acc, last, q_gain, k_gain)
+    )(place, x_last, acc, last, q_gain, k_gain)
 
 
 def attend_kernel(
@@ -418,7 +405,7 @@
             pltpu.VMEM((2, ext), jnp.float32),
             pltpu.SemaphoreType.DMA((7,)),
         ],
-        compiler_params=pltpu.CompilerParams(vmem_limit_bytes=KERNEL_VMEM),
+        compiler_params=pltpu.CompilerParams(vmem_limit_bytes=HELD_VMEM),
         cost_estimate=pl.CostEstimate(
             flops=64 * SLAB * count * window * width,
             bytes_accessed=4 * ext * width + 4 * slab * width,
@@ -429,7 +416,7 @@
 
 
 def out_kernel(
-    place, c20, c01, c31, c30, c11, c21, c10, c00, wa, wb, wc, wd,
+    place, c20, c01, c31, c30, c11, c21, c10, c00, wa0, wb0, wc0, wd0, wa1, wb1, wc1, wd1,
     residual, scale, out, c_all, w_all, total, placed, c_sem, w_sem,
 ):
     z, q = place[0], place[1]
@@ -441,13 +428,13 @@
             dst = c_all.at[i, pl.ds(at, width), :]
             c_copies.append(pltpu.make_async_copy(pair[i], dst, c_sem.at[r, i]))
     start(c_copies)
-    rows = wa.shape[2]
+    rows = wa0.shape[1]
     w_copies = []
     for i in range(2):
-        for r, w in enumerate((wa, wb, wc, wd)):
+        for r, w in enumerate(((wa0, wb0, wc0, wd0), (wa1, wb1, wc1, wd1))[i]):
             for j in range(2):
                 dst = w_all.at[i, pl.ds((2 * r + j) * rows, rows), :]
-                w_copies.append(pltpu.make_async_copy(w.at[i, j], dst, w_sem.at[r, j, i]))
+                w_copies.append(pltpu.make_async_copy(w.at[j], dst, w_sem.at[r, j, i]))
     start(w_copies)
     column = as_column(scale[...])[:out.shape[0]]
     column = jnp.tile(column, (1, out.shape[1] // 128))
@@ -466,13 +453,13 @@
 
 def output(place, blocks, pieces, residual, scale):
     count = blocks[0].shape[1]
-    rows, depth = pieces[0].shape[2:]
+    rows, depth = pieces[0].shape[1:]
     share = residual.shape[0]
     scale = jnp.pad(scale, (0, -share % 128))[None]
     return pl.pallas_call(
         out_kernel,
         out_shape=jax.ShapeDtypeStruct((share, count), jnp.bfloat16),
-        in_specs=[SMEM] + [HBM] * 12 + [VMEM] * 2,
+        in_specs=[SMEM] + [HBM] * 16 + [VMEM] * 2,
         out_specs=VMEM,
         scratch_shapes=[
             pltpu.VMEM((2, depth, count), jnp.bfloat16),
@@ -482,7 +469,7 @@
             pltpu.SemaphoreType.DMA((SLAB, 2)),
             pltpu.SemaphoreType.DMA((SLAB, 2, 2)),
         ],
-        compiler_params=pltpu.CompilerParams(vmem_limit_bytes=KERNEL_VMEM),
+        compiler_params=pltpu.CompilerParams(vmem_limit_bytes=HELD_VMEM),
         cost_estimate=pl.CostEstimate(
             flops=4 * share * count * depth,
             bytes_accessed=4 * share * depth,
@@ -522,7 +509,12 @@
     out_near, out_far = even_pair(out_own), half_pair(out_own)
     gains = [lax.dynamic_slice_in_dim(g, q * width, width, 0)[None] for g in (q_gain, k_gain)]
 
-    x0, out_near, out_far, *gains = tied(x0, out_near, out_far, *gains)
+    outside = jnp.full((half,), -1, jnp.int32)
+    seg = jnp.concatenate([outside, segment_ids, outside], axis=0)
+    seg = lax.dynamic_slice_in_dim(seg, z * slab, slab + 2 * half, 0)
+    spans = key_spans(seg, slab, count, half)
+    seg = seg.astype(jnp.float32)[None]
+    x0, out_near, out_far, seg, spans, *gains = tied(x0, out_near, out_far, seg, spans, *gains)
     out_last = even_pair(out_far)
     x2 = in_slab(x0, 2)
     out_last, own, x0 = tied(out_last, own, x0)
@@ -535,32 +527,25 @@
     keep_x = in_slab(keep, 2)
     near, far, x1, x2, got, keep_x = tied(near, far, x1, x2, got, keep_x)
     last = even_pair(far)
-    x3, got_x = in_slab(x2, 1), in_slab(got, 2)
-    wa = jnp.stack([keep, got])
-    wb = in_slab(wa, 1)
+    x3 = in_slab(x2, 1)
+    got_x, got_c, keep_c = in_slab(got, 2), in_slab(got, 1), in_slab(keep, 1)
+    keep_xc = in_slab(tied(keep_x, x3)[0], 1)
     xs = (x0, x1, x2, x3)
-    acc = early(place, xs, own, near, far)
-    last, acc, wb, got_x = tied(last, acc, wb, got_x)
-    wc = jnp.stack([keep_x, got_x])
-
-    query, keys, values, squares, even, odd = late(place, xs, acc, last, *gains)
+    acc, x_last = early(place, xs, own, near, far)
+    last, acc, x_last = tied(last, acc, x_last)
+    query, keys, values, squares, even, odd = late(place, x_last, acc, last, *gains)
     even, odd = even_pair(even), odd_pair(odd)
+    squares, got_x, got_c, keep_c, keep_xc = tied(squares, got_x, got_c, keep_c, keep_xc)
     sums = squares
     for r in range(1, SLAB):
         sums = sums + in_slab(squares, r)
     sums = sums + across(sums)
     sums = (sums, even_pair(sums), odd_pair(sums))
-    query, wc = tied(query, wc)
-    wd = in_slab(wc, 1)
-
-    outside = jnp.full((half,), -1, jnp.int32)
-    seg = jnp.concatenate([outside, segment_ids, outside], axis=0)
-    seg = lax.dynamic_slice_in_dim(seg, z * slab, slab + 2 * half, 0)
-    spans = key_spans(seg, slab, count, half)
-    seg = seg.astype(jnp.float32)[None]
+    got_xc = in_slab(got_x, 1)
+
     blocks = attend(full_width, place, spans, query, keys, values, even, odd, sums, seg)
-    *blocks, wd = tied(*blocks, wd)
-    pieces = (wa, wb, wc, wd)
+    *blocks, got_xc = tied(*blocks, got_xc)
+    pieces = (keep, keep_c, keep_x, keep_xc, got, got_c, got_x, got_xc)
     spread = []
     for r, i in ((2, 0), (0, 1), (3, 1), (3, 0), (1, 1), (2, 1), (1, 0), (0, 0)):
         to = functools.partial(lambda r, i, z, q, y: (z, q ^ r, y ^ i), r, i)

time: 189 us -> 190 us (level)
  local copies, waits for them, and re-layouts: 12 us -> 18.2 us
  other arithmetic: 9.14 us -> 5.22 us
    unnamed x47, local copies, waits for them, and re-layouts: 4.36 us -> 11.4 us
    another operation x2 -> x0, other arithmetic: 2.63 us -> none  [the longest x1 1.31 us: slab_plan(): wa = jnp.stack([keep, got])]
    dynamic_slice x1, local copies, waits for them, and re-layouts: 0.33 us -> 2.44 us  [slab_plan(): lax.dynamic_slice_in_dim(tokens, tp * share, share, 1)]
    pallas_call x1, Pallas kernels: 9.14 us -> 7.05 us  [attend(): pl.pallas_call(functools.partial(attend_kernel, full_width), out_shape=(j...]
    ppermute x32 -> x34, starting transfers between devices: 34.3 us -> 33 us  [permuted(): return lax.ppermute(x, ('seq', 'tp'), pairs)]
    ppermute x32 -> x34, waiting for transfers between devices: 93.9 us -> 93.8 us  [permuted(): return lax.ppermute(x, ('seq', 'tp'), pairs)]
  transfers between devices with their start and end apart: 32 -> 34, of which waited for: 13 -> 17; matrix products, arithmetic and copies ran while one was open for 9% -> 7% of each run, Pallas kernels for 12% -> 14%
where the time goes in v14:
time: 190 us; the launch traced here: 188 us
  waiting for transfers between devices  93.8 us (49%)
  Pallas kernels  37.5 us (20%)
  starting transfers between devices  33 us (17%)
  local copies, waits for them, and re-layouts  18.2 us (10%)
  other arithmetic  5.22 us (3%)
    ppermute x34, waiting for transfers between devices, permuted(): return lax.ppermute(x, ('seq', 'tp'), pairs)  93.8 us
    ppermute x34, starting transfers between devices, permuted(): return lax.ppermute(x, ('seq', 'tp'), pairs)  33 us
    unnamed x47, local copies, waits for them, and re-layouts  11.4 us
    pallas_call x1, Pallas kernels, output(): pl.pallas_call(out_kernel, out_shape=jax.ShapeDtypeStruct((share, count),...  10.4 us
    pallas_call x1, Pallas kernels, early(): pl.pallas_call(early_kernel, out_shape=(jax.ShapeDtypeStruct((SLAB, kinds...  8.45 us
    pallas_call x1, Pallas kernels, late(): pl.pallas_call(late_kernel, out_shape=(jax.ShapeDtypeStruct((slab, width)...  8.09 us
    pallas_call x1, Pallas kernels, attend(): pl.pallas_call(functools.partial(attend_kernel, full_width), out_shape=(j...  7.05 us
  transfers between devices with their start and end apart: 34, of which 17 were waited for; matrix products, arithmetic and copies ran while one was open for 7% of the time, Pallas kernels for 14%

profile of v14, /device:TPU:9, one launch (start us, length us, event | category | flops | bytes accessed | tf_op | source)
XLA Modules:
  0.0 188.3 jit_solution(936583849829737972)
XLA Ops:
  1.3 2.5 %collective-permute-start.1 = (bf16[208,1024]{1,0:T(8,128)(2,1)S(1)}, bf16[208,1024]{1,0:T(8,128)(2,1)}, u32[]{:S(2)}, u32[]{:S(2)}) collective-permute-start(bf16[208,1024]{1,0:T(8,128)(2,1)S(1)} %get-tuple-element.111), channel_id=1, source_target_pairs={{0,16},{1,17},{2,18},{3,19},{4,20},{5,21},{6,22},{7,23},{8,24},{9,... | collective-permute-start | bytes 1277960 | tf_op jit(solution)/shard_map/ppermute | solution.py:109
  3.9 2.4 %collective-permute-start.3 = (bf16[3,200,256]{2,1,0:T(8,128)(2,1)S(1)}, bf16[3,200,256]{2,1,0:T(8,128)(2,1)}, u32[]{:S(2)}, u32[]{:S(2)}) collective-permute-start(bf16[3,200,256]{2,1,0:T(8,128)(2,1)S(1)} %get-tuple-element.107), channel_id=1, source_target_pairs={{0,6},{1,7},{2,4},{3,5},{4,2},{5,3},{6,0},{7,1},{8,14},{9,15},{10,... | collective-permute-start | bytes 921608 | tf_op jit(solution)/shard_map/ppermute | solution.py:109
  10.2 3.6 %norm.1.xa = bf16[4,256,896]{2,1,0:T(8,128)(2,1)} custom-call(bf16[256,3200]{1,0:T(8,128)(2,1)} %tokens.1, f32[1,3200]{1,0:T(1,128)} %broadcast_in_dim.34.gain), custom_call_target="tpu_custom_call" | custom-call | tf_op jit(solution)/shard_map/norm/pallas_call | solution.py:168
  14.5 4.6 %collective-permute-done = bf16[208,1024]{1,0:T(8,128)(2,1)} collective-permute-done((bf16[208,1024]{1,0:T(8,128)(2,1)S(1)}, bf16[208,1024]{1,0:T(8,128)(2,1)}, u32[]{:S(2)}, u32[]{:S(2)}) %collective-permute-start) | collective-permute-done | bytes 426016 | tf_op jit(solution)/shard_map/ppermute | solution.py:109
  19.1 3.2 %collective-permute-done.1 = bf16[208,1024]{1,0:T(8,128)(2,1)} collective-permute-done((bf16[208,1024]{1,0:T(8,128)(2,1)S(1)}, bf16[208,1024]{1,0:T(8,128)(2,1)}, u32[]{:S(2)}, u32[]{:S(2)}) %collective-permute-start.1) | collective-permute-done | bytes 426016 | tf_op jit(solution)/shard_map/ppermute | solution.py:109
  22.3 1.5 fusion.1
  25.0 7.3 %collective-permute-done.2 = bf16[208,1024]{1,0:T(8,128)(2,1)} collective-permute-done((bf16[208,1024]{1,0:T(8,128)(2,1)}, bf16[208,1024]{1,0:T(8,128)(2,1)}, u32[]{:S(2)}, u32[]{:S(2)}) %collective-permute-start.2) | collective-permute-done | bytes 426016 | tf_op jit(solution)/shard_map/ppermute | solution.py:109
  32.3 2.5 %collective-permute-start.8 = (bf16[4,256,896]{2,1,0:T(8,128)(2,1)S(1)}, bf16[4,256,896]{2,1,0:T(8,128)(2,1)}, u32[]{:S(2)}, u32[]{:S(2)}) collective-permute-start(bf16[4,256,896]{2,1,0:T(8,128)(2,1)S(1)} %copy-done), channel_id=1, source_target_pairs={{0,2},{1,3},{2,0},{3,1},{4,6},{5,7},{6,4},{7,5},{8,10},{9,11},{10,... | collective-permute-start | bytes 5505032 | tf_op jit(solution)/shard_map/ppermute | solution.py:109
  42.3 45.3 %collective-permute-done.6.near = bf16[3,800,256]{2,1,0:T(8,128)(2,1)} collective-permute-done((bf16[3,800,256]{2,1,0:T(8,128)(2,1)}, bf16[3,800,256]{2,1,0:T(8,128)(2,1)}, u32[]{:S(2)}, u32[]{:S(2)}) %collective-permute-start.6) | collective-permute-done | bytes 1228832 | tf_op jit(solution)/shard_map/ppermute | solution.py:109
  87.6 3.4 %collective-permute-done.7.far = bf16[3,800,256]{2,1,0:T(8,128)(2,1)} collective-permute-done((bf16[3,800,256]{2,1,0:T(8,128)(2,1)}, bf16[3,800,256]{2,1,0:T(8,128)(2,1)}, u32[]{:S(2)}, u32[]{:S(2)}) %collective-permute-start.7) | collective-permute-done | bytes 1228832 | tf_op jit(solution)/shard_map/ppermute | solution.py:109
  90.9 3.8 %collective-permute-done.11.wc0 = bf16[2,208,1024]{2,1,0:T(8,128)(2,1)S(1)} collective-permute-done((bf16[2,208,1024]{2,1,0:T(8,128)(2,1)S(1)}, bf16[2,208,1024]{2,1,0:T(8,128)(2,1)S(1)}, u32[]{:S(2)}, u32[]{:S(2)}) %collective-permute-start.11) | collective-permute-done | bytes 852000 | tf_op jit(solution)/shard_map/ppermute | solution.py:109
  97.6 1.5 collective-permute-done.13.xd
  99.5 8.4 %early.1 = (f32[4,3,256,256]{3,2,1,0:T(8,128)S(1)}, bf16[4,256,896]{2,1,0:T(8,128)(2,1)S(1)}) custom-call(s32[3]{0:T(128)S(1)} %pad_add_fusion.1.place, bf16[4,256,896]{2,1,0:T(8,128)(2,1)S(1)} %copy-done, bf16[4,256,896]{2,1,0:T(8,128)(2,1)} %collective-permute-done.8.xb, bf16[4,256,896]{2,1,0:T(8,128)(2,1)} %collective-permute-done.9.xc, ...), custom_call_target="tpu_custom_call" | custom-call | flops 7549747200 | bytes 8601600 | tf_op jit(solution)/shard_map/early/pallas_call | solution.py:216
  108.0 16.4 %collective-permute-done.12.last = bf16[3,800,256]{2,1,0:T(8,128)(2,1)S(1)} collective-permute-done((bf16[3,800,256]{2,1,0:T(8,128)(2,1)}, bf16[3,800,256]{2,1,0:T(8,128)(2,1)S(1)}, u32[]{:S(2)}, u32[]{:S(2)}) %collective-permute-start.12) | collective-permute-done | bytes 1228832 | tf_op jit(solution)/shard_map/ppermute | solution.py:109
  124.4 8.1 %late.1 = (f32[1024,256]{1,0:T(8,128)S(1)}, bf16[1024,256]{1,0:T(8,128)(2,1)S(1)}, bf16[1024,256]{1,0:T(8,128)(2,1)S(1)}, f32[2,1024]{1,0:T(2,128)S(1)}, bf16[2,...) custom-call(s32[3]{0:T(128)S(1)} %pad_add_fusion.1.place, bf16[4,256,896]{2,1,0:T(8,128)(2,1)S(1)} %get-tuple-element.64.x_last, ...), custom_call_target="tpu_custom_call" | custom-call | flops 1258291200 | bytes 2867200 | tf_op jit(solution)/shard_map/late/pallas_call | solution.py:281
  137.6 1.8 collective-permute-done.22
  140.7 1.6 collective-permute-done.23
  143.0 1.8 collective-permute-start.26
  145.7 7.0 %attend.1 = (bf16[256,256]{1,0:T(8,128)(2,1)S(1)}, bf16[256,256]{1,0:T(8,128)(2,1)}, bf16[256,256]{1,0:T(8,128)(2,1)}, bf16[256,256]{1,0:T(8,128)(2,1)}) custom-call(s32[3]{0:T(128)S(1)} %pad_add_fusion.1.place, s32[4,2]{1,0:T(4,128)S(1)} %copy-done.18, f32[1024,256]{1,0:T(8,128)S(1)} %get-tuple-element.69.query, ...), custom_call_target="tpu_custom_call" | custom-call | flops 21474836480 | bytes 3145728 | tf_op jit(solution)/shard_map/attend/pallas_call | solution.py:395
  155.8 3.3 %collective-permute-start.29 = (bf16[256,256]{1,0:T(8,128)(2,1)}, bf16[256,256]{1,0:T(8,128)(2,1)}, u32[]{:S(2)}, u32[]{:S(2)}) collective-permute-start(bf16[256,256]{1,0:T(8,128)(2,1)} %get-tuple-element.87), channel_id=1, source_target_pairs={{0,7},{1,6},{2,5},{3,4},{4,3},{5,2},{6,1},{7,0},{8,15},{9,14},{10,... | collective-permute-start | bytes 393224 | tf_op jit(solution)/shard_map/ppermute | solution.py:109
  161.1 1.9 %collective-permute-start.31 = (bf16[256,256]{1,0:T(8,128)(2,1)}, bf16[256,256]{1,0:T(8,128)(2,1)}, u32[]{:S(2)}, u32[]{:S(2)}) collective-permute-start(bf16[256,256]{1,0:T(8,128)(2,1)} %get-tuple-element.88), channel_id=1, source_target_pairs={{0,3},{1,2},{2,1},{3,0},{4,7},{5,6},{6,5},{7,4},{8,11},{9,10},{10,... | collective-permute-start | bytes 393224 | tf_op jit(solution)/shard_map/ppermute | solution.py:109
  164.1 2.4 %constant_dynamic-slice_fusion = bf16[256,1600]{1,0:T(8,128)(2,1)} fusion(bf16[256,3200]{1,0:T(8,128)(2,1)} %tokens.1, s32[]{:T(128)S(6)} %select_n.169), kind=kLoop, calls=%fused_computation.46 | loop fusion | bytes 1638404 | tf_op jit(solution)/shard_map/dynamic_slice | solution.py:555
  166.6 1.5 copy.33
  177.7 10.4 %output.1 = bf16[1600,256]{1,0:T(8,128)(2,1)} custom-call(s32[3]{0:T(128)S(1)} %pad_add_fusion.1.place, bf16[256,256]{1,0:T(8,128)(2,1)S(1)} %copy-done.14, bf16[256,256]{1,0:T(8,128)(2,1)S(1)} %copy-done.16, bf16[256,256]{1,0:T(8,128)(2,1)} %collective-permute-done.29.c31, bf16[256,256]{1,0:T(8,128)(2,1)} %collective-permute-done.30.c30, ...), custom_call_target="tpu_custom_call" | custom-call | flops 1677721600 | bytes 6553600 | tf_op jit(solution)/shard_map/output/pallas_call | solution.py:459
  (121 shorter events, 41.7 us)
Async XLA Ops:
  1.2 17.9 %collective-permute-start = (bf16[208,1024]{1,0:T(8,128)(2,1)S(1)}, bf16[208,1024]{1,0:T(8,128)(2,1)}, u32[]{:S(2)}, u32[]{:S(2)}) collective-permute-start(bf16[208,1024]{1,0:T(8,128)(2,1)S(1)} %get-tuple-element.111), channel_id=1, source_target_pairs={{0,8},{1,9},{2,10},{3,11},{4,12},{5,13},{6,14},{7,15},{8,0},{9,1},... | collective-permute-start | bytes 1277960 | tf_op jit(solution)/shard_map/ppermute | solution.py:109
  1.3 21.0 %collective-permute-start.1 = (bf16[208,1024]{1,0:T(8,128)(2,1)S(1)}, bf16[208,1024]{1,0:T(8,128)(2,1)}, u32[]{:S(2)}, u32[]{:S(2)}) collective-permute-start(bf16[208,1024]{1,0:T(8,128)(2,1)S(1)} %get-tuple-element.111), channel_id=1, source_target_pairs={{0,16},{1,17},{2,18},{3,19},{4,20},{5,21},{6,22},{7,23},{8,24},{9,... | collective-permute-start | bytes 1277960 | tf_op jit(solution)/shard_map/ppermute | solution.py:109
  3.9 18.4 %collective-permute-start.3 = (bf16[3,200,256]{2,1,0:T(8,128)(2,1)S(1)}, bf16[3,200,256]{2,1,0:T(8,128)(2,1)}, u32[]{:S(2)}, u32[]{:S(2)}) collective-permute-start(bf16[3,200,256]{2,1,0:T(8,128)(2,1)S(1)} %get-tuple-element.107), channel_id=1, source_target_pairs={{0,6},{1,7},{2,4},{3,5},{4,2},{5,3},{6,0},{7,1},{8,14},{9,15},{10,... | collective-permute-start | bytes 921608 | tf_op jit(solution)/shard_map/ppermute | solution.py:109
  6.3 16.0 %collective-permute-start.4 = (bf16[3,200,256]{2,1,0:T(8,128)(2,1)S(1)}, bf16[3,200,256]{2,1,0:T(8,128)(2,1)}, u32[]{:S(2)}, u32[]{:S(2)}) collective-permute-start(bf16[3,200,256]{2,1,0:T(8,128)(2,1)S(1)} %get-tuple-element.108), channel_id=1, source_target_pairs={{0,4},{1,5},{2,6},{3,7},{4,0},{5,1},{6,2},{7,3},{8,12},{9,13},{10,... | collective-permute-start | bytes 921608 | tf_op jit(solution)/shard_map/ppermute | solution.py:109
  6.5 15.7 %collective-permute-start.5 = (bf16[3,200,256]{2,1,0:T(8,128)(2,1)S(1)}, bf16[3,200,256]{2,1,0:T(8,128)(2,1)}, u32[]{:S(2)}, u32[]{:S(2)}) collective-permute-start(bf16[3,200,256]{2,1,0:T(8,128)(2,1)S(1)} %get-tuple-element.109), channel_id=1, source_target_pairs={{0,2},{1,3},{2,0},{3,1},{4,6},{5,7},{6,4},{7,5},{8,10},{9,11},{10,... | collective-permute-start | bytes 921608 | tf_op jit(solution)/shard_map/ppermute | solution.py:109
  22.2 10.0 %collective-permute-start.2 = (bf16[208,1024]{1,0:T(8,128)(2,1)}, bf16[208,1024]{1,0:T(8,128)(2,1)}, u32[]{:S(2)}, u32[]{:S(2)}) collective-permute-start(bf16[208,1024]{1,0:T(8,128)(2,1)} %collective-permute-done.1), channel_id=1, source_target_pairs={{0,8},{1,9},{2,10},{3,11},{4,12},{5,13},{6,14},{7,15},{8,0},{9,1},... | collective-permute-start | bytes 1277960 | tf_op jit(solution)/shard_map/ppermute | solution.py:109
  34.8 56.1 %collective-permute-start.9 = (bf16[4,256,896]{2,1,0:T(8,128)(2,1)S(1)}, bf16[4,256,896]{2,1,0:T(8,128)(2,1)}, u32[]{:S(2)}, u32[]{:S(2)}) collective-permute-start(bf16[4,256,896]{2,1,0:T(8,128)(2,1)S(1)} %copy-done), channel_id=1, source_target_pairs={{0,4},{1,5},{2,6},{3,7},{4,0},{5,1},{6,2},{7,3},{8,12},{9,13},{10,... | collective-permute-start | bytes 5505032 | tf_op jit(solution)/shard_map/ppermute | solution.py:109
  36.0 51.5 %collective-permute-start.6 = (bf16[3,800,256]{2,1,0:T(8,128)(2,1)}, bf16[3,800,256]{2,1,0:T(8,128)(2,1)}, u32[]{:S(2)}, u32[]{:S(2)}) collective-permute-start(bf16[3,800,256]{2,1,0:T(8,128)(2,1)} %pad_maximum_fusion.own), channel_id=1, source_target_pairs={{0,8},{1,9},{2,10},{3,11},{4,12},{5,13},{6,14},{7,15},{8,0},{9,1},... | collective-permute-start | bytes 3686408 | tf_op jit(solution)/shard_map/ppermute | solution.py:109
  36.0 54.9 %collective-permute-start.7 = (bf16[3,800,256]{2,1,0:T(8,128)(2,1)}, bf16[3,800,256]{2,1,0:T(8,128)(2,1)}, u32[]{:S(2)}, u32[]{:S(2)}) collective-permute-start(bf16[3,800,256]{2,1,0:T(8,128)(2,1)} %pad_maximum_fusion.own), channel_id=1, source_target_pairs={{0,16},{1,17},{2,18},{3,19},{4,20},{5,21},{6,22},{7,23},{8,24},{9,... | collective-permute-start | bytes 3686408 | tf_op jit(solution)/shard_map/ppermute | solution.py:109
  39.8 51.2 %collective-permute-start.10 = (bf16[2,208,1024]{2,1,0:T(8,128)(2,1)S(1)}, bf16[2,208,1024]{2,1,0:T(8,128)(2,1)S(1)}, u32[]{:S(2)}, u32[]{:S(2)}) collective-permute-start(bf16[2,208,1024]{2,1,0:T(8,128)(2,1)S(1)} %get-tuple-element.106), channel_id=1, source_target_pairs={{0,1},{1,0},{2,3},{3,2},{4,5},{5,4},{6,7},{7,6},{8,9},{9,8},{10,11... | collective-permute-start | bytes 2555912 | tf_op jit(solution)/shard_map/ppermute | solution.py:109
  41.1 53.6 %collective-permute-start.11 = (bf16[2,208,1024]{2,1,0:T(8,128)(2,1)S(1)}, bf16[2,208,1024]{2,1,0:T(8,128)(2,1)S(1)}, u32[]{:S(2)}, u32[]{:S(2)}) collective-permute-start(bf16[2,208,1024]{2,1,0:T(8,128)(2,1)S(1)} %get-tuple-element.105.wa0), channel_id=1, source_target_pairs={{0,4},{1,5},{2,6},{3,7},{4,0},{5,1},{6,2},{7,3},{8,12},{9,13},{10,... | collective-permute-start | bytes 2555912 | tf_op jit(solution)/shard_map/ppermute | solution.py:109
  95.5 28.9 %collective-permute-start.12 = (bf16[3,800,256]{2,1,0:T(8,128)(2,1)}, bf16[3,800,256]{2,1,0:T(8,128)(2,1)S(1)}, u32[]{:S(2)}, u32[]{:S(2)}) collective-permute-start(bf16[3,800,256]{2,1,0:T(8,128)(2,1)} %collective-permute-done.7.far), channel_id=1, source_target_pairs={{0,8},{1,9},{2,10},{3,11},{4,12},{5,13},{6,14},{7,15},{8,0},{9,1},... | collective-permute-start | bytes 3686408 | tf_op jit(solution)/shard_map/ppermute | solution.py:109
  95.5 37.0 %collective-permute-start.18 = (bf16[2,208,1024]{2,1,0:T(8,128)(2,1)S(1)}, bf16[2,208,1024]{2,1,0:T(8,128)(2,1)S(1)}, u32[]{:S(2)}, u32[]{:S(2)}) collective-permute-start(bf16[2,208,1024]{2,1,0:T(8,128)(2,1)S(1)} %get-tuple-element.105.wa0), channel_id=1, source_target_pairs={{0,2},{1,3},{2,0},{3,1},{4,6},{5,7},{6,4},{7,5},{8,10},{9,11},{10,... | collective-permute-start | bytes 2555912 | tf_op jit(solution)/shard_map/ppermute | solution.py:109
  95.9 37.4 %collective-permute-start.16 = (bf16[2,208,1024]{2,1,0:T(8,128)(2,1)S(1)}, bf16[2,208,1024]{2,1,0:T(8,128)(2,1)S(1)}, u32[]{:S(2)}, u32[]{:S(2)}) collective-permute-start(bf16[2,208,1024]{2,1,0:T(8,128)(2,1)S(1)} %collective-permute-done.10.wa1), channel_id=1, source_target_pairs={{0,4},{1,5},{2,6},{3,7},{4,0},{5,1},{6,2},{7,3},{8,12},{9,13},{10,... | collective-permute-start | bytes 2555912 | tf_op jit(solution)/shard_map/ppermute | solution.py:109
  97.1 36.2 %collective-permute-start.17 = (bf16[2,208,1024]{2,1,0:T(8,128)(2,1)S(1)}, bf16[2,208,1024]{2,1,0:T(8,128)(2,1)S(1)}, u32[]{:S(2)}, u32[]{:S(2)}) collective-permute-start(bf16[2,208,1024]{2,1,0:T(8,128)(2,1)S(1)} %collective-permute-done.10.wa1), channel_id=1, source_target_pairs={{0,2},{1,3},{2,0},{3,1},{4,6},{5,7},{6,4},{7,5},{8,10},{9,11},{10,... | collective-permute-start | bytes 2555912 | tf_op jit(solution)/shard_map/ppermute | solution.py:109
  99.1 34.2 %collective-permute-start.19 = (bf16[2,208,1024]{2,1,0:T(8,128)(2,1)S(1)}, bf16[2,208,1024]{2,1,0:T(8,128)(2,1)S(1)}, u32[]{:S(2)}, u32[]{:S(2)}) collective-permute-start(bf16[2,208,1024]{2,1,0:T(8,128)(2,1)S(1)} %collective-permute-done.11.wc0), channel_id=1, source_target_pairs={{0,2},{1,3},{2,0},{3,1},{4,6},{5,7},{6,4},{7,5},{8,10},{9,11},{10,... | collective-permute-start | bytes 2555912 | tf_op jit(solution)/shard_map/ppermute | solution.py:109
  132.5 12.7 %collective-permute-start.14 = (bf16[2,512,256]{2,1,0:T(8,128)(2,1)S(1)}, bf16[2,512,256]{2,1,0:T(8,128)(2,1)S(1)}, u32[]{:S(2)}, u32[]{:S(2)}) collective-permute-start(bf16[2,512,256]{2,1,0:T(8,128)(2,1)S(1)} %get-tuple-element.72), channel_id=1, source_target_pairs={{0,8},{1,9},{2,10},{3,11},{4,12},{5,13},{6,14},{7,15},{8,0},{9,1},... | collective-permute-start | bytes 1572872 | tf_op jit(solution)/shard_map/ppermute | solution.py:109
  132.6 12.6 %collective-permute-start.15 = (bf16[2,512,256]{2,1,0:T(8,128)(2,1)S(1)}, bf16[2,512,256]{2,1,0:T(8,128)(2,1)S(1)}, u32[]{:S(2)}, u32[]{:S(2)}) collective-permute-start(bf16[2,512,256]{2,1,0:T(8,128)(2,1)S(1)} %get-tuple-element.73), channel_id=1, source_target_pairs={{0,2},{1,3},{2,0},{3,1},{4,6},{5,7},{6,4},{7,5},{8,16},{9,17},{10,... | collective-permute-start | bytes 1572872 | tf_op jit(solution)/shard_map/ppermute | solution.py:109
  143.0 9.8 %collective-permute-start.26 = (bf16[2,208,1024]{2,1,0:T(8,128)(2,1)S(1)}, bf16[2,208,1024]{2,1,0:T(8,128)(2,1)S(1)}, u32[]{:S(2)}, u32[]{:S(2)}) collective-permute-start(bf16[2,208,1024]{2,1,0:T(8,128)(2,1)S(1)} %collective-permute-done.16.wc1), channel_id=1, source_target_pairs={{0,2},{1,3},{2,0},{3,1},{4,6},{5,7},{6,4},{7,5},{8,10},{9,11},{10,... | collective-permute-start | bytes 2555912 | tf_op jit(solution)/shard_map/ppermute | solution.py:109
  154.6 8.4 %collective-permute-start.28 = (bf16[256,256]{1,0:T(8,128)(2,1)S(1)}, bf16[256,256]{1,0:T(8,128)(2,1)S(1)}, u32[]{:S(2)}, u32[]{:S(2)}) collective-permute-start(bf16[256,256]{1,0:T(8,128)(2,1)S(1)} %get-tuple-element.86.c00), channel_id=1, source_target_pairs={{0,1},{1,0},{2,3},{3,2},{4,5},{5,4},{6,7},{7,6},{8,9},{9,8},{10,11... | collective-permute-start | bytes 393224 | tf_op jit(solution)/shard_map/ppermute | solution.py:109
  155.8 12.3 %collective-permute-start.29 = (bf16[256,256]{1,0:T(8,128)(2,1)}, bf16[256,256]{1,0:T(8,128)(2,1)}, u32[]{:S(2)}, u32[]{:S(2)}) collective-permute-start(bf16[256,256]{1,0:T(8,128)(2,1)} %get-tuple-element.87), channel_id=1, source_target_pairs={{0,7},{1,6},{2,5},{3,4},{4,3},{5,2},{6,1},{7,0},{8,15},{9,14},{10,... | collective-permute-start | bytes 393224 | tf_op jit(solution)/shard_map/ppermute | solution.py:109
  159.1 9.0 %collective-permute-start.30 = (bf16[256,256]{1,0:T(8,128)(2,1)}, bf16[256,256]{1,0:T(8,128)(2,1)}, u32[]{:S(2)}, u32[]{:S(2)}) collective-permute-start(bf16[256,256]{1,0:T(8,128)(2,1)} %get-tuple-element.87), channel_id=1, source_target_pairs={{0,6},{1,7},{2,4},{3,5},{4,2},{5,3},{6,0},{7,1},{8,14},{9,15},{10,... | collective-permute-start | bytes 393224 | tf_op jit(solution)/shard_map/ppermute | solution.py:109
  159.2 11.0 %collective-permute-start.32 = (bf16[256,256]{1,0:T(8,128)(2,1)}, bf16[256,256]{1,0:T(8,128)(2,1)}, u32[]{:S(2)}, u32[]{:S(2)}) collective-permute-start(bf16[256,256]{1,0:T(8,128)(2,1)} %get-tuple-element.85), channel_id=1, source_target_pairs={{0,5},{1,4},{2,7},{3,6},{4,1},{5,0},{6,3},{7,2},{8,13},{9,12},{10,... | collective-permute-start | bytes 393224 | tf_op jit(solution)/shard_map/ppermute | solution.py:109
  161.1 8.1 %collective-permute-start.31 = (bf16[256,256]{1,0:T(8,128)(2,1)}, bf16[256,256]{1,0:T(8,128)(2,1)}, u32[]{:S(2)}, u32[]{:S(2)}) collective-permute-start(bf16[256,256]{1,0:T(8,128)(2,1)} %get-tuple-element.88), channel_id=1, source_target_pairs={{0,3},{1,2},{2,1},{3,0},{4,7},{5,6},{6,5},{7,4},{8,11},{9,10},{10,... | collective-permute-start | bytes 393224 | tf_op jit(solution)/shard_map/ppermute | solution.py:109
  (33 other events, 248.6 us)

commit v15 on v14

--- a/solution.py
+++ b/solution.py
@@ -239,15 +239,13 @@
 
 
 def late_kernel(
-    place, x_last, acc, last, q_gain, k_gain, query, keys, values, squares, even, odd,
-    w_all, q_all, k_all, v_all, sems,
+    place, x_last, acc, last, q_gain, k_gain, query, keys, values, squares, even, odd, w_all,
 ):
     z, q = place[0], place[1]
     rows = last.shape[1]
     w_all[:, :rows, :] = last[...]
     blank_tail(w_all, rows)
     count = acc.shape[2]
-    stores = []
     for r in range(SLAB):
         rows = pl.ds(pl.multiple_of((q ^ r) * count, count), count)
         for kind in range(3):
@@ -258,19 +256,13 @@
                 summed = as_row(jnp.sum(part * part, axis=1, keepdims=True))
                 squares[kind:kind + 1, rows] = summed[:1]
                 part = part * (q_gain, k_gain)[kind][...]
-            held_out, out = ((q_all, query), (k_all, keys), (v_all, values))[kind]
-            held_out[rows, :] = part.astype(held_out.dtype)
-            store = pltpu.make_async_copy(held_out.at[rows, :], out.at[rows, :], sems.at[3 * r + kind])
-            store.start()
-            stores.append(store)
+            out = (query, keys, values)[kind]
+            out[rows, :] = part.astype(out.dtype)
     reach = even.shape[1]
-    for n, (out, at) in enumerate(((even, 1 - z % 2), (odd, z % 2))):
+    for out, at in ((even, 1 - z % 2), (odd, z % 2)):
         rows = pl.ds(pl.multiple_of(at * reach, reach), reach)
-        for k, src in enumerate((k_all, v_all)):
-            sem = sems.at[3 * SLAB + 2 * n + k]
-            stores.append(pltpu.make_async_copy(src.at[rows, :], out.at[k], sem))
-            stores[-1].start()
-    wait(stores)
+        out[0] = keys[rows, :]
+        out[1] = values[rows, :]
 
 
 def late(place, x_last, acc, last, q_gain, k_gain):
@@ -289,13 +281,9 @@
             jax.ShapeDtypeStruct((2, 2 * count, width), bf16),
         ),
         in_specs=[SMEM] + [VMEM] * 5,
-        out_specs=(HBM, HBM, HBM, VMEM, HBM, HBM),
+        out_specs=(VMEM,) * 6,
         scratch_shapes=[
             pltpu.VMEM((kinds, wide, width), bf16),
-            pltpu.VMEM((slab, width), f32),
-            pltpu.VMEM((slab, width), bf16),
-            pltpu.VMEM((slab, width), bf16),
-            pltpu.SemaphoreType.DMA((3 * SLAB + 4,)),
         ],
         compiler_params=pltpu.CompilerParams(vmem_limit_bytes=HELD_VMEM),
         cost_estimate=pl.CostEstimate(
@@ -469,7 +457,7 @@
             pltpu.SemaphoreType.DMA((SLAB, 2)),
             pltpu.SemaphoreType.DMA((SLAB, 2, 2)),
         ],
-        compiler_params=pltpu.CompilerParams(vmem_limit_bytes=HELD_VMEM),
+        compiler_params=pltpu.CompilerParams(vmem_limit_bytes=KERNEL_VMEM),
         cost_estimate=pl.CostEstimate(
             flops=4 * share * count * depth,
             bytes_accessed=4 * share * depth,

time: 190 us -> 173 us (0.911)
  local copies, waits for them, and re-layouts: 18.2 us -> 6.09 us
  Pallas kernels: 37.5 us -> 30.1 us
  waiting for transfers between devices: 93.8 us -> 98.1 us
    unnamed x47 -> x41, local copies, waits for them, and re-layouts: 11.4 us -> 1.36 us
    pallas_call x1, Pallas kernels: 8.09 us -> 2.47 us  [late(): pl.pallas_call(late_kernel, out_shape=(jax.ShapeDtypeStruct((slab, width)...]
    ppermute x34, waiting for transfers between devices: 93.8 us -> 98.1 us  [permuted(): return lax.ppermute(x, ('seq', 'tp'), pairs)]
    dynamic_slice x1, local copies, waits for them, and re-layouts: 2.44 us -> 0.33 us  [slab_plan(): lax.dynamic_slice_in_dim(tokens, tp * share, share, 1)]
  transfers between devices with their start and end apart: 34 -> 34, of which waited for: 17 -> 18; matrix products, arithmetic and copies ran while one was open for 7% -> 5% of each run, Pallas kernels for 14% -> 12%
where the time goes in v15:
time: 173 us; the launch traced here: 172 us
  waiting for transfers between devices  98.1 us (57%)
  starting transfers between devices  33.7 us (19%)
  Pallas kernels  30.1 us (17%)
  local copies, waits for them, and re-layouts  6.09 us (4%)
  other arithmetic  3.47 us (2%)
    ppermute x34, waiting for transfers between devices, permuted(): return lax.ppermute(x, ('seq', 'tp'), pairs)  98.1 us
    ppermute x34, starting transfers between devices, permuted(): return lax.ppermute(x, ('seq', 'tp'), pairs)  33.7 us
    pallas_call x1, Pallas kernels, output(): pl.pallas_call(out_kernel, out_shape=jax.ShapeDtypeStruct((share, count),...  8.9 us
    pallas_call x1, Pallas kernels, early(): pl.pallas_call(early_kernel, out_shape=(jax.ShapeDtypeStruct((SLAB, kinds...  8.54 us
    pallas_call x1, Pallas kernels, attend(): pl.pallas_call(functools.partial(attend_kernel, full_width), out_shape=(j...  6.61 us
    pallas_call x1, Pallas kernels, norm(): pl.pallas_call(norm_kernel, out_shape=jax.ShapeDtypeStruct(shape, jnp.bfl...  3.57 us
  transfers between devices with their start and end apart: 34, of which 18 were waited for; matrix products, arithmetic and copies ran while one was open for 5% of the time, Pallas kernels for 12%

profile of v15, /device:TPU:9, one launch (start us, length us, event | category | flops | bytes accessed | tf_op | source)
XLA Modules:
  0.0 172.0 jit_solution(6706270629782249345)
XLA Ops:
  1.2 2.5 %collective-permute-start.1 = (bf16[208,1024]{1,0:T(8,128)(2,1)S(1)}, bf16[208,1024]{1,0:T(8,128)(2,1)}, u32[]{:S(2)}, u32[]{:S(2)}) collective-permute-start(bf16[208,1024]{1,0:T(8,128)(2,1)S(1)} %get-tuple-element.111), channel_id=1, source_target_pairs={{0,16},{1,17},{2,18},{3,19},{4,20},{5,21},{6,22},{7,23},{8,24},{9,... | collective-permute-start | bytes 1277960 | tf_op jit(solution)/shard_map/ppermute | solution.py:109
  3.8 2.4 %collective-permute-start.3 = (bf16[3,200,256]{2,1,0:T(8,128)(2,1)S(1)}, bf16[3,200,256]{2,1,0:T(8,128)(2,1)S(1)}, u32[]{:S(2)}, u32[]{:S(2)}) collective-permute-start(bf16[3,200,256]{2,1,0:T(8,128)(2,1)S(1)} %get-tuple-element.107), channel_id=1, source_target_pairs={{0,6},{1,7},{2,4},{3,5},{4,2},{5,3},{6,0},{7,1},{8,14},{9,15},{10,... | collective-permute-start | bytes 921608 | tf_op jit(solution)/shard_map/ppermute | solution.py:109
  9.6 3.6 %norm.1.xa = bf16[4,256,896]{2,1,0:T(8,128)(2,1)} custom-call(bf16[256,3200]{1,0:T(8,128)(2,1)} %tokens.1, f32[1,3200]{1,0:T(1,128)} %broadcast_in_dim.34.gain), custom_call_target="tpu_custom_call" | custom-call | tf_op jit(solution)/shard_map/norm/pallas_call | solution.py:168
  13.3 5.8 %collective-permute-done = bf16[208,1024]{1,0:T(8,128)(2,1)} collective-permute-done((bf16[208,1024]{1,0:T(8,128)(2,1)S(1)}, bf16[208,1024]{1,0:T(8,128)(2,1)}, u32[]{:S(2)}, u32[]{:S(2)}) %collective-permute-start) | collective-permute-done | bytes 426016 | tf_op jit(solution)/shard_map/ppermute | solution.py:109
  19.1 3.2 %collective-permute-done.1 = bf16[208,1024]{1,0:T(8,128)(2,1)} collective-permute-done((bf16[208,1024]{1,0:T(8,128)(2,1)S(1)}, bf16[208,1024]{1,0:T(8,128)(2,1)}, u32[]{:S(2)}, u32[]{:S(2)}) %collective-permute-start.1) | collective-permute-done | bytes 426016 | tf_op jit(solution)/shard_map/ppermute | solution.py:109
  22.2 1.4 fusion.1
  23.8 8.5 %collective-permute-done.2 = bf16[208,1024]{1,0:T(8,128)(2,1)} collective-permute-done((bf16[208,1024]{1,0:T(8,128)(2,1)}, bf16[208,1024]{1,0:T(8,128)(2,1)}, u32[]{:S(2)}, u32[]{:S(2)}) %collective-permute-start.2) | collective-permute-done | bytes 426016 | tf_op jit(solution)/shard_map/ppermute | solution.py:109
  32.2 2.5 %collective-permute-start.8 = (bf16[4,256,896]{2,1,0:T(8,128)(2,1)S(1)}, bf16[4,256,896]{2,1,0:T(8,128)(2,1)}, u32[]{:S(2)}, u32[]{:S(2)}) collective-permute-start(bf16[4,256,896]{2,1,0:T(8,128)(2,1)S(1)} %copy-done), channel_id=1, source_target_pairs={{0,2},{1,3},{2,0},{3,1},{4,6},{5,7},{6,4},{7,5},{8,10},{9,11},{10,... | collective-permute-start | bytes 5505032 | tf_op jit(solution)/shard_map/ppermute | solution.py:109
  38.3 1.4 broadcast_select_fusion
  42.3 44.9 %collective-permute-done.6.near = bf16[3,800,256]{2,1,0:T(8,128)(2,1)} collective-permute-done((bf16[3,800,256]{2,1,0:T(8,128)(2,1)S(1)}, bf16[3,800,256]{2,1,0:T(8,128)(2,1)}, u32[]{:S(2)}, u32[]{:S(2)}) %collective-permute-start.6) | collective-permute-done | bytes 1228832 | tf_op jit(solution)/shard_map/ppermute | solution.py:109
  87.2 3.5 %collective-permute-done.7.far = bf16[3,800,256]{2,1,0:T(8,128)(2,1)} collective-permute-done((bf16[3,800,256]{2,1,0:T(8,128)(2,1)S(1)}, bf16[3,800,256]{2,1,0:T(8,128)(2,1)}, u32[]{:S(2)}, u32[]{:S(2)}) %collective-permute-start.7) | collective-permute-done | bytes 1228832 | tf_op jit(solution)/shard_map/ppermute | solution.py:109
  90.7 4.0 %collective-permute-done.11.wc0 = bf16[2,208,1024]{2,1,0:T(8,128)(2,1)S(1)} collective-permute-done((bf16[2,208,1024]{2,1,0:T(8,128)(2,1)S(1)}, bf16[2,208,1024]{2,1,0:T(8,128)(2,1)S(1)}, u32[]{:S(2)}, u32[]{:S(2)}) %collective-permute-start.11) | collective-permute-done | bytes 852000 | tf_op jit(solution)/shard_map/ppermute | solution.py:109
  97.5 1.5 collective-permute-done.13.xd
  99.4 8.5 %early.1 = (f32[4,3,256,256]{3,2,1,0:T(8,128)S(1)}, bf16[4,256,896]{2,1,0:T(8,128)(2,1)S(1)}) custom-call(s32[3]{0:T(128)S(1)} %pad_add_fusion.1.place, bf16[4,256,896]{2,1,0:T(8,128)(2,1)S(1)} %copy-done, bf16[4,256,896]{2,1,0:T(8,128)(2,1)} %collective-permute-done.8.xb, bf16[4,256,896]{2,1,0:T(8,128)(2,1)} %collective-permute-done.9.xc, ...), custom_call_target="tpu_custom_call" | custom-call | flops 7549747200 | bytes 8601600 | tf_op jit(solution)/shard_map/early/pallas_call | solution.py:216
  108.0 16.3 %collective-permute-done.12.last = bf16[3,800,256]{2,1,0:T(8,128)(2,1)S(1)} collective-permute-done((bf16[3,800,256]{2,1,0:T(8,128)(2,1)}, bf16[3,800,256]{2,1,0:T(8,128)(2,1)S(1)}, u32[]{:S(2)}, u32[]{:S(2)}) %collective-permute-start.12) | collective-permute-done | bytes 1228832 | tf_op jit(solution)/shard_map/ppermute | solution.py:109
  124.3 2.5 %late.1 = (f32[1024,256]{1,0:T(8,128)S(1)}, bf16[1024,256]{1,0:T(8,128)(2,1)S(1)}, bf16[1024,256]{1,0:T(8,128)(2,1)S(1)}, f32[2,1024]{1,0:T(2,128)S(1)}, bf16[2,...) custom-call(s32[3]{0:T(128)S(1)} %pad_add_fusion.1.place, bf16[4,256,896]{2,1,0:T(8,128)(2,1)S(1)} %get-tuple-element.64.x_last, ...), custom_call_target="tpu_custom_call" | custom-call | flops 1258291200 | bytes 2867200 | tf_op jit(solution)/shard_map/late/pallas_call | solution.py:273
  131.9 1.8 %collective-permute-done.22 = f32[2,1024]{1,0:T(2,128)S(1)} collective-permute-done((f32[2,1024]{1,0:T(2,128)S(1)}, f32[2,1024]{1,0:T(2,128)S(1)}, u32[]{:S(2)}, u32[]{:S(2)}) %collective-permute-start.22) | collective-permute-done | bytes 8224 | tf_op jit(solution)/shard_map/ppermute | solution.py:109
  135.0 1.6 collective-permute-done.23
  137.3 1.8 %collective-permute-start.26 = (bf16[2,208,1024]{2,1,0:T(8,128)(2,1)S(1)}, bf16[2,208,1024]{2,1,0:T(8,128)(2,1)S(1)}, u32[]{:S(2)}, u32[]{:S(2)}) collective-permute-start(bf16[2,208,1024]{2,1,0:T(8,128)(2,1)S(1)} %collective-permute-done.16.wc1), channel_id=1, source_target_pairs={{0,2},{1,3},{2,0},{3,1},{4,6},{5,7},{6,4},{7,5},{8,10},{9,11},{10,... | collective-permute-start | bytes 2555912 | tf_op jit(solution)/shard_map/ppermute | solution.py:109
  140.0 6.6 %attend.1 = (bf16[256,256]{1,0:T(8,128)(2,1)S(1)}, bf16[256,256]{1,0:T(8,128)(2,1)S(1)}, bf16[256,256]{1,0:T(8,128)(2,1)S(1)}, bf16[256,256]{1,0:T(8,128)(2,1)S(1)}) custom-call(s32[3]{0:T(128)S(1)} %pad_add_fusion.1.place, s32[4,2]{1,0:T(4,128)S(1)} %pad_add_fusion.spans, f32[1024,256]{1,0:T(8,128)S(1)} %get-tuple-element.69.query, ...), custom_call_target="tpu_custom_call" | custom-call | flops 21474836480 | bytes 3145728 | tf_op jit(solution)/shard_map/attend/pallas_call | solution.py:383
  148.9 3.2 %collective-permute-start.29 = (bf16[256,256]{1,0:T(8,128)(2,1)S(1)}, bf16[256,256]{1,0:T(8,128)(2,1)S(1)}, u32[]{:S(2)}, u32[]{:S(2)}) collective-permute-start(bf16[256,256]{1,0:T(8,128)(2,1)S(1)} %get-tuple-element.87), channel_id=1, source_target_pairs={{0,7},{1,6},{2,5},{3,4},{4,3},{5,2},{6,1},{7,0},{8,15},{9,14},{10,... | collective-permute-start | bytes 393224 | tf_op jit(solution)/shard_map/ppermute | solution.py:109
  153.5 1.9 %collective-permute-start.31 = (bf16[256,256]{1,0:T(8,128)(2,1)S(1)}, bf16[256,256]{1,0:T(8,128)(2,1)}, u32[]{:S(2)}, u32[]{:S(2)}) collective-permute-start(bf16[256,256]{1,0:T(8,128)(2,1)S(1)} %get-tuple-element.88), channel_id=1, source_target_pairs={{0,3},{1,2},{2,1},{3,0},{4,7},{5,6},{6,5},{7,4},{8,11},{9,10},{10,... | collective-permute-start | bytes 393224 | tf_op jit(solution)/shard_map/ppermute | solution.py:109
  159.8 3.1 %collective-permute-done.32.c21 = bf16[256,256]{1,0:T(8,128)(2,1)} collective-permute-done((bf16[256,256]{1,0:T(8,128)(2,1)S(1)}, bf16[256,256]{1,0:T(8,128)(2,1)}, u32[]{:S(2)}, u32[]{:S(2)}) %collective-permute-start.32) | collective-permute-done | bytes 131104 | tf_op jit(solution)/shard_map/ppermute | solution.py:109
  162.9 8.9 %output.1 = bf16[1600,256]{1,0:T(8,128)(2,1)} custom-call(s32[3]{0:T(128)} %copy-done.2, bf16[256,256]{1,0:T(8,128)(2,1)} %copy-done.13, bf16[256,256]{1,0:T(8,128)(2,1)} %copy-done.14, bf16[256,256]{1,0:T(8,128)(2,1)} %copy-done.15, bf16[256,256]{1,0:T(8,128)(2,1)} %copy-done.16, bf16[256,256]{1,0:T(8,128)(2,1)} %collective-permute-done.31.c11, ...), custom_call_target="tpu_custom_call" | custom-call | flops 1677721600 | bytes 6553600 | tf_op jit(solution)/shard_map/output/pallas_call | solution.py:447
  (115 shorter events, 30.2 us)
Async XLA Ops:
  1.2 17.9 %collective-permute-start = (bf16[208,1024]{1,0:T(8,128)(2,1)S(1)}, bf16[208,1024]{1,0:T(8,128)(2,1)}, u32[]{:S(2)}, u32[]{:S(2)}) collective-permute-start(bf16[208,1024]{1,0:T(8,128)(2,1)S(1)} %get-tuple-element.111), channel_id=1, source_target_pairs={{0,8},{1,9},{2,10},{3,11},{4,12},{5,13},{6,14},{7,15},{8,0},{9,1},... | collective-permute-start | bytes 1277960 | tf_op jit(solution)/shard_map/ppermute | solution.py:109
  1.2 21.0 %collective-permute-start.1 = (bf16[208,1024]{1,0:T(8,128)(2,1)S(1)}, bf16[208,1024]{1,0:T(8,128)(2,1)}, u32[]{:S(2)}, u32[]{:S(2)}) collective-permute-start(bf16[208,1024]{1,0:T(8,128)(2,1)S(1)} %get-tuple-element.111), channel_id=1, source_target_pairs={{0,16},{1,17},{2,18},{3,19},{4,20},{5,21},{6,22},{7,23},{8,24},{9,... | collective-permute-start | bytes 1277960 | tf_op jit(solution)/shard_map/ppermute | solution.py:109
  3.8 18.4 %collective-permute-start.3 = (bf16[3,200,256]{2,1,0:T(8,128)(2,1)S(1)}, bf16[3,200,256]{2,1,0:T(8,128)(2,1)S(1)}, u32[]{:S(2)}, u32[]{:S(2)}) collective-permute-start(bf16[3,200,256]{2,1,0:T(8,128)(2,1)S(1)} %get-tuple-element.107), channel_id=1, source_target_pairs={{0,6},{1,7},{2,4},{3,5},{4,2},{5,3},{6,0},{7,1},{8,14},{9,15},{10,... | collective-permute-start | bytes 921608 | tf_op jit(solution)/shard_map/ppermute | solution.py:109
  6.2 16.0 %collective-permute-start.4 = (bf16[3,200,256]{2,1,0:T(8,128)(2,1)S(1)}, bf16[3,200,256]{2,1,0:T(8,128)(2,1)}, u32[]{:S(2)}, u32[]{:S(2)}) collective-permute-start(bf16[3,200,256]{2,1,0:T(8,128)(2,1)S(1)} %get-tuple-element.108), channel_id=1, source_target_pairs={{0,4},{1,5},{2,6},{3,7},{4,0},{5,1},{6,2},{7,3},{8,12},{9,13},{10,... | collective-permute-start | bytes 921608 | tf_op jit(solution)/shard_map/ppermute | solution.py:109
  6.5 15.7 %collective-permute-start.5 = (bf16[3,200,256]{2,1,0:T(8,128)(2,1)S(1)}, bf16[3,200,256]{2,1,0:T(8,128)(2,1)}, u32[]{:S(2)}, u32[]{:S(2)}) collective-permute-start(bf16[3,200,256]{2,1,0:T(8,128)(2,1)S(1)} %get-tuple-element.109), channel_id=1, source_target_pairs={{0,2},{1,3},{2,0},{3,1},{4,6},{5,7},{6,4},{7,5},{8,10},{9,11},{10,... | collective-permute-start | bytes 921608 | tf_op jit(solution)/shard_map/ppermute | solution.py:109
  22.2 10.0 %collective-permute-start.2 = (bf16[208,1024]{1,0:T(8,128)(2,1)}, bf16[208,1024]{1,0:T(8,128)(2,1)}, u32[]{:S(2)}, u32[]{:S(2)}) collective-permute-start(bf16[208,1024]{1,0:T(8,128)(2,1)} %collective-permute-done.1), channel_id=1, source_target_pairs={{0,8},{1,9},{2,10},{3,11},{4,12},{5,13},{6,14},{7,15},{8,0},{9,1},... | collective-permute-start | bytes 1277960 | tf_op jit(solution)/shard_map/ppermute | solution.py:109
  34.8 55.9 %collective-permute-start.9 = (bf16[4,256,896]{2,1,0:T(8,128)(2,1)S(1)}, bf16[4,256,896]{2,1,0:T(8,128)(2,1)}, u32[]{:S(2)}, u32[]{:S(2)}) collective-permute-start(bf16[4,256,896]{2,1,0:T(8,128)(2,1)S(1)} %copy-done), channel_id=1, source_target_pairs={{0,4},{1,5},{2,6},{3,7},{4,0},{5,1},{6,2},{7,3},{8,12},{9,13},{10,... | collective-permute-start | bytes 5505032 | tf_op jit(solution)/shard_map/ppermute | solution.py:109
  36.0 51.2 %collective-permute-start.6 = (bf16[3,800,256]{2,1,0:T(8,128)(2,1)S(1)}, bf16[3,800,256]{2,1,0:T(8,128)(2,1)}, u32[]{:S(2)}, u32[]{:S(2)}) collective-permute-start(bf16[3,800,256]{2,1,0:T(8,128)(2,1)S(1)} %pad_maximum_fusion.own), channel_id=1, source_target_pairs={{0,8},{1,9},{2,10},{3,11},{4,12},{5,13},{6,14},{7,15},{8,0},{9,1},... | collective-permute-start | bytes 3686408 | tf_op jit(solution)/shard_map/ppermute | solution.py:109
  36.0 54.7 %collective-permute-start.7 = (bf16[3,800,256]{2,1,0:T(8,128)(2,1)S(1)}, bf16[3,800,256]{2,1,0:T(8,128)(2,1)}, u32[]{:S(2)}, u32[]{:S(2)}) collective-permute-start(bf16[3,800,256]{2,1,0:T(8,128)(2,1)S(1)} %pad_maximum_fusion.own), channel_id=1, source_target_pairs={{0,16},{1,17},{2,18},{3,19},{4,20},{5,21},{6,22},{7,23},{8,24},{9,... | collective-permute-start | bytes 3686408 | tf_op jit(solution)/shard_map/ppermute | solution.py:109
  39.7 50.9 %collective-permute-start.10 = (bf16[2,208,1024]{2,1,0:T(8,128)(2,1)S(1)}, bf16[2,208,1024]{2,1,0:T(8,128)(2,1)S(1)}, u32[]{:S(2)}, u32[]{:S(2)}) collective-permute-start(bf16[2,208,1024]{2,1,0:T(8,128)(2,1)S(1)} %get-tuple-element.106), channel_id=1, source_target_pairs={{0,1},{1,0},{2,3},{3,2},{4,5},{5,4},{6,7},{7,6},{8,9},{9,8},{10,11... | collective-permute-start | bytes 2555912 | tf_op jit(solution)/shard_map/ppermute | solution.py:109
  41.1 53.6 %collective-permute-start.11 = (bf16[2,208,1024]{2,1,0:T(8,128)(2,1)S(1)}, bf16[2,208,1024]{2,1,0:T(8,128)(2,1)S(1)}, u32[]{:S(2)}, u32[]{:S(2)}) collective-permute-start(bf16[2,208,1024]{2,1,0:T(8,128)(2,1)S(1)} %get-tuple-element.105.wa0), channel_id=1, source_target_pairs={{0,4},{1,5},{2,6},{3,7},{4,0},{5,1},{6,2},{7,3},{8,12},{9,13},{10,... | collective-permute-start | bytes 2555912 | tf_op jit(solution)/shard_map/ppermute | solution.py:109
  95.4 28.9 %collective-permute-start.12 = (bf16[3,800,256]{2,1,0:T(8,128)(2,1)}, bf16[3,800,256]{2,1,0:T(8,128)(2,1)S(1)}, u32[]{:S(2)}, u32[]{:S(2)}) collective-permute-start(bf16[3,800,256]{2,1,0:T(8,128)(2,1)} %collective-permute-done.7.far), channel_id=1, source_target_pairs={{0,8},{1,9},{2,10},{3,11},{4,12},{5,13},{6,14},{7,15},{8,0},{9,1},... | collective-permute-start | bytes 3686408 | tf_op jit(solution)/shard_map/ppermute | solution.py:109
  95.5 31.4 %collective-permute-start.18 = (bf16[2,208,1024]{2,1,0:T(8,128)(2,1)S(1)}, bf16[2,208,1024]{2,1,0:T(8,128)(2,1)S(1)}, u32[]{:S(2)}, u32[]{:S(2)}) collective-permute-start(bf16[2,208,1024]{2,1,0:T(8,128)(2,1)S(1)} %get-tuple-element.105.wa0), channel_id=1, source_target_pairs={{0,2},{1,3},{2,0},{3,1},{4,6},{5,7},{6,4},{7,5},{8,10},{9,11},{10,... | collective-permute-start | bytes 2555912 | tf_op jit(solution)/shard_map/ppermute | solution.py:109
  95.8 31.8 %collective-permute-start.16 = (bf16[2,208,1024]{2,1,0:T(8,128)(2,1)S(1)}, bf16[2,208,1024]{2,1,0:T(8,128)(2,1)S(1)}, u32[]{:S(2)}, u32[]{:S(2)}) collective-permute-start(bf16[2,208,1024]{2,1,0:T(8,128)(2,1)S(1)} %collective-permute-done.10.wa1), channel_id=1, source_target_pairs={{0,4},{1,5},{2,6},{3,7},{4,0},{5,1},{6,2},{7,3},{8,12},{9,13},{10,... | collective-permute-start | bytes 2555912 | tf_op jit(solution)/shard_map/ppermute | solution.py:109
  97.0 30.6 %collective-permute-start.17 = (bf16[2,208,1024]{2,1,0:T(8,128)(2,1)S(1)}, bf16[2,208,1024]{2,1,0:T(8,128)(2,1)S(1)}, u32[]{:S(2)}, u32[]{:S(2)}) collective-permute-start(bf16[2,208,1024]{2,1,0:T(8,128)(2,1)S(1)} %collective-permute-done.10.wa1), channel_id=1, source_target_pairs={{0,2},{1,3},{2,0},{3,1},{4,6},{5,7},{6,4},{7,5},{8,10},{9,11},{10,... | collective-permute-start | bytes 2555912 | tf_op jit(solution)/shard_map/ppermute | solution.py:109
  99.1 28.6 %collective-permute-start.19 = (bf16[2,208,1024]{2,1,0:T(8,128)(2,1)S(1)}, bf16[2,208,1024]{2,1,0:T(8,128)(2,1)S(1)}, u32[]{:S(2)}, u32[]{:S(2)}) collective-permute-start(bf16[2,208,1024]{2,1,0:T(8,128)(2,1)S(1)} %collective-permute-done.11.wc0), channel_id=1, source_target_pairs={{0,2},{1,3},{2,0},{3,1},{4,6},{5,7},{6,4},{7,5},{8,10},{9,11},{10,... | collective-permute-start | bytes 2555912 | tf_op jit(solution)/shard_map/ppermute | solution.py:109
  126.8 12.7 %collective-permute-start.14 = (bf16[2,512,256]{2,1,0:T(8,128)(2,1)S(1)}, bf16[2,512,256]{2,1,0:T(8,128)(2,1)S(1)}, u32[]{:S(2)}, u32[]{:S(2)}) collective-permute-start(bf16[2,512,256]{2,1,0:T(8,128)(2,1)S(1)} %get-tuple-element.72), channel_id=1, source_target_pairs={{0,8},{1,9},{2,10},{3,11},{4,12},{5,13},{6,14},{7,15},{8,0},{9,1},... | collective-permute-start | bytes 1572872 | tf_op jit(solution)/shard_map/ppermute | solution.py:109
  126.9 12.6 %collective-permute-start.15 = (bf16[2,512,256]{2,1,0:T(8,128)(2,1)S(1)}, bf16[2,512,256]{2,1,0:T(8,128)(2,1)S(1)}, u32[]{:S(2)}, u32[]{:S(2)}) collective-permute-start(bf16[2,512,256]{2,1,0:T(8,128)(2,1)S(1)} %get-tuple-element.73), channel_id=1, source_target_pairs={{0,2},{1,3},{2,0},{3,1},{4,6},{5,7},{6,4},{7,5},{8,16},{9,17},{10,... | collective-permute-start | bytes 1572872 | tf_op jit(solution)/shard_map/ppermute | solution.py:109
  137.3 9.4 %collective-permute-start.26 = (bf16[2,208,1024]{2,1,0:T(8,128)(2,1)S(1)}, bf16[2,208,1024]{2,1,0:T(8,128)(2,1)S(1)}, u32[]{:S(2)}, u32[]{:S(2)}) collective-permute-start(bf16[2,208,1024]{2,1,0:T(8,128)(2,1)S(1)} %collective-permute-done.16.wc1), channel_id=1, source_target_pairs={{0,2},{1,3},{2,0},{3,1},{4,6},{5,7},{6,4},{7,5},{8,10},{9,11},{10,... | collective-permute-start | bytes 2555912 | tf_op jit(solution)/shard_map/ppermute | solution.py:109
  147.6 7.7 %collective-permute-start.28 = (bf16[256,256]{1,0:T(8,128)(2,1)S(1)}, bf16[256,256]{1,0:T(8,128)(2,1)S(1)}, u32[]{:S(2)}, u32[]{:S(2)}) collective-permute-start(bf16[256,256]{1,0:T(8,128)(2,1)S(1)} %get-tuple-element.86.c00), channel_id=1, source_target_pairs={{0,1},{1,0},{2,3},{3,2},{4,5},{5,4},{6,7},{7,6},{8,9},{9,8},{10,11... | collective-permute-start | bytes 393224 | tf_op jit(solution)/shard_map/ppermute | solution.py:109
  148.9 9.9 %collective-permute-start.29 = (bf16[256,256]{1,0:T(8,128)(2,1)S(1)}, bf16[256,256]{1,0:T(8,128)(2,1)S(1)}, u32[]{:S(2)}, u32[]{:S(2)}) collective-permute-start(bf16[256,256]{1,0:T(8,128)(2,1)S(1)} %get-tuple-element.87), channel_id=1, source_target_pairs={{0,7},{1,6},{2,5},{3,4},{4,3},{5,2},{6,1},{7,0},{8,15},{9,14},{10,... | collective-permute-start | bytes 393224 | tf_op jit(solution)/shard_map/ppermute | solution.py:109
  152.1 7.4 %collective-permute-start.30 = (bf16[256,256]{1,0:T(8,128)(2,1)S(1)}, bf16[256,256]{1,0:T(8,128)(2,1)S(1)}, u32[]{:S(2)}, u32[]{:S(2)}) collective-permute-start(bf16[256,256]{1,0:T(8,128)(2,1)S(1)} %get-tuple-element.87), channel_id=1, source_target_pairs={{0,6},{1,7},{2,4},{3,5},{4,2},{5,3},{6,0},{7,1},{8,14},{9,15},{10,... | collective-permute-start | bytes 393224 | tf_op jit(solution)/shard_map/ppermute | solution.py:109
  152.2 10.7 %collective-permute-start.32 = (bf16[256,256]{1,0:T(8,128)(2,1)S(1)}, bf16[256,256]{1,0:T(8,128)(2,1)}, u32[]{:S(2)}, u32[]{:S(2)}) collective-permute-start(bf16[256,256]{1,0:T(8,128)(2,1)S(1)} %get-tuple-element.85), channel_id=1, source_target_pairs={{0,5},{1,4},{2,7},{3,6},{4,1},{5,0},{6,3},{7,2},{8,13},{9,12},{10,... | collective-permute-start | bytes 393224 | tf_op jit(solution)/shard_map/ppermute | solution.py:109
  155.3 7.5 %collective-permute-start.33 = (bf16[256,256]{1,0:T(8,128)(2,1)S(1)}, bf16[256,256]{1,0:T(8,128)(2,1)}, u32[]{:S(2)}, u32[]{:S(2)}) collective-permute-start(bf16[256,256]{1,0:T(8,128)(2,1)S(1)} %get-tuple-element.88), channel_id=1, source_target_pairs={{0,2},{1,3},{2,0},{3,1},{4,6},{5,7},{6,4},{7,5},{8,10},{9,11},{10,... | collective-permute-start | bytes 393224 | tf_op jit(solution)/shard_map/ppermute | solution.py:109
  (30 other events, 350.9 us)

commit v16 on v15

--- a/solution.py
+++ b/solution.py
@@ -297,7 +297,7 @@
 
 def attend_kernel(
     full_width, place, spans, query, keys, values, even, odd, mine, near, mid, seg, o0, o1, o2, o3,
-    q_all, k_all, v_all, o_all, scale_all, sems,
+    k_all, v_all, o_all, scale_all,
 ):
     z, q = place[0], place[1]
     slab = query.shape[0]
@@ -307,18 +307,14 @@
     is_even = z % 2 == 0
     even_at = pl.multiple_of(jnp.where(is_even, upper, 0), half)
     odd_at = pl.multiple_of(jnp.where(is_even, 0, upper), half)
-    copies = [pltpu.make_async_copy(query, q_all, sems.at[0])]
     for k, (whole, out) in enumerate(((keys, k_all), (values, v_all))):
-        for n, (src, at) in enumerate(((whole, half), (even.at[k], even_at), (odd.at[k], odd_at))):
-            dst = out.at[pl.ds(at, src.shape[0]), :]
-            copies.append(pltpu.make_async_copy(src, dst, sems.at[1 + 3 * k + n]))
-    start(copies)
+        out[half:upper, :] = whole[...]
+        out[pl.ds(even_at, half), :] = even[k]
+        out[pl.ds(odd_at, half), :] = odd[k]
     scale = [lax.rsqrt(sums[...] / full_width + eps) for sums in (mine, near, mid)]
     scale_all[:, half:upper] = scale[0]
     scale_all[:, :half] = jnp.where(is_even, scale[2], scale[1])[:, slab - half:]
     scale_all[:, upper:] = jnp.where(is_even, scale[1], scale[2])[:, :half]
-    wait(copies)
-    ext = k_all.shape[0]
     heads = query.shape[1] // HEAD_DIM
     factor = HEAD_DIM ** (-0.5) * math.log2(math.e)
 
@@ -337,7 +333,7 @@
                 k_scale = scale_all[1:2, keys_at] * factor
                 for h in range(heads):
                     cols = slice(h * HEAD_DIM, (h + 1) * HEAD_DIM)
-                    q_low = q_all[pl.ds(pl.multiple_of(b * count, count), count), cols] * q_scale
+                    q_low = query[pl.ds(pl.multiple_of(b * count, count), count), cols] * q_scale
                     scores = lax.dot_general(
                         q_low.astype(jnp.bfloat16), k_all[keys_at, cols],
                         (((1,), (1,)), ((), ())), preferred_element_type=jnp.float32,
@@ -355,11 +351,8 @@
         return 0
 
     lax.fori_loop(0, SLAB, block, 0)
-    stores = [
-        pltpu.make_async_copy(o_all.at[r], out, sems.at[r]) for r, out in enumerate((o0, o1, o2, o3))
-    ]
-    start(stores)
-    wait(stores)
+    for r, out in enumerate((o0, o1, o2, o3)):
+        out[...] = o_all[r]
 
 
 def key_spans(seg, slab, count, half):
@@ -383,15 +376,13 @@
     return pl.pallas_call(
         functools.partial(attend_kernel, full_width),
         out_shape=(jax.ShapeDtypeStruct((width, count), bf16),) * SLAB,
-        in_specs=[SMEM] * 2 + [HBM] * 5 + [VMEM] * 4,
-        out_specs=(HBM,) * SLAB,
+        in_specs=[SMEM] * 2 + [VMEM] * 9,
+        out_specs=(VMEM,) * SLAB,
         scratch_shapes=[
-            pltpu.VMEM((slab, width), jnp.float32),
             pltpu.VMEM((ext, width), bf16),
             pltpu.VMEM((ext, width), bf16),
             pltpu.VMEM((SLAB, width, count), bf16),
             pltpu.VMEM((2, ext), jnp.float32),
-            pltpu.SemaphoreType.DMA((7,)),
         ],
         compiler_params=pltpu.CompilerParams(vmem_limit_bytes=HELD_VMEM),
         cost_estimate=pl.CostEstimate(
@@ -403,34 +394,47 @@
     )(place, spans, query, keys, values, even, odd, *sums, seg)
 
 
+def collect_kernel(wa0, wb0, wc0, wd0, wa1, wb1, wc1, wd1, out, sems):
+    rows = wa0.shape[1]
+    copies = []
+    for i, ws in enumerate(((wa0, wb0, wc0, wd0), (wa1, wb1, wc1, wd1))):
+        for r, w in enumerate(ws):
+            for j in range(2):
+                dst = out.at[i, pl.ds((2 * r + j) * rows, rows), :]
+                copies.append(pltpu.make_async_copy(w.at[j], dst, sems.at[i, r, j]))
+    start(copies)
+    wait(copies)
+
+
+def collect(pieces):
+    rows, depth = pieces[0].shape[1:]
+    return pl.pallas_call(
+        collect_kernel,
+        out_shape=jax.ShapeDtypeStruct((2, 2 * SLAB * rows, depth), jnp.bfloat16),
+        in_specs=[HBM] * 8,
+        out_specs=VMEM,
+        scratch_shapes=[pltpu.SemaphoreType.DMA((2, SLAB, 2))],
+        compiler_params=pltpu.CompilerParams(vmem_limit_bytes=HELD_VMEM),
+        cost_estimate=pl.CostEstimate(
+            flops=0, bytes_accessed=16 * SLAB * rows * depth, transcendentals=0
+        ),
+        name="collect",
+    )(*pieces)
+
+
 def out_kernel(
-    place, c20, c01, c31, c30, c11, c21, c10, c00, wa0, wb0, wc0, wd0, wa1, wb1, wc1, wd1,
-    residual, scale, out, c_all, w_all, total, placed, c_sem, w_sem,
+    place, c20, c01, c31, c30, c11, c21, c10, c00, w, residual, scale, out, c_all, total, placed,
 ):
     z, q = place[0], place[1]
     width = c00.shape[0]
-    c_copies = []
-    for i in range(2):
-        for r, pair in enumerate(((c00, c01), (c10, c11), (c20, c21), (c30, c31))):
-            at = pl.multiple_of((q ^ r) * width, width)
-            dst = c_all.at[i, pl.ds(at, width), :]
-            c_copies.append(pltpu.make_async_copy(pair[i], dst, c_sem.at[r, i]))
-    start(c_copies)
-    rows = wa0.shape[1]
-    w_copies = []
-    for i in range(2):
-        for r, w in enumerate(((wa0, wb0, wc0, wd0), (wa1, wb1, wc1, wd1))[i]):
-            for j in range(2):
-                dst = w_all.at[i, pl.ds((2 * r + j) * rows, rows), :]
-                w_copies.append(pltpu.make_async_copy(w.at[j], dst, w_sem.at[r, j, i]))
-    start(w_copies)
+    for i, blocks in enumerate(((c00, c10, c20, c30), (c01, c11, c21, c31))):
+        for r, c in enumerate(blocks):
+            c_all[i, pl.ds(pl.multiple_of((q ^ r) * width, width), width), :] = c[...]
     column = as_column(scale[...])[:out.shape[0]]
     column = jnp.tile(column, (1, out.shape[1] // 128))
-    wait(c_copies[:SLAB] + w_copies[:2 * SLAB])
-    total[...] = jnp.dot(w_all[0], c_all[0], preferred_element_type=jnp.float32)
-    wait(c_copies[SLAB:] + w_copies[2 * SLAB:])
-    total[...] += jnp.dot(w_all[1], c_all[1], preferred_element_type=jnp.float32)
-    kept = out.shape[0] // (2 * SLAB)
+    total[...] = jnp.dot(w[0], c_all[0], preferred_element_type=jnp.float32)
+    total[...] += jnp.dot(w[1], c_all[1], preferred_element_type=jnp.float32)
+    rows, kept = w.shape[1] // (2 * SLAB), out.shape[0] // (2 * SLAB)
     for r in range(SLAB):
         for j in range(2):
             at = pl.multiple_of((((z % 2) ^ j) * SLAB + (q ^ r)) * kept, 8)
@@ -439,32 +443,28 @@
     out[...] = (residual[...].astype(jnp.float32) + column * placed[...]).astype(jnp.bfloat16)
 
 
-def output(place, blocks, pieces, residual, scale):
+def output(place, blocks, w, residual, scale):
     count = blocks[0].shape[1]
-    rows, depth = pieces[0].shape[1:]
+    rows, depth = w.shape[1:]
     share = residual.shape[0]
-    scale = jnp.pad(scale, (0, -share % 128))[None]
     return pl.pallas_call(
         out_kernel,
         out_shape=jax.ShapeDtypeStruct((share, count), jnp.bfloat16),
-        in_specs=[SMEM] + [HBM] * 16 + [VMEM] * 2,
+        in_specs=[SMEM] + [VMEM] * 11,
         out_specs=VMEM,
         scratch_shapes=[
             pltpu.VMEM((2, depth, count), jnp.bfloat16),
-            pltpu.VMEM((2, 2 * SLAB * rows, depth), jnp.bfloat16),
-            pltpu.VMEM((2 * SLAB * rows, count), jnp.float32),
+            pltpu.VMEM((rows, count), jnp.float32),
             pltpu.VMEM((share, count), jnp.float32),
-            pltpu.SemaphoreType.DMA((SLAB, 2)),
-            pltpu.SemaphoreType.DMA((SLAB, 2, 2)),
         ],
-        compiler_params=pltpu.CompilerParams(vmem_limit_bytes=KERNEL_VMEM),
+        compiler_params=pltpu.CompilerParams(vmem_limit_bytes=HELD_VMEM),
         cost_estimate=pl.CostEstimate(
             flops=4 * share * count * depth,
             bytes_accessed=4 * share * depth,
             transcendentals=0,
         ),
         name="output",
-    )(place, *blocks, *pieces, residual, scale)
+    )(place, *blocks, w, residual, scale)
 
 
 def rows_of_slab(q, got):
@@ -502,7 +502,12 @@
     seg = lax.dynamic_slice_in_dim(seg, z * slab, slab + 2 * half, 0)
     spans = key_spans(seg, slab, count, half)
     seg = seg.astype(jnp.float32)[None]
-    x0, out_near, out_far, seg, spans, *gains = tied(x0, out_near, out_far, seg, spans, *gains)
+    share = layer_scale.shape[0]
+    residual = jnp.transpose(lax.dynamic_slice_in_dim(tokens, tp * share, share, 1))
+    scale = jnp.pad(layer_scale, (0, -share % 128))[None]
+    x0, out_near, out_far, seg, spans, residual, scale, *gains = tied(
+        x0, out_near, out_far, seg, spans, residual, scale, *gains
+    )
     out_last = even_pair(out_far)
     x2 = in_slab(x0, 2)
     out_last, own, x0 = tied(out_last, own, x0)
@@ -539,9 +544,7 @@
         to = functools.partial(lambda r, i, z, q, y: (z, q ^ r, y ^ i), r, i)
         spread.append(permuted(blocks[r], to) if r or i else blocks[r])
 
-    share = layer_scale.shape[0]
-    residual = jnp.transpose(lax.dynamic_slice_in_dim(tokens, tp * share, share, 1))
-    return jnp.transpose(output(place, spread, pieces, residual, layer_scale))
+    return jnp.transpose(output(place, spread, collect(pieces), residual, scale))
 
 
 def solution(mesh):

time: 173 us -> 168 us (0.971)
  waiting for transfers between devices: 98.1 us -> 94.1 us
  Pallas kernels: 30.1 us -> 28.1 us
    pallas_call x1, Pallas kernels: 8.9 us -> 3.83 us  [output(): pl.pallas_call(out_kernel, out_shape=jax.ShapeDtypeStruct((share, count),...]
    ppermute x34, waiting for transfers between devices: 98.1 us -> 94.1 us  [permuted(): return lax.ppermute(x, ('seq', 'tp'), pairs)]
    pallas_call x0 -> x1, Pallas kernels: none -> 3.82 us  [collect(): pl.pallas_call(collect_kernel, out_shape=jax.ShapeDtypeStruct((2, 2 * SLA...]
  transfers between devices with their start and end apart: 34 -> 34, of which waited for: 18 -> 16; matrix products, arithmetic and copies ran while one was open for 5% -> 5% of each run, Pallas kernels for 12% -> 15%
where the time goes in v16:
time: 168 us; the launch traced here: 167 us
  waiting for transfers between devices  94.1 us (56%)
  starting transfers between devices  33.6 us (20%)
  Pallas kernels  28.1 us (17%)
  local copies, waits for them, and re-layouts  6.6 us (4%)
  other arithmetic  4.49 us (3%)
    ppermute x34, waiting for transfers between devices, permuted(): return lax.ppermute(x, ('seq', 'tp'), pairs)  94.1 us
    ppermute x34, starting transfers between devices, permuted(): return lax.ppermute(x, ('seq', 'tp'), pairs)  33.6 us
    pallas_call x1, Pallas kernels, early(): pl.pallas_call(early_kernel, out_shape=(jax.ShapeDtypeStruct((SLAB, kinds...  8.26 us
    pallas_call x1, Pallas kernels, attend(): pl.pallas_call(functools.partial(attend_kernel, full_width), out_shape=(j...  6.14 us
    pallas_call x1, Pallas kernels, output(): pl.pallas_call(out_kernel, out_shape=jax.ShapeDtypeStruct((share, count),...  3.83 us
    pallas_call x1, Pallas kernels, collect(): pl.pallas_call(collect_kernel, out_shape=jax.ShapeDtypeStruct((2, 2 * SLA...  3.82 us
    pallas_call x1, Pallas kernels, norm(): pl.pallas_call(norm_kernel, out_shape=jax.ShapeDtypeStruct(shape, jnp.bfl...  3.56 us
  transfers between devices with their start and end apart: 34, of which 16 were waited for; matrix products, arithmetic and copies ran while one was open for 5% of the time, Pallas kernels for 15%

profile of v16, /device:TPU:9, one launch (start us, length us, event | category | flops | bytes accessed | tf_op | source)
XLA Modules:
  0.0 167.2 jit_solution(3247768617540937913)
XLA Ops:
  0.0 2.1 %pad_bitcast_fusion = (bf16[1,208,1024]{2,1,0:T(8,128)(2,1)}, bf16[208,1024]{1,0:T(8,128)(2,1)}) fusion(bf16[200,1024]{1,0:T(8,128)(2,1)} %bitcast.43), kind=kLoop, calls=%fused_computation.49 | loop fusion | bytes 1261568 | tf_op jit(solution)/shard_map/stack | solution.py:517
  2.2 2.5 %collective-permute-start.1 = (bf16[208,1024]{1,0:T(8,128)(2,1)}, bf16[208,1024]{1,0:T(8,128)(2,1)}, u32[]{:S(2)}, u32[]{:S(2)}) collective-permute-start(bf16[208,1024]{1,0:T(8,128)(2,1)} %get-tuple-element.115), channel_id=1, source_target_pairs={{0,16},{1,17},{2,18},{3,19},{4,20},{5,21},{6,22},{7,23},{8,24},{9,... | collective-permute-start | bytes 1277960 | tf_op jit(solution)/shard_map/ppermute | solution.py:109
  5.6 2.3 %collective-permute-start.3 = (bf16[3,200,256]{2,1,0:T(8,128)(2,1)}, bf16[3,200,256]{2,1,0:T(8,128)(2,1)S(1)}, u32[]{:S(2)}, u32[]{:S(2)}) collective-permute-start(bf16[3,200,256]{2,1,0:T(8,128)(2,1)} %get-tuple-element.111), channel_id=1, source_target_pairs={{0,6},{1,7},{2,4},{3,5},{4,2},{5,3},{6,0},{7,1},{8,14},{9,15},{10,... | collective-permute-start | bytes 921608 | tf_op jit(solution)/shard_map/ppermute | solution.py:109
  12.2 3.6 %norm.1.xa = bf16[4,256,896]{2,1,0:T(8,128)(2,1)} custom-call(bf16[256,3200]{1,0:T(8,128)(2,1)} %tokens.1, f32[1,3200]{1,0:T(1,128)} %broadcast_in_dim.34.gain), custom_call_target="tpu_custom_call" | custom-call | tf_op jit(solution)/shard_map/norm/pallas_call | solution.py:168
  15.9 4.4 %collective-permute-done = bf16[208,1024]{1,0:T(8,128)(2,1)S(1)} collective-permute-done((bf16[208,1024]{1,0:T(8,128)(2,1)}, bf16[208,1024]{1,0:T(8,128)(2,1)S(1)}, u32[]{:S(2)}, u32[]{:S(2)}) %collective-permute-start) | collective-permute-done | bytes 426016 | tf_op jit(solution)/shard_map/ppermute | solution.py:109
  20.3 3.1 %collective-permute-done.1 = bf16[208,1024]{1,0:T(8,128)(2,1)} collective-permute-done((bf16[208,1024]{1,0:T(8,128)(2,1)}, bf16[208,1024]{1,0:T(8,128)(2,1)}, u32[]{:S(2)}, u32[]{:S(2)}) %collective-permute-start.1) | collective-permute-done | bytes 426016 | tf_op jit(solution)/shard_map/ppermute | solution.py:109
  26.0 7.3 %collective-permute-done.2 = bf16[208,1024]{1,0:T(8,128)(2,1)} collective-permute-done((bf16[208,1024]{1,0:T(8,128)(2,1)}, bf16[208,1024]{1,0:T(8,128)(2,1)}, u32[]{:S(2)}, u32[]{:S(2)}) %collective-permute-start.2) | collective-permute-done | bytes 426016 | tf_op jit(solution)/shard_map/ppermute | solution.py:109
  33.4 2.5 %collective-permute-start.8 = (bf16[4,256,896]{2,1,0:T(8,128)(2,1)S(1)}, bf16[4,256,896]{2,1,0:T(8,128)(2,1)}, u32[]{:S(2)}, u32[]{:S(2)}) collective-permute-start(bf16[4,256,896]{2,1,0:T(8,128)(2,1)S(1)} %copy-done), channel_id=1, source_target_pairs={{0,2},{1,3},{2,0},{3,1},{4,6},{5,7},{6,4},{7,5},{8,10},{9,11},{10,... | collective-permute-start | bytes 5505032 | tf_op jit(solution)/shard_map/ppermute | solution.py:109
  43.3 45.4 %collective-permute-done.6.near = bf16[3,800,256]{2,1,0:T(8,128)(2,1)} collective-permute-done((bf16[3,800,256]{2,1,0:T(8,128)(2,1)}, bf16[3,800,256]{2,1,0:T(8,128)(2,1)}, u32[]{:S(2)}, u32[]{:S(2)}) %collective-permute-start.6) | collective-permute-done | bytes 1228832 | tf_op jit(solution)/shard_map/ppermute | solution.py:109
  88.7 3.4 %collective-permute-done.7.far = bf16[3,800,256]{2,1,0:T(8,128)(2,1)} collective-permute-done((bf16[3,800,256]{2,1,0:T(8,128)(2,1)}, bf16[3,800,256]{2,1,0:T(8,128)(2,1)}, u32[]{:S(2)}, u32[]{:S(2)}) %collective-permute-start.7) | collective-permute-done | bytes 1228832 | tf_op jit(solution)/shard_map/ppermute | solution.py:109
  92.0 3.8 %collective-permute-done.11.wc0 = bf16[2,208,1024]{2,1,0:T(8,128)(2,1)S(1)} collective-permute-done((bf16[2,208,1024]{2,1,0:T(8,128)(2,1)S(1)}, bf16[2,208,1024]{2,1,0:T(8,128)(2,1)S(1)}, u32[]{:S(2)}, u32[]{:S(2)}) %collective-permute-start.11) | collective-permute-done | bytes 852000 | tf_op jit(solution)/shard_map/ppermute | solution.py:109
  98.7 1.5 collective-permute-done.13.xd
  100.6 8.3 %early.1 = (f32[4,3,256,256]{3,2,1,0:T(8,128)S(1)}, bf16[4,256,896]{2,1,0:T(8,128)(2,1)S(1)}) custom-call(s32[3]{0:T(128)S(1)} %pad_add_fusion.1.place, bf16[4,256,896]{2,1,0:T(8,128)(2,1)S(1)} %copy-done, bf16[4,256,896]{2,1,0:T(8,128)(2,1)} %collective-permute-done.8.xb, bf16[4,256,896]{2,1,0:T(8,128)(2,1)} %collective-permute-done.9.xc, ...), custom_call_target="tpu_custom_call" | custom-call | flops 7549747200 | bytes 8601600 | tf_op jit(solution)/shard_map/early/pallas_call | solution.py:216
  108.9 16.6 %collective-permute-done.12.last = bf16[3,800,256]{2,1,0:T(8,128)(2,1)S(1)} collective-permute-done((bf16[3,800,256]{2,1,0:T(8,128)(2,1)}, bf16[3,800,256]{2,1,0:T(8,128)(2,1)S(1)}, u32[]{:S(2)}, u32[]{:S(2)}) %collective-permute-start.12) | collective-permute-done | bytes 1228832 | tf_op jit(solution)/shard_map/ppermute | solution.py:109
  125.4 2.5 %late.1 = (f32[1024,256]{1,0:T(8,128)S(1)}, bf16[1024,256]{1,0:T(8,128)(2,1)S(1)}, bf16[1024,256]{1,0:T(8,128)(2,1)S(1)}, f32[2,1024]{1,0:T(2,128)S(1)}, bf16[2,...) custom-call(s32[3]{0:T(128)S(1)} %pad_add_fusion.1.place, bf16[4,256,896]{2,1,0:T(8,128)(2,1)S(1)} %get-tuple-element.66.x_last, ...), custom_call_target="tpu_custom_call" | custom-call | flops 1258291200 | bytes 2867200 | tf_op jit(solution)/shard_map/late/pallas_call | solution.py:273
  133.0 1.8 %collective-permute-done.22 = f32[2,1024]{1,0:T(2,128)S(1)} collective-permute-done((f32[2,1024]{1,0:T(2,128)S(1)}, f32[2,1024]{1,0:T(2,128)S(1)}, u32[]{:S(2)}, u32[]{:S(2)}) %collective-permute-start.22) | collective-permute-done | bytes 8224 | tf_op jit(solution)/shard_map/ppermute | solution.py:109
  136.1 1.6 collective-permute-done.23
  138.4 1.8 %collective-permute-start.26 = (bf16[2,208,1024]{2,1,0:T(8,128)(2,1)S(1)}, bf16[2,208,1024]{2,1,0:T(8,128)(2,1)S(1)}, u32[]{:S(2)}, u32[]{:S(2)}) collective-permute-start(bf16[2,208,1024]{2,1,0:T(8,128)(2,1)S(1)} %collective-permute-done.16.wc1), channel_id=1, source_target_pairs={{0,2},{1,3},{2,0},{3,1},{4,6},{5,7},{6,4},{7,5},{8,10},{9,11},{10,... | collective-permute-start | bytes 2555912 | tf_op jit(solution)/shard_map/ppermute | solution.py:109
  141.1 6.1 %attend.1 = (bf16[256,256]{1,0:T(8,128)(2,1)S(1)}, bf16[256,256]{1,0:T(8,128)(2,1)S(1)}, bf16[256,256]{1,0:T(8,128)(2,1)S(1)}, bf16[256,256]{1,0:T(8,128)(2,1)S(1)}) custom-call(s32[3]{0:T(128)S(1)} %pad_add_fusion.1.place, s32[4,2]{1,0:T(4,128)S(1)} %pad_add_fusion.spans, f32[1024,256]{1,0:T(8,128)S(1)} %get-tuple-element.71.query, ...), custom_call_target="tpu_custom_call" | custom-call | flops 21474836480 | bytes 3145728 | tf_op jit(solution)/shard_map/attend/pallas_call | solution.py:376
  149.5 3.2 %collective-permute-start.29 = (bf16[256,256]{1,0:T(8,128)(2,1)S(1)}, bf16[256,256]{1,0:T(8,128)(2,1)S(1)}, u32[]{:S(2)}, u32[]{:S(2)}) collective-permute-start(bf16[256,256]{1,0:T(8,128)(2,1)S(1)} %get-tuple-element.89), channel_id=1, source_target_pairs={{0,7},{1,6},{2,5},{3,4},{4,3},{5,2},{6,1},{7,0},{8,15},{9,14},{10,... | collective-permute-start | bytes 393224 | tf_op jit(solution)/shard_map/ppermute | solution.py:109
  154.0 1.9 %collective-permute-start.31 = (bf16[256,256]{1,0:T(8,128)(2,1)S(1)}, bf16[256,256]{1,0:T(8,128)(2,1)S(1)}, u32[]{:S(2)}, u32[]{:S(2)}) collective-permute-start(bf16[256,256]{1,0:T(8,128)(2,1)S(1)} %get-tuple-element.90), channel_id=1, source_target_pairs={{0,3},{1,2},{2,1},{3,0},{4,7},{5,6},{6,5},{7,4},{8,11},{9,10},{10,... | collective-permute-start | bytes 393224 | tf_op jit(solution)/shard_map/ppermute | solution.py:109
  157.2 3.8 %collect.1.w = bf16[2,1664,1024]{2,1,0:T(8,128)(2,1)S(1)} custom-call(bf16[2,208,1024]{2,1,0:T(8,128)(2,1)S(1)} %get-tuple-element.109.wa0, bf16[2,208,1024]{2,1,0:T(8,128)(2,1)S(1)} %collective-permute-done.18.wb0, bf16[2,208,1024]{2,1,0:T(8,128)(2,1)S(1)} %collective-permute-done.11.wc0, bf16[2,208,1024]{2,1,0:T(8,128)(2,1)S(1)} %collective-permute-done.19.wd0, ...), custom_call_target="tpu_custom_call" | custom-call | bytes 13631488 | tf_op jit(solution)/shard_map/collect/pallas_call | solution.py:411
  161.0 2.3 %collective-permute-done.32.c21 = bf16[256,256]{1,0:T(8,128)(2,1)S(1)} collective-permute-done((bf16[256,256]{1,0:T(8,128)(2,1)S(1)}, bf16[256,256]{1,0:T(8,128)(2,1)S(1)}, u32[]{:S(2)}, u32[]{:S(2)}) %collective-permute-start.32) | collective-permute-done | bytes 131104 | tf_op jit(solution)/shard_map/ppermute | solution.py:109
  163.3 3.8 %output.1 = bf16[1600,256]{1,0:T(8,128)(2,1)} custom-call(s32[3]{0:T(128)S(1)} %pad_add_fusion.1.place, bf16[256,256]{1,0:T(8,128)(2,1)S(1)} %collective-permute-done.27.c20, bf16[256,256]{1,0:T(8,128)(2,1)S(1)} %collective-permute-done.28.c01, bf16[256,256]{1,0:T(8,128)(2,1)S(1)} %collective-permute-done.29.c31, ...), custom_call_target="tpu_custom_call" | custom-call | flops 1677721600 | bytes 6553600 | tf_op jit(solution)/shard_map/output/pallas_call | solution.py:450
  (90 shorter events, 31.5 us)
Async XLA Ops:
  2.2 18.1 %collective-permute-start = (bf16[208,1024]{1,0:T(8,128)(2,1)}, bf16[208,1024]{1,0:T(8,128)(2,1)S(1)}, u32[]{:S(2)}, u32[]{:S(2)}) collective-permute-start(bf16[208,1024]{1,0:T(8,128)(2,1)} %get-tuple-element.115), channel_id=1, source_target_pairs={{0,8},{1,9},{2,10},{3,11},{4,12},{5,13},{6,14},{7,15},{8,0},{9,1},... | collective-permute-start | bytes 1277960 | tf_op jit(solution)/shard_map/ppermute | solution.py:109
  2.2 21.2 %collective-permute-start.1 = (bf16[208,1024]{1,0:T(8,128)(2,1)}, bf16[208,1024]{1,0:T(8,128)(2,1)}, u32[]{:S(2)}, u32[]{:S(2)}) collective-permute-start(bf16[208,1024]{1,0:T(8,128)(2,1)} %get-tuple-element.115), channel_id=1, source_target_pairs={{0,16},{1,17},{2,18},{3,19},{4,20},{5,21},{6,22},{7,23},{8,24},{9,... | collective-permute-start | bytes 1277960 | tf_op jit(solution)/shard_map/ppermute | solution.py:109
  5.6 17.7 %collective-permute-start.3 = (bf16[3,200,256]{2,1,0:T(8,128)(2,1)}, bf16[3,200,256]{2,1,0:T(8,128)(2,1)S(1)}, u32[]{:S(2)}, u32[]{:S(2)}) collective-permute-start(bf16[3,200,256]{2,1,0:T(8,128)(2,1)} %get-tuple-element.111), channel_id=1, source_target_pairs={{0,6},{1,7},{2,4},{3,5},{4,2},{5,3},{6,0},{7,1},{8,14},{9,15},{10,... | collective-permute-start | bytes 921608 | tf_op jit(solution)/shard_map/ppermute | solution.py:109
  8.0 15.4 %collective-permute-start.4 = (bf16[3,200,256]{2,1,0:T(8,128)(2,1)}, bf16[3,200,256]{2,1,0:T(8,128)(2,1)}, u32[]{:S(2)}, u32[]{:S(2)}) collective-permute-start(bf16[3,200,256]{2,1,0:T(8,128)(2,1)} %get-tuple-element.112), channel_id=1, source_target_pairs={{0,4},{1,5},{2,6},{3,7},{4,0},{5,1},{6,2},{7,3},{8,12},{9,13},{10,... | collective-permute-start | bytes 921608 | tf_op jit(solution)/shard_map/ppermute | solution.py:109
  8.2 15.1 %collective-permute-start.5 = (bf16[3,200,256]{2,1,0:T(8,128)(2,1)}, bf16[3,200,256]{2,1,0:T(8,128)(2,1)}, u32[]{:S(2)}, u32[]{:S(2)}) collective-permute-start(bf16[3,200,256]{2,1,0:T(8,128)(2,1)} %get-tuple-element.113), channel_id=1, source_target_pairs={{0,2},{1,3},{2,0},{3,1},{4,6},{5,7},{6,4},{7,5},{8,10},{9,11},{10,... | collective-permute-start | bytes 921608 | tf_op jit(solution)/shard_map/ppermute | solution.py:109
  23.3 10.0 %collective-permute-start.2 = (bf16[208,1024]{1,0:T(8,128)(2,1)}, bf16[208,1024]{1,0:T(8,128)(2,1)}, u32[]{:S(2)}, u32[]{:S(2)}) collective-permute-start(bf16[208,1024]{1,0:T(8,128)(2,1)} %collective-permute-done.1), channel_id=1, source_target_pairs={{0,8},{1,9},{2,10},{3,11},{4,12},{5,13},{6,14},{7,15},{8,0},{9,1},... | collective-permute-start | bytes 1277960 | tf_op jit(solution)/shard_map/ppermute | solution.py:109
  35.9 56.1 %collective-permute-start.9 = (bf16[4,256,896]{2,1,0:T(8,128)(2,1)S(1)}, bf16[4,256,896]{2,1,0:T(8,128)(2,1)}, u32[]{:S(2)}, u32[]{:S(2)}) collective-permute-start(bf16[4,256,896]{2,1,0:T(8,128)(2,1)S(1)} %copy-done), channel_id=1, source_target_pairs={{0,4},{1,5},{2,6},{3,7},{4,0},{5,1},{6,2},{7,3},{8,12},{9,13},{10,... | collective-permute-start | bytes 5505032 | tf_op jit(solution)/shard_map/ppermute | solution.py:109
  37.1 51.5 %collective-permute-start.6 = (bf16[3,800,256]{2,1,0:T(8,128)(2,1)}, bf16[3,800,256]{2,1,0:T(8,128)(2,1)}, u32[]{:S(2)}, u32[]{:S(2)}) collective-permute-start(bf16[3,800,256]{2,1,0:T(8,128)(2,1)} %pad_maximum_fusion.own), channel_id=1, source_target_pairs={{0,8},{1,9},{2,10},{3,11},{4,12},{5,13},{6,14},{7,15},{8,0},{9,1},... | collective-permute-start | bytes 3686408 | tf_op jit(solution)/shard_map/ppermute | solution.py:109
  37.1 54.9 %collective-permute-start.7 = (bf16[3,800,256]{2,1,0:T(8,128)(2,1)}, bf16[3,800,256]{2,1,0:T(8,128)(2,1)}, u32[]{:S(2)}, u32[]{:S(2)}) collective-permute-start(bf16[3,800,256]{2,1,0:T(8,128)(2,1)} %pad_maximum_fusion.own), channel_id=1, source_target_pairs={{0,16},{1,17},{2,18},{3,19},{4,20},{5,21},{6,22},{7,23},{8,24},{9,... | collective-permute-start | bytes 3686408 | tf_op jit(solution)/shard_map/ppermute | solution.py:109
  40.8 51.2 %collective-permute-start.10 = (bf16[2,208,1024]{2,1,0:T(8,128)(2,1)S(1)}, bf16[2,208,1024]{2,1,0:T(8,128)(2,1)S(1)}, u32[]{:S(2)}, u32[]{:S(2)}) collective-permute-start(bf16[2,208,1024]{2,1,0:T(8,128)(2,1)S(1)} %get-tuple-element.110), channel_id=1, source_target_pairs={{0,1},{1,0},{2,3},{3,2},{4,5},{5,4},{6,7},{7,6},{8,9},{9,8},{10,11... | collective-permute-start | bytes 2555912 | tf_op jit(solution)/shard_map/ppermute | solution.py:109
  42.1 53.7 %collective-permute-start.11 = (bf16[2,208,1024]{2,1,0:T(8,128)(2,1)S(1)}, bf16[2,208,1024]{2,1,0:T(8,128)(2,1)S(1)}, u32[]{:S(2)}, u32[]{:S(2)}) collective-permute-start(bf16[2,208,1024]{2,1,0:T(8,128)(2,1)S(1)} %get-tuple-element.109.wa0), channel_id=1, source_target_pairs={{0,4},{1,5},{2,6},{3,7},{4,0},{5,1},{6,2},{7,3},{8,12},{9,13},{10,... | collective-permute-start | bytes 2555912 | tf_op jit(solution)/shard_map/ppermute | solution.py:109
  96.6 28.9 %collective-permute-start.12 = (bf16[3,800,256]{2,1,0:T(8,128)(2,1)}, bf16[3,800,256]{2,1,0:T(8,128)(2,1)S(1)}, u32[]{:S(2)}, u32[]{:S(2)}) collective-permute-start(bf16[3,800,256]{2,1,0:T(8,128)(2,1)} %collective-permute-done.7.far), channel_id=1, source_target_pairs={{0,8},{1,9},{2,10},{3,11},{4,12},{5,13},{6,14},{7,15},{8,0},{9,1},... | collective-permute-start | bytes 3686408 | tf_op jit(solution)/shard_map/ppermute | solution.py:109
  96.6 31.4 %collective-permute-start.18 = (bf16[2,208,1024]{2,1,0:T(8,128)(2,1)S(1)}, bf16[2,208,1024]{2,1,0:T(8,128)(2,1)S(1)}, u32[]{:S(2)}, u32[]{:S(2)}) collective-permute-start(bf16[2,208,1024]{2,1,0:T(8,128)(2,1)S(1)} %get-tuple-element.109.wa0), channel_id=1, source_target_pairs={{0,2},{1,3},{2,0},{3,1},{4,6},{5,7},{6,4},{7,5},{8,10},{9,11},{10,... | collective-permute-start | bytes 2555912 | tf_op jit(solution)/shard_map/ppermute | solution.py:109
  96.9 31.8 %collective-permute-start.16 = (bf16[2,208,1024]{2,1,0:T(8,128)(2,1)S(1)}, bf16[2,208,1024]{2,1,0:T(8,128)(2,1)S(1)}, u32[]{:S(2)}, u32[]{:S(2)}) collective-permute-start(bf16[2,208,1024]{2,1,0:T(8,128)(2,1)S(1)} %collective-permute-done.10.wa1), channel_id=1, source_target_pairs={{0,4},{1,5},{2,6},{3,7},{4,0},{5,1},{6,2},{7,3},{8,12},{9,13},{10,... | collective-permute-start | bytes 2555912 | tf_op jit(solution)/shard_map/ppermute | solution.py:109
  98.2 30.6 %collective-permute-start.17 = (bf16[2,208,1024]{2,1,0:T(8,128)(2,1)S(1)}, bf16[2,208,1024]{2,1,0:T(8,128)(2,1)S(1)}, u32[]{:S(2)}, u32[]{:S(2)}) collective-permute-start(bf16[2,208,1024]{2,1,0:T(8,128)(2,1)S(1)} %collective-permute-done.10.wa1), channel_id=1, source_target_pairs={{0,2},{1,3},{2,0},{3,1},{4,6},{5,7},{6,4},{7,5},{8,10},{9,11},{10,... | collective-permute-start | bytes 2555912 | tf_op jit(solution)/shard_map/ppermute | solution.py:109
  100.2 28.5 %collective-permute-start.19 = (bf16[2,208,1024]{2,1,0:T(8,128)(2,1)S(1)}, bf16[2,208,1024]{2,1,0:T(8,128)(2,1)S(1)}, u32[]{:S(2)}, u32[]{:S(2)}) collective-permute-start(bf16[2,208,1024]{2,1,0:T(8,128)(2,1)S(1)} %collective-permute-done.11.wc0), channel_id=1, source_target_pairs={{0,2},{1,3},{2,0},{3,1},{4,6},{5,7},{6,4},{7,5},{8,10},{9,11},{10,... | collective-permute-start | bytes 2555912 | tf_op jit(solution)/shard_map/ppermute | solution.py:109
  127.9 12.7 %collective-permute-start.14 = (bf16[2,512,256]{2,1,0:T(8,128)(2,1)S(1)}, bf16[2,512,256]{2,1,0:T(8,128)(2,1)S(1)}, u32[]{:S(2)}, u32[]{:S(2)}) collective-permute-start(bf16[2,512,256]{2,1,0:T(8,128)(2,1)S(1)} %get-tuple-element.74), channel_id=1, source_target_pairs={{0,8},{1,9},{2,10},{3,11},{4,12},{5,13},{6,14},{7,15},{8,0},{9,1},... | collective-permute-start | bytes 1572872 | tf_op jit(solution)/shard_map/ppermute | solution.py:109
  128.0 12.6 %collective-permute-start.15 = (bf16[2,512,256]{2,1,0:T(8,128)(2,1)S(1)}, bf16[2,512,256]{2,1,0:T(8,128)(2,1)S(1)}, u32[]{:S(2)}, u32[]{:S(2)}) collective-permute-start(bf16[2,512,256]{2,1,0:T(8,128)(2,1)S(1)} %get-tuple-element.75), channel_id=1, source_target_pairs={{0,2},{1,3},{2,0},{3,1},{4,6},{5,7},{6,4},{7,5},{8,16},{9,17},{10,... | collective-permute-start | bytes 1572872 | tf_op jit(solution)/shard_map/ppermute | solution.py:109
  138.4 8.9 %collective-permute-start.26 = (bf16[2,208,1024]{2,1,0:T(8,128)(2,1)S(1)}, bf16[2,208,1024]{2,1,0:T(8,128)(2,1)S(1)}, u32[]{:S(2)}, u32[]{:S(2)}) collective-permute-start(bf16[2,208,1024]{2,1,0:T(8,128)(2,1)S(1)} %collective-permute-done.16.wc1), channel_id=1, source_target_pairs={{0,2},{1,3},{2,0},{3,1},{4,6},{5,7},{6,4},{7,5},{8,10},{9,11},{10,... | collective-permute-start | bytes 2555912 | tf_op jit(solution)/shard_map/ppermute | solution.py:109
  148.2 7.7 %collective-permute-start.28 = (bf16[256,256]{1,0:T(8,128)(2,1)S(1)}, bf16[256,256]{1,0:T(8,128)(2,1)S(1)}, u32[]{:S(2)}, u32[]{:S(2)}) collective-permute-start(bf16[256,256]{1,0:T(8,128)(2,1)S(1)} %get-tuple-element.88.c00), channel_id=1, source_target_pairs={{0,1},{1,0},{2,3},{3,2},{4,5},{5,4},{6,7},{7,6},{8,9},{9,8},{10,11... | collective-permute-start | bytes 393224 | tf_op jit(solution)/shard_map/ppermute | solution.py:109
  149.5 11.5 %collective-permute-start.29 = (bf16[256,256]{1,0:T(8,128)(2,1)S(1)}, bf16[256,256]{1,0:T(8,128)(2,1)S(1)}, u32[]{:S(2)}, u32[]{:S(2)}) collective-permute-start(bf16[256,256]{1,0:T(8,128)(2,1)S(1)} %get-tuple-element.89), channel_id=1, source_target_pairs={{0,7},{1,6},{2,5},{3,4},{4,3},{5,2},{6,1},{7,0},{8,15},{9,14},{10,... | collective-permute-start | bytes 393224 | tf_op jit(solution)/shard_map/ppermute | solution.py:109
  152.7 8.3 %collective-permute-start.30 = (bf16[256,256]{1,0:T(8,128)(2,1)S(1)}, bf16[256,256]{1,0:T(8,128)(2,1)S(1)}, u32[]{:S(2)}, u32[]{:S(2)}) collective-permute-start(bf16[256,256]{1,0:T(8,128)(2,1)S(1)} %get-tuple-element.89), channel_id=1, source_target_pairs={{0,6},{1,7},{2,4},{3,5},{4,2},{5,3},{6,0},{7,1},{8,14},{9,15},{10,... | collective-permute-start | bytes 393224 | tf_op jit(solution)/shard_map/ppermute | solution.py:109
  152.8 10.6 %collective-permute-start.32 = (bf16[256,256]{1,0:T(8,128)(2,1)S(1)}, bf16[256,256]{1,0:T(8,128)(2,1)S(1)}, u32[]{:S(2)}, u32[]{:S(2)}) collective-permute-start(bf16[256,256]{1,0:T(8,128)(2,1)S(1)} %get-tuple-element.87), channel_id=1, source_target_pairs={{0,5},{1,4},{2,7},{3,6},{4,1},{5,0},{6,3},{7,2},{8,13},{9,12},{10,... | collective-permute-start | bytes 393224 | tf_op jit(solution)/shard_map/ppermute | solution.py:109
  155.9 7.4 %collective-permute-start.33 = (bf16[256,256]{1,0:T(8,128)(2,1)S(1)}, bf16[256,256]{1,0:T(8,128)(2,1)S(1)}, u32[]{:S(2)}, u32[]{:S(2)}) collective-permute-start(bf16[256,256]{1,0:T(8,128)(2,1)S(1)} %get-tuple-element.90), channel_id=1, source_target_pairs={{0,2},{1,3},{2,0},{3,1},{4,6},{5,7},{6,4},{7,5},{8,10},{9,11},{10,... | collective-permute-start | bytes 393224 | tf_op jit(solution)/shard_map/ppermute | solution.py:109
  (17 other events, 97.6 us)

commit v17 on v16

--- a/solution.py
+++ b/solution.py
@@ -492,7 +492,7 @@
     cut = [lax.dynamic_slice_in_dim(by_kind, (q ^ r) * width, width, 2) for r in range(SLAB)]
     got = [cut[0]] + [in_slab(cut[r], r) for r in range(1, SLAB)]
     x0 = norm(tokens, norm_gain, slabs)
-    out_own = jnp.pad(jnp.transpose(out_weight), ((0, -out_weight.shape[1] % 16), (0, 0)))
+    out_own = jnp.transpose(out_weight)
     own = rows_of_slab(q, got)
     out_near, out_far = even_pair(out_own), half_pair(out_own)
     gains = [lax.dynamic_slice_in_dim(g, q * width, width, 0)[None] for g in (q_gain, k_gain)]
@@ -511,12 +511,13 @@
     out_last = even_pair(out_far)
     x2 = in_slab(x0, 2)
     out_last, own, x0 = tied(out_last, own, x0)
-    near, far = even_pair(own), half_pair(own)
+    far, near = half_pair(own), even_pair(own)
     x1 = in_slab(x0, 1)
     out_last, x1 = tied(out_last, x1)
     close, away = jnp.stack([out_own, out_near]), jnp.stack([out_far, out_last])
-    keep, give = jnp.where(home, close, away), jnp.where(home, away, close)
-    got = across(give)
+    pad = ((0, 0), (0, -close.shape[1] % 16), (0, 0))
+    keep = jnp.pad(jnp.where(home, close, away), pad)
+    got = across(jnp.pad(jnp.where(home, away, close), pad))
     keep_x = in_slab(keep, 2)
     near, far, x1, x2, got, keep_x = tied(near, far, x1, x2, got, keep_x)
     last = even_pair(far)

time: 168 us -> 165 us (0.982)
  waiting for transfers between devices: 94.1 us -> 91.6 us
    ppermute x34, waiting for transfers between devices: 94.1 us -> 91.6 us  [permuted(): return lax.ppermute(x, ('seq', 'tp'), pairs)]
    another operation x1 -> x0, local copies, waits for them, and re-layouts: 2.15 us -> none  [slab_plan(): jnp.stack([out_own, out_near])]
  transfers between devices with their start and end apart: 34 -> 34, of which waited for: 16 -> 17; matrix products, arithmetic and copies ran while one was open for 5% -> 6% of each run, Pallas kernels for 15% -> 15%
where the time goes in v17:
time: 165 us; the launch traced here: 163 us
  waiting for transfers between devices  91.6 us (56%)
  starting transfers between devices  33.7 us (20%)
  Pallas kernels  27.7 us (17%)
  local copies, waits for them, and re-layouts  5.71 us (3%)
  other arithmetic  4.53 us (3%)
    ppermute x34, waiting for transfers between devices, permuted(): return lax.ppermute(x, ('seq', 'tp'), pairs)  91.6 us
    ppermute x34, starting transfers between devices, permuted(): return lax.ppermute(x, ('seq', 'tp'), pairs)  33.7 us
    pallas_call x1, Pallas kernels, early(): pl.pallas_call(early_kernel, out_shape=(jax.ShapeDtypeStruct((SLAB, kinds...  8.26 us
    pallas_call x1, Pallas kernels, attend(): pl.pallas_call(functools.partial(attend_kernel, full_width), out_shape=(j...  5.81 us
    pallas_call x1, Pallas kernels, collect(): pl.pallas_call(collect_kernel, out_shape=jax.ShapeDtypeStruct((2, 2 * SLA...  3.82 us
    pallas_call x1, Pallas kernels, output(): pl.pallas_call(out_kernel, out_shape=jax.ShapeDtypeStruct((share, count),...  3.82 us
    pallas_call x1, Pallas kernels, norm(): pl.pallas_call(norm_kernel, out_shape=jax.ShapeDtypeStruct(shape, jnp.bfl...  3.54 us
  transfers between devices with their start and end apart: 34, of which 17 were waited for; matrix products, arithmetic and copies ran while one was open for 6% of the time, Pallas kernels for 15%

profile of v17, /device:TPU:9, one launch (start us, length us, event | category | flops | bytes accessed | tf_op | source)
XLA Modules:
  0.0 163.5 jit_solution(9792538464040172976)
XLA Ops:
  0.0 2.5 %collective-permute-start.1 = (bf16[200,1024]{1,0:T(8,128)(2,1)}, bf16[200,1024]{1,0:T(8,128)(2,1)}, u32[]{:S(2)}, u32[]{:S(2)}) collective-permute-start(bf16[200,1024]{1,0:T(8,128)(2,1)} %bitcast.43), channel_id=1, source_target_pairs={{0,16},{1,17},{2,18},{3,19},{4,20},{5,21},{6,22},{7,23},{8,24},{9,... | collective-permute-start | bytes 1228808 | tf_op jit(solution)/shard_map/ppermute | solution.py:109
  2.5 2.1 %dynamic-slice_bitcast_fusion.2 = (bf16[3,200,256]{2,1,0:T(8,128)(2,1)}, bf16[3,200,256]{2,1,0:T(8,128)(2,1)}, bf16[3,200,256]{2,1,0:T(8,128)(2,1)}) fusion(bf16[200,3,1024]{2,0,1:T(8,128)(2,1)} %param.10, s32[]{:T(128)S(6)} %select_n.149, s32[]{:T(128)S(6)} %select_n.151, s32[]{:T(128)S(6)} %select_n.153), kind=kLoop, calls=%fused_computation.16 | loop fusion | bytes 1843212 | tf_op jit(solution)/shard_map/dynamic_slice | solution.py:492
  4.6 2.3 %collective-permute-start.3 = (bf16[3,200,256]{2,1,0:T(8,128)(2,1)}, bf16[3,200,256]{2,1,0:T(8,128)(2,1)}, u32[]{:S(2)}, u32[]{:S(2)}) collective-permute-start(bf16[3,200,256]{2,1,0:T(8,128)(2,1)} %get-tuple-element.111), channel_id=1, source_target_pairs={{0,6},{1,7},{2,4},{3,5},{4,2},{5,3},{6,0},{7,1},{8,14},{9,15},{10,... | collective-permute-start | bytes 921608 | tf_op jit(solution)/shard_map/ppermute | solution.py:109
  11.2 3.5 %norm.1.xa = bf16[4,256,896]{2,1,0:T(8,128)(2,1)} custom-call(bf16[256,3200]{1,0:T(8,128)(2,1)} %tokens.1, f32[1,3200]{1,0:T(1,128)} %broadcast_in_dim.34.gain), custom_call_target="tpu_custom_call" | custom-call | tf_op jit(solution)/shard_map/norm/pallas_call | solution.py:168
  14.9 2.6 %collective-permute-done = bf16[200,1024]{1,0:T(8,128)(2,1)} collective-permute-done((bf16[200,1024]{1,0:T(8,128)(2,1)}, bf16[200,1024]{1,0:T(8,128)(2,1)}, u32[]{:S(2)}, u32[]{:S(2)}) %collective-permute-start) | collective-permute-done | bytes 409632 | tf_op jit(solution)/shard_map/ppermute | solution.py:109
  17.4 3.1 %collective-permute-done.1 = bf16[200,1024]{1,0:T(8,128)(2,1)} collective-permute-done((bf16[200,1024]{1,0:T(8,128)(2,1)}, bf16[200,1024]{1,0:T(8,128)(2,1)}, u32[]{:S(2)}, u32[]{:S(2)}) %collective-permute-start.1) | collective-permute-done | bytes 409632 | tf_op jit(solution)/shard_map/ppermute | solution.py:109
  21.9 1.6 fusion.1
  24.6 5.4 %collective-permute-done.2 = bf16[200,1024]{1,0:T(8,128)(2,1)S(1)} collective-permute-done((bf16[200,1024]{1,0:T(8,128)(2,1)}, bf16[200,1024]{1,0:T(8,128)(2,1)S(1)}, u32[]{:S(2)}, u32[]{:S(2)}) %collective-permute-start.2) | collective-permute-done | bytes 409632 | tf_op jit(solution)/shard_map/ppermute | solution.py:109
  30.1 2.5 %collective-permute-start.8 = (bf16[4,256,896]{2,1,0:T(8,128)(2,1)S(1)}, bf16[4,256,896]{2,1,0:T(8,128)(2,1)}, u32[]{:S(2)}, u32[]{:S(2)}) collective-permute-start(bf16[4,256,896]{2,1,0:T(8,128)(2,1)S(1)} %copy-done), channel_id=1, source_target_pairs={{0,2},{1,3},{2,0},{3,1},{4,6},{5,7},{6,4},{7,5},{8,10},{9,11},{10,... | collective-permute-start | bytes 5505032 | tf_op jit(solution)/shard_map/ppermute | solution.py:109
  40.2 45.2 %collective-permute-done.6.near = bf16[3,800,256]{2,1,0:T(8,128)(2,1)} collective-permute-done((bf16[3,800,256]{2,1,0:T(8,128)(2,1)}, bf16[3,800,256]{2,1,0:T(8,128)(2,1)}, u32[]{:S(2)}, u32[]{:S(2)}) %collective-permute-start.6) | collective-permute-done | bytes 1228832 | tf_op jit(solution)/shard_map/ppermute | solution.py:109
  85.3 3.4 %collective-permute-done.7.far = bf16[3,800,256]{2,1,0:T(8,128)(2,1)} collective-permute-done((bf16[3,800,256]{2,1,0:T(8,128)(2,1)}, bf16[3,800,256]{2,1,0:T(8,128)(2,1)}, u32[]{:S(2)}, u32[]{:S(2)}) %collective-permute-start.7) | collective-permute-done | bytes 1228832 | tf_op jit(solution)/shard_map/ppermute | solution.py:109
  88.7 3.8 %collective-permute-done.11.wc0 = bf16[2,208,1024]{2,1,0:T(8,128)(2,1)S(1)} collective-permute-done((bf16[2,208,1024]{2,1,0:T(8,128)(2,1)S(1)}, bf16[2,208,1024]{2,1,0:T(8,128)(2,1)S(1)}, u32[]{:S(2)}, u32[]{:S(2)}) %collective-permute-start.11) | collective-permute-done | bytes 852000 | tf_op jit(solution)/shard_map/ppermute | solution.py:109
  97.3 8.3 %early.1 = (f32[4,3,256,256]{3,2,1,0:T(8,128)S(1)}, bf16[4,256,896]{2,1,0:T(8,128)(2,1)S(1)}) custom-call(s32[3]{0:T(128)S(1)} %pad_add_fusion.1.place, bf16[4,256,896]{2,1,0:T(8,128)(2,1)S(1)} %copy-done, bf16[4,256,896]{2,1,0:T(8,128)(2,1)} %collective-permute-done.8.xb, bf16[4,256,896]{2,1,0:T(8,128)(2,1)} %collective-permute-done.9.xc, ...), custom_call_target="tpu_custom_call" | custom-call | flops 7549747200 | bytes 8601600 | tf_op jit(solution)/shard_map/early/pallas_call | solution.py:216
  105.5 16.6 %collective-permute-done.12.last = bf16[3,800,256]{2,1,0:T(8,128)(2,1)S(1)} collective-permute-done((bf16[3,800,256]{2,1,0:T(8,128)(2,1)}, bf16[3,800,256]{2,1,0:T(8,128)(2,1)S(1)}, u32[]{:S(2)}, u32[]{:S(2)}) %collective-permute-start.12) | collective-permute-done | bytes 1228832 | tf_op jit(solution)/shard_map/ppermute | solution.py:109
  122.1 2.5 %late.1 = (f32[1024,256]{1,0:T(8,128)S(1)}, bf16[1024,256]{1,0:T(8,128)(2,1)S(1)}, bf16[1024,256]{1,0:T(8,128)(2,1)S(1)}, f32[2,1024]{1,0:T(2,128)S(1)}, bf16[2,...) custom-call(s32[3]{0:T(128)S(1)} %pad_add_fusion.1.place, bf16[4,256,896]{2,1,0:T(8,128)(2,1)S(1)} %get-tuple-element.66.x_last, ...), custom_call_target="tpu_custom_call" | custom-call | flops 1258291200 | bytes 2867200 | tf_op jit(solution)/shard_map/late/pallas_call | solution.py:273
  129.7 1.8 %collective-permute-done.22 = f32[2,1024]{1,0:T(2,128)S(1)} collective-permute-done((f32[2,1024]{1,0:T(2,128)S(1)}, f32[2,1024]{1,0:T(2,128)S(1)}, u32[]{:S(2)}, u32[]{:S(2)}) %collective-permute-start.22) | collective-permute-done | bytes 8224 | tf_op jit(solution)/shard_map/ppermute | solution.py:109
  132.8 1.6 collective-permute-done.23
  135.1 1.8 %collective-permute-start.26 = (bf16[2,208,1024]{2,1,0:T(8,128)(2,1)S(1)}, bf16[2,208,1024]{2,1,0:T(8,128)(2,1)S(1)}, u32[]{:S(2)}, u32[]{:S(2)}) collective-permute-start(bf16[2,208,1024]{2,1,0:T(8,128)(2,1)S(1)} %collective-permute-done.16.wc1), channel_id=1, source_target_pairs={{0,2},{1,3},{2,0},{3,1},{4,6},{5,7},{6,4},{7,5},{8,10},{9,11},{10,... | collective-permute-start | bytes 2555912 | tf_op jit(solution)/shard_map/ppermute | solution.py:109
  137.8 5.8 %attend.1 = (bf16[256,256]{1,0:T(8,128)(2,1)S(1)}, bf16[256,256]{1,0:T(8,128)(2,1)S(1)}, bf16[256,256]{1,0:T(8,128)(2,1)S(1)}, bf16[256,256]{1,0:T(8,128)(2,1)S(1)}) custom-call(s32[3]{0:T(128)S(1)} %pad_add_fusion.1.place, s32[4,2]{1,0:T(4,128)S(1)} %pad_add_fusion.spans, f32[1024,256]{1,0:T(8,128)S(1)} %get-tuple-element.71.query, ...), custom_call_target="tpu_custom_call" | custom-call | flops 21474836480 | bytes 3145728 | tf_op jit(solution)/shard_map/attend/pallas_call | solution.py:376
  145.8 3.2 %collective-permute-start.29 = (bf16[256,256]{1,0:T(8,128)(2,1)S(1)}, bf16[256,256]{1,0:T(8,128)(2,1)S(1)}, u32[]{:S(2)}, u32[]{:S(2)}) collective-permute-start(bf16[256,256]{1,0:T(8,128)(2,1)S(1)} %get-tuple-element.89), channel_id=1, source_target_pairs={{0,7},{1,6},{2,5},{3,4},{4,3},{5,2},{6,1},{7,0},{8,15},{9,14},{10,... | collective-permute-start | bytes 393224 | tf_op jit(solution)/shard_map/ppermute | solution.py:109
  150.4 1.9 %collective-permute-start.31 = (bf16[256,256]{1,0:T(8,128)(2,1)S(1)}, bf16[256,256]{1,0:T(8,128)(2,1)S(1)}, u32[]{:S(2)}, u32[]{:S(2)}) collective-permute-start(bf16[256,256]{1,0:T(8,128)(2,1)S(1)} %get-tuple-element.90), channel_id=1, source_target_pairs={{0,3},{1,2},{2,1},{3,0},{4,7},{5,6},{6,5},{7,4},{8,11},{9,10},{10,... | collective-permute-start | bytes 393224 | tf_op jit(solution)/shard_map/ppermute | solution.py:109
  153.5 3.8 %collect.1.w = bf16[2,1664,1024]{2,1,0:T(8,128)(2,1)S(1)} custom-call(bf16[2,208,1024]{2,1,0:T(8,128)(2,1)S(1)} %pad.13.wa0, bf16[2,208,1024]{2,1,0:T(8,128)(2,1)S(1)} %collective-permute-done.18.wb0, bf16[2,208,1024]{2,1,0:T(8,128)(2,1)S(1)} %collective-permute-done.11.wc0, bf16[2,208,1024]{2,1,0:T(8,128)(2,1)S(1)} %collective-permute-done.19.wd0, ...), custom_call_target="tpu_custom_call" | custom-call | bytes 13631488 | tf_op jit(solution)/shard_map/collect/pallas_call | solution.py:411
  157.4 2.3 %collective-permute-done.32.c21 = bf16[256,256]{1,0:T(8,128)(2,1)S(1)} collective-permute-done((bf16[256,256]{1,0:T(8,128)(2,1)S(1)}, bf16[256,256]{1,0:T(8,128)(2,1)S(1)}, u32[]{:S(2)}, u32[]{:S(2)}) %collective-permute-start.32) | collective-permute-done | bytes 131104 | tf_op jit(solution)/shard_map/ppermute | solution.py:109
  159.7 3.8 %output.1 = bf16[1600,256]{1,0:T(8,128)(2,1)} custom-call(s32[3]{0:T(128)S(1)} %pad_add_fusion.1.place, bf16[256,256]{1,0:T(8,128)(2,1)S(1)} %collective-permute-done.27.c20, bf16[256,256]{1,0:T(8,128)(2,1)S(1)} %collective-permute-done.28.c01, bf16[256,256]{1,0:T(8,128)(2,1)S(1)} %collective-permute-done.29.c31, ...), custom_call_target="tpu_custom_call" | custom-call | flops 1677721600 | bytes 6553600 | tf_op jit(solution)/shard_map/output/pallas_call | solution.py:450
  (89 shorter events, 32.0 us)
Async XLA Ops:
  0.0 17.4 %collective-permute-start = (bf16[200,1024]{1,0:T(8,128)(2,1)}, bf16[200,1024]{1,0:T(8,128)(2,1)}, u32[]{:S(2)}, u32[]{:S(2)}) collective-permute-start(bf16[200,1024]{1,0:T(8,128)(2,1)} %bitcast.42), channel_id=1, source_target_pairs={{0,8},{1,9},{2,10},{3,11},{4,12},{5,13},{6,14},{7,15},{8,0},{9,1},... | collective-permute-start | bytes 1228808 | tf_op jit(solution)/shard_map/ppermute | solution.py:109
  0.0 20.5 %collective-permute-start.1 = (bf16[200,1024]{1,0:T(8,128)(2,1)}, bf16[200,1024]{1,0:T(8,128)(2,1)}, u32[]{:S(2)}, u32[]{:S(2)}) collective-permute-start(bf16[200,1024]{1,0:T(8,128)(2,1)} %bitcast.43), channel_id=1, source_target_pairs={{0,16},{1,17},{2,18},{3,19},{4,20},{5,21},{6,22},{7,23},{8,24},{9,... | collective-permute-start | bytes 1228808 | tf_op jit(solution)/shard_map/ppermute | solution.py:109
  4.6 15.9 %collective-permute-start.3 = (bf16[3,200,256]{2,1,0:T(8,128)(2,1)}, bf16[3,200,256]{2,1,0:T(8,128)(2,1)}, u32[]{:S(2)}, u32[]{:S(2)}) collective-permute-start(bf16[3,200,256]{2,1,0:T(8,128)(2,1)} %get-tuple-element.111), channel_id=1, source_target_pairs={{0,6},{1,7},{2,4},{3,5},{4,2},{5,3},{6,0},{7,1},{8,14},{9,15},{10,... | collective-permute-start | bytes 921608 | tf_op jit(solution)/shard_map/ppermute | solution.py:109
  6.9 14.9 %collective-permute-start.4 = (bf16[3,200,256]{2,1,0:T(8,128)(2,1)}, bf16[3,200,256]{2,1,0:T(8,128)(2,1)}, u32[]{:S(2)}, u32[]{:S(2)}) collective-permute-start(bf16[3,200,256]{2,1,0:T(8,128)(2,1)} %get-tuple-element.112), channel_id=1, source_target_pairs={{0,4},{1,5},{2,6},{3,7},{4,0},{5,1},{6,2},{7,3},{8,12},{9,13},{10,... | collective-permute-start | bytes 921608 | tf_op jit(solution)/shard_map/ppermute | solution.py:109
  7.2 14.7 %collective-permute-start.5 = (bf16[3,200,256]{2,1,0:T(8,128)(2,1)}, bf16[3,200,256]{2,1,0:T(8,128)(2,1)}, u32[]{:S(2)}, u32[]{:S(2)}) collective-permute-start(bf16[3,200,256]{2,1,0:T(8,128)(2,1)} %get-tuple-element.113), channel_id=1, source_target_pairs={{0,2},{1,3},{2,0},{3,1},{4,6},{5,7},{6,4},{7,5},{8,10},{9,11},{10,... | collective-permute-start | bytes 921608 | tf_op jit(solution)/shard_map/ppermute | solution.py:109
  20.5 9.6 %collective-permute-start.2 = (bf16[200,1024]{1,0:T(8,128)(2,1)}, bf16[200,1024]{1,0:T(8,128)(2,1)S(1)}, u32[]{:S(2)}, u32[]{:S(2)}) collective-permute-start(bf16[200,1024]{1,0:T(8,128)(2,1)} %collective-permute-done.1), channel_id=1, source_target_pairs={{0,8},{1,9},{2,10},{3,11},{4,12},{5,13},{6,14},{7,15},{8,0},{9,1},... | collective-permute-start | bytes 1228808 | tf_op jit(solution)/shard_map/ppermute | solution.py:109
  32.6 56.1 %collective-permute-start.9 = (bf16[4,256,896]{2,1,0:T(8,128)(2,1)S(1)}, bf16[4,256,896]{2,1,0:T(8,128)(2,1)}, u32[]{:S(2)}, u32[]{:S(2)}) collective-permute-start(bf16[4,256,896]{2,1,0:T(8,128)(2,1)S(1)} %copy-done), channel_id=1, source_target_pairs={{0,4},{1,5},{2,6},{3,7},{4,0},{5,1},{6,2},{7,3},{8,12},{9,13},{10,... | collective-permute-start | bytes 5505032 | tf_op jit(solution)/shard_map/ppermute | solution.py:109
  33.8 51.5 %collective-permute-start.6 = (bf16[3,800,256]{2,1,0:T(8,128)(2,1)}, bf16[3,800,256]{2,1,0:T(8,128)(2,1)}, u32[]{:S(2)}, u32[]{:S(2)}) collective-permute-start(bf16[3,800,256]{2,1,0:T(8,128)(2,1)} %pad_maximum_fusion.own), channel_id=1, source_target_pairs={{0,8},{1,9},{2,10},{3,11},{4,12},{5,13},{6,14},{7,15},{8,0},{9,1},... | collective-permute-start | bytes 3686408 | tf_op jit(solution)/shard_map/ppermute | solution.py:109
  33.8 54.9 %collective-permute-start.7 = (bf16[3,800,256]{2,1,0:T(8,128)(2,1)}, bf16[3,800,256]{2,1,0:T(8,128)(2,1)}, u32[]{:S(2)}, u32[]{:S(2)}) collective-permute-start(bf16[3,800,256]{2,1,0:T(8,128)(2,1)} %pad_maximum_fusion.own), channel_id=1, source_target_pairs={{0,16},{1,17},{2,18},{3,19},{4,20},{5,21},{6,22},{7,23},{8,24},{9,... | collective-permute-start | bytes 3686408 | tf_op jit(solution)/shard_map/ppermute | solution.py:109
  37.5 51.2 %collective-permute-start.10 = (bf16[2,208,1024]{2,1,0:T(8,128)(2,1)S(1)}, bf16[2,208,1024]{2,1,0:T(8,128)(2,1)S(1)}, u32[]{:S(2)}, u32[]{:S(2)}) collective-permute-start(bf16[2,208,1024]{2,1,0:T(8,128)(2,1)S(1)} %pad.12), channel_id=1, source_target_pairs={{0,1},{1,0},{2,3},{3,2},{4,5},{5,4},{6,7},{7,6},{8,9},{9,8},{10,11... | collective-permute-start | bytes 2555912 | tf_op jit(solution)/shard_map/ppermute | solution.py:109
  38.9 53.6 %collective-permute-start.11 = (bf16[2,208,1024]{2,1,0:T(8,128)(2,1)S(1)}, bf16[2,208,1024]{2,1,0:T(8,128)(2,1)S(1)}, u32[]{:S(2)}, u32[]{:S(2)}) collective-permute-start(bf16[2,208,1024]{2,1,0:T(8,128)(2,1)S(1)} %pad.13.wa0), channel_id=1, source_target_pairs={{0,4},{1,5},{2,6},{3,7},{4,0},{5,1},{6,2},{7,3},{8,12},{9,13},{10,... | collective-permute-start | bytes 2555912 | tf_op jit(solution)/shard_map/ppermute | solution.py:109
  93.3 28.9 %collective-permute-start.12 = (bf16[3,800,256]{2,1,0:T(8,128)(2,1)}, bf16[3,800,256]{2,1,0:T(8,128)(2,1)S(1)}, u32[]{:S(2)}, u32[]{:S(2)}) collective-permute-start(bf16[3,800,256]{2,1,0:T(8,128)(2,1)} %collective-permute-done.7.far), channel_id=1, source_target_pairs={{0,8},{1,9},{2,10},{3,11},{4,12},{5,13},{6,14},{7,15},{8,0},{9,1},... | collective-permute-start | bytes 3686408 | tf_op jit(solution)/shard_map/ppermute | solution.py:109
  93.3 31.4 %collective-permute-start.18 = (bf16[2,208,1024]{2,1,0:T(8,128)(2,1)S(1)}, bf16[2,208,1024]{2,1,0:T(8,128)(2,1)S(1)}, u32[]{:S(2)}, u32[]{:S(2)}) collective-permute-start(bf16[2,208,1024]{2,1,0:T(8,128)(2,1)S(1)} %pad.13.wa0), channel_id=1, source_target_pairs={{0,2},{1,3},{2,0},{3,1},{4,6},{5,7},{6,4},{7,5},{8,10},{9,11},{10,... | collective-permute-start | bytes 2555912 | tf_op jit(solution)/shard_map/ppermute | solution.py:109
  93.6 31.8 %collective-permute-start.16 = (bf16[2,208,1024]{2,1,0:T(8,128)(2,1)S(1)}, bf16[2,208,1024]{2,1,0:T(8,128)(2,1)S(1)}, u32[]{:S(2)}, u32[]{:S(2)}) collective-permute-start(bf16[2,208,1024]{2,1,0:T(8,128)(2,1)S(1)} %collective-permute-done.10.wa1), channel_id=1, source_target_pairs={{0,4},{1,5},{2,6},{3,7},{4,0},{5,1},{6,2},{7,3},{8,12},{9,13},{10,... | collective-permute-start | bytes 2555912 | tf_op jit(solution)/shard_map/ppermute | solution.py:109
  94.9 30.6 %collective-permute-start.17 = (bf16[2,208,1024]{2,1,0:T(8,128)(2,1)S(1)}, bf16[2,208,1024]{2,1,0:T(8,128)(2,1)S(1)}, u32[]{:S(2)}, u32[]{:S(2)}) collective-permute-start(bf16[2,208,1024]{2,1,0:T(8,128)(2,1)S(1)} %collective-permute-done.10.wa1), channel_id=1, source_target_pairs={{0,2},{1,3},{2,0},{3,1},{4,6},{5,7},{6,4},{7,5},{8,10},{9,11},{10,... | collective-permute-start | bytes 2555912 | tf_op jit(solution)/shard_map/ppermute | solution.py:109
  96.9 28.5 %collective-permute-start.19 = (bf16[2,208,1024]{2,1,0:T(8,128)(2,1)S(1)}, bf16[2,208,1024]{2,1,0:T(8,128)(2,1)S(1)}, u32[]{:S(2)}, u32[]{:S(2)}) collective-permute-start(bf16[2,208,1024]{2,1,0:T(8,128)(2,1)S(1)} %collective-permute-done.11.wc0), channel_id=1, source_target_pairs={{0,2},{1,3},{2,0},{3,1},{4,6},{5,7},{6,4},{7,5},{8,10},{9,11},{10,... | collective-permute-start | bytes 2555912 | tf_op jit(solution)/shard_map/ppermute | solution.py:109
  124.6 12.7 %collective-permute-start.14 = (bf16[2,512,256]{2,1,0:T(8,128)(2,1)S(1)}, bf16[2,512,256]{2,1,0:T(8,128)(2,1)S(1)}, u32[]{:S(2)}, u32[]{:S(2)}) collective-permute-start(bf16[2,512,256]{2,1,0:T(8,128)(2,1)S(1)} %get-tuple-element.74), channel_id=1, source_target_pairs={{0,8},{1,9},{2,10},{3,11},{4,12},{5,13},{6,14},{7,15},{8,0},{9,1},... | collective-permute-start | bytes 1572872 | tf_op jit(solution)/shard_map/ppermute | solution.py:109
  124.7 12.6 %collective-permute-start.15 = (bf16[2,512,256]{2,1,0:T(8,128)(2,1)S(1)}, bf16[2,512,256]{2,1,0:T(8,128)(2,1)S(1)}, u32[]{:S(2)}, u32[]{:S(2)}) collective-permute-start(bf16[2,512,256]{2,1,0:T(8,128)(2,1)S(1)} %get-tuple-element.75), channel_id=1, source_target_pairs={{0,2},{1,3},{2,0},{3,1},{4,6},{5,7},{6,4},{7,5},{8,16},{9,17},{10,... | collective-permute-start | bytes 1572872 | tf_op jit(solution)/shard_map/ppermute | solution.py:109
  135.1 8.5 %collective-permute-start.26 = (bf16[2,208,1024]{2,1,0:T(8,128)(2,1)S(1)}, bf16[2,208,1024]{2,1,0:T(8,128)(2,1)S(1)}, u32[]{:S(2)}, u32[]{:S(2)}) collective-permute-start(bf16[2,208,1024]{2,1,0:T(8,128)(2,1)S(1)} %collective-permute-done.16.wc1), channel_id=1, source_target_pairs={{0,2},{1,3},{2,0},{3,1},{4,6},{5,7},{6,4},{7,5},{8,10},{9,11},{10,... | collective-permute-start | bytes 2555912 | tf_op jit(solution)/shard_map/ppermute | solution.py:109
  144.6 7.7 %collective-permute-start.28 = (bf16[256,256]{1,0:T(8,128)(2,1)S(1)}, bf16[256,256]{1,0:T(8,128)(2,1)S(1)}, u32[]{:S(2)}, u32[]{:S(2)}) collective-permute-start(bf16[256,256]{1,0:T(8,128)(2,1)S(1)} %get-tuple-element.88.c00), channel_id=1, source_target_pairs={{0,1},{1,0},{2,3},{3,2},{4,5},{5,4},{6,7},{7,6},{8,9},{9,8},{10,11... | collective-permute-start | bytes 393224 | tf_op jit(solution)/shard_map/ppermute | solution.py:109
  145.8 11.5 %collective-permute-start.29 = (bf16[256,256]{1,0:T(8,128)(2,1)S(1)}, bf16[256,256]{1,0:T(8,128)(2,1)S(1)}, u32[]{:S(2)}, u32[]{:S(2)}) collective-permute-start(bf16[256,256]{1,0:T(8,128)(2,1)S(1)} %get-tuple-element.89), channel_id=1, source_target_pairs={{0,7},{1,6},{2,5},{3,4},{4,3},{5,2},{6,1},{7,0},{8,15},{9,14},{10,... | collective-permute-start | bytes 393224 | tf_op jit(solution)/shard_map/ppermute | solution.py:109
  149.1 8.3 %collective-permute-start.30 = (bf16[256,256]{1,0:T(8,128)(2,1)S(1)}, bf16[256,256]{1,0:T(8,128)(2,1)S(1)}, u32[]{:S(2)}, u32[]{:S(2)}) collective-permute-start(bf16[256,256]{1,0:T(8,128)(2,1)S(1)} %get-tuple-element.89), channel_id=1, source_target_pairs={{0,6},{1,7},{2,4},{3,5},{4,2},{5,3},{6,0},{7,1},{8,14},{9,15},{10,... | collective-permute-start | bytes 393224 | tf_op jit(solution)/shard_map/ppermute | solution.py:109
  149.1 10.6 %collective-permute-start.32 = (bf16[256,256]{1,0:T(8,128)(2,1)S(1)}, bf16[256,256]{1,0:T(8,128)(2,1)S(1)}, u32[]{:S(2)}, u32[]{:S(2)}) collective-permute-start(bf16[256,256]{1,0:T(8,128)(2,1)S(1)} %get-tuple-element.87), channel_id=1, source_target_pairs={{0,5},{1,4},{2,7},{3,6},{4,1},{5,0},{6,3},{7,2},{8,13},{9,12},{10,... | collective-permute-start | bytes 393224 | tf_op jit(solution)/shard_map/ppermute | solution.py:109
  152.3 7.4 %collective-permute-start.33 = (bf16[256,256]{1,0:T(8,128)(2,1)S(1)}, bf16[256,256]{1,0:T(8,128)(2,1)S(1)}, u32[]{:S(2)}, u32[]{:S(2)}) collective-permute-start(bf16[256,256]{1,0:T(8,128)(2,1)S(1)} %get-tuple-element.90), channel_id=1, source_target_pairs={{0,2},{1,3},{2,0},{3,1},{4,6},{5,7},{6,4},{7,5},{8,10},{9,11},{10,... | collective-permute-start | bytes 393224 | tf_op jit(solution)/shard_map/ppermute | solution.py:109
  (16 other events, 87.1 us)

commit v18 on v17

--- a/solution.py
+++ b/solution.py
@@ -505,15 +505,14 @@
     share = layer_scale.shape[0]
     residual = jnp.transpose(lax.dynamic_slice_in_dim(tokens, tp * share, share, 1))
     scale = jnp.pad(layer_scale, (0, -share % 128))[None]
-    x0, out_near, out_far, seg, spans, residual, scale, *gains = tied(
-        x0, out_near, out_far, seg, spans, residual, scale, *gains
+    own, x0, out_near, out_far, seg, spans, residual, scale, *gains = tied(
+        own, x0, out_near, out_far, seg, spans, residual, scale, *gains
     )
     out_last = even_pair(out_far)
     x2 = in_slab(x0, 2)
-    out_last, own, x0 = tied(out_last, own, x0)
-    far, near = half_pair(own), even_pair(own)
-    x1 = in_slab(x0, 1)
-    out_last, x1 = tied(out_last, x1)
+    far, x1 = half_pair(own), in_slab(x0, 1)
+    out_last, own, x1 = tied(out_last, own, x1)
+    near = even_pair(own)
     close, away = jnp.stack([out_own, out_near]), jnp.stack([out_far, out_last])
     pad = ((0, 0), (0, -close.shape[1] % 16), (0, 0))
     keep = jnp.pad(jnp.where(home, close, away), pad)

time: 165 us -> 167 us (1.012)
  waiting for transfers between devices: 91.6 us -> 85.1 us
  starting transfers between devices: 33.7 us -> 39.4 us
  local copies, waits for them, and re-layouts: 5.71 us -> 7.72 us
    ppermute x34, waiting for transfers between devices: 91.6 us -> 85.1 us  [permuted(): return lax.ppermute(x, ('seq', 'tp'), pairs)]
    ppermute x34, starting transfers between devices: 33.7 us -> 39.4 us  [permuted(): return lax.ppermute(x, ('seq', 'tp'), pairs)]
    unnamed x13 -> x17, local copies, waits for them, and re-layouts: 0.6 us -> 2.64 us
  transfers between devices with their start and end apart: 34 -> 34, of which waited for: 17 -> 13; matrix products, arithmetic and copies ran while one was open for 6% -> 6% of each run, Pallas kernels for 15% -> 15%
where the time goes in v18:
time: 167 us; the launch traced here: 166 us
  waiting for transfers between devices  85.1 us (51%)
  starting transfers between devices  39.4 us (24%)
  Pallas kernels  29.2 us (17%)
  local copies, waits for them, and re-layouts  7.72 us (5%)
  other arithmetic  4.52 us (3%)
    ppermute x34, waiting for transfers between devices, permuted(): return lax.ppermute(x, ('seq', 'tp'), pairs)  85.1 us
    ppermute x34, starting transfers between devices, permuted(): return lax.ppermute(x, ('seq', 'tp'), pairs)  39.4 us
    pallas_call x1, Pallas kernels, early(): pl.pallas_call(early_kernel, out_shape=(jax.ShapeDtypeStruct((SLAB, kinds...  9.35 us
    pallas_call x1, Pallas kernels, attend(): pl.pallas_call(functools.partial(attend_kernel, full_width), out_shape=(j...  6.24 us
    pallas_call x1, Pallas kernels, collect(): pl.pallas_call(collect_kernel, out_shape=jax.ShapeDtypeStruct((2, 2 * SLA...  3.82 us
    pallas_call x1, Pallas kernels, output(): pl.pallas_call(out_kernel, out_shape=jax.ShapeDtypeStruct((share, count),...  3.81 us
    pallas_call x1, Pallas kernels, norm(): pl.pallas_call(norm_kernel, out_shape=jax.ShapeDtypeStruct(shape, jnp.bfl...  3.56 us
  transfers between devices with their start and end apart: 34, of which 13 were waited for; matrix products, arithmetic and copies ran while one was open for 6% of the time, Pallas kernels for 15%

profile of v18, /device:TPU:9, one launch (start us, length us, event | category | flops | bytes accessed | tf_op | source)
XLA Modules:
  0.0 166.2 jit_solution(4475633201121995218)
XLA Ops:
  0.0 2.5 %collective-permute-start.4 = (bf16[200,1024]{1,0:T(8,128)(2,1)}, bf16[200,1024]{1,0:T(8,128)(2,1)}, u32[]{:S(2)}, u32[]{:S(2)}) collective-permute-start(bf16[200,1024]{1,0:T(8,128)(2,1)} %bitcast.43), channel_id=1, source_target_pairs={{0,16},{1,17},{2,18},{3,19},{4,20},{5,21},{6,22},{7,23},{8,24},{9,... | collective-permute-start | bytes 1228808 | tf_op jit(solution)/shard_map/ppermute | solution.py:109
  2.5 2.1 %dynamic-slice_bitcast_fusion.2 = (bf16[3,200,256]{2,1,0:T(8,128)(2,1)}, bf16[3,200,256]{2,1,0:T(8,128)(2,1)}, bf16[3,200,256]{2,1,0:T(8,128)(2,1)}) fusion(bf16[200,3,1024]{2,0,1:T(8,128)(2,1)} %param.10, s32[]{:T(128)S(6)} %select_n.142, s32[]{:T(128)S(6)} %select_n.144, s32[]{:T(128)S(6)} %select_n.146), kind=kLoop, calls=%fused_computation.16 | loop fusion | bytes 1843212 | tf_op jit(solution)/shard_map/dynamic_slice | solution.py:492
  4.6 2.3 %collective-permute-start = (bf16[3,200,256]{2,1,0:T(8,128)(2,1)}, bf16[3,200,256]{2,1,0:T(8,128)(2,1)}, u32[]{:S(2)}, u32[]{:S(2)}) collective-permute-start(bf16[3,200,256]{2,1,0:T(8,128)(2,1)} %get-tuple-element.109), channel_id=1, source_target_pairs={{0,6},{1,7},{2,4},{3,5},{4,2},{5,3},{6,0},{7,1},{8,14},{9,15},{10,... | collective-permute-start | bytes 921608 | tf_op jit(solution)/shard_map/ppermute | solution.py:109
  11.2 3.6 %norm.1.xa = bf16[4,256,896]{2,1,0:T(8,128)(2,1)} custom-call(bf16[256,3200]{1,0:T(8,128)(2,1)} %tokens.1, f32[1,3200]{1,0:T(1,128)} %broadcast_in_dim.34.gain), custom_call_target="tpu_custom_call" | custom-call | tf_op jit(solution)/shard_map/norm/pallas_call | solution.py:168
  15.4 6.5 %collective-permute-done.1 = bf16[3,200,256]{2,1,0:T(8,128)(2,1)} collective-permute-done((bf16[3,200,256]{2,1,0:T(8,128)(2,1)}, bf16[3,200,256]{2,1,0:T(8,128)(2,1)}, u32[]{:S(2)}, u32[]{:S(2)}) %collective-permute-start.1) | collective-permute-done | bytes 307232 | tf_op jit(solution)/shard_map/ppermute | solution.py:109
  27.5 15.9 %collective-permute-done.5 = bf16[200,1024]{1,0:T(8,128)(2,1)S(1)} collective-permute-done((bf16[200,1024]{1,0:T(8,128)(2,1)}, bf16[200,1024]{1,0:T(8,128)(2,1)S(1)}, u32[]{:S(2)}, u32[]{:S(2)}) %collective-permute-start.5) | collective-permute-done | bytes 409632 | tf_op jit(solution)/shard_map/ppermute | solution.py:109
  44.6 2.2 %collective-permute-start.7 = (bf16[3,800,256]{2,1,0:T(8,128)(2,1)}, bf16[3,800,256]{2,1,0:T(8,128)(2,1)}, u32[]{:S(2)}, u32[]{:S(2)}) collective-permute-start(bf16[3,800,256]{2,1,0:T(8,128)(2,1)} %pad_maximum_fusion.own), channel_id=1, source_target_pairs={{0,8},{1,9},{2,10},{3,11},{4,12},{5,13},{6,14},{7,15},{8,0},{9,1},... | collective-permute-start | bytes 3686408 | tf_op jit(solution)/shard_map/ppermute | solution.py:109
  49.5 1.7 %collective-permute-start.11 = (bf16[2,208,1024]{2,1,0:T(8,128)(2,1)S(1)}, bf16[2,208,1024]{2,1,0:T(8,128)(2,1)S(1)}, u32[]{:S(2)}, u32[]{:S(2)}) collective-permute-start(bf16[2,208,1024]{2,1,0:T(8,128)(2,1)S(1)} %pad.13.wa0), channel_id=1, source_target_pairs={{0,4},{1,5},{2,6},{3,7},{4,0},{5,1},{6,2},{7,3},{8,12},{9,13},{10,... | collective-permute-start | bytes 2555912 | tf_op jit(solution)/shard_map/ppermute | solution.py:109
  51.2 28.3 %collective-permute-done.8.far = bf16[3,800,256]{2,1,0:T(8,128)(2,1)} collective-permute-done((bf16[3,800,256]{2,1,0:T(8,128)(2,1)}, bf16[3,800,256]{2,1,0:T(8,128)(2,1)}, u32[]{:S(2)}, u32[]{:S(2)}) %collective-permute-start.8) | collective-permute-done | bytes 1228832 | tf_op jit(solution)/shard_map/ppermute | solution.py:109
  79.5 6.3 %collective-permute-done.11.wc0 = bf16[2,208,1024]{2,1,0:T(8,128)(2,1)S(1)} collective-permute-done((bf16[2,208,1024]{2,1,0:T(8,128)(2,1)S(1)}, bf16[2,208,1024]{2,1,0:T(8,128)(2,1)S(1)}, u32[]{:S(2)}, u32[]{:S(2)}) %collective-permute-start.11) | collective-permute-done | bytes 852000 | tf_op jit(solution)/shard_map/ppermute | solution.py:109
  85.8 4.9 %collective-permute-done.7.near = bf16[3,800,256]{2,1,0:T(8,128)(2,1)} collective-permute-done((bf16[3,800,256]{2,1,0:T(8,128)(2,1)}, bf16[3,800,256]{2,1,0:T(8,128)(2,1)}, u32[]{:S(2)}, u32[]{:S(2)}) %collective-permute-start.7) | collective-permute-done | bytes 1228832 | tf_op jit(solution)/shard_map/ppermute | solution.py:109
  90.7 2.4 %collective-permute-start.13 = (bf16[4,256,896]{2,1,0:T(8,128)(2,1)}, bf16[4,256,896]{2,1,0:T(8,128)(2,1)S(1)}, u32[]{:S(2)}, u32[]{:S(2)}) collective-permute-start(bf16[4,256,896]{2,1,0:T(8,128)(2,1)} %collective-permute-done.9.xc), channel_id=1, source_target_pairs={{0,2},{1,3},{2,0},{3,1},{4,6},{5,7},{6,4},{7,5},{8,10},{9,11},{10,... | collective-permute-start | bytes 5505032 | tf_op jit(solution)/shard_map/ppermute | solution.py:109
  93.1 2.2 %collective-permute-start.12 = (bf16[3,800,256]{2,1,0:T(8,128)(2,1)}, bf16[3,800,256]{2,1,0:T(8,128)(2,1)S(1)}, u32[]{:S(2)}, u32[]{:S(2)}) collective-permute-start(bf16[3,800,256]{2,1,0:T(8,128)(2,1)} %collective-permute-done.8.far), channel_id=1, source_target_pairs={{0,8},{1,9},{2,10},{3,11},{4,12},{5,13},{6,14},{7,15},{8,0},{9,1},... | collective-permute-start | bytes 3686408 | tf_op jit(solution)/shard_map/ppermute | solution.py:109
  97.8 9.3 %early.1 = (f32[4,3,256,256]{3,2,1,0:T(8,128)S(1)}, bf16[4,256,896]{2,1,0:T(8,128)(2,1)S(1)}) custom-call(s32[3]{0:T(128)S(1)} %pad_add_fusion.1.place, bf16[4,256,896]{2,1,0:T(8,128)(2,1)S(1)} %copy-done, bf16[4,256,896]{2,1,0:T(8,128)(2,1)S(1)} %copy-done.2, bf16[4,256,896]{2,1,0:T(8,128)(2,1)} %collective-permute-done.9.xc, ...), custom_call_target="tpu_custom_call" | custom-call | flops 7549747200 | bytes 8601600 | tf_op jit(solution)/shard_map/early/pallas_call | solution.py:216
  107.2 15.8 %collective-permute-done.12.last = bf16[3,800,256]{2,1,0:T(8,128)(2,1)S(1)} collective-permute-done((bf16[3,800,256]{2,1,0:T(8,128)(2,1)}, bf16[3,800,256]{2,1,0:T(8,128)(2,1)S(1)}, u32[]{:S(2)}, u32[]{:S(2)}) %collective-permute-start.12) | collective-permute-done | bytes 1228832 | tf_op jit(solution)/shard_map/ppermute | solution.py:109
  122.9 2.5 %late.1 = (f32[1024,256]{1,0:T(8,128)S(1)}, bf16[1024,256]{1,0:T(8,128)(2,1)S(1)}, bf16[1024,256]{1,0:T(8,128)(2,1)S(1)}, f32[2,1024]{1,0:T(2,128)S(1)}, bf16[2,...) custom-call(s32[3]{0:T(128)S(1)} %pad_add_fusion.1.place, bf16[4,256,896]{2,1,0:T(8,128)(2,1)S(1)} %get-tuple-element.64.x_last, ...), custom_call_target="tpu_custom_call" | custom-call | flops 1258291200 | bytes 2867200 | tf_op jit(solution)/shard_map/late/pallas_call | solution.py:273
  130.8 2.1 %collective-permute-done.22 = f32[2,1024]{1,0:T(2,128)S(1)} collective-permute-done((f32[2,1024]{1,0:T(2,128)S(1)}, f32[2,1024]{1,0:T(2,128)S(1)}, u32[]{:S(2)}, u32[]{:S(2)}) %collective-permute-start.22) | collective-permute-done | bytes 8224 | tf_op jit(solution)/shard_map/ppermute | solution.py:109
  135.9 1.7 %collective-permute-start.25 = (f32[2,1024]{1,0:T(2,128)S(1)}, f32[2,1024]{1,0:T(2,128)S(1)}, u32[]{:S(2)}, u32[]{:S(2)}) collective-permute-start(f32[2,1024]{1,0:T(2,128)S(1)} %add.114.mine), channel_id=1, source_target_pairs={{0,2},{1,3},{2,0},{3,1},{4,6},{5,7},{6,4},{7,5},{8,16},{9,17},{10,... | collective-permute-start | bytes 24584 | tf_op jit(solution)/shard_map/ppermute | solution.py:109
  139.2 6.2 %attend.1 = (bf16[256,256]{1,0:T(8,128)(2,1)S(1)}, bf16[256,256]{1,0:T(8,128)(2,1)S(1)}, bf16[256,256]{1,0:T(8,128)(2,1)S(1)}, bf16[256,256]{1,0:T(8,128)(2,1)S(1)}) custom-call(s32[3]{0:T(128)S(1)} %pad_add_fusion.1.place, s32[4,2]{1,0:T(4,128)S(1)} %pad_add_fusion.spans, f32[1024,256]{1,0:T(8,128)S(1)} %get-tuple-element.69.query, ...), custom_call_target="tpu_custom_call" | custom-call | flops 21474836480 | bytes 3145728 | tf_op jit(solution)/shard_map/attend/pallas_call | solution.py:376
  148.4 2.2 %collective-permute-start.29 = (bf16[256,256]{1,0:T(8,128)(2,1)S(1)}, bf16[256,256]{1,0:T(8,128)(2,1)S(1)}, u32[]{:S(2)}, u32[]{:S(2)}) collective-permute-start(bf16[256,256]{1,0:T(8,128)(2,1)S(1)} %get-tuple-element.87), channel_id=1, source_target_pairs={{0,7},{1,6},{2,5},{3,4},{4,3},{5,2},{6,1},{7,0},{8,15},{9,14},{10,... | collective-permute-start | bytes 393224 | tf_op jit(solution)/shard_map/ppermute | solution.py:109
  150.7 2.5 %collective-permute-start.32 = (bf16[256,256]{1,0:T(8,128)(2,1)S(1)}, bf16[256,256]{1,0:T(8,128)(2,1)S(1)}, u32[]{:S(2)}, u32[]{:S(2)}) collective-permute-start(bf16[256,256]{1,0:T(8,128)(2,1)S(1)} %get-tuple-element.85), channel_id=1, source_target_pairs={{0,5},{1,4},{2,7},{3,6},{4,1},{5,0},{6,3},{7,2},{8,13},{9,12},{10,... | collective-permute-start | bytes 393224 | tf_op jit(solution)/shard_map/ppermute | solution.py:109
  153.9 3.2 %collective-permute-start.33 = (bf16[256,256]{1,0:T(8,128)(2,1)S(1)}, bf16[256,256]{1,0:T(8,128)(2,1)S(1)}, u32[]{:S(2)}, u32[]{:S(2)}) collective-permute-start(bf16[256,256]{1,0:T(8,128)(2,1)S(1)} %get-tuple-element.88), channel_id=1, source_target_pairs={{0,2},{1,3},{2,0},{3,1},{4,6},{5,7},{6,4},{7,5},{8,10},{9,11},{10,... | collective-permute-start | bytes 393224 | tf_op jit(solution)/shard_map/ppermute | solution.py:109
  157.0 3.8 %collect.1.w = bf16[2,1664,1024]{2,1,0:T(8,128)(2,1)S(1)} custom-call(bf16[2,208,1024]{2,1,0:T(8,128)(2,1)S(1)} %pad.13.wa0, bf16[2,208,1024]{2,1,0:T(8,128)(2,1)S(1)} %collective-permute-done.18.wb0, bf16[2,208,1024]{2,1,0:T(8,128)(2,1)S(1)} %collective-permute-done.11.wc0, bf16[2,208,1024]{2,1,0:T(8,128)(2,1)S(1)} %collective-permute-done.19.wd0, ...), custom_call_target="tpu_custom_call" | custom-call | bytes 13631488 | tf_op jit(solution)/shard_map/collect/pallas_call | solution.py:411
  162.4 3.8 %output.1 = bf16[1600,256]{1,0:T(8,128)(2,1)} custom-call(s32[3]{0:T(128)S(1)} %pad_add_fusion.1.place, bf16[256,256]{1,0:T(8,128)(2,1)S(1)} %collective-permute-done.27.c20, bf16[256,256]{1,0:T(8,128)(2,1)S(1)} %collective-permute-done.28.c01, bf16[256,256]{1,0:T(8,128)(2,1)S(1)} %collective-permute-done.29.c31, ...), custom_call_target="tpu_custom_call" | custom-call | flops 1677721600 | bytes 6553600 | tf_op jit(solution)/shard_map/output/pallas_call | solution.py:450
  (93 shorter events, 32.1 us)
Async XLA Ops:
  0.0 24.6 %collective-permute-start.3 = (bf16[200,1024]{1,0:T(8,128)(2,1)}, bf16[200,1024]{1,0:T(8,128)(2,1)}, u32[]{:S(2)}, u32[]{:S(2)}) collective-permute-start(bf16[200,1024]{1,0:T(8,128)(2,1)} %bitcast.42), channel_id=1, source_target_pairs={{0,8},{1,9},{2,10},{3,11},{4,12},{5,13},{6,14},{7,15},{8,0},{9,1},... | collective-permute-start | bytes 1228808 | tf_op jit(solution)/shard_map/ppermute | solution.py:109
  0.0 24.6 %collective-permute-start.4 = (bf16[200,1024]{1,0:T(8,128)(2,1)}, bf16[200,1024]{1,0:T(8,128)(2,1)}, u32[]{:S(2)}, u32[]{:S(2)}) collective-permute-start(bf16[200,1024]{1,0:T(8,128)(2,1)} %bitcast.43), channel_id=1, source_target_pairs={{0,16},{1,17},{2,18},{3,19},{4,20},{5,21},{6,22},{7,23},{8,24},{9,... | collective-permute-start | bytes 1228808 | tf_op jit(solution)/shard_map/ppermute | solution.py:109
  4.6 10.8 %collective-permute-start = (bf16[3,200,256]{2,1,0:T(8,128)(2,1)}, bf16[3,200,256]{2,1,0:T(8,128)(2,1)}, u32[]{:S(2)}, u32[]{:S(2)}) collective-permute-start(bf16[3,200,256]{2,1,0:T(8,128)(2,1)} %get-tuple-element.109), channel_id=1, source_target_pairs={{0,6},{1,7},{2,4},{3,5},{4,2},{5,3},{6,0},{7,1},{8,14},{9,15},{10,... | collective-permute-start | bytes 921608 | tf_op jit(solution)/shard_map/ppermute | solution.py:109
  6.9 14.9 %collective-permute-start.1 = (bf16[3,200,256]{2,1,0:T(8,128)(2,1)}, bf16[3,200,256]{2,1,0:T(8,128)(2,1)}, u32[]{:S(2)}, u32[]{:S(2)}) collective-permute-start(bf16[3,200,256]{2,1,0:T(8,128)(2,1)} %get-tuple-element.110), channel_id=1, source_target_pairs={{0,4},{1,5},{2,6},{3,7},{4,0},{5,1},{6,2},{7,3},{8,12},{9,13},{10,... | collective-permute-start | bytes 921608 | tf_op jit(solution)/shard_map/ppermute | solution.py:109
  7.2 14.7 %collective-permute-start.2 = (bf16[3,200,256]{2,1,0:T(8,128)(2,1)}, bf16[3,200,256]{2,1,0:T(8,128)(2,1)}, u32[]{:S(2)}, u32[]{:S(2)}) collective-permute-start(bf16[3,200,256]{2,1,0:T(8,128)(2,1)} %get-tuple-element.111), channel_id=1, source_target_pairs={{0,2},{1,3},{2,0},{3,1},{4,6},{5,7},{6,4},{7,5},{8,10},{9,11},{10,... | collective-permute-start | bytes 921608 | tf_op jit(solution)/shard_map/ppermute | solution.py:109
  25.4 18.0 %collective-permute-start.6 = (bf16[4,256,896]{2,1,0:T(8,128)(2,1)S(1)}, bf16[4,256,896]{2,1,0:T(8,128)(2,1)S(1)}, u32[]{:S(2)}, u32[]{:S(2)}) collective-permute-start(bf16[4,256,896]{2,1,0:T(8,128)(2,1)S(1)} %copy-done), channel_id=1, source_target_pairs={{0,2},{1,3},{2,0},{3,1},{4,6},{5,7},{6,4},{7,5},{8,10},{9,11},{10,... | collective-permute-start | bytes 5505032 | tf_op jit(solution)/shard_map/ppermute | solution.py:109
  25.9 53.7 %collective-permute-start.9 = (bf16[4,256,896]{2,1,0:T(8,128)(2,1)S(1)}, bf16[4,256,896]{2,1,0:T(8,128)(2,1)}, u32[]{:S(2)}, u32[]{:S(2)}) collective-permute-start(bf16[4,256,896]{2,1,0:T(8,128)(2,1)S(1)} %copy-done), channel_id=1, source_target_pairs={{0,4},{1,5},{2,6},{3,7},{4,0},{5,1},{6,2},{7,3},{8,12},{9,13},{10,... | collective-permute-start | bytes 5505032 | tf_op jit(solution)/shard_map/ppermute | solution.py:109
  26.1 17.2 %collective-permute-start.5 = (bf16[200,1024]{1,0:T(8,128)(2,1)}, bf16[200,1024]{1,0:T(8,128)(2,1)S(1)}, u32[]{:S(2)}, u32[]{:S(2)}) collective-permute-start(bf16[200,1024]{1,0:T(8,128)(2,1)} %collective-permute-done.4), channel_id=1, source_target_pairs={{0,8},{1,9},{2,10},{3,11},{4,12},{5,13},{6,14},{7,15},{8,0},{9,1},... | collective-permute-start | bytes 1228808 | tf_op jit(solution)/shard_map/ppermute | solution.py:109
  27.4 52.1 %collective-permute-start.8 = (bf16[3,800,256]{2,1,0:T(8,128)(2,1)}, bf16[3,800,256]{2,1,0:T(8,128)(2,1)}, u32[]{:S(2)}, u32[]{:S(2)}) collective-permute-start(bf16[3,800,256]{2,1,0:T(8,128)(2,1)} %pad_maximum_fusion.own), channel_id=1, source_target_pairs={{0,16},{1,17},{2,18},{3,19},{4,20},{5,21},{6,22},{7,23},{8,24},{9,... | collective-permute-start | bytes 3686408 | tf_op jit(solution)/shard_map/ppermute | solution.py:109
  44.6 46.1 %collective-permute-start.7 = (bf16[3,800,256]{2,1,0:T(8,128)(2,1)}, bf16[3,800,256]{2,1,0:T(8,128)(2,1)}, u32[]{:S(2)}, u32[]{:S(2)}) collective-permute-start(bf16[3,800,256]{2,1,0:T(8,128)(2,1)} %pad_maximum_fusion.own), channel_id=1, source_target_pairs={{0,8},{1,9},{2,10},{3,11},{4,12},{5,13},{6,14},{7,15},{8,0},{9,1},... | collective-permute-start | bytes 3686408 | tf_op jit(solution)/shard_map/ppermute | solution.py:109
  48.2 31.4 %collective-permute-start.10 = (bf16[2,208,1024]{2,1,0:T(8,128)(2,1)S(1)}, bf16[2,208,1024]{2,1,0:T(8,128)(2,1)S(1)}, u32[]{:S(2)}, u32[]{:S(2)}) collective-permute-start(bf16[2,208,1024]{2,1,0:T(8,128)(2,1)S(1)} %pad.12), channel_id=1, source_target_pairs={{0,1},{1,0},{2,3},{3,2},{4,5},{5,4},{6,7},{7,6},{8,9},{9,8},{10,11... | collective-permute-start | bytes 2555912 | tf_op jit(solution)/shard_map/ppermute | solution.py:109
  49.5 36.3 %collective-permute-start.11 = (bf16[2,208,1024]{2,1,0:T(8,128)(2,1)S(1)}, bf16[2,208,1024]{2,1,0:T(8,128)(2,1)S(1)}, u32[]{:S(2)}, u32[]{:S(2)}) collective-permute-start(bf16[2,208,1024]{2,1,0:T(8,128)(2,1)S(1)} %pad.13.wa0), channel_id=1, source_target_pairs={{0,4},{1,5},{2,6},{3,7},{4,0},{5,1},{6,2},{7,3},{8,12},{9,13},{10,... | collective-permute-start | bytes 2555912 | tf_op jit(solution)/shard_map/ppermute | solution.py:109
  93.1 29.8 %collective-permute-start.12 = (bf16[3,800,256]{2,1,0:T(8,128)(2,1)}, bf16[3,800,256]{2,1,0:T(8,128)(2,1)S(1)}, u32[]{:S(2)}, u32[]{:S(2)}) collective-permute-start(bf16[3,800,256]{2,1,0:T(8,128)(2,1)} %collective-permute-done.8.far), channel_id=1, source_target_pairs={{0,8},{1,9},{2,10},{3,11},{4,12},{5,13},{6,14},{7,15},{8,0},{9,1},... | collective-permute-start | bytes 3686408 | tf_op jit(solution)/shard_map/ppermute | solution.py:109
  95.3 31.4 %collective-permute-start.18 = (bf16[2,208,1024]{2,1,0:T(8,128)(2,1)S(1)}, bf16[2,208,1024]{2,1,0:T(8,128)(2,1)S(1)}, u32[]{:S(2)}, u32[]{:S(2)}) collective-permute-start(bf16[2,208,1024]{2,1,0:T(8,128)(2,1)S(1)} %pad.13.wa0), channel_id=1, source_target_pairs={{0,2},{1,3},{2,0},{3,1},{4,6},{5,7},{6,4},{7,5},{8,10},{9,11},{10,... | collective-permute-start | bytes 2555912 | tf_op jit(solution)/shard_map/ppermute | solution.py:109
  95.7 31.0 %collective-permute-start.16 = (bf16[2,208,1024]{2,1,0:T(8,128)(2,1)S(1)}, bf16[2,208,1024]{2,1,0:T(8,128)(2,1)S(1)}, u32[]{:S(2)}, u32[]{:S(2)}) collective-permute-start(bf16[2,208,1024]{2,1,0:T(8,128)(2,1)S(1)} %collective-permute-done.10.wa1), channel_id=1, source_target_pairs={{0,4},{1,5},{2,6},{3,7},{4,0},{5,1},{6,2},{7,3},{8,12},{9,13},{10,... | collective-permute-start | bytes 2555912 | tf_op jit(solution)/shard_map/ppermute | solution.py:109
  97.3 29.4 %collective-permute-start.17 = (bf16[2,208,1024]{2,1,0:T(8,128)(2,1)S(1)}, bf16[2,208,1024]{2,1,0:T(8,128)(2,1)S(1)}, u32[]{:S(2)}, u32[]{:S(2)}) collective-permute-start(bf16[2,208,1024]{2,1,0:T(8,128)(2,1)S(1)} %collective-permute-done.10.wa1), channel_id=1, source_target_pairs={{0,2},{1,3},{2,0},{3,1},{4,6},{5,7},{6,4},{7,5},{8,10},{9,11},{10,... | collective-permute-start | bytes 2555912 | tf_op jit(solution)/shard_map/ppermute | solution.py:109
  97.8 28.9 %collective-permute-start.19 = (bf16[2,208,1024]{2,1,0:T(8,128)(2,1)S(1)}, bf16[2,208,1024]{2,1,0:T(8,128)(2,1)S(1)}, u32[]{:S(2)}, u32[]{:S(2)}) collective-permute-start(bf16[2,208,1024]{2,1,0:T(8,128)(2,1)S(1)} %collective-permute-done.11.wc0), channel_id=1, source_target_pairs={{0,2},{1,3},{2,0},{3,1},{4,6},{5,7},{6,4},{7,5},{8,10},{9,11},{10,... | collective-permute-start | bytes 2555912 | tf_op jit(solution)/shard_map/ppermute | solution.py:109
  125.4 13.3 %collective-permute-start.14 = (bf16[2,512,256]{2,1,0:T(8,128)(2,1)S(1)}, bf16[2,512,256]{2,1,0:T(8,128)(2,1)S(1)}, u32[]{:S(2)}, u32[]{:S(2)}) collective-permute-start(bf16[2,512,256]{2,1,0:T(8,128)(2,1)S(1)} %get-tuple-element.72), channel_id=1, source_target_pairs={{0,8},{1,9},{2,10},{3,11},{4,12},{5,13},{6,14},{7,15},{8,0},{9,1},... | collective-permute-start | bytes 1572872 | tf_op jit(solution)/shard_map/ppermute | solution.py:109
  126.7 12.4 %collective-permute-start.15 = (bf16[2,512,256]{2,1,0:T(8,128)(2,1)S(1)}, bf16[2,512,256]{2,1,0:T(8,128)(2,1)S(1)}, u32[]{:S(2)}, u32[]{:S(2)}) collective-permute-start(bf16[2,512,256]{2,1,0:T(8,128)(2,1)S(1)} %get-tuple-element.73), channel_id=1, source_target_pairs={{0,2},{1,3},{2,0},{3,1},{4,6},{5,7},{6,4},{7,5},{8,16},{9,17},{10,... | collective-permute-start | bytes 1572872 | tf_op jit(solution)/shard_map/ppermute | solution.py:109
  148.4 12.4 %collective-permute-start.29 = (bf16[256,256]{1,0:T(8,128)(2,1)S(1)}, bf16[256,256]{1,0:T(8,128)(2,1)S(1)}, u32[]{:S(2)}, u32[]{:S(2)}) collective-permute-start(bf16[256,256]{1,0:T(8,128)(2,1)S(1)} %get-tuple-element.87), channel_id=1, source_target_pairs={{0,7},{1,6},{2,5},{3,4},{4,3},{5,2},{6,1},{7,0},{8,15},{9,14},{10,... | collective-permute-start | bytes 393224 | tf_op jit(solution)/shard_map/ppermute | solution.py:109
  150.6 10.2 %collective-permute-start.30 = (bf16[256,256]{1,0:T(8,128)(2,1)S(1)}, bf16[256,256]{1,0:T(8,128)(2,1)S(1)}, u32[]{:S(2)}, u32[]{:S(2)}) collective-permute-start(bf16[256,256]{1,0:T(8,128)(2,1)S(1)} %get-tuple-element.87), channel_id=1, source_target_pairs={{0,6},{1,7},{2,4},{3,5},{4,2},{5,3},{6,0},{7,1},{8,14},{9,15},{10,... | collective-permute-start | bytes 393224 | tf_op jit(solution)/shard_map/ppermute | solution.py:109
  150.7 11.7 %collective-permute-start.32 = (bf16[256,256]{1,0:T(8,128)(2,1)S(1)}, bf16[256,256]{1,0:T(8,128)(2,1)S(1)}, u32[]{:S(2)}, u32[]{:S(2)}) collective-permute-start(bf16[256,256]{1,0:T(8,128)(2,1)S(1)} %get-tuple-element.85), channel_id=1, source_target_pairs={{0,5},{1,4},{2,7},{3,6},{4,1},{5,0},{6,3},{7,2},{8,13},{9,12},{10,... | collective-permute-start | bytes 393224 | tf_op jit(solution)/shard_map/ppermute | solution.py:109
  153.2 9.2 %collective-permute-start.31 = (bf16[256,256]{1,0:T(8,128)(2,1)S(1)}, bf16[256,256]{1,0:T(8,128)(2,1)S(1)}, u32[]{:S(2)}, u32[]{:S(2)}) collective-permute-start(bf16[256,256]{1,0:T(8,128)(2,1)S(1)} %get-tuple-element.88), channel_id=1, source_target_pairs={{0,3},{1,2},{2,1},{3,0},{4,7},{5,6},{6,5},{7,4},{8,11},{9,10},{10,... | collective-permute-start | bytes 393224 | tf_op jit(solution)/shard_map/ppermute | solution.py:109
  153.9 8.5 %collective-permute-start.33 = (bf16[256,256]{1,0:T(8,128)(2,1)S(1)}, bf16[256,256]{1,0:T(8,128)(2,1)S(1)}, u32[]{:S(2)}, u32[]{:S(2)}) collective-permute-start(bf16[256,256]{1,0:T(8,128)(2,1)S(1)} %get-tuple-element.88), channel_id=1, source_target_pairs={{0,2},{1,3},{2,0},{3,1},{4,6},{5,7},{6,4},{7,5},{8,10},{9,11},{10,... | collective-permute-start | bytes 393224 | tf_op jit(solution)/shard_map/ppermute | solution.py:109
  (18 other events, 151.5 us)

commit v19 on v18

--- a/solution.py
+++ b/solution.py
@@ -510,17 +510,15 @@
     )
     out_last = even_pair(out_far)
     x2 = in_slab(x0, 2)
-    far, x1 = half_pair(own), in_slab(x0, 1)
-    out_last, own, x1 = tied(out_last, own, x1)
-    near = even_pair(own)
+    far, near = half_pair(own), even_pair(own)
     close, away = jnp.stack([out_own, out_near]), jnp.stack([out_far, out_last])
     pad = ((0, 0), (0, -close.shape[1] % 16), (0, 0))
     keep = jnp.pad(jnp.where(home, close, away), pad)
     got = across(jnp.pad(jnp.where(home, away, close), pad))
     keep_x = in_slab(keep, 2)
-    near, far, x1, x2, got, keep_x = tied(near, far, x1, x2, got, keep_x)
+    near, far, x0, x2, got, keep_x = tied(near, far, x0, x2, got, keep_x)
     last = even_pair(far)
-    x3 = in_slab(x2, 1)
+    x1, x3 = in_slab(x0, 1), in_slab(x2, 1)
     got_x, got_c, keep_c = in_slab(got, 2), in_slab(got, 1), in_slab(keep, 1)
     keep_xc = in_slab(tied(keep_x, x3)[0], 1)
     xs = (x0, x1, x2, x3)

time: 167 us -> 163 us (0.976)
  starting transfers between devices: 39.4 us -> 34.2 us
  waiting for transfers between devices: 85.1 us -> 87.1 us
    ppermute x34, starting transfers between devices: 39.4 us -> 34.2 us  [permuted(): return lax.ppermute(x, ('seq', 'tp'), pairs)]
    ppermute x34, waiting for transfers between devices: 85.1 us -> 87.1 us  [permuted(): return lax.ppermute(x, ('seq', 'tp'), pairs)]
  transfers between devices with their start and end apart: 34 -> 34, of which waited for: 13 -> 13; matrix products, arithmetic and copies ran while one was open for 6% -> 6% of each run, Pallas kernels for 15% -> 16%
where the time goes in v19:
time: 163 us; the launch traced here: 162 us
  waiting for transfers between devices  87.1 us (53%)
  starting transfers between devices  34.2 us (21%)
  Pallas kernels  29.1 us (18%)
  local copies, waits for them, and re-layouts  6.51 us (4%)
  other arithmetic  4.53 us (3%)
    ppermute x34, waiting for transfers between devices, permuted(): return lax.ppermute(x, ('seq', 'tp'), pairs)  87.1 us
    ppermute x34, starting transfers between devices, permuted(): return lax.ppermute(x, ('seq', 'tp'), pairs)  34.2 us
    pallas_call x1, Pallas kernels, early(): pl.pallas_call(early_kernel, out_shape=(jax.ShapeDtypeStruct((SLAB, kinds...  9.34 us
    pallas_call x1, Pallas kernels, attend(): pl.pallas_call(functools.partial(attend_kernel, full_width), out_shape=(j...  6.16 us
    pallas_call x1, Pallas kernels, collect(): pl.pallas_call(collect_kernel, out_shape=jax.ShapeDtypeStruct((2, 2 * SLA...  3.82 us
    pallas_call x1, Pallas kernels, output(): pl.pallas_call(out_kernel, out_shape=jax.ShapeDtypeStruct((share, count),...  3.82 us
    pallas_call x1, Pallas kernels, norm(): pl.pallas_call(norm_kernel, out_shape=jax.ShapeDtypeStruct(shape, jnp.bfl...  3.54 us
  transfers between devices with their start and end apart: 34, of which 13 were waited for; matrix products, arithmetic and copies ran while one was open for 6% of the time, Pallas kernels for 16%

profile of v19, /device:TPU:9, one launch (start us, length us, event | category | flops | bytes accessed | tf_op | source)
XLA Modules:
  0.0 161.7 jit_solution(16368437210562705812)
XLA Ops:
  0.0 2.5 %collective-permute-start.4 = (bf16[200,1024]{1,0:T(8,128)(2,1)}, bf16[200,1024]{1,0:T(8,128)(2,1)}, u32[]{:S(2)}, u32[]{:S(2)}) collective-permute-start(bf16[200,1024]{1,0:T(8,128)(2,1)} %bitcast.43), channel_id=1, source_target_pairs={{0,16},{1,17},{2,18},{3,19},{4,20},{5,21},{6,22},{7,23},{8,24},{9,... | collective-permute-start | bytes 1228808 | tf_op jit(solution)/shard_map/ppermute | solution.py:109
  2.5 2.1 %dynamic-slice_bitcast_fusion.2 = (bf16[3,200,256]{2,1,0:T(8,128)(2,1)}, bf16[3,200,256]{2,1,0:T(8,128)(2,1)}, bf16[3,200,256]{2,1,0:T(8,128)(2,1)}) fusion(bf16[200,3,1024]{2,0,1:T(8,128)(2,1)} %param.10, s32[]{:T(128)S(6)} %select_n.142, s32[]{:T(128)S(6)} %select_n.144, s32[]{:T(128)S(6)} %select_n.146), kind=kLoop, calls=%fused_computation.16 | loop fusion | bytes 1843212 | tf_op jit(solution)/shard_map/dynamic_slice | solution.py:492
  4.6 2.3 %collective-permute-start = (bf16[3,200,256]{2,1,0:T(8,128)(2,1)}, bf16[3,200,256]{2,1,0:T(8,128)(2,1)}, u32[]{:S(2)}, u32[]{:S(2)}) collective-permute-start(bf16[3,200,256]{2,1,0:T(8,128)(2,1)} %get-tuple-element.103), channel_id=1, source_target_pairs={{0,6},{1,7},{2,4},{3,5},{4,2},{5,3},{6,0},{7,1},{8,14},{9,15},{10,... | collective-permute-start | bytes 921608 | tf_op jit(solution)/shard_map/ppermute | solution.py:109
  11.2 3.5 %norm.1.xa = bf16[4,256,896]{2,1,0:T(8,128)(2,1)} custom-call(bf16[256,3200]{1,0:T(8,128)(2,1)} %tokens.1, f32[1,3200]{1,0:T(1,128)} %broadcast_in_dim.34.gain), custom_call_target="tpu_custom_call" | custom-call | tf_op jit(solution)/shard_map/norm/pallas_call | solution.py:168
  15.4 6.5 %collective-permute-done.1 = bf16[3,200,256]{2,1,0:T(8,128)(2,1)} collective-permute-done((bf16[3,200,256]{2,1,0:T(8,128)(2,1)}, bf16[3,200,256]{2,1,0:T(8,128)(2,1)}, u32[]{:S(2)}, u32[]{:S(2)}) %collective-permute-start.1) | collective-permute-done | bytes 307232 | tf_op jit(solution)/shard_map/ppermute | solution.py:109
  21.9 1.6 fusion.1
  27.8 35.0 %collective-permute-done.8 = bf16[200,1024]{1,0:T(8,128)(2,1)S(1)} collective-permute-done((bf16[200,1024]{1,0:T(8,128)(2,1)}, bf16[200,1024]{1,0:T(8,128)(2,1)S(1)}, u32[]{:S(2)}, u32[]{:S(2)}) %collective-permute-start.8) | collective-permute-done | bytes 409632 | tf_op jit(solution)/shard_map/ppermute | solution.py:109
  65.7 23.4 %collective-permute-done.5.near = bf16[3,800,256]{2,1,0:T(8,128)(2,1)} collective-permute-done((bf16[3,800,256]{2,1,0:T(8,128)(2,1)}, bf16[3,800,256]{2,1,0:T(8,128)(2,1)}, u32[]{:S(2)}, u32[]{:S(2)}) %collective-permute-start.5) | collective-permute-done | bytes 1228832 | tf_op jit(solution)/shard_map/ppermute | solution.py:109
  94.0 2.4 %collective-permute-done.13.xd = bf16[4,256,896]{2,1,0:T(8,128)(2,1)S(1)} collective-permute-done((bf16[4,256,896]{2,1,0:T(8,128)(2,1)}, bf16[4,256,896]{2,1,0:T(8,128)(2,1)S(1)}, u32[]{:S(2)}, u32[]{:S(2)}) %collective-permute-start.13) | collective-permute-done | bytes 1835040 | tf_op jit(solution)/shard_map/ppermute | solution.py:109
  97.4 9.3 %early.1 = (f32[4,3,256,256]{3,2,1,0:T(8,128)S(1)}, bf16[4,256,896]{2,1,0:T(8,128)(2,1)S(1)}) custom-call(s32[3]{0:T(128)S(1)} %pad_add_fusion.1.place, bf16[4,256,896]{2,1,0:T(8,128)(2,1)S(1)} %copy-done, bf16[4,256,896]{2,1,0:T(8,128)(2,1)S(1)} %collective-permute-done.12.xb, bf16[4,256,896]{2,1,0:T(8,128)(2,1)} %collective-permute-done.7.xc, ...), custom_call_target="tpu_custom_call" | custom-call | flops 7549747200 | bytes 8601600 | tf_op jit(solution)/shard_map/early/pallas_call | solution.py:216
  106.7 12.7 %collective-permute-done.11.last = bf16[3,800,256]{2,1,0:T(8,128)(2,1)S(1)} collective-permute-done((bf16[3,800,256]{2,1,0:T(8,128)(2,1)}, bf16[3,800,256]{2,1,0:T(8,128)(2,1)S(1)}, u32[]{:S(2)}, u32[]{:S(2)}) %collective-permute-start.11) | collective-permute-done | bytes 1228832 | tf_op jit(solution)/shard_map/ppermute | solution.py:109
  119.4 2.5 %late.1 = (f32[1024,256]{1,0:T(8,128)S(1)}, bf16[1024,256]{1,0:T(8,128)(2,1)S(1)}, bf16[1024,256]{1,0:T(8,128)(2,1)S(1)}, f32[2,1024]{1,0:T(2,128)S(1)}, bf16[2,...) custom-call(s32[3]{0:T(128)S(1)} %pad_add_fusion.1.place, bf16[4,256,896]{2,1,0:T(8,128)(2,1)S(1)} %get-tuple-element.58.x_last, ...), custom_call_target="tpu_custom_call" | custom-call | flops 1258291200 | bytes 2867200 | tf_op jit(solution)/shard_map/late/pallas_call | solution.py:273
  123.6 1.6 collective-permute-start.20
  130.6 1.6 collective-permute-done.23
  132.2 1.7 %collective-permute-start.25 = (f32[2,1024]{1,0:T(2,128)S(1)}, f32[2,1024]{1,0:T(2,128)S(1)}, u32[]{:S(2)}, u32[]{:S(2)}) collective-permute-start(f32[2,1024]{1,0:T(2,128)S(1)} %add.114.mine), channel_id=1, source_target_pairs={{0,2},{1,3},{2,0},{3,1},{4,6},{5,7},{6,4},{7,5},{8,16},{9,17},{10,... | collective-permute-start | bytes 24584 | tf_op jit(solution)/shard_map/ppermute | solution.py:109
  133.8 1.5 collective-permute-start.26
  135.4 6.2 %attend.1 = (bf16[256,256]{1,0:T(8,128)(2,1)S(1)}, bf16[256,256]{1,0:T(8,128)(2,1)S(1)}, bf16[256,256]{1,0:T(8,128)(2,1)S(1)}, bf16[256,256]{1,0:T(8,128)(2,1)S(1)}) custom-call(s32[3]{0:T(128)S(1)} %pad_add_fusion.1.place, s32[4,2]{1,0:T(4,128)S(1)} %pad_add_fusion.spans, f32[1024,256]{1,0:T(8,128)S(1)} %get-tuple-element.63.query, ...), custom_call_target="tpu_custom_call" | custom-call | flops 21474836480 | bytes 3145728 | tf_op jit(solution)/shard_map/attend/pallas_call | solution.py:376
  143.6 3.6 %collective-permute-start.29 = (bf16[256,256]{1,0:T(8,128)(2,1)S(1)}, bf16[256,256]{1,0:T(8,128)(2,1)S(1)}, u32[]{:S(2)}, u32[]{:S(2)}) collective-permute-start(bf16[256,256]{1,0:T(8,128)(2,1)S(1)} %get-tuple-element.81), channel_id=1, source_target_pairs={{0,7},{1,6},{2,5},{3,4},{4,3},{5,2},{6,1},{7,0},{8,15},{9,14},{10,... | collective-permute-start | bytes 393224 | tf_op jit(solution)/shard_map/ppermute | solution.py:109
  147.2 1.7 %collective-permute-start.32 = (bf16[256,256]{1,0:T(8,128)(2,1)S(1)}, bf16[256,256]{1,0:T(8,128)(2,1)S(1)}, u32[]{:S(2)}, u32[]{:S(2)}) collective-permute-start(bf16[256,256]{1,0:T(8,128)(2,1)S(1)} %get-tuple-element.79), channel_id=1, source_target_pairs={{0,5},{1,4},{2,7},{3,6},{4,1},{5,0},{6,3},{7,2},{8,13},{9,12},{10,... | collective-permute-start | bytes 393224 | tf_op jit(solution)/shard_map/ppermute | solution.py:109
  148.9 1.5 collective-permute-start.31
  150.4 2.1 %collective-permute-start.33 = (bf16[256,256]{1,0:T(8,128)(2,1)S(1)}, bf16[256,256]{1,0:T(8,128)(2,1)S(1)}, u32[]{:S(2)}, u32[]{:S(2)}) collective-permute-start(bf16[256,256]{1,0:T(8,128)(2,1)S(1)} %get-tuple-element.82), channel_id=1, source_target_pairs={{0,2},{1,3},{2,0},{3,1},{4,6},{5,7},{6,4},{7,5},{8,10},{9,11},{10,... | collective-permute-start | bytes 393224 | tf_op jit(solution)/shard_map/ppermute | solution.py:109
  152.5 3.8 %collect.1.w = bf16[2,1664,1024]{2,1,0:T(8,128)(2,1)S(1)} custom-call(bf16[2,208,1024]{2,1,0:T(8,128)(2,1)S(1)} %pad.13.wa0, bf16[2,208,1024]{2,1,0:T(8,128)(2,1)S(1)} %collective-permute-done.18.wb0, bf16[2,208,1024]{2,1,0:T(8,128)(2,1)S(1)} %collective-permute-done.10.wc0, bf16[2,208,1024]{2,1,0:T(8,128)(2,1)S(1)} %collective-permute-done.19.wd0, ...), custom_call_target="tpu_custom_call" | custom-call | bytes 13631488 | tf_op jit(solution)/shard_map/collect/pallas_call | solution.py:411
  156.4 1.5 collective-permute-done.32.c21
  157.9 3.8 %output.1 = bf16[1600,256]{1,0:T(8,128)(2,1)} custom-call(s32[3]{0:T(128)S(1)} %pad_add_fusion.1.place, bf16[256,256]{1,0:T(8,128)(2,1)S(1)} %collective-permute-done.27.c20, bf16[256,256]{1,0:T(8,128)(2,1)S(1)} %collective-permute-done.28.c01, bf16[256,256]{1,0:T(8,128)(2,1)S(1)} %collective-permute-done.29.c31, ...), custom_call_target="tpu_custom_call" | custom-call | flops 1677721600 | bytes 6553600 | tf_op jit(solution)/shard_map/output/pallas_call | solution.py:450
  (89 shorter events, 27.3 us)
Async XLA Ops:
  0.0 24.6 %collective-permute-start.3 = (bf16[200,1024]{1,0:T(8,128)(2,1)}, bf16[200,1024]{1,0:T(8,128)(2,1)}, u32[]{:S(2)}, u32[]{:S(2)}) collective-permute-start(bf16[200,1024]{1,0:T(8,128)(2,1)} %bitcast.42), channel_id=1, source_target_pairs={{0,8},{1,9},{2,10},{3,11},{4,12},{5,13},{6,14},{7,15},{8,0},{9,1},... | collective-permute-start | bytes 1228808 | tf_op jit(solution)/shard_map/ppermute | solution.py:109
  0.0 24.6 %collective-permute-start.4 = (bf16[200,1024]{1,0:T(8,128)(2,1)}, bf16[200,1024]{1,0:T(8,128)(2,1)}, u32[]{:S(2)}, u32[]{:S(2)}) collective-permute-start(bf16[200,1024]{1,0:T(8,128)(2,1)} %bitcast.43), channel_id=1, source_target_pairs={{0,16},{1,17},{2,18},{3,19},{4,20},{5,21},{6,22},{7,23},{8,24},{9,... | collective-permute-start | bytes 1228808 | tf_op jit(solution)/shard_map/ppermute | solution.py:109
  4.6 10.8 %collective-permute-start = (bf16[3,200,256]{2,1,0:T(8,128)(2,1)}, bf16[3,200,256]{2,1,0:T(8,128)(2,1)}, u32[]{:S(2)}, u32[]{:S(2)}) collective-permute-start(bf16[3,200,256]{2,1,0:T(8,128)(2,1)} %get-tuple-element.103), channel_id=1, source_target_pairs={{0,6},{1,7},{2,4},{3,5},{4,2},{5,3},{6,0},{7,1},{8,14},{9,15},{10,... | collective-permute-start | bytes 921608 | tf_op jit(solution)/shard_map/ppermute | solution.py:109
  6.9 14.9 %collective-permute-start.1 = (bf16[3,200,256]{2,1,0:T(8,128)(2,1)}, bf16[3,200,256]{2,1,0:T(8,128)(2,1)}, u32[]{:S(2)}, u32[]{:S(2)}) collective-permute-start(bf16[3,200,256]{2,1,0:T(8,128)(2,1)} %get-tuple-element.104), channel_id=1, source_target_pairs={{0,4},{1,5},{2,6},{3,7},{4,0},{5,1},{6,2},{7,3},{8,12},{9,13},{10,... | collective-permute-start | bytes 921608 | tf_op jit(solution)/shard_map/ppermute | solution.py:109
  7.2 14.7 %collective-permute-start.2 = (bf16[3,200,256]{2,1,0:T(8,128)(2,1)}, bf16[3,200,256]{2,1,0:T(8,128)(2,1)}, u32[]{:S(2)}, u32[]{:S(2)}) collective-permute-start(bf16[3,200,256]{2,1,0:T(8,128)(2,1)} %get-tuple-element.105), channel_id=1, source_target_pairs={{0,2},{1,3},{2,0},{3,1},{4,6},{5,7},{6,4},{7,5},{8,10},{9,11},{10,... | collective-permute-start | bytes 921608 | tf_op jit(solution)/shard_map/ppermute | solution.py:109
  25.4 64.5 %collective-permute-start.7 = (bf16[4,256,896]{2,1,0:T(8,128)(2,1)S(1)}, bf16[4,256,896]{2,1,0:T(8,128)(2,1)}, u32[]{:S(2)}, u32[]{:S(2)}) collective-permute-start(bf16[4,256,896]{2,1,0:T(8,128)(2,1)S(1)} %copy-done), channel_id=1, source_target_pairs={{0,4},{1,5},{2,6},{3,7},{4,0},{5,1},{6,2},{7,3},{8,12},{9,13},{10,... | collective-permute-start | bytes 5505032 | tf_op jit(solution)/shard_map/ppermute | solution.py:109
  26.1 36.6 %collective-permute-start.8 = (bf16[200,1024]{1,0:T(8,128)(2,1)}, bf16[200,1024]{1,0:T(8,128)(2,1)S(1)}, u32[]{:S(2)}, u32[]{:S(2)}) collective-permute-start(bf16[200,1024]{1,0:T(8,128)(2,1)} %collective-permute-done.4), channel_id=1, source_target_pairs={{0,8},{1,9},{2,10},{3,11},{4,12},{5,13},{6,14},{7,15},{8,0},{9,1},... | collective-permute-start | bytes 1228808 | tf_op jit(solution)/shard_map/ppermute | solution.py:109
  27.4 61.7 %collective-permute-start.5 = (bf16[3,800,256]{2,1,0:T(8,128)(2,1)}, bf16[3,800,256]{2,1,0:T(8,128)(2,1)}, u32[]{:S(2)}, u32[]{:S(2)}) collective-permute-start(bf16[3,800,256]{2,1,0:T(8,128)(2,1)} %pad_maximum_fusion.own), channel_id=1, source_target_pairs={{0,8},{1,9},{2,10},{3,11},{4,12},{5,13},{6,14},{7,15},{8,0},{9,1},... | collective-permute-start | bytes 3686408 | tf_op jit(solution)/shard_map/ppermute | solution.py:109
  27.6 62.3 %collective-permute-start.6 = (bf16[3,800,256]{2,1,0:T(8,128)(2,1)}, bf16[3,800,256]{2,1,0:T(8,128)(2,1)}, u32[]{:S(2)}, u32[]{:S(2)}) collective-permute-start(bf16[3,800,256]{2,1,0:T(8,128)(2,1)} %pad_maximum_fusion.own), channel_id=1, source_target_pairs={{0,16},{1,17},{2,18},{3,19},{4,20},{5,21},{6,22},{7,23},{8,24},{9,... | collective-permute-start | bytes 3686408 | tf_op jit(solution)/shard_map/ppermute | solution.py:109
  64.1 25.8 %collective-permute-start.10 = (bf16[2,208,1024]{2,1,0:T(8,128)(2,1)S(1)}, bf16[2,208,1024]{2,1,0:T(8,128)(2,1)S(1)}, u32[]{:S(2)}, u32[]{:S(2)}) collective-permute-start(bf16[2,208,1024]{2,1,0:T(8,128)(2,1)S(1)} %pad.13.wa0), channel_id=1, source_target_pairs={{0,4},{1,5},{2,6},{3,7},{4,0},{5,1},{6,2},{7,3},{8,12},{9,13},{10,... | collective-permute-start | bytes 2555912 | tf_op jit(solution)/shard_map/ppermute | solution.py:109
  64.4 25.5 %collective-permute-start.9 = (bf16[2,208,1024]{2,1,0:T(8,128)(2,1)S(1)}, bf16[2,208,1024]{2,1,0:T(8,128)(2,1)S(1)}, u32[]{:S(2)}, u32[]{:S(2)}) collective-permute-start(bf16[2,208,1024]{2,1,0:T(8,128)(2,1)S(1)} %pad.12), channel_id=1, source_target_pairs={{0,1},{1,0},{2,3},{3,2},{4,5},{5,4},{6,7},{7,6},{8,9},{9,8},{10,11... | collective-permute-start | bytes 2555912 | tf_op jit(solution)/shard_map/ppermute | solution.py:109
  91.0 28.4 %collective-permute-start.11 = (bf16[3,800,256]{2,1,0:T(8,128)(2,1)}, bf16[3,800,256]{2,1,0:T(8,128)(2,1)S(1)}, u32[]{:S(2)}, u32[]{:S(2)}) collective-permute-start(bf16[3,800,256]{2,1,0:T(8,128)(2,1)} %collective-permute-done.6.far), channel_id=1, source_target_pairs={{0,8},{1,9},{2,10},{3,11},{4,12},{5,13},{6,14},{7,15},{8,0},{9,1},... | collective-permute-start | bytes 3686408 | tf_op jit(solution)/shard_map/ppermute | solution.py:109
  92.5 30.9 %collective-permute-start.18 = (bf16[2,208,1024]{2,1,0:T(8,128)(2,1)S(1)}, bf16[2,208,1024]{2,1,0:T(8,128)(2,1)S(1)}, u32[]{:S(2)}, u32[]{:S(2)}) collective-permute-start(bf16[2,208,1024]{2,1,0:T(8,128)(2,1)S(1)} %pad.13.wa0), channel_id=1, source_target_pairs={{0,2},{1,3},{2,0},{3,1},{4,6},{5,7},{6,4},{7,5},{8,10},{9,11},{10,... | collective-permute-start | bytes 2555912 | tf_op jit(solution)/shard_map/ppermute | solution.py:109
  93.3 30.3 %collective-permute-start.16 = (bf16[2,208,1024]{2,1,0:T(8,128)(2,1)S(1)}, bf16[2,208,1024]{2,1,0:T(8,128)(2,1)S(1)}, u32[]{:S(2)}, u32[]{:S(2)}) collective-permute-start(bf16[2,208,1024]{2,1,0:T(8,128)(2,1)S(1)} %collective-permute-done.9.wa1), channel_id=1, source_target_pairs={{0,4},{1,5},{2,6},{3,7},{4,0},{5,1},{6,2},{7,3},{8,12},{9,13},{10,... | collective-permute-start | bytes 2555912 | tf_op jit(solution)/shard_map/ppermute | solution.py:109
  96.4 27.1 %collective-permute-start.17 = (bf16[2,208,1024]{2,1,0:T(8,128)(2,1)S(1)}, bf16[2,208,1024]{2,1,0:T(8,128)(2,1)S(1)}, u32[]{:S(2)}, u32[]{:S(2)}) collective-permute-start(bf16[2,208,1024]{2,1,0:T(8,128)(2,1)S(1)} %collective-permute-done.9.wa1), channel_id=1, source_target_pairs={{0,2},{1,3},{2,0},{3,1},{4,6},{5,7},{6,4},{7,5},{8,10},{9,11},{10,... | collective-permute-start | bytes 2555912 | tf_op jit(solution)/shard_map/ppermute | solution.py:109
  97.0 26.6 %collective-permute-start.19 = (bf16[2,208,1024]{2,1,0:T(8,128)(2,1)S(1)}, bf16[2,208,1024]{2,1,0:T(8,128)(2,1)S(1)}, u32[]{:S(2)}, u32[]{:S(2)}) collective-permute-start(bf16[2,208,1024]{2,1,0:T(8,128)(2,1)S(1)} %collective-permute-done.10.wc0), channel_id=1, source_target_pairs={{0,2},{1,3},{2,0},{3,1},{4,6},{5,7},{6,4},{7,5},{8,10},{9,11},{10,... | collective-permute-start | bytes 2555912 | tf_op jit(solution)/shard_map/ppermute | solution.py:109
  121.9 13.4 %collective-permute-start.14 = (bf16[2,512,256]{2,1,0:T(8,128)(2,1)S(1)}, bf16[2,512,256]{2,1,0:T(8,128)(2,1)S(1)}, u32[]{:S(2)}, u32[]{:S(2)}) collective-permute-start(bf16[2,512,256]{2,1,0:T(8,128)(2,1)S(1)} %get-tuple-element.66), channel_id=1, source_target_pairs={{0,8},{1,9},{2,10},{3,11},{4,12},{5,13},{6,14},{7,15},{8,0},{9,1},... | collective-permute-start | bytes 1572872 | tf_op jit(solution)/shard_map/ppermute | solution.py:109
  123.3 12.0 %collective-permute-start.15 = (bf16[2,512,256]{2,1,0:T(8,128)(2,1)S(1)}, bf16[2,512,256]{2,1,0:T(8,128)(2,1)S(1)}, u32[]{:S(2)}, u32[]{:S(2)}) collective-permute-start(bf16[2,512,256]{2,1,0:T(8,128)(2,1)S(1)} %get-tuple-element.67), channel_id=1, source_target_pairs={{0,2},{1,3},{2,0},{3,1},{4,6},{5,7},{6,4},{7,5},{8,16},{9,17},{10,... | collective-permute-start | bytes 1572872 | tf_op jit(solution)/shard_map/ppermute | solution.py:109
  133.8 7.7 %collective-permute-start.26 = (bf16[2,208,1024]{2,1,0:T(8,128)(2,1)S(1)}, bf16[2,208,1024]{2,1,0:T(8,128)(2,1)S(1)}, u32[]{:S(2)}, u32[]{:S(2)}) collective-permute-start(bf16[2,208,1024]{2,1,0:T(8,128)(2,1)S(1)} %collective-permute-done.16.wc1), channel_id=1, source_target_pairs={{0,2},{1,3},{2,0},{3,1},{4,6},{5,7},{6,4},{7,5},{8,10},{9,11},{10,... | collective-permute-start | bytes 2555912 | tf_op jit(solution)/shard_map/ppermute | solution.py:109
  142.4 8.0 %collective-permute-start.28 = (bf16[256,256]{1,0:T(8,128)(2,1)S(1)}, bf16[256,256]{1,0:T(8,128)(2,1)S(1)}, u32[]{:S(2)}, u32[]{:S(2)}) collective-permute-start(bf16[256,256]{1,0:T(8,128)(2,1)S(1)} %get-tuple-element.80.c00), channel_id=1, source_target_pairs={{0,1},{1,0},{2,3},{3,2},{4,5},{5,4},{6,7},{7,6},{8,9},{9,8},{10,11... | collective-permute-start | bytes 393224 | tf_op jit(solution)/shard_map/ppermute | solution.py:109
  143.6 12.7 %collective-permute-start.29 = (bf16[256,256]{1,0:T(8,128)(2,1)S(1)}, bf16[256,256]{1,0:T(8,128)(2,1)S(1)}, u32[]{:S(2)}, u32[]{:S(2)}) collective-permute-start(bf16[256,256]{1,0:T(8,128)(2,1)S(1)} %get-tuple-element.81), channel_id=1, source_target_pairs={{0,7},{1,6},{2,5},{3,4},{4,3},{5,2},{6,1},{7,0},{8,15},{9,14},{10,... | collective-permute-start | bytes 393224 | tf_op jit(solution)/shard_map/ppermute | solution.py:109
  147.2 9.2 %collective-permute-start.30 = (bf16[256,256]{1,0:T(8,128)(2,1)S(1)}, bf16[256,256]{1,0:T(8,128)(2,1)S(1)}, u32[]{:S(2)}, u32[]{:S(2)}) collective-permute-start(bf16[256,256]{1,0:T(8,128)(2,1)S(1)} %get-tuple-element.81), channel_id=1, source_target_pairs={{0,6},{1,7},{2,4},{3,5},{4,2},{5,3},{6,0},{7,1},{8,14},{9,15},{10,... | collective-permute-start | bytes 393224 | tf_op jit(solution)/shard_map/ppermute | solution.py:109
  147.2 10.6 %collective-permute-start.32 = (bf16[256,256]{1,0:T(8,128)(2,1)S(1)}, bf16[256,256]{1,0:T(8,128)(2,1)S(1)}, u32[]{:S(2)}, u32[]{:S(2)}) collective-permute-start(bf16[256,256]{1,0:T(8,128)(2,1)S(1)} %get-tuple-element.79), channel_id=1, source_target_pairs={{0,5},{1,4},{2,7},{3,6},{4,1},{5,0},{6,3},{7,2},{8,13},{9,12},{10,... | collective-permute-start | bytes 393224 | tf_op jit(solution)/shard_map/ppermute | solution.py:109
  150.4 7.5 %collective-permute-start.33 = (bf16[256,256]{1,0:T(8,128)(2,1)S(1)}, bf16[256,256]{1,0:T(8,128)(2,1)S(1)}, u32[]{:S(2)}, u32[]{:S(2)}) collective-permute-start(bf16[256,256]{1,0:T(8,128)(2,1)S(1)} %get-tuple-element.82), channel_id=1, source_target_pairs={{0,2},{1,3},{2,0},{3,1},{4,6},{5,7},{6,4},{7,5},{8,10},{9,11},{10,... | collective-permute-start | bytes 393224 | tf_op jit(solution)/shard_map/ppermute | solution.py:109
  (16 other events, 114.4 us)

commit v20 on v19

--- a/solution.py
+++ b/solution.py
@@ -490,9 +490,9 @@
 
     by_kind = jnp.transpose(qkv_weight, (1, 0, 2))
     cut = [lax.dynamic_slice_in_dim(by_kind, (q ^ r) * width, width, 2) for r in range(SLAB)]
+    *cut, out_own = tied(*cut, jnp.transpose(out_weight))
     got = [cut[0]] + [in_slab(cut[r], r) for r in range(1, SLAB)]
     x0 = norm(tokens, norm_gain, slabs)
-    out_own = jnp.transpose(out_weight)
     own = rows_of_slab(q, got)
     out_near, out_far = even_pair(out_own), half_pair(out_own)
     gains = [lax.dynamic_slice_in_dim(g, q * width, width, 0)[None] for g in (q_gain, k_gain)]
@@ -505,8 +505,8 @@
     share = layer_scale.shape[0]
     residual = jnp.transpose(lax.dynamic_slice_in_dim(tokens, tp * share, share, 1))
     scale = jnp.pad(layer_scale, (0, -share % 128))[None]
-    own, x0, out_near, out_far, seg, spans, residual, scale, *gains = tied(
-        own, x0, out_near, out_far, seg, spans, residual, scale, *gains
+    x0, out_near, out_far, seg, spans, residual, scale, *gains = tied(
+        x0, out_near, out_far, seg, spans, residual, scale, *gains
     )
     out_last = even_pair(out_far)
     x2 = in_slab(x0, 2)

time: 163 us -> 160 us (0.982)
  waiting for transfers between devices: 87.1 us -> 84.6 us
    ppermute x34, waiting for transfers between devices: 87.1 us -> 84.6 us  [permuted(): return lax.ppermute(x, ('seq', 'tp'), pairs)]
  transfers between devices with their start and end apart: 34 -> 34, of which waited for: 13 -> 12; matrix products, arithmetic and copies ran while one was open for 6% -> 4% of each run, Pallas kernels for 16% -> 16%
where the time goes in v20:
time: 160 us; the launch traced here: 159 us
  waiting for transfers between devices  84.6 us (53%)
  starting transfers between devices  35.7 us (22%)
  Pallas kernels  29 us (18%)
  local copies, waits for them, and re-layouts  5.94 us (4%)
  other arithmetic  3.42 us (2%)
    ppermute x34, waiting for transfers between devices, permuted(): return lax.ppermute(x, ('seq', 'tp'), pairs)  84.6 us
    ppermute x34, starting transfers between devices, permuted(): return lax.ppermute(x, ('seq', 'tp'), pairs)  35.7 us
    pallas_call x1, Pallas kernels, early(): pl.pallas_call(early_kernel, out_shape=(jax.ShapeDtypeStruct((SLAB, kinds...  9.54 us
    pallas_call x1, Pallas kernels, attend(): pl.pallas_call(functools.partial(attend_kernel, full_width), out_shape=(j...  5.88 us
    pallas_call x1, Pallas kernels, collect(): pl.pallas_call(collect_kernel, out_shape=jax.ShapeDtypeStruct((2, 2 * SLA...  3.82 us
    pallas_call x1, Pallas kernels, output(): pl.pallas_call(out_kernel, out_shape=jax.ShapeDtypeStruct((share, count),...  3.82 us
    pallas_call x1, Pallas kernels, norm(): pl.pallas_call(norm_kernel, out_shape=jax.ShapeDtypeStruct(shape, jnp.bfl...  3.52 us
  transfers between devices with their start and end apart: 34, of which 12 were waited for; matrix products, arithmetic and copies ran while one was open for 4% of the time, Pallas kernels for 16%

profile of v20, /device:TPU:9, one launch (start us, length us, event | category | flops | bytes accessed | tf_op | source)
XLA Modules:
  0.0 158.9 jit_solution(5858884235809862647)
XLA Ops:
  0.0 2.3 %dynamic-slice_bitcast_fusion = (bf16[3,200,256]{2,1,0:T(8,128)(2,1)}, bf16[3,200,256]{2,1,0:T(8,128)(2,1)}, bf16[3,200,256]{2,1,0:T(8,128)(2,1)S(1)}, bf16[3,200,256]{2,1,0:T(8,128)(2,1)}) fusion(bf16[200,3,1024]{2,0,1:T(8,128)(2,1)} %param.10, s32[]{:T(128)S(6)} %select_n.144, s32[]{:T(128)S(6)} %select_n.142, s32[]{:T(128)S(6)} %select_n.141, s32[]{:T(128)S(6)} %select_n.143), kind=kLoop, calls=%fused_computation.9 | loop fusion | bytes 2457616 | tf_op jit(solution)/shard_map/dynamic_slice | solution.py:492
  2.4 2.5 %collective-permute-start.1 = (bf16[200,1024]{1,0:T(8,128)(2,1)S(1)}, bf16[200,1024]{1,0:T(8,128)(2,1)}, u32[]{:S(2)}, u32[]{:S(2)}) collective-permute-start(bf16[200,1024]{1,0:T(8,128)(2,1)S(1)} %bitcast.30), channel_id=1, source_target_pairs={{0,16},{1,17},{2,18},{3,19},{4,20},{5,21},{6,22},{7,23},{8,24},{9,... | collective-permute-start | bytes 1228808 | tf_op jit(solution)/shard_map/ppermute | solution.py:109
  4.9 2.3 %collective-permute-start.2 = (bf16[3,200,256]{2,1,0:T(8,128)(2,1)}, bf16[3,200,256]{2,1,0:T(8,128)(2,1)}, u32[]{:S(2)}, u32[]{:S(2)}) collective-permute-start(bf16[3,200,256]{2,1,0:T(8,128)(2,1)} %get-tuple-element.53), channel_id=1, source_target_pairs={{0,6},{1,7},{2,4},{3,5},{4,2},{5,3},{6,0},{7,1},{8,14},{9,15},{10,... | collective-permute-start | bytes 921608 | tf_op jit(solution)/shard_map/ppermute | solution.py:109
  11.5 3.5 %norm.1.xa = bf16[4,256,896]{2,1,0:T(8,128)(2,1)} custom-call(bf16[256,3200]{1,0:T(8,128)(2,1)} %tokens.1, f32[1,3200]{1,0:T(1,128)} %broadcast_in_dim.34.gain), custom_call_target="tpu_custom_call" | custom-call | tf_op jit(solution)/shard_map/norm/pallas_call | solution.py:168
  15.1 4.4 %collective-permute-done = bf16[200,1024]{1,0:T(8,128)(2,1)} collective-permute-done((bf16[200,1024]{1,0:T(8,128)(2,1)S(1)}, bf16[200,1024]{1,0:T(8,128)(2,1)}, u32[]{:S(2)}, u32[]{:S(2)}) %collective-permute-start) | collective-permute-done | bytes 409632 | tf_op jit(solution)/shard_map/ppermute | solution.py:109
  19.5 3.2 %collective-permute-done.1 = bf16[200,1024]{1,0:T(8,128)(2,1)} collective-permute-done((bf16[200,1024]{1,0:T(8,128)(2,1)S(1)}, bf16[200,1024]{1,0:T(8,128)(2,1)}, u32[]{:S(2)}, u32[]{:S(2)}) %collective-permute-start.1) | collective-permute-done | bytes 409632 | tf_op jit(solution)/shard_map/ppermute | solution.py:109
  26.9 29.3 %collective-permute-done.8 = bf16[200,1024]{1,0:T(8,128)(2,1)} collective-permute-done((bf16[200,1024]{1,0:T(8,128)(2,1)}, bf16[200,1024]{1,0:T(8,128)(2,1)}, u32[]{:S(2)}, u32[]{:S(2)}) %collective-permute-start.8) | collective-permute-done | bytes 409632 | tf_op jit(solution)/shard_map/ppermute | solution.py:109
  59.4 22.9 %collective-permute-done.5.near = bf16[3,800,256]{2,1,0:T(8,128)(2,1)S(1)} collective-permute-done((bf16[3,800,256]{2,1,0:T(8,128)(2,1)S(1)}, bf16[3,800,256]{2,1,0:T(8,128)(2,1)S(1)}, u32[]{:S(2)}, u32[]{:S(2)}) %collective-permute-start.5) | collective-permute-done | bytes 1228832 | tf_op jit(solution)/shard_map/ppermute | solution.py:109
  82.4 2.8 %collective-permute-done.6.far = bf16[3,800,256]{2,1,0:T(8,128)(2,1)} collective-permute-done((bf16[3,800,256]{2,1,0:T(8,128)(2,1)S(1)}, bf16[3,800,256]{2,1,0:T(8,128)(2,1)}, u32[]{:S(2)}, u32[]{:S(2)}) %collective-permute-start.6) | collective-permute-done | bytes 1228832 | tf_op jit(solution)/shard_map/ppermute | solution.py:109
  85.2 3.6 %collective-permute-start.13 = (bf16[4,256,896]{2,1,0:T(8,128)(2,1)}, bf16[4,256,896]{2,1,0:T(8,128)(2,1)S(1)}, u32[]{:S(2)}, u32[]{:S(2)}) collective-permute-start(bf16[4,256,896]{2,1,0:T(8,128)(2,1)} %collective-permute-done.7.xc), channel_id=1, source_target_pairs={{0,2},{1,3},{2,0},{3,1},{4,6},{5,7},{6,4},{7,5},{8,10},{9,11},{10,... | collective-permute-start | bytes 5505032 | tf_op jit(solution)/shard_map/ppermute | solution.py:109
  89.9 4.2 %collective-permute-done.13.xd = bf16[4,256,896]{2,1,0:T(8,128)(2,1)S(1)} collective-permute-done((bf16[4,256,896]{2,1,0:T(8,128)(2,1)}, bf16[4,256,896]{2,1,0:T(8,128)(2,1)S(1)}, u32[]{:S(2)}, u32[]{:S(2)}) %collective-permute-start.13) | collective-permute-done | bytes 1835040 | tf_op jit(solution)/shard_map/ppermute | solution.py:109
  95.1 9.5 %early.1 = (f32[4,3,256,256]{3,2,1,0:T(8,128)S(1)}, bf16[4,256,896]{2,1,0:T(8,128)(2,1)S(1)}) custom-call(s32[3]{0:T(128)S(1)} %pad_add_fusion.1.place, bf16[4,256,896]{2,1,0:T(8,128)(2,1)S(1)} %copy-done, bf16[4,256,896]{2,1,0:T(8,128)(2,1)S(1)} %collective-permute-done.12.xb, bf16[4,256,896]{2,1,0:T(8,128)(2,1)} %collective-permute-done.7.xc, ...), custom_call_target="tpu_custom_call" | custom-call | flops 7549747200 | bytes 8601600 | tf_op jit(solution)/shard_map/early/pallas_call | solution.py:216
  104.7 12.5 %collective-permute-done.11.last = bf16[3,800,256]{2,1,0:T(8,128)(2,1)S(1)} collective-permute-done((bf16[3,800,256]{2,1,0:T(8,128)(2,1)}, bf16[3,800,256]{2,1,0:T(8,128)(2,1)S(1)}, u32[]{:S(2)}, u32[]{:S(2)}) %collective-permute-start.11) | collective-permute-done | bytes 1228832 | tf_op jit(solution)/shard_map/ppermute | solution.py:109
  117.2 2.5 %late.1 = (f32[1024,256]{1,0:T(8,128)S(1)}, bf16[1024,256]{1,0:T(8,128)(2,1)S(1)}, bf16[1024,256]{1,0:T(8,128)(2,1)S(1)}, f32[2,1024]{1,0:T(2,128)S(1)}, bf16[2,...) custom-call(s32[3]{0:T(128)S(1)} %pad_add_fusion.1.place, bf16[4,256,896]{2,1,0:T(8,128)(2,1)S(1)} %get-tuple-element.66.x_last, ...), custom_call_target="tpu_custom_call" | custom-call | flops 1258291200 | bytes 2867200 | tf_op jit(solution)/shard_map/late/pallas_call | solution.py:273
  119.7 1.6 %collective-permute-start.15 = (bf16[2,512,256]{2,1,0:T(8,128)(2,1)S(1)}, bf16[2,512,256]{2,1,0:T(8,128)(2,1)S(1)}, u32[]{:S(2)}, u32[]{:S(2)}) collective-permute-start(bf16[2,512,256]{2,1,0:T(8,128)(2,1)S(1)} %get-tuple-element.75), channel_id=1, source_target_pairs={{0,2},{1,3},{2,0},{3,1},{4,6},{5,7},{6,4},{7,5},{8,16},{9,17},{10,... | collective-permute-start | bytes 1572872 | tf_op jit(solution)/shard_map/ppermute | solution.py:109
  121.3 1.6 collective-permute-start.20
  127.9 1.6 collective-permute-done.23
  130.9 1.7 %collective-permute-start.26 = (bf16[2,208,1024]{2,1,0:T(8,128)(2,1)S(1)}, bf16[2,208,1024]{2,1,0:T(8,128)(2,1)S(1)}, u32[]{:S(2)}, u32[]{:S(2)}) collective-permute-start(bf16[2,208,1024]{2,1,0:T(8,128)(2,1)S(1)} %collective-permute-done.16.wc1), channel_id=1, source_target_pairs={{0,2},{1,3},{2,0},{3,1},{4,6},{5,7},{6,4},{7,5},{8,10},{9,11},{10,... | collective-permute-start | bytes 2555912 | tf_op jit(solution)/shard_map/ppermute | solution.py:109
  132.6 5.9 %attend.1 = (bf16[256,256]{1,0:T(8,128)(2,1)S(1)}, bf16[256,256]{1,0:T(8,128)(2,1)S(1)}, bf16[256,256]{1,0:T(8,128)(2,1)S(1)}, bf16[256,256]{1,0:T(8,128)(2,1)S(1)}) custom-call(s32[3]{0:T(128)S(1)} %pad_add_fusion.1.place, s32[4,2]{1,0:T(4,128)S(1)} %pad_add_fusion.spans, f32[1024,256]{1,0:T(8,128)S(1)} %get-tuple-element.71.query, ...), custom_call_target="tpu_custom_call" | custom-call | flops 21474836480 | bytes 3145728 | tf_op jit(solution)/shard_map/attend/pallas_call | solution.py:376
  141.0 2.7 %collective-permute-start.29 = (bf16[256,256]{1,0:T(8,128)(2,1)S(1)}, bf16[256,256]{1,0:T(8,128)(2,1)S(1)}, u32[]{:S(2)}, u32[]{:S(2)}) collective-permute-start(bf16[256,256]{1,0:T(8,128)(2,1)S(1)} %get-tuple-element.89), channel_id=1, source_target_pairs={{0,7},{1,6},{2,5},{3,4},{4,3},{5,2},{6,1},{7,0},{8,15},{9,14},{10,... | collective-permute-start | bytes 393224 | tf_op jit(solution)/shard_map/ppermute | solution.py:109
  143.8 2.1 %collective-permute-start.32 = (bf16[256,256]{1,0:T(8,128)(2,1)S(1)}, bf16[256,256]{1,0:T(8,128)(2,1)S(1)}, u32[]{:S(2)}, u32[]{:S(2)}) collective-permute-start(bf16[256,256]{1,0:T(8,128)(2,1)S(1)} %get-tuple-element.87), channel_id=1, source_target_pairs={{0,5},{1,4},{2,7},{3,6},{4,1},{5,0},{6,3},{7,2},{8,13},{9,12},{10,... | collective-permute-start | bytes 393224 | tf_op jit(solution)/shard_map/ppermute | solution.py:109
  147.0 2.8 %collective-permute-start.33 = (bf16[256,256]{1,0:T(8,128)(2,1)S(1)}, bf16[256,256]{1,0:T(8,128)(2,1)S(1)}, u32[]{:S(2)}, u32[]{:S(2)}) collective-permute-start(bf16[256,256]{1,0:T(8,128)(2,1)S(1)} %get-tuple-element.90), channel_id=1, source_target_pairs={{0,2},{1,3},{2,0},{3,1},{4,6},{5,7},{6,4},{7,5},{8,10},{9,11},{10,... | collective-permute-start | bytes 393224 | tf_op jit(solution)/shard_map/ppermute | solution.py:109
  149.8 3.8 %collect.1.w = bf16[2,1664,1024]{2,1,0:T(8,128)(2,1)S(1)} custom-call(bf16[2,208,1024]{2,1,0:T(8,128)(2,1)S(1)} %pad.13.wa0, bf16[2,208,1024]{2,1,0:T(8,128)(2,1)S(1)} %collective-permute-done.18.wb0, bf16[2,208,1024]{2,1,0:T(8,128)(2,1)S(1)} %collective-permute-done.10.wc0, bf16[2,208,1024]{2,1,0:T(8,128)(2,1)S(1)} %collective-permute-done.19.wd0, ...), custom_call_target="tpu_custom_call" | custom-call | bytes 13631488 | tf_op jit(solution)/shard_map/collect/pallas_call | solution.py:411
  155.1 3.8 %output.1 = bf16[1600,256]{1,0:T(8,128)(2,1)} custom-call(s32[3]{0:T(128)S(1)} %pad_add_fusion.1.place, bf16[256,256]{1,0:T(8,128)(2,1)S(1)} %collective-permute-done.27.c20, bf16[256,256]{1,0:T(8,128)(2,1)S(1)} %collective-permute-done.28.c01, bf16[256,256]{1,0:T(8,128)(2,1)S(1)} %collective-permute-done.29.c31, ...), custom_call_target="tpu_custom_call" | custom-call | flops 1677721600 | bytes 6553600 | tf_op jit(solution)/shard_map/output/pallas_call | solution.py:450
  (89 shorter events, 25.5 us)
Async XLA Ops:
  2.4 17.1 %collective-permute-start = (bf16[200,1024]{1,0:T(8,128)(2,1)S(1)}, bf16[200,1024]{1,0:T(8,128)(2,1)}, u32[]{:S(2)}, u32[]{:S(2)}) collective-permute-start(bf16[200,1024]{1,0:T(8,128)(2,1)S(1)} %bitcast.29), channel_id=1, source_target_pairs={{0,8},{1,9},{2,10},{3,11},{4,12},{5,13},{6,14},{7,15},{8,0},{9,1},... | collective-permute-start | bytes 1228808 | tf_op jit(solution)/shard_map/ppermute | solution.py:109
  2.4 20.3 %collective-permute-start.1 = (bf16[200,1024]{1,0:T(8,128)(2,1)S(1)}, bf16[200,1024]{1,0:T(8,128)(2,1)}, u32[]{:S(2)}, u32[]{:S(2)}) collective-permute-start(bf16[200,1024]{1,0:T(8,128)(2,1)S(1)} %bitcast.30), channel_id=1, source_target_pairs={{0,16},{1,17},{2,18},{3,19},{4,20},{5,21},{6,22},{7,23},{8,24},{9,... | collective-permute-start | bytes 1228808 | tf_op jit(solution)/shard_map/ppermute | solution.py:109
  4.9 19.0 %collective-permute-start.2 = (bf16[3,200,256]{2,1,0:T(8,128)(2,1)}, bf16[3,200,256]{2,1,0:T(8,128)(2,1)}, u32[]{:S(2)}, u32[]{:S(2)}) collective-permute-start(bf16[3,200,256]{2,1,0:T(8,128)(2,1)} %get-tuple-element.53), channel_id=1, source_target_pairs={{0,6},{1,7},{2,4},{3,5},{4,2},{5,3},{6,0},{7,1},{8,14},{9,15},{10,... | collective-permute-start | bytes 921608 | tf_op jit(solution)/shard_map/ppermute | solution.py:109
  7.2 16.7 %collective-permute-start.3 = (bf16[3,200,256]{2,1,0:T(8,128)(2,1)}, bf16[3,200,256]{2,1,0:T(8,128)(2,1)}, u32[]{:S(2)}, u32[]{:S(2)}) collective-permute-start(bf16[3,200,256]{2,1,0:T(8,128)(2,1)} %get-tuple-element.54), channel_id=1, source_target_pairs={{0,4},{1,5},{2,6},{3,7},{4,0},{5,1},{6,2},{7,3},{8,12},{9,13},{10,... | collective-permute-start | bytes 921608 | tf_op jit(solution)/shard_map/ppermute | solution.py:109
  7.5 16.4 %collective-permute-start.4 = (bf16[3,200,256]{2,1,0:T(8,128)(2,1)}, bf16[3,200,256]{2,1,0:T(8,128)(2,1)}, u32[]{:S(2)}, u32[]{:S(2)}) collective-permute-start(bf16[3,200,256]{2,1,0:T(8,128)(2,1)} %get-tuple-element.55), channel_id=1, source_target_pairs={{0,2},{1,3},{2,0},{3,1},{4,6},{5,7},{6,4},{7,5},{8,10},{9,11},{10,... | collective-permute-start | bytes 921608 | tf_op jit(solution)/shard_map/ppermute | solution.py:109
  22.7 62.5 %collective-permute-start.7 = (bf16[4,256,896]{2,1,0:T(8,128)(2,1)}, bf16[4,256,896]{2,1,0:T(8,128)(2,1)}, u32[]{:S(2)}, u32[]{:S(2)}) collective-permute-start(bf16[4,256,896]{2,1,0:T(8,128)(2,1)} %norm.1.xa), channel_id=1, source_target_pairs={{0,4},{1,5},{2,6},{3,7},{4,0},{5,1},{6,2},{7,3},{8,12},{9,13},{10,... | collective-permute-start | bytes 5505032 | tf_op jit(solution)/shard_map/ppermute | solution.py:109
  23.9 32.2 %collective-permute-start.8 = (bf16[200,1024]{1,0:T(8,128)(2,1)}, bf16[200,1024]{1,0:T(8,128)(2,1)}, u32[]{:S(2)}, u32[]{:S(2)}) collective-permute-start(bf16[200,1024]{1,0:T(8,128)(2,1)} %collective-permute-done.1), channel_id=1, source_target_pairs={{0,8},{1,9},{2,10},{3,11},{4,12},{5,13},{6,14},{7,15},{8,0},{9,1},... | collective-permute-start | bytes 1228808 | tf_op jit(solution)/shard_map/ppermute | solution.py:109
  25.3 57.0 %collective-permute-start.5 = (bf16[3,800,256]{2,1,0:T(8,128)(2,1)S(1)}, bf16[3,800,256]{2,1,0:T(8,128)(2,1)S(1)}, u32[]{:S(2)}, u32[]{:S(2)}) collective-permute-start(bf16[3,800,256]{2,1,0:T(8,128)(2,1)S(1)} %pad_maximum_fusion.own), channel_id=1, source_target_pairs={{0,8},{1,9},{2,10},{3,11},{4,12},{5,13},{6,14},{7,15},{8,0},{9,1},... | collective-permute-start | bytes 3686408 | tf_op jit(solution)/shard_map/ppermute | solution.py:109
  26.8 58.3 %collective-permute-start.6 = (bf16[3,800,256]{2,1,0:T(8,128)(2,1)S(1)}, bf16[3,800,256]{2,1,0:T(8,128)(2,1)}, u32[]{:S(2)}, u32[]{:S(2)}) collective-permute-start(bf16[3,800,256]{2,1,0:T(8,128)(2,1)S(1)} %pad_maximum_fusion.own), channel_id=1, source_target_pairs={{0,16},{1,17},{2,18},{3,19},{4,20},{5,21},{6,22},{7,23},{8,24},{9,... | collective-permute-start | bytes 3686408 | tf_op jit(solution)/shard_map/ppermute | solution.py:109
  57.7 27.4 %collective-permute-start.10 = (bf16[2,208,1024]{2,1,0:T(8,128)(2,1)S(1)}, bf16[2,208,1024]{2,1,0:T(8,128)(2,1)S(1)}, u32[]{:S(2)}, u32[]{:S(2)}) collective-permute-start(bf16[2,208,1024]{2,1,0:T(8,128)(2,1)S(1)} %pad.13.wa0), channel_id=1, source_target_pairs={{0,4},{1,5},{2,6},{3,7},{4,0},{5,1},{6,2},{7,3},{8,12},{9,13},{10,... | collective-permute-start | bytes 2555912 | tf_op jit(solution)/shard_map/ppermute | solution.py:109
  58.1 27.0 %collective-permute-start.9 = (bf16[2,208,1024]{2,1,0:T(8,128)(2,1)S(1)}, bf16[2,208,1024]{2,1,0:T(8,128)(2,1)S(1)}, u32[]{:S(2)}, u32[]{:S(2)}) collective-permute-start(bf16[2,208,1024]{2,1,0:T(8,128)(2,1)S(1)} %pad.12), channel_id=1, source_target_pairs={{0,1},{1,0},{2,3},{3,2},{4,5},{5,4},{6,7},{7,6},{8,9},{9,8},{10,11... | collective-permute-start | bytes 2555912 | tf_op jit(solution)/shard_map/ppermute | solution.py:109
  85.2 8.9 %collective-permute-start.13 = (bf16[4,256,896]{2,1,0:T(8,128)(2,1)}, bf16[4,256,896]{2,1,0:T(8,128)(2,1)S(1)}, u32[]{:S(2)}, u32[]{:S(2)}) collective-permute-start(bf16[4,256,896]{2,1,0:T(8,128)(2,1)} %collective-permute-done.7.xc), channel_id=1, source_target_pairs={{0,2},{1,3},{2,0},{3,1},{4,6},{5,7},{6,4},{7,5},{8,10},{9,11},{10,... | collective-permute-start | bytes 5505032 | tf_op jit(solution)/shard_map/ppermute | solution.py:109
  88.8 28.4 %collective-permute-start.11 = (bf16[3,800,256]{2,1,0:T(8,128)(2,1)}, bf16[3,800,256]{2,1,0:T(8,128)(2,1)S(1)}, u32[]{:S(2)}, u32[]{:S(2)}) collective-permute-start(bf16[3,800,256]{2,1,0:T(8,128)(2,1)} %collective-permute-done.6.far), channel_id=1, source_target_pairs={{0,8},{1,9},{2,10},{3,11},{4,12},{5,13},{6,14},{7,15},{8,0},{9,1},... | collective-permute-start | bytes 3686408 | tf_op jit(solution)/shard_map/ppermute | solution.py:109
  88.8 30.9 %collective-permute-start.18 = (bf16[2,208,1024]{2,1,0:T(8,128)(2,1)S(1)}, bf16[2,208,1024]{2,1,0:T(8,128)(2,1)S(1)}, u32[]{:S(2)}, u32[]{:S(2)}) collective-permute-start(bf16[2,208,1024]{2,1,0:T(8,128)(2,1)S(1)} %pad.13.wa0), channel_id=1, source_target_pairs={{0,2},{1,3},{2,0},{3,1},{4,6},{5,7},{6,4},{7,5},{8,10},{9,11},{10,... | collective-permute-start | bytes 2555912 | tf_op jit(solution)/shard_map/ppermute | solution.py:109
  89.6 31.7 %collective-permute-start.16 = (bf16[2,208,1024]{2,1,0:T(8,128)(2,1)S(1)}, bf16[2,208,1024]{2,1,0:T(8,128)(2,1)S(1)}, u32[]{:S(2)}, u32[]{:S(2)}) collective-permute-start(bf16[2,208,1024]{2,1,0:T(8,128)(2,1)S(1)} %collective-permute-done.9.wa1), channel_id=1, source_target_pairs={{0,4},{1,5},{2,6},{3,7},{4,0},{5,1},{6,2},{7,3},{8,12},{9,13},{10,... | collective-permute-start | bytes 2555912 | tf_op jit(solution)/shard_map/ppermute | solution.py:109
  94.1 27.2 %collective-permute-start.17 = (bf16[2,208,1024]{2,1,0:T(8,128)(2,1)S(1)}, bf16[2,208,1024]{2,1,0:T(8,128)(2,1)S(1)}, u32[]{:S(2)}, u32[]{:S(2)}) collective-permute-start(bf16[2,208,1024]{2,1,0:T(8,128)(2,1)S(1)} %collective-permute-done.9.wa1), channel_id=1, source_target_pairs={{0,2},{1,3},{2,0},{3,1},{4,6},{5,7},{6,4},{7,5},{8,10},{9,11},{10,... | collective-permute-start | bytes 2555912 | tf_op jit(solution)/shard_map/ppermute | solution.py:109
  94.8 26.6 %collective-permute-start.19 = (bf16[2,208,1024]{2,1,0:T(8,128)(2,1)S(1)}, bf16[2,208,1024]{2,1,0:T(8,128)(2,1)S(1)}, u32[]{:S(2)}, u32[]{:S(2)}) collective-permute-start(bf16[2,208,1024]{2,1,0:T(8,128)(2,1)S(1)} %collective-permute-done.10.wc0), channel_id=1, source_target_pairs={{0,2},{1,3},{2,0},{3,1},{4,6},{5,7},{6,4},{7,5},{8,10},{9,11},{10,... | collective-permute-start | bytes 2555912 | tf_op jit(solution)/shard_map/ppermute | solution.py:109
  119.7 12.9 %collective-permute-start.14 = (bf16[2,512,256]{2,1,0:T(8,128)(2,1)S(1)}, bf16[2,512,256]{2,1,0:T(8,128)(2,1)S(1)}, u32[]{:S(2)}, u32[]{:S(2)}) collective-permute-start(bf16[2,512,256]{2,1,0:T(8,128)(2,1)S(1)} %get-tuple-element.74), channel_id=1, source_target_pairs={{0,8},{1,9},{2,10},{3,11},{4,12},{5,13},{6,14},{7,15},{8,0},{9,1},... | collective-permute-start | bytes 1572872 | tf_op jit(solution)/shard_map/ppermute | solution.py:109
  119.7 12.9 %collective-permute-start.15 = (bf16[2,512,256]{2,1,0:T(8,128)(2,1)S(1)}, bf16[2,512,256]{2,1,0:T(8,128)(2,1)S(1)}, u32[]{:S(2)}, u32[]{:S(2)}) collective-permute-start(bf16[2,512,256]{2,1,0:T(8,128)(2,1)S(1)} %get-tuple-element.75), channel_id=1, source_target_pairs={{0,2},{1,3},{2,0},{3,1},{4,6},{5,7},{6,4},{7,5},{8,16},{9,17},{10,... | collective-permute-start | bytes 1572872 | tf_op jit(solution)/shard_map/ppermute | solution.py:109
  141.0 12.6 %collective-permute-start.29 = (bf16[256,256]{1,0:T(8,128)(2,1)S(1)}, bf16[256,256]{1,0:T(8,128)(2,1)S(1)}, u32[]{:S(2)}, u32[]{:S(2)}) collective-permute-start(bf16[256,256]{1,0:T(8,128)(2,1)S(1)} %get-tuple-element.89), channel_id=1, source_target_pairs={{0,7},{1,6},{2,5},{3,4},{4,3},{5,2},{6,1},{7,0},{8,15},{9,14},{10,... | collective-permute-start | bytes 393224 | tf_op jit(solution)/shard_map/ppermute | solution.py:109
  143.7 9.9 %collective-permute-start.30 = (bf16[256,256]{1,0:T(8,128)(2,1)S(1)}, bf16[256,256]{1,0:T(8,128)(2,1)S(1)}, u32[]{:S(2)}, u32[]{:S(2)}) collective-permute-start(bf16[256,256]{1,0:T(8,128)(2,1)S(1)} %get-tuple-element.89), channel_id=1, source_target_pairs={{0,6},{1,7},{2,4},{3,5},{4,2},{5,3},{6,0},{7,1},{8,14},{9,15},{10,... | collective-permute-start | bytes 393224 | tf_op jit(solution)/shard_map/ppermute | solution.py:109
  143.8 11.3 %collective-permute-start.32 = (bf16[256,256]{1,0:T(8,128)(2,1)S(1)}, bf16[256,256]{1,0:T(8,128)(2,1)S(1)}, u32[]{:S(2)}, u32[]{:S(2)}) collective-permute-start(bf16[256,256]{1,0:T(8,128)(2,1)S(1)} %get-tuple-element.87), channel_id=1, source_target_pairs={{0,5},{1,4},{2,7},{3,6},{4,1},{5,0},{6,3},{7,2},{8,13},{9,12},{10,... | collective-permute-start | bytes 393224 | tf_op jit(solution)/shard_map/ppermute | solution.py:109
  145.9 9.2 %collective-permute-start.31 = (bf16[256,256]{1,0:T(8,128)(2,1)S(1)}, bf16[256,256]{1,0:T(8,128)(2,1)S(1)}, u32[]{:S(2)}, u32[]{:S(2)}) collective-permute-start(bf16[256,256]{1,0:T(8,128)(2,1)S(1)} %get-tuple-element.90), channel_id=1, source_target_pairs={{0,3},{1,2},{2,1},{3,0},{4,7},{5,6},{6,5},{7,4},{8,11},{9,10},{10,... | collective-permute-start | bytes 393224 | tf_op jit(solution)/shard_map/ppermute | solution.py:109
  147.0 8.1 %collective-permute-start.33 = (bf16[256,256]{1,0:T(8,128)(2,1)S(1)}, bf16[256,256]{1,0:T(8,128)(2,1)S(1)}, u32[]{:S(2)}, u32[]{:S(2)}) collective-permute-start(bf16[256,256]{1,0:T(8,128)(2,1)S(1)} %get-tuple-element.90), channel_id=1, source_target_pairs={{0,2},{1,3},{2,0},{3,1},{4,6},{5,7},{6,4},{7,5},{8,10},{9,11},{10,... | collective-permute-start | bytes 393224 | tf_op jit(solution)/shard_map/ppermute | solution.py:109
  (16 other events, 108.7 us)

commit v21 on v20

--- a/solution.py
+++ b/solution.py
@@ -331,16 +331,19 @@
                 keys_at = pl.ds(begin, width)
                 mask = jnp.tile(query_seg, (1, width // 128)) == seg[:, keys_at]
                 k_scale = scale_all[1:2, keys_at] * factor
-                for h in range(heads):
-                    cols = slice(h * HEAD_DIM, (h + 1) * HEAD_DIM)
-                    q_low = query[pl.ds(pl.multiple_of(b * count, count), count), cols] * q_scale
-                    scores = lax.dot_general(
-                        q_low.astype(jnp.bfloat16), k_all[keys_at, cols],
+                all_cols = [slice(h * HEAD_DIM, (h + 1) * HEAD_DIM) for h in range(heads)]
+                rows = pl.ds(pl.multiple_of(b * count, count), count)
+                scores = [
+                    lax.dot_general(
+                        (query[rows, cols] * q_scale).astype(jnp.bfloat16), k_all[keys_at, cols],
                         (((1,), (1,)), ((), ())), preferred_element_type=jnp.float32,
                     )
-                    scores = jnp.where(mask, scores * k_scale, floor_score)
-                    peak = jnp.max(scores, axis=1, keepdims=True)
-                    weights = jnp.exp2(scores - peak)
+                    for cols in all_cols
+                ]
+                for cols, s in zip(all_cols, scores):
+                    s = jnp.where(mask, s * k_scale, floor_score)
+                    peak = jnp.max(s, axis=1, keepdims=True)
+                    weights = jnp.exp2(s - peak)
                     total = jnp.sum(weights, axis=1, keepdims=True)
                     summed = jnp.dot(
                         weights.astype(jnp.bfloat16), v_all[keys_at, cols],
@@ -490,9 +493,9 @@
 
     by_kind = jnp.transpose(qkv_weight, (1, 0, 2))
     cut = [lax.dynamic_slice_in_dim(by_kind, (q ^ r) * width, width, 2) for r in range(SLAB)]
-    *cut, out_own = tied(*cut, jnp.transpose(out_weight))
     got = [cut[0]] + [in_slab(cut[r], r) for r in range(1, SLAB)]
     x0 = norm(tokens, norm_gain, slabs)
+    out_own = jnp.transpose(out_weight)
     own = rows_of_slab(q, got)
     out_near, out_far = even_pair(out_own), half_pair(out_own)
     gains = [lax.dynamic_slice_in_dim(g, q * width, width, 0)[None] for g in (q_gain, k_gain)]

time: 160 us -> 157 us (0.981)
  waiting for transfers between devices: 84.6 us -> 82.6 us
    ppermute x34, waiting for transfers between devices: 84.6 us -> 82.6 us  [permuted(): return lax.ppermute(x, ('seq', 'tp'), pairs)]
  transfers between devices with their start and end apart: 34 -> 34, of which waited for: 12 -> 13; matrix products, arithmetic and copies ran while one was open for 4% -> 6% of each run, Pallas kernels for 16% -> 16%
where the time goes in v21:
time: 157 us; the launch traced here: 156 us
  waiting for transfers between devices  82.6 us (53%)
  starting transfers between devices  35.4 us (23%)
  Pallas kernels  28.3 us (18%)
  local copies, waits for them, and re-layouts  5.71 us (4%)
  other arithmetic  3.73 us (2%)
    ppermute x34, waiting for transfers between devices, permuted(): return lax.ppermute(x, ('seq', 'tp'), pairs)  82.6 us
    ppermute x34, starting transfers between devices, permuted(): return lax.ppermute(x, ('seq', 'tp'), pairs)  35.4 us
    pallas_call x1, Pallas kernels, early(): pl.pallas_call(early_kernel, out_shape=(jax.ShapeDtypeStruct((SLAB, kinds...  9.54 us
    pallas_call x1, Pallas kernels, attend(): pl.pallas_call(functools.partial(attend_kernel, full_width), out_shape=(j...  5.08 us
    pallas_call x1, Pallas kernels, output(): pl.pallas_call(out_kernel, out_shape=jax.ShapeDtypeStruct((share, count),...  3.83 us
    pallas_call x1, Pallas kernels, collect(): pl.pallas_call(collect_kernel, out_shape=jax.ShapeDtypeStruct((2, 2 * SLA...  3.82 us
    pallas_call x1, Pallas kernels, norm(): pl.pallas_call(norm_kernel, out_shape=jax.ShapeDtypeStruct(shape, jnp.bfl...  3.58 us
  transfers between devices with their start and end apart: 34, of which 13 were waited for; matrix products, arithmetic and copies ran while one was open for 6% of the time, Pallas kernels for 16%

profile of v21, /device:TPU:9, one launch (start us, length us, event | category | flops | bytes accessed | tf_op | source)
XLA Modules:
  0.0 155.9 jit_solution(4707589184772770518)
XLA Ops:
  0.0 2.5 %collective-permute-start.1 = (bf16[200,1024]{1,0:T(8,128)(2,1)}, bf16[200,1024]{1,0:T(8,128)(2,1)}, u32[]{:S(2)}, u32[]{:S(2)}) collective-permute-start(bf16[200,1024]{1,0:T(8,128)(2,1)} %bitcast.43), channel_id=1, source_target_pairs={{0,16},{1,17},{2,18},{3,19},{4,20},{5,21},{6,22},{7,23},{8,24},{9,... | collective-permute-start | bytes 1228808 | tf_op jit(solution)/shard_map/ppermute | solution.py:109
  2.5 2.1 %dynamic-slice_bitcast_fusion.2 = (bf16[3,200,256]{2,1,0:T(8,128)(2,1)}, bf16[3,200,256]{2,1,0:T(8,128)(2,1)}, bf16[3,200,256]{2,1,0:T(8,128)(2,1)}) fusion(bf16[200,3,1024]{2,0,1:T(8,128)(2,1)} %param.10, s32[]{:T(128)S(6)} %select_n.149, s32[]{:T(128)S(6)} %select_n.151, s32[]{:T(128)S(6)} %select_n.153), kind=kLoop, calls=%fused_computation.16 | loop fusion | bytes 1843212 | tf_op jit(solution)/shard_map/dynamic_slice | solution.py:495
  4.6 2.3 %collective-permute-start.2 = (bf16[3,200,256]{2,1,0:T(8,128)(2,1)}, bf16[3,200,256]{2,1,0:T(8,128)(2,1)}, u32[]{:S(2)}, u32[]{:S(2)}) collective-permute-start(bf16[3,200,256]{2,1,0:T(8,128)(2,1)} %get-tuple-element.101), channel_id=1, source_target_pairs={{0,6},{1,7},{2,4},{3,5},{4,2},{5,3},{6,0},{7,1},{8,14},{9,15},{10,... | collective-permute-start | bytes 921608 | tf_op jit(solution)/shard_map/ppermute | solution.py:109
  11.2 3.6 %norm.1.xa = bf16[4,256,896]{2,1,0:T(8,128)(2,1)} custom-call(bf16[256,3200]{1,0:T(8,128)(2,1)} %tokens.1, f32[1,3200]{1,0:T(1,128)} %broadcast_in_dim.34.gain), custom_call_target="tpu_custom_call" | custom-call | tf_op jit(solution)/shard_map/norm/pallas_call | solution.py:168
  14.9 2.5 %collective-permute-done = bf16[200,1024]{1,0:T(8,128)(2,1)} collective-permute-done((bf16[200,1024]{1,0:T(8,128)(2,1)}, bf16[200,1024]{1,0:T(8,128)(2,1)}, u32[]{:S(2)}, u32[]{:S(2)}) %collective-permute-start) | collective-permute-done | bytes 409632 | tf_op jit(solution)/shard_map/ppermute | solution.py:109
  17.4 3.1 %collective-permute-done.1 = bf16[200,1024]{1,0:T(8,128)(2,1)} collective-permute-done((bf16[200,1024]{1,0:T(8,128)(2,1)}, bf16[200,1024]{1,0:T(8,128)(2,1)}, u32[]{:S(2)}, u32[]{:S(2)}) %collective-permute-start.1) | collective-permute-done | bytes 409632 | tf_op jit(solution)/shard_map/ppermute | solution.py:109
  21.9 1.6 %fusion.1 = (bf16[3,200,256]{2,1,0:T(8,128)(2,1)S(1)}, bf16[3,200,256]{2,1,0:T(8,128)(2,1)S(1)}, bf16[3,200,256]{2,1,0:T(8,128)(2,1)S(1)}, bf16[3,200,256]{2,1,0:T(8,128)(2,1)S(1)}) fusion(bf16[3,200,256]{2,1,0:T(8,128)(2,1)} %collective-permute-done.2, bf16[3,200,256]{2,1,0:T(8,128)(2,1)} %collective-permute-done.3, ...), kind=kLoop, calls=%fused_computation.10 | loop fusion | flops 1843200 | bytes 2457607 | tf_op jit(solution)/shard_map/jit(_where)/select_n | solution.py:478
  25.0 28.9 %collective-permute-done.8 = bf16[200,1024]{1,0:T(8,128)(2,1)} collective-permute-done((bf16[200,1024]{1,0:T(8,128)(2,1)}, bf16[200,1024]{1,0:T(8,128)(2,1)}, u32[]{:S(2)}, u32[]{:S(2)}) %collective-permute-start.8) | collective-permute-done | bytes 409632 | tf_op jit(solution)/shard_map/ppermute | solution.py:109
  57.1 23.1 %collective-permute-done.5.near = bf16[3,800,256]{2,1,0:T(8,128)(2,1)S(1)} collective-permute-done((bf16[3,800,256]{2,1,0:T(8,128)(2,1)S(1)}, bf16[3,800,256]{2,1,0:T(8,128)(2,1)S(1)}, u32[]{:S(2)}, u32[]{:S(2)}) %collective-permute-start.5) | collective-permute-done | bytes 1228832 | tf_op jit(solution)/shard_map/ppermute | solution.py:109
  80.2 2.8 %collective-permute-done.6.far = bf16[3,800,256]{2,1,0:T(8,128)(2,1)} collective-permute-done((bf16[3,800,256]{2,1,0:T(8,128)(2,1)S(1)}, bf16[3,800,256]{2,1,0:T(8,128)(2,1)}, u32[]{:S(2)}, u32[]{:S(2)}) %collective-permute-start.6) | collective-permute-done | bytes 1228832 | tf_op jit(solution)/shard_map/ppermute | solution.py:109
  83.0 3.6 %collective-permute-start.13 = (bf16[4,256,896]{2,1,0:T(8,128)(2,1)}, bf16[4,256,896]{2,1,0:T(8,128)(2,1)S(1)}, u32[]{:S(2)}, u32[]{:S(2)}) collective-permute-start(bf16[4,256,896]{2,1,0:T(8,128)(2,1)} %collective-permute-done.7.xc), channel_id=1, source_target_pairs={{0,2},{1,3},{2,0},{3,1},{4,6},{5,7},{6,4},{7,5},{8,10},{9,11},{10,... | collective-permute-start | bytes 5505032 | tf_op jit(solution)/shard_map/ppermute | solution.py:109
  87.7 4.2 %collective-permute-done.13.xd = bf16[4,256,896]{2,1,0:T(8,128)(2,1)S(1)} collective-permute-done((bf16[4,256,896]{2,1,0:T(8,128)(2,1)}, bf16[4,256,896]{2,1,0:T(8,128)(2,1)S(1)}, u32[]{:S(2)}, u32[]{:S(2)}) %collective-permute-start.13) | collective-permute-done | bytes 1835040 | tf_op jit(solution)/shard_map/ppermute | solution.py:109
  92.9 9.5 %early.1 = (f32[4,3,256,256]{3,2,1,0:T(8,128)S(1)}, bf16[4,256,896]{2,1,0:T(8,128)(2,1)S(1)}) custom-call(s32[3]{0:T(128)S(1)} %pad_add_fusion.1.place, bf16[4,256,896]{2,1,0:T(8,128)(2,1)S(1)} %copy-done, bf16[4,256,896]{2,1,0:T(8,128)(2,1)S(1)} %collective-permute-done.12.xb, bf16[4,256,896]{2,1,0:T(8,128)(2,1)} %collective-permute-done.7.xc, ...), custom_call_target="tpu_custom_call" | custom-call | flops 7549747200 | bytes 8601600 | tf_op jit(solution)/shard_map/early/pallas_call | solution.py:216
  102.5 12.5 %collective-permute-done.11.last = bf16[3,800,256]{2,1,0:T(8,128)(2,1)S(1)} collective-permute-done((bf16[3,800,256]{2,1,0:T(8,128)(2,1)}, bf16[3,800,256]{2,1,0:T(8,128)(2,1)S(1)}, u32[]{:S(2)}, u32[]{:S(2)}) %collective-permute-start.11) | collective-permute-done | bytes 1228832 | tf_op jit(solution)/shard_map/ppermute | solution.py:109
  115.0 2.5 %late.1 = (f32[1024,256]{1,0:T(8,128)S(1)}, bf16[1024,256]{1,0:T(8,128)(2,1)S(1)}, bf16[1024,256]{1,0:T(8,128)(2,1)S(1)}, f32[2,1024]{1,0:T(2,128)S(1)}, bf16[2,...) custom-call(s32[3]{0:T(128)S(1)} %pad_add_fusion.1.place, bf16[4,256,896]{2,1,0:T(8,128)(2,1)S(1)} %get-tuple-element.56.x_last, ...), custom_call_target="tpu_custom_call" | custom-call | flops 1258291200 | bytes 2867200 | tf_op jit(solution)/shard_map/late/pallas_call | solution.py:273
  117.5 1.6 %collective-permute-start.15 = (bf16[2,512,256]{2,1,0:T(8,128)(2,1)S(1)}, bf16[2,512,256]{2,1,0:T(8,128)(2,1)S(1)}, u32[]{:S(2)}, u32[]{:S(2)}) collective-permute-start(bf16[2,512,256]{2,1,0:T(8,128)(2,1)S(1)} %get-tuple-element.65), channel_id=1, source_target_pairs={{0,2},{1,3},{2,0},{3,1},{4,6},{5,7},{6,4},{7,5},{8,16},{9,17},{10,... | collective-permute-start | bytes 1572872 | tf_op jit(solution)/shard_map/ppermute | solution.py:109
  119.1 1.6 %collective-permute-start.20 = (f32[2,1024]{1,0:T(2,128)S(1)}, f32[2,1024]{1,0:T(2,128)S(1)}, u32[]{:S(2)}, u32[]{:S(2)}) collective-permute-start(f32[2,1024]{1,0:T(2,128)S(1)} %get-tuple-element.70), channel_id=1, source_target_pairs={{0,2},{1,3},{2,0},{3,1},{4,6},{5,7},{6,4},{7,5},{8,10},{9,11},{10,... | collective-permute-start | bytes 24584 | tf_op jit(solution)/shard_map/ppermute | solution.py:109
  128.7 1.7 %collective-permute-start.26 = (bf16[2,208,1024]{2,1,0:T(8,128)(2,1)S(1)}, bf16[2,208,1024]{2,1,0:T(8,128)(2,1)S(1)}, u32[]{:S(2)}, u32[]{:S(2)}) collective-permute-start(bf16[2,208,1024]{2,1,0:T(8,128)(2,1)S(1)} %collective-permute-done.16.wc1), channel_id=1, source_target_pairs={{0,2},{1,3},{2,0},{3,1},{4,6},{5,7},{6,4},{7,5},{8,10},{9,11},{10,... | collective-permute-start | bytes 2555912 | tf_op jit(solution)/shard_map/ppermute | solution.py:109
  130.4 5.1 %attend.1 = (bf16[256,256]{1,0:T(8,128)(2,1)S(1)}, bf16[256,256]{1,0:T(8,128)(2,1)S(1)}, bf16[256,256]{1,0:T(8,128)(2,1)S(1)}, bf16[256,256]{1,0:T(8,128)(2,1)S(1)}) custom-call(s32[3]{0:T(128)S(1)} %pad_add_fusion.1.place, s32[4,2]{1,0:T(4,128)S(1)} %pad_add_fusion.spans, f32[1024,256]{1,0:T(8,128)S(1)} %get-tuple-element.61.query, ...), custom_call_target="tpu_custom_call" | custom-call | flops 21474836480 | bytes 3145728 | tf_op jit(solution)/shard_map/attend/pallas_call | solution.py:379
  138.0 2.7 %collective-permute-start.29 = (bf16[256,256]{1,0:T(8,128)(2,1)S(1)}, bf16[256,256]{1,0:T(8,128)(2,1)S(1)}, u32[]{:S(2)}, u32[]{:S(2)}) collective-permute-start(bf16[256,256]{1,0:T(8,128)(2,1)S(1)} %get-tuple-element.79), channel_id=1, source_target_pairs={{0,7},{1,6},{2,5},{3,4},{4,3},{5,2},{6,1},{7,0},{8,15},{9,14},{10,... | collective-permute-start | bytes 393224 | tf_op jit(solution)/shard_map/ppermute | solution.py:109
  140.8 2.1 %collective-permute-start.32 = (bf16[256,256]{1,0:T(8,128)(2,1)S(1)}, bf16[256,256]{1,0:T(8,128)(2,1)S(1)}, u32[]{:S(2)}, u32[]{:S(2)}) collective-permute-start(bf16[256,256]{1,0:T(8,128)(2,1)S(1)} %get-tuple-element.77), channel_id=1, source_target_pairs={{0,5},{1,4},{2,7},{3,6},{4,1},{5,0},{6,3},{7,2},{8,13},{9,12},{10,... | collective-permute-start | bytes 393224 | tf_op jit(solution)/shard_map/ppermute | solution.py:109
  144.0 2.8 %collective-permute-start.33 = (bf16[256,256]{1,0:T(8,128)(2,1)S(1)}, bf16[256,256]{1,0:T(8,128)(2,1)S(1)}, u32[]{:S(2)}, u32[]{:S(2)}) collective-permute-start(bf16[256,256]{1,0:T(8,128)(2,1)S(1)} %get-tuple-element.80), channel_id=1, source_target_pairs={{0,2},{1,3},{2,0},{3,1},{4,6},{5,7},{6,4},{7,5},{8,10},{9,11},{10,... | collective-permute-start | bytes 393224 | tf_op jit(solution)/shard_map/ppermute | solution.py:109
  146.8 3.8 %collect.1.w = bf16[2,1664,1024]{2,1,0:T(8,128)(2,1)S(1)} custom-call(bf16[2,208,1024]{2,1,0:T(8,128)(2,1)S(1)} %pad.13.wa0, bf16[2,208,1024]{2,1,0:T(8,128)(2,1)S(1)} %collective-permute-done.18.wb0, bf16[2,208,1024]{2,1,0:T(8,128)(2,1)S(1)} %collective-permute-done.10.wc0, bf16[2,208,1024]{2,1,0:T(8,128)(2,1)S(1)} %collective-permute-done.19.wd0, ...), custom_call_target="tpu_custom_call" | custom-call | bytes 13631488 | tf_op jit(solution)/shard_map/collect/pallas_call | solution.py:414
  152.1 3.8 %output.1 = bf16[1600,256]{1,0:T(8,128)(2,1)} custom-call(s32[3]{0:T(128)S(1)} %pad_add_fusion.1.place, bf16[256,256]{1,0:T(8,128)(2,1)S(1)} %collective-permute-done.27.c20, bf16[256,256]{1,0:T(8,128)(2,1)S(1)} %collective-permute-done.28.c01, bf16[256,256]{1,0:T(8,128)(2,1)S(1)} %collective-permute-done.29.c31, ...), custom_call_target="tpu_custom_call" | custom-call | flops 1677721600 | bytes 6553600 | tf_op jit(solution)/shard_map/output/pallas_call | solution.py:453
  (87 shorter events, 25.7 us)
Async XLA Ops:
  0.0 17.4 %collective-permute-start = (bf16[200,1024]{1,0:T(8,128)(2,1)}, bf16[200,1024]{1,0:T(8,128)(2,1)}, u32[]{:S(2)}, u32[]{:S(2)}) collective-permute-start(bf16[200,1024]{1,0:T(8,128)(2,1)} %bitcast.42), channel_id=1, source_target_pairs={{0,8},{1,9},{2,10},{3,11},{4,12},{5,13},{6,14},{7,15},{8,0},{9,1},... | collective-permute-start | bytes 1228808 | tf_op jit(solution)/shard_map/ppermute | solution.py:109
  0.0 20.5 %collective-permute-start.1 = (bf16[200,1024]{1,0:T(8,128)(2,1)}, bf16[200,1024]{1,0:T(8,128)(2,1)}, u32[]{:S(2)}, u32[]{:S(2)}) collective-permute-start(bf16[200,1024]{1,0:T(8,128)(2,1)} %bitcast.43), channel_id=1, source_target_pairs={{0,16},{1,17},{2,18},{3,19},{4,20},{5,21},{6,22},{7,23},{8,24},{9,... | collective-permute-start | bytes 1228808 | tf_op jit(solution)/shard_map/ppermute | solution.py:109
  4.6 17.1 %collective-permute-start.2 = (bf16[3,200,256]{2,1,0:T(8,128)(2,1)}, bf16[3,200,256]{2,1,0:T(8,128)(2,1)}, u32[]{:S(2)}, u32[]{:S(2)}) collective-permute-start(bf16[3,200,256]{2,1,0:T(8,128)(2,1)} %get-tuple-element.101), channel_id=1, source_target_pairs={{0,6},{1,7},{2,4},{3,5},{4,2},{5,3},{6,0},{7,1},{8,14},{9,15},{10,... | collective-permute-start | bytes 921608 | tf_op jit(solution)/shard_map/ppermute | solution.py:109
  6.9 14.9 %collective-permute-start.3 = (bf16[3,200,256]{2,1,0:T(8,128)(2,1)}, bf16[3,200,256]{2,1,0:T(8,128)(2,1)}, u32[]{:S(2)}, u32[]{:S(2)}) collective-permute-start(bf16[3,200,256]{2,1,0:T(8,128)(2,1)} %get-tuple-element.102), channel_id=1, source_target_pairs={{0,4},{1,5},{2,6},{3,7},{4,0},{5,1},{6,2},{7,3},{8,12},{9,13},{10,... | collective-permute-start | bytes 921608 | tf_op jit(solution)/shard_map/ppermute | solution.py:109
  7.2 14.7 %collective-permute-start.4 = (bf16[3,200,256]{2,1,0:T(8,128)(2,1)}, bf16[3,200,256]{2,1,0:T(8,128)(2,1)}, u32[]{:S(2)}, u32[]{:S(2)}) collective-permute-start(bf16[3,200,256]{2,1,0:T(8,128)(2,1)} %get-tuple-element.103), channel_id=1, source_target_pairs={{0,2},{1,3},{2,0},{3,1},{4,6},{5,7},{6,4},{7,5},{8,10},{9,11},{10,... | collective-permute-start | bytes 921608 | tf_op jit(solution)/shard_map/ppermute | solution.py:109
  20.5 62.5 %collective-permute-start.7 = (bf16[4,256,896]{2,1,0:T(8,128)(2,1)}, bf16[4,256,896]{2,1,0:T(8,128)(2,1)}, u32[]{:S(2)}, u32[]{:S(2)}) collective-permute-start(bf16[4,256,896]{2,1,0:T(8,128)(2,1)} %norm.1.xa), channel_id=1, source_target_pairs={{0,4},{1,5},{2,6},{3,7},{4,0},{5,1},{6,2},{7,3},{8,12},{9,13},{10,... | collective-permute-start | bytes 5505032 | tf_op jit(solution)/shard_map/ppermute | solution.py:109
  21.7 32.2 %collective-permute-start.8 = (bf16[200,1024]{1,0:T(8,128)(2,1)}, bf16[200,1024]{1,0:T(8,128)(2,1)}, u32[]{:S(2)}, u32[]{:S(2)}) collective-permute-start(bf16[200,1024]{1,0:T(8,128)(2,1)} %collective-permute-done.1), channel_id=1, source_target_pairs={{0,8},{1,9},{2,10},{3,11},{4,12},{5,13},{6,14},{7,15},{8,0},{9,1},... | collective-permute-start | bytes 1228808 | tf_op jit(solution)/shard_map/ppermute | solution.py:109
  23.6 56.6 %collective-permute-start.5 = (bf16[3,800,256]{2,1,0:T(8,128)(2,1)S(1)}, bf16[3,800,256]{2,1,0:T(8,128)(2,1)S(1)}, u32[]{:S(2)}, u32[]{:S(2)}) collective-permute-start(bf16[3,800,256]{2,1,0:T(8,128)(2,1)S(1)} %pad_maximum_fusion.own), channel_id=1, source_target_pairs={{0,8},{1,9},{2,10},{3,11},{4,12},{5,13},{6,14},{7,15},{8,0},{9,1},... | collective-permute-start | bytes 3686408 | tf_op jit(solution)/shard_map/ppermute | solution.py:109
  25.0 58.0 %collective-permute-start.6 = (bf16[3,800,256]{2,1,0:T(8,128)(2,1)S(1)}, bf16[3,800,256]{2,1,0:T(8,128)(2,1)}, u32[]{:S(2)}, u32[]{:S(2)}) collective-permute-start(bf16[3,800,256]{2,1,0:T(8,128)(2,1)S(1)} %pad_maximum_fusion.own), channel_id=1, source_target_pairs={{0,16},{1,17},{2,18},{3,19},{4,20},{5,21},{6,22},{7,23},{8,24},{9,... | collective-permute-start | bytes 3686408 | tf_op jit(solution)/shard_map/ppermute | solution.py:109
  55.5 27.4 %collective-permute-start.10 = (bf16[2,208,1024]{2,1,0:T(8,128)(2,1)S(1)}, bf16[2,208,1024]{2,1,0:T(8,128)(2,1)S(1)}, u32[]{:S(2)}, u32[]{:S(2)}) collective-permute-start(bf16[2,208,1024]{2,1,0:T(8,128)(2,1)S(1)} %pad.13.wa0), channel_id=1, source_target_pairs={{0,4},{1,5},{2,6},{3,7},{4,0},{5,1},{6,2},{7,3},{8,12},{9,13},{10,... | collective-permute-start | bytes 2555912 | tf_op jit(solution)/shard_map/ppermute | solution.py:109
  55.8 27.2 %collective-permute-start.9 = (bf16[2,208,1024]{2,1,0:T(8,128)(2,1)S(1)}, bf16[2,208,1024]{2,1,0:T(8,128)(2,1)S(1)}, u32[]{:S(2)}, u32[]{:S(2)}) collective-permute-start(bf16[2,208,1024]{2,1,0:T(8,128)(2,1)S(1)} %pad.12), channel_id=1, source_target_pairs={{0,1},{1,0},{2,3},{3,2},{4,5},{5,4},{6,7},{7,6},{8,9},{9,8},{10,11... | collective-permute-start | bytes 2555912 | tf_op jit(solution)/shard_map/ppermute | solution.py:109
  83.0 8.9 %collective-permute-start.13 = (bf16[4,256,896]{2,1,0:T(8,128)(2,1)}, bf16[4,256,896]{2,1,0:T(8,128)(2,1)S(1)}, u32[]{:S(2)}, u32[]{:S(2)}) collective-permute-start(bf16[4,256,896]{2,1,0:T(8,128)(2,1)} %collective-permute-done.7.xc), channel_id=1, source_target_pairs={{0,2},{1,3},{2,0},{3,1},{4,6},{5,7},{6,4},{7,5},{8,10},{9,11},{10,... | collective-permute-start | bytes 5505032 | tf_op jit(solution)/shard_map/ppermute | solution.py:109
  86.6 28.4 %collective-permute-start.11 = (bf16[3,800,256]{2,1,0:T(8,128)(2,1)}, bf16[3,800,256]{2,1,0:T(8,128)(2,1)S(1)}, u32[]{:S(2)}, u32[]{:S(2)}) collective-permute-start(bf16[3,800,256]{2,1,0:T(8,128)(2,1)} %collective-permute-done.6.far), channel_id=1, source_target_pairs={{0,8},{1,9},{2,10},{3,11},{4,12},{5,13},{6,14},{7,15},{8,0},{9,1},... | collective-permute-start | bytes 3686408 | tf_op jit(solution)/shard_map/ppermute | solution.py:109
  86.6 30.9 %collective-permute-start.18 = (bf16[2,208,1024]{2,1,0:T(8,128)(2,1)S(1)}, bf16[2,208,1024]{2,1,0:T(8,128)(2,1)S(1)}, u32[]{:S(2)}, u32[]{:S(2)}) collective-permute-start(bf16[2,208,1024]{2,1,0:T(8,128)(2,1)S(1)} %pad.13.wa0), channel_id=1, source_target_pairs={{0,2},{1,3},{2,0},{3,1},{4,6},{5,7},{6,4},{7,5},{8,10},{9,11},{10,... | collective-permute-start | bytes 2555912 | tf_op jit(solution)/shard_map/ppermute | solution.py:109
  87.4 31.7 %collective-permute-start.16 = (bf16[2,208,1024]{2,1,0:T(8,128)(2,1)S(1)}, bf16[2,208,1024]{2,1,0:T(8,128)(2,1)S(1)}, u32[]{:S(2)}, u32[]{:S(2)}) collective-permute-start(bf16[2,208,1024]{2,1,0:T(8,128)(2,1)S(1)} %collective-permute-done.9.wa1), channel_id=1, source_target_pairs={{0,4},{1,5},{2,6},{3,7},{4,0},{5,1},{6,2},{7,3},{8,12},{9,13},{10,... | collective-permute-start | bytes 2555912 | tf_op jit(solution)/shard_map/ppermute | solution.py:109
  91.9 27.2 %collective-permute-start.17 = (bf16[2,208,1024]{2,1,0:T(8,128)(2,1)S(1)}, bf16[2,208,1024]{2,1,0:T(8,128)(2,1)S(1)}, u32[]{:S(2)}, u32[]{:S(2)}) collective-permute-start(bf16[2,208,1024]{2,1,0:T(8,128)(2,1)S(1)} %collective-permute-done.9.wa1), channel_id=1, source_target_pairs={{0,2},{1,3},{2,0},{3,1},{4,6},{5,7},{6,4},{7,5},{8,10},{9,11},{10,... | collective-permute-start | bytes 2555912 | tf_op jit(solution)/shard_map/ppermute | solution.py:109
  92.6 26.6 %collective-permute-start.19 = (bf16[2,208,1024]{2,1,0:T(8,128)(2,1)S(1)}, bf16[2,208,1024]{2,1,0:T(8,128)(2,1)S(1)}, u32[]{:S(2)}, u32[]{:S(2)}) collective-permute-start(bf16[2,208,1024]{2,1,0:T(8,128)(2,1)S(1)} %collective-permute-done.10.wc0), channel_id=1, source_target_pairs={{0,2},{1,3},{2,0},{3,1},{4,6},{5,7},{6,4},{7,5},{8,10},{9,11},{10,... | collective-permute-start | bytes 2555912 | tf_op jit(solution)/shard_map/ppermute | solution.py:109
  117.5 12.9 %collective-permute-start.14 = (bf16[2,512,256]{2,1,0:T(8,128)(2,1)S(1)}, bf16[2,512,256]{2,1,0:T(8,128)(2,1)S(1)}, u32[]{:S(2)}, u32[]{:S(2)}) collective-permute-start(bf16[2,512,256]{2,1,0:T(8,128)(2,1)S(1)} %get-tuple-element.64), channel_id=1, source_target_pairs={{0,8},{1,9},{2,10},{3,11},{4,12},{5,13},{6,14},{7,15},{8,0},{9,1},... | collective-permute-start | bytes 1572872 | tf_op jit(solution)/shard_map/ppermute | solution.py:109
  117.5 12.9 %collective-permute-start.15 = (bf16[2,512,256]{2,1,0:T(8,128)(2,1)S(1)}, bf16[2,512,256]{2,1,0:T(8,128)(2,1)S(1)}, u32[]{:S(2)}, u32[]{:S(2)}) collective-permute-start(bf16[2,512,256]{2,1,0:T(8,128)(2,1)S(1)} %get-tuple-element.65), channel_id=1, source_target_pairs={{0,2},{1,3},{2,0},{3,1},{4,6},{5,7},{6,4},{7,5},{8,16},{9,17},{10,... | collective-permute-start | bytes 1572872 | tf_op jit(solution)/shard_map/ppermute | solution.py:109
  138.0 12.6 %collective-permute-start.29 = (bf16[256,256]{1,0:T(8,128)(2,1)S(1)}, bf16[256,256]{1,0:T(8,128)(2,1)S(1)}, u32[]{:S(2)}, u32[]{:S(2)}) collective-permute-start(bf16[256,256]{1,0:T(8,128)(2,1)S(1)} %get-tuple-element.79), channel_id=1, source_target_pairs={{0,7},{1,6},{2,5},{3,4},{4,3},{5,2},{6,1},{7,0},{8,15},{9,14},{10,... | collective-permute-start | bytes 393224 | tf_op jit(solution)/shard_map/ppermute | solution.py:109
  140.7 9.9 %collective-permute-start.30 = (bf16[256,256]{1,0:T(8,128)(2,1)S(1)}, bf16[256,256]{1,0:T(8,128)(2,1)S(1)}, u32[]{:S(2)}, u32[]{:S(2)}) collective-permute-start(bf16[256,256]{1,0:T(8,128)(2,1)S(1)} %get-tuple-element.79), channel_id=1, source_target_pairs={{0,6},{1,7},{2,4},{3,5},{4,2},{5,3},{6,0},{7,1},{8,14},{9,15},{10,... | collective-permute-start | bytes 393224 | tf_op jit(solution)/shard_map/ppermute | solution.py:109
  140.8 11.3 %collective-permute-start.32 = (bf16[256,256]{1,0:T(8,128)(2,1)S(1)}, bf16[256,256]{1,0:T(8,128)(2,1)S(1)}, u32[]{:S(2)}, u32[]{:S(2)}) collective-permute-start(bf16[256,256]{1,0:T(8,128)(2,1)S(1)} %get-tuple-element.77), channel_id=1, source_target_pairs={{0,5},{1,4},{2,7},{3,6},{4,1},{5,0},{6,3},{7,2},{8,13},{9,12},{10,... | collective-permute-start | bytes 393224 | tf_op jit(solution)/shard_map/ppermute | solution.py:109
  142.9 9.2 %collective-permute-start.31 = (bf16[256,256]{1,0:T(8,128)(2,1)S(1)}, bf16[256,256]{1,0:T(8,128)(2,1)S(1)}, u32[]{:S(2)}, u32[]{:S(2)}) collective-permute-start(bf16[256,256]{1,0:T(8,128)(2,1)S(1)} %get-tuple-element.80), channel_id=1, source_target_pairs={{0,3},{1,2},{2,1},{3,0},{4,7},{5,6},{6,5},{7,4},{8,11},{9,10},{10,... | collective-permute-start | bytes 393224 | tf_op jit(solution)/shard_map/ppermute | solution.py:109
  144.0 8.1 %collective-permute-start.33 = (bf16[256,256]{1,0:T(8,128)(2,1)S(1)}, bf16[256,256]{1,0:T(8,128)(2,1)S(1)}, u32[]{:S(2)}, u32[]{:S(2)}) collective-permute-start(bf16[256,256]{1,0:T(8,128)(2,1)S(1)} %get-tuple-element.80), channel_id=1, source_target_pairs={{0,2},{1,3},{2,0},{3,1},{4,6},{5,7},{6,4},{7,5},{8,10},{9,11},{10,... | collective-permute-start | bytes 393224 | tf_op jit(solution)/shard_map/ppermute | solution.py:109
  (15 other events, 102.5 us)

commit v22 on v21

--- a/solution.py
+++ b/solution.py
@@ -340,14 +340,15 @@
                     )
                     for cols in all_cols
                 ]
-                for cols, s in zip(all_cols, scores):
+                parts = []
+                for s in scores:
                     s = jnp.where(mask, s * k_scale, floor_score)
-                    peak = jnp.max(s, axis=1, keepdims=True)
-                    weights = jnp.exp2(s - peak)
+                    weights = jnp.exp2(s - jnp.max(s, axis=1, keepdims=True))
                     total = jnp.sum(weights, axis=1, keepdims=True)
+                    parts.append((weights.astype(jnp.bfloat16), total))
+                for cols, (probs, total) in zip(all_cols, parts):
                     summed = jnp.dot(
-                        weights.astype(jnp.bfloat16), v_all[keys_at, cols],
-                        preferred_element_type=jnp.float32,
+                        probs, v_all[keys_at, cols], preferred_element_type=jnp.float32
                     )
                     o_all[r, cols, :] = jnp.transpose(summed / total).astype(jnp.bfloat16)
 
@@ -398,12 +399,12 @@
 
 
 def collect_kernel(wa0, wb0, wc0, wd0, wa1, wb1, wc1, wd1, out, sems):
-    rows = wa0.shape[1]
+    rows, depth = wa0.shape[1:]
     copies = []
     for i, ws in enumerate(((wa0, wb0, wc0, wd0), (wa1, wb1, wc1, wd1))):
         for r, w in enumerate(ws):
             for j in range(2):
-                dst = out.at[i, pl.ds((2 * r + j) * rows, rows), :]
+                dst = out.at[pl.ds((2 * r + j) * rows, rows), pl.ds(i * depth, depth)]
                 copies.append(pltpu.make_async_copy(w.at[j], dst, sems.at[i, r, j]))
     start(copies)
     wait(copies)
@@ -413,7 +414,7 @@
     rows, depth = pieces[0].shape[1:]
     return pl.pallas_call(
         collect_kernel,
-        out_shape=jax.ShapeDtypeStruct((2, 2 * SLAB * rows, depth), jnp.bfloat16),
+        out_shape=jax.ShapeDtypeStruct((2 * SLAB * rows, 2 * depth), jnp.bfloat16),
         in_specs=[HBM] * 8,
         out_specs=VMEM,
         scratch_shapes=[pltpu.SemaphoreType.DMA((2, SLAB, 2))],
@@ -432,12 +433,12 @@
     width = c00.shape[0]
     for i, blocks in enumerate(((c00, c10, c20, c30), (c01, c11, c21, c31))):
         for r, c in enumerate(blocks):
-            c_all[i, pl.ds(pl.multiple_of((q ^ r) * width, width), width), :] = c[...]
+            at = pl.multiple_of((i * SLAB + (q ^ r)) * width, width)
+            c_all[pl.ds(at, width), :] = c[...]
     column = as_column(scale[...])[:out.shape[0]]
     column = jnp.tile(column, (1, out.shape[1] // 128))
-    total[...] = jnp.dot(w[0], c_all[0], preferred_element_type=jnp.float32)
-    total[...] += jnp.dot(w[1], c_all[1], preferred_element_type=jnp.float32)
-    rows, kept = w.shape[1] // (2 * SLAB), out.shape[0] // (2 * SLAB)
+    total[...] = jnp.dot(w[...], c_all[...], preferred_element_type=jnp.float32)
+    rows, kept = w.shape[0] // (2 * SLAB), out.shape[0] // (2 * SLAB)
     for r in range(SLAB):
         for j in range(2):
             at = pl.multiple_of((((z % 2) ^ j) * SLAB + (q ^ r)) * kept, 8)
@@ -448,7 +449,7 @@
 
 def output(place, blocks, w, residual, scale):
     count = blocks[0].shape[1]
-    rows, depth = w.shape[1:]
+    rows, depth = w.shape
     share = residual.shape[0]
     return pl.pallas_call(
         out_kernel,
@@ -456,14 +457,14 @@
         in_specs=[SMEM] + [VMEM] * 11,
         out_specs=VMEM,
         scratch_shapes=[
-            pltpu.VMEM((2, depth, count), jnp.bfloat16),
+            pltpu.VMEM((depth, count), jnp.bfloat16),
             pltpu.VMEM((rows, count), jnp.float32),
             pltpu.VMEM((share, count), jnp.float32),
         ],
         compiler_params=pltpu.CompilerParams(vmem_limit_bytes=HELD_VMEM),
         cost_estimate=pl.CostEstimate(
-            flops=4 * share * count * depth,
-            bytes_accessed=4 * share * depth,
+            flops=2 * share * count * depth,
+            bytes_accessed=2 * share * depth,
             transcendentals=0,
         ),
         name="output",

time: 157 us -> 157 us (level)
  waiting for transfers between devices: 82.6 us -> 85.6 us
  Pallas kernels: 28.3 us -> 25.6 us
    ppermute x34, waiting for transfers between devices: 82.6 us -> 85.6 us  [permuted(): return lax.ppermute(x, ('seq', 'tp'), pairs)]
    pallas_call x1, Pallas kernels: 3.82 us -> 0.77 us  [collect(): pl.pallas_call(collect_kernel, out_shape=jax.ShapeDtypeStruct((2 * SLAB *...]
  transfers between devices with their start and end apart: 34 -> 34, of which waited for: 13 -> 13; matrix products, arithmetic and copies ran while one was open for 6% -> 6% of each run, Pallas kernels for 16% -> 14%
where the time goes in v22:
time: 157 us; the launch traced here: 156 us
  waiting for transfers between devices  85.6 us (55%)
  starting transfers between devices  35.4 us (23%)
  Pallas kernels  25.6 us (16%)
  local copies, waits for them, and re-layouts  5.71 us (4%)
  other arithmetic  3.73 us (2%)
    ppermute x34, waiting for transfers between devices, permuted(): return lax.ppermute(x, ('seq', 'tp'), pairs)  85.6 us
    ppermute x34, starting transfers between devices, permuted(): return lax.ppermute(x, ('seq', 'tp'), pairs)  35.4 us
    pallas_call x1, Pallas kernels, early(): pl.pallas_call(early_kernel, out_shape=(jax.ShapeDtypeStruct((SLAB, kinds...  9.54 us
    pallas_call x1, Pallas kernels, attend(): pl.pallas_call(functools.partial(attend_kernel, full_width), out_shape=(j...  5.36 us
    pallas_call x1, Pallas kernels, output(): pl.pallas_call(out_kernel, out_shape=jax.ShapeDtypeStruct((share, count),...  3.83 us
    pallas_call x1, Pallas kernels, norm(): pl.pallas_call(norm_kernel, out_shape=jax.ShapeDtypeStruct(shape, jnp.bfl...  3.58 us
  transfers between devices with their start and end apart: 34, of which 13 were waited for; matrix products, arithmetic and copies ran while one was open for 6% of the time, Pallas kernels for 14%

profile of v22, /device:TPU:9, one launch (start us, length us, event | category | flops | bytes accessed | tf_op | source)
XLA Modules:
  0.0 156.2 jit_solution(2293144983416916721)
XLA Ops:
  0.0 2.5 %collective-permute-start.1 = (bf16[200,1024]{1,0:T(8,128)(2,1)}, bf16[200,1024]{1,0:T(8,128)(2,1)}, u32[]{:S(2)}, u32[]{:S(2)}) collective-permute-start(bf16[200,1024]{1,0:T(8,128)(2,1)} %bitcast.43), channel_id=1, source_target_pairs={{0,16},{1,17},{2,18},{3,19},{4,20},{5,21},{6,22},{7,23},{8,24},{9,... | collective-permute-start | bytes 1228808 | tf_op jit(solution)/shard_map/ppermute | solution.py:109
  2.5 2.1 %dynamic-slice_bitcast_fusion.2 = (bf16[3,200,256]{2,1,0:T(8,128)(2,1)}, bf16[3,200,256]{2,1,0:T(8,128)(2,1)}, bf16[3,200,256]{2,1,0:T(8,128)(2,1)}) fusion(bf16[200,3,1024]{2,0,1:T(8,128)(2,1)} %param.10, s32[]{:T(128)S(6)} %select_n.149, s32[]{:T(128)S(6)} %select_n.151, s32[]{:T(128)S(6)} %select_n.153), kind=kLoop, calls=%fused_computation.16 | loop fusion | bytes 1843212 | tf_op jit(solution)/shard_map/dynamic_slice | solution.py:496
  4.6 2.3 %collective-permute-start.2 = (bf16[3,200,256]{2,1,0:T(8,128)(2,1)}, bf16[3,200,256]{2,1,0:T(8,128)(2,1)}, u32[]{:S(2)}, u32[]{:S(2)}) collective-permute-start(bf16[3,200,256]{2,1,0:T(8,128)(2,1)} %get-tuple-element.101), channel_id=1, source_target_pairs={{0,6},{1,7},{2,4},{3,5},{4,2},{5,3},{6,0},{7,1},{8,14},{9,15},{10,... | collective-permute-start | bytes 921608 | tf_op jit(solution)/shard_map/ppermute | solution.py:109
  11.2 3.6 %norm.1.xa = bf16[4,256,896]{2,1,0:T(8,128)(2,1)} custom-call(bf16[256,3200]{1,0:T(8,128)(2,1)} %tokens.1, f32[1,3200]{1,0:T(1,128)} %broadcast_in_dim.34.gain), custom_call_target="tpu_custom_call" | custom-call | tf_op jit(solution)/shard_map/norm/pallas_call | solution.py:168
  14.9 2.5 %collective-permute-done = bf16[200,1024]{1,0:T(8,128)(2,1)} collective-permute-done((bf16[200,1024]{1,0:T(8,128)(2,1)}, bf16[200,1024]{1,0:T(8,128)(2,1)}, u32[]{:S(2)}, u32[]{:S(2)}) %collective-permute-start) | collective-permute-done | bytes 409632 | tf_op jit(solution)/shard_map/ppermute | solution.py:109
  17.4 3.1 %collective-permute-done.1 = bf16[200,1024]{1,0:T(8,128)(2,1)} collective-permute-done((bf16[200,1024]{1,0:T(8,128)(2,1)}, bf16[200,1024]{1,0:T(8,128)(2,1)}, u32[]{:S(2)}, u32[]{:S(2)}) %collective-permute-start.1) | collective-permute-done | bytes 409632 | tf_op jit(solution)/shard_map/ppermute | solution.py:109
  21.9 1.6 %fusion.1 = (bf16[3,200,256]{2,1,0:T(8,128)(2,1)S(1)}, bf16[3,200,256]{2,1,0:T(8,128)(2,1)S(1)}, bf16[3,200,256]{2,1,0:T(8,128)(2,1)S(1)}, bf16[3,200,256]{2,1,0:T(8,128)(2,1)S(1)}) fusion(bf16[3,200,256]{2,1,0:T(8,128)(2,1)} %collective-permute-done.2, bf16[3,200,256]{2,1,0:T(8,128)(2,1)} %collective-permute-done.3, ...), kind=kLoop, calls=%fused_computation.10 | loop fusion | flops 1843200 | bytes 2457607 | tf_op jit(solution)/shard_map/jit(_where)/select_n | solution.py:479
  25.0 28.9 %collective-permute-done.8 = bf16[200,1024]{1,0:T(8,128)(2,1)} collective-permute-done((bf16[200,1024]{1,0:T(8,128)(2,1)}, bf16[200,1024]{1,0:T(8,128)(2,1)}, u32[]{:S(2)}, u32[]{:S(2)}) %collective-permute-start.8) | collective-permute-done | bytes 409632 | tf_op jit(solution)/shard_map/ppermute | solution.py:109
  57.1 23.1 %collective-permute-done.5.near = bf16[3,800,256]{2,1,0:T(8,128)(2,1)S(1)} collective-permute-done((bf16[3,800,256]{2,1,0:T(8,128)(2,1)S(1)}, bf16[3,800,256]{2,1,0:T(8,128)(2,1)S(1)}, u32[]{:S(2)}, u32[]{:S(2)}) %collective-permute-start.5) | collective-permute-done | bytes 1228832 | tf_op jit(solution)/shard_map/ppermute | solution.py:109
  80.2 2.8 %collective-permute-done.6.far = bf16[3,800,256]{2,1,0:T(8,128)(2,1)} collective-permute-done((bf16[3,800,256]{2,1,0:T(8,128)(2,1)S(1)}, bf16[3,800,256]{2,1,0:T(8,128)(2,1)}, u32[]{:S(2)}, u32[]{:S(2)}) %collective-permute-start.6) | collective-permute-done | bytes 1228832 | tf_op jit(solution)/shard_map/ppermute | solution.py:109
  83.0 3.6 %collective-permute-start.13 = (bf16[4,256,896]{2,1,0:T(8,128)(2,1)}, bf16[4,256,896]{2,1,0:T(8,128)(2,1)S(1)}, u32[]{:S(2)}, u32[]{:S(2)}) collective-permute-start(bf16[4,256,896]{2,1,0:T(8,128)(2,1)} %collective-permute-done.7.xc), channel_id=1, source_target_pairs={{0,2},{1,3},{2,0},{3,1},{4,6},{5,7},{6,4},{7,5},{8,10},{9,11},{10,... | collective-permute-start | bytes 5505032 | tf_op jit(solution)/shard_map/ppermute | solution.py:109
  87.7 4.2 %collective-permute-done.13.xd = bf16[4,256,896]{2,1,0:T(8,128)(2,1)S(1)} collective-permute-done((bf16[4,256,896]{2,1,0:T(8,128)(2,1)}, bf16[4,256,896]{2,1,0:T(8,128)(2,1)S(1)}, u32[]{:S(2)}, u32[]{:S(2)}) %collective-permute-start.13) | collective-permute-done | bytes 1835040 | tf_op jit(solution)/shard_map/ppermute | solution.py:109
  92.9 9.5 %early.1 = (f32[4,3,256,256]{3,2,1,0:T(8,128)S(1)}, bf16[4,256,896]{2,1,0:T(8,128)(2,1)S(1)}) custom-call(s32[3]{0:T(128)S(1)} %pad_add_fusion.1.place, bf16[4,256,896]{2,1,0:T(8,128)(2,1)S(1)} %copy-done, bf16[4,256,896]{2,1,0:T(8,128)(2,1)S(1)} %collective-permute-done.12.xb, bf16[4,256,896]{2,1,0:T(8,128)(2,1)} %collective-permute-done.7.xc, ...), custom_call_target="tpu_custom_call" | custom-call | flops 7549747200 | bytes 8601600 | tf_op jit(solution)/shard_map/early/pallas_call | solution.py:216
  102.5 12.5 %collective-permute-done.11.last = bf16[3,800,256]{2,1,0:T(8,128)(2,1)S(1)} collective-permute-done((bf16[3,800,256]{2,1,0:T(8,128)(2,1)}, bf16[3,800,256]{2,1,0:T(8,128)(2,1)S(1)}, u32[]{:S(2)}, u32[]{:S(2)}) %collective-permute-start.11) | collective-permute-done | bytes 1228832 | tf_op jit(solution)/shard_map/ppermute | solution.py:109
  115.0 2.5 %late.1 = (f32[1024,256]{1,0:T(8,128)S(1)}, bf16[1024,256]{1,0:T(8,128)(2,1)S(1)}, bf16[1024,256]{1,0:T(8,128)(2,1)S(1)}, f32[2,1024]{1,0:T(2,128)S(1)}, bf16[2,...) custom-call(s32[3]{0:T(128)S(1)} %pad_add_fusion.1.place, bf16[4,256,896]{2,1,0:T(8,128)(2,1)S(1)} %get-tuple-element.56.x_last, ...), custom_call_target="tpu_custom_call" | custom-call | flops 1258291200 | bytes 2867200 | tf_op jit(solution)/shard_map/late/pallas_call | solution.py:273
  117.5 1.6 %collective-permute-start.15 = (bf16[2,512,256]{2,1,0:T(8,128)(2,1)S(1)}, bf16[2,512,256]{2,1,0:T(8,128)(2,1)S(1)}, u32[]{:S(2)}, u32[]{:S(2)}) collective-permute-start(bf16[2,512,256]{2,1,0:T(8,128)(2,1)S(1)} %get-tuple-element.65), channel_id=1, source_target_pairs={{0,2},{1,3},{2,0},{3,1},{4,6},{5,7},{6,4},{7,5},{8,16},{9,17},{10,... | collective-permute-start | bytes 1572872 | tf_op jit(solution)/shard_map/ppermute | solution.py:109
  119.1 1.6 %collective-permute-start.20 = (f32[2,1024]{1,0:T(2,128)S(1)}, f32[2,1024]{1,0:T(2,128)S(1)}, u32[]{:S(2)}, u32[]{:S(2)}) collective-permute-start(f32[2,1024]{1,0:T(2,128)S(1)} %get-tuple-element.70), channel_id=1, source_target_pairs={{0,2},{1,3},{2,0},{3,1},{4,6},{5,7},{6,4},{7,5},{8,10},{9,11},{10,... | collective-permute-start | bytes 24584 | tf_op jit(solution)/shard_map/ppermute | solution.py:109
  128.7 1.7 %collective-permute-start.26 = (bf16[2,208,1024]{2,1,0:T(8,128)(2,1)S(1)}, bf16[2,208,1024]{2,1,0:T(8,128)(2,1)S(1)}, u32[]{:S(2)}, u32[]{:S(2)}) collective-permute-start(bf16[2,208,1024]{2,1,0:T(8,128)(2,1)S(1)} %collective-permute-done.16.wc1), channel_id=1, source_target_pairs={{0,2},{1,3},{2,0},{3,1},{4,6},{5,7},{6,4},{7,5},{8,10},{9,11},{10,... | collective-permute-start | bytes 2555912 | tf_op jit(solution)/shard_map/ppermute | solution.py:109
  130.4 5.4 %attend.1 = (bf16[256,256]{1,0:T(8,128)(2,1)S(1)}, bf16[256,256]{1,0:T(8,128)(2,1)S(1)}, bf16[256,256]{1,0:T(8,128)(2,1)S(1)}, bf16[256,256]{1,0:T(8,128)(2,1)S(1)}) custom-call(s32[3]{0:T(128)S(1)} %pad_add_fusion.1.place, s32[4,2]{1,0:T(4,128)S(1)} %pad_add_fusion.spans, f32[1024,256]{1,0:T(8,128)S(1)} %get-tuple-element.61.query, ...), custom_call_target="tpu_custom_call" | custom-call | flops 21474836480 | bytes 3145728 | tf_op jit(solution)/shard_map/attend/pallas_call | solution.py:380
  138.3 2.7 %collective-permute-start.29 = (bf16[256,256]{1,0:T(8,128)(2,1)S(1)}, bf16[256,256]{1,0:T(8,128)(2,1)S(1)}, u32[]{:S(2)}, u32[]{:S(2)}) collective-permute-start(bf16[256,256]{1,0:T(8,128)(2,1)S(1)} %get-tuple-element.79), channel_id=1, source_target_pairs={{0,7},{1,6},{2,5},{3,4},{4,3},{5,2},{6,1},{7,0},{8,15},{9,14},{10,... | collective-permute-start | bytes 393224 | tf_op jit(solution)/shard_map/ppermute | solution.py:109
  141.1 2.1 %collective-permute-start.32 = (bf16[256,256]{1,0:T(8,128)(2,1)S(1)}, bf16[256,256]{1,0:T(8,128)(2,1)S(1)}, u32[]{:S(2)}, u32[]{:S(2)}) collective-permute-start(bf16[256,256]{1,0:T(8,128)(2,1)S(1)} %get-tuple-element.77), channel_id=1, source_target_pairs={{0,5},{1,4},{2,7},{3,6},{4,1},{5,0},{6,3},{7,2},{8,13},{9,12},{10,... | collective-permute-start | bytes 393224 | tf_op jit(solution)/shard_map/ppermute | solution.py:109
  144.2 2.8 %collective-permute-start.33 = (bf16[256,256]{1,0:T(8,128)(2,1)S(1)}, bf16[256,256]{1,0:T(8,128)(2,1)S(1)}, u32[]{:S(2)}, u32[]{:S(2)}) collective-permute-start(bf16[256,256]{1,0:T(8,128)(2,1)S(1)} %get-tuple-element.80), channel_id=1, source_target_pairs={{0,2},{1,3},{2,0},{3,1},{4,6},{5,7},{6,4},{7,5},{8,10},{9,11},{10,... | collective-permute-start | bytes 393224 | tf_op jit(solution)/shard_map/ppermute | solution.py:109
  147.9 4.5 %collective-permute-done.31.c11 = bf16[256,256]{1,0:T(8,128)(2,1)S(1)} collective-permute-done((bf16[256,256]{1,0:T(8,128)(2,1)S(1)}, bf16[256,256]{1,0:T(8,128)(2,1)S(1)}, u32[]{:S(2)}, u32[]{:S(2)}) %collective-permute-start.31) | collective-permute-done | bytes 131104 | tf_op jit(solution)/shard_map/ppermute | solution.py:109
  152.4 3.8 %output.1 = bf16[1600,256]{1,0:T(8,128)(2,1)} custom-call(s32[3]{0:T(128)S(1)} %pad_add_fusion.1.place, bf16[256,256]{1,0:T(8,128)(2,1)S(1)} %collective-permute-done.27.c20, bf16[256,256]{1,0:T(8,128)(2,1)S(1)} %collective-permute-done.28.c01, bf16[256,256]{1,0:T(8,128)(2,1)S(1)} %collective-permute-done.29.c31, ...), custom_call_target="tpu_custom_call" | custom-call | flops 1677721600 | bytes 6553600 | tf_op jit(solution)/shard_map/output/pallas_call | solution.py:454
  (87 shorter events, 25.0 us)
Async XLA Ops:
  0.0 17.4 %collective-permute-start = (bf16[200,1024]{1,0:T(8,128)(2,1)}, bf16[200,1024]{1,0:T(8,128)(2,1)}, u32[]{:S(2)}, u32[]{:S(2)}) collective-permute-start(bf16[200,1024]{1,0:T(8,128)(2,1)} %bitcast.42), channel_id=1, source_target_pairs={{0,8},{1,9},{2,10},{3,11},{4,12},{5,13},{6,14},{7,15},{8,0},{9,1},... | collective-permute-start | bytes 1228808 | tf_op jit(solution)/shard_map/ppermute | solution.py:109
  0.0 20.5 %collective-permute-start.1 = (bf16[200,1024]{1,0:T(8,128)(2,1)}, bf16[200,1024]{1,0:T(8,128)(2,1)}, u32[]{:S(2)}, u32[]{:S(2)}) collective-permute-start(bf16[200,1024]{1,0:T(8,128)(2,1)} %bitcast.43), channel_id=1, source_target_pairs={{0,16},{1,17},{2,18},{3,19},{4,20},{5,21},{6,22},{7,23},{8,24},{9,... | collective-permute-start | bytes 1228808 | tf_op jit(solution)/shard_map/ppermute | solution.py:109
  4.6 17.1 %collective-permute-start.2 = (bf16[3,200,256]{2,1,0:T(8,128)(2,1)}, bf16[3,200,256]{2,1,0:T(8,128)(2,1)}, u32[]{:S(2)}, u32[]{:S(2)}) collective-permute-start(bf16[3,200,256]{2,1,0:T(8,128)(2,1)} %get-tuple-element.101), channel_id=1, source_target_pairs={{0,6},{1,7},{2,4},{3,5},{4,2},{5,3},{6,0},{7,1},{8,14},{9,15},{10,... | collective-permute-start | bytes 921608 | tf_op jit(solution)/shard_map/ppermute | solution.py:109
  6.9 14.9 %collective-permute-start.3 = (bf16[3,200,256]{2,1,0:T(8,128)(2,1)}, bf16[3,200,256]{2,1,0:T(8,128)(2,1)}, u32[]{:S(2)}, u32[]{:S(2)}) collective-permute-start(bf16[3,200,256]{2,1,0:T(8,128)(2,1)} %get-tuple-element.102), channel_id=1, source_target_pairs={{0,4},{1,5},{2,6},{3,7},{4,0},{5,1},{6,2},{7,3},{8,12},{9,13},{10,... | collective-permute-start | bytes 921608 | tf_op jit(solution)/shard_map/ppermute | solution.py:109
  7.2 14.7 %collective-permute-start.4 = (bf16[3,200,256]{2,1,0:T(8,128)(2,1)}, bf16[3,200,256]{2,1,0:T(8,128)(2,1)}, u32[]{:S(2)}, u32[]{:S(2)}) collective-permute-start(bf16[3,200,256]{2,1,0:T(8,128)(2,1)} %get-tuple-element.103), channel_id=1, source_target_pairs={{0,2},{1,3},{2,0},{3,1},{4,6},{5,7},{6,4},{7,5},{8,10},{9,11},{10,... | collective-permute-start | bytes 921608 | tf_op jit(solution)/shard_map/ppermute | solution.py:109
  20.5 62.5 %collective-permute-start.7 = (bf16[4,256,896]{2,1,0:T(8,128)(2,1)}, bf16[4,256,896]{2,1,0:T(8,128)(2,1)}, u32[]{:S(2)}, u32[]{:S(2)}) collective-permute-start(bf16[4,256,896]{2,1,0:T(8,128)(2,1)} %norm.1.xa), channel_id=1, source_target_pairs={{0,4},{1,5},{2,6},{3,7},{4,0},{5,1},{6,2},{7,3},{8,12},{9,13},{10,... | collective-permute-start | bytes 5505032 | tf_op jit(solution)/shard_map/ppermute | solution.py:109
  21.7 32.2 %collective-permute-start.8 = (bf16[200,1024]{1,0:T(8,128)(2,1)}, bf16[200,1024]{1,0:T(8,128)(2,1)}, u32[]{:S(2)}, u32[]{:S(2)}) collective-permute-start(bf16[200,1024]{1,0:T(8,128)(2,1)} %collective-permute-done.1), channel_id=1, source_target_pairs={{0,8},{1,9},{2,10},{3,11},{4,12},{5,13},{6,14},{7,15},{8,0},{9,1},... | collective-permute-start | bytes 1228808 | tf_op jit(solution)/shard_map/ppermute | solution.py:109
  23.6 56.6 %collective-permute-start.5 = (bf16[3,800,256]{2,1,0:T(8,128)(2,1)S(1)}, bf16[3,800,256]{2,1,0:T(8,128)(2,1)S(1)}, u32[]{:S(2)}, u32[]{:S(2)}) collective-permute-start(bf16[3,800,256]{2,1,0:T(8,128)(2,1)S(1)} %pad_maximum_fusion.own), channel_id=1, source_target_pairs={{0,8},{1,9},{2,10},{3,11},{4,12},{5,13},{6,14},{7,15},{8,0},{9,1},... | collective-permute-start | bytes 3686408 | tf_op jit(solution)/shard_map/ppermute | solution.py:109
  25.0 58.0 %collective-permute-start.6 = (bf16[3,800,256]{2,1,0:T(8,128)(2,1)S(1)}, bf16[3,800,256]{2,1,0:T(8,128)(2,1)}, u32[]{:S(2)}, u32[]{:S(2)}) collective-permute-start(bf16[3,800,256]{2,1,0:T(8,128)(2,1)S(1)} %pad_maximum_fusion.own), channel_id=1, source_target_pairs={{0,16},{1,17},{2,18},{3,19},{4,20},{5,21},{6,22},{7,23},{8,24},{9,... | collective-permute-start | bytes 3686408 | tf_op jit(solution)/shard_map/ppermute | solution.py:109
  55.5 27.4 %collective-permute-start.10 = (bf16[2,208,1024]{2,1,0:T(8,128)(2,1)S(1)}, bf16[2,208,1024]{2,1,0:T(8,128)(2,1)S(1)}, u32[]{:S(2)}, u32[]{:S(2)}) collective-permute-start(bf16[2,208,1024]{2,1,0:T(8,128)(2,1)S(1)} %pad.13.wa0), channel_id=1, source_target_pairs={{0,4},{1,5},{2,6},{3,7},{4,0},{5,1},{6,2},{7,3},{8,12},{9,13},{10,... | collective-permute-start | bytes 2555912 | tf_op jit(solution)/shard_map/ppermute | solution.py:109
  55.8 27.2 %collective-permute-start.9 = (bf16[2,208,1024]{2,1,0:T(8,128)(2,1)S(1)}, bf16[2,208,1024]{2,1,0:T(8,128)(2,1)S(1)}, u32[]{:S(2)}, u32[]{:S(2)}) collective-permute-start(bf16[2,208,1024]{2,1,0:T(8,128)(2,1)S(1)} %pad.12), channel_id=1, source_target_pairs={{0,1},{1,0},{2,3},{3,2},{4,5},{5,4},{6,7},{7,6},{8,9},{9,8},{10,11... | collective-permute-start | bytes 2555912 | tf_op jit(solution)/shard_map/ppermute | solution.py:109
  83.0 8.9 %collective-permute-start.13 = (bf16[4,256,896]{2,1,0:T(8,128)(2,1)}, bf16[4,256,896]{2,1,0:T(8,128)(2,1)S(1)}, u32[]{:S(2)}, u32[]{:S(2)}) collective-permute-start(bf16[4,256,896]{2,1,0:T(8,128)(2,1)} %collective-permute-done.7.xc), channel_id=1, source_target_pairs={{0,2},{1,3},{2,0},{3,1},{4,6},{5,7},{6,4},{7,5},{8,10},{9,11},{10,... | collective-permute-start | bytes 5505032 | tf_op jit(solution)/shard_map/ppermute | solution.py:109
  86.6 28.4 %collective-permute-start.11 = (bf16[3,800,256]{2,1,0:T(8,128)(2,1)}, bf16[3,800,256]{2,1,0:T(8,128)(2,1)S(1)}, u32[]{:S(2)}, u32[]{:S(2)}) collective-permute-start(bf16[3,800,256]{2,1,0:T(8,128)(2,1)} %collective-permute-done.6.far), channel_id=1, source_target_pairs={{0,8},{1,9},{2,10},{3,11},{4,12},{5,13},{6,14},{7,15},{8,0},{9,1},... | collective-permute-start | bytes 3686408 | tf_op jit(solution)/shard_map/ppermute | solution.py:109
  86.6 30.9 %collective-permute-start.18 = (bf16[2,208,1024]{2,1,0:T(8,128)(2,1)S(1)}, bf16[2,208,1024]{2,1,0:T(8,128)(2,1)S(1)}, u32[]{:S(2)}, u32[]{:S(2)}) collective-permute-start(bf16[2,208,1024]{2,1,0:T(8,128)(2,1)S(1)} %pad.13.wa0), channel_id=1, source_target_pairs={{0,2},{1,3},{2,0},{3,1},{4,6},{5,7},{6,4},{7,5},{8,10},{9,11},{10,... | collective-permute-start | bytes 2555912 | tf_op jit(solution)/shard_map/ppermute | solution.py:109
  87.4 31.7 %collective-permute-start.16 = (bf16[2,208,1024]{2,1,0:T(8,128)(2,1)S(1)}, bf16[2,208,1024]{2,1,0:T(8,128)(2,1)S(1)}, u32[]{:S(2)}, u32[]{:S(2)}) collective-permute-start(bf16[2,208,1024]{2,1,0:T(8,128)(2,1)S(1)} %collective-permute-done.9.wa1), channel_id=1, source_target_pairs={{0,4},{1,5},{2,6},{3,7},{4,0},{5,1},{6,2},{7,3},{8,12},{9,13},{10,... | collective-permute-start | bytes 2555912 | tf_op jit(solution)/shard_map/ppermute | solution.py:109
  91.9 27.2 %collective-permute-start.17 = (bf16[2,208,1024]{2,1,0:T(8,128)(2,1)S(1)}, bf16[2,208,1024]{2,1,0:T(8,128)(2,1)S(1)}, u32[]{:S(2)}, u32[]{:S(2)}) collective-permute-start(bf16[2,208,1024]{2,1,0:T(8,128)(2,1)S(1)} %collective-permute-done.9.wa1), channel_id=1, source_target_pairs={{0,2},{1,3},{2,0},{3,1},{4,6},{5,7},{6,4},{7,5},{8,10},{9,11},{10,... | collective-permute-start | bytes 2555912 | tf_op jit(solution)/shard_map/ppermute | solution.py:109
  92.6 26.6 %collective-permute-start.19 = (bf16[2,208,1024]{2,1,0:T(8,128)(2,1)S(1)}, bf16[2,208,1024]{2,1,0:T(8,128)(2,1)S(1)}, u32[]{:S(2)}, u32[]{:S(2)}) collective-permute-start(bf16[2,208,1024]{2,1,0:T(8,128)(2,1)S(1)} %collective-permute-done.10.wc0), channel_id=1, source_target_pairs={{0,2},{1,3},{2,0},{3,1},{4,6},{5,7},{6,4},{7,5},{8,10},{9,11},{10,... | collective-permute-start | bytes 2555912 | tf_op jit(solution)/shard_map/ppermute | solution.py:109
  117.5 12.9 %collective-permute-start.14 = (bf16[2,512,256]{2,1,0:T(8,128)(2,1)S(1)}, bf16[2,512,256]{2,1,0:T(8,128)(2,1)S(1)}, u32[]{:S(2)}, u32[]{:S(2)}) collective-permute-start(bf16[2,512,256]{2,1,0:T(8,128)(2,1)S(1)} %get-tuple-element.64), channel_id=1, source_target_pairs={{0,8},{1,9},{2,10},{3,11},{4,12},{5,13},{6,14},{7,15},{8,0},{9,1},... | collective-permute-start | bytes 1572872 | tf_op jit(solution)/shard_map/ppermute | solution.py:109
  117.5 12.9 %collective-permute-start.15 = (bf16[2,512,256]{2,1,0:T(8,128)(2,1)S(1)}, bf16[2,512,256]{2,1,0:T(8,128)(2,1)S(1)}, u32[]{:S(2)}, u32[]{:S(2)}) collective-permute-start(bf16[2,512,256]{2,1,0:T(8,128)(2,1)S(1)} %get-tuple-element.65), channel_id=1, source_target_pairs={{0,2},{1,3},{2,0},{3,1},{4,6},{5,7},{6,4},{7,5},{8,16},{9,17},{10,... | collective-permute-start | bytes 1572872 | tf_op jit(solution)/shard_map/ppermute | solution.py:109
  135.8 7.4 %collective-permute-start.27 = (bf16[256,256]{1,0:T(8,128)(2,1)S(1)}, bf16[256,256]{1,0:T(8,128)(2,1)S(1)}, u32[]{:S(2)}, u32[]{:S(2)}) collective-permute-start(bf16[256,256]{1,0:T(8,128)(2,1)S(1)} %get-tuple-element.77), channel_id=1, source_target_pairs={{0,4},{1,5},{2,6},{3,7},{4,0},{5,1},{6,2},{7,3},{8,12},{9,13},{10,... | collective-permute-start | bytes 393224 | tf_op jit(solution)/shard_map/ppermute | solution.py:109
  138.3 9.5 %collective-permute-start.29 = (bf16[256,256]{1,0:T(8,128)(2,1)S(1)}, bf16[256,256]{1,0:T(8,128)(2,1)S(1)}, u32[]{:S(2)}, u32[]{:S(2)}) collective-permute-start(bf16[256,256]{1,0:T(8,128)(2,1)S(1)} %get-tuple-element.79), channel_id=1, source_target_pairs={{0,7},{1,6},{2,5},{3,4},{4,3},{5,2},{6,1},{7,0},{8,15},{9,14},{10,... | collective-permute-start | bytes 393224 | tf_op jit(solution)/shard_map/ppermute | solution.py:109
  141.1 11.3 %collective-permute-start.32 = (bf16[256,256]{1,0:T(8,128)(2,1)S(1)}, bf16[256,256]{1,0:T(8,128)(2,1)S(1)}, u32[]{:S(2)}, u32[]{:S(2)}) collective-permute-start(bf16[256,256]{1,0:T(8,128)(2,1)S(1)} %get-tuple-element.77), channel_id=1, source_target_pairs={{0,5},{1,4},{2,7},{3,6},{4,1},{5,0},{6,3},{7,2},{8,13},{9,12},{10,... | collective-permute-start | bytes 393224 | tf_op jit(solution)/shard_map/ppermute | solution.py:109
  143.2 9.2 %collective-permute-start.31 = (bf16[256,256]{1,0:T(8,128)(2,1)S(1)}, bf16[256,256]{1,0:T(8,128)(2,1)S(1)}, u32[]{:S(2)}, u32[]{:S(2)}) collective-permute-start(bf16[256,256]{1,0:T(8,128)(2,1)S(1)} %get-tuple-element.80), channel_id=1, source_target_pairs={{0,3},{1,2},{2,1},{3,0},{4,7},{5,6},{6,5},{7,4},{8,11},{9,10},{10,... | collective-permute-start | bytes 393224 | tf_op jit(solution)/shard_map/ppermute | solution.py:109
  144.2 8.2 %collective-permute-start.33 = (bf16[256,256]{1,0:T(8,128)(2,1)S(1)}, bf16[256,256]{1,0:T(8,128)(2,1)S(1)}, u32[]{:S(2)}, u32[]{:S(2)}) collective-permute-start(bf16[256,256]{1,0:T(8,128)(2,1)S(1)} %get-tuple-element.80), channel_id=1, source_target_pairs={{0,2},{1,3},{2,0},{3,1},{4,6},{5,7},{6,4},{7,5},{8,10},{9,11},{10,... | collective-permute-start | bytes 393224 | tf_op jit(solution)/shard_map/ppermute | solution.py:109
  (15 other events, 102.3 us)

commit v23 on v22

--- a/solution.py
+++ b/solution.py
@@ -427,7 +427,7 @@
 
 
 def out_kernel(
-    place, c20, c01, c31, c30, c11, c21, c10, c00, w, residual, scale, out, c_all, total, placed,
+    place, c31, c21, c20, c01, c30, c11, c10, c00, w, residual, scale, out, c_all, total, placed,
 ):
     z, q = place[0], place[1]
     width = c00.shape[0]
@@ -542,7 +542,7 @@
     *blocks, got_xc = tied(*blocks, got_xc)
     pieces = (keep, keep_c, keep_x, keep_xc, got, got_c, got_x, got_xc)
     spread = []
-    for r, i in ((2, 0), (0, 1), (3, 1), (3, 0), (1, 1), (2, 1), (1, 0), (0, 0)):
+    for r, i in ((3, 1), (2, 1), (2, 0), (0, 1), (3, 0), (1, 1), (1, 0), (0, 0)):
         to = functools.partial(lambda r, i, z, q, y: (z, q ^ r, y ^ i), r, i)
         spread.append(permuted(blocks[r], to) if r or i else blocks[r])
 

time: 157 us -> 157 us (level)
  waiting for transfers between devices: 85.6 us -> 88.2 us
  starting transfers between devices: 35.4 us -> 33.1 us
    ppermute x34, waiting for transfers between devices: 85.6 us -> 88.2 us  [permuted(): return lax.ppermute(x, ('seq', 'tp'), pairs)]
    ppermute x34, starting transfers between devices: 35.4 us -> 33.1 us  [permuted(): return lax.ppermute(x, ('seq', 'tp'), pairs)]
  transfers between devices with their start and end apart: 34 -> 34, of which waited for: 13 -> 17; matrix products, arithmetic and copies ran while one was open for 6% -> 6% of each run, Pallas kernels for 14% -> 14%
where the time goes in v23:
time: 157 us
  waiting for transfers between devices  88.2 us (56%)
  starting transfers between devices  33.1 us (21%)
  Pallas kernels  25.7 us (16%)
  local copies, waits for them, and re-layouts  5.71 us (4%)
  other arithmetic  3.73 us (2%)
    ppermute x34, waiting for transfers between devices, permuted(): return lax.ppermute(x, ('seq', 'tp'), pairs)  88.2 us
    ppermute x34, starting transfers between devices, permuted(): return lax.ppermute(x, ('seq', 'tp'), pairs)  33.1 us
    pallas_call x1, Pallas kernels, early(): pl.pallas_call(early_kernel, out_shape=(jax.ShapeDtypeStruct((SLAB, kinds...  9.54 us
    pallas_call x1, Pallas kernels, attend(): pl.pallas_call(functools.partial(attend_kernel, full_width), out_shape=(j...  5.53 us
    pallas_call x1, Pallas kernels, output(): pl.pallas_call(out_kernel, out_shape=jax.ShapeDtypeStruct((share, count),...  3.83 us
    pallas_call x1, Pallas kernels, norm(): pl.pallas_call(norm_kernel, out_shape=jax.ShapeDtypeStruct(shape, jnp.bfl...  3.58 us
  transfers between devices with their start and end apart: 34, of which 17 were waited for; matrix products, arithmetic and copies ran while one was open for 6% of the time, Pallas kernels for 14%

profile of v23, /device:TPU:9, one launch (start us, length us, event | category | flops | bytes accessed | tf_op | source)
XLA Modules:
  0.0 156.6 jit_solution(4792502539980819526)
XLA Ops:
  0.0 2.5 %collective-permute-start.1 = (bf16[200,1024]{1,0:T(8,128)(2,1)}, bf16[200,1024]{1,0:T(8,128)(2,1)}, u32[]{:S(2)}, u32[]{:S(2)}) collective-permute-start(bf16[200,1024]{1,0:T(8,128)(2,1)} %bitcast.43), channel_id=1, source_target_pairs={{0,16},{1,17},{2,18},{3,19},{4,20},{5,21},{6,22},{7,23},{8,24},{9,... | collective-permute-start | bytes 1228808 | tf_op jit(solution)/shard_map/ppermute | solution.py:109
  2.5 2.1 %dynamic-slice_bitcast_fusion.2 = (bf16[3,200,256]{2,1,0:T(8,128)(2,1)}, bf16[3,200,256]{2,1,0:T(8,128)(2,1)}, bf16[3,200,256]{2,1,0:T(8,128)(2,1)}) fusion(bf16[200,3,1024]{2,0,1:T(8,128)(2,1)} %param.10, s32[]{:T(128)S(6)} %select_n.149, s32[]{:T(128)S(6)} %select_n.151, s32[]{:T(128)S(6)} %select_n.153), kind=kLoop, calls=%fused_computation.16 | loop fusion | bytes 1843212 | tf_op jit(solution)/shard_map/dynamic_slice | solution.py:496
  4.6 2.3 %collective-permute-start.2 = (bf16[3,200,256]{2,1,0:T(8,128)(2,1)}, bf16[3,200,256]{2,1,0:T(8,128)(2,1)}, u32[]{:S(2)}, u32[]{:S(2)}) collective-permute-start(bf16[3,200,256]{2,1,0:T(8,128)(2,1)} %get-tuple-element.101), channel_id=1, source_target_pairs={{0,6},{1,7},{2,4},{3,5},{4,2},{5,3},{6,0},{7,1},{8,14},{9,15},{10,... | collective-permute-start | bytes 921608 | tf_op jit(solution)/shard_map/ppermute | solution.py:109
  11.2 3.6 %norm.1.xa = bf16[4,256,896]{2,1,0:T(8,128)(2,1)} custom-call(bf16[256,3200]{1,0:T(8,128)(2,1)} %tokens.1, f32[1,3200]{1,0:T(1,128)} %broadcast_in_dim.34.gain), custom_call_target="tpu_custom_call" | custom-call | tf_op jit(solution)/shard_map/norm/pallas_call | solution.py:168
  14.9 2.5 %collective-permute-done = bf16[200,1024]{1,0:T(8,128)(2,1)} collective-permute-done((bf16[200,1024]{1,0:T(8,128)(2,1)}, bf16[200,1024]{1,0:T(8,128)(2,1)}, u32[]{:S(2)}, u32[]{:S(2)}) %collective-permute-start) | collective-permute-done | bytes 409632 | tf_op jit(solution)/shard_map/ppermute | solution.py:109
  17.4 3.1 %collective-permute-done.1 = bf16[200,1024]{1,0:T(8,128)(2,1)} collective-permute-done((bf16[200,1024]{1,0:T(8,128)(2,1)}, bf16[200,1024]{1,0:T(8,128)(2,1)}, u32[]{:S(2)}, u32[]{:S(2)}) %collective-permute-start.1) | collective-permute-done | bytes 409632 | tf_op jit(solution)/shard_map/ppermute | solution.py:109
  21.9 1.6 %fusion.1 = (bf16[3,200,256]{2,1,0:T(8,128)(2,1)S(1)}, bf16[3,200,256]{2,1,0:T(8,128)(2,1)S(1)}, bf16[3,200,256]{2,1,0:T(8,128)(2,1)S(1)}, bf16[3,200,256]{2,1,0:T(8,128)(2,1)S(1)}) fusion(bf16[3,200,256]{2,1,0:T(8,128)(2,1)} %collective-permute-done.2, bf16[3,200,256]{2,1,0:T(8,128)(2,1)} %collective-permute-done.3, ...), kind=kLoop, calls=%fused_computation.10 | loop fusion | flops 1843200 | bytes 2457607 | tf_op jit(solution)/shard_map/jit(_where)/select_n | solution.py:479
  25.0 28.9 %collective-permute-done.8 = bf16[200,1024]{1,0:T(8,128)(2,1)} collective-permute-done((bf16[200,1024]{1,0:T(8,128)(2,1)}, bf16[200,1024]{1,0:T(8,128)(2,1)}, u32[]{:S(2)}, u32[]{:S(2)}) %collective-permute-start.8) | collective-permute-done | bytes 409632 | tf_op jit(solution)/shard_map/ppermute | solution.py:109
  57.1 23.1 %collective-permute-done.5.near = bf16[3,800,256]{2,1,0:T(8,128)(2,1)S(1)} collective-permute-done((bf16[3,800,256]{2,1,0:T(8,128)(2,1)S(1)}, bf16[3,800,256]{2,1,0:T(8,128)(2,1)S(1)}, u32[]{:S(2)}, u32[]{:S(2)}) %collective-permute-start.5) | collective-permute-done | bytes 1228832 | tf_op jit(solution)/shard_map/ppermute | solution.py:109
  80.2 2.8 %collective-permute-done.6.far = bf16[3,800,256]{2,1,0:T(8,128)(2,1)} collective-permute-done((bf16[3,800,256]{2,1,0:T(8,128)(2,1)S(1)}, bf16[3,800,256]{2,1,0:T(8,128)(2,1)}, u32[]{:S(2)}, u32[]{:S(2)}) %collective-permute-start.6) | collective-permute-done | bytes 1228832 | tf_op jit(solution)/shard_map/ppermute | solution.py:109
  83.0 3.6 %collective-permute-start.13 = (bf16[4,256,896]{2,1,0:T(8,128)(2,1)}, bf16[4,256,896]{2,1,0:T(8,128)(2,1)S(1)}, u32[]{:S(2)}, u32[]{:S(2)}) collective-permute-start(bf16[4,256,896]{2,1,0:T(8,128)(2,1)} %collective-permute-done.7.xc), channel_id=1, source_target_pairs={{0,2},{1,3},{2,0},{3,1},{4,6},{5,7},{6,4},{7,5},{8,10},{9,11},{10,... | collective-permute-start | bytes 5505032 | tf_op jit(solution)/shard_map/ppermute | solution.py:109
  87.7 4.2 %collective-permute-done.13.xd = bf16[4,256,896]{2,1,0:T(8,128)(2,1)S(1)} collective-permute-done((bf16[4,256,896]{2,1,0:T(8,128)(2,1)}, bf16[4,256,896]{2,1,0:T(8,128)(2,1)S(1)}, u32[]{:S(2)}, u32[]{:S(2)}) %collective-permute-start.13) | collective-permute-done | bytes 1835040 | tf_op jit(solution)/shard_map/ppermute | solution.py:109
  92.9 9.5 %early.1 = (f32[4,3,256,256]{3,2,1,0:T(8,128)S(1)}, bf16[4,256,896]{2,1,0:T(8,128)(2,1)S(1)}) custom-call(s32[3]{0:T(128)S(1)} %pad_add_fusion.1.place, bf16[4,256,896]{2,1,0:T(8,128)(2,1)S(1)} %copy-done, bf16[4,256,896]{2,1,0:T(8,128)(2,1)S(1)} %collective-permute-done.12.xb, bf16[4,256,896]{2,1,0:T(8,128)(2,1)} %collective-permute-done.7.xc, ...), custom_call_target="tpu_custom_call" | custom-call | flops 7549747200 | bytes 8601600 | tf_op jit(solution)/shard_map/early/pallas_call | solution.py:216
  102.5 12.5 %collective-permute-done.11.last = bf16[3,800,256]{2,1,0:T(8,128)(2,1)S(1)} collective-permute-done((bf16[3,800,256]{2,1,0:T(8,128)(2,1)}, bf16[3,800,256]{2,1,0:T(8,128)(2,1)S(1)}, u32[]{:S(2)}, u32[]{:S(2)}) %collective-permute-start.11) | collective-permute-done | bytes 1228832 | tf_op jit(solution)/shard_map/ppermute | solution.py:109
  115.0 2.5 %late.1 = (f32[1024,256]{1,0:T(8,128)S(1)}, bf16[1024,256]{1,0:T(8,128)(2,1)S(1)}, bf16[1024,256]{1,0:T(8,128)(2,1)S(1)}, f32[2,1024]{1,0:T(2,128)S(1)}, bf16[2,...) custom-call(s32[3]{0:T(128)S(1)} %pad_add_fusion.1.place, bf16[4,256,896]{2,1,0:T(8,128)(2,1)S(1)} %get-tuple-element.56.x_last, ...), custom_call_target="tpu_custom_call" | custom-call | flops 1258291200 | bytes 2867200 | tf_op jit(solution)/shard_map/late/pallas_call | solution.py:273
  117.5 1.6 %collective-permute-start.15 = (bf16[2,512,256]{2,1,0:T(8,128)(2,1)S(1)}, bf16[2,512,256]{2,1,0:T(8,128)(2,1)S(1)}, u32[]{:S(2)}, u32[]{:S(2)}) collective-permute-start(bf16[2,512,256]{2,1,0:T(8,128)(2,1)S(1)} %get-tuple-element.65), channel_id=1, source_target_pairs={{0,2},{1,3},{2,0},{3,1},{4,6},{5,7},{6,4},{7,5},{8,16},{9,17},{10,... | collective-permute-start | bytes 1572872 | tf_op jit(solution)/shard_map/ppermute | solution.py:109
  119.1 1.6 %collective-permute-start.20 = (f32[2,1024]{1,0:T(2,128)S(1)}, f32[2,1024]{1,0:T(2,128)S(1)}, u32[]{:S(2)}, u32[]{:S(2)}) collective-permute-start(f32[2,1024]{1,0:T(2,128)S(1)} %get-tuple-element.70), channel_id=1, source_target_pairs={{0,2},{1,3},{2,0},{3,1},{4,6},{5,7},{6,4},{7,5},{8,10},{9,11},{10,... | collective-permute-start | bytes 24584 | tf_op jit(solution)/shard_map/ppermute | solution.py:109
  128.7 1.7 %collective-permute-start.26 = (bf16[2,208,1024]{2,1,0:T(8,128)(2,1)S(1)}, bf16[2,208,1024]{2,1,0:T(8,128)(2,1)S(1)}, u32[]{:S(2)}, u32[]{:S(2)}) collective-permute-start(bf16[2,208,1024]{2,1,0:T(8,128)(2,1)S(1)} %collective-permute-done.16.wc1), channel_id=1, source_target_pairs={{0,2},{1,3},{2,0},{3,1},{4,6},{5,7},{6,4},{7,5},{8,10},{9,11},{10,... | collective-permute-start | bytes 2555912 | tf_op jit(solution)/shard_map/ppermute | solution.py:109
  130.4 5.5 %attend.1 = (bf16[256,256]{1,0:T(8,128)(2,1)S(1)}, bf16[256,256]{1,0:T(8,128)(2,1)S(1)}, bf16[256,256]{1,0:T(8,128)(2,1)S(1)}, bf16[256,256]{1,0:T(8,128)(2,1)S(1)}) custom-call(s32[3]{0:T(128)S(1)} %pad_add_fusion.1.place, s32[4,2]{1,0:T(4,128)S(1)} %pad_add_fusion.spans, f32[1024,256]{1,0:T(8,128)S(1)} %get-tuple-element.61.query, ...), custom_call_target="tpu_custom_call" | custom-call | flops 21474836480 | bytes 3145728 | tf_op jit(solution)/shard_map/attend/pallas_call | solution.py:380
  136.0 4.1 %collective-permute-start.27 = (bf16[256,256]{1,0:T(8,128)(2,1)S(1)}, bf16[256,256]{1,0:T(8,128)(2,1)S(1)}, u32[]{:S(2)}, u32[]{:S(2)}) collective-permute-start(bf16[256,256]{1,0:T(8,128)(2,1)S(1)} %get-tuple-element.77), channel_id=1, source_target_pairs={{0,7},{1,6},{2,5},{3,4},{4,3},{5,2},{6,1},{7,0},{8,15},{9,14},{10,... | collective-permute-start | bytes 393224 | tf_op jit(solution)/shard_map/ppermute | solution.py:109
  144.3 1.6 %collective-permute-start.32 = (bf16[256,256]{1,0:T(8,128)(2,1)S(1)}, bf16[256,256]{1,0:T(8,128)(2,1)S(1)}, u32[]{:S(2)}, u32[]{:S(2)}) collective-permute-start(bf16[256,256]{1,0:T(8,128)(2,1)S(1)} %get-tuple-element.80), channel_id=1, source_target_pairs={{0,3},{1,2},{2,1},{3,0},{4,7},{5,6},{6,5},{7,4},{8,11},{9,10},{10,... | collective-permute-start | bytes 393224 | tf_op jit(solution)/shard_map/ppermute | solution.py:109
  148.5 1.6 collective-permute-done.29.c20
  151.0 1.8 %collective-permute-done.32.c11 = bf16[256,256]{1,0:T(8,128)(2,1)S(1)} collective-permute-done((bf16[256,256]{1,0:T(8,128)(2,1)S(1)}, bf16[256,256]{1,0:T(8,128)(2,1)S(1)}, u32[]{:S(2)}, u32[]{:S(2)}) %collective-permute-start.32) | collective-permute-done | bytes 131104 | tf_op jit(solution)/shard_map/ppermute | solution.py:109
  152.8 3.8 %output.1 = bf16[1600,256]{1,0:T(8,128)(2,1)} custom-call(s32[3]{0:T(128)S(1)} %pad_add_fusion.1.place, bf16[256,256]{1,0:T(8,128)(2,1)S(1)} %collective-permute-done.27.c31, bf16[256,256]{1,0:T(8,128)(2,1)S(1)} %collective-permute-done.28.c21, bf16[256,256]{1,0:T(8,128)(2,1)S(1)} %collective-permute-done.29.c20, ...), custom_call_target="tpu_custom_call" | custom-call | flops 1677721600 | bytes 6553600 | tf_op jit(solution)/shard_map/output/pallas_call | solution.py:454
  (87 shorter events, 28.3 us)
Async XLA Ops:
  0.0 17.4 %collective-permute-start = (bf16[200,1024]{1,0:T(8,128)(2,1)}, bf16[200,1024]{1,0:T(8,128)(2,1)}, u32[]{:S(2)}, u32[]{:S(2)}) collective-permute-start(bf16[200,1024]{1,0:T(8,128)(2,1)} %bitcast.42), channel_id=1, source_target_pairs={{0,8},{1,9},{2,10},{3,11},{4,12},{5,13},{6,14},{7,15},{8,0},{9,1},... | collective-permute-start | bytes 1228808 | tf_op jit(solution)/shard_map/ppermute | solution.py:109
  0.0 20.5 %collective-permute-start.1 = (bf16[200,1024]{1,0:T(8,128)(2,1)}, bf16[200,1024]{1,0:T(8,128)(2,1)}, u32[]{:S(2)}, u32[]{:S(2)}) collective-permute-start(bf16[200,1024]{1,0:T(8,128)(2,1)} %bitcast.43), channel_id=1, source_target_pairs={{0,16},{1,17},{2,18},{3,19},{4,20},{5,21},{6,22},{7,23},{8,24},{9,... | collective-permute-start | bytes 1228808 | tf_op jit(solution)/shard_map/ppermute | solution.py:109
  4.6 17.1 %collective-permute-start.2 = (bf16[3,200,256]{2,1,0:T(8,128)(2,1)}, bf16[3,200,256]{2,1,0:T(8,128)(2,1)}, u32[]{:S(2)}, u32[]{:S(2)}) collective-permute-start(bf16[3,200,256]{2,1,0:T(8,128)(2,1)} %get-tuple-element.101), channel_id=1, source_target_pairs={{0,6},{1,7},{2,4},{3,5},{4,2},{5,3},{6,0},{7,1},{8,14},{9,15},{10,... | collective-permute-start | bytes 921608 | tf_op jit(solution)/shard_map/ppermute | solution.py:109
  6.9 14.9 %collective-permute-start.3 = (bf16[3,200,256]{2,1,0:T(8,128)(2,1)}, bf16[3,200,256]{2,1,0:T(8,128)(2,1)}, u32[]{:S(2)}, u32[]{:S(2)}) collective-permute-start(bf16[3,200,256]{2,1,0:T(8,128)(2,1)} %get-tuple-element.102), channel_id=1, source_target_pairs={{0,4},{1,5},{2,6},{3,7},{4,0},{5,1},{6,2},{7,3},{8,12},{9,13},{10,... | collective-permute-start | bytes 921608 | tf_op jit(solution)/shard_map/ppermute | solution.py:109
  7.2 14.7 %collective-permute-start.4 = (bf16[3,200,256]{2,1,0:T(8,128)(2,1)}, bf16[3,200,256]{2,1,0:T(8,128)(2,1)}, u32[]{:S(2)}, u32[]{:S(2)}) collective-permute-start(bf16[3,200,256]{2,1,0:T(8,128)(2,1)} %get-tuple-element.103), channel_id=1, source_target_pairs={{0,2},{1,3},{2,0},{3,1},{4,6},{5,7},{6,4},{7,5},{8,10},{9,11},{10,... | collective-permute-start | bytes 921608 | tf_op jit(solution)/shard_map/ppermute | solution.py:109
  20.5 62.5 %collective-permute-start.7 = (bf16[4,256,896]{2,1,0:T(8,128)(2,1)}, bf16[4,256,896]{2,1,0:T(8,128)(2,1)}, u32[]{:S(2)}, u32[]{:S(2)}) collective-permute-start(bf16[4,256,896]{2,1,0:T(8,128)(2,1)} %norm.1.xa), channel_id=1, source_target_pairs={{0,4},{1,5},{2,6},{3,7},{4,0},{5,1},{6,2},{7,3},{8,12},{9,13},{10,... | collective-permute-start | bytes 5505032 | tf_op jit(solution)/shard_map/ppermute | solution.py:109
  21.7 32.2 %collective-permute-start.8 = (bf16[200,1024]{1,0:T(8,128)(2,1)}, bf16[200,1024]{1,0:T(8,128)(2,1)}, u32[]{:S(2)}, u32[]{:S(2)}) collective-permute-start(bf16[200,1024]{1,0:T(8,128)(2,1)} %collective-permute-done.1), channel_id=1, source_target_pairs={{0,8},{1,9},{2,10},{3,11},{4,12},{5,13},{6,14},{7,15},{8,0},{9,1},... | collective-permute-start | bytes 1228808 | tf_op jit(solution)/shard_map/ppermute | solution.py:109
  23.6 56.6 %collective-permute-start.5 = (bf16[3,800,256]{2,1,0:T(8,128)(2,1)S(1)}, bf16[3,800,256]{2,1,0:T(8,128)(2,1)S(1)}, u32[]{:S(2)}, u32[]{:S(2)}) collective-permute-start(bf16[3,800,256]{2,1,0:T(8,128)(2,1)S(1)} %pad_maximum_fusion.own), channel_id=1, source_target_pairs={{0,8},{1,9},{2,10},{3,11},{4,12},{5,13},{6,14},{7,15},{8,0},{9,1},... | collective-permute-start | bytes 3686408 | tf_op jit(solution)/shard_map/ppermute | solution.py:109
  25.0 58.0 %collective-permute-start.6 = (bf16[3,800,256]{2,1,0:T(8,128)(2,1)S(1)}, bf16[3,800,256]{2,1,0:T(8,128)(2,1)}, u32[]{:S(2)}, u32[]{:S(2)}) collective-permute-start(bf16[3,800,256]{2,1,0:T(8,128)(2,1)S(1)} %pad_maximum_fusion.own), channel_id=1, source_target_pairs={{0,16},{1,17},{2,18},{3,19},{4,20},{5,21},{6,22},{7,23},{8,24},{9,... | collective-permute-start | bytes 3686408 | tf_op jit(solution)/shard_map/ppermute | solution.py:109
  55.5 27.4 %collective-permute-start.10 = (bf16[2,208,1024]{2,1,0:T(8,128)(2,1)S(1)}, bf16[2,208,1024]{2,1,0:T(8,128)(2,1)S(1)}, u32[]{:S(2)}, u32[]{:S(2)}) collective-permute-start(bf16[2,208,1024]{2,1,0:T(8,128)(2,1)S(1)} %pad.13.wa0), channel_id=1, source_target_pairs={{0,4},{1,5},{2,6},{3,7},{4,0},{5,1},{6,2},{7,3},{8,12},{9,13},{10,... | collective-permute-start | bytes 2555912 | tf_op jit(solution)/shard_map/ppermute | solution.py:109
  55.8 27.2 %collective-permute-start.9 = (bf16[2,208,1024]{2,1,0:T(8,128)(2,1)S(1)}, bf16[2,208,1024]{2,1,0:T(8,128)(2,1)S(1)}, u32[]{:S(2)}, u32[]{:S(2)}) collective-permute-start(bf16[2,208,1024]{2,1,0:T(8,128)(2,1)S(1)} %pad.12), channel_id=1, source_target_pairs={{0,1},{1,0},{2,3},{3,2},{4,5},{5,4},{6,7},{7,6},{8,9},{9,8},{10,11... | collective-permute-start | bytes 2555912 | tf_op jit(solution)/shard_map/ppermute | solution.py:109
  83.0 8.9 %collective-permute-start.13 = (bf16[4,256,896]{2,1,0:T(8,128)(2,1)}, bf16[4,256,896]{2,1,0:T(8,128)(2,1)S(1)}, u32[]{:S(2)}, u32[]{:S(2)}) collective-permute-start(bf16[4,256,896]{2,1,0:T(8,128)(2,1)} %collective-permute-done.7.xc), channel_id=1, source_target_pairs={{0,2},{1,3},{2,0},{3,1},{4,6},{5,7},{6,4},{7,5},{8,10},{9,11},{10,... | collective-permute-start | bytes 5505032 | tf_op jit(solution)/shard_map/ppermute | solution.py:109
  86.6 28.4 %collective-permute-start.11 = (bf16[3,800,256]{2,1,0:T(8,128)(2,1)}, bf16[3,800,256]{2,1,0:T(8,128)(2,1)S(1)}, u32[]{:S(2)}, u32[]{:S(2)}) collective-permute-start(bf16[3,800,256]{2,1,0:T(8,128)(2,1)} %collective-permute-done.6.far), channel_id=1, source_target_pairs={{0,8},{1,9},{2,10},{3,11},{4,12},{5,13},{6,14},{7,15},{8,0},{9,1},... | collective-permute-start | bytes 3686408 | tf_op jit(solution)/shard_map/ppermute | solution.py:109
  86.6 30.9 %collective-permute-start.18 = (bf16[2,208,1024]{2,1,0:T(8,128)(2,1)S(1)}, bf16[2,208,1024]{2,1,0:T(8,128)(2,1)S(1)}, u32[]{:S(2)}, u32[]{:S(2)}) collective-permute-start(bf16[2,208,1024]{2,1,0:T(8,128)(2,1)S(1)} %pad.13.wa0), channel_id=1, source_target_pairs={{0,2},{1,3},{2,0},{3,1},{4,6},{5,7},{6,4},{7,5},{8,10},{9,11},{10,... | collective-permute-start | bytes 2555912 | tf_op jit(solution)/shard_map/ppermute | solution.py:109
  87.4 31.7 %collective-permute-start.16 = (bf16[2,208,1024]{2,1,0:T(8,128)(2,1)S(1)}, bf16[2,208,1024]{2,1,0:T(8,128)(2,1)S(1)}, u32[]{:S(2)}, u32[]{:S(2)}) collective-permute-start(bf16[2,208,1024]{2,1,0:T(8,128)(2,1)S(1)} %collective-permute-done.9.wa1), channel_id=1, source_target_pairs={{0,4},{1,5},{2,6},{3,7},{4,0},{5,1},{6,2},{7,3},{8,12},{9,13},{10,... | collective-permute-start | bytes 2555912 | tf_op jit(solution)/shard_map/ppermute | solution.py:109
  91.9 27.2 %collective-permute-start.17 = (bf16[2,208,1024]{2,1,0:T(8,128)(2,1)S(1)}, bf16[2,208,1024]{2,1,0:T(8,128)(2,1)S(1)}, u32[]{:S(2)}, u32[]{:S(2)}) collective-permute-start(bf16[2,208,1024]{2,1,0:T(8,128)(2,1)S(1)} %collective-permute-done.9.wa1), channel_id=1, source_target_pairs={{0,2},{1,3},{2,0},{3,1},{4,6},{5,7},{6,4},{7,5},{8,10},{9,11},{10,... | collective-permute-start | bytes 2555912 | tf_op jit(solution)/shard_map/ppermute | solution.py:109
  92.6 26.6 %collective-permute-start.19 = (bf16[2,208,1024]{2,1,0:T(8,128)(2,1)S(1)}, bf16[2,208,1024]{2,1,0:T(8,128)(2,1)S(1)}, u32[]{:S(2)}, u32[]{:S(2)}) collective-permute-start(bf16[2,208,1024]{2,1,0:T(8,128)(2,1)S(1)} %collective-permute-done.10.wc0), channel_id=1, source_target_pairs={{0,2},{1,3},{2,0},{3,1},{4,6},{5,7},{6,4},{7,5},{8,10},{9,11},{10,... | collective-permute-start | bytes 2555912 | tf_op jit(solution)/shard_map/ppermute | solution.py:109
  117.5 12.9 %collective-permute-start.14 = (bf16[2,512,256]{2,1,0:T(8,128)(2,1)S(1)}, bf16[2,512,256]{2,1,0:T(8,128)(2,1)S(1)}, u32[]{:S(2)}, u32[]{:S(2)}) collective-permute-start(bf16[2,512,256]{2,1,0:T(8,128)(2,1)S(1)} %get-tuple-element.64), channel_id=1, source_target_pairs={{0,8},{1,9},{2,10},{3,11},{4,12},{5,13},{6,14},{7,15},{8,0},{9,1},... | collective-permute-start | bytes 1572872 | tf_op jit(solution)/shard_map/ppermute | solution.py:109
  117.5 12.9 %collective-permute-start.15 = (bf16[2,512,256]{2,1,0:T(8,128)(2,1)S(1)}, bf16[2,512,256]{2,1,0:T(8,128)(2,1)S(1)}, u32[]{:S(2)}, u32[]{:S(2)}) collective-permute-start(bf16[2,512,256]{2,1,0:T(8,128)(2,1)S(1)} %get-tuple-element.65), channel_id=1, source_target_pairs={{0,2},{1,3},{2,0},{3,1},{4,6},{5,7},{6,4},{7,5},{8,16},{9,17},{10,... | collective-permute-start | bytes 1572872 | tf_op jit(solution)/shard_map/ppermute | solution.py:109
  136.0 8.3 %collective-permute-start.27 = (bf16[256,256]{1,0:T(8,128)(2,1)S(1)}, bf16[256,256]{1,0:T(8,128)(2,1)S(1)}, u32[]{:S(2)}, u32[]{:S(2)}) collective-permute-start(bf16[256,256]{1,0:T(8,128)(2,1)S(1)} %get-tuple-element.77), channel_id=1, source_target_pairs={{0,7},{1,6},{2,5},{3,4},{4,3},{5,2},{6,1},{7,0},{8,15},{9,14},{10,... | collective-permute-start | bytes 393224 | tf_op jit(solution)/shard_map/ppermute | solution.py:109
  140.3 9.7 %collective-permute-start.29 = (bf16[256,256]{1,0:T(8,128)(2,1)S(1)}, bf16[256,256]{1,0:T(8,128)(2,1)S(1)}, u32[]{:S(2)}, u32[]{:S(2)}) collective-permute-start(bf16[256,256]{1,0:T(8,128)(2,1)S(1)} %get-tuple-element.78), channel_id=1, source_target_pairs={{0,4},{1,5},{2,6},{3,7},{4,0},{5,1},{6,2},{7,3},{8,12},{9,13},{10,... | collective-permute-start | bytes 393224 | tf_op jit(solution)/shard_map/ppermute | solution.py:109
  141.5 9.5 %collective-permute-start.31 = (bf16[256,256]{1,0:T(8,128)(2,1)S(1)}, bf16[256,256]{1,0:T(8,128)(2,1)S(1)}, u32[]{:S(2)}, u32[]{:S(2)}) collective-permute-start(bf16[256,256]{1,0:T(8,128)(2,1)S(1)} %get-tuple-element.77), channel_id=1, source_target_pairs={{0,6},{1,7},{2,4},{3,5},{4,2},{5,3},{6,0},{7,1},{8,14},{9,15},{10,... | collective-permute-start | bytes 393224 | tf_op jit(solution)/shard_map/ppermute | solution.py:109
  142.2 7.8 %collective-permute-start.30 = (bf16[256,256]{1,0:T(8,128)(2,1)S(1)}, bf16[256,256]{1,0:T(8,128)(2,1)S(1)}, u32[]{:S(2)}, u32[]{:S(2)}) collective-permute-start(bf16[256,256]{1,0:T(8,128)(2,1)S(1)} %get-tuple-element.79.c00), channel_id=1, source_target_pairs={{0,1},{1,0},{2,3},{3,2},{4,5},{5,4},{6,7},{7,6},{8,9},{9,8},{10,11... | collective-permute-start | bytes 393224 | tf_op jit(solution)/shard_map/ppermute | solution.py:109
  144.3 8.5 %collective-permute-start.32 = (bf16[256,256]{1,0:T(8,128)(2,1)S(1)}, bf16[256,256]{1,0:T(8,128)(2,1)S(1)}, u32[]{:S(2)}, u32[]{:S(2)}) collective-permute-start(bf16[256,256]{1,0:T(8,128)(2,1)S(1)} %get-tuple-element.80), channel_id=1, source_target_pairs={{0,3},{1,2},{2,1},{3,0},{4,7},{5,6},{6,5},{7,4},{8,11},{9,10},{10,... | collective-permute-start | bytes 393224 | tf_op jit(solution)/shard_map/ppermute | solution.py:109
  (15 other events, 101.1 us)

commit v24 on v22

--- a/solution.py
+++ b/solution.py
@@ -427,7 +427,7 @@
 
 
 def out_kernel(
-    place, c20, c01, c31, c30, c11, c21, c10, c00, w, residual, scale, out, c_all, total, placed,
+    place, c20, c01, c31, c30, c11, c21, c10, c00, w, residual, scale, out, c_all, placed,
 ):
     z, q = place[0], place[1]
     width = c00.shape[0]
@@ -437,13 +437,15 @@
             c_all[pl.ds(at, width), :] = c[...]
     column = as_column(scale[...])[:out.shape[0]]
     column = jnp.tile(column, (1, out.shape[1] // 128))
-    total[...] = jnp.dot(w[...], c_all[...], preferred_element_type=jnp.float32)
     rows, kept = w.shape[0] // (2 * SLAB), out.shape[0] // (2 * SLAB)
     for r in range(SLAB):
         for j in range(2):
             at = pl.multiple_of((((z % 2) ^ j) * SLAB + (q ^ r)) * kept, 8)
             begin = (2 * r + j) * rows
-            placed[pl.ds(at, kept), :] = total[begin:begin + kept, :]
+            total = jnp.dot(
+                w[begin:begin + rows, :], c_all[...], preferred_element_type=jnp.float32
+            )
+            placed[pl.ds(at, kept), :] = total[:kept]
     out[...] = (residual[...].astype(jnp.float32) + column * placed[...]).astype(jnp.bfloat16)
 
 
@@ -458,7 +460,6 @@
         out_specs=VMEM,
         scratch_shapes=[
             pltpu.VMEM((depth, count), jnp.bfloat16),
-            pltpu.VMEM((rows, count), jnp.float32),
             pltpu.VMEM((share, count), jnp.float32),
         ],
         compiler_params=pltpu.CompilerParams(vmem_limit_bytes=HELD_VMEM),

time: 157 us -> 157 us (level)
  no operation moved by 1% of the time
where the time goes in v24:
time: 157 us; the launch traced here: 156 us
  waiting for transfers between devices  85.6 us (55%)
  starting transfers between devices  35.4 us (23%)
  Pallas kernels  24.9 us (16%)
  local copies, waits for them, and re-layouts  5.71 us (4%)
  other arithmetic  3.73 us (2%)
    ppermute x34, waiting for transfers between devices, permuted(): return lax.ppermute(x, ('seq', 'tp'), pairs)  85.6 us
    ppermute x34, starting transfers between devices, permuted(): return lax.ppermute(x, ('seq', 'tp'), pairs)  35.4 us
    pallas_call x1, Pallas kernels, early(): pl.pallas_call(early_kernel, out_shape=(jax.ShapeDtypeStruct((SLAB, kinds...  9.54 us
    pallas_call x1, Pallas kernels, attend(): pl.pallas_call(functools.partial(attend_kernel, full_width), out_shape=(j...  4.65 us
    pallas_call x1, Pallas kernels, output(): pl.pallas_call(out_kernel, out_shape=jax.ShapeDtypeStruct((share, count),...  3.85 us
    pallas_call x1, Pallas kernels, norm(): pl.pallas_call(norm_kernel, out_shape=jax.ShapeDtypeStruct(shape, jnp.bfl...  3.58 us
  transfers between devices with their start and end apart: 34, of which 13 were waited for; matrix products, arithmetic and copies ran while one was open for 6% of the time, Pallas kernels for 14%

profile of v24, /device:TPU:9, one launch (start us, length us, event | category | flops | bytes accessed | tf_op | source)
XLA Modules:
  0.0 155.5 jit_solution(16110047903606635747)
XLA Ops:
  0.0 2.5 %collective-permute-start.1 = (bf16[200,1024]{1,0:T(8,128)(2,1)}, bf16[200,1024]{1,0:T(8,128)(2,1)}, u32[]{:S(2)}, u32[]{:S(2)}) collective-permute-start(bf16[200,1024]{1,0:T(8,128)(2,1)} %bitcast.43), channel_id=1, source_target_pairs={{0,16},{1,17},{2,18},{3,19},{4,20},{5,21},{6,22},{7,23},{8,24},{9,... | collective-permute-start | bytes 1228808 | tf_op jit(solution)/shard_map/ppermute | solution.py:109
  2.5 2.1 %dynamic-slice_bitcast_fusion.2 = (bf16[3,200,256]{2,1,0:T(8,128)(2,1)}, bf16[3,200,256]{2,1,0:T(8,128)(2,1)}, bf16[3,200,256]{2,1,0:T(8,128)(2,1)}) fusion(bf16[200,3,1024]{2,0,1:T(8,128)(2,1)} %param.10, s32[]{:T(128)S(6)} %select_n.149, s32[]{:T(128)S(6)} %select_n.151, s32[]{:T(128)S(6)} %select_n.153), kind=kLoop, calls=%fused_computation.16 | loop fusion | bytes 1843212 | tf_op jit(solution)/shard_map/dynamic_slice | solution.py:497
  4.6 2.3 %collective-permute-start.2 = (bf16[3,200,256]{2,1,0:T(8,128)(2,1)}, bf16[3,200,256]{2,1,0:T(8,128)(2,1)}, u32[]{:S(2)}, u32[]{:S(2)}) collective-permute-start(bf16[3,200,256]{2,1,0:T(8,128)(2,1)} %get-tuple-element.101), channel_id=1, source_target_pairs={{0,6},{1,7},{2,4},{3,5},{4,2},{5,3},{6,0},{7,1},{8,14},{9,15},{10,... | collective-permute-start | bytes 921608 | tf_op jit(solution)/shard_map/ppermute | solution.py:109
  11.2 3.6 %norm.1.xa = bf16[4,256,896]{2,1,0:T(8,128)(2,1)} custom-call(bf16[256,3200]{1,0:T(8,128)(2,1)} %tokens.1, f32[1,3200]{1,0:T(1,128)} %broadcast_in_dim.34.gain), custom_call_target="tpu_custom_call" | custom-call | tf_op jit(solution)/shard_map/norm/pallas_call | solution.py:168
  14.9 2.5 %collective-permute-done = bf16[200,1024]{1,0:T(8,128)(2,1)} collective-permute-done((bf16[200,1024]{1,0:T(8,128)(2,1)}, bf16[200,1024]{1,0:T(8,128)(2,1)}, u32[]{:S(2)}, u32[]{:S(2)}) %collective-permute-start) | collective-permute-done | bytes 409632 | tf_op jit(solution)/shard_map/ppermute | solution.py:109
  17.4 3.1 %collective-permute-done.1 = bf16[200,1024]{1,0:T(8,128)(2,1)} collective-permute-done((bf16[200,1024]{1,0:T(8,128)(2,1)}, bf16[200,1024]{1,0:T(8,128)(2,1)}, u32[]{:S(2)}, u32[]{:S(2)}) %collective-permute-start.1) | collective-permute-done | bytes 409632 | tf_op jit(solution)/shard_map/ppermute | solution.py:109
  21.9 1.6 %fusion.1 = (bf16[3,200,256]{2,1,0:T(8,128)(2,1)S(1)}, bf16[3,200,256]{2,1,0:T(8,128)(2,1)S(1)}, bf16[3,200,256]{2,1,0:T(8,128)(2,1)S(1)}, bf16[3,200,256]{2,1,0:T(8,128)(2,1)S(1)}) fusion(bf16[3,200,256]{2,1,0:T(8,128)(2,1)} %collective-permute-done.2, bf16[3,200,256]{2,1,0:T(8,128)(2,1)} %collective-permute-done.3, ...), kind=kLoop, calls=%fused_computation.10 | loop fusion | flops 1843200 | bytes 2457607 | tf_op jit(solution)/shard_map/jit(_where)/select_n | solution.py:480
  25.0 28.9 %collective-permute-done.8 = bf16[200,1024]{1,0:T(8,128)(2,1)} collective-permute-done((bf16[200,1024]{1,0:T(8,128)(2,1)}, bf16[200,1024]{1,0:T(8,128)(2,1)}, u32[]{:S(2)}, u32[]{:S(2)}) %collective-permute-start.8) | collective-permute-done | bytes 409632 | tf_op jit(solution)/shard_map/ppermute | solution.py:109
  57.1 23.1 %collective-permute-done.5.near = bf16[3,800,256]{2,1,0:T(8,128)(2,1)S(1)} collective-permute-done((bf16[3,800,256]{2,1,0:T(8,128)(2,1)S(1)}, bf16[3,800,256]{2,1,0:T(8,128)(2,1)S(1)}, u32[]{:S(2)}, u32[]{:S(2)}) %collective-permute-start.5) | collective-permute-done | bytes 1228832 | tf_op jit(solution)/shard_map/ppermute | solution.py:109
  80.2 2.8 %collective-permute-done.6.far = bf16[3,800,256]{2,1,0:T(8,128)(2,1)} collective-permute-done((bf16[3,800,256]{2,1,0:T(8,128)(2,1)S(1)}, bf16[3,800,256]{2,1,0:T(8,128)(2,1)}, u32[]{:S(2)}, u32[]{:S(2)}) %collective-permute-start.6) | collective-permute-done | bytes 1228832 | tf_op jit(solution)/shard_map/ppermute | solution.py:109
  83.0 3.6 %collective-permute-start.13 = (bf16[4,256,896]{2,1,0:T(8,128)(2,1)}, bf16[4,256,896]{2,1,0:T(8,128)(2,1)S(1)}, u32[]{:S(2)}, u32[]{:S(2)}) collective-permute-start(bf16[4,256,896]{2,1,0:T(8,128)(2,1)} %collective-permute-done.7.xc), channel_id=1, source_target_pairs={{0,2},{1,3},{2,0},{3,1},{4,6},{5,7},{6,4},{7,5},{8,10},{9,11},{10,... | collective-permute-start | bytes 5505032 | tf_op jit(solution)/shard_map/ppermute | solution.py:109
  87.7 4.2 %collective-permute-done.13.xd = bf16[4,256,896]{2,1,0:T(8,128)(2,1)S(1)} collective-permute-done((bf16[4,256,896]{2,1,0:T(8,128)(2,1)}, bf16[4,256,896]{2,1,0:T(8,128)(2,1)S(1)}, u32[]{:S(2)}, u32[]{:S(2)}) %collective-permute-start.13) | collective-permute-done | bytes 1835040 | tf_op jit(solution)/shard_map/ppermute | solution.py:109
  92.9 9.5 %early.1 = (f32[4,3,256,256]{3,2,1,0:T(8,128)S(1)}, bf16[4,256,896]{2,1,0:T(8,128)(2,1)S(1)}) custom-call(s32[3]{0:T(128)S(1)} %pad_add_fusion.1.place, bf16[4,256,896]{2,1,0:T(8,128)(2,1)S(1)} %copy-done, bf16[4,256,896]{2,1,0:T(8,128)(2,1)S(1)} %collective-permute-done.12.xb, bf16[4,256,896]{2,1,0:T(8,128)(2,1)} %collective-permute-done.7.xc, ...), custom_call_target="tpu_custom_call" | custom-call | flops 7549747200 | bytes 8601600 | tf_op jit(solution)/shard_map/early/pallas_call | solution.py:216
  102.5 12.5 %collective-permute-done.11.last = bf16[3,800,256]{2,1,0:T(8,128)(2,1)S(1)} collective-permute-done((bf16[3,800,256]{2,1,0:T(8,128)(2,1)}, bf16[3,800,256]{2,1,0:T(8,128)(2,1)S(1)}, u32[]{:S(2)}, u32[]{:S(2)}) %collective-permute-start.11) | collective-permute-done | bytes 1228832 | tf_op jit(solution)/shard_map/ppermute | solution.py:109
  115.0 2.5 %late.1 = (f32[1024,256]{1,0:T(8,128)S(1)}, bf16[1024,256]{1,0:T(8,128)(2,1)S(1)}, bf16[1024,256]{1,0:T(8,128)(2,1)S(1)}, f32[2,1024]{1,0:T(2,128)S(1)}, bf16[2,...) custom-call(s32[3]{0:T(128)S(1)} %pad_add_fusion.1.place, bf16[4,256,896]{2,1,0:T(8,128)(2,1)S(1)} %get-tuple-element.56.x_last, ...), custom_call_target="tpu_custom_call" | custom-call | flops 1258291200 | bytes 2867200 | tf_op jit(solution)/shard_map/late/pallas_call | solution.py:273
  117.5 1.6 %collective-permute-start.15 = (bf16[2,512,256]{2,1,0:T(8,128)(2,1)S(1)}, bf16[2,512,256]{2,1,0:T(8,128)(2,1)S(1)}, u32[]{:S(2)}, u32[]{:S(2)}) collective-permute-start(bf16[2,512,256]{2,1,0:T(8,128)(2,1)S(1)} %get-tuple-element.65), channel_id=1, source_target_pairs={{0,2},{1,3},{2,0},{3,1},{4,6},{5,7},{6,4},{7,5},{8,16},{9,17},{10,... | collective-permute-start | bytes 1572872 | tf_op jit(solution)/shard_map/ppermute | solution.py:109
  119.1 1.6 %collective-permute-start.20 = (f32[2,1024]{1,0:T(2,128)S(1)}, f32[2,1024]{1,0:T(2,128)S(1)}, u32[]{:S(2)}, u32[]{:S(2)}) collective-permute-start(f32[2,1024]{1,0:T(2,128)S(1)} %get-tuple-element.70), channel_id=1, source_target_pairs={{0,2},{1,3},{2,0},{3,1},{4,6},{5,7},{6,4},{7,5},{8,10},{9,11},{10,... | collective-permute-start | bytes 24584 | tf_op jit(solution)/shard_map/ppermute | solution.py:109
  128.7 1.7 %collective-permute-start.26 = (bf16[2,208,1024]{2,1,0:T(8,128)(2,1)S(1)}, bf16[2,208,1024]{2,1,0:T(8,128)(2,1)S(1)}, u32[]{:S(2)}, u32[]{:S(2)}) collective-permute-start(bf16[2,208,1024]{2,1,0:T(8,128)(2,1)S(1)} %collective-permute-done.16.wc1), channel_id=1, source_target_pairs={{0,2},{1,3},{2,0},{3,1},{4,6},{5,7},{6,4},{7,5},{8,10},{9,11},{10,... | collective-permute-start | bytes 2555912 | tf_op jit(solution)/shard_map/ppermute | solution.py:109
  130.4 4.7 %attend.1 = (bf16[256,256]{1,0:T(8,128)(2,1)S(1)}, bf16[256,256]{1,0:T(8,128)(2,1)S(1)}, bf16[256,256]{1,0:T(8,128)(2,1)S(1)}, bf16[256,256]{1,0:T(8,128)(2,1)S(1)}) custom-call(s32[3]{0:T(128)S(1)} %pad_add_fusion.1.place, s32[4,2]{1,0:T(4,128)S(1)} %pad_add_fusion.spans, f32[1024,256]{1,0:T(8,128)S(1)} %get-tuple-element.61.query, ...), custom_call_target="tpu_custom_call" | custom-call | flops 21474836480 | bytes 3145728 | tf_op jit(solution)/shard_map/attend/pallas_call | solution.py:380
  137.6 2.7 %collective-permute-start.29 = (bf16[256,256]{1,0:T(8,128)(2,1)S(1)}, bf16[256,256]{1,0:T(8,128)(2,1)S(1)}, u32[]{:S(2)}, u32[]{:S(2)}) collective-permute-start(bf16[256,256]{1,0:T(8,128)(2,1)S(1)} %get-tuple-element.79), channel_id=1, source_target_pairs={{0,7},{1,6},{2,5},{3,4},{4,3},{5,2},{6,1},{7,0},{8,15},{9,14},{10,... | collective-permute-start | bytes 393224 | tf_op jit(solution)/shard_map/ppermute | solution.py:109
  140.4 2.1 %collective-permute-start.32 = (bf16[256,256]{1,0:T(8,128)(2,1)S(1)}, bf16[256,256]{1,0:T(8,128)(2,1)S(1)}, u32[]{:S(2)}, u32[]{:S(2)}) collective-permute-start(bf16[256,256]{1,0:T(8,128)(2,1)S(1)} %get-tuple-element.77), channel_id=1, source_target_pairs={{0,5},{1,4},{2,7},{3,6},{4,1},{5,0},{6,3},{7,2},{8,13},{9,12},{10,... | collective-permute-start | bytes 393224 | tf_op jit(solution)/shard_map/ppermute | solution.py:109
  143.5 2.8 %collective-permute-start.33 = (bf16[256,256]{1,0:T(8,128)(2,1)S(1)}, bf16[256,256]{1,0:T(8,128)(2,1)S(1)}, u32[]{:S(2)}, u32[]{:S(2)}) collective-permute-start(bf16[256,256]{1,0:T(8,128)(2,1)S(1)} %get-tuple-element.80), channel_id=1, source_target_pairs={{0,2},{1,3},{2,0},{3,1},{4,6},{5,7},{6,4},{7,5},{8,10},{9,11},{10,... | collective-permute-start | bytes 393224 | tf_op jit(solution)/shard_map/ppermute | solution.py:109
  147.1 4.5 %collective-permute-done.31.c11 = bf16[256,256]{1,0:T(8,128)(2,1)S(1)} collective-permute-done((bf16[256,256]{1,0:T(8,128)(2,1)S(1)}, bf16[256,256]{1,0:T(8,128)(2,1)S(1)}, u32[]{:S(2)}, u32[]{:S(2)}) %collective-permute-start.31) | collective-permute-done | bytes 131104 | tf_op jit(solution)/shard_map/ppermute | solution.py:109
  151.7 3.9 %output.1 = bf16[1600,256]{1,0:T(8,128)(2,1)} custom-call(s32[3]{0:T(128)S(1)} %pad_add_fusion.1.place, bf16[256,256]{1,0:T(8,128)(2,1)S(1)} %collective-permute-done.27.c20, bf16[256,256]{1,0:T(8,128)(2,1)S(1)} %collective-permute-done.28.c01, bf16[256,256]{1,0:T(8,128)(2,1)S(1)} %collective-permute-done.29.c31, ...), custom_call_target="tpu_custom_call" | custom-call | flops 1677721600 | bytes 6553600 | tf_op jit(solution)/shard_map/output/pallas_call | solution.py:456
  (87 shorter events, 25.0 us)
Async XLA Ops:
  0.0 17.4 %collective-permute-start = (bf16[200,1024]{1,0:T(8,128)(2,1)}, bf16[200,1024]{1,0:T(8,128)(2,1)}, u32[]{:S(2)}, u32[]{:S(2)}) collective-permute-start(bf16[200,1024]{1,0:T(8,128)(2,1)} %bitcast.42), channel_id=1, source_target_pairs={{0,8},{1,9},{2,10},{3,11},{4,12},{5,13},{6,14},{7,15},{8,0},{9,1},... | collective-permute-start | bytes 1228808 | tf_op jit(solution)/shard_map/ppermute | solution.py:109
  0.0 20.5 %collective-permute-start.1 = (bf16[200,1024]{1,0:T(8,128)(2,1)}, bf16[200,1024]{1,0:T(8,128)(2,1)}, u32[]{:S(2)}, u32[]{:S(2)}) collective-permute-start(bf16[200,1024]{1,0:T(8,128)(2,1)} %bitcast.43), channel_id=1, source_target_pairs={{0,16},{1,17},{2,18},{3,19},{4,20},{5,21},{6,22},{7,23},{8,24},{9,... | collective-permute-start | bytes 1228808 | tf_op jit(solution)/shard_map/ppermute | solution.py:109
  4.6 17.1 %collective-permute-start.2 = (bf16[3,200,256]{2,1,0:T(8,128)(2,1)}, bf16[3,200,256]{2,1,0:T(8,128)(2,1)}, u32[]{:S(2)}, u32[]{:S(2)}) collective-permute-start(bf16[3,200,256]{2,1,0:T(8,128)(2,1)} %get-tuple-element.101), channel_id=1, source_target_pairs={{0,6},{1,7},{2,4},{3,5},{4,2},{5,3},{6,0},{7,1},{8,14},{9,15},{10,... | collective-permute-start | bytes 921608 | tf_op jit(solution)/shard_map/ppermute | solution.py:109
  6.9 14.9 %collective-permute-start.3 = (bf16[3,200,256]{2,1,0:T(8,128)(2,1)}, bf16[3,200,256]{2,1,0:T(8,128)(2,1)}, u32[]{:S(2)}, u32[]{:S(2)}) collective-permute-start(bf16[3,200,256]{2,1,0:T(8,128)(2,1)} %get-tuple-element.102), channel_id=1, source_target_pairs={{0,4},{1,5},{2,6},{3,7},{4,0},{5,1},{6,2},{7,3},{8,12},{9,13},{10,... | collective-permute-start | bytes 921608 | tf_op jit(solution)/shard_map/ppermute | solution.py:109
  7.2 14.7 %collective-permute-start.4 = (bf16[3,200,256]{2,1,0:T(8,128)(2,1)}, bf16[3,200,256]{2,1,0:T(8,128)(2,1)}, u32[]{:S(2)}, u32[]{:S(2)}) collective-permute-start(bf16[3,200,256]{2,1,0:T(8,128)(2,1)} %get-tuple-element.103), channel_id=1, source_target_pairs={{0,2},{1,3},{2,0},{3,1},{4,6},{5,7},{6,4},{7,5},{8,10},{9,11},{10,... | collective-permute-start | bytes 921608 | tf_op jit(solution)/shard_map/ppermute | solution.py:109
  20.5 62.5 %collective-permute-start.7 = (bf16[4,256,896]{2,1,0:T(8,128)(2,1)}, bf16[4,256,896]{2,1,0:T(8,128)(2,1)}, u32[]{:S(2)}, u32[]{:S(2)}) collective-permute-start(bf16[4,256,896]{2,1,0:T(8,128)(2,1)} %norm.1.xa), channel_id=1, source_target_pairs={{0,4},{1,5},{2,6},{3,7},{4,0},{5,1},{6,2},{7,3},{8,12},{9,13},{10,... | collective-permute-start | bytes 5505032 | tf_op jit(solution)/shard_map/ppermute | solution.py:109
  21.7 32.2 %collective-permute-start.8 = (bf16[200,1024]{1,0:T(8,128)(2,1)}, bf16[200,1024]{1,0:T(8,128)(2,1)}, u32[]{:S(2)}, u32[]{:S(2)}) collective-permute-start(bf16[200,1024]{1,0:T(8,128)(2,1)} %collective-permute-done.1), channel_id=1, source_target_pairs={{0,8},{1,9},{2,10},{3,11},{4,12},{5,13},{6,14},{7,15},{8,0},{9,1},... | collective-permute-start | bytes 1228808 | tf_op jit(solution)/shard_map/ppermute | solution.py:109
  23.6 56.6 %collective-permute-start.5 = (bf16[3,800,256]{2,1,0:T(8,128)(2,1)S(1)}, bf16[3,800,256]{2,1,0:T(8,128)(2,1)S(1)}, u32[]{:S(2)}, u32[]{:S(2)}) collective-permute-start(bf16[3,800,256]{2,1,0:T(8,128)(2,1)S(1)} %pad_maximum_fusion.own), channel_id=1, source_target_pairs={{0,8},{1,9},{2,10},{3,11},{4,12},{5,13},{6,14},{7,15},{8,0},{9,1},... | collective-permute-start | bytes 3686408 | tf_op jit(solution)/shard_map/ppermute | solution.py:109
  25.0 58.0 %collective-permute-start.6 = (bf16[3,800,256]{2,1,0:T(8,128)(2,1)S(1)}, bf16[3,800,256]{2,1,0:T(8,128)(2,1)}, u32[]{:S(2)}, u32[]{:S(2)}) collective-permute-start(bf16[3,800,256]{2,1,0:T(8,128)(2,1)S(1)} %pad_maximum_fusion.own), channel_id=1, source_target_pairs={{0,16},{1,17},{2,18},{3,19},{4,20},{5,21},{6,22},{7,23},{8,24},{9,... | collective-permute-start | bytes 3686408 | tf_op jit(solution)/shard_map/ppermute | solution.py:109
  55.5 27.4 %collective-permute-start.10 = (bf16[2,208,1024]{2,1,0:T(8,128)(2,1)S(1)}, bf16[2,208,1024]{2,1,0:T(8,128)(2,1)S(1)}, u32[]{:S(2)}, u32[]{:S(2)}) collective-permute-start(bf16[2,208,1024]{2,1,0:T(8,128)(2,1)S(1)} %pad.13.wa0), channel_id=1, source_target_pairs={{0,4},{1,5},{2,6},{3,7},{4,0},{5,1},{6,2},{7,3},{8,12},{9,13},{10,... | collective-permute-start | bytes 2555912 | tf_op jit(solution)/shard_map/ppermute | solution.py:109
  55.8 27.2 %collective-permute-start.9 = (bf16[2,208,1024]{2,1,0:T(8,128)(2,1)S(1)}, bf16[2,208,1024]{2,1,0:T(8,128)(2,1)S(1)}, u32[]{:S(2)}, u32[]{:S(2)}) collective-permute-start(bf16[2,208,1024]{2,1,0:T(8,128)(2,1)S(1)} %pad.12), channel_id=1, source_target_pairs={{0,1},{1,0},{2,3},{3,2},{4,5},{5,4},{6,7},{7,6},{8,9},{9,8},{10,11... | collective-permute-start | bytes 2555912 | tf_op jit(solution)/shard_map/ppermute | solution.py:109
  83.0 8.9 %collective-permute-start.13 = (bf16[4,256,896]{2,1,0:T(8,128)(2,1)}, bf16[4,256,896]{2,1,0:T(8,128)(2,1)S(1)}, u32[]{:S(2)}, u32[]{:S(2)}) collective-permute-start(bf16[4,256,896]{2,1,0:T(8,128)(2,1)} %collective-permute-done.7.xc), channel_id=1, source_target_pairs={{0,2},{1,3},{2,0},{3,1},{4,6},{5,7},{6,4},{7,5},{8,10},{9,11},{10,... | collective-permute-start | bytes 5505032 | tf_op jit(solution)/shard_map/ppermute | solution.py:109
  86.6 28.4 %collective-permute-start.11 = (bf16[3,800,256]{2,1,0:T(8,128)(2,1)}, bf16[3,800,256]{2,1,0:T(8,128)(2,1)S(1)}, u32[]{:S(2)}, u32[]{:S(2)}) collective-permute-start(bf16[3,800,256]{2,1,0:T(8,128)(2,1)} %collective-permute-done.6.far), channel_id=1, source_target_pairs={{0,8},{1,9},{2,10},{3,11},{4,12},{5,13},{6,14},{7,15},{8,0},{9,1},... | collective-permute-start | bytes 3686408 | tf_op jit(solution)/shard_map/ppermute | solution.py:109
  86.6 30.9 %collective-permute-start.18 = (bf16[2,208,1024]{2,1,0:T(8,128)(2,1)S(1)}, bf16[2,208,1024]{2,1,0:T(8,128)(2,1)S(1)}, u32[]{:S(2)}, u32[]{:S(2)}) collective-permute-start(bf16[2,208,1024]{2,1,0:T(8,128)(2,1)S(1)} %pad.13.wa0), channel_id=1, source_target_pairs={{0,2},{1,3},{2,0},{3,1},{4,6},{5,7},{6,4},{7,5},{8,10},{9,11},{10,... | collective-permute-start | bytes 2555912 | tf_op jit(solution)/shard_map/ppermute | solution.py:109
  87.4 31.7 %collective-permute-start.16 = (bf16[2,208,1024]{2,1,0:T(8,128)(2,1)S(1)}, bf16[2,208,1024]{2,1,0:T(8,128)(2,1)S(1)}, u32[]{:S(2)}, u32[]{:S(2)}) collective-permute-start(bf16[2,208,1024]{2,1,0:T(8,128)(2,1)S(1)} %collective-permute-done.9.wa1), channel_id=1, source_target_pairs={{0,4},{1,5},{2,6},{3,7},{4,0},{5,1},{6,2},{7,3},{8,12},{9,13},{10,... | collective-permute-start | bytes 2555912 | tf_op jit(solution)/shard_map/ppermute | solution.py:109
  91.9 27.2 %collective-permute-start.17 = (bf16[2,208,1024]{2,1,0:T(8,128)(2,1)S(1)}, bf16[2,208,1024]{2,1,0:T(8,128)(2,1)S(1)}, u32[]{:S(2)}, u32[]{:S(2)}) collective-permute-start(bf16[2,208,1024]{2,1,0:T(8,128)(2,1)S(1)} %collective-permute-done.9.wa1), channel_id=1, source_target_pairs={{0,2},{1,3},{2,0},{3,1},{4,6},{5,7},{6,4},{7,5},{8,10},{9,11},{10,... | collective-permute-start | bytes 2555912 | tf_op jit(solution)/shard_map/ppermute | solution.py:109
  92.6 26.6 %collective-permute-start.19 = (bf16[2,208,1024]{2,1,0:T(8,128)(2,1)S(1)}, bf16[2,208,1024]{2,1,0:T(8,128)(2,1)S(1)}, u32[]{:S(2)}, u32[]{:S(2)}) collective-permute-start(bf16[2,208,1024]{2,1,0:T(8,128)(2,1)S(1)} %collective-permute-done.10.wc0), channel_id=1, source_target_pairs={{0,2},{1,3},{2,0},{3,1},{4,6},{5,7},{6,4},{7,5},{8,10},{9,11},{10,... | collective-permute-start | bytes 2555912 | tf_op jit(solution)/shard_map/ppermute | solution.py:109
  117.5 12.9 %collective-permute-start.14 = (bf16[2,512,256]{2,1,0:T(8,128)(2,1)S(1)}, bf16[2,512,256]{2,1,0:T(8,128)(2,1)S(1)}, u32[]{:S(2)}, u32[]{:S(2)}) collective-permute-start(bf16[2,512,256]{2,1,0:T(8,128)(2,1)S(1)} %get-tuple-element.64), channel_id=1, source_target_pairs={{0,8},{1,9},{2,10},{3,11},{4,12},{5,13},{6,14},{7,15},{8,0},{9,1},... | collective-permute-start | bytes 1572872 | tf_op jit(solution)/shard_map/ppermute | solution.py:109
  117.5 12.9 %collective-permute-start.15 = (bf16[2,512,256]{2,1,0:T(8,128)(2,1)S(1)}, bf16[2,512,256]{2,1,0:T(8,128)(2,1)S(1)}, u32[]{:S(2)}, u32[]{:S(2)}) collective-permute-start(bf16[2,512,256]{2,1,0:T(8,128)(2,1)S(1)} %get-tuple-element.65), channel_id=1, source_target_pairs={{0,2},{1,3},{2,0},{3,1},{4,6},{5,7},{6,4},{7,5},{8,16},{9,17},{10,... | collective-permute-start | bytes 1572872 | tf_op jit(solution)/shard_map/ppermute | solution.py:109
  135.1 7.4 %collective-permute-start.27 = (bf16[256,256]{1,0:T(8,128)(2,1)S(1)}, bf16[256,256]{1,0:T(8,128)(2,1)S(1)}, u32[]{:S(2)}, u32[]{:S(2)}) collective-permute-start(bf16[256,256]{1,0:T(8,128)(2,1)S(1)} %get-tuple-element.77), channel_id=1, source_target_pairs={{0,4},{1,5},{2,6},{3,7},{4,0},{5,1},{6,2},{7,3},{8,12},{9,13},{10,... | collective-permute-start | bytes 393224 | tf_op jit(solution)/shard_map/ppermute | solution.py:109
  137.6 9.5 %collective-permute-start.29 = (bf16[256,256]{1,0:T(8,128)(2,1)S(1)}, bf16[256,256]{1,0:T(8,128)(2,1)S(1)}, u32[]{:S(2)}, u32[]{:S(2)}) collective-permute-start(bf16[256,256]{1,0:T(8,128)(2,1)S(1)} %get-tuple-element.79), channel_id=1, source_target_pairs={{0,7},{1,6},{2,5},{3,4},{4,3},{5,2},{6,1},{7,0},{8,15},{9,14},{10,... | collective-permute-start | bytes 393224 | tf_op jit(solution)/shard_map/ppermute | solution.py:109
  140.4 11.3 %collective-permute-start.32 = (bf16[256,256]{1,0:T(8,128)(2,1)S(1)}, bf16[256,256]{1,0:T(8,128)(2,1)S(1)}, u32[]{:S(2)}, u32[]{:S(2)}) collective-permute-start(bf16[256,256]{1,0:T(8,128)(2,1)S(1)} %get-tuple-element.77), channel_id=1, source_target_pairs={{0,5},{1,4},{2,7},{3,6},{4,1},{5,0},{6,3},{7,2},{8,13},{9,12},{10,... | collective-permute-start | bytes 393224 | tf_op jit(solution)/shard_map/ppermute | solution.py:109
  142.5 9.2 %collective-permute-start.31 = (bf16[256,256]{1,0:T(8,128)(2,1)S(1)}, bf16[256,256]{1,0:T(8,128)(2,1)S(1)}, u32[]{:S(2)}, u32[]{:S(2)}) collective-permute-start(bf16[256,256]{1,0:T(8,128)(2,1)S(1)} %get-tuple-element.80), channel_id=1, source_target_pairs={{0,3},{1,2},{2,1},{3,0},{4,7},{5,6},{6,5},{7,4},{8,11},{9,10},{10,... | collective-permute-start | bytes 393224 | tf_op jit(solution)/shard_map/ppermute | solution.py:109
  143.5 8.2 %collective-permute-start.33 = (bf16[256,256]{1,0:T(8,128)(2,1)S(1)}, bf16[256,256]{1,0:T(8,128)(2,1)S(1)}, u32[]{:S(2)}, u32[]{:S(2)}) collective-permute-start(bf16[256,256]{1,0:T(8,128)(2,1)S(1)} %get-tuple-element.80), channel_id=1, source_target_pairs={{0,2},{1,3},{2,0},{3,1},{4,6},{5,7},{6,4},{7,5},{8,10},{9,11},{10,... | collective-permute-start | bytes 393224 | tf_op jit(solution)/shard_map/ppermute | solution.py:109
  (15 other events, 101.5 us)
